TPU v7x, 256 devices: a whole 4x4x8 slice. The times are simulated.
256 devices in a mesh: face: 4 (over z_lo), tile: 64 (over z_hi, x, y, core).
Axes of the slice: x: 4, y: 4, z: 8 (z_hi: 2, z_lo: 4; z = z_hi * 4 + z_lo), core: 2. Of those that a mesh axis runs over, the one named last changes fastest.
Arguments:
- inputs: bfloat16 [12, 64, 8, 8, 256], P('face', 'tile'), may hold values from -6 to 6
- cotangent: bfloat16 [12, 64, 8, 8, 256], P('face', 'tile'), may hold values from -6 to 6
- kernel_one: bfloat16 [3, 3, 256, 256], replicated, may hold values from -0.125 to 0.125
- kernel_two: bfloat16 [3, 3, 256, 256], replicated, may hold values from -0.125 to 0.125
- neighbour: int32 [12, 4], replicated, may hold values from 0 to 11, as said below
- seam_codes: int32 [12, 4], replicated, may hold values from 0 to 3
Outputs:
- input_grad: bfloat16 [12, 64, 8, 8, 256], P('face', 'tile')
- kernel_one_grad: float32 [3, 3, 256, 256], replicated
- kernel_two_grad: float32 [3, 3, 256, 256], replicated
Inputs may be any that keep to these rules, and one draw needn't show every extreme that they name: neighbour[f, s] is never f itself. `seam_codes`: bit 0 picks the neighbour's edge on the same side, bit 1 reverses it.
All inputs are finite; a program needn't handle non-finite values.
Results may differ from a plain program's by a relative error of at most 0.015.
Values may be sent and summed in bfloat16 or wider, within the bound.
No kernel may reach another device: no remote copies, remote signals or barrier semaphores. Data moves between devices by JAX's collectives and lax.ppermute only.
A program may use at most 64 MiB of HBM per device.

v0:
```python
import math

import jax
import jax.numpy as jnp
from jax import lax
from jax.sharding import PartitionSpec as P


def shifted(x, axis, by):
    length = lax.axis_size(axis)
    pairs = [(i, i + by) for i in range(length) if 0 <= i + by < length]
    return lax.ppermute(x, axis, pairs)


def swapped(x, axis, distance):
    return lax.ppermute(x, axis, [(i, i ^ 1 << distance) for i in range(lax.axis_size(axis))])


def slope_of(pre_act):
    logistic = jax.nn.sigmoid(pre_act)
    return logistic * (1.0 + pre_act * (1.0 - logistic))


def rim_forward(payload, offset):
    return shifted(payload, "tile", offset)


def rim_backward(payload, offset):
    return shifted(payload, "tile", offset)


def seam_forward(payload, bit_index):
    return swapped(payload, "tile", bit_index)


def seam_backward(payload, bit_index):
    return swapped(payload.astype(jnp.bfloat16), "tile", bit_index).astype(payload.dtype)


def route_seams(seam_buf, context, swapper):
    position_mask = context["xor_mask"][:, context["side_of"]]
    for bit_index in range(context["bits"]):
        moved_seams = swapper(seam_buf, bit_index)
        take_flag = position_mask // 2**bit_index % 2 == 1
        seam_buf = jnp.where(take_flag[:, :, None], moved_seams, seam_buf)
    return seam_buf


def flip_strip(strip_piece, flip_flag):
    return jnp.where(flip_flag[:, None, None] == 1, strip_piece[:, ::-1], strip_piece)


def pad_tile(tile_field, context):
    faces_dev, rows_len, cols_len, channels = tile_field.shape
    rim_strips = jnp.concatenate(
        [
            jnp.stack([tile_field[:, 0], tile_field[:, -1]], axis=1),
            jnp.stack([tile_field[:, :, 0], tile_field[:, :, -1]], axis=1),
        ],
        axis=2,
    )
    everyone = lax.all_gather(rim_strips, "face", axis=0, tiled=True)
    flat_rows = everyone.reshape(everyone.shape[0] * 2, -1)
    chosen = jnp.dot(
        context["selector"].astype(jnp.bfloat16), flat_rows, preferred_element_type=jnp.float32
    )
    chosen = chosen.astype(jnp.bfloat16).reshape(faces_dev, 4, rows_len + cols_len, channels)
    packed = jnp.concatenate(
        [
            chosen[:, 0, :cols_len],
            chosen[:, 1, :cols_len],
            chosen[:, 2, cols_len:],
            chosen[:, 3, cols_len:],
        ],
        axis=1,
    )
    packed = route_seams(packed, context, seam_forward)
    edge_flag = context["on_edge"][context["side_of"]]
    packed = jnp.where(edge_flag[None, :, None], packed, jnp.zeros_like(packed))
    flipped = context["flipped"]
    seam_top = flip_strip(packed[:, :cols_len], flipped[:, 0])
    seam_bottom = flip_strip(packed[:, cols_len : 2 * cols_len], flipped[:, 1])
    seam_left = flip_strip(packed[:, 2 * cols_len : 2 * cols_len + rows_len], flipped[:, 2])
    seam_right = flip_strip(packed[:, 2 * cols_len + rows_len :], flipped[:, 3])
    extended = jnp.concatenate([seam_top[:, None], tile_field, seam_bottom[:, None]], axis=1)
    col_pos = context["col_pos"]
    row_pos = context["row_pos"]
    edge_pad = ((0, 0), (1, 1), (0, 0))
    from_left = rim_forward(extended[:, :, -1], 1)
    left_column = jnp.where(col_pos > 0, from_left, jnp.pad(seam_left, edge_pad))
    from_right = rim_forward(extended[:, :, 0], -1)
    right_column = jnp.where(col_pos < 7, from_right, jnp.pad(seam_right, edge_pad))
    widened = jnp.concatenate([left_column[:, :, None], extended, right_column[:, :, None]], axis=2)
    from_above = rim_forward(widened[:, -2], 8)
    top_row = jnp.where(row_pos > 0, from_above, widened[:, 0])
    from_below = rim_forward(widened[:, 1], -8)
    bottom_row = jnp.where(row_pos < context["grid_rows"] - 1, from_below, widened[:, -1])
    return jnp.concatenate([top_row[:, None], widened[:, 1:-1], bottom_row[:, None]], axis=1)


def unpad_tile(pad_grad, context):
    faces_dev = pad_grad.shape[0]
    rows_len = pad_grad.shape[1] - 2
    cols_len = pad_grad.shape[2] - 2
    channels = pad_grad.shape[3]
    col_pos = context["col_pos"]
    row_pos = context["row_pos"]
    last_row = context["grid_rows"] - 1
    top_grad = pad_grad[:, 0]
    bottom_grad = pad_grad[:, -1]
    sent_up = rim_backward(jnp.where(row_pos > 0, top_grad, 0.0), -8)
    sent_down = rim_backward(jnp.where(row_pos < last_row, bottom_grad, 0.0), 8)
    row_zero = jnp.where(row_pos == 0, top_grad, 0.0)
    row_last = jnp.where(row_pos == last_row, bottom_grad, 0.0)
    wide_grad = jnp.concatenate([row_zero[:, None], pad_grad[:, 1:-1], row_last[:, None]], axis=1)
    wide_grad = wide_grad.at[:, -2].add(sent_up).at[:, 1].add(sent_down)
    left_grad = wide_grad[:, :, 0]
    right_grad = wide_grad[:, :, -1]
    sent_left = rim_backward(jnp.where(col_pos > 0, left_grad, 0.0), -1)
    sent_right = rim_backward(jnp.where(col_pos < 7, right_grad, 0.0), 1)
    ext_grad = wide_grad[:, :, 1:-1]
    ext_grad = ext_grad.at[:, :, -1].add(sent_left).at[:, :, 0].add(sent_right)
    seam_left = jnp.where(col_pos == 0, left_grad[:, 1:-1], 0.0)
    seam_right = jnp.where(col_pos == 7, right_grad[:, 1:-1], 0.0)
    seam_top = jnp.where(row_pos == 0, ext_grad[:, 0], 0.0)
    seam_bottom = jnp.where(row_pos == last_row, ext_grad[:, -1], 0.0)
    field_grad = ext_grad[:, 1:-1]
    flipped = context["flipped"]
    packed = jnp.concatenate(
        [
            flip_strip(seam_top, flipped[:, 0]),
            flip_strip(seam_bottom, flipped[:, 1]),
            flip_strip(seam_left, flipped[:, 2]),
            flip_strip(seam_right, flipped[:, 3]),
        ],
        axis=1,
    )
    packed = route_seams(packed, context, seam_backward)
    zero_rows = jnp.zeros((faces_dev, rows_len, channels), jnp.float32)
    zero_cols = jnp.zeros((faces_dev, cols_len, channels), jnp.float32)
    seam_buf = jnp.stack(
        [
            jnp.concatenate([packed[:, :cols_len], zero_rows], axis=1),
            jnp.concatenate([packed[:, cols_len : 2 * cols_len], zero_rows], axis=1),
            jnp.concatenate([zero_cols, packed[:, 2 * cols_len : 2 * cols_len + rows_len]], axis=1),
            jnp.concatenate([zero_cols, packed[:, 2 * cols_len + rows_len :]], axis=1),
        ],
        axis=1,
    )
    spread = jnp.dot(
        context["selector"].astype(jnp.float32).T,
        seam_buf.reshape(faces_dev * 4, -1),
        precision=lax.Precision.HIGHEST,
    )
    spread = spread.reshape(spread.shape[0] // 2, 2, rows_len + cols_len, channels)
    own_edges = lax.psum_scatter(
        spread.astype(jnp.bfloat16), "face", scatter_dimension=0, tiled=True
    ).astype(jnp.float32)
    field_grad = field_grad.at[:, 0].add(own_edges[:, 0, :cols_len])
    field_grad = field_grad.at[:, -1].add(own_edges[:, 1, :cols_len])
    field_grad = field_grad.at[:, :, 0].add(own_edges[:, 0, cols_len:])
    field_grad = field_grad.at[:, :, -1].add(own_edges[:, 1, cols_len:])
    return field_grad


def patches_of(padded, rows_len, cols_len):
    shifted_views = [
        padded[:, shift_row : shift_row + rows_len, shift_col : shift_col + cols_len]
        for shift_row in range(3)
        for shift_col in range(3)
    ]
    return jnp.concatenate(shifted_views, axis=-1).reshape(-1, 9 * padded.shape[-1])


def padded_gradient(delta, flat_kernel, shape_four):
    faces_dev, rows_len, cols_len, channels = shape_four
    spread = lax.dot_general(
        delta, flat_kernel, (((1,), (1,)), ((), ())), preferred_element_type=jnp.float32
    )
    pad_grad = jnp.zeros((faces_dev, rows_len + 2, cols_len + 2, channels), jnp.float32)
    for shift_row in range(3):
        for shift_col in range(3):
            offset_index = shift_row * 3 + shift_col
            block = spread[:, offset_index * channels : (offset_index + 1) * channels]
            pad_grad = pad_grad.at[
                :, shift_row : shift_row + rows_len, shift_col : shift_col + cols_len
            ].add(block.reshape(faces_dev, rows_len, cols_len, channels))
    return lax.optimization_barrier(pad_grad.astype(jnp.bfloat16)).astype(jnp.float32)


def body(inputs, cotangent, kernel_one, kernel_two, neighbour, seam_codes):
    tile_field = inputs[:, 0]
    faces_dev, rows_len, cols_len, channels = tile_field.shape
    shape_four = (faces_dev, rows_len, cols_len, channels)
    tile_count = lax.axis_size("tile")
    grid_rows = tile_count // 8
    tile_index = lax.axis_index("tile")
    face_count = faces_dev * lax.axis_size("face")
    first_face = lax.axis_index("face") * faces_dev
    local_next = lax.dynamic_slice_in_dim(neighbour, first_face, faces_dev, 0)
    local_codes = lax.dynamic_slice_in_dim(seam_codes, first_face, faces_dev, 0)
    same_side = local_codes % 2
    flipped = local_codes // 2
    parity = jnp.arange(4, dtype=jnp.int32) % 2
    which_edge = jnp.where(same_side == 1, parity[None, :], 1 - parity[None, :])
    source_row = (local_next * 2 + which_edge).reshape(-1)
    selector = source_row[:, None] == jnp.arange(face_count * 2, dtype=jnp.int32)[None, :]
    across = (grid_rows - 1) * 8
    horizontal = jnp.arange(4, dtype=jnp.int32) < 2
    opposite_mask = jnp.where(horizontal, across, 7)
    reverse_mask = jnp.where(horizontal, 7, across)
    xor_mask = jnp.where(same_side == 1, 0, opposite_mask[None, :]) + jnp.where(
        flipped == 1, reverse_mask[None, :], 0
    )
    side_of = jnp.concatenate(
        [
            jnp.zeros((cols_len,), jnp.int32),
            jnp.ones((cols_len,), jnp.int32),
            jnp.full((rows_len,), 2, jnp.int32),
            jnp.full((rows_len,), 3, jnp.int32),
        ]
    )
    col_pos = tile_index % 8
    row_pos = tile_index // 8
    on_edge = jnp.stack([row_pos == 0, row_pos == grid_rows - 1, col_pos == 0, col_pos == 7])
    context = {
        "bits": tile_count.bit_length() - 1,
        "xor_mask": xor_mask,
        "selector": selector,
        "flipped": flipped,
        "on_edge": on_edge,
        "col_pos": col_pos,
        "row_pos": row_pos,
        "grid_rows": grid_rows,
        "side_of": side_of,
    }
    flat_one = kernel_one.reshape(9 * channels, channels)
    flat_two = kernel_two.reshape(9 * channels, channels)
    padded_in = pad_tile(tile_field, context)
    patches_in = patches_of(padded_in, rows_len, cols_len)
    pre_one = jnp.dot(patches_in, flat_one, preferred_element_type=jnp.float32)
    hidden = jax.nn.silu(pre_one).astype(jnp.bfloat16).reshape(shape_four)
    padded_hidden = pad_tile(hidden, context)
    patches_hidden = patches_of(padded_hidden, rows_len, cols_len)
    pre_two = jnp.dot(patches_hidden, flat_two, preferred_element_type=jnp.float32)
    delta_two = (
        cotangent[:, 0].reshape(-1, channels).astype(jnp.float32) * slope_of(pre_two)
    ).astype(jnp.bfloat16)
    contract_rows = (((0,), (0,)), ((), ()))
    grad_two = lax.dot_general(
        patches_hidden, delta_two, contract_rows, preferred_element_type=jnp.float32
    )
    hidden_grad = unpad_tile(padded_gradient(delta_two, flat_two, shape_four), context).reshape(
        -1, channels
    )
    delta_one = (hidden_grad * slope_of(pre_one)).astype(jnp.bfloat16)
    grad_one = lax.dot_general(
        patches_in, delta_one, contract_rows, preferred_element_type=jnp.float32
    )
    input_grad = unpad_tile(padded_gradient(delta_one, flat_one, shape_four), context).astype(
        jnp.bfloat16
    )
    cell_total = face_count * (grid_rows * rows_len) * (8 * cols_len)
    grad_scale = 1.0 / math.sqrt(cell_total)
    grad_one = grad_one * grad_scale
    grad_two = grad_two * grad_scale
    total_one, total_two = lax.psum((grad_one, grad_two), ("face", "tile"))
    kernel_shape = (3, 3, channels, channels)
    return (input_grad[:, None], total_one.reshape(kernel_shape), total_two.reshape(kernel_shape))


def solution(mesh):
    placed = (
        P("face", "tile", None, None, None),
        P("face", "tile", None, None, None),
        P(),
        P(),
        P(),
        P(),
    )
    return jax.shard_map(
        body,
        mesh=mesh,
        in_specs=placed,
        out_specs=(P("face", "tile", None, None, None), P(), P()),
        check_vma=False,
    )
```

profile of v0, /device:TPU:1, one launch (start us, length us, event | category | flops | bytes accessed | tf_op | source)
XLA Modules:
  0.0 648.7 jit_solution(2181856975407413227)
XLA Ops:
  9.1 13.5 %all_gather.6 = bf16[12,2,16,256]{3,2,1,0:T(8,128)(2,1)S(1)} all-gather(bf16[3,2,16,256]{3,2,1,0:T(8,128)(2,1)S(1)} %copy.1680), channel_id=1, replica_groups=mesh['face'=4,'tile'=64] {'face'}, dimensions={0}, use_global_device_ids=true | all-gather | bytes 245760 | tf_op jit(solution)/shard_map/all_gather | solution.py:62
  23.9 3.6 collective-permute-start
  28.9 2.6 collective-permute-done.1
  31.6 2.1 collective-permute-start.2
  33.7 2.5 collective-permute-done.2
  36.6 2.7 collective-permute-done.3
  39.3 1.9 collective-permute-start.4
  41.3 2.8 collective-permute-done.4
  44.2 4.8 collective-permute-start.5
  49.1 2.1 collective-permute-done.5
  51.8 7.7 %collective-permute-start.7 = (bf16[3,10,256]{2,1,0:T(8,128)(2,1)S(1)}, bf16[3,10,256]{2,1,0:T(8,128)(2,1)S(1)}, u32[]{:S(2)}, u32[]{:S(2)}) collective-permute-start(bf16[3,10,256]{2,1,0:T(8,128)(2,1)S(1)} %get-tuple-element.553), channel_id=1, source_target_pairs={{1,0},{2,1},{3,2},{4,3},{5,4},{6,5},{7,6},{8,7},{9,8},{10,9},{11,1... | collective-permute-start | bytes 46088 | tf_op jit(solution)/shard_map/ppermute | solution.py:12
  59.6 2.5 collective-permute-start.6
  64.8 4.1 collective-permute-start.8
  71.0 11.4 %all_gather.7 = bf16[12,2,16,256]{3,2,0,1:T(8,128)(2,1)S(1)} all-gather(bf16[3,2,16,256]{3,2,0,1:T(8,128)(2,1)S(1)} %maximum_maximum_fusion.1), channel_id=1, replica_groups=mesh['face'=4,'tile'=64] {'face'}, dimensions={0}, use_global_device_ids=true | all-gather | bytes 245760 | tf_op jit(solution)/shard_map/all_gather | solution.py:62
  82.8 6.5 %collective-permute-start.10 = (bf16[3,32,256]{2,1,0:T(8,128)(2,1)S(1)}, bf16[3,32,256]{2,1,0:T(8,128)(2,1)S(1)}, u32[]{:S(2)}, u32[]{:S(2)}) collective-permute-start(bf16[3,32,256]{2,1,0:T(8,128)(2,1)S(1)} %pad_maximum_fusion.21), channel_id=1, source_target_pairs={{0,1},{1,0},{2,3},{3,2},{4,5},{5,4},{6,7},{7,6},{8,9},{9,8},{10,11... | collective-permute-start | bytes 147464 | tf_op jit(solution)/shard_map/ppermute | solution.py:16
  90.4 2.9 collective-permute-done.11
  94.5 3.5 collective-permute-done.12
  98.1 2.2 collective-permute-start.13
  101.8 11.6 %collective-permute-start.14 = (bf16[3,32,256]{2,1,0:T(8,128)(2,1)S(1)}, bf16[3,32,256]{2,1,0:T(8,128)(2,1)S(1)}, u32[]{:S(2)}, u32[]{:S(2)}) collective-permute-start(bf16[3,32,256]{2,1,0:T(8,128)(2,1)S(1)} %broadcast_select_fusion.10), channel_id=1, source_target_pairs={{0,16},{1,17},{2,18},{3,19},{4,20},{5,21},{6,22},{7,23},{8,24},{9,... | collective-permute-start | bytes 147464 | tf_op jit(solution)/shard_map/ppermute | solution.py:16
  115.0 9.0 %collective-permute-start.15 = (bf16[3,32,256]{2,1,0:T(8,128)(2,1)S(1)}, bf16[3,32,256]{2,1,0:T(8,128)(2,1)S(1)}, u32[]{:S(2)}, u32[]{:S(2)}) collective-permute-start(bf16[3,32,256]{2,1,0:T(8,128)(2,1)S(1)} %broadcast_select_fusion.12), channel_id=1, source_target_pairs={{0,32},{1,33},{2,34},{3,35},{4,36},{5,37},{6,38},{7,39},{8,40},{9,... | collective-permute-start | bytes 147464 | tf_op jit(solution)/shard_map/ppermute | solution.py:16
  126.2 7.7 %collective-permute-start.17 = (bf16[3,10,256]{2,1,0:T(8,128)(2,1)S(1)}, bf16[3,10,256]{2,1,0:T(8,128)(2,1)S(1)}, u32[]{:S(2)}, u32[]{:S(2)}) collective-permute-start(bf16[3,10,256]{2,1,0:T(8,128)(2,1)S(1)} %copy.1711), channel_id=1, source_target_pairs={{1,0},{2,1},{3,2},{4,3},{5,4},{6,5},{7,6},{8,7},{9,8},{10,9},{11,1... | collective-permute-start | bytes 46088 | tf_op jit(solution)/shard_map/ppermute | solution.py:12
  134.6 1.9 collective-permute-start.16
  139.2 4.2 collective-permute-start.18
  148.5 2.1 fusion
  154.8 3.6 collective-permute-done.20
  158.5 3.4 collective-permute-start.21
  163.8 7.7 %collective-permute-start.22 = (f32[3,10,256]{2,1,0:T(8,128)S(1)}, f32[3,10,256]{2,1,0:T(8,128)S(1)}, u32[]{:S(2)}, u32[]{:S(2)}) collective-permute-start(f32[3,10,256]{2,1,0:T(8,128)S(1)} %get-tuple-element.509), channel_id=1, source_target_pairs={{1,0},{2,1},{3,2},{4,3},{5,4},{6,5},{7,6},{8,7},{9,8},{10,9},{11,1... | collective-permute-start | bytes 92168 | tf_op jit(solution)/shard_map/ppermute | solution.py:12
  171.5 1.9 collective-permute-start.23
  183.5 13.0 %collective-permute-start.26 = (bf16[3,32,256]{2,1,0:T(8,128)(2,1)S(1)}, bf16[3,32,256]{2,1,0:T(8,128)(2,1)S(1)}, u32[]{:S(2)}, u32[]{:S(2)}) collective-permute-start(bf16[3,32,256]{2,1,0:T(8,128)(2,1)S(1)} %get-tuple-element.476), channel_id=1, source_target_pairs={{0,4},{1,5},{2,6},{3,7},{4,0},{5,1},{6,2},{7,3},{8,12},{9,13},{10,... | collective-permute-start | bytes 147464 | tf_op jit(solution)/shard_map/ppermute | solution.py:16
  198.1 8.1 %collective-permute-start.27 = (bf16[3,32,256]{2,1,0:T(8,128)(2,1)S(1)}, bf16[3,32,256]{2,1,0:T(8,128)(2,1)S(1)}, u32[]{:S(2)}, u32[]{:S(2)}) collective-permute-start(bf16[3,32,256]{2,1,0:T(8,128)(2,1)S(1)} %fusion.36), channel_id=1, source_target_pairs={{0,8},{1,9},{2,10},{3,11},{4,12},{5,13},{6,14},{7,15},{8,0},{9,1},... | collective-permute-start | bytes 147464 | tf_op jit(solution)/shard_map/ppermute | solution.py:16
  208.5 10.2 %collective-permute-start.28 = (bf16[3,32,256]{2,1,0:T(8,128)(2,1)S(1)}, bf16[3,32,256]{2,1,0:T(8,128)(2,1)S(1)}, u32[]{:S(2)}, u32[]{:S(2)}) collective-permute-start(bf16[3,32,256]{2,1,0:T(8,128)(2,1)S(1)} %get-tuple-element.474), channel_id=1, source_target_pairs={{0,16},{1,17},{2,18},{3,19},{4,20},{5,21},{6,22},{7,23},{8,24},{9,... | collective-permute-start | bytes 147464 | tf_op jit(solution)/shard_map/ppermute | solution.py:16
  220.5 11.2 %collective-permute-start.29 = (bf16[3,32,256]{2,1,0:T(8,128)(2,1)S(1)}, bf16[3,32,256]{2,1,0:T(8,128)(2,1)S(1)}, u32[]{:S(2)}, u32[]{:S(2)}) collective-permute-start(bf16[3,32,256]{2,1,0:T(8,128)(2,1)S(1)} %fusion.37), channel_id=1, source_target_pairs={{0,32},{1,33},{2,34},{3,35},{4,36},{5,37},{6,38},{7,39},{8,40},{9,... | collective-permute-start | bytes 147464 | tf_op jit(solution)/shard_map/ppermute | solution.py:16
  236.0 24.3 %reduce-scatter.3.cloned.1.call-done = bf16[3,2,16,256]{3,2,1,0:T(8,128)(2,1)} async-done(((bf16[12,2,16,256]{3,2,1,0:T(8,128)(2,1)}), bf16[3,2,16,256]{3,2,1,0:T(8,128)(2,1)}) %reduce-scatter.3.cloned.1.call-update) | async-done | bytes 49168 | tf_op jit(solution)/shard_map/reduce_scatter | solution.py:156
  264.4 2.1 fusion.1
  270.7 3.3 collective-permute-done.30
  274.1 3.1 collective-permute-start.31
  278.5 6.7 %collective-permute-start.32 = (f32[3,10,256]{2,1,0:T(8,128)S(1)}, f32[3,10,256]{2,1,0:T(8,128)S(1)}, u32[]{:S(2)}, u32[]{:S(2)}) collective-permute-start(f32[3,10,256]{2,1,0:T(8,128)S(1)} %get-tuple-element.504), channel_id=1, source_target_pairs={{1,0},{2,1},{3,2},{4,3},{5,4},{6,5},{7,6},{8,7},{9,8},{10,9},{11,1... | collective-permute-start | bytes 92168 | tf_op jit(solution)/shard_map/ppermute | solution.py:12
  285.3 3.0 collective-permute-start.33
  293.8 1.9 collective-permute-start.35
  298.0 3.1 collective-permute-start.36
  302.6 6.2 collective-permute-start.37
  311.1 8.2 %collective-permute-start.38 = (bf16[3,32,256]{2,1,0:T(8,128)(2,1)S(1)}, bf16[3,32,256]{2,1,0:T(8,128)(2,1)S(1)}, u32[]{:S(2)}, u32[]{:S(2)}) collective-permute-start(bf16[3,32,256]{2,1,0:T(8,128)(2,1)S(1)} %get-tuple-element.470), channel_id=1, source_target_pairs={{0,16},{1,17},{2,18},{3,19},{4,20},{5,21},{6,22},{7,23},{8,24},{9,... | collective-permute-start | bytes 147464 | tf_op jit(solution)/shard_map/ppermute | solution.py:16
  321.1 11.0 %collective-permute-start.39 = (bf16[3,32,256]{2,1,0:T(8,128)(2,1)S(1)}, bf16[3,32,256]{2,1,0:T(8,128)(2,1)S(1)}, u32[]{:S(2)}, u32[]{:S(2)}) collective-permute-start(bf16[3,32,256]{2,1,0:T(8,128)(2,1)S(1)} %fusion.40), channel_id=1, source_target_pairs={{0,32},{1,33},{2,34},{3,35},{4,36},{5,37},{6,38},{7,39},{8,40},{9,... | collective-permute-start | bytes 147464 | tf_op jit(solution)/shard_map/ppermute | solution.py:16
  336.4 2.0 convolution_multiply_fusion
  338.4 1.9 convolution_multiply_fusion.1
  340.4 20.4 %reduce-scatter.5.cloned.1.call-done = bf16[3,2,16,256]{3,2,1,0:T(8,128)(2,1)} async-done(((bf16[12,2,16,256]{3,2,1,0:T(8,128)(2,1)}), bf16[3,2,16,256]{3,2,1,0:T(8,128)(2,1)}) %reduce-scatter.5.cloned.1.call-update) | async-done | bytes 49168 | tf_op jit(solution)/shard_map/reduce_scatter | solution.py:156
  362.7 274.7 %all-reduce.15.cloned.1.call-done = (f32[3,3,256,256]{3,2,1,0:T(8,128)}, f32[3,3,256,256]{3,2,1,0:T(8,128)}) async-done(((f32[3,3,256,256]{3,2,1,0:T(8,128)}, f32[3,3,256,256]{3,2,1,0:T(8,128)}), (f32[3,3,256,256]{3,2,1,0:T(8,128)}, f32[3,3,256,256]{3,2,1,0:T(8,128)})) %all-reduce.15.cloned.1.call-update) | async-done | bytes 4718608 | tf_op jit(solution)/shard_map/psum | solution.py:267
  637.4 3.4 copy.1916
  (355 shorter events, 82.4 us)
Async XLA Ops:
  7.2 253.1 %reduce-scatter.3.cloned.1.call-start = ((), (), s32[]{:S(2)}) async-start(), calls=%async_computation.2 | async-start | bytes 245760 | tf_op jit(solution)/shard_map/reduce_scatter | solution.py:156
  23.9 4.5 collective-permute-start
  28.2 97.2 %copy-start.9 = (pred[3,32]{1,0:T(4,128)(4,1)}, pred[3,32]{1,0:T(4,128)(4,1)S(1)}, u32[]{:S(2)}) copy-start(pred[3,32]{1,0:T(4,128)(4,1)S(1)} %get-tuple-element.478) | copy-start | bytes 292
  28.5 3.0 collective-permute-start.1
  31.6 4.5 collective-permute-start.2
  36.2 3.0 collective-permute-start.3
  39.3 4.8 collective-permute-start.4
  41.2 84.7 %copy-start.10 = (pred[3]{0:T(512)(128)(4,1)}, pred[3]{0:T(512)(128)(4,1)S(1)}, u32[]{:S(2)}) copy-start(pred[3]{0:T(512)(128)(4,1)S(1)} %get-tuple-element.608) | copy-start | bytes 13
  41.2 84.7 %copy-start.11 = (pred[3]{0:T(512)(128)(4,1)}, pred[3]{0:T(512)(128)(4,1)S(1)}, u32[]{:S(2)}) copy-start(pred[3]{0:T(512)(128)(4,1)S(1)} %get-tuple-element.606) | copy-start | bytes 13
  41.3 84.7 %copy-start.12 = (pred[3]{0:T(512)(128)(4,1)}, pred[3]{0:T(512)(128)(4,1)S(1)}, u32[]{:S(2)}) copy-start(pred[3]{0:T(512)(128)(4,1)S(1)} %get-tuple-element.605) | copy-start | bytes 13
  41.3 84.7 %copy-start.13 = (pred[3]{0:T(512)(128)(4,1)}, pred[3]{0:T(512)(128)(4,1)S(1)}, u32[]{:S(2)}) copy-start(pred[3]{0:T(512)(128)(4,1)S(1)} %get-tuple-element.607) | copy-start | bytes 13
  44.2 6.9 %collective-permute-start.5 = (bf16[3,32,256]{2,1,0:T(8,128)(2,1)S(1)}, bf16[3,32,256]{2,1,0:T(8,128)(2,1)S(1)}, u32[]{:S(2)}, u32[]{:S(2)}) collective-permute-start(bf16[3,32,256]{2,1,0:T(8,128)(2,1)S(1)} %broadcast_select_fusion.13), channel_id=1, source_target_pairs={{0,32},{1,33},{2,34},{3,35},{4,36},{5,37},{6,38},{7,39},{8,40},{9,... | collective-permute-start | bytes 147464 | tf_op jit(solution)/shard_map/ppermute | solution.py:16
  51.8 10.2 %collective-permute-start.7 = (bf16[3,10,256]{2,1,0:T(8,128)(2,1)S(1)}, bf16[3,10,256]{2,1,0:T(8,128)(2,1)S(1)}, u32[]{:S(2)}, u32[]{:S(2)}) collective-permute-start(bf16[3,10,256]{2,1,0:T(8,128)(2,1)S(1)} %get-tuple-element.553), channel_id=1, source_target_pairs={{1,0},{2,1},{3,2},{4,3},{5,4},{6,5},{7,6},{8,7},{9,8},{10,9},{11,1... | collective-permute-start | bytes 46088 | tf_op jit(solution)/shard_map/ppermute | solution.py:12
  59.6 3.4 collective-permute-start.6
  63.4 5.6 collective-permute-start.9
  64.8 5.0 collective-permute-start.8
  82.8 7.4 %collective-permute-start.10 = (bf16[3,32,256]{2,1,0:T(8,128)(2,1)S(1)}, bf16[3,32,256]{2,1,0:T(8,128)(2,1)S(1)}, u32[]{:S(2)}, u32[]{:S(2)}) collective-permute-start(bf16[3,32,256]{2,1,0:T(8,128)(2,1)S(1)} %pad_maximum_fusion.21), channel_id=1, source_target_pairs={{0,1},{1,0},{2,3},{3,2},{4,5},{5,4},{6,7},{7,6},{8,9},{9,8},{10,11... | collective-permute-start | bytes 147464 | tf_op jit(solution)/shard_map/ppermute | solution.py:16
  90.3 3.0 collective-permute-start.11
  93.4 4.5 collective-permute-start.12
  98.1 3.6 collective-permute-start.13
  101.8 13.1 %collective-permute-start.14 = (bf16[3,32,256]{2,1,0:T(8,128)(2,1)S(1)}, bf16[3,32,256]{2,1,0:T(8,128)(2,1)S(1)}, u32[]{:S(2)}, u32[]{:S(2)}) collective-permute-start(bf16[3,32,256]{2,1,0:T(8,128)(2,1)S(1)} %broadcast_select_fusion.10), channel_id=1, source_target_pairs={{0,16},{1,17},{2,18},{3,19},{4,20},{5,21},{6,22},{7,23},{8,24},{9,... | collective-permute-start | bytes 147464 | tf_op jit(solution)/shard_map/ppermute | solution.py:16
  115.0 10.5 %collective-permute-start.15 = (bf16[3,32,256]{2,1,0:T(8,128)(2,1)S(1)}, bf16[3,32,256]{2,1,0:T(8,128)(2,1)S(1)}, u32[]{:S(2)}, u32[]{:S(2)}) collective-permute-start(bf16[3,32,256]{2,1,0:T(8,128)(2,1)S(1)} %broadcast_select_fusion.12), channel_id=1, source_target_pairs={{0,32},{1,33},{2,34},{3,35},{4,36},{5,37},{6,38},{7,39},{8,40},{9,... | collective-permute-start | bytes 147464 | tf_op jit(solution)/shard_map/ppermute | solution.py:16
  126.2 10.3 %collective-permute-start.17 = (bf16[3,10,256]{2,1,0:T(8,128)(2,1)S(1)}, bf16[3,10,256]{2,1,0:T(8,128)(2,1)S(1)}, u32[]{:S(2)}, u32[]{:S(2)}) collective-permute-start(bf16[3,10,256]{2,1,0:T(8,128)(2,1)S(1)} %copy.1711), channel_id=1, source_target_pairs={{1,0},{2,1},{3,2},{4,3},{5,4},{6,5},{7,6},{8,7},{9,8},{10,9},{11,1... | collective-permute-start | bytes 46088 | tf_op jit(solution)/shard_map/ppermute | solution.py:12
  134.6 3.1 collective-permute-start.16
  137.9 5.7 collective-permute-start.19
  139.2 4.9 collective-permute-start.18
  153.4 5.0 collective-permute-start.20
  158.5 4.4 collective-permute-start.21
  163.8 9.7 %collective-permute-start.22 = (f32[3,10,256]{2,1,0:T(8,128)S(1)}, f32[3,10,256]{2,1,0:T(8,128)S(1)}, u32[]{:S(2)}, u32[]{:S(2)}) collective-permute-start(f32[3,10,256]{2,1,0:T(8,128)S(1)} %get-tuple-element.509), channel_id=1, source_target_pairs={{1,0},{2,1},{3,2},{4,3},{5,4},{6,5},{7,6},{8,7},{9,8},{10,9},{11,1... | collective-permute-start | bytes 92168 | tf_op jit(solution)/shard_map/ppermute | solution.py:12
  171.5 3.5 collective-permute-start.23
  177.5 2.1 collective-permute-start.24
  179.7 3.0 collective-permute-start.25
  183.5 14.5 %collective-permute-start.26 = (bf16[3,32,256]{2,1,0:T(8,128)(2,1)S(1)}, bf16[3,32,256]{2,1,0:T(8,128)(2,1)S(1)}, u32[]{:S(2)}, u32[]{:S(2)}) collective-permute-start(bf16[3,32,256]{2,1,0:T(8,128)(2,1)S(1)} %get-tuple-element.476), channel_id=1, source_target_pairs={{0,4},{1,5},{2,6},{3,7},{4,0},{5,1},{6,2},{7,3},{8,12},{9,13},{10,... | collective-permute-start | bytes 147464 | tf_op jit(solution)/shard_map/ppermute | solution.py:16
  198.1 9.6 %collective-permute-start.27 = (bf16[3,32,256]{2,1,0:T(8,128)(2,1)S(1)}, bf16[3,32,256]{2,1,0:T(8,128)(2,1)S(1)}, u32[]{:S(2)}, u32[]{:S(2)}) collective-permute-start(bf16[3,32,256]{2,1,0:T(8,128)(2,1)S(1)} %fusion.36), channel_id=1, source_target_pairs={{0,8},{1,9},{2,10},{3,11},{4,12},{5,13},{6,14},{7,15},{8,0},{9,1},... | collective-permute-start | bytes 147464 | tf_op jit(solution)/shard_map/ppermute | solution.py:16
  208.5 11.9 %collective-permute-start.28 = (bf16[3,32,256]{2,1,0:T(8,128)(2,1)S(1)}, bf16[3,32,256]{2,1,0:T(8,128)(2,1)S(1)}, u32[]{:S(2)}, u32[]{:S(2)}) collective-permute-start(bf16[3,32,256]{2,1,0:T(8,128)(2,1)S(1)} %get-tuple-element.474), channel_id=1, source_target_pairs={{0,16},{1,17},{2,18},{3,19},{4,20},{5,21},{6,22},{7,23},{8,24},{9,... | collective-permute-start | bytes 147464 | tf_op jit(solution)/shard_map/ppermute | solution.py:16
  220.5 12.7 %collective-permute-start.29 = (bf16[3,32,256]{2,1,0:T(8,128)(2,1)S(1)}, bf16[3,32,256]{2,1,0:T(8,128)(2,1)S(1)}, u32[]{:S(2)}, u32[]{:S(2)}) collective-permute-start(bf16[3,32,256]{2,1,0:T(8,128)(2,1)S(1)} %fusion.37), channel_id=1, source_target_pairs={{0,32},{1,33},{2,34},{3,35},{4,36},{5,37},{6,38},{7,39},{8,40},{9,... | collective-permute-start | bytes 147464 | tf_op jit(solution)/shard_map/ppermute | solution.py:16
  235.9 124.8 %reduce-scatter.5.cloned.1.call-start = ((), (), s32[]{:S(2)}) async-start(), calls=%async_computation.3 | async-start | bytes 245760 | tf_op jit(solution)/shard_map/reduce_scatter | solution.py:156
  269.3 4.7 collective-permute-start.30
  274.1 4.2 collective-permute-start.31
  278.5 9.8 %collective-permute-start.32 = (f32[3,10,256]{2,1,0:T(8,128)S(1)}, f32[3,10,256]{2,1,0:T(8,128)S(1)}, u32[]{:S(2)}, u32[]{:S(2)}) collective-permute-start(f32[3,10,256]{2,1,0:T(8,128)S(1)} %get-tuple-element.504), channel_id=1, source_target_pairs={{1,0},{2,1},{3,2},{4,3},{5,4},{6,5},{7,6},{8,7},{9,8},{10,9},{11,1... | collective-permute-start | bytes 92168 | tf_op jit(solution)/shard_map/ppermute | solution.py:12
  285.3 4.6 collective-permute-start.33
  292.4 1.3 collective-permute-start.34
  293.8 3.4 collective-permute-start.35
  298.0 4.5 collective-permute-start.36
  302.6 7.7 %collective-permute-start.37 = (bf16[3,32,256]{2,1,0:T(8,128)(2,1)S(1)}, bf16[3,32,256]{2,1,0:T(8,128)(2,1)S(1)}, u32[]{:S(2)}, u32[]{:S(2)}) collective-permute-start(bf16[3,32,256]{2,1,0:T(8,128)(2,1)S(1)} %fusion.39), channel_id=1, source_target_pairs={{0,8},{1,9},{2,10},{3,11},{4,12},{5,13},{6,14},{7,15},{8,0},{9,1},... | collective-permute-start | bytes 147464 | tf_op jit(solution)/shard_map/ppermute | solution.py:16
  311.1 9.9 %collective-permute-start.38 = (bf16[3,32,256]{2,1,0:T(8,128)(2,1)S(1)}, bf16[3,32,256]{2,1,0:T(8,128)(2,1)S(1)}, u32[]{:S(2)}, u32[]{:S(2)}) collective-permute-start(bf16[3,32,256]{2,1,0:T(8,128)(2,1)S(1)} %get-tuple-element.470), channel_id=1, source_target_pairs={{0,16},{1,17},{2,18},{3,19},{4,20},{5,21},{6,22},{7,23},{8,24},{9,... | collective-permute-start | bytes 147464 | tf_op jit(solution)/shard_map/ppermute | solution.py:16
  321.1 12.5 %collective-permute-start.39 = (bf16[3,32,256]{2,1,0:T(8,128)(2,1)S(1)}, bf16[3,32,256]{2,1,0:T(8,128)(2,1)S(1)}, u32[]{:S(2)}, u32[]{:S(2)}) collective-permute-start(bf16[3,32,256]{2,1,0:T(8,128)(2,1)S(1)} %fusion.40), channel_id=1, source_target_pairs={{0,32},{1,33},{2,34},{3,35},{4,36},{5,37},{6,38},{7,39},{8,40},{9,... | collective-permute-start | bytes 147464 | tf_op jit(solution)/shard_map/ppermute | solution.py:16
  336.4 301.1 %all-reduce.15.cloned.1.call-start = ((), (), s32[]{:S(2)}) async-start(), calls=%async_computation.4 | async-start | bytes 9437184 | tf_op jit(solution)/shard_map/psum | solution.py:267
  (16 other events, 463.8 us)
Sparse Core Ops, SparseCore 0:
  236.1 24.2 reduce-scatter.2
  336.5 24.2 reduce-scatter.4
  366.9 270.4 all-reduce.14
where the time goes:
time: 651 us; the launch traced here: 649 us
  waiting for transfers between devices  372 us (57%)
  starting transfers between devices  179 us (27%)
  other arithmetic  33.6 us (5%)
  blocking collectives  25 us (4%)
  local copies, waits for them, and re-layouts  16.5 us (3%)
  between operations  15.8 us (2%)
  matrix products  7.19 us (1%)
    psum x1, waiting for transfers between devices, body(): total_one, total_two = lax.psum((grad_one, grad_two), ('face', 'tile'))  275 us
    ppermute x24, starting transfers between devices, swapped(): lax.ppermute(x, axis, [(i, i ^ 1 << distance) for i in range(lax.axis_siz...  119 us
    ppermute x16, starting transfers between devices, shifted(): return lax.ppermute(x, axis, pairs)  59.2 us
    reduce_scatter x2, waiting for transfers between devices, unpad_tile(): lax.psum_scatter(spread.astype(jnp.bfloat16), 'face', scatter_dimension=0...  44.7 us
    ppermute x24, waiting for transfers between devices, swapped(): lax.ppermute(x, axis, [(i, i ^ 1 << distance) for i in range(lax.axis_siz...  40.6 us
    all_gather x2, blocking collectives, pad_tile(): everyone = lax.all_gather(rim_strips, 'face', axis=0, tiled=True)  25 us
  transfers between devices with their start and end apart: 43, of which 35 were waited for; matrix products, arithmetic and copies ran while one was open for 2% of the time, Pallas kernels for 0%

commit v1 on v0

v1 whole, which is shorter than its diff:
```python
import math

import jax
import jax.numpy as jnp
import numpy as np
from jax import lax
from jax.sharding import Mesh, PartitionSpec as P

AXES = ("face", "zh", "x", "y", "core")
TILE = ("zh", "x", "y", "core")
F32 = jnp.float32
BF16 = jnp.bfloat16
MIRRORS = (0, 7, 56, 63)


def swap_pairs(pairs):
    return [(a, b) for a, b in pairs] + [(b, a) for a, b in pairs]


ODD_COLS = swap_pairs([(r * 8 + c, r * 8 + c + 1) for r in range(8) for c in (1, 3, 5)])
EVEN_ROWS = swap_pairs([(r * 8 + c, r * 8 + 8 + c) for r in (0, 2, 4, 6) for c in range(8)])
ODD_ROWS = swap_pairs([(r * 8 + c, r * 8 + 8 + c) for r in (1, 3, 5) for c in range(8)])
SEAM_GROUPS = [
    [f * 64 + (t ^ m) for f in range(4) for m in MIRRORS]
    for t in range(64)
    if t == min(t ^ m for m in MIRRORS)
]


def slope_of(pre_act):
    logistic = jax.nn.sigmoid(pre_act)
    return logistic * (1.0 + pre_act * (1.0 - logistic))


def halo(v, d, row, col):
    even = col % 2 == 0
    left, right = v[:, :, :d], v[:, :, -d:]
    s1 = lax.ppermute(jnp.where(even, right, left), "core", [(0, 1), (1, 0)])
    s2 = lax.ppermute(jnp.where(even, left, right), TILE, ODD_COLS)
    wide = jnp.concatenate([jnp.where(even, s2, s1), v, jnp.where(even, s1, s2)], axis=2)
    even = row % 2 == 0
    up, down = wide[:, :d], wide[:, -d:]
    s1 = lax.ppermute(jnp.where(even, down, up), TILE, EVEN_ROWS)
    s2 = lax.ppermute(jnp.where(even, up, down), TILE, ODD_ROWS)
    return jnp.concatenate([jnp.where(even, s2, s1), wide, jnp.where(even, s1, s2)], axis=1)


def seam_swap(row_strip, col_strip, select, mirror):
    length, channels = row_strip.shape[1:]
    mine = jnp.stack([row_strip, col_strip], axis=1)
    back = mine[:, :, ::-1]
    rel = jnp.arange(4, dtype=jnp.int32) ^ mirror
    reverse = jnp.stack([rel % 2, rel // 2], axis=1) == 1
    send = jnp.where(reverse[:, None, :, None, None], back[None], mine[None])
    send = jnp.broadcast_to(send[None], (4,) + send.shape).reshape(16, 6 * length, channels)
    got = lax.all_to_all(send, AXES, 0, 0, axis_index_groups=SEAM_GROUPS)
    got = got.reshape(96, length * channels)
    out = jnp.dot(select.astype(BF16), got, preferred_element_type=F32)
    return out.reshape(3, 2, length, channels)


def patches_of(padded, length):
    views = [padded[:, a : a + length, b : b + length] for a in range(3) for b in range(3)]
    return jnp.concatenate(views, axis=-1).reshape(-1, 9 * padded.shape[-1])


def reduce_grads(grad_one, grad_two, core):
    both = jnp.stack([grad_one, grad_two])
    low, high = both[:, :1152], both[:, 1152:]
    got = lax.ppermute(jnp.where(core == 0, high, low).astype(BF16), "core", [(0, 1), (1, 0)])
    part = jnp.where(core == 0, low, high) + got.astype(F32)
    part = part.astype(BF16).reshape(2, 16, 72, 256).transpose(1, 0, 2, 3)
    part = lax.all_to_all(part, ("x", "y"), 0, 0).astype(F32).sum(0)
    part = part.reshape(8, 18, 256).astype(BF16)
    part = lax.all_to_all(part, ("face", "zh"), 0, 0).astype(F32).sum(0).astype(BF16)
    part = lax.all_to_all(jnp.broadcast_to(part, (8, 18, 256)), ("face", "zh"), 0, 0)
    part = part.reshape(2, 72, 256)
    part = lax.all_to_all(jnp.broadcast_to(part, (16, 2, 72, 256)), ("x", "y"), 0, 0)
    part = part.transpose(1, 0, 2, 3).reshape(2, 1152, 256)
    got = lax.ppermute(part, "core", [(0, 1), (1, 0)])
    low, high = jnp.where(core == 0, part, got), jnp.where(core == 0, got, part)
    return jnp.concatenate([low, high], axis=1).astype(F32)


def body(inputs, cotangent, kernel_one, kernel_two, neighbour, seam_codes):
    x = inputs[:, 0]
    channels = x.shape[-1]
    face_group = lax.axis_index("face")
    core = lax.axis_index("core")
    row = lax.axis_index("zh") * 4 + lax.axis_index("x")
    col = lax.axis_index("y") * 2 + core
    mirror = col // 4 + 2 * (row // 4)
    on_row = (row == 0) | (row == 7)
    on_col = (col == 0) | (col == 7)
    on_edge = jnp.stack([on_row, on_col])
    bottom, right = row // 4, col // 4
    own_side = jnp.stack([bottom, 2 + right])

    first = face_group * 3
    opposite, reverse = 1 - seam_codes % 2, seam_codes // 2
    types = jnp.arange(4) // 2
    rel_of = jnp.where(types == 0, 2 * opposite + reverse, 2 * reverse + opposite)
    slot_mirror = jnp.arange(4, dtype=jnp.int32)
    slot_type = jnp.arange(2, dtype=jnp.int32)

    def on_side(table, side):
        return jnp.sum(jnp.where(side[..., None] == jnp.arange(4), table, 0), axis=-1)

    own_next = lax.dynamic_slice_in_dim(neighbour, first, 3, 0)
    own_rel = lax.dynamic_slice_in_dim(rel_of, first, 3, 0)
    next_face = on_side(own_next[:, None, :], own_side[None])
    next_rel = on_side(own_rel[:, None, :], own_side[None])
    faces = jnp.arange(12, dtype=jnp.int32).reshape(4, 1, 3, 1)
    gather_sel = (
        (next_face[:, :, None, None, None, None] == faces)
        & ((next_rel ^ mirror)[:, :, None, None, None, None] == slot_mirror[:, None, None])
        & (slot_type[:, None, None, None, None] == slot_type)
        & on_edge[:, None, None, None, None]
    ).reshape(6, 96)
    rel = slot_mirror ^ mirror
    from_side = jnp.stack([bottom ^ (rel // 2), 2 + (right ^ (rel % 2))], axis=1)
    from_side = from_side[None, :, None, :]
    slot_next = on_side(neighbour.reshape(4, 1, 3, 1, 4), from_side)
    slot_rel = on_side(rel_of.reshape(4, 1, 3, 1, 4), from_side)
    valid = slot_rel == rel[:, None, None]
    own_faces = (first + jnp.arange(3, dtype=jnp.int32))[:, None, None, None, None, None]
    add_sel = (
        (slot_next == own_faces)
        & valid
        & (slot_type[:, None, None, None, None] == slot_type)
        & on_edge[:, None, None, None, None]
    ).reshape(6, 96)

    def inside(depth):
        span = jnp.arange(8 + 2 * depth, dtype=jnp.int32) - depth
        rows, cols = row * 8 + span, col * 8 + span
        rows_in, cols_in = (rows >= 0) & (rows < 64), (cols >= 0) & (cols < 64)
        return rows_in, cols_in

    def edge_row(field, first_at, last_at):
        return jnp.where(bottom == 1, field[:, last_at], field[:, first_at])

    def edge_col(field, first_at, last_at):
        return jnp.where(right == 1, field[:, :, last_at], field[:, :, first_at])

    def fill(field, strips, depth):
        span = jnp.arange(field.shape[1])
        at_row = jnp.where(bottom == 1, 8 + depth, depth - 1)
        at_col = jnp.where(right == 1, 8 + depth, depth - 1)
        is_row = ((span == at_row) & on_row)[None, :, None, None]
        is_col = ((span == at_col) & on_col)[None, None, :, None]
        field = jnp.where(is_row, strips[:, 0][:, None], field)
        return jnp.where(is_col, strips[:, 1][:, :, None], field)

    def add_edges(field, strips, depth):
        span = jnp.arange(field.shape[1])
        at_row = jnp.where(bottom == 1, 7 + depth, depth)
        at_col = jnp.where(right == 1, 7 + depth, depth)
        is_row = (span == at_row)[None, :, None, None]
        is_col = (span == at_col)[None, None, :, None]
        field = field + jnp.where(is_row, strips[:, 0][:, None], 0.0)
        return field + jnp.where(is_col, strips[:, 1][:, :, None], 0.0)

    flat_one = kernel_one.reshape(9 * channels, channels)
    flat_two = kernel_two.reshape(9 * channels, channels)
    back_one = kernel_one[::-1, ::-1].transpose(0, 1, 3, 2).reshape(9 * channels, channels)
    back_two = kernel_two[::-1, ::-1].transpose(0, 1, 3, 2).reshape(9 * channels, channels)
    rows_in, cols_in = inside(1)
    mask = (rows_in[:, None] & cols_in)[None, :, :, None]

    near = halo(x, 2, row, col)
    strips = seam_swap(edge_row(near, 2, 9), edge_col(near, 2, 9), gather_sel, mirror)
    padded_in = fill(near, strips.astype(BF16), 2)
    patches_in = patches_of(padded_in, 10)
    pre_one = jnp.dot(patches_in, flat_one, preferred_element_type=F32)
    pre_one = pre_one.reshape(3, 10, 10, channels)
    hidden = jnp.where(mask, jax.nn.silu(pre_one), 0.0).astype(BF16)
    strips = seam_swap(edge_row(hidden, 1, 8), edge_col(hidden, 1, 8), gather_sel, mirror)
    padded_hidden = fill(hidden, strips.astype(BF16), 1)
    patches_hidden = patches_of(padded_hidden, 8)
    pre_two = jnp.dot(patches_hidden, flat_two, preferred_element_type=F32)
    delta_two = cotangent[:, 0].reshape(-1, channels).astype(F32) * slope_of(pre_two)
    delta_two = delta_two.astype(BF16)
    contract_rows = (((0,), (0,)), ((), ()))
    grad_two = lax.dot_general(
        patches_hidden, delta_two, contract_rows, preferred_element_type=F32
    )
    near = halo(delta_two.reshape(3, 8, 8, channels), 2, row, col)
    back = jnp.dot(patches_of(near, 10), back_two, preferred_element_type=F32)
    back = back.astype(BF16).reshape(3, 10, 10, channels)
    row_strip = jnp.where(cols_in[:, None], edge_row(back, 0, 9), 0)
    col_strip = jnp.where(rows_in[:, None], edge_col(back, 0, 9), 0)
    strips = seam_swap(row_strip, col_strip, add_sel, mirror)
    hidden_grad = add_edges(back.astype(F32), strips, 1)
    delta_one = jnp.where(mask, hidden_grad * slope_of(pre_one), 0.0).astype(BF16)
    own = patches_in.reshape(3, 10, 10, 9 * channels)[:, 1:9, 1:9].reshape(192, 9 * channels)
    grad_one = lax.dot_general(
        own,
        delta_one[:, 1:9, 1:9].reshape(192, channels),
        contract_rows,
        preferred_element_type=F32,
    )
    wide = jnp.pad(delta_one, ((0, 0), (1, 1), (1, 1), (0, 0)))
    back = jnp.dot(patches_of(wide, 10), back_one, preferred_element_type=F32)
    back = back.astype(BF16).reshape(3, 10, 10, channels)
    strips = seam_swap(
        edge_row(back, 0, 9)[:, 1:9], edge_col(back, 0, 9)[:, 1:9], add_sel, mirror
    )
    input_grad = add_edges(back[:, 1:9, 1:9].astype(F32), strips, 0).astype(BF16)

    scale = 1.0 / math.sqrt(12 * 64 * 64)
    total = reduce_grads(grad_one * scale, grad_two * scale, core)
    shape = (3, 3, channels, channels)
    return (input_grad[:, None], total[0].reshape(shape), total[1].reshape(shape))


def solution(mesh):
    fine = Mesh(np.asarray(mesh.devices).reshape(4, 2, 4, 4, 2), AXES)
    field = P("face", TILE, None, None, None)
    return jax.shard_map(
        body,
        mesh=fine,
        in_specs=(field, field, P(), P(), P(), P()),
        out_specs=(field, P(), P()),
        check_vma=False,
    )
```

time: 651 us -> 249 us (0.38)
  waiting for transfers between devices: 372 us -> 105 us
  starting transfers between devices: 179 us -> 77.8 us
  blocking collectives: 25 us -> 0 us
  local copies, waits for them, and re-layouts: 16.5 us -> 36.8 us
  other arithmetic: 33.6 us -> 14.1 us
  between operations: 15.8 us -> 1.78 us
    psum x1 -> x0, waiting for transfers between devices: 275 us -> none  [body(): total_one, total_two = lax.psum((grad_one, grad_two), ('face', 'tile'))]
    ppermute x40 -> x10, starting transfers between devices: 178 us -> 13.4 us  [the longest x2 6.52 us: halo(): s2 = lax.ppermute(jnp.where(even, left, right), TILE, ODD_COLS)]
    all_to_all x0 -> x8, waiting for transfers between devices: none -> 98.6 us  [the longest x4 69.4 us: seam_swap(): got = lax.all_to_all(send, AXES, 0, 0, axis_index_groups=SEAM_GROUPS)]
    all_to_all x0 -> x8, starting transfers between devices: none -> 64.4 us  [the longest x4 34.3 us: seam_swap(): got = lax.all_to_all(send, AXES, 0, 0, axis_index_groups=SEAM_GROUPS)]
    ppermute x40 -> x10, waiting for transfers between devices: 52.7 us -> 6.22 us  [the longest x1 2.83 us: reduce_grads(): lax.ppermute(jnp.where(core == 0, high, low).astype(BF16), 'core', [(0, 1...]
    reduce_scatter x2 -> x0, waiting for transfers between devices: 44.7 us -> none  [unpad_tile(): lax.psum_scatter(spread.astype(jnp.bfloat16), 'face', scatter_dimension=0...]
    all_gather x2 -> x0, blocking collectives: 25 us -> none  [pad_tile(): everyone = lax.all_gather(rim_strips, 'face', axis=0, tiled=True)]
    scatter-add x22 -> x0, other arithmetic: 14 us -> none  [the longest x16 12.3 us: padded_gradient(): pad_grad = pad_grad.at[:, shift_row:shift_row + rows_len, shift_col:shift...]
  transfers between devices with their start and end apart: 43 -> 18, of which waited for: 35 -> 11; matrix products, arithmetic and copies ran while one was open for 2% -> 11% of each run, Pallas kernels for 0% -> 0%
where the time goes in v1:
time: 249 us; the launch traced here: 247 us
  waiting for transfers between devices  105 us (42%)
  starting transfers between devices  77.8 us (31%)
  local copies, waits for them, and re-layouts  36.8 us (15%)
  other arithmetic  14.1 us (6%)
  matrix products  11.8 us (5%)
    all_to_all x4, waiting for transfers between devices, seam_swap(): got = lax.all_to_all(send, AXES, 0, 0, axis_index_groups=SEAM_GROUPS)  69.4 us
    all_to_all x4, starting transfers between devices, seam_swap(): got = lax.all_to_all(send, AXES, 0, 0, axis_index_groups=SEAM_GROUPS)  34.3 us
    all_to_all x1, starting transfers between devices, reduce_grads(): part = lax.all_to_all(part, ('x', 'y'), 0, 0).astype(F32).sum(0)  17.1 us
    unnamed x58, local copies, waits for them, and re-layouts  11.2 us
    all_to_all x1, waiting for transfers between devices, reduce_grads(): part = lax.all_to_all(part, ('x', 'y'), 0, 0).astype(F32).sum(0)  10.8 us
    all_to_all x1, waiting for transfers between devices, reduce_grads(): lax.all_to_all(jnp.broadcast_to(part, (16, 2, 72, 256)), ('x', 'y'), 0, 0)  10.7 us
    ppermute x2, starting transfers between devices, halo(): s2 = lax.ppermute(jnp.where(even, left, right), TILE, ODD_COLS)  6.52 us
    all_to_all x1, waiting for transfers between devices, reduce_grads(): lax.all_to_all(part, ('face', 'zh'), 0, 0).astype(F32).sum(0).astype(BF16)  5.15 us
  transfers between devices with their start and end apart: 18, of which 11 were waited for; matrix products, arithmetic and copies ran while one was open for 11% of the time, Pallas kernels for 0%

profile of v1, /device:TPU:1, one launch (start us, length us, event | category | flops | bytes accessed | tf_op | source)
XLA Modules:
  0.0 247.1 jit_solution(805891285204089848)
XLA Ops:
  0.6 1.0 broadcast_select_fusion.17
  1.7 4.6 %collective-permute-start = (bf16[3,8,2,256]{3,2,1,0:T(2,128)(2,1)S(1)}, bf16[3,8,2,256]{3,2,1,0:T(2,128)(2,1)S(1)}, u32[]{:S(2)}, u32[]{:S(2)}) collective-permute-start(bf16[3,8,2,256]{3,2,1,0:T(2,128)(2,1)S(1)} %get-tuple-element.44), channel_id=1, source_target_pairs={{1,2},{3,4},{5,6},{9,10},{11,12},{13,14},{17,18},{19,20},{21,22},{... | collective-permute-start | bytes 73736 | tf_op jit(solution)/shard_map/ppermute | solution.py:39
  10.4 3.8 %collective-permute-start.3 = (bf16[3,2,12,256]{3,2,1,0:T(8,128)(2,1)S(1)}, bf16[3,2,12,256]{3,2,1,0:T(8,128)(2,1)S(1)}, u32[]{:S(2)}, u32[]{:S(2)}) collective-permute-start(bf16[3,2,12,256]{3,2,1,0:T(8,128)(2,1)S(1)} %get-tuple-element.37), channel_id=1, source_target_pairs={{0,8},{1,9},{2,10},{3,11},{4,12},{5,13},{6,14},{7,15},{16,24},{17,... | collective-permute-start | bytes 110600 | tf_op jit(solution)/shard_map/ppermute | solution.py:43
  15.7 1.0 pad_maximum_fusion.1
  17.4 1.0 copy.251
  18.4 11.8 %all-to-all-start = ((bf16[16,72,256]{2,1,0:T(8,128)(2,1)}), bf16[16,72,256]{2,1,0:T(8,128)(2,1)S(1)}, u32[]{:S(2)}, u32[]{:S(2)}) async-start(bf16[16,72,256]{2,1,0:T(8,128)(2,1)} %copy.251), calls=%async_computation | async-start | bytes 1179648 | tf_op jit(solution)/shard_map/all_to_all | solution.py:56
  30.8 19.0 %all-to-all-done = bf16[16,72,256]{2,1,0:T(8,128)(2,1)S(1)} async-done(((bf16[16,72,256]{2,1,0:T(8,128)(2,1)}), bf16[16,72,256]{2,1,0:T(8,128)(2,1)S(1)}, u32[]{:S(2)}, u32[]{:S(2)}) %all-to-all-start) | async-done | bytes 589856 | tf_op jit(solution)/shard_map/all_to_all | solution.py:56
  52.2 1.5 select_convert_fusion.2
  54.4 0.9 copy.257
  55.3 5.9 %all-to-all-start.1 = ((bf16[16,60,256]{2,1,0:T(8,128)(2,1)}), bf16[16,60,256]{2,1,0:T(8,128)(2,1)S(1)}, u32[]{:S(2)}, u32[]{:S(2)}) async-start(bf16[16,60,256]{2,1,0:T(8,128)(2,1)} %copy.257), calls=%async_computation.1 | async-start | bytes 1048576 | tf_op jit(solution)/shard_map/all_to_all | solution.py:56
  61.3 18.1 %all-to-all-done.1 = bf16[16,60,256]{2,1,0:T(8,128)(2,1)S(1)} async-done(((bf16[16,60,256]{2,1,0:T(8,128)(2,1)}), bf16[16,60,256]{2,1,0:T(8,128)(2,1)S(1)}, u32[]{:S(2)}, u32[]{:S(2)}) %all-to-all-start.1) | async-done | bytes 491552 | tf_op jit(solution)/shard_map/all_to_all | solution.py:56
  81.1 0.9 copy-done.5
  82.1 1.1 fusion.8
  83.2 1.9 collective-permute-start.4
  85.7 2.7 %collective-permute-done.4 = bf16[3,8,2,256]{3,2,1,0:T(2,128)(2,1)S(1)} collective-permute-done((bf16[3,8,2,256]{3,2,1,0:T(2,128)(2,1)S(1)}, bf16[3,8,2,256]{3,2,1,0:T(2,128)(2,1)S(1)}, u32[]{:S(2)}, u32[]{:S(2)}) %collective-permute-start.4) | collective-permute-done | bytes 24608 | tf_op jit(solution)/shard_map/ppermute | solution.py:39
  89.2 0.8 collective-permute-start.6
  90.0 0.9 select_reduce_fusion
  91.7 1.1 rev.20
  93.6 1.5 reshape.561
  95.2 1.9 convolution_convert_fusion.1
  98.2 0.9 copy.270
  99.1 5.5 %all-to-all-start.2 = ((bf16[16,60,256]{2,1,0:T(8,128)(2,1)}), bf16[16,60,256]{2,1,0:T(8,128)(2,1)S(1)}, u32[]{:S(2)}, u32[]{:S(2)}) async-start(bf16[16,60,256]{2,1,0:T(8,128)(2,1)} %copy.270), calls=%async_computation.2 | async-start | bytes 1048576 | tf_op jit(solution)/shard_map/all_to_all | solution.py:56
  106.7 1.7 fusion.1
  108.4 13.3 %all-to-all-done.2 = bf16[16,60,256]{2,1,0:T(8,128)(2,1)S(1)} async-done(((bf16[16,60,256]{2,1,0:T(8,128)(2,1)}), bf16[16,60,256]{2,1,0:T(8,128)(2,1)S(1)}, u32[]{:S(2)}, u32[]{:S(2)}) %all-to-all-start.2) | async-done | bytes 491552 | tf_op jit(solution)/shard_map/all_to_all | solution.py:56
  121.7 1.3 reshape.565
  123.1 1.4 copy.271
  124.4 0.9 fusion.16
  125.4 1.4 select_convert_fusion.1
  126.9 2.1 fusion.2
  129.4 2.8 %collective-permute-done.8 = bf16[2,1152,256]{2,1,0:T(8,128)(2,1)S(1)} collective-permute-done((bf16[2,1152,256]{2,1,0:T(8,128)(2,1)S(1)}, bf16[2,1152,256]{2,1,0:T(8,128)(2,1)S(1)}, u32[]{:S(2)}, u32[]{:S(2)}) %collective-permute-start.8) | collective-permute-done | bytes 1179680 | tf_op jit(solution)/shard_map/ppermute | solution.py:70
  132.6 1.1 copy.319
  133.7 17.1 %all-to-all-start.4 = ((bf16[16,2,72,256]{3,2,1,0:T(8,128)(2,1)}), bf16[16,2,72,256]{3,2,1,0:T(8,128)(2,1)S(1)}, u32[]{:S(2)}, u32[]{:S(2)}) async-start(bf16[16,2,72,256]{3,2,1,0:T(8,128)(2,1)} %bitcast.139), calls=%async_computation.4 | async-start | bytes 2359296 | tf_op jit(solution)/shard_map/all_to_all | solution.py:73
  150.9 1.6 copy.275
  152.6 1.1 rev.22
  157.4 10.8 %all-to-all-done.4 = bf16[16,2,72,256]{3,2,1,0:T(8,128)(2,1)S(1)} async-done(((bf16[16,2,72,256]{3,2,1,0:T(8,128)(2,1)}), bf16[16,2,72,256]{3,2,1,0:T(8,128)(2,1)S(1)}, u32[]{:S(2)}, u32[]{:S(2)}) %all-to-all-start.4) | async-done | bytes 1179680 | tf_op jit(solution)/shard_map/all_to_all | solution.py:73
  169.0 4.8 %all-to-all-start.5 = ((bf16[8,18,256]{2,1,0:T(8,128)(2,1)}), bf16[8,18,256]{2,1,0:T(8,128)(2,1)S(1)}, u32[]{:S(2)}, u32[]{:S(2)}) async-start(bf16[8,18,256]{2,1,0:T(8,128)(2,1)} %convert_element_type.79), calls=%async_computation.5 | async-start | bytes 196608 | tf_op jit(solution)/shard_map/all_to_all | solution.py:75
  175.3 5.1 %all-to-all-done.5 = bf16[8,18,256]{2,1,0:T(8,128)(2,1)S(1)} async-done(((bf16[8,18,256]{2,1,0:T(8,128)(2,1)}), bf16[8,18,256]{2,1,0:T(8,128)(2,1)S(1)}, u32[]{:S(2)}, u32[]{:S(2)}) %all-to-all-start.5) | async-done | bytes 73760 | tf_op jit(solution)/shard_map/all_to_all | solution.py:75
  181.1 3.4 %all-to-all-start.6 = ((bf16[8,18,256]{2,1,0:T(8,128)(2,1)}), bf16[8,18,256]{2,1,0:T(8,128)(2,1)S(1)}, u32[]{:S(2)}, u32[]{:S(2)}) async-start(bf16[8,18,256]{2,1,0:T(8,128)(2,1)} %broadcast_in_dim.471), calls=%async_computation.6 | async-start | bytes 196608 | tf_op jit(solution)/shard_map/all_to_all | solution.py:76
  186.0 2.5 %reshape.566 = bf16[300,2304]{1,0:T(8,128)(2,1)S(1)} reshape(bf16[3,10,10,2304]{3,2,1,0:T(8,128)(2,1)} %slice_dynamic-update-slice_fusion.18) | data formatting | bytes 2764800 | tf_op jit(solution)/shard_map/reshape | solution.py:64
  188.5 2.6 %all-to-all-done.6 = bf16[8,18,256]{2,1,0:T(8,128)(2,1)S(1)} async-done(((bf16[8,18,256]{2,1,0:T(8,128)(2,1)}), bf16[8,18,256]{2,1,0:T(8,128)(2,1)S(1)}, u32[]{:S(2)}, u32[]{:S(2)}) %all-to-all-start.6) | async-done | bytes 73760 | tf_op jit(solution)/shard_map/all_to_all | solution.py:76
  191.1 1.1 broadcast_in_dim.472
  192.2 4.8 %all-to-all-start.7 = ((bf16[16,2,72,256]{3,2,1,0:T(8,128)(2,1)}), bf16[16,2,72,256]{3,2,1,0:T(8,128)(2,1)S(1)}, u32[]{:S(2)}, u32[]{:S(2)}) async-start(bf16[16,2,72,256]{3,2,1,0:T(8,128)(2,1)} %broadcast_in_dim.472), calls=%async_computation.7 | async-start | bytes 2359296 | tf_op jit(solution)/shard_map/all_to_all | solution.py:78
  197.0 1.8 convolution_convert_fusion
  199.2 10.7 %all-to-all-done.7 = bf16[16,2,72,256]{3,2,1,0:T(8,128)(2,1)S(1)} async-done(((bf16[16,2,72,256]{3,2,1,0:T(8,128)(2,1)}), bf16[16,2,72,256]{3,2,1,0:T(8,128)(2,1)S(1)}, u32[]{:S(2)}, u32[]{:S(2)}) %all-to-all-start.7) | async-done | bytes 1179680 | tf_op jit(solution)/shard_map/all_to_all | solution.py:78
  210.7 11.1 %all-to-all-start.3 = ((bf16[16,48,256]{2,1,0:T(8,128)(2,1)}), bf16[16,48,256]{2,1,0:T(8,128)(2,1)S(1)}, u32[]{:S(2)}, u32[]{:S(2)}) async-start(bf16[16,48,256]{2,1,0:T(8,128)(2,1)} %bitcast.41), calls=%async_computation.3 | async-start | bytes 786432 | tf_op jit(solution)/shard_map/all_to_all | solution.py:56
  222.6 19.0 %all-to-all-done.3 = bf16[16,48,256]{2,1,0:T(8,128)(2,1)S(1)} async-done(((bf16[16,48,256]{2,1,0:T(8,128)(2,1)}), bf16[16,48,256]{2,1,0:T(8,128)(2,1)S(1)}, u32[]{:S(2)}, u32[]{:S(2)}) %all-to-all-start.3) | async-done | bytes 393248 | tf_op jit(solution)/shard_map/all_to_all | solution.py:56
  242.8 1.4 broadcast_select_fusion.1
  244.6 2.5 %fusion.31 = (f32[1,2304,256]{2,1,0:T(8,128)}, f32[1,2304,256]{2,1,0:T(8,128)}) fusion(f32[2,2304,256]{2,1,0:T(8,128)S(1)} %maximum_convert_fusion), kind=kLoop, calls=%fused_computation.202 | loop fusion | bytes 9437184 | tf_op jit(solution)/shard_map/slice | solution.py:214
  (195 shorter events, 29.7 us)
Async XLA Ops:
  1.7 7.2 %collective-permute-start = (bf16[3,8,2,256]{3,2,1,0:T(2,128)(2,1)S(1)}, bf16[3,8,2,256]{3,2,1,0:T(2,128)(2,1)S(1)}, u32[]{:S(2)}, u32[]{:S(2)}) collective-permute-start(bf16[3,8,2,256]{3,2,1,0:T(2,128)(2,1)S(1)} %get-tuple-element.44), channel_id=1, source_target_pairs={{1,2},{3,4},{5,6},{9,10},{11,12},{13,14},{17,18},{19,20},{21,22},{... | collective-permute-start | bytes 73736 | tf_op jit(solution)/shard_map/ppermute | solution.py:39
  6.3 2.6 %collective-permute-start.1 = (bf16[3,8,2,256]{3,2,1,0:T(2,128)(2,1)S(1)}, bf16[3,8,2,256]{3,2,1,0:T(2,128)(2,1)S(1)}, u32[]{:S(2)}, u32[]{:S(2)}) collective-permute-start(bf16[3,8,2,256]{3,2,1,0:T(2,128)(2,1)S(1)} %get-tuple-element.45), channel_id=1, source_target_pairs={{0,1},{1,0},{2,3},{3,2},{4,5},{5,4},{6,7},{7,6},{8,9},{9,8},{10,11... | collective-permute-start | bytes 73736 | tf_op jit(solution)/shard_map/ppermute | solution.py:38
  9.7 5.2 %collective-permute-start.2 = (bf16[3,2,12,256]{3,2,1,0:T(8,128)(2,1)S(1)}, bf16[3,2,12,256]{3,2,1,0:T(8,128)(2,1)S(1)}, u32[]{:S(2)}, u32[]{:S(2)}) collective-permute-start(bf16[3,2,12,256]{3,2,1,0:T(8,128)(2,1)S(1)} %get-tuple-element.36), channel_id=1, source_target_pairs={{8,16},{9,17},{10,18},{11,19},{12,20},{13,21},{14,22},{15,23},{24,... | collective-permute-start | bytes 110600 | tf_op jit(solution)/shard_map/ppermute | solution.py:44
  10.4 5.2 %collective-permute-start.3 = (bf16[3,2,12,256]{3,2,1,0:T(8,128)(2,1)S(1)}, bf16[3,2,12,256]{3,2,1,0:T(8,128)(2,1)S(1)}, u32[]{:S(2)}, u32[]{:S(2)}) collective-permute-start(bf16[3,2,12,256]{3,2,1,0:T(8,128)(2,1)S(1)} %get-tuple-element.37), channel_id=1, source_target_pairs={{0,8},{1,9},{2,10},{3,11},{4,12},{5,13},{6,14},{7,15},{16,24},{17,... | collective-permute-start | bytes 110600 | tf_op jit(solution)/shard_map/ppermute | solution.py:43
  17.4 33.3 %copy-start = (bf16[3,1,8,8,256]{4,3,2,1,0:T(8,128)(2,1)S(1)}, bf16[3,1,8,8,256]{4,3,2,1,0:T(8,128)(2,1)}, u32[]{:S(2)}) copy-start(bf16[3,1,8,8,256]{4,3,2,1,0:T(8,128)(2,1)} %param.6) | copy-start | bytes 294916
  18.4 31.3 %all-to-all-start = ((bf16[16,72,256]{2,1,0:T(8,128)(2,1)}), bf16[16,72,256]{2,1,0:T(8,128)(2,1)S(1)}, u32[]{:S(2)}, u32[]{:S(2)}) async-start(bf16[16,72,256]{2,1,0:T(8,128)(2,1)} %copy.251), calls=%async_computation | async-start | bytes 1179648 | tf_op jit(solution)/shard_map/all_to_all | solution.py:56
  51.0 1.3 copy-start.3
  51.5 2.3 copy-start.8
  55.3 24.1 %all-to-all-start.1 = ((bf16[16,60,256]{2,1,0:T(8,128)(2,1)}), bf16[16,60,256]{2,1,0:T(8,128)(2,1)S(1)}, u32[]{:S(2)}, u32[]{:S(2)}) async-start(bf16[16,60,256]{2,1,0:T(8,128)(2,1)} %copy.257), calls=%async_computation.1 | async-start | bytes 1048576 | tf_op jit(solution)/shard_map/all_to_all | solution.py:56
  80.0 2.1 copy-start.2
  80.0 2.0 copy-start.7
  80.9 4.5 %copy-start.9 = (s32[12,4]{0,1:T(4,128)S(1)}, s32[12,4]{0,1:T(4,128)}, u32[]{:S(2)}) copy-start(s32[12,4]{0,1:T(4,128)} %param.10) | copy-start | bytes 580
  81.1 0.9 copy-start.5
  83.2 5.1 %collective-permute-start.4 = (bf16[3,8,2,256]{3,2,1,0:T(2,128)(2,1)S(1)}, bf16[3,8,2,256]{3,2,1,0:T(2,128)(2,1)S(1)}, u32[]{:S(2)}, u32[]{:S(2)}) collective-permute-start(bf16[3,8,2,256]{3,2,1,0:T(2,128)(2,1)S(1)} %get-tuple-element.40), channel_id=1, source_target_pairs={{1,2},{3,4},{5,6},{9,10},{11,12},{13,14},{17,18},{19,20},{21,22},{... | collective-permute-start | bytes 73736 | tf_op jit(solution)/shard_map/ppermute | solution.py:39
  85.2 3.2 %collective-permute-start.5 = (bf16[3,8,2,256]{3,2,1,0:T(2,128)(2,1)S(1)}, bf16[3,8,2,256]{3,2,1,0:T(2,128)(2,1)S(1)}, u32[]{:S(2)}, u32[]{:S(2)}) collective-permute-start(bf16[3,8,2,256]{3,2,1,0:T(2,128)(2,1)S(1)} %get-tuple-element.41), channel_id=1, source_target_pairs={{0,1},{1,0},{2,3},{3,2},{4,5},{5,4},{6,7},{7,6},{8,9},{9,8},{10,11... | collective-permute-start | bytes 73736 | tf_op jit(solution)/shard_map/ppermute | solution.py:38
  88.5 4.3 %collective-permute-start.7 = (bf16[3,2,12,256]{3,2,1,0:T(8,128)(2,1)S(1)}, bf16[3,2,12,256]{3,2,1,0:T(8,128)(2,1)S(1)}, u32[]{:S(2)}, u32[]{:S(2)}) collective-permute-start(bf16[3,2,12,256]{3,2,1,0:T(8,128)(2,1)S(1)} %get-tuple-element.34), channel_id=1, source_target_pairs={{0,8},{1,9},{2,10},{3,11},{4,12},{5,13},{6,14},{7,15},{16,24},{17,... | collective-permute-start | bytes 110600 | tf_op jit(solution)/shard_map/ppermute | solution.py:43
  89.2 3.6 %collective-permute-start.6 = (bf16[3,2,12,256]{3,2,1,0:T(8,128)(2,1)S(1)}, bf16[3,2,12,256]{3,2,1,0:T(8,128)(2,1)S(1)}, u32[]{:S(2)}, u32[]{:S(2)}) collective-permute-start(bf16[3,2,12,256]{3,2,1,0:T(8,128)(2,1)S(1)} %get-tuple-element.35), channel_id=1, source_target_pairs={{8,16},{9,17},{10,18},{11,19},{12,20},{13,21},{14,22},{15,23},{24,... | collective-permute-start | bytes 110600 | tf_op jit(solution)/shard_map/ppermute | solution.py:44
  93.5 1.7 copy-start.4
  97.1 0.7 copy-start.1
  97.2 9.5 %copy-start.6 = (f32[192,256]{1,0:T(8,128)S(1)}, f32[192,256]{1,0:T(8,128)}, u32[]{:S(2)}) copy-start(f32[192,256]{1,0:T(8,128)} %get-tuple-element.61) | copy-start | bytes 589828
  99.1 22.6 %all-to-all-start.2 = ((bf16[16,60,256]{2,1,0:T(8,128)(2,1)}), bf16[16,60,256]{2,1,0:T(8,128)(2,1)S(1)}, u32[]{:S(2)}, u32[]{:S(2)}) async-start(bf16[16,60,256]{2,1,0:T(8,128)(2,1)} %copy.270), calls=%async_computation.2 | async-start | bytes 1048576 | tf_op jit(solution)/shard_map/all_to_all | solution.py:56
  129.3 2.9 %collective-permute-start.8 = (bf16[2,1152,256]{2,1,0:T(8,128)(2,1)S(1)}, bf16[2,1152,256]{2,1,0:T(8,128)(2,1)S(1)}, u32[]{:S(2)}, u32[]{:S(2)}) collective-permute-start(bf16[2,1152,256]{2,1,0:T(8,128)(2,1)S(1)} %select_convert_fusion), channel_id=1, source_target_pairs={{0,1},{1,0},{2,3},{3,2},{4,5},{5,4},{6,7},{7,6},{8,9},{9,8},{10,11... | collective-permute-start | bytes 3538952 | tf_op jit(solution)/shard_map/ppermute | solution.py:70
  133.7 34.4 %all-to-all-start.4 = ((bf16[16,2,72,256]{3,2,1,0:T(8,128)(2,1)}), bf16[16,2,72,256]{3,2,1,0:T(8,128)(2,1)S(1)}, u32[]{:S(2)}, u32[]{:S(2)}) async-start(bf16[16,2,72,256]{3,2,1,0:T(8,128)(2,1)} %bitcast.139), calls=%async_computation.4 | async-start | bytes 2359296 | tf_op jit(solution)/shard_map/all_to_all | solution.py:73
  169.0 11.4 %all-to-all-start.5 = ((bf16[8,18,256]{2,1,0:T(8,128)(2,1)}), bf16[8,18,256]{2,1,0:T(8,128)(2,1)S(1)}, u32[]{:S(2)}, u32[]{:S(2)}) async-start(bf16[8,18,256]{2,1,0:T(8,128)(2,1)} %convert_element_type.79), calls=%async_computation.5 | async-start | bytes 196608 | tf_op jit(solution)/shard_map/all_to_all | solution.py:75
  181.1 9.9 %all-to-all-start.6 = ((bf16[8,18,256]{2,1,0:T(8,128)(2,1)}), bf16[8,18,256]{2,1,0:T(8,128)(2,1)S(1)}, u32[]{:S(2)}, u32[]{:S(2)}) async-start(bf16[8,18,256]{2,1,0:T(8,128)(2,1)} %broadcast_in_dim.471), calls=%async_computation.6 | async-start | bytes 196608 | tf_op jit(solution)/shard_map/all_to_all | solution.py:76
  192.2 17.7 %all-to-all-start.7 = ((bf16[16,2,72,256]{3,2,1,0:T(8,128)(2,1)}), bf16[16,2,72,256]{3,2,1,0:T(8,128)(2,1)S(1)}, u32[]{:S(2)}, u32[]{:S(2)}) async-start(bf16[16,2,72,256]{3,2,1,0:T(8,128)(2,1)} %broadcast_in_dim.472), calls=%async_computation.7 | async-start | bytes 2359296 | tf_op jit(solution)/shard_map/all_to_all | solution.py:78
  199.2 42.5 %copy-start.10 = (pred[3,96]{1,0:T(4,128)(4,1)S(1)}, pred[3,96]{1,0:T(4,128)(4,1)}, u32[]{:S(2)}) copy-start(pred[3,96]{1,0:T(4,128)(4,1)} %compare_and_fusion) | copy-start | bytes 868
  210.7 30.9 %all-to-all-start.3 = ((bf16[16,48,256]{2,1,0:T(8,128)(2,1)}), bf16[16,48,256]{2,1,0:T(8,128)(2,1)S(1)}, u32[]{:S(2)}, u32[]{:S(2)}) async-start(bf16[16,48,256]{2,1,0:T(8,128)(2,1)} %bitcast.41), calls=%async_computation.3 | async-start | bytes 786432 | tf_op jit(solution)/shard_map/all_to_all | solution.py:56
  221.9 20.9 %collective-permute-start.9 = (bf16[2,1152,256]{2,1,0:T(8,128)(2,1)S(1)}, bf16[2,1152,256]{2,1,0:T(8,128)(2,1)}, u32[]{:S(2)}, u32[]{:S(2)}) collective-permute-start(bf16[2,1152,256]{2,1,0:T(8,128)(2,1)S(1)} %bitcast.153), channel_id=1, source_target_pairs={{0,1},{1,0},{2,3},{3,2},{4,5},{5,4},{6,7},{7,6},{8,9},{9,8},{10,11... | collective-permute-start | bytes 3538952 | tf_op jit(solution)/shard_map/ppermute | solution.py:80

commit v2 on v1

--- a/solution.py
+++ b/solution.py
@@ -64,18 +64,24 @@
     return jnp.concatenate(views, axis=-1).reshape(-1, 9 * padded.shape[-1])
 
 
-def reduce_grads(grad_one, grad_two, core):
-    both = jnp.stack([grad_one, grad_two])
-    low, high = both[:, :1152], both[:, 1152:]
-    got = lax.ppermute(jnp.where(core == 0, high, low).astype(BF16), "core", [(0, 1), (1, 0)])
-    part = jnp.where(core == 0, low, high) + got.astype(F32)
-    part = part.astype(BF16).reshape(2, 16, 72, 256).transpose(1, 0, 2, 3)
-    part = lax.all_to_all(part, ("x", "y"), 0, 0).astype(F32).sum(0)
-    part = part.reshape(8, 18, 256).astype(BF16)
+HALVINGS = (("core", 1), ("y1", 6), ("y0", 2), ("x1", 24), ("x0", 8))
+
+
+def scatter_sum(grad, bits):
+    for name, mask in HALVINGS:
+        half = grad.shape[0] // 2
+        low, high = grad[:half], grad[half:]
+        up = bits[name] == 1
+        payload = jnp.where(up, low, high).astype(BF16)
+        got = lax.ppermute(payload, TILE, [(t, t ^ mask) for t in range(64)])
+        grad = jnp.where(up, high, low) + got.astype(F32)
+    return grad
+
+
+def gather_sum(part, core):
+    part = jnp.broadcast_to(part.astype(BF16), (8,) + part.shape)
     part = lax.all_to_all(part, ("face", "zh"), 0, 0).astype(F32).sum(0).astype(BF16)
-    part = lax.all_to_all(jnp.broadcast_to(part, (8, 18, 256)), ("face", "zh"), 0, 0)
-    part = part.reshape(2, 72, 256)
-    part = lax.all_to_all(jnp.broadcast_to(part, (16, 2, 72, 256)), ("x", "y"), 0, 0)
+    part = lax.all_to_all(jnp.broadcast_to(part, (16,) + part.shape), ("y", "x"), 0, 0)
     part = part.transpose(1, 0, 2, 3).reshape(2, 1152, 256)
     got = lax.ppermute(part, "core", [(0, 1), (1, 0)])
     low, high = jnp.where(core == 0, part, got), jnp.where(core == 0, got, part)
@@ -185,8 +191,13 @@
     grad_two = lax.dot_general(
         patches_hidden, delta_two, contract_rows, preferred_element_type=F32
     )
+    y_at, x_at = lax.axis_index("y"), lax.axis_index("x")
+    bits = {"core": core, "y1": y_at // 2, "y0": y_at % 2, "x1": x_at // 2, "x0": x_at % 2}
     near = halo(delta_two.reshape(3, 8, 8, channels), 2, row, col)
+    scale = 1.0 / math.sqrt(12 * 64 * 64)
     back = jnp.dot(patches_of(near, 10), back_two, preferred_element_type=F32)
+    grad_two, back = lax.optimization_barrier((grad_two, back))
+    part_two = scatter_sum(grad_two * scale, bits)
     back = back.astype(BF16).reshape(3, 10, 10, channels)
     row_strip = jnp.where(cols_in[:, None], edge_row(back, 0, 9), 0)
     col_strip = jnp.where(rows_in[:, None], edge_col(back, 0, 9), 0)
@@ -208,8 +219,9 @@
     )
     input_grad = add_edges(back[:, 1:9, 1:9].astype(F32), strips, 0).astype(BF16)
 
-    scale = 1.0 / math.sqrt(12 * 64 * 64)
-    total = reduce_grads(grad_one * scale, grad_two * scale, core)
+    part_one = scatter_sum(grad_one * scale, bits)
+    part, input_grad = lax.optimization_barrier((jnp.stack([part_one, part_two]), input_grad))
+    total = gather_sum(part, core)
     shape = (3, 3, channels, channels)
     return (input_grad[:, None], total[0].reshape(shape), total[1].reshape(shape))
 

time: 249 us -> 250 us (level)
  blocking collectives: 0 us -> 33.5 us
  waiting for transfers between devices: 105 us -> 76.7 us
  local copies, waits for them, and re-layouts: 36.8 us -> 27.1 us
  other arithmetic: 14.1 us -> 21.2 us
  starting transfers between devices: 77.8 us -> 74 us
    all_to_all x0 -> x2, blocking collectives: none -> 33.5 us  [the longest x1 17.4 us: gather_sum(): lax.all_to_all(jnp.broadcast_to(part, (16,) + part.shape), ('y', 'x'), 0, 0)]
    all_to_all x4 -> x0, starting transfers between devices: 30.1 us -> none  [the longest x1 17.1 us: reduce_grads(): part = lax.all_to_all(part, ('x', 'y'), 0, 0).astype(F32).sum(0)]
    all_to_all x4 -> x0, waiting for transfers between devices: 29.2 us -> none  [the longest x1 10.8 us: reduce_grads(): part = lax.all_to_all(part, ('x', 'y'), 0, 0).astype(F32).sum(0)]
    ppermute x2 -> x11, starting transfers between devices: 0.75 us -> 28.5 us  [the longest x10 22.3 us: scatter_sum(): got = lax.ppermute(payload, TILE, [(t, t ^ mask) for t in range(64)])]
    ppermute x2 -> x11, waiting for transfers between devices: 2.84 us -> 22.8 us  [the longest x10 20.4 us: scatter_sum(): got = lax.ppermute(payload, TILE, [(t, t ^ mask) for t in range(64)])]
    all_to_all x4, waiting for transfers between devices: 69.4 us -> 53.2 us  [seam_swap(): got = lax.all_to_all(send, AXES, 0, 0, axis_index_groups=SEAM_GROUPS)]
    unnamed x58 -> x86, local copies, waits for them, and re-layouts: 11.2 us -> 5.53 us
    all_to_all x4, starting transfers between devices: 34.3 us -> 30.1 us  [seam_swap(): got = lax.all_to_all(send, AXES, 0, 0, axis_index_groups=SEAM_GROUPS)]
  transfers between devices with their start and end apart: 18 -> 23, of which waited for: 11 -> 10; matrix products, arithmetic and copies ran while one was open for 11% -> 14% of each run, Pallas kernels for 0% -> 0%
where the time goes in v2:
time: 250 us; the launch traced here: 247 us
  waiting for transfers between devices  76.7 us (31%)
  starting transfers between devices  74 us (30%)
  blocking collectives  33.5 us (13%)
  local copies, waits for them, and re-layouts  27.1 us (11%)
  other arithmetic  21.2 us (8%)
  matrix products  12.1 us (5%)
    all_to_all x4, waiting for transfers between devices, seam_swap(): got = lax.all_to_all(send, AXES, 0, 0, axis_index_groups=SEAM_GROUPS)  53.2 us
    all_to_all x4, starting transfers between devices, seam_swap(): got = lax.all_to_all(send, AXES, 0, 0, axis_index_groups=SEAM_GROUPS)  30.1 us
    ppermute x10, starting transfers between devices, scatter_sum(): got = lax.ppermute(payload, TILE, [(t, t ^ mask) for t in range(64)])  22.3 us
    ppermute x10, waiting for transfers between devices, scatter_sum(): got = lax.ppermute(payload, TILE, [(t, t ^ mask) for t in range(64)])  20.4 us
    all_to_all x1, blocking collectives, gather_sum(): lax.all_to_all(jnp.broadcast_to(part, (16,) + part.shape), ('y', 'x'), 0, 0)  17.4 us
    all_to_all x1, blocking collectives, gather_sum(): lax.all_to_all(part, ('face', 'zh'), 0, 0).astype(F32).sum(0).astype(BF16)  16.1 us
    ppermute x2, starting transfers between devices, halo(): s1 = lax.ppermute(jnp.where(even, down, up), TILE, EVEN_ROWS)  7.37 us
    ppermute x2, starting transfers between devices, halo(): s2 = lax.ppermute(jnp.where(even, left, right), TILE, ODD_COLS)  6.5 us
  transfers between devices with their start and end apart: 23, of which 10 were waited for; matrix products, arithmetic and copies ran while one was open for 14% of the time, Pallas kernels for 0%

profile of v2, /device:TPU:1, one launch (start us, length us, event | category | flops | bytes accessed | tf_op | source)
XLA Modules:
  0.0 246.7 jit_solution(4020480340919310617)
XLA Ops:
  0.6 1.0 broadcast_select_fusion.25
  1.7 4.6 %collective-permute-start = (bf16[3,8,2,256]{3,2,1,0:T(2,128)(2,1)S(1)}, bf16[3,8,2,256]{3,2,1,0:T(2,128)(2,1)S(1)}, u32[]{:S(2)}, u32[]{:S(2)}) collective-permute-start(bf16[3,8,2,256]{3,2,1,0:T(2,128)(2,1)S(1)} %get-tuple-element.55), channel_id=1, source_target_pairs={{1,2},{3,4},{5,6},{9,10},{11,12},{13,14},{17,18},{19,20},{21,22},{... | collective-permute-start | bytes 73736 | tf_op jit(solution)/shard_map/ppermute | solution.py:39
  10.4 3.8 %collective-permute-start.3 = (bf16[3,2,12,256]{3,2,1,0:T(8,128)(2,1)S(1)}, bf16[3,2,12,256]{3,2,1,0:T(8,128)(2,1)S(1)}, u32[]{:S(2)}, u32[]{:S(2)}) collective-permute-start(bf16[3,2,12,256]{3,2,1,0:T(8,128)(2,1)S(1)} %get-tuple-element.48), channel_id=1, source_target_pairs={{0,8},{1,9},{2,10},{3,11},{4,12},{5,13},{6,14},{7,15},{16,24},{17,... | collective-permute-start | bytes 110600 | tf_op jit(solution)/shard_map/ppermute | solution.py:43
  15.7 1.0 pad_maximum_fusion
  17.4 1.0 copy.284
  18.4 11.8 %all-to-all-start = ((bf16[16,72,256]{2,1,0:T(8,128)(2,1)}), bf16[16,72,256]{2,1,0:T(8,128)(2,1)S(1)}, u32[]{:S(2)}, u32[]{:S(2)}) async-start(bf16[16,72,256]{2,1,0:T(8,128)(2,1)} %copy.284), calls=%async_computation | async-start | bytes 1179648 | tf_op jit(solution)/shard_map/all_to_all | solution.py:56
  30.8 19.0 %all-to-all-done = bf16[16,72,256]{2,1,0:T(8,128)(2,1)S(1)} async-done(((bf16[16,72,256]{2,1,0:T(8,128)(2,1)}), bf16[16,72,256]{2,1,0:T(8,128)(2,1)S(1)}, u32[]{:S(2)}, u32[]{:S(2)}) %all-to-all-start) | async-done | bytes 589856 | tf_op jit(solution)/shard_map/all_to_all | solution.py:56
  52.3 1.5 select_convert_fusion.5
  54.5 0.9 copy.290
  55.4 5.9 %all-to-all-start.1 = ((bf16[16,60,256]{2,1,0:T(8,128)(2,1)}), bf16[16,60,256]{2,1,0:T(8,128)(2,1)S(1)}, u32[]{:S(2)}, u32[]{:S(2)}) async-start(bf16[16,60,256]{2,1,0:T(8,128)(2,1)} %copy.290), calls=%async_computation.1 | async-start | bytes 1048576 | tf_op jit(solution)/shard_map/all_to_all | solution.py:56
  62.8 16.7 %all-to-all-done.1 = bf16[16,60,256]{2,1,0:T(8,128)(2,1)S(1)} async-done(((bf16[16,60,256]{2,1,0:T(8,128)(2,1)}), bf16[16,60,256]{2,1,0:T(8,128)(2,1)S(1)}, u32[]{:S(2)}, u32[]{:S(2)}) %all-to-all-start.1) | async-done | bytes 491552 | tf_op jit(solution)/shard_map/all_to_all | solution.py:56
  81.4 1.4 fusion.5
  83.5 1.9 collective-permute-start.4
  86.1 1.6 copy.295
  87.7 1.6 copy.308
  89.2 1.3 copy.309
  90.5 1.1 rev.20
  93.1 1.1 rev.22
  95.7 3.6 %collective-permute-start.7 = (bf16[3,2,12,256]{3,2,1,0:T(8,128)(2,1)S(1)}, bf16[3,2,12,256]{3,2,1,0:T(8,128)(2,1)S(1)}, u32[]{:S(2)}, u32[]{:S(2)}) collective-permute-start(bf16[3,2,12,256]{3,2,1,0:T(8,128)(2,1)S(1)} %get-tuple-element.45), channel_id=1, source_target_pairs={{0,8},{1,9},{2,10},{3,11},{4,12},{5,13},{6,14},{7,15},{16,24},{17,... | collective-permute-start | bytes 110600 | tf_op jit(solution)/shard_map/ppermute | solution.py:43
  99.3 2.0 fusion.6
  102.1 1.6 reshape.553
  103.7 1.9 fusion.29
  105.7 1.9 broadcast_multiply_fusion
  108.5 1.1 collective-permute-start.13
  111.4 3.6 %all-to-all-start.2 = ((bf16[16,60,256]{2,1,0:T(8,128)(2,1)}), bf16[16,60,256]{2,1,0:T(8,128)(2,1)S(1)}, u32[]{:S(2)}, u32[]{:S(2)}) async-start(bf16[16,60,256]{2,1,0:T(8,128)(2,1)} %copy.303), calls=%async_computation.2 | async-start | bytes 1048576 | tf_op jit(solution)/shard_map/all_to_all | solution.py:56
  114.9 1.3 convert_add_fusion
  116.3 3.0 %collective-permute-start.14 = (bf16[576,256]{1,0:T(8,128)(2,1)S(1)}, bf16[576,256]{1,0:T(8,128)(2,1)S(1)}, u32[]{:S(2)}, u32[]{:S(2)}) collective-permute-start(bf16[576,256]{1,0:T(8,128)(2,1)S(1)} %select_convert_fusion.2), channel_id=1, source_target_pairs={{0,6},{1,7},{2,4},{3,5},{4,2},{5,3},{6,0},{7,1},{8,14},{9,15},{10,... | collective-permute-start | bytes 884744 | tf_op jit(solution)/shard_map/ppermute | solution.py:76
  119.3 10.4 %collective-permute-done.14 = bf16[576,256]{1,0:T(8,128)(2,1)S(1)} collective-permute-done((bf16[576,256]{1,0:T(8,128)(2,1)S(1)}, bf16[576,256]{1,0:T(8,128)(2,1)S(1)}, u32[]{:S(2)}, u32[]{:S(2)}) %collective-permute-start.14) | collective-permute-done | bytes 294944 | tf_op jit(solution)/shard_map/ppermute | solution.py:76
  130.6 3.6 %all-to-all-done.2 = bf16[16,60,256]{2,1,0:T(8,128)(2,1)S(1)} async-done(((bf16[16,60,256]{2,1,0:T(8,128)(2,1)}), bf16[16,60,256]{2,1,0:T(8,128)(2,1)S(1)}, u32[]{:S(2)}, u32[]{:S(2)}) %all-to-all-start.2) | async-done | bytes 491552 | tf_op jit(solution)/shard_map/all_to_all | solution.py:56
  136.3 1.5 reshape.558
  137.9 2.2 convolution_convert_fusion
  140.2 2.1 fusion
  143.8 1.0 convert_add_fusion.4
  144.8 14.2 %collective-permute-start.16 = (bf16[144,256]{1,0:T(8,128)(2,1)S(1)}, bf16[144,256]{1,0:T(8,128)(2,1)S(1)}, u32[]{:S(2)}, u32[]{:S(2)}) collective-permute-start(bf16[144,256]{1,0:T(8,128)(2,1)S(1)} %select_convert_fusion.8), channel_id=1, source_target_pairs={{0,24},{1,25},{2,26},{3,27},{4,28},{5,29},{6,30},{7,31},{8,16},{9,... | collective-permute-start | bytes 221192 | tf_op jit(solution)/shard_map/ppermute | solution.py:76
  159.9 8.9 %all-to-all-start.3 = ((bf16[16,48,256]{2,1,0:T(8,128)(2,1)}), bf16[16,48,256]{2,1,0:T(8,128)(2,1)}, u32[]{:S(2)}, u32[]{:S(2)}) async-start(bf16[16,48,256]{2,1,0:T(8,128)(2,1)} %bitcast.45), calls=%async_computation.3 | async-start | bytes 786432 | tf_op jit(solution)/shard_map/all_to_all | solution.py:56
  169.0 1.3 convert_add_fusion.1
  170.3 2.9 %collective-permute-start.9 = (bf16[576,256]{1,0:T(8,128)(2,1)S(1)}, bf16[576,256]{1,0:T(8,128)(2,1)S(1)}, u32[]{:S(2)}, u32[]{:S(2)}) collective-permute-start(bf16[576,256]{1,0:T(8,128)(2,1)S(1)} %select_convert_fusion.3), channel_id=1, source_target_pairs={{0,6},{1,7},{2,4},{3,5},{4,2},{5,3},{6,0},{7,1},{8,14},{9,15},{10,... | collective-permute-start | bytes 884744 | tf_op jit(solution)/shard_map/ppermute | solution.py:76
  173.2 13.9 %all-to-all-done.3 = bf16[16,48,256]{2,1,0:T(8,128)(2,1)} async-done(((bf16[16,48,256]{2,1,0:T(8,128)(2,1)}), bf16[16,48,256]{2,1,0:T(8,128)(2,1)}, u32[]{:S(2)}, u32[]{:S(2)}) %all-to-all-start.3) | async-done | bytes 393248 | tf_op jit(solution)/shard_map/all_to_all | solution.py:56
  187.2 1.2 reshape.562
  188.8 4.8 %collective-permute-done.10 = bf16[288,256]{1,0:T(8,128)(2,1)S(1)} collective-permute-done((bf16[288,256]{1,0:T(8,128)(2,1)S(1)}, bf16[288,256]{1,0:T(8,128)(2,1)S(1)}, u32[]{:S(2)}, u32[]{:S(2)}) %collective-permute-start.10) | collective-permute-done | bytes 147488 | tf_op jit(solution)/shard_map/ppermute | solution.py:76
  194.2 4.0 %collective-permute-done.11 = bf16[144,256]{1,0:T(8,128)(2,1)S(1)} collective-permute-done((bf16[144,256]{1,0:T(8,128)(2,1)S(1)}, bf16[144,256]{1,0:T(8,128)(2,1)S(1)}, u32[]{:S(2)}, u32[]{:S(2)}) %collective-permute-start.11) | collective-permute-done | bytes 73760 | tf_op jit(solution)/shard_map/ppermute | solution.py:76
  198.3 1.7 add_convert_fusion
  200.0 1.1 collective-permute-done.12
  201.2 16.1 %all_to_all.30 = bf16[8,2,72,256]{3,2,1,0:T(8,128)(2,1)S(1)} all-to-all(bf16[8,2,72,256]{3,2,1,0:T(8,128)(2,1)S(1)} %broadcast_in_dim.471), channel_id=1, replica_groups=mesh['face'=4,'zh'=2,'x'=4,'y'=4,'core'=2] {'face','zh'}, dimensions={0} | all-to-all | bytes 1179648 | tf_op jit(solution)/shard_map/all_to_all | solution.py:83
  217.5 17.4 %all_to_all.31 = bf16[16,2,72,256]{3,2,1,0:T(8,128)(2,1)S(1)} all-to-all(bf16[16,2,72,256]{3,2,1,0:T(8,128)(2,1)S(1)} %broadcast_in_dim.472), channel_id=1, replica_groups=mesh['face'=4,'zh'=2,'x'=4,'y'=4,'core'=2] {'y','x'}, dimensions={0} | all-to-all | bytes 2359296 | tf_op jit(solution)/shard_map/all_to_all | solution.py:84
  235.0 6.1 %collective-permute-start.18 = (bf16[2,1152,256]{2,1,0:T(8,128)(2,1)S(1)}, bf16[2,1152,256]{2,1,0:T(8,128)(2,1)S(1)}, u32[]{:S(2)}, u32[]{:S(2)}) collective-permute-start(bf16[2,1152,256]{2,1,0:T(8,128)(2,1)S(1)} %bitcast.147), channel_id=1, source_target_pairs={{0,1},{1,0},{2,3},{3,2},{4,5},{5,4},{6,7},{7,6},{8,9},{9,8},{10,11... | collective-permute-start | bytes 3538952 | tf_op jit(solution)/shard_map/ppermute | solution.py:86
  241.2 2.5 %collective-permute-done.18 = bf16[2,1152,256]{2,1,0:T(8,128)(2,1)S(1)} collective-permute-done((bf16[2,1152,256]{2,1,0:T(8,128)(2,1)S(1)}, bf16[2,1152,256]{2,1,0:T(8,128)(2,1)S(1)}, u32[]{:S(2)}, u32[]{:S(2)}) %collective-permute-start.18) | collective-permute-done | bytes 1179680 | tf_op jit(solution)/shard_map/ppermute | solution.py:86
  244.2 2.5 %fusion.28 = (f32[1,2304,256]{2,1,0:T(8,128)}, f32[1,2304,256]{2,1,0:T(8,128)}) fusion(f32[2,2304,256]{2,1,0:T(8,128)S(1)} %maximum_convert_fusion), kind=kLoop, calls=%fused_computation.213 | loop fusion | bytes 9437184 | tf_op jit(solution)/shard_map/slice | solution.py:226
  (251 shorter events, 28.2 us)
Async XLA Ops:
  1.7 7.2 %collective-permute-start = (bf16[3,8,2,256]{3,2,1,0:T(2,128)(2,1)S(1)}, bf16[3,8,2,256]{3,2,1,0:T(2,128)(2,1)S(1)}, u32[]{:S(2)}, u32[]{:S(2)}) collective-permute-start(bf16[3,8,2,256]{3,2,1,0:T(2,128)(2,1)S(1)} %get-tuple-element.55), channel_id=1, source_target_pairs={{1,2},{3,4},{5,6},{9,10},{11,12},{13,14},{17,18},{19,20},{21,22},{... | collective-permute-start | bytes 73736 | tf_op jit(solution)/shard_map/ppermute | solution.py:39
  6.3 2.6 %collective-permute-start.1 = (bf16[3,8,2,256]{3,2,1,0:T(2,128)(2,1)S(1)}, bf16[3,8,2,256]{3,2,1,0:T(2,128)(2,1)S(1)}, u32[]{:S(2)}, u32[]{:S(2)}) collective-permute-start(bf16[3,8,2,256]{3,2,1,0:T(2,128)(2,1)S(1)} %get-tuple-element.56), channel_id=1, source_target_pairs={{0,1},{1,0},{2,3},{3,2},{4,5},{5,4},{6,7},{7,6},{8,9},{9,8},{10,11... | collective-permute-start | bytes 73736 | tf_op jit(solution)/shard_map/ppermute | solution.py:38
  6.5 23.9 %copy-start.23 = (pred[2,2]{1,0:T(4,128)(4,1)}, pred[2,2]{1,0:T(4,128)(4,1)S(1)}, u32[]{:S(2)}) copy-start(pred[2,2]{1,0:T(4,128)(4,1)S(1)} %iota_compare_fusion.2) | copy-start | bytes 16
  8.7 45.4 %copy-start.13 = (pred[4,2]{0,1:T(4,128)(4,1)}, pred[4,2]{0,1:T(4,128)(4,1)S(1)}, u32[]{:S(2)}) copy-start(pred[4,2]{0,1:T(4,128)(4,1)S(1)} %add_compare_fusion) | copy-start | bytes 28
  8.8 21.5 %copy-start.19 = (pred[2]{0:T(512)(128)(4,1)}, pred[2]{0:T(512)(128)(4,1)S(1)}, u32[]{:S(2)}) copy-start(pred[2]{0:T(512)(128)(4,1)S(1)} %pad_add_fusion) | copy-start | bytes 10
  9.8 5.2 %collective-permute-start.2 = (bf16[3,2,12,256]{3,2,1,0:T(8,128)(2,1)S(1)}, bf16[3,2,12,256]{3,2,1,0:T(8,128)(2,1)S(1)}, u32[]{:S(2)}, u32[]{:S(2)}) collective-permute-start(bf16[3,2,12,256]{3,2,1,0:T(8,128)(2,1)S(1)} %get-tuple-element.47), channel_id=1, source_target_pairs={{8,16},{9,17},{10,18},{11,19},{12,20},{13,21},{14,22},{15,23},{24,... | collective-permute-start | bytes 110600 | tf_op jit(solution)/shard_map/ppermute | solution.py:44
  10.4 5.2 %collective-permute-start.3 = (bf16[3,2,12,256]{3,2,1,0:T(8,128)(2,1)S(1)}, bf16[3,2,12,256]{3,2,1,0:T(8,128)(2,1)S(1)}, u32[]{:S(2)}, u32[]{:S(2)}) collective-permute-start(bf16[3,2,12,256]{3,2,1,0:T(8,128)(2,1)S(1)} %get-tuple-element.48), channel_id=1, source_target_pairs={{0,8},{1,9},{2,10},{3,11},{4,12},{5,13},{6,14},{7,15},{16,24},{17,... | collective-permute-start | bytes 110600 | tf_op jit(solution)/shard_map/ppermute | solution.py:43
  17.4 33.3 %copy-start = (bf16[3,1,8,8,256]{4,3,2,1,0:T(8,128)(2,1)S(1)}, bf16[3,1,8,8,256]{4,3,2,1,0:T(8,128)(2,1)}, u32[]{:S(2)}) copy-start(bf16[3,1,8,8,256]{4,3,2,1,0:T(8,128)(2,1)} %param.6) | copy-start | bytes 294916
  18.4 31.4 %all-to-all-start = ((bf16[16,72,256]{2,1,0:T(8,128)(2,1)}), bf16[16,72,256]{2,1,0:T(8,128)(2,1)S(1)}, u32[]{:S(2)}, u32[]{:S(2)}) async-start(bf16[16,72,256]{2,1,0:T(8,128)(2,1)} %copy.284), calls=%async_computation | async-start | bytes 1179648 | tf_op jit(solution)/shard_map/all_to_all | solution.py:56
  30.7 20.5 %copy-start.15 = (pred[10]{0:T(512)(128)(4,1)}, pred[10]{0:T(512)(128)(4,1)S(1)}, u32[]{:S(2)}) copy-start(pred[10]{0:T(512)(128)(4,1)S(1)} %get-tuple-element.74) | copy-start | bytes 34
  30.8 20.5 %copy-start.17 = (pred[10]{0:T(512)(128)(4,1)}, pred[10]{0:T(512)(128)(4,1)S(1)}, u32[]{:S(2)}) copy-start(pred[10]{0:T(512)(128)(4,1)S(1)} %get-tuple-element.73) | copy-start | bytes 34
  30.8 20.7 %copy-start.10 = (pred[10,10]{1,0:T(8,128)(4,1)}, pred[10,10]{1,0:T(8,128)(4,1)S(1)}, u32[]{:S(2)}) copy-start(pred[10,10]{1,0:T(8,128)(4,1)S(1)} %broadcast_and_fusion.1) | copy-start | bytes 304
  51.0 1.3 copy-start.4
  51.5 2.3 copy-start.9
  53.8 7.6 %copy-start.12 = (s32[12,4]{0,1:T(4,128)S(1)}, s32[12,4]{0,1:T(4,128)}, u32[]{:S(2)}) copy-start(s32[12,4]{0,1:T(4,128)} %param.10) | copy-start | bytes 580
  55.4 24.1 %all-to-all-start.1 = ((bf16[16,60,256]{2,1,0:T(8,128)(2,1)}), bf16[16,60,256]{2,1,0:T(8,128)(2,1)S(1)}, u32[]{:S(2)}, u32[]{:S(2)}) async-start(bf16[16,60,256]{2,1,0:T(8,128)(2,1)} %copy.290), calls=%async_computation.1 | async-start | bytes 1048576 | tf_op jit(solution)/shard_map/all_to_all | solution.py:56
  80.1 1.3 copy-start.3
  83.5 10.8 %collective-permute-start.4 = (bf16[3,8,2,256]{3,2,1,0:T(2,128)(2,1)}, bf16[3,8,2,256]{3,2,1,0:T(2,128)(2,1)}, u32[]{:S(2)}, u32[]{:S(2)}) collective-permute-start(bf16[3,8,2,256]{3,2,1,0:T(2,128)(2,1)} %get-tuple-element.51), channel_id=1, source_target_pairs={{1,2},{3,4},{5,6},{9,10},{11,12},{13,14},{17,18},{19,20},{21,22},{... | collective-permute-start | bytes 73736 | tf_op jit(solution)/shard_map/ppermute | solution.py:39
  85.4 8.8 %collective-permute-start.5 = (bf16[3,8,2,256]{3,2,1,0:T(2,128)(2,1)}, bf16[3,8,2,256]{3,2,1,0:T(2,128)(2,1)}, u32[]{:S(2)}, u32[]{:S(2)}) collective-permute-start(bf16[3,8,2,256]{3,2,1,0:T(2,128)(2,1)} %get-tuple-element.52), channel_id=1, source_target_pairs={{0,1},{1,0},{2,3},{3,2},{4,5},{5,4},{6,7},{7,6},{8,9},{9,8},{10,11... | collective-permute-start | bytes 73736 | tf_op jit(solution)/shard_map/ppermute | solution.py:38
  91.6 7.7 %copy-start.8 = (bf16[3,1,8,8,256]{4,3,2,1,0:T(8,128)(2,1)S(1)}, bf16[3,1,8,8,256]{4,3,2,1,0:T(8,128)(2,1)}, u32[]{:S(2)}) copy-start(bf16[3,1,8,8,256]{4,3,2,1,0:T(8,128)(2,1)} %param.7) | copy-start | bytes 294916
  95.0 6.3 %collective-permute-start.6 = (bf16[3,2,12,256]{3,2,1,0:T(8,128)(2,1)S(1)}, bf16[3,2,12,256]{3,2,1,0:T(8,128)(2,1)S(1)}, u32[]{:S(2)}, u32[]{:S(2)}) collective-permute-start(bf16[3,2,12,256]{3,2,1,0:T(8,128)(2,1)S(1)} %get-tuple-element.46), channel_id=1, source_target_pairs={{8,16},{9,17},{10,18},{11,19},{12,20},{13,21},{14,22},{15,23},{24,... | collective-permute-start | bytes 110600 | tf_op jit(solution)/shard_map/ppermute | solution.py:44
  95.7 5.6 %collective-permute-start.7 = (bf16[3,2,12,256]{3,2,1,0:T(8,128)(2,1)S(1)}, bf16[3,2,12,256]{3,2,1,0:T(8,128)(2,1)S(1)}, u32[]{:S(2)}, u32[]{:S(2)}) collective-permute-start(bf16[3,2,12,256]{3,2,1,0:T(8,128)(2,1)S(1)} %get-tuple-element.45), channel_id=1, source_target_pairs={{0,8},{1,9},{2,10},{3,11},{4,12},{5,13},{6,14},{7,15},{16,24},{17,... | collective-permute-start | bytes 110600 | tf_op jit(solution)/shard_map/ppermute | solution.py:43
  101.9 1.7 copy-start.5
  105.6 4.1 %copy-start.1 = (bf16[3,10,10,256]{3,2,1,0:T(8,128)(2,1)}, bf16[3,10,10,256]{3,2,1,0:T(8,128)(2,1)S(1)}, u32[]{:S(2)}) copy-start(bf16[3,10,10,256]{3,2,1,0:T(8,128)(2,1)S(1)} %reshape.555) | copy-start | bytes 460804
  105.7 4.0 %copy-start.18 = (pred[10]{0:T(512)(128)(4,1)S(1)}, pred[10]{0:T(512)(128)(4,1)}, u32[]{:S(2)}) copy-start(pred[10]{0:T(512)(128)(4,1)} %copy-done.17) | copy-start | bytes 34
  105.7 4.1 %copy-start.16 = (pred[10]{0:T(512)(128)(4,1)S(1)}, pred[10]{0:T(512)(128)(4,1)}, u32[]{:S(2)}) copy-start(pred[10]{0:T(512)(128)(4,1)} %copy-done.15) | copy-start | bytes 34
  105.7 4.3 %copy-start.14 = (pred[4,2]{0,1:T(4,128)(4,1)S(1)}, pred[4,2]{0,1:T(4,128)(4,1)}, u32[]{:S(2)}) copy-start(pred[4,2]{0,1:T(4,128)(4,1)} %copy-done.13) | copy-start | bytes 28
  108.5 6.4 %collective-permute-start.13 = (bf16[1152,256]{1,0:T(8,128)(2,1)}, bf16[1152,256]{1,0:T(8,128)(2,1)}, u32[]{:S(2)}, u32[]{:S(2)}) collective-permute-start(bf16[1152,256]{1,0:T(8,128)(2,1)} %select_convert_fusion), channel_id=1, source_target_pairs={{0,1},{1,0},{2,3},{3,2},{4,5},{5,4},{6,7},{7,6},{8,9},{9,8},{10,11... | collective-permute-start | bytes 1769480 | tf_op jit(solution)/shard_map/ppermute | solution.py:76
  111.4 22.8 %all-to-all-start.2 = ((bf16[16,60,256]{2,1,0:T(8,128)(2,1)}), bf16[16,60,256]{2,1,0:T(8,128)(2,1)S(1)}, u32[]{:S(2)}, u32[]{:S(2)}) async-start(bf16[16,60,256]{2,1,0:T(8,128)(2,1)} %copy.303), calls=%async_computation.2 | async-start | bytes 1048576 | tf_op jit(solution)/shard_map/all_to_all | solution.py:56
  116.3 13.5 %collective-permute-start.14 = (bf16[576,256]{1,0:T(8,128)(2,1)S(1)}, bf16[576,256]{1,0:T(8,128)(2,1)S(1)}, u32[]{:S(2)}, u32[]{:S(2)}) collective-permute-start(bf16[576,256]{1,0:T(8,128)(2,1)S(1)} %select_convert_fusion.2), channel_id=1, source_target_pairs={{0,6},{1,7},{2,4},{3,5},{4,2},{5,3},{6,0},{7,1},{8,14},{9,15},{10,... | collective-permute-start | bytes 884744 | tf_op jit(solution)/shard_map/ppermute | solution.py:76
  119.3 15.7 %copy-start.20 = (pred[2]{0:T(512)(128)(4,1)S(1)}, pred[2]{0:T(512)(128)(4,1)}, u32[]{:S(2)}) copy-start(pred[2]{0:T(512)(128)(4,1)} %copy-done.19) | copy-start | bytes 10
  129.8 5.6 %copy-start.2 = (bf16[3,10,10,256]{3,2,1,0:T(8,128)(2,1)S(1)}, bf16[3,10,10,256]{3,2,1,0:T(8,128)(2,1)}, u32[]{:S(2)}) copy-start(bf16[3,10,10,256]{3,2,1,0:T(8,128)(2,1)} %copy-done.1) | copy-start | bytes 460804
  129.8 5.6 %copy-start.7 = (f32[3,10,10,256]{3,2,1,0:T(8,128)S(1)}, f32[3,10,10,256]{3,2,1,0:T(8,128)}, u32[]{:S(2)}) copy-start(f32[3,10,10,256]{3,2,1,0:T(8,128)} %get-tuple-element.70) | copy-start | bytes 921604
  129.9 5.6 %copy-start.11 = (pred[10,10]{1,0:T(8,128)(4,1)S(1)}, pred[10,10]{1,0:T(8,128)(4,1)}, u32[]{:S(2)}) copy-start(pred[10,10]{1,0:T(8,128)(4,1)} %copy-done.10) | copy-start | bytes 304
  129.9 5.6 %copy-start.21 = (pred[10]{0:T(512)(128)(4,1)S(1)}, pred[10]{0:T(512)(128)(4,1)}, u32[]{:S(2)}) copy-start(pred[10]{0:T(512)(128)(4,1)} %get-tuple-element.85) | copy-start | bytes 34
  129.9 5.6 %copy-start.22 = (pred[10]{0:T(512)(128)(4,1)S(1)}, pred[10]{0:T(512)(128)(4,1)}, u32[]{:S(2)}) copy-start(pred[10]{0:T(512)(128)(4,1)} %get-tuple-element.86) | copy-start | bytes 34
  130.6 13.3 %collective-permute-start.15 = (bf16[288,256]{1,0:T(8,128)(2,1)}, bf16[288,256]{1,0:T(8,128)(2,1)}, u32[]{:S(2)}, u32[]{:S(2)}) collective-permute-start(bf16[288,256]{1,0:T(8,128)(2,1)} %select_convert_fusion.6), channel_id=1, source_target_pairs={{0,2},{1,3},{2,0},{3,1},{4,6},{5,7},{6,4},{7,5},{8,10},{9,11},{10,... | collective-permute-start | bytes 442376 | tf_op jit(solution)/shard_map/ppermute | solution.py:76
  140.1 2.2 copy-start.6
  142.4 16.7 %copy-start.24 = (pred[4,2]{1,0:T(4,128)(4,1)S(1)}, pred[4,2]{1,0:T(4,128)(4,1)}, u32[]{:S(2)}) copy-start(pred[4,2]{1,0:T(4,128)(4,1)} %copy.309) | copy-start | bytes 28
  143.5 25.5 %collective-permute-start.8 = (bf16[1152,256]{1,0:T(8,128)(2,1)}, bf16[1152,256]{1,0:T(8,128)(2,1)}, u32[]{:S(2)}, u32[]{:S(2)}) collective-permute-start(bf16[1152,256]{1,0:T(8,128)(2,1)} %select_convert_fusion.1), channel_id=1, source_target_pairs={{0,1},{1,0},{2,3},{3,2},{4,5},{5,4},{6,7},{7,6},{8,9},{9,8},{10,11... | collective-permute-start | bytes 1769480 | tf_op jit(solution)/shard_map/ppermute | solution.py:76
  144.8 24.0 %collective-permute-start.16 = (bf16[144,256]{1,0:T(8,128)(2,1)S(1)}, bf16[144,256]{1,0:T(8,128)(2,1)S(1)}, u32[]{:S(2)}, u32[]{:S(2)}) collective-permute-start(bf16[144,256]{1,0:T(8,128)(2,1)S(1)} %select_convert_fusion.8), channel_id=1, source_target_pairs={{0,24},{1,25},{2,26},{3,27},{4,28},{5,29},{6,30},{7,31},{8,16},{9,... | collective-permute-start | bytes 221192 | tf_op jit(solution)/shard_map/ppermute | solution.py:76
  159.9 27.2 %all-to-all-start.3 = ((bf16[16,48,256]{2,1,0:T(8,128)(2,1)}), bf16[16,48,256]{2,1,0:T(8,128)(2,1)}, u32[]{:S(2)}, u32[]{:S(2)}) async-start(bf16[16,48,256]{2,1,0:T(8,128)(2,1)} %bitcast.45), calls=%async_computation.3 | async-start | bytes 786432 | tf_op jit(solution)/shard_map/all_to_all | solution.py:56
  168.9 4.4 %collective-permute-start.17 = (bf16[72,256]{1,0:T(8,128)(2,1)S(1)}, bf16[72,256]{1,0:T(8,128)(2,1)S(1)}, u32[]{:S(2)}, u32[]{:S(2)}) collective-permute-start(bf16[72,256]{1,0:T(8,128)(2,1)S(1)} %select_convert_fusion.10), channel_id=1, source_target_pairs={{0,8},{1,9},{2,10},{3,11},{4,12},{5,13},{6,14},{7,15},{8,0},{9,1},... | collective-permute-start | bytes 110600 | tf_op jit(solution)/shard_map/ppermute | solution.py:76
  170.3 18.1 %collective-permute-start.9 = (bf16[576,256]{1,0:T(8,128)(2,1)S(1)}, bf16[576,256]{1,0:T(8,128)(2,1)S(1)}, u32[]{:S(2)}, u32[]{:S(2)}) collective-permute-start(bf16[576,256]{1,0:T(8,128)(2,1)S(1)} %select_convert_fusion.3), channel_id=1, source_target_pairs={{0,6},{1,7},{2,4},{3,5},{4,2},{5,3},{6,0},{7,1},{8,14},{9,15},{10,... | collective-permute-start | bytes 884744 | tf_op jit(solution)/shard_map/ppermute | solution.py:76
  188.5 5.1 %collective-permute-start.10 = (bf16[288,256]{1,0:T(8,128)(2,1)S(1)}, bf16[288,256]{1,0:T(8,128)(2,1)S(1)}, u32[]{:S(2)}, u32[]{:S(2)}) collective-permute-start(bf16[288,256]{1,0:T(8,128)(2,1)S(1)} %select_convert_fusion.7), channel_id=1, source_target_pairs={{0,2},{1,3},{2,0},{3,1},{4,6},{5,7},{6,4},{7,5},{8,10},{9,11},{10,... | collective-permute-start | bytes 442376 | tf_op jit(solution)/shard_map/ppermute | solution.py:76
  193.7 4.5 %collective-permute-start.11 = (bf16[144,256]{1,0:T(8,128)(2,1)S(1)}, bf16[144,256]{1,0:T(8,128)(2,1)S(1)}, u32[]{:S(2)}, u32[]{:S(2)}) collective-permute-start(bf16[144,256]{1,0:T(8,128)(2,1)S(1)} %select_convert_fusion.9), channel_id=1, source_target_pairs={{0,24},{1,25},{2,26},{3,27},{4,28},{5,29},{6,30},{7,31},{8,16},{9,... | collective-permute-start | bytes 221192 | tf_op jit(solution)/shard_map/ppermute | solution.py:76
  198.2 2.9 %collective-permute-start.12 = (bf16[72,256]{1,0:T(8,128)(2,1)S(1)}, bf16[72,256]{1,0:T(8,128)(2,1)S(1)}, u32[]{:S(2)}, u32[]{:S(2)}) collective-permute-start(bf16[72,256]{1,0:T(8,128)(2,1)S(1)} %select_convert_fusion.11), channel_id=1, source_target_pairs={{0,8},{1,9},{2,10},{3,11},{4,12},{5,13},{6,14},{7,15},{8,0},{9,1},... | collective-permute-start | bytes 110600 | tf_op jit(solution)/shard_map/ppermute | solution.py:76
  235.0 8.6 %collective-permute-start.18 = (bf16[2,1152,256]{2,1,0:T(8,128)(2,1)S(1)}, bf16[2,1152,256]{2,1,0:T(8,128)(2,1)S(1)}, u32[]{:S(2)}, u32[]{:S(2)}) collective-permute-start(bf16[2,1152,256]{2,1,0:T(8,128)(2,1)S(1)} %bitcast.147), channel_id=1, source_target_pairs={{0,1},{1,0},{2,3},{3,2},{4,5},{5,4},{6,7},{7,6},{8,9},{9,8},{10,11... | collective-permute-start | bytes 3538952 | tf_op jit(solution)/shard_map/ppermute | solution.py:86

commit v3 on v2

--- a/solution.py
+++ b/solution.py
@@ -45,18 +45,29 @@
     return jnp.concatenate([jnp.where(even, s2, s1), wide, jnp.where(even, s1, s2)], axis=1)
 
 
-def seam_swap(row_strip, col_strip, select, mirror):
+def seam_send(row_strip, col_strip, mirror):
     length, channels = row_strip.shape[1:]
     mine = jnp.stack([row_strip, col_strip], axis=1)
     back = mine[:, :, ::-1]
     rel = jnp.arange(4, dtype=jnp.int32) ^ mirror
     reverse = jnp.stack([rel % 2, rel // 2], axis=1) == 1
     send = jnp.where(reverse[:, None, :, None, None], back[None], mine[None])
-    send = jnp.broadcast_to(send[None], (4,) + send.shape).reshape(16, 6 * length, channels)
-    got = lax.all_to_all(send, AXES, 0, 0, axis_index_groups=SEAM_GROUPS)
-    got = got.reshape(96, length * channels)
+    return jnp.broadcast_to(send[None], (4,) + send.shape).reshape(16, 6 * length, channels)
+
+
+def seam_take(got, select):
+    channels = got.shape[-1]
+    got = got.reshape(96, -1)
     out = jnp.dot(select.astype(BF16), got, preferred_element_type=F32)
-    return out.reshape(3, 2, length, channels)
+    return out.reshape(3, 2, -1, channels)
+
+
+def seam_exchange(send):
+    return lax.all_to_all(send, AXES, 0, 0, axis_index_groups=SEAM_GROUPS)
+
+
+def seam_swap(row_strip, col_strip, select, mirror):
+    return seam_take(seam_exchange(seam_send(row_strip, col_strip, mirror)), select)
 
 
 def patches_of(padded, length):
@@ -78,9 +89,21 @@
     return grad
 
 
-def gather_sum(part, core):
+def scatter_sum_bulk(grad, bits):
+    low, high = grad[:1152], grad[1152:]
+    up = bits["core"] == 1
+    payload = jnp.where(up, low, high).astype(BF16)
+    got = lax.ppermute(payload, "core", [(0, 1), (1, 0)])
+    grad = (jnp.where(up, high, low) + got.astype(F32)).astype(BF16).reshape(16, 72, 256)
+    return lax.all_to_all(grad, ("y", "x"), 0, 0).astype(F32).sum(0)
+
+
+def across_sum(part):
     part = jnp.broadcast_to(part.astype(BF16), (8,) + part.shape)
-    part = lax.all_to_all(part, ("face", "zh"), 0, 0).astype(F32).sum(0).astype(BF16)
+    return lax.all_to_all(part, ("face", "zh"), 0, 0).astype(F32).sum(0).astype(BF16)
+
+
+def gather_pieces(part, core):
     part = lax.all_to_all(jnp.broadcast_to(part, (16,) + part.shape), ("y", "x"), 0, 0)
     part = part.transpose(1, 0, 2, 3).reshape(2, 1152, 256)
     got = lax.ppermute(part, "core", [(0, 1), (1, 0)])
@@ -196,14 +219,21 @@
     near = halo(delta_two.reshape(3, 8, 8, channels), 2, row, col)
     scale = 1.0 / math.sqrt(12 * 64 * 64)
     back = jnp.dot(patches_of(near, 10), back_two, preferred_element_type=F32)
-    grad_two, back = lax.optimization_barrier((grad_two, back))
-    part_two = scatter_sum(grad_two * scale, bits)
+    part_two = scatter_sum_bulk(grad_two * scale, bits)
     back = back.astype(BF16).reshape(3, 10, 10, channels)
     row_strip = jnp.where(cols_in[:, None], edge_row(back, 0, 9), 0)
     col_strip = jnp.where(rows_in[:, None], edge_col(back, 0, 9), 0)
-    strips = seam_swap(row_strip, col_strip, add_sel, mirror)
-    hidden_grad = add_edges(back.astype(F32), strips, 1)
+    send = seam_send(row_strip, col_strip, mirror)
+    send, part_two = lax.optimization_barrier((send, part_two))
+    got = seam_exchange(send)
+    got, part_two = lax.optimization_barrier((got, part_two))
+    part_two = across_sum(part_two)
+    hidden_grad = add_edges(back.astype(F32), seam_take(got, add_sel), 1)
     delta_one = jnp.where(mask, hidden_grad * slope_of(pre_one), 0.0).astype(BF16)
+    wide = jnp.pad(delta_one, ((0, 0), (1, 1), (1, 1), (0, 0)))
+    back = jnp.dot(patches_of(wide, 10), back_one, preferred_element_type=F32)
+    back = back.astype(BF16).reshape(3, 10, 10, channels)
+    send = seam_send(edge_row(back, 0, 9)[:, 1:9], edge_col(back, 0, 9)[:, 1:9], mirror)
     own = patches_in.reshape(3, 10, 10, 9 * channels)[:, 1:9, 1:9].reshape(192, 9 * channels)
     grad_one = lax.dot_general(
         own,
@@ -211,17 +241,13 @@
         contract_rows,
         preferred_element_type=F32,
     )
-    wide = jnp.pad(delta_one, ((0, 0), (1, 1), (1, 1), (0, 0)))
-    back = jnp.dot(patches_of(wide, 10), back_one, preferred_element_type=F32)
-    back = back.astype(BF16).reshape(3, 10, 10, channels)
-    strips = seam_swap(
-        edge_row(back, 0, 9)[:, 1:9], edge_col(back, 0, 9)[:, 1:9], add_sel, mirror
-    )
-    input_grad = add_edges(back[:, 1:9, 1:9].astype(F32), strips, 0).astype(BF16)
-
+    send, grad_one, part_two = lax.optimization_barrier((send, grad_one, part_two))
+    got = seam_exchange(send)
     part_one = scatter_sum(grad_one * scale, bits)
-    part, input_grad = lax.optimization_barrier((jnp.stack([part_one, part_two]), input_grad))
-    total = gather_sum(part, core)
+    got, part_one = lax.optimization_barrier((got, part_one))
+    input_grad = add_edges(back[:, 1:9, 1:9].astype(F32), seam_take(got, add_sel), 0).astype(BF16)
+    part_one = across_sum(part_one)
+    total = gather_pieces(jnp.stack([part_one, part_two]), core)
     shape = (3, 3, channels, channels)
     return (input_grad[:, None], total[0].reshape(shape), total[1].reshape(shape))
 

time: 250 us -> 276 us (1.10)
  waiting for transfers between devices: 76.7 us -> 105 us
  local copies, waits for them, and re-layouts: 27.1 us -> 31.4 us
  other arithmetic: 21.2 us -> 17.3 us
    all_to_all x4 -> x6, waiting for transfers between devices: 53.2 us -> 82.9 us  [the longest x4 68.4 us: seam_exchange(): return lax.all_to_all(send, AXES, 0, 0, axis_index_groups=SEAM_GROUPS)]
    all_to_all x4 -> x6, starting transfers between devices: 30.1 us -> 54.3 us  [the longest x4 32.6 us: seam_exchange(): return lax.all_to_all(send, AXES, 0, 0, axis_index_groups=SEAM_GROUPS)]
    ppermute x10 -> x5, starting transfers between devices: 22.3 us -> 4.82 us  [scatter_sum(): got = lax.ppermute(payload, TILE, [(t, t ^ mask) for t in range(64)])]
    unnamed x86 -> x56, local copies, waits for them, and re-layouts: 5.53 us -> 9.19 us
    ppermute x2, starting transfers between devices: 7.37 us -> 4.46 us  [halo(): s1 = lax.ppermute(jnp.where(even, down, up), TILE, EVEN_ROWS)]
    ppermute x10 -> x5, waiting for transfers between devices: 20.4 us -> 17.6 us  [scatter_sum(): got = lax.ppermute(payload, TILE, [(t, t ^ mask) for t in range(64)])]
    ppermute x1 -> x2, starting transfers between devices: 6.13 us -> 3.49 us  [the longest x1 3.21 us: gather_pieces(): got = lax.ppermute(part, 'core', [(0, 1), (1, 0)])]
    reshape x10 -> x9, local copies, waits for them, and re-layouts: 6.22 us -> 4.29 us  [the longest x5 2.31 us: seam_send(): jnp.broadcast_to(send[None], (4,) + send.shape)]
  transfers between devices with their start and end apart: 23 -> 21, of which waited for: 10 -> 14; matrix products, arithmetic and copies ran while one was open for 14% -> 11% of each run, Pallas kernels for 0% -> 0%
where the time goes in v3:
time: 276 us; the launch traced here: 275 us
  waiting for transfers between devices  105 us (38%)
  starting transfers between devices  75.1 us (27%)
  blocking collectives  32.3 us (12%)
  local copies, waits for them, and re-layouts  31.4 us (11%)
  other arithmetic  17.3 us (6%)
  matrix products  11.5 us (4%)
    all_to_all x4, waiting for transfers between devices, seam_exchange(): return lax.all_to_all(send, AXES, 0, 0, axis_index_groups=SEAM_GROUPS)  68.4 us
    all_to_all x4, starting transfers between devices, seam_exchange(): return lax.all_to_all(send, AXES, 0, 0, axis_index_groups=SEAM_GROUPS)  32.6 us
    all_to_all x1, blocking collectives, gather_pieces(): lax.all_to_all(jnp.broadcast_to(part, (16,) + part.shape), ('y', 'x'), 0, 0)  19.4 us
    all_to_all x1, starting transfers between devices, scatter_sum_bulk(): return lax.all_to_all(grad, ('y', 'x'), 0, 0).astype(F32).sum(0)  18.3 us
    ppermute x5, waiting for transfers between devices, scatter_sum(): got = lax.ppermute(payload, TILE, [(t, t ^ mask) for t in range(64)])  17.6 us
    all_to_all x1, blocking collectives, across_sum(): lax.all_to_all(part, ('face', 'zh'), 0, 0).astype(F32).sum(0).astype(BF16)  12.9 us
    all_to_all x1, waiting for transfers between devices, scatter_sum_bulk(): return lax.all_to_all(grad, ('y', 'x'), 0, 0).astype(F32).sum(0)  10.1 us
    unnamed x56, local copies, waits for them, and re-layouts  9.19 us
  transfers between devices with their start and end apart: 21, of which 14 were waited for; matrix products, arithmetic and copies ran while one was open for 11% of the time, Pallas kernels for 0%

profile of v3, /device:TPU:1, one launch (start us, length us, event | category | flops | bytes accessed | tf_op | source)
XLA Modules:
  0.0 274.8 jit_solution(3999794674385688683)
XLA Ops:
  0.6 1.0 broadcast_select_fusion.17
  1.7 4.6 %collective-permute-start = (bf16[3,8,2,256]{3,2,1,0:T(2,128)(2,1)S(1)}, bf16[3,8,2,256]{3,2,1,0:T(2,128)(2,1)S(1)}, u32[]{:S(2)}, u32[]{:S(2)}) collective-permute-start(bf16[3,8,2,256]{3,2,1,0:T(2,128)(2,1)S(1)} %get-tuple-element.65), channel_id=1, source_target_pairs={{1,2},{3,4},{5,6},{9,10},{11,12},{13,14},{17,18},{19,20},{21,22},{... | collective-permute-start | bytes 73736 | tf_op jit(solution)/shard_map/ppermute | solution.py:39
  8.9 0.8 broadcast_select_fusion.25
  10.4 3.8 %collective-permute-start.3 = (bf16[3,2,12,256]{3,2,1,0:T(8,128)(2,1)S(1)}, bf16[3,2,12,256]{3,2,1,0:T(8,128)(2,1)S(1)}, u32[]{:S(2)}, u32[]{:S(2)}) collective-permute-start(bf16[3,2,12,256]{3,2,1,0:T(8,128)(2,1)S(1)} %get-tuple-element.58), channel_id=1, source_target_pairs={{0,8},{1,9},{2,10},{3,11},{4,12},{5,13},{6,14},{7,15},{16,24},{17,... | collective-permute-start | bytes 110600 | tf_op jit(solution)/shard_map/ppermute | solution.py:43
  15.7 1.0 pad_maximum_fusion
  17.4 1.0 copy.284
  18.4 11.8 %all-to-all-start = ((bf16[16,72,256]{2,1,0:T(8,128)(2,1)}), bf16[16,72,256]{2,1,0:T(8,128)(2,1)S(1)}, u32[]{:S(2)}, u32[]{:S(2)}) async-start(bf16[16,72,256]{2,1,0:T(8,128)(2,1)} %copy.284), calls=%async_computation | async-start | bytes 1179648 | tf_op jit(solution)/shard_map/all_to_all | solution.py:66
  30.8 19.0 %all-to-all-done = bf16[16,72,256]{2,1,0:T(8,128)(2,1)S(1)} async-done(((bf16[16,72,256]{2,1,0:T(8,128)(2,1)}), bf16[16,72,256]{2,1,0:T(8,128)(2,1)S(1)}, u32[]{:S(2)}, u32[]{:S(2)}) %all-to-all-start) | async-done | bytes 589856 | tf_op jit(solution)/shard_map/all_to_all | solution.py:66
  52.2 1.5 select_convert_fusion.4
  54.4 0.9 copy.290
  55.3 5.9 %all-to-all-start.1 = ((bf16[16,60,256]{2,1,0:T(8,128)(2,1)}), bf16[16,60,256]{2,1,0:T(8,128)(2,1)S(1)}, u32[]{:S(2)}, u32[]{:S(2)}) async-start(bf16[16,60,256]{2,1,0:T(8,128)(2,1)} %copy.290), calls=%async_computation.1 | async-start | bytes 1048576 | tf_op jit(solution)/shard_map/all_to_all | solution.py:66
  62.0 1.1 rev.20
  63.2 16.2 %all-to-all-done.1 = bf16[16,60,256]{2,1,0:T(8,128)(2,1)S(1)} async-done(((bf16[16,60,256]{2,1,0:T(8,128)(2,1)}), bf16[16,60,256]{2,1,0:T(8,128)(2,1)S(1)}, u32[]{:S(2)}, u32[]{:S(2)}) %all-to-all-start.1) | async-done | bytes 491552 | tf_op jit(solution)/shard_map/all_to_all | solution.py:66
  81.7 1.9 collective-permute-start.4
  84.2 2.6 collective-permute-done.4
  88.6 1.3 collective-permute-done.7
  90.9 0.8 slice_dynamic-update-slice_fusion.7
  96.9 3.6 %reshape.556 = bf16[300,2304]{1,0:T(8,128)(2,1)} reshape(bf16[3,10,10,2304]{3,2,1,0:T(8,128)(2,1)} %slice_dynamic-update-slice_fusion) | data formatting | bytes 2764800 | tf_op jit(solution)/shard_map/reshape | solution.py:75
  100.5 2.2 convolution_convert_fusion.1
  102.9 2.1 add_convert_fusion
  105.0 18.3 %all-to-all-start.2 = ((bf16[16,72,256]{2,1,0:T(8,128)(2,1)}), bf16[16,72,256]{2,1,0:T(8,128)(2,1)S(1)}, u32[]{:S(2)}, u32[]{:S(2)}) async-start(bf16[16,72,256]{2,1,0:T(8,128)(2,1)} %bitcast.29), calls=%async_computation.2 | async-start | bytes 1179648 | tf_op jit(solution)/shard_map/all_to_all | solution.py:98
  123.9 10.1 %all-to-all-done.2 = bf16[16,72,256]{2,1,0:T(8,128)(2,1)S(1)} async-done(((bf16[16,72,256]{2,1,0:T(8,128)(2,1)}), bf16[16,72,256]{2,1,0:T(8,128)(2,1)S(1)}, u32[]{:S(2)}, u32[]{:S(2)}) %all-to-all-start.2) | async-done | bytes 589856 | tf_op jit(solution)/shard_map/all_to_all | solution.py:98
  134.1 0.9 copy.303
  135.0 6.7 %all-to-all-start.3 = ((bf16[16,60,256]{2,1,0:T(8,128)(2,1)}), bf16[16,60,256]{2,1,0:T(8,128)(2,1)S(1)}, u32[]{:S(2)}, u32[]{:S(2)}) async-start(bf16[16,60,256]{2,1,0:T(8,128)(2,1)} %copy.303), calls=%async_computation.3 | async-start | bytes 1048576 | tf_op jit(solution)/shard_map/all_to_all | solution.py:66
  143.1 0.9 select_reduce_fusion
  144.8 1.1 rev.22
  146.0 17.3 %all-to-all-done.3 = bf16[16,60,256]{2,1,0:T(8,128)(2,1)S(1)} async-done(((bf16[16,60,256]{2,1,0:T(8,128)(2,1)}), bf16[16,60,256]{2,1,0:T(8,128)(2,1)S(1)}, u32[]{:S(2)}, u32[]{:S(2)}) %all-to-all-start.3) | async-done | bytes 491552 | tf_op jit(solution)/shard_map/all_to_all | solution.py:66
  165.4 1.5 reshape.562
  166.9 2.2 convolution_convert_fusion
  170.2 3.4 %all-to-all-start.4 = ((bf16[8,72,256]{2,1,0:T(8,128)(2,1)}), bf16[8,72,256]{2,1,0:T(8,128)(2,1)S(1)}, u32[]{:S(2)}, u32[]{:S(2)}) async-start(bf16[8,72,256]{2,1,0:T(8,128)(2,1)} %broadcast_in_dim.467), calls=%async_computation.4 | async-start | bytes 589824 | tf_op jit(solution)/shard_map/all_to_all | solution.py:103
  173.7 3.5 %convolution_bitcast_fusion = f32[2304,256]{1,0:T(8,128)} fusion(bf16[3,10,10,2304]{3,2,1,0:T(8,128)(2,1)} %copy-done.8, bf16[3,10,10,256]{3,2,1,0:T(8,128)(2,1)S(1)} %select_convert_fusion.3), kind=kOutput, calls=%fused_computation.1 | convolution fusion | flops 226492416 | bytes 3342336 | tf_op jit(solution)/shard_map/dot_general | solution.py:238
  177.3 4.4 %all-to-all-done.4 = bf16[8,72,256]{2,1,0:T(8,128)(2,1)S(1)} async-done(((bf16[8,72,256]{2,1,0:T(8,128)(2,1)}), bf16[8,72,256]{2,1,0:T(8,128)(2,1)S(1)}, u32[]{:S(2)}, u32[]{:S(2)}) %all-to-all-start.4) | async-done | bytes 294944 | tf_op jit(solution)/shard_map/all_to_all | solution.py:103
  182.3 0.8 broadcast_in_dim.466
  183.1 1.9 broadcast_multiply_fusion
  185.1 2.6 collective-permute-start.9
  187.7 1.8 collective-permute-done.9
  189.4 1.3 convert_add_fusion
  191.2 9.1 %collective-permute-done.10 = bf16[576,256]{1,0:T(8,128)(2,1)S(1)} collective-permute-done((bf16[576,256]{1,0:T(8,128)(2,1)S(1)}, bf16[576,256]{1,0:T(8,128)(2,1)S(1)}, u32[]{:S(2)}, u32[]{:S(2)}) %collective-permute-start.10) | collective-permute-done | bytes 294944 | tf_op jit(solution)/shard_map/ppermute | solution.py:87
  200.5 4.0 %collective-permute-done.11 = bf16[288,256]{1,0:T(8,128)(2,1)S(1)} collective-permute-done((bf16[288,256]{1,0:T(8,128)(2,1)S(1)}, bf16[288,256]{1,0:T(8,128)(2,1)S(1)}, u32[]{:S(2)}, u32[]{:S(2)}) %collective-permute-start.11) | collective-permute-done | bytes 147488 | tf_op jit(solution)/shard_map/ppermute | solution.py:87
  204.6 1.4 collective-permute-start.12
  206.0 8.3 %all-to-all-start.5 = ((bf16[16,48,256]{2,1,0:T(8,128)(2,1)}), bf16[16,48,256]{2,1,0:T(8,128)(2,1)S(1)}, u32[]{:S(2)}, u32[]{:S(2)}) async-start(bf16[16,48,256]{2,1,0:T(8,128)(2,1)} %bitcast.42), calls=%async_computation.5 | async-start | bytes 786432 | tf_op jit(solution)/shard_map/all_to_all | solution.py:66
  214.6 2.8 %collective-permute-done.13 = bf16[72,256]{1,0:T(8,128)(2,1)S(1)} collective-permute-done((bf16[72,256]{1,0:T(8,128)(2,1)S(1)}, bf16[72,256]{1,0:T(8,128)(2,1)S(1)}, u32[]{:S(2)}, u32[]{:S(2)}) %collective-permute-start.13) | collective-permute-done | bytes 36896 | tf_op jit(solution)/shard_map/ppermute | solution.py:87
  217.5 16.0 %all-to-all-done.5 = bf16[16,48,256]{2,1,0:T(8,128)(2,1)S(1)} async-done(((bf16[16,48,256]{2,1,0:T(8,128)(2,1)}), bf16[16,48,256]{2,1,0:T(8,128)(2,1)S(1)}, u32[]{:S(2)}, u32[]{:S(2)}) %all-to-all-start.5) | async-done | bytes 393248 | tf_op jit(solution)/shard_map/all_to_all | solution.py:66
  233.4 12.9 %all_to_all.40 = bf16[8,72,256]{2,1,0:T(8,128)(2,1)S(1)} all-to-all(bf16[8,72,256]{2,1,0:T(8,128)(2,1)S(1)} %broadcast_in_dim.475), channel_id=1, replica_groups=mesh['face'=4,'zh'=2,'x'=4,'y'=4,'core'=2] {'face','zh'}, dimensions={0} | all-to-all | bytes 589824 | tf_op jit(solution)/shard_map/all_to_all | solution.py:103
  246.5 19.4 %all_to_all.41 = bf16[16,2,72,256]{3,2,1,0:T(8,128)(2,1)S(1)} all-to-all(bf16[16,2,72,256]{3,2,1,0:T(8,128)(2,1)S(1)} %broadcast_in_dim.476), channel_id=1, replica_groups=mesh['face'=4,'zh'=2,'x'=4,'y'=4,'core'=2] {'y','x'}, dimensions={0} | all-to-all | bytes 2359296 | tf_op jit(solution)/shard_map/all_to_all | solution.py:107
  266.0 3.2 %collective-permute-start.14 = (bf16[2,1152,256]{2,1,0:T(8,128)(2,1)S(1)}, bf16[2,1152,256]{2,1,0:T(8,128)(2,1)S(1)}, u32[]{:S(2)}, u32[]{:S(2)}) collective-permute-start(bf16[2,1152,256]{2,1,0:T(8,128)(2,1)S(1)} %bitcast.145), channel_id=1, source_target_pairs={{0,1},{1,0},{2,3},{3,2},{4,5},{5,4},{6,7},{7,6},{8,9},{9,8},{10,11... | collective-permute-start | bytes 3538952 | tf_op jit(solution)/shard_map/ppermute | solution.py:109
  269.7 1.7 fusion.6
  272.3 2.5 fusion.27
  (212 shorter events, 30.0 us)
Async XLA Ops:
  1.7 7.2 %collective-permute-start = (bf16[3,8,2,256]{3,2,1,0:T(2,128)(2,1)S(1)}, bf16[3,8,2,256]{3,2,1,0:T(2,128)(2,1)S(1)}, u32[]{:S(2)}, u32[]{:S(2)}) collective-permute-start(bf16[3,8,2,256]{3,2,1,0:T(2,128)(2,1)S(1)} %get-tuple-element.65), channel_id=1, source_target_pairs={{1,2},{3,4},{5,6},{9,10},{11,12},{13,14},{17,18},{19,20},{21,22},{... | collective-permute-start | bytes 73736 | tf_op jit(solution)/shard_map/ppermute | solution.py:39
  6.3 2.6 collective-permute-start.1
  9.7 5.2 %collective-permute-start.2 = (bf16[3,2,12,256]{3,2,1,0:T(8,128)(2,1)S(1)}, bf16[3,2,12,256]{3,2,1,0:T(8,128)(2,1)S(1)}, u32[]{:S(2)}, u32[]{:S(2)}) collective-permute-start(bf16[3,2,12,256]{3,2,1,0:T(8,128)(2,1)S(1)} %get-tuple-element.57), channel_id=1, source_target_pairs={{8,16},{9,17},{10,18},{11,19},{12,20},{13,21},{14,22},{15,23},{24,... | collective-permute-start | bytes 110600 | tf_op jit(solution)/shard_map/ppermute | solution.py:44
  10.4 5.2 %collective-permute-start.3 = (bf16[3,2,12,256]{3,2,1,0:T(8,128)(2,1)S(1)}, bf16[3,2,12,256]{3,2,1,0:T(8,128)(2,1)S(1)}, u32[]{:S(2)}, u32[]{:S(2)}) collective-permute-start(bf16[3,2,12,256]{3,2,1,0:T(8,128)(2,1)S(1)} %get-tuple-element.58), channel_id=1, source_target_pairs={{0,8},{1,9},{2,10},{3,11},{4,12},{5,13},{6,14},{7,15},{16,24},{17,... | collective-permute-start | bytes 110600 | tf_op jit(solution)/shard_map/ppermute | solution.py:43
  17.4 33.3 %copy-start = (bf16[3,1,8,8,256]{4,3,2,1,0:T(8,128)(2,1)S(1)}, bf16[3,1,8,8,256]{4,3,2,1,0:T(8,128)(2,1)}, u32[]{:S(2)}) copy-start(bf16[3,1,8,8,256]{4,3,2,1,0:T(8,128)(2,1)} %param.6) | copy-start | bytes 294916
  18.4 31.3 %all-to-all-start = ((bf16[16,72,256]{2,1,0:T(8,128)(2,1)}), bf16[16,72,256]{2,1,0:T(8,128)(2,1)S(1)}, u32[]{:S(2)}, u32[]{:S(2)}) async-start(bf16[16,72,256]{2,1,0:T(8,128)(2,1)} %copy.284), calls=%async_computation | async-start | bytes 1179648 | tf_op jit(solution)/shard_map/all_to_all | solution.py:66
  51.0 1.3 copy-start.2
  51.5 2.2 copy-start.8
  53.7 7.5 %copy-start.1 = (bf16[3,3,256,256]{3,2,1,0:T(8,128)(2,1)S(1)}, bf16[3,3,256,256]{3,2,1,0:T(8,128)(2,1)}, u32[]{:S(2)}) copy-start(bf16[3,3,256,256]{3,2,1,0:T(8,128)(2,1)} %param.9) | copy-start | bytes 3538948
  55.3 24.1 %all-to-all-start.1 = ((bf16[16,60,256]{2,1,0:T(8,128)(2,1)}), bf16[16,60,256]{2,1,0:T(8,128)(2,1)S(1)}, u32[]{:S(2)}, u32[]{:S(2)}) async-start(bf16[16,60,256]{2,1,0:T(8,128)(2,1)} %copy.290), calls=%async_computation.1 | async-start | bytes 1048576 | tf_op jit(solution)/shard_map/all_to_all | solution.py:66
  80.0 1.1 copy-start.7
  81.7 5.1 %collective-permute-start.4 = (bf16[3,8,2,256]{3,2,1,0:T(2,128)(2,1)S(1)}, bf16[3,8,2,256]{3,2,1,0:T(2,128)(2,1)S(1)}, u32[]{:S(2)}, u32[]{:S(2)}) collective-permute-start(bf16[3,8,2,256]{3,2,1,0:T(2,128)(2,1)S(1)} %get-tuple-element.61), channel_id=1, source_target_pairs={{1,2},{3,4},{5,6},{9,10},{11,12},{13,14},{17,18},{19,20},{21,22},{... | collective-permute-start | bytes 73736 | tf_op jit(solution)/shard_map/ppermute | solution.py:39
  83.6 3.2 %collective-permute-start.5 = (bf16[3,8,2,256]{3,2,1,0:T(2,128)(2,1)S(1)}, bf16[3,8,2,256]{3,2,1,0:T(2,128)(2,1)S(1)}, u32[]{:S(2)}, u32[]{:S(2)}) collective-permute-start(bf16[3,8,2,256]{3,2,1,0:T(2,128)(2,1)S(1)} %get-tuple-element.62), channel_id=1, source_target_pairs={{0,1},{1,0},{2,3},{3,2},{4,5},{5,4},{6,7},{7,6},{8,9},{9,8},{10,11... | collective-permute-start | bytes 73736 | tf_op jit(solution)/shard_map/ppermute | solution.py:38
  86.9 3.0 %collective-permute-start.7 = (bf16[3,2,12,256]{3,2,1,0:T(8,128)(2,1)S(1)}, bf16[3,2,12,256]{3,2,1,0:T(8,128)(2,1)S(1)}, u32[]{:S(2)}, u32[]{:S(2)}) collective-permute-start(bf16[3,2,12,256]{3,2,1,0:T(8,128)(2,1)S(1)} %get-tuple-element.55), channel_id=1, source_target_pairs={{0,8},{1,9},{2,10},{3,11},{4,12},{5,13},{6,14},{7,15},{16,24},{17,... | collective-permute-start | bytes 110600 | tf_op jit(solution)/shard_map/ppermute | solution.py:43
  87.6 2.3 collective-permute-start.6
  88.4 14.6 %collective-permute-start.8 = (bf16[1152,256]{1,0:T(8,128)(2,1)S(1)}, bf16[1152,256]{1,0:T(8,128)(2,1)}, u32[]{:S(2)}, u32[]{:S(2)}) collective-permute-start(bf16[1152,256]{1,0:T(8,128)(2,1)S(1)} %select_convert_fusion.1), channel_id=1, source_target_pairs={{0,1},{1,0},{2,3},{3,2},{4,5},{5,4},{6,7},{7,6},{8,9},{9,8},{10,11... | collective-permute-start | bytes 1769480 | tf_op jit(solution)/shard_map/ppermute | solution.py:96
  105.0 29.0 %all-to-all-start.2 = ((bf16[16,72,256]{2,1,0:T(8,128)(2,1)}), bf16[16,72,256]{2,1,0:T(8,128)(2,1)S(1)}, u32[]{:S(2)}, u32[]{:S(2)}) async-start(bf16[16,72,256]{2,1,0:T(8,128)(2,1)} %bitcast.29), calls=%async_computation.2 | async-start | bytes 1179648 | tf_op jit(solution)/shard_map/all_to_all | solution.py:98
  123.5 18.3 %copy-start.9 = (s32[12,4]{0,1:T(4,128)S(1)}, s32[12,4]{0,1:T(4,128)}, u32[]{:S(2)}) copy-start(s32[12,4]{0,1:T(4,128)} %param.10) | copy-start | bytes 580
  123.7 18.3 %copy-start.3 = (bf16[3,3,256,256]{3,2,1,0:T(8,128)(2,1)S(1)}, bf16[3,3,256,256]{3,2,1,0:T(8,128)(2,1)}, u32[]{:S(2)}) copy-start(bf16[3,3,256,256]{3,2,1,0:T(8,128)(2,1)} %param.8) | copy-start | bytes 3538948
  135.0 28.2 %all-to-all-start.3 = ((bf16[16,60,256]{2,1,0:T(8,128)(2,1)}), bf16[16,60,256]{2,1,0:T(8,128)(2,1)S(1)}, u32[]{:S(2)}, u32[]{:S(2)}) async-start(bf16[16,60,256]{2,1,0:T(8,128)(2,1)} %copy.303), calls=%async_computation.3 | async-start | bytes 1048576 | tf_op jit(solution)/shard_map/all_to_all | solution.py:66
  145.9 18.6 %copy-start.5 = (f32[3,10,10,256]{3,2,1,0:T(8,128)S(1)}, f32[3,10,10,256]{3,2,1,0:T(8,128)}, u32[]{:S(2)}) copy-start(f32[3,10,10,256]{3,2,1,0:T(8,128)} %get-tuple-element.80) | copy-start | bytes 921604
  169.2 8.0 %copy-start.4 = (bf16[3,10,10,256]{3,2,1,0:T(8,128)(2,1)}, bf16[3,10,10,256]{3,2,1,0:T(8,128)(2,1)S(1)}, u32[]{:S(2)}) copy-start(bf16[3,10,10,256]{3,2,1,0:T(8,128)(2,1)S(1)} %reshape.564) | copy-start | bytes 460804
  170.2 11.4 %all-to-all-start.4 = ((bf16[8,72,256]{2,1,0:T(8,128)(2,1)}), bf16[8,72,256]{2,1,0:T(8,128)(2,1)S(1)}, u32[]{:S(2)}, u32[]{:S(2)}) async-start(bf16[8,72,256]{2,1,0:T(8,128)(2,1)} %broadcast_in_dim.467), calls=%async_computation.4 | async-start | bytes 589824 | tf_op jit(solution)/shard_map/all_to_all | solution.py:103
  185.1 4.4 %collective-permute-start.9 = (bf16[1152,256]{1,0:T(8,128)(2,1)S(1)}, bf16[1152,256]{1,0:T(8,128)(2,1)}, u32[]{:S(2)}, u32[]{:S(2)}) collective-permute-start(bf16[1152,256]{1,0:T(8,128)(2,1)S(1)} %select_convert_fusion), channel_id=1, source_target_pairs={{0,1},{1,0},{2,3},{3,2},{4,5},{5,4},{6,7},{7,6},{8,9},{9,8},{10,11... | collective-permute-start | bytes 1769480 | tf_op jit(solution)/shard_map/ppermute | solution.py:87
  190.8 9.5 %collective-permute-start.10 = (bf16[576,256]{1,0:T(8,128)(2,1)S(1)}, bf16[576,256]{1,0:T(8,128)(2,1)S(1)}, u32[]{:S(2)}, u32[]{:S(2)}) collective-permute-start(bf16[576,256]{1,0:T(8,128)(2,1)S(1)} %select_convert_fusion.2), channel_id=1, source_target_pairs={{0,6},{1,7},{2,4},{3,5},{4,2},{5,3},{6,0},{7,1},{8,14},{9,15},{10,... | collective-permute-start | bytes 884744 | tf_op jit(solution)/shard_map/ppermute | solution.py:87
  200.4 46.0 %copy-start.6 = (bf16[72,256]{1,0:T(8,128)(2,1)S(1)}, bf16[72,256]{1,0:T(8,128)(2,1)}, u32[]{:S(2)}) copy-start(bf16[72,256]{1,0:T(8,128)(2,1)} %reduce_sum.74) | copy-start | bytes 110596
  200.4 4.1 %collective-permute-start.11 = (bf16[288,256]{1,0:T(8,128)(2,1)S(1)}, bf16[288,256]{1,0:T(8,128)(2,1)S(1)}, u32[]{:S(2)}, u32[]{:S(2)}) collective-permute-start(bf16[288,256]{1,0:T(8,128)(2,1)S(1)} %select_convert_fusion.5), channel_id=1, source_target_pairs={{0,2},{1,3},{2,0},{3,1},{4,6},{5,7},{6,4},{7,5},{8,10},{9,11},{10,... | collective-permute-start | bytes 442376 | tf_op jit(solution)/shard_map/ppermute | solution.py:87
  204.6 9.7 %collective-permute-start.12 = (bf16[144,256]{1,0:T(8,128)(2,1)S(1)}, bf16[144,256]{1,0:T(8,128)(2,1)S(1)}, u32[]{:S(2)}, u32[]{:S(2)}) collective-permute-start(bf16[144,256]{1,0:T(8,128)(2,1)S(1)} %select_convert_fusion.6), channel_id=1, source_target_pairs={{0,24},{1,25},{2,26},{3,27},{4,28},{5,29},{6,30},{7,31},{8,16},{9,... | collective-permute-start | bytes 221192 | tf_op jit(solution)/shard_map/ppermute | solution.py:87
  206.0 27.4 %all-to-all-start.5 = ((bf16[16,48,256]{2,1,0:T(8,128)(2,1)}), bf16[16,48,256]{2,1,0:T(8,128)(2,1)S(1)}, u32[]{:S(2)}, u32[]{:S(2)}) async-start(bf16[16,48,256]{2,1,0:T(8,128)(2,1)} %bitcast.42), calls=%async_computation.5 | async-start | bytes 786432 | tf_op jit(solution)/shard_map/all_to_all | solution.py:66
  214.3 3.1 %collective-permute-start.13 = (bf16[72,256]{1,0:T(8,128)(2,1)S(1)}, bf16[72,256]{1,0:T(8,128)(2,1)S(1)}, u32[]{:S(2)}, u32[]{:S(2)}) collective-permute-start(bf16[72,256]{1,0:T(8,128)(2,1)S(1)} %select_convert_fusion.7), channel_id=1, source_target_pairs={{0,8},{1,9},{2,10},{3,11},{4,12},{5,13},{6,14},{7,15},{8,0},{9,1},... | collective-permute-start | bytes 110600 | tf_op jit(solution)/shard_map/ppermute | solution.py:87
  266.0 5.7 %collective-permute-start.14 = (bf16[2,1152,256]{2,1,0:T(8,128)(2,1)S(1)}, bf16[2,1152,256]{2,1,0:T(8,128)(2,1)S(1)}, u32[]{:S(2)}, u32[]{:S(2)}) collective-permute-start(bf16[2,1152,256]{2,1,0:T(8,128)(2,1)S(1)} %bitcast.145), channel_id=1, source_target_pairs={{0,1},{1,0},{2,3},{3,2},{4,5},{5,4},{6,7},{7,6},{8,9},{9,8},{10,11... | collective-permute-start | bytes 3538952 | tf_op jit(solution)/shard_map/ppermute | solution.py:109

commit v4 on v3

--- a/solution.py
+++ b/solution.py
@@ -75,27 +75,14 @@
     return jnp.concatenate(views, axis=-1).reshape(-1, 9 * padded.shape[-1])
 
 
-HALVINGS = (("core", 1), ("y1", 6), ("y0", 2), ("x1", 24), ("x0", 8))
-
-
-def scatter_sum(grad, bits):
-    for name, mask in HALVINGS:
-        half = grad.shape[0] // 2
-        low, high = grad[:half], grad[half:]
-        up = bits[name] == 1
-        payload = jnp.where(up, low, high).astype(BF16)
-        got = lax.ppermute(payload, TILE, [(t, t ^ mask) for t in range(64)])
-        grad = jnp.where(up, high, low) + got.astype(F32)
-    return grad
-
-
-def scatter_sum_bulk(grad, bits):
-    low, high = grad[:1152], grad[1152:]
-    up = bits["core"] == 1
-    payload = jnp.where(up, low, high).astype(BF16)
+def scatter_sum(grads, core):
+    low = jnp.stack([grad[:1152] for grad in grads])
+    high = jnp.stack([grad[1152:] for grad in grads])
+    payload = jnp.where(core == 1, low, high).astype(BF16)
     got = lax.ppermute(payload, "core", [(0, 1), (1, 0)])
-    grad = (jnp.where(up, high, low) + got.astype(F32)).astype(BF16).reshape(16, 72, 256)
-    return lax.all_to_all(grad, ("y", "x"), 0, 0).astype(F32).sum(0)
+    part = (jnp.where(core == 1, high, low) + got.astype(F32)).astype(BF16)
+    part = part.reshape(2, 16, 72, 256).transpose(1, 0, 2, 3)
+    return part
 
 
 def across_sum(part):
@@ -214,20 +201,14 @@
     grad_two = lax.dot_general(
         patches_hidden, delta_two, contract_rows, preferred_element_type=F32
     )
-    y_at, x_at = lax.axis_index("y"), lax.axis_index("x")
-    bits = {"core": core, "y1": y_at // 2, "y0": y_at % 2, "x1": x_at // 2, "x0": x_at % 2}
     near = halo(delta_two.reshape(3, 8, 8, channels), 2, row, col)
     scale = 1.0 / math.sqrt(12 * 64 * 64)
     back = jnp.dot(patches_of(near, 10), back_two, preferred_element_type=F32)
-    part_two = scatter_sum_bulk(grad_two * scale, bits)
     back = back.astype(BF16).reshape(3, 10, 10, channels)
     row_strip = jnp.where(cols_in[:, None], edge_row(back, 0, 9), 0)
     col_strip = jnp.where(rows_in[:, None], edge_col(back, 0, 9), 0)
     send = seam_send(row_strip, col_strip, mirror)
-    send, part_two = lax.optimization_barrier((send, part_two))
     got = seam_exchange(send)
-    got, part_two = lax.optimization_barrier((got, part_two))
-    part_two = across_sum(part_two)
     hidden_grad = add_edges(back.astype(F32), seam_take(got, add_sel), 1)
     delta_one = jnp.where(mask, hidden_grad * slope_of(pre_one), 0.0).astype(BF16)
     wide = jnp.pad(delta_one, ((0, 0), (1, 1), (1, 1), (0, 0)))
@@ -241,13 +222,13 @@
         contract_rows,
         preferred_element_type=F32,
     )
-    send, grad_one, part_two = lax.optimization_barrier((send, grad_one, part_two))
     got = seam_exchange(send)
-    part_one = scatter_sum(grad_one * scale, bits)
-    got, part_one = lax.optimization_barrier((got, part_one))
+    part = scatter_sum((grad_one * scale, grad_two * scale), core)
+    got, part = lax.optimization_barrier((got, part))
     input_grad = add_edges(back[:, 1:9, 1:9].astype(F32), seam_take(got, add_sel), 0).astype(BF16)
-    part_one = across_sum(part_one)
-    total = gather_pieces(jnp.stack([part_one, part_two]), core)
+    part = lax.all_to_all(part, ("y", "x"), 0, 0).astype(F32).sum(0)
+    part = across_sum(part)
+    total = gather_pieces(part, core)
     shape = (3, 3, channels, channels)
     return (input_grad[:, None], total[0].reshape(shape), total[1].reshape(shape))
 

time: 276 us -> 260 us (0.942)
  waiting for transfers between devices: 105 us -> 66.1 us
  blocking collectives: 32.3 us -> 70.3 us
  starting transfers between devices: 75.1 us -> 48.5 us
  local copies, waits for them, and re-layouts: 31.4 us -> 37.8 us
  other arithmetic: 17.3 us -> 21.2 us
    all_to_all x0 -> x1, blocking collectives: none -> 34.5 us  [body(): part = lax.all_to_all(part, ('y', 'x'), 0, 0).astype(F32).sum(0)]
    all_to_all x2 -> x0, starting transfers between devices: 21.7 us -> none  [the longest x1 18.3 us: scatter_sum_bulk(): return lax.all_to_all(grad, ('y', 'x'), 0, 0).astype(F32).sum(0)]
    ppermute x6 -> x1, waiting for transfers between devices: 17.6 us -> 0.01 us  [scatter_sum(): got = lax.ppermute(payload, 'core', [(0, 1), (1, 0)])]
    all_to_all x2 -> x0, waiting for transfers between devices: 14.4 us -> none  [the longest x1 10.1 us: scatter_sum_bulk(): return lax.all_to_all(grad, ('y', 'x'), 0, 0).astype(F32).sum(0)]
    all_to_all x4, waiting for transfers between devices: 68.4 us -> 62.9 us  [seam_exchange(): return lax.all_to_all(send, AXES, 0, 0, axis_index_groups=SEAM_GROUPS)]
    ppermute x6 -> x1, starting transfers between devices: 5.09 us -> 0.01 us  [scatter_sum(): got = lax.ppermute(payload, 'core', [(0, 1), (1, 0)])]
    all_to_all x1, blocking collectives: 12.9 us -> 17.3 us  [across_sum(): lax.all_to_all(part, ('face', 'zh'), 0, 0).astype(F32).sum(0).astype(BF16)]
    unnamed x56 -> x84, local copies, waits for them, and re-layouts: 9.19 us -> 11 us
  transfers between devices with their start and end apart: 21 -> 14, of which waited for: 14 -> 6; matrix products, arithmetic and copies ran while one was open for 11% -> 8% of each run, Pallas kernels for 0% -> 0%
where the time goes in v4:
time: 260 us; the launch traced here: 258 us
  blocking collectives  70.3 us (27%)
  waiting for transfers between devices  66.1 us (25%)
  starting transfers between devices  48.5 us (19%)
  local copies, waits for them, and re-layouts  37.8 us (15%)
  other arithmetic  21.2 us (8%)
  matrix products  12.2 us (5%)
    all_to_all x4, waiting for transfers between devices, seam_exchange(): return lax.all_to_all(send, AXES, 0, 0, axis_index_groups=SEAM_GROUPS)  62.9 us
    all_to_all x1, blocking collectives, body(): part = lax.all_to_all(part, ('y', 'x'), 0, 0).astype(F32).sum(0)  34.5 us
    all_to_all x4, starting transfers between devices, seam_exchange(): return lax.all_to_all(send, AXES, 0, 0, axis_index_groups=SEAM_GROUPS)  30.1 us
    all_to_all x1, blocking collectives, gather_pieces(): lax.all_to_all(jnp.broadcast_to(part, (16,) + part.shape), ('y', 'x'), 0, 0)  18.4 us
    all_to_all x1, blocking collectives, across_sum(): lax.all_to_all(part, ('face', 'zh'), 0, 0).astype(F32).sum(0).astype(BF16)  17.3 us
    unnamed x84, local copies, waits for them, and re-layouts  11 us
    ppermute x2, starting transfers between devices, halo(): s2 = lax.ppermute(jnp.where(even, left, right), TILE, ODD_COLS)  6.52 us
    ppermute x1, starting transfers between devices, gather_pieces(): got = lax.ppermute(part, 'core', [(0, 1), (1, 0)])  5.36 us
  transfers between devices with their start and end apart: 14, of which 6 were waited for; matrix products, arithmetic and copies ran while one was open for 8% of the time, Pallas kernels for 0%

profile of v4, /device:TPU:1, one launch (start us, length us, event | category | flops | bytes accessed | tf_op | source)
XLA Modules:
  0.0 257.9 jit_solution(15986340134558447053)
XLA Ops:
  0.6 1.0 broadcast_select_fusion.17
  1.7 4.6 %collective-permute-start = (bf16[3,8,2,256]{3,2,1,0:T(2,128)(2,1)S(1)}, bf16[3,8,2,256]{3,2,1,0:T(2,128)(2,1)S(1)}, u32[]{:S(2)}, u32[]{:S(2)}) collective-permute-start(bf16[3,8,2,256]{3,2,1,0:T(2,128)(2,1)S(1)} %get-tuple-element.55), channel_id=1, source_target_pairs={{1,2},{3,4},{5,6},{9,10},{11,12},{13,14},{17,18},{19,20},{21,22},{... | collective-permute-start | bytes 73736 | tf_op jit(solution)/shard_map/ppermute | solution.py:39
  8.9 0.8 broadcast_select_fusion.25
  10.4 3.8 %collective-permute-start.3 = (bf16[3,2,12,256]{3,2,1,0:T(8,128)(2,1)S(1)}, bf16[3,2,12,256]{3,2,1,0:T(8,128)(2,1)S(1)}, u32[]{:S(2)}, u32[]{:S(2)}) collective-permute-start(bf16[3,2,12,256]{3,2,1,0:T(8,128)(2,1)S(1)} %get-tuple-element.48), channel_id=1, source_target_pairs={{0,8},{1,9},{2,10},{3,11},{4,12},{5,13},{6,14},{7,15},{16,24},{17,... | collective-permute-start | bytes 110600 | tf_op jit(solution)/shard_map/ppermute | solution.py:43
  15.7 1.0 pad_maximum_fusion.2
  17.4 1.0 copy.287
  18.4 11.8 %all-to-all-start = ((bf16[16,72,256]{2,1,0:T(8,128)(2,1)}), bf16[16,72,256]{2,1,0:T(8,128)(2,1)S(1)}, u32[]{:S(2)}, u32[]{:S(2)}) async-start(bf16[16,72,256]{2,1,0:T(8,128)(2,1)} %copy.287), calls=%async_computation | async-start | bytes 1179648 | tf_op jit(solution)/shard_map/all_to_all | solution.py:66
  30.8 18.9 %all-to-all-done = bf16[16,72,256]{2,1,0:T(8,128)(2,1)S(1)} async-done(((bf16[16,72,256]{2,1,0:T(8,128)(2,1)}), bf16[16,72,256]{2,1,0:T(8,128)(2,1)S(1)}, u32[]{:S(2)}, u32[]{:S(2)}) %all-to-all-start) | async-done | bytes 589856 | tf_op jit(solution)/shard_map/all_to_all | solution.py:66
  52.2 1.5 select_convert_fusion.2
  54.4 0.9 copy.293
  55.4 5.9 %all-to-all-start.1 = ((bf16[16,60,256]{2,1,0:T(8,128)(2,1)}), bf16[16,60,256]{2,1,0:T(8,128)(2,1)S(1)}, u32[]{:S(2)}, u32[]{:S(2)}) async-start(bf16[16,60,256]{2,1,0:T(8,128)(2,1)} %copy.293), calls=%async_computation.1 | async-start | bytes 1048576 | tf_op jit(solution)/shard_map/all_to_all | solution.py:66
  61.8 0.9 select_reduce_fusion
  62.7 16.7 %all-to-all-done.1 = bf16[16,60,256]{2,1,0:T(8,128)(2,1)S(1)} async-done(((bf16[16,60,256]{2,1,0:T(8,128)(2,1)}), bf16[16,60,256]{2,1,0:T(8,128)(2,1)S(1)}, u32[]{:S(2)}, u32[]{:S(2)}) %all-to-all-start.1) | async-done | bytes 491552 | tf_op jit(solution)/shard_map/all_to_all | solution.py:66
  81.1 0.9 copy-done.7
  82.0 1.1 fusion.5
  83.2 1.9 collective-permute-start.4
  85.9 2.5 collective-permute-done.4
  89.7 1.3 collective-permute-start.6
  92.5 0.8 broadcast_select_fusion.18
  94.1 1.5 reshape.556
  95.6 1.9 convolution_convert_fusion.1
  98.7 0.9 copy.306
  99.6 6.7 %all-to-all-start.2 = ((bf16[16,60,256]{2,1,0:T(8,128)(2,1)}), bf16[16,60,256]{2,1,0:T(8,128)(2,1)S(1)}, u32[]{:S(2)}, u32[]{:S(2)}) async-start(bf16[16,60,256]{2,1,0:T(8,128)(2,1)} %copy.306), calls=%async_computation.2 | async-start | bytes 1048576 | tf_op jit(solution)/shard_map/all_to_all | solution.py:66
  108.5 1.1 rev.22
  110.4 12.5 %all-to-all-done.2 = bf16[16,60,256]{2,1,0:T(8,128)(2,1)S(1)} async-done(((bf16[16,60,256]{2,1,0:T(8,128)(2,1)}), bf16[16,60,256]{2,1,0:T(8,128)(2,1)S(1)}, u32[]{:S(2)}, u32[]{:S(2)}) %all-to-all-start.2) | async-done | bytes 491552 | tf_op jit(solution)/shard_map/all_to_all | solution.py:66
  124.3 1.4 select_convert_fusion.1
  126.4 3.5 %fusion = f32[2304,256]{1,0:T(8,128)} fusion(bf16[3,10,10,2304]{3,2,1,0:T(8,128)(2,1)} %copy-done.12, bf16[3,10,10,256]{3,2,1,0:T(8,128)(2,1)S(1)} %select_convert_fusion.1), kind=kOutput, calls=%fused_computation.2 | convolution fusion | flops 227082240 | bytes 3342336 | tf_op jit(solution)/shard_map/dot_general | solution.py:219
  131.4 0.8 slice_dynamic-update-slice_fusion.22
  135.9 3.6 %reshape.561 = bf16[300,2304]{1,0:T(8,128)(2,1)} reshape(bf16[3,10,10,2304]{3,2,1,0:T(8,128)(2,1)} %slice_dynamic-update-slice_fusion.18) | data formatting | bytes 2764800 | tf_op jit(solution)/shard_map/reshape | solution.py:75
  139.5 2.6 convolution_convert_fusion
  142.0 1.7 reshape.563
  143.7 1.8 slice_bitcast_fusion.3
  145.5 1.4 select_convert_fusion
  146.9 1.0 broadcast_select_fusion.7
  147.9 0.8 fusion.10
  149.9 1.3 rev.23
  151.3 0.8 broadcast_select_fusion.5
  152.1 0.8 broadcast_in_dim.463
  152.9 5.7 %all-to-all-start.3 = ((bf16[16,48,256]{2,1,0:T(8,128)(2,1)}), bf16[16,48,256]{2,1,0:T(8,128)(2,1)}, u32[]{:S(2)}, u32[]{:S(2)}) async-start(bf16[16,48,256]{2,1,0:T(8,128)(2,1)} %bitcast.172), calls=%async_computation.3 | async-start | bytes 786432 | tf_op jit(solution)/shard_map/all_to_all | solution.py:66
  158.6 2.0 add_convert_fusion
  160.7 14.7 %all-to-all-done.3 = bf16[16,48,256]{2,1,0:T(8,128)(2,1)} async-done(((bf16[16,48,256]{2,1,0:T(8,128)(2,1)}), bf16[16,48,256]{2,1,0:T(8,128)(2,1)}, u32[]{:S(2)}, u32[]{:S(2)}) %all-to-all-start.3) | async-done | bytes 393248 | tf_op jit(solution)/shard_map/all_to_all | solution.py:66
  175.5 34.5 %all_to_all.35 = bf16[16,2,72,256]{3,2,1,0:T(8,128)(2,1)S(1)} all-to-all(bf16[16,2,72,256]{3,2,1,0:T(8,128)(2,1)S(1)} %bitcast.158), channel_id=1, replica_groups=mesh['face'=4,'zh'=2,'x'=4,'y'=4,'core'=2] {'y','x'}, dimensions={0} | all-to-all | bytes 2359296 | tf_op jit(solution)/shard_map/all_to_all | solution.py:229
  210.2 17.3 %all_to_all.36 = bf16[8,2,72,256]{3,2,1,0:T(8,128)(2,1)S(1)} all-to-all(bf16[8,2,72,256]{3,2,1,0:T(8,128)(2,1)S(1)} %broadcast_in_dim.471), channel_id=1, replica_groups=mesh['face'=4,'zh'=2,'x'=4,'y'=4,'core'=2] {'face','zh'}, dimensions={0} | all-to-all | bytes 1179648 | tf_op jit(solution)/shard_map/all_to_all | solution.py:90
  227.7 18.4 %all_to_all.37 = bf16[16,2,72,256]{3,2,1,0:T(8,128)(2,1)S(1)} all-to-all(bf16[16,2,72,256]{3,2,1,0:T(8,128)(2,1)S(1)} %broadcast_in_dim.472), channel_id=1, replica_groups=mesh['face'=4,'zh'=2,'x'=4,'y'=4,'core'=2] {'y','x'}, dimensions={0} | all-to-all | bytes 2359296 | tf_op jit(solution)/shard_map/all_to_all | solution.py:94
  246.2 5.4 %collective-permute-start.9 = (bf16[2,1152,256]{2,1,0:T(8,128)(2,1)S(1)}, bf16[2,1152,256]{2,1,0:T(8,128)(2,1)S(1)}, u32[]{:S(2)}, u32[]{:S(2)}) collective-permute-start(bf16[2,1152,256]{2,1,0:T(8,128)(2,1)S(1)} %bitcast.156), channel_id=1, source_target_pairs={{0,1},{1,0},{2,3},{3,2},{4,5},{5,4},{6,7},{7,6},{8,9},{9,8},{10,11... | collective-permute-start | bytes 3538952 | tf_op jit(solution)/shard_map/ppermute | solution.py:96
  251.6 1.2 reshape.566
  253.1 1.7 fusion.7
  255.4 2.5 fusion.28
  (216 shorter events, 29.0 us)
Async XLA Ops:
  1.7 7.2 %collective-permute-start = (bf16[3,8,2,256]{3,2,1,0:T(2,128)(2,1)S(1)}, bf16[3,8,2,256]{3,2,1,0:T(2,128)(2,1)S(1)}, u32[]{:S(2)}, u32[]{:S(2)}) collective-permute-start(bf16[3,8,2,256]{3,2,1,0:T(2,128)(2,1)S(1)} %get-tuple-element.55), channel_id=1, source_target_pairs={{1,2},{3,4},{5,6},{9,10},{11,12},{13,14},{17,18},{19,20},{21,22},{... | collective-permute-start | bytes 73736 | tf_op jit(solution)/shard_map/ppermute | solution.py:39
  6.3 2.6 %collective-permute-start.1 = (bf16[3,8,2,256]{3,2,1,0:T(2,128)(2,1)S(1)}, bf16[3,8,2,256]{3,2,1,0:T(2,128)(2,1)S(1)}, u32[]{:S(2)}, u32[]{:S(2)}) collective-permute-start(bf16[3,8,2,256]{3,2,1,0:T(2,128)(2,1)S(1)} %get-tuple-element.56), channel_id=1, source_target_pairs={{0,1},{1,0},{2,3},{3,2},{4,5},{5,4},{6,7},{7,6},{8,9},{9,8},{10,11... | collective-permute-start | bytes 73736 | tf_op jit(solution)/shard_map/ppermute | solution.py:38
  6.4 23.9 %copy-start.22 = (pred[2,2]{1,0:T(4,128)(4,1)}, pred[2,2]{1,0:T(4,128)(4,1)S(1)}, u32[]{:S(2)}) copy-start(pred[2,2]{1,0:T(4,128)(4,1)S(1)} %iota_compare_fusion.2) | copy-start | bytes 16
  8.8 21.6 %copy-start.14 = (pred[2]{0:T(512)(128)(4,1)}, pred[2]{0:T(512)(128)(4,1)S(1)}, u32[]{:S(2)}) copy-start(pred[2]{0:T(512)(128)(4,1)S(1)} %pad_add_fusion) | copy-start | bytes 10
  9.8 5.2 %collective-permute-start.2 = (bf16[3,2,12,256]{3,2,1,0:T(8,128)(2,1)S(1)}, bf16[3,2,12,256]{3,2,1,0:T(8,128)(2,1)S(1)}, u32[]{:S(2)}, u32[]{:S(2)}) collective-permute-start(bf16[3,2,12,256]{3,2,1,0:T(8,128)(2,1)S(1)} %get-tuple-element.47), channel_id=1, source_target_pairs={{8,16},{9,17},{10,18},{11,19},{12,20},{13,21},{14,22},{15,23},{24,... | collective-permute-start | bytes 110600 | tf_op jit(solution)/shard_map/ppermute | solution.py:44
  10.4 5.2 %collective-permute-start.3 = (bf16[3,2,12,256]{3,2,1,0:T(8,128)(2,1)S(1)}, bf16[3,2,12,256]{3,2,1,0:T(8,128)(2,1)S(1)}, u32[]{:S(2)}, u32[]{:S(2)}) collective-permute-start(bf16[3,2,12,256]{3,2,1,0:T(8,128)(2,1)S(1)} %get-tuple-element.48), channel_id=1, source_target_pairs={{0,8},{1,9},{2,10},{3,11},{4,12},{5,13},{6,14},{7,15},{16,24},{17,... | collective-permute-start | bytes 110600 | tf_op jit(solution)/shard_map/ppermute | solution.py:43
  17.4 33.3 %copy-start.1 = (bf16[3,1,8,8,256]{4,3,2,1,0:T(8,128)(2,1)S(1)}, bf16[3,1,8,8,256]{4,3,2,1,0:T(8,128)(2,1)}, u32[]{:S(2)}) copy-start(bf16[3,1,8,8,256]{4,3,2,1,0:T(8,128)(2,1)} %param.6) | copy-start | bytes 294916
  18.4 31.3 %all-to-all-start = ((bf16[16,72,256]{2,1,0:T(8,128)(2,1)}), bf16[16,72,256]{2,1,0:T(8,128)(2,1)S(1)}, u32[]{:S(2)}, u32[]{:S(2)}) async-start(bf16[16,72,256]{2,1,0:T(8,128)(2,1)} %copy.287), calls=%async_computation | async-start | bytes 1179648 | tf_op jit(solution)/shard_map/all_to_all | solution.py:66
  51.0 1.3 copy-start.4
  51.5 2.3 copy-start.12
  53.8 7.6 %copy-start.13 = (s32[12,4]{0,1:T(4,128)S(1)}, s32[12,4]{0,1:T(4,128)}, u32[]{:S(2)}) copy-start(s32[12,4]{0,1:T(4,128)} %param.10) | copy-start | bytes 580
  55.4 24.1 %all-to-all-start.1 = ((bf16[16,60,256]{2,1,0:T(8,128)(2,1)}), bf16[16,60,256]{2,1,0:T(8,128)(2,1)S(1)}, u32[]{:S(2)}, u32[]{:S(2)}) async-start(bf16[16,60,256]{2,1,0:T(8,128)(2,1)} %copy.293), calls=%async_computation.1 | async-start | bytes 1048576 | tf_op jit(solution)/shard_map/all_to_all | solution.py:66
  80.0 2.0 copy-start.3
  80.0 2.0 copy-start.11
  81.1 0.9 copy-start.7
  83.2 5.1 %collective-permute-start.4 = (bf16[3,8,2,256]{3,2,1,0:T(2,128)(2,1)S(1)}, bf16[3,8,2,256]{3,2,1,0:T(2,128)(2,1)S(1)}, u32[]{:S(2)}, u32[]{:S(2)}) collective-permute-start(bf16[3,8,2,256]{3,2,1,0:T(2,128)(2,1)S(1)} %get-tuple-element.51), channel_id=1, source_target_pairs={{1,2},{3,4},{5,6},{9,10},{11,12},{13,14},{17,18},{19,20},{21,22},{... | collective-permute-start | bytes 73736 | tf_op jit(solution)/shard_map/ppermute | solution.py:39
  85.2 3.2 %collective-permute-start.5 = (bf16[3,8,2,256]{3,2,1,0:T(2,128)(2,1)S(1)}, bf16[3,8,2,256]{3,2,1,0:T(2,128)(2,1)S(1)}, u32[]{:S(2)}, u32[]{:S(2)}) collective-permute-start(bf16[3,8,2,256]{3,2,1,0:T(2,128)(2,1)S(1)} %get-tuple-element.52), channel_id=1, source_target_pairs={{0,1},{1,0},{2,3},{3,2},{4,5},{5,4},{6,7},{7,6},{8,9},{9,8},{10,11... | collective-permute-start | bytes 73736 | tf_op jit(solution)/shard_map/ppermute | solution.py:38
  89.1 3.4 %collective-permute-start.7 = (bf16[3,2,12,256]{3,2,1,0:T(8,128)(2,1)}, bf16[3,2,12,256]{3,2,1,0:T(8,128)(2,1)}, u32[]{:S(2)}, u32[]{:S(2)}) collective-permute-start(bf16[3,2,12,256]{3,2,1,0:T(8,128)(2,1)} %get-tuple-element.45), channel_id=1, source_target_pairs={{0,8},{1,9},{2,10},{3,11},{4,12},{5,13},{6,14},{7,15},{16,24},{17,... | collective-permute-start | bytes 110600 | tf_op jit(solution)/shard_map/ppermute | solution.py:43
  89.7 2.7 %collective-permute-start.6 = (bf16[3,2,12,256]{3,2,1,0:T(8,128)(2,1)}, bf16[3,2,12,256]{3,2,1,0:T(8,128)(2,1)}, u32[]{:S(2)}, u32[]{:S(2)}) collective-permute-start(bf16[3,2,12,256]{3,2,1,0:T(8,128)(2,1)} %get-tuple-element.46), channel_id=1, source_target_pairs={{8,16},{9,17},{10,18},{11,19},{12,20},{13,21},{14,22},{15,23},{24,... | collective-permute-start | bytes 110600 | tf_op jit(solution)/shard_map/ppermute | solution.py:44
  97.6 0.7 copy-start.2
  97.6 9.3 %copy-start.5 = (bf16[3,3,256,256]{3,2,1,0:T(8,128)(2,1)S(1)}, bf16[3,3,256,256]{3,2,1,0:T(8,128)(2,1)}, u32[]{:S(2)}) copy-start(bf16[3,3,256,256]{3,2,1,0:T(8,128)(2,1)} %param.8) | copy-start | bytes 3538948
  98.7 9.7 %copy-start.23 = (pred[2,2]{1,0:T(4,128)(4,1)S(1)}, pred[2,2]{1,0:T(4,128)(4,1)}, u32[]{:S(2)}) copy-start(pred[2,2]{1,0:T(4,128)(4,1)} %copy-done.22) | copy-start | bytes 16
  99.6 23.3 %all-to-all-start.2 = ((bf16[16,60,256]{2,1,0:T(8,128)(2,1)}), bf16[16,60,256]{2,1,0:T(8,128)(2,1)S(1)}, u32[]{:S(2)}, u32[]{:S(2)}) async-start(bf16[16,60,256]{2,1,0:T(8,128)(2,1)} %copy.306), calls=%async_computation.2 | async-start | bytes 1048576 | tf_op jit(solution)/shard_map/all_to_all | solution.py:66
  106.9 2.7 %copy-start.9 = (f32[192,256]{1,0:T(8,128)S(1)}, f32[192,256]{1,0:T(8,128)}, u32[]{:S(2)}) copy-start(f32[192,256]{1,0:T(8,128)} %get-tuple-element.72) | copy-start | bytes 589828
  107.7 2.0 copy-start.8
  108.5 15.3 %copy-start.16 = (pred[2,96]{1,0:T(4,128)(4,1)}, pred[2,96]{1,0:T(4,128)(4,1)S(1)}, u32[]{:S(2)}) copy-start(pred[2,96]{1,0:T(4,128)(4,1)S(1)} %and.340) | copy-start | bytes 580
  110.2 13.7 %copy-start.15 = (pred[2]{0:T(512)(128)(4,1)S(1)}, pred[2]{0:T(512)(128)(4,1)}, u32[]{:S(2)}) copy-start(pred[2]{0:T(512)(128)(4,1)} %copy-done.14) | copy-start | bytes 10
  110.2 13.7 %copy-start.18 = (pred[3,96]{1,0:T(4,128)(4,1)S(1)}, pred[3,96]{1,0:T(4,128)(4,1)}, u32[]{:S(2)}) copy-start(pred[3,96]{1,0:T(4,128)(4,1)} %compare_and_fusion) | copy-start | bytes 868
  110.4 13.9 %copy-start.20 = (pred[10]{0:T(512)(128)(4,1)S(1)}, pred[10]{0:T(512)(128)(4,1)}, u32[]{:S(2)}) copy-start(pred[10]{0:T(512)(128)(4,1)} %get-tuple-element.85) | copy-start | bytes 34
  110.4 13.9 %copy-start.21 = (pred[10]{0:T(512)(128)(4,1)S(1)}, pred[10]{0:T(512)(128)(4,1)}, u32[]{:S(2)}) copy-start(pred[10]{0:T(512)(128)(4,1)} %get-tuple-element.86) | copy-start | bytes 34
  134.4 5.1 %copy-start.6 = (bf16[3,3,256,256]{2,3,1,0:T(8,128)(2,1)S(1)}, bf16[3,3,256,256]{2,3,1,0:T(8,128)(2,1)}, u32[]{:S(2)}) copy-start(bf16[3,3,256,256]{2,3,1,0:T(8,128)(2,1)} %rev.22) | copy-start | bytes 3538948
  145.5 1.4 copy-start
  146.9 11.7 %collective-permute-start.8 = (bf16[2,1152,256]{2,1,0:T(8,128)(2,1)}, bf16[2,1152,256]{2,1,0:T(8,128)(2,1)}, u32[]{:S(2)}, u32[]{:S(2)}) collective-permute-start(bf16[2,1152,256]{2,1,0:T(8,128)(2,1)} %select_convert_fusion), channel_id=1, source_target_pairs={{0,1},{1,0},{2,3},{3,2},{4,5},{5,4},{6,7},{7,6},{8,9},{9,8},{10,11... | collective-permute-start | bytes 3538952 | tf_op jit(solution)/shard_map/ppermute | solution.py:82
  148.7 0.6 copy-start.10
  152.9 22.6 %all-to-all-start.3 = ((bf16[16,48,256]{2,1,0:T(8,128)(2,1)}), bf16[16,48,256]{2,1,0:T(8,128)(2,1)}, u32[]{:S(2)}, u32[]{:S(2)}) async-start(bf16[16,48,256]{2,1,0:T(8,128)(2,1)} %bitcast.172), calls=%async_computation.3 | async-start | bytes 786432 | tf_op jit(solution)/shard_map/all_to_all | solution.py:66
  227.7 25.1 %copy-start.17 = (pred[2,96]{1,0:T(4,128)(4,1)S(1)}, pred[2,96]{1,0:T(4,128)(4,1)}, u32[]{:S(2)}) copy-start(pred[2,96]{1,0:T(4,128)(4,1)} %copy-done.16) | copy-start | bytes 580
  227.7 25.1 %copy-start.19 = (pred[3,96]{1,0:T(4,128)(4,1)S(1)}, pred[3,96]{1,0:T(4,128)(4,1)}, u32[]{:S(2)}) copy-start(pred[3,96]{1,0:T(4,128)(4,1)} %compare_and_fusion) | copy-start | bytes 868
  246.2 8.5 %collective-permute-start.9 = (bf16[2,1152,256]{2,1,0:T(8,128)(2,1)S(1)}, bf16[2,1152,256]{2,1,0:T(8,128)(2,1)S(1)}, u32[]{:S(2)}, u32[]{:S(2)}) collective-permute-start(bf16[2,1152,256]{2,1,0:T(8,128)(2,1)S(1)} %bitcast.156), channel_id=1, source_target_pairs={{0,1},{1,0},{2,3},{3,2},{4,5},{5,4},{6,7},{7,6},{8,9},{9,8},{10,11... | collective-permute-start | bytes 3538952 | tf_op jit(solution)/shard_map/ppermute | solution.py:96

commit v5 on v1

v5 whole, which is shorter than its diff:
```python
import math

import jax
import jax.numpy as jnp
import numpy as np
from jax import lax
from jax.experimental import pallas as pl
from jax.experimental.pallas import tpu as pltpu
from jax.sharding import Mesh, PartitionSpec as P

AXES = ("face", "zh", "x", "y", "core")
TILE = ("zh", "x", "y", "core")
F32 = jnp.float32
BF16 = jnp.bfloat16
MIRRORS = (0, 7, 56, 63)
C = 256
PITCH = 16
SCALE = 1.0 / math.sqrt(12 * 64 * 64)


def swap_pairs(pairs):
    return [(a, b) for a, b in pairs] + [(b, a) for a, b in pairs]


CORES = [(0, 1), (1, 0)]
ODD_COLS = swap_pairs([(r * 8 + c, r * 8 + c + 1) for r in range(8) for c in (1, 3, 5)])
EVEN_ROWS = swap_pairs([(r * 8 + c, r * 8 + 8 + c) for r in (0, 2, 4, 6) for c in range(8)])
ODD_ROWS = swap_pairs([(r * 8 + c, r * 8 + 8 + c) for r in (1, 3, 5) for c in range(8)])
SEAM_GROUPS = [
    [f * 64 + (t ^ m) for f in range(4) for m in MIRRORS]
    for t in range(64)
    if t == min(t ^ m for m in MIRRORS)
]


def run(kernel, outs, scratch, pos, *args):
    vmem = pl.BlockSpec(memory_space=pltpu.VMEM)
    return pl.pallas_call(
        kernel,
        out_shape=[jax.ShapeDtypeStruct(shape, dtype) for shape, dtype in outs],
        in_specs=[pl.BlockSpec(memory_space=pltpu.SMEM)] + [vmem] * len(args),
        out_specs=[vmem] * len(outs),
        scratch_shapes=[pltpu.VMEM(shape, dtype) for shape, dtype in scratch],
        compiler_params=pltpu.CompilerParams(vmem_limit_bytes=24 * 2**20),
    )(pos, *args)


def slope_of(v):
    s = 1.0 / (1.0 + jnp.exp(-v))
    return s * (1.0 + v * (1.0 - s))


def dot(a, b, contract):
    return lax.dot_general(a, b, ((contract[0], contract[1]), ((), ())), preferred_element_type=F32)


def convolve(cells, shifts, height, lines, col0, kernel, transposed):
    total = None
    size = 3 * height * PITCH
    for b in range(3):
        shifts[0:size, :] = cells[col0 + b : col0 + b + size, :].astype(BF16)
        taps = []
        for a in range(3):
            at = [(f * height + a) * PITCH for f in range(3)]
            taps.append(jnp.concatenate([shifts[i : i + lines * PITCH, :] for i in at], axis=0))
        left = jnp.concatenate(taps, axis=1)
        if transposed:
            right = jnp.concatenate([kernel[2 - a, 2 - b] for a in range(3)], axis=1)
            part = dot(left, right, ((1,), (1,)))
        else:
            right = jnp.concatenate([kernel[a, b] for a in range(3)], axis=0)
            part = dot(left, right, ((1,), (0,)))
        total = part if total is None else total + part
    return total


def cell_mask(row, col):
    i = lax.broadcasted_iota(jnp.int32, (10 * PITCH, C), 0)
    v, w = i // PITCH, i % PITCH
    v_low, v_high = jnp.where(row > 0, 0, 1), jnp.where(row < 7, 9, 8)
    w_low, w_high = jnp.where(col > 0, 0, 1), jnp.where(col < 7, 9, 8)
    return (v >= v_low) & (v <= v_high) & (w >= w_low) & (w <= w_high)


def take_strips(cells, strips, row, col, height, first, last, begin, length):
    for f in range(3):
        base = f * height * PITCH
        top = cells[base + first * PITCH + begin : base + first * PITCH + begin + length, :]
        low = cells[base + last * PITCH + begin : base + last * PITCH + begin + length, :]
        strips[2 * f * length : (2 * f + 1) * length, :] = jnp.where(row >= 4, low, top)
        for i in range(length):
            at = base + (begin + i) * PITCH
            left, right = cells[at + first : at + first + 1, :], cells[at + last : at + last + 1, :]
            to = (2 * f + 1) * length + i
            strips[to : to + 1, :] = jnp.where(col >= 4, right, left)


def post_strips(strips, send):
    block = strips[...].astype(BF16)
    for i in range(16):
        send[i] = block


def fill_strips(cells, strips, row, col, height, first, last, length):
    for f in range(3):
        base = f * height * PITCH
        for at, here in ((first, row == 0), (last, row == 7)):

            @pl.when(here)
            def _(at=at):
                cells[base + at * PITCH : base + at * PITCH + length, :] = strips[2 * f * length : (2 * f + 1) * length, :]

    for f in range(3):
        base = f * height * PITCH
        for at, here in ((first, col == 0), (last, col == 7)):

            @pl.when(here)
            def _(at=at):
                for i in range(length):
                    to = base + at + i * PITCH
                    cells[to : to + 1, :] = strips[(2 * f + 1) * length + i : (2 * f + 1) * length + i + 1, :]


def widen_kernel(pos, own, swapped, odd, wide, first, second, cells):
    row, col = pos[0], pos[1]
    even = col % 2 == 0
    cells[...] = jnp.zeros_like(cells)
    core_tile, odd_tile = swapped[...].astype(F32), odd[...].astype(F32)
    left = jnp.where(even, odd_tile, core_tile).reshape(24, 8, C)
    right = jnp.where(even, core_tile, odd_tile).reshape(24, 8, C)
    cells[:, 0:2, :] = left[:, 6:8, :]
    cells[:, 2:10, :] = own[...].astype(F32).reshape(24, 8, C)
    cells[:, 10:12, :] = right[:, 0:2, :]
    wide[...] = cells[...].reshape(24 * PITCH, C).astype(BF16)
    even = row % 2 == 0
    for f in range(3):
        up = cells[8 * f : 8 * f + 2].reshape(2 * PITCH, C)
        down = cells[8 * f + 6 : 8 * f + 8].reshape(2 * PITCH, C)
        first[2 * f * PITCH : (2 * f + 2) * PITCH, :] = jnp.where(even, down, up).astype(BF16)
        second[2 * f * PITCH : (2 * f + 2) * PITCH, :] = jnp.where(even, up, down).astype(BF16)


def stack_lines(row, wide, first, second, cells):
    even = row % 2 == 0
    one, two = first[...].astype(F32), second[...].astype(F32)
    above, below = jnp.where(even, two, one), jnp.where(even, one, two)
    for f in range(3):
        base = f * 12 * PITCH
        lines = slice(2 * f * PITCH, (2 * f + 2) * PITCH)
        cells[base : base + 2 * PITCH, :] = above[lines]
        cells[base + 2 * PITCH : base + 10 * PITCH, :] = wide[8 * f * PITCH : (8 * f + 8) * PITCH, :].astype(F32)
        cells[base + 10 * PITCH : base + 12 * PITCH, :] = below[lines]
    cells[36 * PITCH :, :] = jnp.zeros((8, C), F32)


def input_kernel(pos, wide, first, second, near, send, cells, strips):
    row, col = pos[0], pos[1]
    stack_lines(row, wide, first, second, cells)
    near[...] = cells[0 : 36 * PITCH, :].astype(BF16)
    strips[...] = jnp.zeros_like(strips)
    take_strips(cells, strips, row, col, 12, 2, 9, 0, 12)
    post_strips(strips, send)


def one_kernel(pos, near, got, pick, kernel, filled, pre, hidden, send, cells, shifts, strips, lines):
    row, col = pos[0], pos[1]
    lines[...] = dot(pick[...], got[...], ((1,), (0,)))
    cells[0 : 36 * PITCH, :] = near[...].astype(F32)
    cells[36 * PITCH :, :] = jnp.zeros((8, C), F32)
    fill_strips(cells, lines, row, col, 12, 1, 10, 12)
    filled[...] = cells[0 : 36 * PITCH, :].astype(BF16)
    total = convolve(cells, shifts, 12, 10, 0, kernel, False)
    pre[...] = total
    inside = cell_mask(row, col)
    for f in range(3):
        v = total[f * 10 * PITCH : (f + 1) * 10 * PITCH]
        cells[f * 10 * PITCH : (f + 1) * 10 * PITCH, :] = jnp.where(inside, v / (1.0 + jnp.exp(-v)), 0.0)
    hidden[...] = cells[0 : 30 * PITCH, :].astype(BF16)
    strips[...] = jnp.zeros_like(strips)
    take_strips(cells, strips, row, col, 10, 1, 8, 0, 10)
    post_strips(strips, send)


def two_kernel(pos, hidden, got, pick, kernel, cotangent, filled, delta, wide_delta, cells, shifts, lines):
    row, col = pos[0], pos[1]
    lines[...] = dot(pick[...], got[...], ((1,), (0,)))
    cells[0 : 30 * PITCH, :] = hidden[...].astype(F32)
    cells[30 * PITCH :, :] = jnp.zeros((8, C), F32)
    fill_strips(cells, lines, row, col, 10, 0, 9, 10)
    filled[...] = cells[0 : 30 * PITCH, :].astype(BF16)
    total = convolve(cells, shifts, 10, 8, 0, kernel, False).reshape(24, PITCH, C)[:, 0:8, :]
    product = cotangent[...].astype(F32).reshape(24, 8, C) * slope_of(total)
    delta[...] = product.reshape(192, C).astype(BF16)
    padded = jnp.concatenate([product, jnp.zeros((24, 8, C), F32)], axis=1)
    wide_delta[...] = padded.reshape(24 * PITCH, C).astype(BF16)


def back_kernel(pos, wide, first, second, kernel, back, send, cells, shifts, strips):
    row, col = pos[0], pos[1]
    stack_lines(row, wide, first, second, cells)
    total = convolve(cells, shifts, 12, 10, 0, kernel, True)
    back[...] = total.astype(BF16)
    cells[0 : 30 * PITCH, :] = total
    strips[...] = jnp.zeros_like(strips)
    take_strips(cells, strips, row, col, 10, 0, 9, 0, 10)
    at = lax.broadcasted_iota(jnp.int32, (10, C), 0)
    for f in range(3):
        for kind, where in ((0, col), (1, row)):
            low, high = jnp.where(where > 0, 0, 1), jnp.where(where < 7, 9, 8)
            lines = slice((2 * f + kind) * 10, (2 * f + kind + 1) * 10)
            strips[lines, :] = jnp.where((at >= low) & (at <= high), strips[lines, :], 0.0)
    post_strips(strips, send)


def delta_kernel(pos, back, got, pick, pre, kernel, wide_delta, own, send, cells, grads, shifts, strips, lines):
    row, col = pos[0], pos[1]
    lines[...] = dot(pick[...], got[...], ((1,), (0,)))
    grads[...] = back[...].astype(F32)
    for f in range(3):
        base = f * 10 * PITCH
        for at, here in ((1, row == 0), (8, row == 7)):

            @pl.when(here)
            def _(at=at):
                where = slice(base + at * PITCH, base + at * PITCH + 10)
                grads[where, :] = grads[where, :] + lines[2 * f * 10 : (2 * f + 1) * 10, :]

        for at, here in ((1, col == 0), (8, col == 7)):

            @pl.when(here)
            def _(at=at):
                for i in range(10):
                    where = slice(base + at + i * PITCH, base + at + i * PITCH + 1)
                    grads[where, :] = grads[where, :] + lines[(2 * f + 1) * 10 + i : (2 * f + 1) * 10 + i + 1, :]

    cells[...] = jnp.zeros_like(cells)
    inside = cell_mask(row, col)
    for f in range(3):
        where = slice(f * 10 * PITCH, (f + 1) * 10 * PITCH)
        value = jnp.where(inside, grads[where, :] * slope_of(pre[where, :]), 0.0)
        at = (f * 12 + 1) * PITCH + 1
        cells[at : at + 10 * PITCH, :] = value.astype(BF16).astype(F32)
    at = lax.broadcasted_iota(jnp.int32, (8 * PITCH, C), 0) % PITCH
    for f in range(3):
        begin = (f * 12 + 2) * PITCH + 2
        mine = jnp.where(at < 8, cells[begin : begin + 8 * PITCH, :], 0.0)
        wide_delta[f * 8 * PITCH : (f + 1) * 8 * PITCH, :] = mine.astype(BF16)
    total = convolve(cells, shifts, 12, 10, 0, kernel, True)
    grads[...] = total
    take_strips(grads, strips, row, col, 10, 0, 9, 1, 8)
    post_strips(strips, send)
    for f in range(3):
        for i in range(8):
            begin = (f * 10 + i + 1) * PITCH + 1
            lines[0:8, :] = grads[begin : begin + 8, :]
            cells[(f * 8 + i) * 8 : (f * 8 + i + 1) * 8, :] = lines[0:8, :]
    own[...] = cells[0:192, :].astype(BF16)


def final_kernel(pos, own, got, pick, out, cells, lines):
    row, col = pos[0], pos[1]
    lines[...] = dot(pick[...], got[...], ((1,), (0,)))
    cells[...] = own[...].astype(F32)
    for f in range(3):
        base = f * 64
        for at, here in ((0, row == 0), (7, row == 7)):

            @pl.when(here)
            def _(at=at):
                where = slice(base + at * 8, base + at * 8 + 8)
                cells[where, :] = cells[where, :] + lines[2 * f * 8 : (2 * f + 1) * 8, :]

        for at, here in ((0, col == 0), (7, col == 7)):

            @pl.when(here)
            def _(at=at):
                for i in range(8):
                    where = slice(base + at + i * 8, base + at + i * 8 + 1)
                    cells[where, :] = cells[where, :] + lines[(2 * f + 1) * 8 + i : (2 * f + 1) * 8 + i + 1, :]

    out[...] = cells[...].astype(BF16)


def grad_kernel(height, line0, col0, pos, source, delta, keep, send, cells, shifts, sums):
    core = pos[2]
    size = 3 * height * PITCH
    cells[0:size, :] = source[...].astype(F32)
    cells[size:, :] = jnp.zeros((8, C), F32)
    right = delta[...]
    for b in range(3):
        shifts[...] = cells[col0 + b : col0 + b + size, :].astype(BF16)
        for a in range(3):
            at = [(f * height + line0 + a) * PITCH for f in range(3)]
            left = jnp.concatenate([shifts[i : i + 8 * PITCH, :] for i in at], axis=0)
            total = dot(left, right, ((0,), (0,))) * SCALE
            low, high = total[0:128], total[128:256]
            lines = slice((a * 3 + b) * 8, (a * 3 + b + 1) * 8)
            keep[:, lines, :] = jnp.where(core == 0, low, high).reshape(16, 8, C)
            sums[:, lines, :] = jnp.where(core == 0, high, low).reshape(16, 8, C)
    send[...] = sums[...].astype(BF16)


def pair_kernel(pos, keep_one, got_one, keep_two, got_two, out):
    for i in range(16):
        one = keep_one[i] + got_one[i].astype(F32)
        two = keep_two[i] + got_two[i].astype(F32)
        out[i] = jnp.concatenate([one, two], axis=0).astype(BF16)


def sum_kernel(copies, pos, parts, out):
    total = parts[0].astype(F32)
    for i in range(1, parts.shape[0]):
        total = total + parts[i].astype(F32)
    total = total.astype(BF16)
    for i in range(copies):
        out[i] = total


def tall_region(field, pos):
    swapped = lax.ppermute(field, "core", CORES)
    odd = lax.ppermute(field, TILE, ODD_COLS)
    wide, first, second = run(
        widen_kernel,
        [((24 * PITCH, C), BF16), ((6 * PITCH, C), BF16), ((6 * PITCH, C), BF16)],
        [((24, PITCH, C), F32)],
        pos,
        field,
        swapped,
        odd,
    )
    return wide, lax.ppermute(first, TILE, EVEN_ROWS), lax.ppermute(second, TILE, ODD_ROWS)


def seam_exchange(send):
    got = lax.all_to_all(send, AXES, 0, 0, axis_index_groups=SEAM_GROUPS)
    return got.reshape(-1, C)


def seam_picks(neighbour, seam_codes, row, col, face_group):
    mirror = col // 4 + 2 * (row // 4)
    on_edge = jnp.stack([(row == 0) | (row == 7), (col == 0) | (col == 7)])
    bottom, right = row // 4, col // 4
    own_side = jnp.stack([bottom, 2 + right])
    first = face_group * 3
    opposite, reverse = 1 - seam_codes % 2, seam_codes // 2
    types = jnp.arange(4) // 2
    rel_of = jnp.where(types == 0, 2 * opposite + reverse, 2 * reverse + opposite)
    slot_mirror = jnp.arange(4, dtype=jnp.int32)
    slot_type = jnp.arange(2, dtype=jnp.int32)

    def on_side(table, side):
        return jnp.sum(jnp.where(side[..., None] == jnp.arange(4), table, 0), axis=-1)

    own_next = lax.dynamic_slice_in_dim(neighbour, first, 3, 0)
    own_rel = lax.dynamic_slice_in_dim(rel_of, first, 3, 0)
    next_face = on_side(own_next[:, None, :], own_side[None])
    next_rel = on_side(own_rel[:, None, :], own_side[None])
    faces = jnp.arange(12, dtype=jnp.int32).reshape(4, 1, 3, 1)
    same_type = (slot_type[:, None, None, None, None] == slot_type) & on_edge[:, None, None, None, None]
    gather = (
        (next_face[:, :, None, None, None, None] == faces)
        & ((next_rel ^ mirror)[:, :, None, None, None, None] == slot_mirror[:, None, None])
        & same_type
    )
    rel = slot_mirror ^ mirror
    from_side = jnp.stack([bottom ^ (rel // 2), 2 + (right ^ (rel % 2))], axis=1)[None, :, None, :]
    slot_next = on_side(neighbour.reshape(4, 1, 3, 1, 4), from_side)
    slot_rel = on_side(rel_of.reshape(4, 1, 3, 1, 4), from_side)
    own_faces = (first + jnp.arange(3, dtype=jnp.int32))[:, None, None, None, None, None]
    add = (slot_next == own_faces) & (slot_rel == rel[:, None, None]) & same_type
    turned = jnp.stack([rel % 2, rel // 2], axis=1) == 1

    def expand(select, length, block):
        select = select.reshape(6, 16, 6).astype(BF16)
        flip = jnp.broadcast_to(turned[None, :, None, :], (4, 4, 3, 2)).reshape(16, 6)
        at = jnp.arange(length, dtype=jnp.int32)
        here = jnp.where(flip[None, :, :, None], at[:, None, None, None] + at == length - 1, at[:, None, None, None] == at)
        full = select[:, None, :, :, None] * here[None].astype(BF16)
        full = full.reshape(6 * length, 16, 6 * length)
        rows = -(-6 * length // 16) * 16
        full = jnp.pad(full, ((0, rows - 6 * length), (0, 0), (0, block - 6 * length)))
        return full.reshape(rows, 16 * block)

    return expand(gather, 12, 80), expand(gather, 10, 64), expand(add, 10, 64), expand(add, 8, 48)


def body(inputs, cotangent, kernel_one, kernel_two, neighbour, seam_codes):
    face_group = lax.axis_index("face")
    core = lax.axis_index("core")
    row = lax.axis_index("zh") * 4 + lax.axis_index("x")
    col = lax.axis_index("y") * 2 + core
    pos = jnp.stack([row, col, core, face_group]).astype(jnp.int32)
    pick_12, pick_10, add_10, add_8 = seam_picks(neighbour, seam_codes, row, col, face_group)
    flat = 36 * PITCH
    spare = flat + 8

    wide, first, second = tall_region(inputs.reshape(192, C), pos)
    near, send = run(
        input_kernel,
        [((flat, C), BF16), ((16, 80, C), BF16)],
        [((spare, C), F32), ((80, C), F32)],
        pos,
        wide,
        first,
        second,
    )
    filled_in, pre_one, hidden, send = run(
        one_kernel,
        [((flat, C), BF16), ((30 * PITCH, C), F32), ((30 * PITCH, C), BF16), ((16, 64, C), BF16)],
        [((spare, C), F32), ((flat, C), BF16), ((64, C), F32), ((80, C), F32)],
        pos,
        near,
        seam_exchange(send),
        pick_12,
        kernel_one,
    )
    filled_hidden, delta, wide_two = run(
        two_kernel,
        [((30 * PITCH, C), BF16), ((192, C), BF16), ((24 * PITCH, C), BF16)],
        [((30 * PITCH + 8, C), F32), ((30 * PITCH, C), BF16), ((64, C), F32)],
        pos,
        hidden,
        seam_exchange(send),
        pick_10,
        kernel_two,
        cotangent.reshape(192, C),
    )
    wide, first, second = tall_region(delta, pos)
    back, send = run(
        back_kernel,
        [((30 * PITCH, C), BF16), ((16, 64, C), BF16)],
        [((spare, C), F32), ((flat, C), BF16), ((64, C), F32)],
        pos,
        wide,
        first,
        second,
        kernel_two,
    )
    got = seam_exchange(send)
    pieces = [((16, 72, C), F32), ((16, 72, C), BF16)]

    def grad_of(height, line0, col0, source, delta):
        size = 3 * height * PITCH
        return run(
            lambda *refs: grad_kernel(height, line0, col0, *refs),
            pieces,
            [((size + 8, C), F32), ((size, C), BF16), ((16, 72, C), F32)],
            pos,
            source,
            delta,
        )

    keep_two, payload_two = grad_of(10, 0, 0, filled_hidden, wide_two)
    got_two = lax.ppermute(payload_two, "core", CORES)
    wide_one, own, send = run(
        delta_kernel,
        [((24 * PITCH, C), BF16), ((192, C), BF16), ((16, 48, C), BF16)],
        [((spare, C), F32), ((30 * PITCH, C), F32), ((flat, C), BF16), ((48, C), F32), ((64, C), F32)],
        pos,
        back,
        got,
        add_10,
        pre_one,
        kernel_one,
    )
    got = seam_exchange(send)
    keep_one, payload_one = grad_of(12, 1, 1, filled_in, wide_one)
    got_one = lax.ppermute(payload_one, "core", CORES)
    part = run(pair_kernel, [((16, 144, C), BF16)], [], pos, keep_one, got_one, keep_two, got_two)[0]
    got, part = lax.optimization_barrier((got, part))
    input_grad = run(
        final_kernel,
        [((192, C), BF16)],
        [((192, C), F32), ((48, C), F32)],
        pos,
        own,
        got,
        add_8,
    )[0]
    part = lax.all_to_all(part, ("y", "x"), 0, 0)
    part = run(lambda *refs: sum_kernel(8, *refs), [((8, 144, C), BF16)], [], pos, part)[0]
    part = lax.all_to_all(part, ("face", "zh"), 0, 0)
    part = run(lambda *refs: sum_kernel(16, *refs), [((16, 144, C), BF16)], [], pos, part)[0]
    part = lax.all_to_all(part, ("y", "x"), 0, 0)
    got = lax.ppermute(part, "core", CORES)
    low, high = jnp.where(core == 0, part, got), jnp.where(core == 0, got, part)
    both = jnp.stack([low, high]).reshape(2, 16, 2, 9, 8, C).transpose(2, 3, 0, 1, 4, 5)
    both = both.reshape(2, 3, 3, C, C).astype(F32)
    return (input_grad.reshape(inputs.shape), both[0], both[1])


def solution(mesh):
    fine = Mesh(np.asarray(mesh.devices).reshape(4, 2, 4, 4, 2), AXES)
    field = P("face", TILE, None, None, None)
    return jax.shard_map(
        body,
        mesh=fine,
        in_specs=(field, field, P(), P(), P(), P()),
        out_specs=(field, P(), P()),
        check_vma=False,
    )
```

time: 249 us -> 237 us (0.952)
  blocking collectives: 0 us -> 76 us
  waiting for transfers between devices: 105 us -> 52.1 us
  starting transfers between devices: 77.8 us -> 48.1 us
  Pallas kernels: 0 us -> 18.5 us
  matrix products: 11.8 us -> 0 us
  local copies, waits for them, and re-layouts: 36.8 us -> 29 us
  other arithmetic: 14.1 us -> 10.5 us
    all_to_all x0 -> x3, blocking collectives: none -> 76 us  [the longest x2 57.5 us: body(): part = lax.all_to_all(part, ('y', 'x'), 0, 0)]
    all_to_all x8 -> x4, waiting for transfers between devices: 98.6 us -> 44.7 us  [seam_exchange(): got = lax.all_to_all(send, AXES, 0, 0, axis_index_groups=SEAM_GROUPS)]
    all_to_all x8 -> x4, starting transfers between devices: 64.4 us -> 31.7 us  [seam_exchange(): got = lax.all_to_all(send, AXES, 0, 0, axis_index_groups=SEAM_GROUPS)]
    pallas_call x0 -> x13, Pallas kernels: none -> 18.5 us  [run(): pl.pallas_call(kernel, out_shape=[jax.ShapeDtypeStruct(shape, dtype) for...]
    mul x0 -> x4, local copies, waits for them, and re-layouts: none -> 11.9 us  [expand(): full = select[:, None, :, :, None] * here[None].astype(BF16)]
    dot_general x10 -> x0, matrix products: 11.8 us -> none  [the longest x1 2.13 us: body(): lax.dot_general(own, delta_one[:, 1:9, 1:9].reshape(192, channels), contr...]
    reshape x16 -> x3, local copies, waits for them, and re-layouts: 11.3 us -> 1.64 us  [expand(): return full.reshape(rows, 16 * block)]
    mul x0 -> x3, other arithmetic: none -> 5.51 us  [expand(): full = select[:, None, :, :, None] * here[None].astype(BF16)]
  transfers between devices with their start and end apart: 18 -> 15, of which waited for: 11 -> 8; matrix products, arithmetic and copies ran while one was open for 11% -> 11% of each run, Pallas kernels for 0% -> 2%
where the time goes in v5:
time: 237 us; the launch traced here: 235 us
  blocking collectives  76 us (32%)
  waiting for transfers between devices  52.1 us (22%)
  starting transfers between devices  48.1 us (20%)
  local copies, waits for them, and re-layouts  29 us (12%)
  Pallas kernels  18.5 us (8%)
  other arithmetic  10.5 us (4%)
    all_to_all x2, blocking collectives, body(): part = lax.all_to_all(part, ('y', 'x'), 0, 0)  57.5 us
    all_to_all x4, waiting for transfers between devices, seam_exchange(): got = lax.all_to_all(send, AXES, 0, 0, axis_index_groups=SEAM_GROUPS)  44.7 us
    all_to_all x4, starting transfers between devices, seam_exchange(): got = lax.all_to_all(send, AXES, 0, 0, axis_index_groups=SEAM_GROUPS)  31.7 us
    all_to_all x1, blocking collectives, body(): part = lax.all_to_all(part, ('face', 'zh'), 0, 0)  18.5 us
    pallas_call x13, Pallas kernels, run(): pl.pallas_call(kernel, out_shape=[jax.ShapeDtypeStruct(shape, dtype) for...  18.5 us
    mul x4, local copies, waits for them, and re-layouts, expand(): full = select[:, None, :, :, None] * here[None].astype(BF16)  11.9 us
    unnamed x28, local copies, waits for them, and re-layouts  7.14 us
    ppermute x2, starting transfers between devices, tall_region(): odd = lax.ppermute(field, TILE, ODD_COLS)  6.51 us
  transfers between devices with their start and end apart: 15, of which 8 were waited for; matrix products, arithmetic and copies ran while one was open for 11% of the time, Pallas kernels for 2%

profile of v5, /device:TPU:1, one launch (start us, length us, event | category | flops | bytes accessed | tf_op | source)
XLA Modules:
  0.0 235.4 jit_solution(2829923681405910425)
XLA Ops:
  0.6 4.6 %collective-permute-start.1 = (bf16[192,256]{1,0:T(8,128)(2,1)}, bf16[192,256]{1,0:T(8,128)(2,1)S(1)}, u32[]{:S(2)}, u32[]{:S(2)}) collective-permute-start(bf16[192,256]{1,0:T(8,128)(2,1)} %bitcast.38), channel_id=1, source_target_pairs={{1,2},{3,4},{5,6},{9,10},{11,12},{13,14},{17,18},{19,20},{21,22},{... | collective-permute-start | bytes 294920 | tf_op jit(solution)/shard_map/ppermute | solution.py:321
  5.9 0.8 add_select_fusion.2
  6.7 0.8 broadcast_in_dim.221
  7.5 0.8 constant_dynamic-slice_fusion
  9.1 0.9 select_reduce_fusion
  10.1 0.9 copy-done.13
  11.7 1.3 collective-permute-start.2
  13.7 1.1 collective-permute-done.2.first
  14.7 1.5 shard_map.86
  16.2 13.0 %all-to-all-start = ((bf16[16,80,256]{2,1,0:T(8,128)(2,1)}), bf16[16,80,256]{2,1,0:T(8,128)(2,1)S(1)}, u32[]{:S(2)}, u32[]{:S(2)}) async-start(bf16[16,80,256]{2,1,0:T(8,128)(2,1)} %get-tuple-element.33), calls=%async_computation | async-start | bytes 1310720 | tf_op jit(solution)/shard_map/all_to_all | solution.py:335
  30.3 1.7 broadcast_multiply_fusion
  32.0 3.2 %mul.93 = bf16[72,16,72]{2,1,0:T(8,128)(2,1)S(1)} reshape(bf16[6,12,16,6,12]{4,3,2,1,0:T(8,128)(2,1)} %broadcast_multiply_fusion) | data formatting | bytes 331776 | tf_op jit(solution)/shard_map/mul | solution.py:378
  35.5 14.9 %all-to-all-done = bf16[16,80,256]{2,1,0:T(8,128)(2,1)S(1)} async-done(((bf16[16,80,256]{2,1,0:T(8,128)(2,1)}), bf16[16,80,256]{2,1,0:T(8,128)(2,1)S(1)}, u32[]{:S(2)}, u32[]{:S(2)}) %all-to-all-start) | async-done | bytes 655392 | tf_op jit(solution)/shard_map/all_to_all | solution.py:335
  50.5 2.6 %shard_map.87 = (bf16[576,256]{1,0:T(8,128)(2,1)S(1)}, f32[480,256]{1,0:T(8,128)S(1)}, bf16[480,256]{1,0:T(8,128)(2,1)S(1)}, bf16[16,64,256]{2,1,0:T(8,128)(2,1)}) custom-call(s32[4]{0:T(128)S(1)} %pad_add_fusion.2.pos.refs_0_, bf16[576,256]{1,0:T(8,128)(2,1)S(1)} %get-tuple-element.32.near, bf16[1280,256]{1,0:T(8,128)(2,1)S(1)} %bitcast.33, ...), custom_call_target="tpu_custom_call" | custom-call | tf_op jit(solution)/shard_map/pallas_call | solution.py:38
  54.5 6.3 %all-to-all-start.1 = ((bf16[16,64,256]{2,1,0:T(8,128)(2,1)}), bf16[16,64,256]{2,1,0:T(8,128)(2,1)S(1)}, u32[]{:S(2)}, u32[]{:S(2)}) async-start(bf16[16,64,256]{2,1,0:T(8,128)(2,1)} %get-tuple-element.35), calls=%async_computation.1 | async-start | bytes 1048576 | tf_op jit(solution)/shard_map/all_to_all | solution.py:335
  61.2 2.4 %broadcast_multiply_fusion.1 = (bf16[6,10,16,6,10]{4,3,2,1,0:T(8,128)(2,1)}, bf16[6,10,16,6,10]{4,3,2,1,0:T(8,128)(2,1)}) fusion(bf16[6,16,6]{2,1,0:T(8,128)(2,1)S(1)} %copy.61, bf16[10,16,6,10]{3,2,1,0:T(8,128)(2,1)S(1)} %select_convert_fusion.1, bf16[6,16,6]{2,1,0:T(8,128)(2,1)S(1)} %copy.53), kind=kLoop, calls=%fused_computation.4 | loop fusion | flops 115200 | bytes 251904 | tf_op jit(solution)/shard_map/mul | solution.py:378
  63.6 3.5 %mul.97 = bf16[60,16,60]{2,1,0:T(8,128)(2,1)} reshape(bf16[6,10,16,6,10]{4,3,2,1,0:T(8,128)(2,1)} %get-tuple-element.76) | data formatting | bytes 230400 | tf_op jit(solution)/shard_map/mul | solution.py:378
  67.1 1.7 pad.12
  68.8 1.1 reshape.411.pick
  69.9 9.7 %all-to-all-done.1 = bf16[16,64,256]{2,1,0:T(8,128)(2,1)S(1)} async-done(((bf16[16,64,256]{2,1,0:T(8,128)(2,1)}), bf16[16,64,256]{2,1,0:T(8,128)(2,1)S(1)}, u32[]{:S(2)}, u32[]{:S(2)}) %all-to-all-start.1) | async-done | bytes 524320 | tf_op jit(solution)/shard_map/all_to_all | solution.py:335
  79.7 0.9 copy-done.7
  80.6 0.9 copy-done.12
  81.5 1.6 shard_map.88
  84.5 1.9 collective-permute-start.5
  86.5 3.9 %collective-permute-done.5.odd = bf16[192,256]{1,0:T(8,128)(2,1)S(1)} collective-permute-done((bf16[192,256]{1,0:T(8,128)(2,1)S(1)}, bf16[192,256]{1,0:T(8,128)(2,1)S(1)}, u32[]{:S(2)}, u32[]{:S(2)}) %collective-permute-start.5) | collective-permute-done | bytes 98336 | tf_op jit(solution)/shard_map/ppermute | solution.py:321
  91.1 2.0 collective-permute-start.6
  93.7 0.8 collective-permute-done.6.first
  94.5 2.2 shard_map.90
  96.8 6.7 %all-to-all-start.2 = ((bf16[16,64,256]{2,1,0:T(8,128)(2,1)}), bf16[16,64,256]{2,1,0:T(8,128)(2,1)S(1)}, u32[]{:S(2)}, u32[]{:S(2)}) async-start(bf16[16,64,256]{2,1,0:T(8,128)(2,1)} %get-tuple-element.41), calls=%async_computation.2 | async-start | bytes 1048576 | tf_op jit(solution)/shard_map/all_to_all | solution.py:335
  103.5 2.8 %mul.100 = bf16[60,16,60]{2,1,0:T(8,128)(2,1)S(1)} reshape(bf16[6,10,16,6,10]{4,3,2,1,0:T(8,128)(2,1)} %get-tuple-element.75) | data formatting | bytes 230400 | tf_op jit(solution)/shard_map/mul | solution.py:378
  106.6 12.6 %all-to-all-done.2 = bf16[16,64,256]{2,1,0:T(8,128)(2,1)S(1)} async-done(((bf16[16,64,256]{2,1,0:T(8,128)(2,1)}), bf16[16,64,256]{2,1,0:T(8,128)(2,1)S(1)}, u32[]{:S(2)}, u32[]{:S(2)}) %all-to-all-start.2) | async-done | bytes 524320 | tf_op jit(solution)/shard_map/all_to_all | solution.py:335
  119.2 2.9 %shard_map.91 = (bf16[384,256]{1,0:T(8,128)(2,1)S(1)}, bf16[192,256]{1,0:T(8,128)(2,1)S(1)}, bf16[16,48,256]{2,1,0:T(8,128)(2,1)}) custom-call(s32[4]{0:T(128)S(1)} %pad_add_fusion.2.pos.refs_0_, bf16[480,256]{1,0:T(8,128)(2,1)S(1)} %get-tuple-element.40.back, bf16[1024,256]{1,0:T(8,128)(2,1)S(1)} %bitcast.35, bf16[64,1024]{1,0:T(8,128)(2,1)S(1)} %reshape.414.pick, ...), custom_call_target="tpu_custom_call" | custom-call | tf_op jit(solution)/shard_map/pallas_call | solution.py:38
  122.7 5.7 %all-to-all-start.3 = ((bf16[16,48,256]{2,1,0:T(8,128)(2,1)}), bf16[16,48,256]{2,1,0:T(8,128)(2,1)S(1)}, u32[]{:S(2)}, u32[]{:S(2)}) async-start(bf16[16,48,256]{2,1,0:T(8,128)(2,1)} %get-tuple-element.44), calls=%async_computation.3 | async-start | bytes 786432 | tf_op jit(solution)/shard_map/all_to_all | solution.py:335
  128.4 1.4 shard_map.93
  129.9 0.9 copy-done.11
  130.9 1.4 shard_map.92
  132.9 1.6 collective-permute-done.8.got_one
  135.2 7.4 %all-to-all-done.3 = bf16[16,48,256]{2,1,0:T(8,128)(2,1)S(1)} async-done(((bf16[16,48,256]{2,1,0:T(8,128)(2,1)}), bf16[16,48,256]{2,1,0:T(8,128)(2,1)S(1)}, u32[]{:S(2)}, u32[]{:S(2)}) %all-to-all-start.3) | async-done | bytes 393248 | tf_op jit(solution)/shard_map/all_to_all | solution.py:335
  142.7 38.5 %all_to_all.35.refs_1_ = bf16[16,144,256]{2,1,0:T(8,128)(2,1)S(1)} all-to-all(bf16[16,144,256]{2,1,0:T(8,128)(2,1)S(1)} %shard_map.94), channel_id=1, replica_groups=mesh['face'=4,'zh'=2,'x'=4,'y'=4,'core'=2] {'y','x'}, dimensions={0} | all-to-all | bytes 2359296 | tf_op jit(solution)/shard_map/all_to_all | solution.py:480
  181.9 18.5 %all_to_all.36.refs_1_ = bf16[8,144,256]{2,1,0:T(8,128)(2,1)S(1)} all-to-all(bf16[8,144,256]{2,1,0:T(8,128)(2,1)S(1)} %shard_map.96), channel_id=1, replica_groups=mesh['face'=4,'zh'=2,'x'=4,'y'=4,'core'=2] {'face','zh'}, dimensions={0} | all-to-all | bytes 1179648 | tf_op jit(solution)/shard_map/all_to_all | solution.py:482
  201.1 19.0 %all_to_all.37 = bf16[16,144,256]{2,1,0:T(8,128)(2,1)S(1)} all-to-all(bf16[16,144,256]{2,1,0:T(8,128)(2,1)S(1)} %shard_map.97), channel_id=1, replica_groups=mesh['face'=4,'zh'=2,'x'=4,'y'=4,'core'=2] {'y','x'}, dimensions={0} | all-to-all | bytes 2359296 | tf_op jit(solution)/shard_map/all_to_all | solution.py:484
  220.0 4.5 %collective-permute-start.10 = (bf16[16,144,256]{2,1,0:T(8,128)(2,1)S(1)}, bf16[16,144,256]{2,1,0:T(8,128)(2,1)}, u32[]{:S(2)}, u32[]{:S(2)}) collective-permute-start(bf16[16,144,256]{2,1,0:T(8,128)(2,1)S(1)} %all_to_all.37), channel_id=1, source_target_pairs={{0,1},{1,0},{2,3},{3,2},{4,5},{5,4},{6,7},{7,6},{8,9},{9,8},{10,11... | collective-permute-start | bytes 3538952 | tf_op jit(solution)/shard_map/ppermute | solution.py:485
  224.7 1.3 broadcast_multiply_fusion.3
  226.0 2.5 %mul.104.pick = bf16[48,768]{1,0:T(8,128)(2,1)S(1)} reshape(bf16[6,8,16,6,8]{4,3,2,1,0:T(8,128)(2,1)} %broadcast_multiply_fusion.3) | data formatting | bytes 147456 | tf_op jit(solution)/shard_map/mul | solution.py:378
  228.5 1.4 shard_map.95
  229.9 1.4 broadcast_select_fusion.1
  232.1 1.7 copy.65
  233.8 1.7 copy.64
  (93 shorter events, 13.3 us)
Async XLA Ops:
  0.6 9.5 %collective-permute-start.1 = (bf16[192,256]{1,0:T(8,128)(2,1)}, bf16[192,256]{1,0:T(8,128)(2,1)S(1)}, u32[]{:S(2)}, u32[]{:S(2)}) collective-permute-start(bf16[192,256]{1,0:T(8,128)(2,1)} %bitcast.38), channel_id=1, source_target_pairs={{1,2},{3,4},{5,6},{9,10},{11,12},{13,14},{17,18},{19,20},{21,22},{... | collective-permute-start | bytes 294920 | tf_op jit(solution)/shard_map/ppermute | solution.py:321
  5.2 4.9 %collective-permute-start = (bf16[192,256]{1,0:T(8,128)(2,1)}, bf16[192,256]{1,0:T(8,128)(2,1)S(1)}, u32[]{:S(2)}, u32[]{:S(2)}) collective-permute-start(bf16[192,256]{1,0:T(8,128)(2,1)} %bitcast.39), channel_id=1, source_target_pairs={{0,1},{1,0},{2,3},{3,2},{4,5},{5,4},{6,7},{7,6},{8,9},{9,8},{10,11... | collective-permute-start | bytes 294920 | tf_op jit(solution)/shard_map/ppermute | solution.py:320
  10.1 0.9 copy-start.13
  11.7 3.0 %collective-permute-start.2 = (bf16[96,256]{1,0:T(8,128)(2,1)S(1)}, bf16[96,256]{1,0:T(8,128)(2,1)S(1)}, u32[]{:S(2)}, u32[]{:S(2)}) collective-permute-start(bf16[96,256]{1,0:T(8,128)(2,1)S(1)} %get-tuple-element.30), channel_id=1, source_target_pairs={{0,8},{1,9},{2,10},{3,11},{4,12},{5,13},{6,14},{7,15},{16,24},{17,... | collective-permute-start | bytes 147464 | tf_op jit(solution)/shard_map/ppermute | solution.py:331
  13.0 1.7 collective-permute-start.3
  16.2 34.2 %all-to-all-start = ((bf16[16,80,256]{2,1,0:T(8,128)(2,1)}), bf16[16,80,256]{2,1,0:T(8,128)(2,1)S(1)}, u32[]{:S(2)}, u32[]{:S(2)}) async-start(bf16[16,80,256]{2,1,0:T(8,128)(2,1)} %get-tuple-element.33), calls=%async_computation | async-start | bytes 1310720 | tf_op jit(solution)/shard_map/all_to_all | solution.py:335
  32.0 18.5 %copy-start.1 = (bf16[3,3,256,256]{3,2,1,0:T(8,128)(2,1)S(1)}, bf16[3,3,256,256]{3,2,1,0:T(8,128)(2,1)}, u32[]{:S(2)}) copy-start(bf16[3,3,256,256]{3,2,1,0:T(8,128)(2,1)} %kernel.7) | copy-start | bytes 3538948
  53.1 0.7 copy-start.2
  53.9 0.7 copy-start.6
  54.5 25.1 %all-to-all-start.1 = ((bf16[16,64,256]{2,1,0:T(8,128)(2,1)}), bf16[16,64,256]{2,1,0:T(8,128)(2,1)S(1)}, u32[]{:S(2)}, u32[]{:S(2)}) async-start(bf16[16,64,256]{2,1,0:T(8,128)(2,1)} %get-tuple-element.35), calls=%async_computation.1 | async-start | bytes 1048576 | tf_op jit(solution)/shard_map/all_to_all | solution.py:335
  63.6 16.1 %copy-start = (bf16[3,3,256,256]{3,2,1,0:T(8,128)(2,1)S(1)}, bf16[3,3,256,256]{3,2,1,0:T(8,128)(2,1)}, u32[]{:S(2)}) copy-start(bf16[3,3,256,256]{3,2,1,0:T(8,128)(2,1)} %kernel.6) | copy-start | bytes 3538948
  79.7 0.9 copy-start.7
  80.6 0.9 copy-start.12
  83.1 0.7 copy-start.4
  83.8 0.7 copy-start.8
  84.5 5.9 %collective-permute-start.5 = (bf16[192,256]{1,0:T(8,128)(2,1)S(1)}, bf16[192,256]{1,0:T(8,128)(2,1)S(1)}, u32[]{:S(2)}, u32[]{:S(2)}) collective-permute-start(bf16[192,256]{1,0:T(8,128)(2,1)S(1)} %get-tuple-element.36.own), channel_id=1, source_target_pairs={{1,2},{3,4},{5,6},{9,10},{11,12},{13,14},{17,18},{19,20},{21,22},{... | collective-permute-start | bytes 294920 | tf_op jit(solution)/shard_map/ppermute | solution.py:321
  86.4 4.0 %collective-permute-start.4 = (bf16[192,256]{1,0:T(8,128)(2,1)S(1)}, bf16[192,256]{1,0:T(8,128)(2,1)S(1)}, u32[]{:S(2)}, u32[]{:S(2)}) collective-permute-start(bf16[192,256]{1,0:T(8,128)(2,1)S(1)} %get-tuple-element.36.own), channel_id=1, source_target_pairs={{0,1},{1,0},{2,3},{3,2},{4,5},{5,4},{6,7},{7,6},{8,9},{9,8},{10,11... | collective-permute-start | bytes 294920 | tf_op jit(solution)/shard_map/ppermute | solution.py:320
  91.1 3.5 %collective-permute-start.6 = (bf16[96,256]{1,0:T(8,128)(2,1)S(1)}, bf16[96,256]{1,0:T(8,128)(2,1)S(1)}, u32[]{:S(2)}, u32[]{:S(2)}) collective-permute-start(bf16[96,256]{1,0:T(8,128)(2,1)S(1)} %get-tuple-element.38), channel_id=1, source_target_pairs={{0,8},{1,9},{2,10},{3,11},{4,12},{5,13},{6,14},{7,15},{16,24},{17,... | collective-permute-start | bytes 147464 | tf_op jit(solution)/shard_map/ppermute | solution.py:331
  93.1 1.5 collective-permute-start.7
  96.8 22.4 %all-to-all-start.2 = ((bf16[16,64,256]{2,1,0:T(8,128)(2,1)}), bf16[16,64,256]{2,1,0:T(8,128)(2,1)S(1)}, u32[]{:S(2)}, u32[]{:S(2)}) async-start(bf16[16,64,256]{2,1,0:T(8,128)(2,1)} %get-tuple-element.41), calls=%async_computation.2 | async-start | bytes 1048576 | tf_op jit(solution)/shard_map/all_to_all | solution.py:335
  106.3 22.0 %copy-start.5 = (bf16[480,256]{1,0:T(8,128)(2,1)S(1)}, bf16[480,256]{1,0:T(8,128)(2,1)}, u32[]{:S(2)}) copy-start(bf16[480,256]{1,0:T(8,128)(2,1)} %copy-done.4) | copy-start | bytes 737284
  106.3 22.0 %copy-start.9 = (bf16[384,256]{1,0:T(8,128)(2,1)S(1)}, bf16[384,256]{1,0:T(8,128)(2,1)}, u32[]{:S(2)}) copy-start(bf16[384,256]{1,0:T(8,128)(2,1)} %copy-done.8) | copy-start | bytes 589828
  106.6 23.4 %copy-start.3 = (bf16[576,256]{1,0:T(8,128)(2,1)S(1)}, bf16[576,256]{1,0:T(8,128)(2,1)}, u32[]{:S(2)}) copy-start(bf16[576,256]{1,0:T(8,128)(2,1)} %copy-done.2) | copy-start | bytes 884740
  122.0 0.7 copy-start.10
  122.7 20.0 %all-to-all-start.3 = ((bf16[16,48,256]{2,1,0:T(8,128)(2,1)}), bf16[16,48,256]{2,1,0:T(8,128)(2,1)S(1)}, u32[]{:S(2)}, u32[]{:S(2)}) async-start(bf16[16,48,256]{2,1,0:T(8,128)(2,1)} %get-tuple-element.44), calls=%async_computation.3 | async-start | bytes 786432 | tf_op jit(solution)/shard_map/all_to_all | solution.py:335
  129.8 3.1 %collective-permute-start.9 = (bf16[16,72,256]{2,1,0:T(8,128)(2,1)S(1)}, bf16[16,72,256]{2,1,0:T(8,128)(2,1)S(1)}, u32[]{:S(2)}, u32[]{:S(2)}) collective-permute-start(bf16[16,72,256]{2,1,0:T(8,128)(2,1)S(1)} %get-tuple-element.52), channel_id=1, source_target_pairs={{0,1},{1,0},{2,3},{3,2},{4,5},{5,4},{6,7},{7,6},{8,9},{9,8},{10,11... | collective-permute-start | bytes 1769480 | tf_op jit(solution)/shard_map/ppermute | solution.py:454
  129.9 0.9 copy-start.11
  132.3 2.2 collective-permute-start.8
  220.0 9.9 %collective-permute-start.10 = (bf16[16,144,256]{2,1,0:T(8,128)(2,1)S(1)}, bf16[16,144,256]{2,1,0:T(8,128)(2,1)}, u32[]{:S(2)}, u32[]{:S(2)}) collective-permute-start(bf16[16,144,256]{2,1,0:T(8,128)(2,1)S(1)} %all_to_all.37), channel_id=1, source_target_pairs={{0,1},{1,0},{2,3},{3,2},{4,5},{5,4},{6,7},{7,6},{8,9},{9,8},{10,11... | collective-permute-start | bytes 3538952 | tf_op jit(solution)/shard_map/ppermute | solution.py:485

commit v6 on v5

--- a/solution.py
+++ b/solution.py
@@ -26,11 +26,29 @@
 ODD_COLS = swap_pairs([(r * 8 + c, r * 8 + c + 1) for r in range(8) for c in (1, 3, 5)])
 EVEN_ROWS = swap_pairs([(r * 8 + c, r * 8 + 8 + c) for r in (0, 2, 4, 6) for c in range(8)])
 ODD_ROWS = swap_pairs([(r * 8 + c, r * 8 + 8 + c) for r in (1, 3, 5) for c in range(8)])
-SEAM_GROUPS = [
-    [f * 64 + (t ^ m) for f in range(4) for m in MIRRORS]
-    for t in range(64)
-    if t == min(t ^ m for m in MIRRORS)
+
+
+def seam_groups():
+    groups = []
+    for t in range(64):
+        row, col = divmod(t, 8)
+        if row < 4 and col < 4 and (min(row, col) == 0 or row == col == 1):
+            groups.append([f * 64 + (t ^ m) for f in range(4) for m in MIRRORS])
+    inner = [t for t in range(64) if 0 < t // 8 < 7 and 0 < t % 8 < 7 and t not in (9, 14, 49, 54)]
+    for f in range(4):
+        groups.append([f * 64 + t for t in inner if t < 32])
+        groups.append([f * 64 + t for t in inner if t >= 32])
+    return groups
+
+
+SEAM_GROUPS = seam_groups()
+PLANE_GROUPS = [
+    [f * 64 + zh * 32 + (3 - q if zh else q) * 8 + y * 2 + core for y in range(4) for q in range(4)]
+    for f in range(4)
+    for zh in range(2)
+    for core in range(2)
 ]
+ACROSS_GROUPS = [[f * 64 + (t ^ m) for f in range(4) for m in (0, 56)] for t in range(32)]
 
 
 def run(kernel, outs, scratch, pos, *args):
@@ -248,7 +266,7 @@
     total = convolve(cells, shifts, 12, 10, 0, kernel, True)
     grads[...] = total
     take_strips(grads, strips, row, col, 10, 0, 9, 1, 8)
-    post_strips(strips, send)
+    send[...] = strips[...].astype(BF16)
     for f in range(3):
         for i in range(8):
             begin = (f * 10 + i + 1) * PITCH + 1
@@ -259,7 +277,8 @@
 
 def final_kernel(pos, own, got, pick, out, cells, lines):
     row, col = pos[0], pos[1]
-    lines[...] = dot(pick[...], got[...], ((1,), (0,)))
+    strips = jnp.concatenate([got[i, 144:240, :] for i in range(8)], axis=0)
+    lines[...] = dot(pick[...], strips, ((1,), (0,)))
     cells[...] = own[...].astype(F32)
     for f in range(3):
         base = f * 64
@@ -307,13 +326,38 @@
         out[i] = jnp.concatenate([one, two], axis=0).astype(BF16)
 
 
-def sum_kernel(copies, pos, parts, out):
+def across_kernel(pos, parts, mine, mirrored, out):
     total = parts[0].astype(F32)
-    for i in range(1, parts.shape[0]):
+    for i in range(1, 16):
         total = total + parts[i].astype(F32)
+    total = jnp.concatenate([total.astype(BF16), mine[...], mirrored[...]], axis=0)
+    for i in range(8):
+        out[i] = total
+
+
+def gather_kernel(pos, parts, out):
+    total = parts[0, 0:144, :].astype(F32)
+    for i in range(1, 8):
+        total = total + parts[i, 0:144, :].astype(F32)
     total = total.astype(BF16)
-    for i in range(copies):
+    for i in range(16):
         out[i] = total
+
+
+def place_kernel(pos, mine, other, one, two, rows, sems):
+    core = pos[2]
+    copies = []
+    for at, source in ((core, mine), (1 - core, other)):
+        begin = pl.multiple_of(at * 128, 128)
+        for p in range(16):
+            block = source[p].astype(F32)
+            for k in range(18):
+                rows[k, pl.ds(begin + p * 8, 8), :] = block[k * 8 : (k + 1) * 8]
+    for k, target in ((0, one), (1, two)):
+        copies.append(pltpu.make_async_copy(rows.at[pl.ds(9 * k, 9)], target, sems.at[k]))
+        copies[-1].start()
+    for copy in copies:
+        copy.wait()
 
 
 def tall_region(field, pos):
@@ -337,6 +381,15 @@
 
 
 def seam_picks(neighbour, seam_codes, row, col, face_group):
+    in_group = seam_select(neighbour, seam_codes, row, col, face_group, 0)
+    gather, add, turned = in_group
+    wide_pick, pick = expand(gather, turned, 12, 80), expand(gather, turned, 10, 64)
+    add_10 = expand(add, turned, 10, 64)
+    _, add, turned = seam_select(neighbour, seam_codes, row, col, face_group, col // 4)
+    return wide_pick, pick, add_10, expand(add, turned, 8, 48)
+
+
+def seam_select(neighbour, seam_codes, row, col, face_group, order):
     mirror = col // 4 + 2 * (row // 4)
     on_edge = jnp.stack([(row == 0) | (row == 7), (col == 0) | (col == 7)])
     bottom, right = row // 4, col // 4
@@ -345,7 +398,7 @@
     opposite, reverse = 1 - seam_codes % 2, seam_codes // 2
     types = jnp.arange(4) // 2
     rel_of = jnp.where(types == 0, 2 * opposite + reverse, 2 * reverse + opposite)
-    slot_mirror = jnp.arange(4, dtype=jnp.int32)
+    slot_mirror = jnp.arange(4, dtype=jnp.int32) ^ order
     slot_type = jnp.arange(2, dtype=jnp.int32)
 
     def on_side(table, side):
@@ -370,18 +423,19 @@
     add = (slot_next == own_faces) & (slot_rel == rel[:, None, None]) & same_type
     turned = jnp.stack([rel % 2, rel // 2], axis=1) == 1
 
-    def expand(select, length, block):
-        select = select.reshape(6, 16, 6).astype(BF16)
-        flip = jnp.broadcast_to(turned[None, :, None, :], (4, 4, 3, 2)).reshape(16, 6)
-        at = jnp.arange(length, dtype=jnp.int32)
-        here = jnp.where(flip[None, :, :, None], at[:, None, None, None] + at == length - 1, at[:, None, None, None] == at)
-        full = select[:, None, :, :, None] * here[None].astype(BF16)
-        full = full.reshape(6 * length, 16, 6 * length)
-        rows = -(-6 * length // 16) * 16
-        full = jnp.pad(full, ((0, rows - 6 * length), (0, 0), (0, block - 6 * length)))
-        return full.reshape(rows, 16 * block)
-
-    return expand(gather, 12, 80), expand(gather, 10, 64), expand(add, 10, 64), expand(add, 8, 48)
+    return gather, add, turned
+
+
+def expand(select, turned, length, block):
+    select = select.reshape(6, 16, 6).astype(BF16)
+    flip = jnp.broadcast_to(turned[None, :, None, :], (4, 4, 3, 2)).reshape(16, 6)
+    at = jnp.arange(length, dtype=jnp.int32)
+    here = jnp.where(flip[None, :, :, None], at[:, None, None, None] + at == length - 1, at[:, None, None, None] == at)
+    full = select[:, None, :, :, None] * here[None].astype(BF16)
+    full = full.reshape(6 * length, 16, 6 * length)
+    rows = -(-6 * length // 16) * 16
+    full = jnp.pad(full, ((0, rows - 6 * length), (0, 0), (0, block - 6 * length)))
+    return full.reshape(rows, 16 * block)
 
 
 def body(inputs, cotangent, kernel_one, kernel_two, neighbour, seam_codes):
@@ -389,7 +443,7 @@
     core = lax.axis_index("core")
     row = lax.axis_index("zh") * 4 + lax.axis_index("x")
     col = lax.axis_index("y") * 2 + core
-    pos = jnp.stack([row, col, core, face_group]).astype(jnp.int32)
+    pos = jnp.stack([row, col, core]).astype(jnp.int32)
     pick_12, pick_10, add_10, add_8 = seam_picks(neighbour, seam_codes, row, col, face_group)
     flat = 36 * PITCH
     spare = flat + 8
@@ -452,9 +506,10 @@
 
     keep_two, payload_two = grad_of(10, 0, 0, filled_hidden, wide_two)
     got_two = lax.ppermute(payload_two, "core", CORES)
-    wide_one, own, send = run(
+    got, add_8 = lax.optimization_barrier((got, add_8))
+    wide_one, own, strips = run(
         delta_kernel,
-        [((24 * PITCH, C), BF16), ((192, C), BF16), ((16, 48, C), BF16)],
+        [((24 * PITCH, C), BF16), ((192, C), BF16), ((48, C), BF16)],
         [((spare, C), F32), ((30 * PITCH, C), F32), ((flat, C), BF16), ((48, C), F32), ((64, C), F32)],
         pos,
         back,
@@ -463,11 +518,14 @@
         pre_one,
         kernel_one,
     )
-    got = seam_exchange(send)
+    mirrored = lax.ppermute(strips, TILE, [(t, t ^ 7) for t in range(64)])
     keep_one, payload_one = grad_of(12, 1, 1, filled_in, wide_one)
     got_one = lax.ppermute(payload_one, "core", CORES)
     part = run(pair_kernel, [((16, 144, C), BF16)], [], pos, keep_one, got_one, keep_two, got_two)[0]
-    got, part = lax.optimization_barrier((got, part))
+    part = lax.all_to_all(part, AXES, 0, 0, axis_index_groups=PLANE_GROUPS)
+    part = run(across_kernel, [((8, 240, C), BF16)], [], pos, part, strips, mirrored)[0]
+    got = lax.all_to_all(part, AXES, 0, 0, axis_index_groups=ACROSS_GROUPS)
+    part = run(gather_kernel, [((16, 144, C), BF16)], [], pos, got)[0]
     input_grad = run(
         final_kernel,
         [((192, C), BF16)],
@@ -477,16 +535,18 @@
         got,
         add_8,
     )[0]
-    part = lax.all_to_all(part, ("y", "x"), 0, 0)
-    part = run(lambda *refs: sum_kernel(8, *refs), [((8, 144, C), BF16)], [], pos, part)[0]
-    part = lax.all_to_all(part, ("face", "zh"), 0, 0)
-    part = run(lambda *refs: sum_kernel(16, *refs), [((16, 144, C), BF16)], [], pos, part)[0]
-    part = lax.all_to_all(part, ("y", "x"), 0, 0)
+    part = lax.all_to_all(part, AXES, 0, 0, axis_index_groups=PLANE_GROUPS)
     got = lax.ppermute(part, "core", CORES)
-    low, high = jnp.where(core == 0, part, got), jnp.where(core == 0, got, part)
-    both = jnp.stack([low, high]).reshape(2, 16, 2, 9, 8, C).transpose(2, 3, 0, 1, 4, 5)
-    both = both.reshape(2, 3, 3, C, C).astype(F32)
-    return (input_grad.reshape(inputs.shape), both[0], both[1])
+    grads = pl.pallas_call(
+        place_kernel,
+        out_shape=[jax.ShapeDtypeStruct((9, C, C), F32)] * 2,
+        in_specs=[pl.BlockSpec(memory_space=pltpu.SMEM)] + [pl.BlockSpec(memory_space=pltpu.VMEM)] * 2,
+        out_specs=[pl.BlockSpec(memory_space=pl.ANY)] * 2,
+        scratch_shapes=[pltpu.VMEM((18, C, C), F32), pltpu.SemaphoreType.DMA((2,))],
+        compiler_params=pltpu.CompilerParams(vmem_limit_bytes=24 * 2**20),
+    )(pos, part, got)
+    one, two = (grad.reshape(3, 3, C, C) for grad in grads)
+    return (input_grad.reshape(inputs.shape), one, two)
 
 
 def solution(mesh):

time: 237 us -> 215 us (0.907)
  blocking collectives: 76 us -> 46.6 us
  waiting for transfers between devices: 52.1 us -> 58.7 us
  Pallas kernels: 18.5 us -> 22.6 us
  local copies, waits for them, and re-layouts: 29 us -> 25.2 us
    all_to_all x3 -> x2, blocking collectives: 76 us -> 46.6 us  [the longest x1 26.6 us: body(): got = lax.all_to_all(part, AXES, 0, 0, axis_index_groups=ACROSS_GROUPS)]
    all_to_all x4 -> x3, waiting for transfers between devices: 44.7 us -> 34.2 us  [seam_exchange(): got = lax.all_to_all(send, AXES, 0, 0, axis_index_groups=SEAM_GROUPS)]
    ppermute x0 -> x1, waiting for transfers between devices: none -> 10.4 us  [body(): mirrored = lax.ppermute(strips, TILE, [(t, t ^ 7) for t in range(64)])]
    all_to_all x4 -> x3, starting transfers between devices: 31.7 us -> 25.9 us  [seam_exchange(): got = lax.all_to_all(send, AXES, 0, 0, axis_index_groups=SEAM_GROUPS)]
    all_to_all x0 -> x1, starting transfers between devices: none -> 4.3 us  [body(): part = lax.all_to_all(part, AXES, 0, 0, axis_index_groups=PLANE_GROUPS)]
    all_to_all x0 -> x1, waiting for transfers between devices: none -> 4.24 us  [body(): part = lax.all_to_all(part, AXES, 0, 0, axis_index_groups=PLANE_GROUPS)]
    slice x3 -> x0, local copies, waits for them, and re-layouts: 3.75 us -> none  [body(): return (input_grad.reshape(inputs.shape), both[0], both[1])]
    ppermute x0 -> x1, starting transfers between devices: none -> 3.38 us  [body(): mirrored = lax.ppermute(strips, TILE, [(t, t ^ 7) for t in range(64)])]
  transfers between devices with their start and end apart: 15 -> 16, of which waited for: 8 -> 10; matrix products, arithmetic and copies ran while one was open for 11% -> 12% of each run, Pallas kernels for 2% -> 3%
where the time goes in v6:
time: 215 us; the launch traced here: 211 us
  waiting for transfers between devices  58.7 us (27%)
  starting transfers between devices  48.4 us (23%)
  blocking collectives  46.6 us (22%)
  local copies, waits for them, and re-layouts  25.2 us (12%)
  Pallas kernels  22.6 us (11%)
  other arithmetic  8.62 us (4%)
    all_to_all x3, waiting for transfers between devices, seam_exchange(): got = lax.all_to_all(send, AXES, 0, 0, axis_index_groups=SEAM_GROUPS)  34.2 us
    all_to_all x1, blocking collectives, body(): got = lax.all_to_all(part, AXES, 0, 0, axis_index_groups=ACROSS_GROUPS)  26.6 us
    all_to_all x3, starting transfers between devices, seam_exchange(): got = lax.all_to_all(send, AXES, 0, 0, axis_index_groups=SEAM_GROUPS)  25.9 us
    all_to_all x1, blocking collectives, body(): part = lax.all_to_all(part, AXES, 0, 0, axis_index_groups=PLANE_GROUPS)  20.1 us
    pallas_call x13, Pallas kernels, run(): pl.pallas_call(kernel, out_shape=[jax.ShapeDtypeStruct(shape, dtype) for...  19.5 us
    mul x4, local copies, waits for them, and re-layouts, expand(): full = select[:, None, :, :, None] * here[None].astype(BF16)  10.7 us
    ppermute x1, waiting for transfers between devices, body(): mirrored = lax.ppermute(strips, TILE, [(t, t ^ 7) for t in range(64)])  10.4 us
    unnamed x40, local copies, waits for them, and re-layouts  8.13 us
  transfers between devices with their start and end apart: 16, of which 10 were waited for; matrix products, arithmetic and copies ran while one was open for 12% of the time, Pallas kernels for 3%

profile of v6, /device:TPU:1, one launch (start us, length us, event | category | flops | bytes accessed | tf_op | source)
XLA Modules:
  0.0 211.5 jit_solution(12358553345214865844)
XLA Ops:
  0.6 4.6 %collective-permute-start.1 = (bf16[192,256]{1,0:T(8,128)(2,1)}, bf16[192,256]{1,0:T(8,128)(2,1)S(1)}, u32[]{:S(2)}, u32[]{:S(2)}) collective-permute-start(bf16[192,256]{1,0:T(8,128)(2,1)} %bitcast.35), channel_id=1, source_target_pairs={{1,2},{3,4},{5,6},{9,10},{11,12},{13,14},{17,18},{19,20},{21,22},{... | collective-permute-start | bytes 294920 | tf_op jit(solution)/shard_map/ppermute | solution.py:365
  6.0 0.8 add_select_fusion.2
  6.8 0.8 broadcast_in_dim.251
  9.2 1.8 select_reduce_fusion.1
  11.1 0.9 copy-done.17
  12.7 1.3 collective-permute-start.2
  14.6 1.1 collective-permute-done.2.first
  15.7 1.5 shard_map.86
  17.2 13.0 %all-to-all-start = ((bf16[16,80,256]{2,1,0:T(8,128)(2,1)}), bf16[16,80,256]{2,1,0:T(8,128)(2,1)S(1)}, u32[]{:S(2)}, u32[]{:S(2)}) async-start(bf16[16,80,256]{2,1,0:T(8,128)(2,1)} %get-tuple-element.35), calls=%async_computation | async-start | bytes 1310720 | tf_op jit(solution)/shard_map/all_to_all | solution.py:379
  31.4 1.7 broadcast_multiply_fusion
  33.1 3.2 %mul.97 = bf16[72,16,72]{2,1,0:T(8,128)(2,1)S(1)} reshape(bf16[6,12,16,6,12]{4,3,2,1,0:T(8,128)(2,1)} %broadcast_multiply_fusion) | data formatting | bytes 331776 | tf_op jit(solution)/shard_map/mul | solution.py:434
  36.7 14.8 %all-to-all-done = bf16[16,80,256]{2,1,0:T(8,128)(2,1)S(1)} async-done(((bf16[16,80,256]{2,1,0:T(8,128)(2,1)}), bf16[16,80,256]{2,1,0:T(8,128)(2,1)S(1)}, u32[]{:S(2)}, u32[]{:S(2)}) %all-to-all-start) | async-done | bytes 655392 | tf_op jit(solution)/shard_map/all_to_all | solution.py:379
  51.5 2.7 %shard_map.87 = (bf16[576,256]{1,0:T(8,128)(2,1)S(1)}, f32[480,256]{1,0:T(8,128)S(1)}, bf16[480,256]{1,0:T(8,128)(2,1)S(1)}, bf16[16,64,256]{2,1,0:T(8,128)(2,1)}) custom-call(s32[3]{0:T(128)S(1)} %pad_add_fusion.3.pos.refs_0_, bf16[576,256]{1,0:T(8,128)(2,1)S(1)} %get-tuple-element.34.near, bf16[1280,256]{1,0:T(8,128)(2,1)S(1)} %bitcast.31, ...), custom_call_target="tpu_custom_call" | custom-call | tf_op jit(solution)/shard_map/pallas_call | solution.py:56
  54.2 0.8 copy-done.3
  55.7 6.2 %all-to-all-start.1 = ((bf16[16,64,256]{2,1,0:T(8,128)(2,1)}), bf16[16,64,256]{2,1,0:T(8,128)(2,1)S(1)}, u32[]{:S(2)}, u32[]{:S(2)}) async-start(bf16[16,64,256]{2,1,0:T(8,128)(2,1)} %get-tuple-element.37), calls=%async_computation.1 | async-start | bytes 1048576 | tf_op jit(solution)/shard_map/all_to_all | solution.py:379
  62.2 2.4 %broadcast_multiply_fusion.1 = (bf16[6,10,16,6,10]{4,3,2,1,0:T(8,128)(2,1)}, bf16[6,10,16,6,10]{4,3,2,1,0:T(8,128)(2,1)}) fusion(bf16[6,16,6]{2,1,0:T(8,128)(2,1)S(1)} %copy.63, bf16[10,16,6,10]{3,2,1,0:T(8,128)(2,1)S(1)} %select_convert_fusion.1, bf16[6,16,6]{2,1,0:T(8,128)(2,1)S(1)} %copy.51), kind=kLoop, calls=%fused_computation.1 | loop fusion | flops 115200 | bytes 251904 | tf_op jit(solution)/shard_map/mul | solution.py:434
  64.6 2.9 %mul.101 = bf16[60,16,60]{2,1,0:T(8,128)(2,1)S(1)} reshape(bf16[6,10,16,6,10]{4,3,2,1,0:T(8,128)(2,1)} %get-tuple-element.82) | data formatting | bytes 230400 | tf_op jit(solution)/shard_map/mul | solution.py:434
  67.5 0.8 pad.12
  68.3 1.1 reshape.538.pick
  69.4 11.5 %all-to-all-done.1 = bf16[16,64,256]{2,1,0:T(8,128)(2,1)S(1)} async-done(((bf16[16,64,256]{2,1,0:T(8,128)(2,1)}), bf16[16,64,256]{2,1,0:T(8,128)(2,1)S(1)}, u32[]{:S(2)}, u32[]{:S(2)}) %all-to-all-start.1) | async-done | bytes 524320 | tf_op jit(solution)/shard_map/all_to_all | solution.py:379
  80.9 1.6 shard_map.88
  83.9 1.9 collective-permute-start.5
  85.9 3.9 %collective-permute-done.5.odd = bf16[192,256]{1,0:T(8,128)(2,1)S(1)} collective-permute-done((bf16[192,256]{1,0:T(8,128)(2,1)S(1)}, bf16[192,256]{1,0:T(8,128)(2,1)S(1)}, u32[]{:S(2)}, u32[]{:S(2)}) %collective-permute-start.5) | collective-permute-done | bytes 98336 | tf_op jit(solution)/shard_map/ppermute | solution.py:365
  91.6 1.9 collective-permute-done.6.first
  93.5 2.2 %shard_map.90 = (bf16[480,256]{1,0:T(8,128)(2,1)S(1)}, bf16[16,64,256]{2,1,0:T(8,128)(2,1)}) custom-call(s32[3]{0:T(128)S(1)} %pad_add_fusion.3.pos.refs_0_, bf16[384,256]{1,0:T(8,128)(2,1)S(1)} %get-tuple-element.39.wide, bf16[96,256]{1,0:T(8,128)(2,1)S(1)} %collective-permute-done.6.first, bf16[96,256]{1,0:T(8,128)(2,1)S(1)} %collective-permute-done.7.second, ...), custom_call_target="tpu_custom_call" | custom-call | tf_op jit(solution)/shard_map/pallas_call | solution.py:56
  96.4 6.7 %all-to-all-start.2 = ((bf16[16,64,256]{2,1,0:T(8,128)(2,1)}), bf16[16,64,256]{2,1,0:T(8,128)(2,1)S(1)}, u32[]{:S(2)}, u32[]{:S(2)}) async-start(bf16[16,64,256]{2,1,0:T(8,128)(2,1)} %get-tuple-element.43), calls=%async_computation.2 | async-start | bytes 1048576 | tf_op jit(solution)/shard_map/all_to_all | solution.py:379
  103.8 1.9 mul.105.pick
  105.7 2.8 %mul.108 = bf16[60,16,60]{2,1,0:T(8,128)(2,1)S(1)} reshape(bf16[6,10,16,6,10]{4,3,2,1,0:T(8,128)(2,1)} %get-tuple-element.81) | data formatting | bytes 230400 | tf_op jit(solution)/shard_map/mul | solution.py:434
  108.6 0.8 reshape.541.pick
  109.4 2.2 %shard_map.93 = (f32[16,72,256]{2,1,0:T(8,128)S(1)}, bf16[16,72,256]{2,1,0:T(8,128)(2,1)}) custom-call(s32[3]{0:T(128)S(1)} %pad_add_fusion.3.pos.refs_0_, bf16[480,256]{1,0:T(8,128)(2,1)S(1)} %copy-done.9, bf16[384,256]{1,0:T(8,128)(2,1)S(1)} %copy-done.13), custom_call_target="tpu_custom_call" | custom-call | tf_op jit(solution)/shard_map/pallas_call | solution.py:56
  111.7 7.9 %all-to-all-done.2 = bf16[16,64,256]{2,1,0:T(8,128)(2,1)S(1)} async-done(((bf16[16,64,256]{2,1,0:T(8,128)(2,1)}), bf16[16,64,256]{2,1,0:T(8,128)(2,1)S(1)}, u32[]{:S(2)}, u32[]{:S(2)}) %all-to-all-start.2) | async-done | bytes 524320 | tf_op jit(solution)/shard_map/all_to_all | solution.py:379
  119.6 0.9 copy-done.2
  120.5 1.0 copy-done.4
  121.5 0.9 copy-done.11
  122.5 1.9 shard_map.91
  124.5 1.4 shard_map.92
  126.0 2.0 collective-permute-done.8.got_one
  128.0 1.7 shard_map.94
  129.8 4.3 %all-to-all-start.3 = ((bf16[16,144,256]{2,1,0:T(8,128)(2,1)}), bf16[16,144,256]{2,1,0:T(8,128)(2,1)S(1)}, u32[]{:S(2)}, u32[]{:S(2)}) async-start(bf16[16,144,256]{2,1,0:T(8,128)(2,1)} %shard_map.94), calls=%async_computation.3 | async-start | bytes 2359296 | tf_op jit(solution)/shard_map/all_to_all | solution.py:525
  134.1 3.4 %collective-permute-start.10 = (bf16[48,256]{1,0:T(8,128)(2,1)}, bf16[48,256]{1,0:T(8,128)(2,1)S(1)}, u32[]{:S(2)}, u32[]{:S(2)}) collective-permute-start(bf16[48,256]{1,0:T(8,128)(2,1)} %copy-done.18), channel_id=1, source_target_pairs={{0,7},{1,6},{2,5},{3,4},{4,3},{5,2},{6,1},{7,0},{8,15},{9,14},{10,... | collective-permute-start | bytes 73736 | tf_op jit(solution)/shard_map/ppermute | solution.py:521
  137.5 10.4 %collective-permute-done.10.mirrored = bf16[48,256]{1,0:T(8,128)(2,1)S(1)} collective-permute-done((bf16[48,256]{1,0:T(8,128)(2,1)}, bf16[48,256]{1,0:T(8,128)(2,1)S(1)}, u32[]{:S(2)}, u32[]{:S(2)}) %collective-permute-start.10) | collective-permute-done | bytes 24608 | tf_op jit(solution)/shard_map/ppermute | solution.py:521
  147.8 4.2 %all-to-all-done.3.parts = bf16[16,144,256]{2,1,0:T(8,128)(2,1)S(1)} async-done(((bf16[16,144,256]{2,1,0:T(8,128)(2,1)}), bf16[16,144,256]{2,1,0:T(8,128)(2,1)S(1)}, u32[]{:S(2)}, u32[]{:S(2)}) %all-to-all-start.3) | async-done | bytes 1179680 | tf_op jit(solution)/shard_map/all_to_all | solution.py:525
  153.5 26.6 %all_to_all.30.got.parts = bf16[8,240,256]{2,1,0:T(8,128)(2,1)S(1)} all-to-all(bf16[8,240,256]{2,1,0:T(8,128)(2,1)S(1)} %shard_map.95), channel_id=1, replica_groups={{0,56,64,120,128,184,192,248},{1,57,65,121,129,185,193,249},{2,58,66,12..., dimensions={0} | all-to-all | bytes 1966080 | tf_op jit(solution)/shard_map/all_to_all | solution.py:527
  180.7 20.1 %all_to_all.31.mine = bf16[16,144,256]{2,1,0:T(8,128)(2,1)S(1)} all-to-all(bf16[16,144,256]{2,1,0:T(8,128)(2,1)S(1)} %shard_map.97), channel_id=1, replica_groups={{0,8,16,24,2,10,18,26,4,12,20,28,6,14,22,30},{1,9,17,25,3,11,19,27,5,13..., dimensions={0} | all-to-all | bytes 2359296 | tf_op jit(solution)/shard_map/all_to_all | solution.py:538
  200.8 5.0 %collective-permute-start.11 = (bf16[16,144,256]{2,1,0:T(8,128)(2,1)S(1)}, bf16[16,144,256]{2,1,0:T(8,128)(2,1)S(1)}, u32[]{:S(2)}, u32[]{:S(2)}) collective-permute-start(bf16[16,144,256]{2,1,0:T(8,128)(2,1)S(1)} %all_to_all.31.mine), channel_id=1, source_target_pairs={{0,1},{1,0},{2,3},{3,2},{4,5},{5,4},{6,7},{7,6},{8,9},{9,8},{10,11... | collective-permute-start | bytes 3538952 | tf_op jit(solution)/shard_map/ppermute | solution.py:539
  205.8 1.4 shard_map.96
  207.2 1.1 collective-permute-done.11.other
  208.3 3.1 %shard_map.98 = (f32[9,256,256]{2,1,0:T(8,128)}, f32[9,256,256]{2,1,0:T(8,128)}) custom-call(s32[3]{0:T(128)S(1)} %pad_add_fusion.3.pos.refs_0_, bf16[16,144,256]{2,1,0:T(8,128)(2,1)S(1)} %all_to_all.31.mine, bf16[16,144,256]{2,1,0:T(8,128)(2,1)S(1)} %collective-permute-done.11.other), custom_call_target="tpu_custom_call" | custom-call | tf_op jit(solution)/shard_map/pallas_call | solution.py:540
  (115 shorter events, 13.2 us)
Async XLA Ops:
  0.6 10.5 %collective-permute-start.1 = (bf16[192,256]{1,0:T(8,128)(2,1)}, bf16[192,256]{1,0:T(8,128)(2,1)S(1)}, u32[]{:S(2)}, u32[]{:S(2)}) collective-permute-start(bf16[192,256]{1,0:T(8,128)(2,1)} %bitcast.35), channel_id=1, source_target_pairs={{1,2},{3,4},{5,6},{9,10},{11,12},{13,14},{17,18},{19,20},{21,22},{... | collective-permute-start | bytes 294920 | tf_op jit(solution)/shard_map/ppermute | solution.py:365
  5.2 5.8 %collective-permute-start = (bf16[192,256]{1,0:T(8,128)(2,1)}, bf16[192,256]{1,0:T(8,128)(2,1)S(1)}, u32[]{:S(2)}, u32[]{:S(2)}) collective-permute-start(bf16[192,256]{1,0:T(8,128)(2,1)} %bitcast.36), channel_id=1, source_target_pairs={{0,1},{1,0},{2,3},{3,2},{4,5},{5,4},{6,7},{7,6},{8,9},{9,8},{10,11... | collective-permute-start | bytes 294920 | tf_op jit(solution)/shard_map/ppermute | solution.py:364
  11.1 0.9 copy-start.17
  12.7 3.0 %collective-permute-start.2 = (bf16[96,256]{1,0:T(8,128)(2,1)S(1)}, bf16[96,256]{1,0:T(8,128)(2,1)S(1)}, u32[]{:S(2)}, u32[]{:S(2)}) collective-permute-start(bf16[96,256]{1,0:T(8,128)(2,1)S(1)} %get-tuple-element.32), channel_id=1, source_target_pairs={{0,8},{1,9},{2,10},{3,11},{4,12},{5,13},{6,14},{7,15},{16,24},{17,... | collective-permute-start | bytes 147464 | tf_op jit(solution)/shard_map/ppermute | solution.py:375
  14.0 1.7 collective-permute-start.3
  17.2 34.3 %all-to-all-start = ((bf16[16,80,256]{2,1,0:T(8,128)(2,1)}), bf16[16,80,256]{2,1,0:T(8,128)(2,1)S(1)}, u32[]{:S(2)}, u32[]{:S(2)}) async-start(bf16[16,80,256]{2,1,0:T(8,128)(2,1)} %get-tuple-element.35), calls=%async_computation | async-start | bytes 1310720 | tf_op jit(solution)/shard_map/all_to_all | solution.py:379
  33.1 18.3 %copy-start.1 = (bf16[3,3,256,256]{3,2,1,0:T(8,128)(2,1)S(1)}, bf16[3,3,256,256]{3,2,1,0:T(8,128)(2,1)}, u32[]{:S(2)}) copy-start(bf16[3,3,256,256]{3,2,1,0:T(8,128)(2,1)} %kernel.7) | copy-start | bytes 3538948
  54.2 0.8 copy-start.3
  55.0 0.7 copy-start.6
  55.7 25.2 %all-to-all-start.1 = ((bf16[16,64,256]{2,1,0:T(8,128)(2,1)}), bf16[16,64,256]{2,1,0:T(8,128)(2,1)S(1)}, u32[]{:S(2)}, u32[]{:S(2)}) async-start(bf16[16,64,256]{2,1,0:T(8,128)(2,1)} %get-tuple-element.37), calls=%async_computation.1 | async-start | bytes 1048576 | tf_op jit(solution)/shard_map/all_to_all | solution.py:379
  64.6 16.2 %copy-start = (bf16[3,3,256,256]{3,2,1,0:T(8,128)(2,1)S(1)}, bf16[3,3,256,256]{3,2,1,0:T(8,128)(2,1)}, u32[]{:S(2)}) copy-start(bf16[3,3,256,256]{3,2,1,0:T(8,128)(2,1)} %kernel.6) | copy-start | bytes 3538948
  64.6 16.2 %copy-start.14 = (bf16[3,1,8,8,256]{4,3,2,1,0:T(8,128)(2,1)S(1)}, bf16[3,1,8,8,256]{4,3,2,1,0:T(8,128)(2,1)}, u32[]{:S(2)}) copy-start(bf16[3,1,8,8,256]{4,3,2,1,0:T(8,128)(2,1)} %param.7) | copy-start | bytes 294916
  82.5 0.7 copy-start.8
  83.2 0.7 copy-start.12
  83.9 5.9 %collective-permute-start.5 = (bf16[192,256]{1,0:T(8,128)(2,1)S(1)}, bf16[192,256]{1,0:T(8,128)(2,1)S(1)}, u32[]{:S(2)}, u32[]{:S(2)}) collective-permute-start(bf16[192,256]{1,0:T(8,128)(2,1)S(1)} %get-tuple-element.38.own), channel_id=1, source_target_pairs={{1,2},{3,4},{5,6},{9,10},{11,12},{13,14},{17,18},{19,20},{21,22},{... | collective-permute-start | bytes 294920 | tf_op jit(solution)/shard_map/ppermute | solution.py:365
  85.8 4.0 %collective-permute-start.4 = (bf16[192,256]{1,0:T(8,128)(2,1)S(1)}, bf16[192,256]{1,0:T(8,128)(2,1)S(1)}, u32[]{:S(2)}, u32[]{:S(2)}) collective-permute-start(bf16[192,256]{1,0:T(8,128)(2,1)S(1)} %get-tuple-element.38.own), channel_id=1, source_target_pairs={{0,1},{1,0},{2,3},{3,2},{4,5},{5,4},{6,7},{7,6},{8,9},{9,8},{10,11... | collective-permute-start | bytes 294920 | tf_op jit(solution)/shard_map/ppermute | solution.py:364
  90.5 3.0 %collective-permute-start.6 = (bf16[96,256]{1,0:T(8,128)(2,1)S(1)}, bf16[96,256]{1,0:T(8,128)(2,1)S(1)}, u32[]{:S(2)}, u32[]{:S(2)}) collective-permute-start(bf16[96,256]{1,0:T(8,128)(2,1)S(1)} %get-tuple-element.40), channel_id=1, source_target_pairs={{0,8},{1,9},{2,10},{3,11},{4,12},{5,13},{6,14},{7,15},{16,24},{17,... | collective-permute-start | bytes 147464 | tf_op jit(solution)/shard_map/ppermute | solution.py:375
  91.0 2.6 %collective-permute-start.7 = (bf16[96,256]{1,0:T(8,128)(2,1)S(1)}, bf16[96,256]{1,0:T(8,128)(2,1)S(1)}, u32[]{:S(2)}, u32[]{:S(2)}) collective-permute-start(bf16[96,256]{1,0:T(8,128)(2,1)S(1)} %get-tuple-element.41), channel_id=1, source_target_pairs={{8,16},{9,17},{10,18},{11,19},{12,20},{13,21},{14,22},{15,23},{24,... | collective-permute-start | bytes 147464 | tf_op jit(solution)/shard_map/ppermute | solution.py:375
  95.7 0.7 copy-start.10
  96.4 23.2 %all-to-all-start.2 = ((bf16[16,64,256]{2,1,0:T(8,128)(2,1)}), bf16[16,64,256]{2,1,0:T(8,128)(2,1)S(1)}, u32[]{:S(2)}, u32[]{:S(2)}) async-start(bf16[16,64,256]{2,1,0:T(8,128)(2,1)} %get-tuple-element.43), calls=%async_computation.2 | async-start | bytes 1048576 | tf_op jit(solution)/shard_map/all_to_all | solution.py:379
  105.7 3.7 %copy-start.9 = (bf16[480,256]{1,0:T(8,128)(2,1)S(1)}, bf16[480,256]{1,0:T(8,128)(2,1)}, u32[]{:S(2)}) copy-start(bf16[480,256]{1,0:T(8,128)(2,1)} %copy-done.8) | copy-start | bytes 737284
  105.7 3.7 %copy-start.13 = (bf16[384,256]{1,0:T(8,128)(2,1)S(1)}, bf16[384,256]{1,0:T(8,128)(2,1)}, u32[]{:S(2)}) copy-start(bf16[384,256]{1,0:T(8,128)(2,1)} %copy-done.12) | copy-start | bytes 589828
  111.7 14.4 %collective-permute-start.9 = (bf16[16,72,256]{2,1,0:T(8,128)(2,1)}, bf16[16,72,256]{2,1,0:T(8,128)(2,1)S(1)}, u32[]{:S(2)}, u32[]{:S(2)}) collective-permute-start(bf16[16,72,256]{2,1,0:T(8,128)(2,1)} %get-tuple-element.54), channel_id=1, source_target_pairs={{0,1},{1,0},{2,3},{3,2},{4,5},{5,4},{6,7},{7,6},{8,9},{9,8},{10,11... | collective-permute-start | bytes 1769480 | tf_op jit(solution)/shard_map/ppermute | solution.py:508
  119.6 0.9 copy-start.2
  120.5 1.0 copy-start.4
  121.5 0.9 copy-start.11
  122.5 2.0 copy-start.7
  124.4 3.6 %copy-start.15 = (bf16[192,256]{1,0:T(8,128)(2,1)}, bf16[192,256]{1,0:T(8,128)(2,1)S(1)}, u32[]{:S(2)}) copy-start(bf16[192,256]{1,0:T(8,128)(2,1)S(1)} %get-tuple-element.46.own) | copy-start | bytes 294916
  124.5 5.3 %copy-start.18 = (bf16[48,256]{1,0:T(8,128)(2,1)}, bf16[48,256]{1,0:T(8,128)(2,1)S(1)}, u32[]{:S(2)}) copy-start(bf16[48,256]{1,0:T(8,128)(2,1)S(1)} %get-tuple-element.55.mine) | copy-start | bytes 73732
  125.9 2.1 collective-permute-start.8
  129.8 22.3 %all-to-all-start.3 = ((bf16[16,144,256]{2,1,0:T(8,128)(2,1)}), bf16[16,144,256]{2,1,0:T(8,128)(2,1)S(1)}, u32[]{:S(2)}, u32[]{:S(2)}) async-start(bf16[16,144,256]{2,1,0:T(8,128)(2,1)} %shard_map.94), calls=%async_computation.3 | async-start | bytes 2359296 | tf_op jit(solution)/shard_map/all_to_all | solution.py:525
  134.1 13.8 %collective-permute-start.10 = (bf16[48,256]{1,0:T(8,128)(2,1)}, bf16[48,256]{1,0:T(8,128)(2,1)S(1)}, u32[]{:S(2)}, u32[]{:S(2)}) collective-permute-start(bf16[48,256]{1,0:T(8,128)(2,1)} %copy-done.18), channel_id=1, source_target_pairs={{0,7},{1,6},{2,5},{3,4},{4,3},{5,2},{6,1},{7,0},{8,15},{9,14},{10,... | collective-permute-start | bytes 73736 | tf_op jit(solution)/shard_map/ppermute | solution.py:521
  152.1 0.7 copy-start.19
  180.1 25.7 %copy-start.5 = (bf16[48,768]{1,0:T(8,128)(2,1)S(1)}, bf16[48,768]{1,0:T(8,128)(2,1)}, u32[]{:S(2)}) copy-start(bf16[48,768]{1,0:T(8,128)(2,1)} %mul.105.pick) | copy-start | bytes 221188
  180.1 25.7 %copy-start.16 = (bf16[192,256]{1,0:T(8,128)(2,1)S(1)}, bf16[192,256]{1,0:T(8,128)(2,1)}, u32[]{:S(2)}) copy-start(bf16[192,256]{1,0:T(8,128)(2,1)} %copy-done.15) | copy-start | bytes 294916
  200.8 7.4 %collective-permute-start.11 = (bf16[16,144,256]{2,1,0:T(8,128)(2,1)S(1)}, bf16[16,144,256]{2,1,0:T(8,128)(2,1)S(1)}, u32[]{:S(2)}, u32[]{:S(2)}) collective-permute-start(bf16[16,144,256]{2,1,0:T(8,128)(2,1)S(1)} %all_to_all.31.mine), channel_id=1, source_target_pairs={{0,1},{1,0},{2,3},{3,2},{4,5},{5,4},{6,7},{7,6},{8,9},{9,8},{10,11... | collective-permute-start | bytes 3538952 | tf_op jit(solution)/shard_map/ppermute | solution.py:539

commit v7 on v6

--- a/solution.py
+++ b/solution.py
@@ -26,6 +26,7 @@
 ODD_COLS = swap_pairs([(r * 8 + c, r * 8 + c + 1) for r in range(8) for c in (1, 3, 5)])
 EVEN_ROWS = swap_pairs([(r * 8 + c, r * 8 + 8 + c) for r in (0, 2, 4, 6) for c in range(8)])
 ODD_ROWS = swap_pairs([(r * 8 + c, r * 8 + 8 + c) for r in (1, 3, 5) for c in range(8)])
+NEAR_ROWS = swap_pairs([(r * 8 + c, r * 8 + 8 + c) for r in (1, 5) for c in range(8)])
 
 
 def seam_groups():
@@ -139,7 +140,26 @@
                     cells[to : to + 1, :] = strips[(2 * f + 1) * length + i : (2 * f + 1) * length + i + 1, :]
 
 
-def widen_kernel(pos, own, swapped, odd, wide, first, second, cells):
+def post_ends(row, col, cells, first, second, ends):
+    even = row % 2 == 0
+    ends[...] = jnp.zeros_like(ends)
+    for f in range(3):
+        for i in range(2):
+            for base, line in ((0, i), (16, 6 + i)):
+                at = f * 64 + line * 8
+                left, right = cells[at : at + 1, :], cells[at + 7 : at + 8, :]
+                ends[base + 2 * f + i : base + 2 * f + i + 1, :] = jnp.where(col >= 4, right, left)
+    up, down = ends[0:16, :], ends[16:32, :]
+    first[...] = jnp.where(even, down, up).astype(BF16)
+    second[...] = jnp.where(even, up, down).astype(BF16)
+
+
+def ends_kernel(pos, own, first, second, cells, ends):
+    cells[...] = own[...].astype(F32)
+    post_ends(pos[0], pos[1], cells, first, second, ends)
+
+
+def widen(pos, own, swapped, odd, end_one, end_two, wide, first, second, cells, ends, strips, length):
     row, col = pos[0], pos[1]
     even = col % 2 == 0
     cells[...] = jnp.zeros_like(cells)
@@ -151,11 +171,54 @@
     cells[:, 10:12, :] = right[:, 0:2, :]
     wide[...] = cells[...].reshape(24 * PITCH, C).astype(BF16)
     even = row % 2 == 0
+    one, two = end_one[...].astype(F32), end_two[...].astype(F32)
+    ends[0:16, :] = jnp.where(even, two, one)
+    ends[16:32, :] = jnp.where(even, one, two)
     for f in range(3):
         up = cells[8 * f : 8 * f + 2].reshape(2 * PITCH, C)
         down = cells[8 * f + 6 : 8 * f + 8].reshape(2 * PITCH, C)
         first[2 * f * PITCH : (2 * f + 2) * PITCH, :] = jnp.where(even, down, up).astype(BF16)
         second[2 * f * PITCH : (2 * f + 2) * PITCH, :] = jnp.where(even, up, down).astype(BF16)
+        at = 2 * f * length
+        strips[at : at + 12, :] = jnp.where(row >= 4, cells[8 * f + 7, 0:12, :], cells[8 * f, 0:12, :])
+        at = (2 * f + 1) * length
+        strips[at : at + 2, :] = ends[2 * f : 2 * f + 2, :]
+        for i in range(8):
+            rim = jnp.where(col >= 4, cells[8 * f + i, 9:10, :], cells[8 * f + i, 2:3, :])
+            strips[at + 2 + i : at + 3 + i, :] = rim
+        strips[at + 10 : at + 12, :] = ends[16 + 2 * f : 18 + 2 * f, :]
+
+
+def input_kernel(pos, own, swapped, odd, end_one, end_two, wide, first, second, send, cells, ends, strips):
+    strips[...] = jnp.zeros_like(strips)
+    widen(pos, own, swapped, odd, end_one, end_two, wide, first, second, cells, ends, strips, 12)
+    post_strips(strips, send)
+
+
+def rim_kernel(pos, own, swapped, odd, end_one, end_two, kernel, wide, first, second, send, cells, ends, lines, strips):
+    row, col = pos[0], pos[1]
+    lines[...] = jnp.zeros_like(lines)
+    widen(pos, own, swapped, odd, end_one, end_two, wide, first, second, cells, ends, lines, PITCH)
+    bottom, right = 2 * (row // 4), 2 * (col // 4)
+    totals = []
+    for kind in range(2):
+        total = None
+        for k in range(3):
+            at = [(2 * f + kind) * PITCH + k for f in range(3)]
+            left = jnp.concatenate([lines[i : i + PITCH, :] for i in at], axis=0).astype(BF16)
+            tap = kernel[bottom, 2 - k] if kind == 0 else kernel[2 - k, right]
+            part = dot(left, tap, ((1,), (1,)))
+            total = part if total is None else total + part
+        totals.append(total)
+    strips[...] = jnp.zeros_like(strips)
+    at = lax.broadcasted_iota(jnp.int32, (PITCH, C), 0)
+    for f in range(3):
+        for kind, where in ((0, col), (1, row)):
+            low, high = jnp.where(where > 0, 0, 1), jnp.where(where < 7, 9, 8)
+            value = jnp.where((at >= low) & (at <= high), totals[kind][f * PITCH : (f + 1) * PITCH], 0.0)
+            begin = (2 * f + kind) * 10
+            strips[begin : begin + 10, :] = value[0:10]
+    post_strips(strips, send)
 
 
 def stack_lines(row, wide, first, second, cells):
@@ -171,20 +234,10 @@
     cells[36 * PITCH :, :] = jnp.zeros((8, C), F32)
 
 
-def input_kernel(pos, wide, first, second, near, send, cells, strips):
-    row, col = pos[0], pos[1]
-    stack_lines(row, wide, first, second, cells)
-    near[...] = cells[0 : 36 * PITCH, :].astype(BF16)
-    strips[...] = jnp.zeros_like(strips)
-    take_strips(cells, strips, row, col, 12, 2, 9, 0, 12)
-    post_strips(strips, send)
-
-
-def one_kernel(pos, near, got, pick, kernel, filled, pre, hidden, send, cells, shifts, strips, lines):
+def one_kernel(pos, wide, first, second, got, pick, kernel, filled, pre, hidden, send, cells, shifts, strips, lines):
     row, col = pos[0], pos[1]
     lines[...] = dot(pick[...], got[...], ((1,), (0,)))
-    cells[0 : 36 * PITCH, :] = near[...].astype(F32)
-    cells[36 * PITCH :, :] = jnp.zeros((8, C), F32)
+    stack_lines(row, wide, first, second, cells)
     fill_strips(cells, lines, row, col, 12, 1, 10, 12)
     filled[...] = cells[0 : 36 * PITCH, :].astype(BF16)
     total = convolve(cells, shifts, 12, 10, 0, kernel, False)
@@ -199,7 +252,9 @@
     post_strips(strips, send)
 
 
-def two_kernel(pos, hidden, got, pick, kernel, cotangent, filled, delta, wide_delta, cells, shifts, lines):
+def two_kernel(
+    pos, hidden, got, pick, kernel, cotangent, filled, delta, wide_delta, first, second, cells, shifts, lines, ends
+):
     row, col = pos[0], pos[1]
     lines[...] = dot(pick[...], got[...], ((1,), (0,)))
     cells[0 : 30 * PITCH, :] = hidden[...].astype(F32)
@@ -211,23 +266,13 @@
     delta[...] = product.reshape(192, C).astype(BF16)
     padded = jnp.concatenate([product, jnp.zeros((24, 8, C), F32)], axis=1)
     wide_delta[...] = padded.reshape(24 * PITCH, C).astype(BF16)
-
-
-def back_kernel(pos, wide, first, second, kernel, back, send, cells, shifts, strips):
-    row, col = pos[0], pos[1]
-    stack_lines(row, wide, first, second, cells)
-    total = convolve(cells, shifts, 12, 10, 0, kernel, True)
-    back[...] = total.astype(BF16)
-    cells[0 : 30 * PITCH, :] = total
-    strips[...] = jnp.zeros_like(strips)
-    take_strips(cells, strips, row, col, 10, 0, 9, 0, 10)
-    at = lax.broadcasted_iota(jnp.int32, (10, C), 0)
-    for f in range(3):
-        for kind, where in ((0, col), (1, row)):
-            low, high = jnp.where(where > 0, 0, 1), jnp.where(where < 7, 9, 8)
-            lines = slice((2 * f + kind) * 10, (2 * f + kind + 1) * 10)
-            strips[lines, :] = jnp.where((at >= low) & (at <= high), strips[lines, :], 0.0)
-    post_strips(strips, send)
+    cells[0:192, :] = product.reshape(192, C)
+    post_ends(row, col, cells, first, second, ends)
+
+
+def back_kernel(pos, wide, first, second, kernel, back, cells, shifts):
+    stack_lines(pos[0], wide, first, second, cells)
+    back[...] = convolve(cells, shifts, 12, 10, 0, kernel, True).astype(BF16)
 
 
 def delta_kernel(pos, back, got, pick, pre, kernel, wide_delta, own, send, cells, grads, shifts, strips, lines):
@@ -275,10 +320,16 @@
     own[...] = cells[0:192, :].astype(BF16)
 
 
-def final_kernel(pos, own, got, pick, out, cells, lines):
+def share_kernel(pos, got, pick, own, mirrored):
+    strips = jnp.concatenate([got[i, 144:192, :] for i in range(8)], axis=0)
+    total = dot(pick[...], strips, ((1,), (0,)))
+    own[...] = total[0:48]
+    mirrored[...] = total[48:96].astype(BF16)
+
+
+def final_kernel(pos, own, one, two, out, cells, lines):
     row, col = pos[0], pos[1]
-    strips = jnp.concatenate([got[i, 144:240, :] for i in range(8)], axis=0)
-    lines[...] = dot(pick[...], strips, ((1,), (0,)))
+    lines[...] = one[...] + two[...].astype(F32)
     cells[...] = own[...].astype(F32)
     for f in range(3):
         base = f * 64
@@ -326,11 +377,11 @@
         out[i] = jnp.concatenate([one, two], axis=0).astype(BF16)
 
 
-def across_kernel(pos, parts, mine, mirrored, out):
+def across_kernel(pos, parts, strips, out):
     total = parts[0].astype(F32)
     for i in range(1, 16):
         total = total + parts[i].astype(F32)
-    total = jnp.concatenate([total.astype(BF16), mine[...], mirrored[...]], axis=0)
+    total = jnp.concatenate([total.astype(BF16), strips[...]], axis=0)
     for i in range(8):
         out[i] = total
 
@@ -360,36 +411,27 @@
         copy.wait()
 
 
-def tall_region(field, pos):
-    swapped = lax.ppermute(field, "core", CORES)
-    odd = lax.ppermute(field, TILE, ODD_COLS)
-    wide, first, second = run(
-        widen_kernel,
-        [((24 * PITCH, C), BF16), ((6 * PITCH, C), BF16), ((6 * PITCH, C), BF16)],
-        [((24, PITCH, C), F32)],
-        pos,
-        field,
-        swapped,
-        odd,
-    )
-    return wide, lax.ppermute(first, TILE, EVEN_ROWS), lax.ppermute(second, TILE, ODD_ROWS)
-
-
 def seam_exchange(send):
     got = lax.all_to_all(send, AXES, 0, 0, axis_index_groups=SEAM_GROUPS)
     return got.reshape(-1, C)
 
 
 def seam_picks(neighbour, seam_codes, row, col, face_group):
-    in_group = seam_select(neighbour, seam_codes, row, col, face_group, 0)
-    gather, add, turned = in_group
-    wide_pick, pick = expand(gather, turned, 12, 80), expand(gather, turned, 10, 64)
-    add_10 = expand(add, turned, 10, 64)
-    _, add, turned = seam_select(neighbour, seam_codes, row, col, face_group, col // 4)
-    return wide_pick, pick, add_10, expand(add, turned, 8, 48)
-
-
-def seam_select(neighbour, seam_codes, row, col, face_group, order):
+    tables = (neighbour, seam_codes, face_group, row)
+    gather, add, turned = seam_select(*tables, col, jnp.arange(4, dtype=jnp.int32))
+    centre = (row == 3) | (row == 4)
+    pick_12, pick_10 = expand(gather, turned, 12, 80, centre), expand(gather, turned, 10, 64)
+    add_10 = expand(add, turned, 10, 64, centre)
+    same_side = 2 * jnp.arange(2, dtype=jnp.int32) + col // 4
+    shares = []
+    for to in (col, 7 - col):
+        _, add, turned = seam_select(*tables, to, same_side)
+        shares.append(expand(add, turned, 8, 48))
+    return pick_12, pick_10, add_10, jnp.concatenate(shares, axis=0)
+
+
+def seam_select(neighbour, seam_codes, face_group, row, col, slot_mirror):
+    slots = slot_mirror.shape[0]
     mirror = col // 4 + 2 * (row // 4)
     on_edge = jnp.stack([(row == 0) | (row == 7), (col == 0) | (col == 7)])
     bottom, right = row // 4, col // 4
@@ -398,7 +440,6 @@
     opposite, reverse = 1 - seam_codes % 2, seam_codes // 2
     types = jnp.arange(4) // 2
     rel_of = jnp.where(types == 0, 2 * opposite + reverse, 2 * reverse + opposite)
-    slot_mirror = jnp.arange(4, dtype=jnp.int32) ^ order
     slot_type = jnp.arange(2, dtype=jnp.int32)
 
     def on_side(table, side):
@@ -422,20 +463,32 @@
     own_faces = (first + jnp.arange(3, dtype=jnp.int32))[:, None, None, None, None, None]
     add = (slot_next == own_faces) & (slot_rel == rel[:, None, None]) & same_type
     turned = jnp.stack([rel % 2, rel // 2], axis=1) == 1
-
     return gather, add, turned
 
 
-def expand(select, turned, length, block):
-    select = select.reshape(6, 16, 6).astype(BF16)
-    flip = jnp.broadcast_to(turned[None, :, None, :], (4, 4, 3, 2)).reshape(16, 6)
+def expand(select, turned, length, block, centre=None):
+    slots = turned.shape[0]
     at = jnp.arange(length, dtype=jnp.int32)
-    here = jnp.where(flip[None, :, :, None], at[:, None, None, None] + at == length - 1, at[:, None, None, None] == at)
-    full = select[:, None, :, :, None] * here[None].astype(BF16)
-    full = full.reshape(6 * length, 16, 6 * length)
+    source = jnp.where(turned[:, :, None], length - 1 - at, at)
+    here = source[..., None] == at
+
+    def over_cells(select, here):
+        select = select.reshape(6, 1, 4, slots, 3, 2, 1).astype(BF16)
+        here = here.transpose(2, 0, 1, 3).reshape(1, length, 1, slots, 1, 2, length).astype(BF16)
+        return select * here
+
+    full = over_cells(select, here)
+    if centre is not None:
+        source = jnp.roll(source, 2, axis=0)
+        upper = (jnp.arange(4) < 2)[:, None, None]
+        moved = jnp.where(upper, source + 8, source - 8)
+        across = jnp.where(upper, source <= 1, source >= length - 2)
+        across = across & centre & (jnp.arange(2) == 1)[None, :, None]
+        full = full + over_cells(jnp.roll(select, 2, axis=3), (moved[..., None] == at) & across[..., None])
+    full = full.reshape(6 * length, 4 * slots, 6 * length)
     rows = -(-6 * length // 16) * 16
     full = jnp.pad(full, ((0, rows - 6 * length), (0, 0), (0, block - 6 * length)))
-    return full.reshape(rows, 16 * block)
+    return full.reshape(rows, 4 * slots * block)
 
 
 def body(inputs, cotangent, kernel_one, kernel_two, neighbour, seam_codes):
@@ -444,34 +497,48 @@
     row = lax.axis_index("zh") * 4 + lax.axis_index("x")
     col = lax.axis_index("y") * 2 + core
     pos = jnp.stack([row, col, core]).astype(jnp.int32)
-    pick_12, pick_10, add_10, add_8 = seam_picks(neighbour, seam_codes, row, col, face_group)
     flat = 36 * PITCH
     spare = flat + 8
-
-    wide, first, second = tall_region(inputs.reshape(192, C), pos)
-    near, send = run(
+    ends = [((16, C), BF16), ((16, C), BF16)]
+    regions = [((24 * PITCH, C), BF16), ((6 * PITCH, C), BF16), ((6 * PITCH, C), BF16)]
+
+    def beside(field, first, second):
+        return (
+            field,
+            lax.ppermute(field, "core", CORES),
+            lax.ppermute(field, TILE, ODD_COLS),
+            lax.ppermute(first, TILE, EVEN_ROWS),
+            lax.ppermute(second, TILE, NEAR_ROWS),
+        )
+
+    x = inputs.reshape(192, C)
+    first, second = run(ends_kernel, ends, [((192, C), F32), ((32, C), F32)], pos, x)
+    wide, first, second, send = run(
         input_kernel,
-        [((flat, C), BF16), ((16, 80, C), BF16)],
-        [((spare, C), F32), ((80, C), F32)],
+        regions + [((16, 80, C), BF16)],
+        [((24, PITCH, C), F32), ((32, C), F32), ((80, C), F32)],
         pos,
-        wide,
-        first,
-        second,
+        *beside(x, first, second),
     )
+    send, neighbour, seam_codes = lax.optimization_barrier((send, neighbour, seam_codes))
+    pick_12, pick_10, add_10, add_8 = seam_picks(neighbour, seam_codes, row, col, face_group)
+    first, second = lax.ppermute(first, TILE, EVEN_ROWS), lax.ppermute(second, TILE, ODD_ROWS)
     filled_in, pre_one, hidden, send = run(
         one_kernel,
         [((flat, C), BF16), ((30 * PITCH, C), F32), ((30 * PITCH, C), BF16), ((16, 64, C), BF16)],
         [((spare, C), F32), ((flat, C), BF16), ((64, C), F32), ((80, C), F32)],
         pos,
-        near,
+        wide,
+        first,
+        second,
         seam_exchange(send),
         pick_12,
         kernel_one,
     )
-    filled_hidden, delta, wide_two = run(
+    filled_hidden, delta, wide_two, first, second = run(
         two_kernel,
-        [((30 * PITCH, C), BF16), ((192, C), BF16), ((24 * PITCH, C), BF16)],
-        [((30 * PITCH + 8, C), F32), ((30 * PITCH, C), BF16), ((64, C), F32)],
+        [((30 * PITCH, C), BF16), ((192, C), BF16), ((24 * PITCH, C), BF16)] + ends,
+        [((30 * PITCH + 8, C), F32), ((30 * PITCH, C), BF16), ((64, C), F32), ((32, C), F32)],
         pos,
         hidden,
         seam_exchange(send),
@@ -479,18 +546,26 @@
         kernel_two,
         cotangent.reshape(192, C),
     )
-    wide, first, second = tall_region(delta, pos)
-    back, send = run(
+    wide, first, second, send = run(
+        rim_kernel,
+        regions + [((16, 64, C), BF16)],
+        [((24, PITCH, C), F32), ((32, C), F32), ((6 * PITCH + 8, C), F32), ((64, C), F32)],
+        pos,
+        *beside(delta, first, second),
+        kernel_two,
+    )
+    got = seam_exchange(send)
+    first, second = lax.ppermute(first, TILE, EVEN_ROWS), lax.ppermute(second, TILE, ODD_ROWS)
+    back = run(
         back_kernel,
-        [((30 * PITCH, C), BF16), ((16, 64, C), BF16)],
-        [((spare, C), F32), ((flat, C), BF16), ((64, C), F32)],
+        [((30 * PITCH, C), BF16)],
+        [((spare, C), F32), ((flat, C), BF16)],
         pos,
         wide,
         first,
         second,
         kernel_two,
-    )
-    got = seam_exchange(send)
+    )[0]
     pieces = [((16, 72, C), F32), ((16, 72, C), BF16)]
 
     def grad_of(height, line0, col0, source, delta):
@@ -518,22 +593,23 @@
         pre_one,
         kernel_one,
     )
-    mirrored = lax.ppermute(strips, TILE, [(t, t ^ 7) for t in range(64)])
     keep_one, payload_one = grad_of(12, 1, 1, filled_in, wide_one)
     got_one = lax.ppermute(payload_one, "core", CORES)
     part = run(pair_kernel, [((16, 144, C), BF16)], [], pos, keep_one, got_one, keep_two, got_two)[0]
     part = lax.all_to_all(part, AXES, 0, 0, axis_index_groups=PLANE_GROUPS)
-    part = run(across_kernel, [((8, 240, C), BF16)], [], pos, part, strips, mirrored)[0]
+    part = run(across_kernel, [((8, 192, C), BF16)], [], pos, part, strips)[0]
     got = lax.all_to_all(part, AXES, 0, 0, axis_index_groups=ACROSS_GROUPS)
     part = run(gather_kernel, [((16, 144, C), BF16)], [], pos, got)[0]
+    share, mirrored = run(share_kernel, [((48, C), F32), ((48, C), BF16)], [], pos, got, add_8)
+    mirrored = lax.ppermute(mirrored, TILE, [(t, t ^ 7) for t in range(64)])
     input_grad = run(
         final_kernel,
         [((192, C), BF16)],
         [((192, C), F32), ((48, C), F32)],
         pos,
         own,
-        got,
-        add_8,
+        share,
+        mirrored,
     )[0]
     part = lax.all_to_all(part, AXES, 0, 0, axis_index_groups=PLANE_GROUPS)
     got = lax.ppermute(part, "core", CORES)

time: 215 us -> 226 us (1.051)
  waiting for transfers between devices: 58.7 us -> 20.2 us
  blocking collectives: 46.6 us -> 70.4 us
  local copies, waits for them, and re-layouts: 25.2 us -> 39.6 us
  other arithmetic: 8.62 us -> 21.8 us
  starting transfers between devices: 48.4 us -> 45.4 us
    all_to_all x1 -> x2, blocking collectives: 20.1 us -> 46.2 us  [body(): part = lax.all_to_all(part, AXES, 0, 0, axis_index_groups=PLANE_GROUPS)]
    all_to_all x3, waiting for transfers between devices: 34.2 us -> 12.9 us  [seam_exchange(): got = lax.all_to_all(send, AXES, 0, 0, axis_index_groups=SEAM_GROUPS)]
    ppermute x9 -> x13, waiting for transfers between devices: 17.2 us -> 5.72 us  [the longest x1 4 us: body(): mirrored = lax.ppermute(mirrored, TILE, [(t, t ^ 7) for t in range(64)])]
    add x0 -> x2, other arithmetic: none -> 9.17 us  [expand(): full + over_cells(jnp.roll(select, 2, axis=3), (moved[..., None] == at) &...]
    add x0 -> x2, local copies, waits for them, and re-layouts: none -> 7.29 us  [expand(): full + over_cells(jnp.roll(select, 2, axis=3), (moved[..., None] == at) &...]
    all_to_all x3, starting transfers between devices: 25.9 us -> 21.1 us  [seam_exchange(): got = lax.all_to_all(send, AXES, 0, 0, axis_index_groups=SEAM_GROUPS)]
    ppermute x9 -> x13, starting transfers between devices: 13.2 us -> 17.9 us  [the longest x2 6.65 us: beside(): lax.ppermute(field, TILE, ODD_COLS)]
    all_to_all x1 -> x0, starting transfers between devices: 4.3 us -> none  [body(): part = lax.all_to_all(part, AXES, 0, 0, axis_index_groups=PLANE_GROUPS)]
  transfers between devices with their start and end apart: 16 -> 19, of which waited for: 10 -> 6; matrix products, arithmetic and copies ran while one was open for 12% -> 22% of each run, Pallas kernels for 3% -> 4%
where the time goes in v7:
time: 226 us; the launch traced here: 222 us
  blocking collectives  70.4 us (31%)
  starting transfers between devices  45.4 us (20%)
  local copies, waits for them, and re-layouts  39.6 us (18%)
  Pallas kernels  23.2 us (10%)
  other arithmetic  21.8 us (10%)
  waiting for transfers between devices  20.2 us (9%)
    all_to_all x2, blocking collectives, body(): part = lax.all_to_all(part, AXES, 0, 0, axis_index_groups=PLANE_GROUPS)  46.2 us
    all_to_all x1, blocking collectives, body(): got = lax.all_to_all(part, AXES, 0, 0, axis_index_groups=ACROSS_GROUPS)  24.2 us
    all_to_all x3, starting transfers between devices, seam_exchange(): got = lax.all_to_all(send, AXES, 0, 0, axis_index_groups=SEAM_GROUPS)  21.1 us
    pallas_call x14, Pallas kernels, run(): pl.pallas_call(kernel, out_shape=[jax.ShapeDtypeStruct(shape, dtype) for...  20.1 us
    all_to_all x3, waiting for transfers between devices, seam_exchange(): got = lax.all_to_all(send, AXES, 0, 0, axis_index_groups=SEAM_GROUPS)  12.9 us
    unnamed x62, local copies, waits for them, and re-layouts  9.46 us
    add x2, other arithmetic, expand(): full + over_cells(jnp.roll(select, 2, axis=3), (moved[..., None] == at) &...  9.17 us
    add x2, local copies, waits for them, and re-layouts, expand(): full + over_cells(jnp.roll(select, 2, axis=3), (moved[..., None] == at) &...  7.29 us
  transfers between devices with their start and end apart: 19, of which 6 were waited for; matrix products, arithmetic and copies ran while one was open for 22% of the time, Pallas kernels for 4%

profile of v7, /device:TPU:1, one launch (start us, length us, event | category | flops | bytes accessed | tf_op | source)
XLA Modules:
  0.0 222.2 jit_solution(14019829835462348135)
XLA Ops:
  0.6 4.6 %collective-permute-start.1 = (bf16[192,256]{1,0:T(8,128)(2,1)}, bf16[192,256]{1,0:T(8,128)(2,1)S(1)}, u32[]{:S(2)}, u32[]{:S(2)}) collective-permute-start(bf16[192,256]{1,0:T(8,128)(2,1)} %bitcast.48), channel_id=1, source_target_pairs={{1,2},{3,4},{5,6},{9,10},{11,12},{13,14},{17,18},{19,20},{21,22},{... | collective-permute-start | bytes 294920 | tf_op jit(solution)/shard_map/ppermute | solution.py:509
  6.9 1.3 collective-permute-start.2
  17.8 1.6 shard_map.86
  22.8 11.4 %all-to-all-start = ((bf16[16,80,256]{2,1,0:T(8,128)(2,1)}), bf16[16,80,256]{2,1,0:T(8,128)(2,1)S(1)}, u32[]{:S(2)}, u32[]{:S(2)}) async-start(bf16[16,80,256]{2,1,0:T(8,128)(2,1)} %get-tuple-element.44), calls=%async_computation | async-start | bytes 1310720 | tf_op jit(solution)/shard_map/all_to_all | solution.py:415
  36.0 1.7 collective-permute-start.4
  39.8 3.9 %multiply_add_fusion = bf16[6,12,4,4,3,2,12]{6,5,4,3,2,1,0:T(2,128)(2,1)} fusion(bf16[12,4,2,12]{3,2,1,0:T(2,128)(2,1)S(1)} %and_convert_fusion, bf16[6,4,4,3,2]{4,3,2,1,0:T(4,128)(2,1)S(1)} %copy.120, bf16[12,4,2,12]{3,2,1,0:T(2,128)(2,1)S(1)} %compare_convert_fusion, bf16[6,4,4,3,2]{4,3,2,1,0:T(4,128)(2,1)S(1)} %copy.117), kind=kLoop, calls=%fused_computation | loop fusion | flops 248832 | bytes 172800 | tf_op jit(solution)/shard_map/add | solution.py:487
  44.1 1.3 copy.140
  45.4 1.3 copy.139
  46.7 3.5 %add.316 = bf16[72,16,72]{2,1,0:T(8,128)(2,1)S(1)} reshape(bf16[6,12,4,4,3,2,12]{6,5,4,3,2,1,0:T(2,128)(2,1)} %multiply_add_fusion) | data formatting | bytes 331776 | tf_op jit(solution)/shard_map/add | solution.py:487
  50.6 7.0 %all-to-all-done = bf16[16,80,256]{2,1,0:T(8,128)(2,1)S(1)} async-done(((bf16[16,80,256]{2,1,0:T(8,128)(2,1)}), bf16[16,80,256]{2,1,0:T(8,128)(2,1)S(1)}, u32[]{:S(2)}, u32[]{:S(2)}) %all-to-all-start) | async-done | bytes 655392 | tf_op jit(solution)/shard_map/all_to_all | solution.py:415
  57.6 2.7 %shard_map.87 = (bf16[576,256]{1,0:T(8,128)(2,1)S(1)}, f32[480,256]{1,0:T(8,128)S(1)}, bf16[480,256]{1,0:T(8,128)(2,1)S(1)}, bf16[16,64,256]{2,1,0:T(8,128)(2,1)}) custom-call(s32[3]{0:T(128)S(1)} %pad_add_fusion.7.pos.refs_0_, bf16[384,256]{1,0:T(8,128)(2,1)S(1)} %get-tuple-element.40.wide, bf16[96,256]{1,0:T(8,128)(2,1)S(1)} %collective-permute-done.4.first, ...), custom_call_target="tpu_custom_call" | custom-call | tf_op jit(solution)/shard_map/pallas_call | solution.py:57
  61.0 3.9 %all-to-all-start.1 = ((bf16[16,64,256]{2,1,0:T(8,128)(2,1)}), bf16[16,64,256]{2,1,0:T(8,128)(2,1)S(1)}, u32[]{:S(2)}, u32[]{:S(2)}) async-start(bf16[16,64,256]{2,1,0:T(8,128)(2,1)} %get-tuple-element.48), calls=%async_computation.1 | async-start | bytes 1048576 | tf_op jit(solution)/shard_map/all_to_all | solution.py:415
  65.0 5.3 %multiply_add_fusion.1 = (bf16[6,10,4,4,3,2,10]{6,5,4,3,2,1,0:T(2,128)(2,1)}, bf16[6,10,4,4,3,2,10]{6,5,4,3,2,1,0:T(2,128)(2,1)}) fusion(bf16[10,4,2,10]{3,2,1,0:T(2,128)(2,1)S(1)} %and_convert_fusion.1, bf16[6,4,4,3,2]{4,3,2,1,0:T(4,128)(2,1)S(1)} %copy-done.19, bf16[6,4,4,3,2]{4,3,2,1,0:T(4,128)(2,1)} %copy.139, ...), kind=kLoop, calls=%fused_computation.1 | loop fusion | flops 230400 | bytes 237056 | tf_op jit(solution)/shard_map/add | solution.py:487
  70.3 3.8 %mul.205 = bf16[60,16,60]{2,1,0:T(8,128)(2,1)} reshape(bf16[6,10,4,4,3,2,10]{6,5,4,3,2,1,0:T(2,128)(2,1)} %get-tuple-element.102) | data formatting | bytes 230400 | tf_op jit(solution)/shard_map/mul | solution.py:478
  74.1 1.7 pad.12
  75.8 1.1 reshape.842.pick
  77.0 1.5 select_reduce_fusion.5
  78.5 5.9 %all-to-all-done.1 = bf16[16,64,256]{2,1,0:T(8,128)(2,1)S(1)} async-done(((bf16[16,64,256]{2,1,0:T(8,128)(2,1)}), bf16[16,64,256]{2,1,0:T(8,128)(2,1)S(1)}, u32[]{:S(2)}, u32[]{:S(2)}) %all-to-all-start.1) | async-done | bytes 524320 | tf_op jit(solution)/shard_map/all_to_all | solution.py:415
  84.4 1.6 shard_map.88
  87.4 2.1 collective-permute-start.7
  91.8 0.9 collective-permute-done.8.end_one
  94.4 1.8 shard_map.89
  96.2 5.8 %all-to-all-start.2 = ((bf16[16,64,256]{2,1,0:T(8,128)(2,1)}), bf16[16,64,256]{2,1,0:T(8,128)(2,1)S(1)}, u32[]{:S(2)}, u32[]{:S(2)}) async-start(bf16[16,64,256]{2,1,0:T(8,128)(2,1)} %get-tuple-element.55), calls=%async_computation.2 | async-start | bytes 1048576 | tf_op jit(solution)/shard_map/all_to_all | solution.py:415
  102.7 1.3 broadcast_multiply_fusion.1
  104.0 1.6 mul.215
  105.7 1.3 broadcast_multiply_fusion.2
  107.0 1.6 mul.211
  108.6 3.6 %collective-permute-start.10 = (bf16[96,256]{1,0:T(8,128)(2,1)}, bf16[96,256]{1,0:T(8,128)(2,1)}, u32[]{:S(2)}, u32[]{:S(2)}) collective-permute-start(bf16[96,256]{1,0:T(8,128)(2,1)} %get-tuple-element.53), channel_id=1, source_target_pairs={{0,8},{1,9},{2,10},{3,11},{4,12},{5,13},{6,14},{7,15},{16,24},{17,... | collective-permute-start | bytes 147464 | tf_op jit(solution)/shard_map/ppermute | solution.py:558
  112.2 1.3 collective-permute-start.11
  113.5 3.7 %add.331 = bf16[60,16,60]{2,1,0:T(8,128)(2,1)} reshape(bf16[6,10,4,4,3,2,10]{6,5,4,3,2,1,0:T(2,128)(2,1)} %get-tuple-element.101) | data formatting | bytes 230400 | tf_op jit(solution)/shard_map/add | solution.py:487
  117.2 1.7 pad.13
  118.9 1.1 reshape.845.pick
  121.0 2.3 %shard_map.93 = (f32[16,72,256]{2,1,0:T(8,128)S(1)}, bf16[16,72,256]{2,1,0:T(8,128)(2,1)}) custom-call(s32[3]{0:T(128)S(1)} %pad_add_fusion.7.pos.refs_0_, bf16[480,256]{1,0:T(8,128)(2,1)S(1)} %copy-done.11, bf16[384,256]{1,0:T(8,128)(2,1)S(1)} %copy-done.13), custom_call_target="tpu_custom_call" | custom-call | tf_op jit(solution)/shard_map/pallas_call | solution.py:57
  123.3 1.0 copy-done.2
  124.4 1.6 shard_map.90.back
  126.1 1.0 copy-done.5
  127.1 1.9 shard_map.91
  129.0 1.0 copy-done.9
  130.0 1.4 shard_map.92
  131.9 1.6 collective-permute-done.12.got_one
  133.6 1.3 shard_map.94
  134.9 29.8 %all_to_all.30.parts = bf16[16,144,256]{2,1,0:T(8,128)(2,1)S(1)} all-to-all(bf16[16,144,256]{2,1,0:T(8,128)(2,1)S(1)} %shard_map.94), channel_id=1, replica_groups={{0,8,16,24,2,10,18,26,4,12,20,28,6,14,22,30},{1,9,17,25,3,11,19,27,5,13..., dimensions={0} | all-to-all | bytes 2359296 | tf_op jit(solution)/shard_map/all_to_all | solution.py:599
  165.4 24.2 %all_to_all.31.got.parts = bf16[8,192,256]{2,1,0:T(8,128)(2,1)S(1)} all-to-all(bf16[8,192,256]{2,1,0:T(8,128)(2,1)S(1)} %shard_map.95), channel_id=1, replica_groups={{0,56,64,120,128,184,192,248},{1,57,65,121,129,185,193,249},{2,58,66,12..., dimensions={0} | all-to-all | bytes 1572864 | tf_op jit(solution)/shard_map/all_to_all | solution.py:601
  190.2 16.5 %all_to_all.32.mine = bf16[16,144,256]{2,1,0:T(8,128)(2,1)S(1)} all-to-all(bf16[16,144,256]{2,1,0:T(8,128)(2,1)S(1)} %shard_map.98), channel_id=1, replica_groups={{0,8,16,24,2,10,18,26,4,12,20,28,6,14,22,30},{1,9,17,25,3,11,19,27,5,13..., dimensions={0} | all-to-all | bytes 2359296 | tf_op jit(solution)/shard_map/all_to_all | solution.py:614
  206.6 5.8 %collective-permute-start.15 = (bf16[16,144,256]{2,1,0:T(8,128)(2,1)S(1)}, bf16[16,144,256]{2,1,0:T(8,128)(2,1)S(1)}, u32[]{:S(2)}, u32[]{:S(2)}) collective-permute-start(bf16[16,144,256]{2,1,0:T(8,128)(2,1)S(1)} %all_to_all.32.mine), channel_id=1, source_target_pairs={{0,1},{1,0},{2,3},{3,2},{4,5},{5,4},{6,7},{7,6},{8,9},{9,8},{10,11... | collective-permute-start | bytes 3538952 | tf_op jit(solution)/shard_map/ppermute | solution.py:615
  213.7 4.0 %collective-permute-done.14.two = bf16[48,256]{1,0:T(8,128)(2,1)S(1)} collective-permute-done((bf16[48,256]{1,0:T(8,128)(2,1)S(1)}, bf16[48,256]{1,0:T(8,128)(2,1)S(1)}, u32[]{:S(2)}, u32[]{:S(2)}) %collective-permute-start.14) | collective-permute-done | bytes 24608 | tf_op jit(solution)/shard_map/ppermute | solution.py:604
  217.7 1.3 shard_map.97
  218.9 3.1 %shard_map.99 = (f32[9,256,256]{2,1,0:T(8,128)}, f32[9,256,256]{2,1,0:T(8,128)}) custom-call(s32[3]{0:T(128)S(1)} %pad_add_fusion.7.pos.refs_0_, bf16[16,144,256]{2,1,0:T(8,128)(2,1)S(1)} %all_to_all.32.mine, bf16[16,144,256]{2,1,0:T(8,128)(2,1)S(1)} %collective-permute-done.15.other), custom_call_target="tpu_custom_call" | custom-call | tf_op jit(solution)/shard_map/pallas_call | solution.py:616
  (195 shorter events, 29.9 us)
Async XLA Ops:
  0.6 16.2 %collective-permute-start.1 = (bf16[192,256]{1,0:T(8,128)(2,1)}, bf16[192,256]{1,0:T(8,128)(2,1)S(1)}, u32[]{:S(2)}, u32[]{:S(2)}) collective-permute-start(bf16[192,256]{1,0:T(8,128)(2,1)} %bitcast.48), channel_id=1, source_target_pairs={{1,2},{3,4},{5,6},{9,10},{11,12},{13,14},{17,18},{19,20},{21,22},{... | collective-permute-start | bytes 294920 | tf_op jit(solution)/shard_map/ppermute | solution.py:509
  5.2 11.6 %collective-permute-start = (bf16[192,256]{1,0:T(8,128)(2,1)}, bf16[192,256]{1,0:T(8,128)(2,1)S(1)}, u32[]{:S(2)}, u32[]{:S(2)}) collective-permute-start(bf16[192,256]{1,0:T(8,128)(2,1)} %bitcast.49), channel_id=1, source_target_pairs={{0,1},{1,0},{2,3},{3,2},{4,5},{5,4},{6,7},{7,6},{8,9},{9,8},{10,11... | collective-permute-start | bytes 294920 | tf_op jit(solution)/shard_map/ppermute | solution.py:508
  5.4 0.9 copy-start.6
  6.9 9.9 %collective-permute-start.2 = (bf16[16,256]{1,0:T(8,128)(2,1)S(1)}, bf16[16,256]{1,0:T(8,128)(2,1)S(1)}, u32[]{:S(2)}, u32[]{:S(2)}) collective-permute-start(bf16[16,256]{1,0:T(8,128)(2,1)S(1)} %get-tuple-element.38), channel_id=1, source_target_pairs={{0,8},{1,9},{2,10},{3,11},{4,12},{5,13},{6,14},{7,15},{16,24},{17,... | collective-permute-start | bytes 24584 | tf_op jit(solution)/shard_map/ppermute | solution.py:510
  8.2 8.7 %collective-permute-start.3 = (bf16[16,256]{1,0:T(8,128)(2,1)S(1)}, bf16[16,256]{1,0:T(8,128)(2,1)S(1)}, u32[]{:S(2)}, u32[]{:S(2)}) collective-permute-start(bf16[16,256]{1,0:T(8,128)(2,1)S(1)} %get-tuple-element.39), channel_id=1, source_target_pairs={{8,16},{9,17},{10,18},{11,19},{12,20},{13,21},{14,22},{15,23},{40,... | collective-permute-start | bytes 24584 | tf_op jit(solution)/shard_map/ppermute | solution.py:511
  15.0 20.7 %copy-start.25 = (s32[3]{0:T(128)}, s32[3]{0:T(128)S(1)}, u32[]{:S(2)}) copy-start(s32[3]{0:T(128)S(1)} %iota_add_fusion) | copy-start | bytes 40
  16.9 0.9 copy-start.7
  22.8 34.8 %all-to-all-start = ((bf16[16,80,256]{2,1,0:T(8,128)(2,1)}), bf16[16,80,256]{2,1,0:T(8,128)(2,1)S(1)}, u32[]{:S(2)}, u32[]{:S(2)}) async-start(bf16[16,80,256]{2,1,0:T(8,128)(2,1)} %get-tuple-element.44), calls=%async_computation | async-start | bytes 1310720 | tf_op jit(solution)/shard_map/all_to_all | solution.py:415
  36.0 14.6 %collective-permute-start.4 = (bf16[96,256]{1,0:T(8,128)(2,1)S(1)}, bf16[96,256]{1,0:T(8,128)(2,1)S(1)}, u32[]{:S(2)}, u32[]{:S(2)}) collective-permute-start(bf16[96,256]{1,0:T(8,128)(2,1)S(1)} %get-tuple-element.41), channel_id=1, source_target_pairs={{0,8},{1,9},{2,10},{3,11},{4,12},{5,13},{6,14},{7,15},{16,24},{17,... | collective-permute-start | bytes 147464 | tf_op jit(solution)/shard_map/ppermute | solution.py:525
  37.7 12.9 %collective-permute-start.5 = (bf16[96,256]{1,0:T(8,128)(2,1)S(1)}, bf16[96,256]{1,0:T(8,128)(2,1)S(1)}, u32[]{:S(2)}, u32[]{:S(2)}) collective-permute-start(bf16[96,256]{1,0:T(8,128)(2,1)S(1)} %get-tuple-element.42), channel_id=1, source_target_pairs={{8,16},{9,17},{10,18},{11,19},{12,20},{13,21},{14,22},{15,23},{24,... | collective-permute-start | bytes 147464 | tf_op jit(solution)/shard_map/ppermute | solution.py:525
  39.8 6.8 %copy-start.17 = (bf16[6,4,4,3,2]{4,3,2,1,0:T(4,128)(2,1)}, bf16[6,4,4,3,2]{4,3,2,1,0:T(4,128)(2,1)S(1)}, u32[]{:S(2)}) copy-start(bf16[6,4,4,3,2]{4,3,2,1,0:T(4,128)(2,1)S(1)} %copy.117) | copy-start | bytes 3460
  46.7 10.9 %copy-start.1 = (bf16[3,3,256,256]{3,2,1,0:T(8,128)(2,1)S(1)}, bf16[3,3,256,256]{3,2,1,0:T(8,128)(2,1)}, u32[]{:S(2)}) copy-start(bf16[3,3,256,256]{3,2,1,0:T(8,128)(2,1)} %kernel.9) | copy-start | bytes 3538948
  57.6 7.4 %copy-start.18 = (bf16[6,4,4,3,2]{4,3,2,1,0:T(4,128)(2,1)S(1)}, bf16[6,4,4,3,2]{4,3,2,1,0:T(4,128)(2,1)}, u32[]{:S(2)}) copy-start(bf16[6,4,4,3,2]{4,3,2,1,0:T(4,128)(2,1)} %copy-done.17) | copy-start | bytes 3460
  57.6 7.4 %copy-start.19 = (bf16[6,4,4,3,2]{4,3,2,1,0:T(4,128)(2,1)S(1)}, bf16[6,4,4,3,2]{4,3,2,1,0:T(4,128)(2,1)}, u32[]{:S(2)}) copy-start(bf16[6,4,4,3,2]{4,3,2,1,0:T(4,128)(2,1)} %copy.140) | copy-start | bytes 3460
  60.2 0.8 copy-start.4
  61.0 3.9 %copy-start.8 = (bf16[576,256]{1,0:T(8,128)(2,1)}, bf16[576,256]{1,0:T(8,128)(2,1)S(1)}, u32[]{:S(2)}) copy-start(bf16[576,256]{1,0:T(8,128)(2,1)S(1)} %get-tuple-element.59.refs_1_) | copy-start | bytes 884740
  61.0 23.4 %all-to-all-start.1 = ((bf16[16,64,256]{2,1,0:T(8,128)(2,1)}), bf16[16,64,256]{2,1,0:T(8,128)(2,1)S(1)}, u32[]{:S(2)}, u32[]{:S(2)}) async-start(bf16[16,64,256]{2,1,0:T(8,128)(2,1)} %get-tuple-element.48), calls=%async_computation.1 | async-start | bytes 1048576 | tf_op jit(solution)/shard_map/all_to_all | solution.py:415
  70.3 6.7 %copy-start.23 = (pred[2,2,4]{2,1,0:T(4,128)(4,1)S(1)}, pred[2,2,4]{2,1,0:T(4,128)(4,1)}, u32[]{:S(2)}) copy-start(pred[2,2,4]{2,1,0:T(4,128)(4,1)} %iota_compare_fusion.2) | copy-start | bytes 52
  70.3 6.7 %copy-start.24 = (pred[2,2,4]{2,1,0:T(4,128)(4,1)S(1)}, pred[2,2,4]{2,1,0:T(4,128)(4,1)}, u32[]{:S(2)}) copy-start(pred[2,2,4]{2,1,0:T(4,128)(4,1)} %iota_compare_fusion.3) | copy-start | bytes 52
  70.3 14.2 %copy-start = (bf16[3,3,256,256]{3,2,1,0:T(8,128)(2,1)S(1)}, bf16[3,3,256,256]{3,2,1,0:T(8,128)(2,1)}, u32[]{:S(2)}) copy-start(bf16[3,3,256,256]{3,2,1,0:T(8,128)(2,1)} %kernel.8) | copy-start | bytes 3538948
  70.3 14.2 %copy-start.14 = (bf16[3,1,8,8,256]{4,3,2,1,0:T(8,128)(2,1)S(1)}, bf16[3,1,8,8,256]{4,3,2,1,0:T(8,128)(2,1)}, u32[]{:S(2)}) copy-start(bf16[3,1,8,8,256]{4,3,2,1,0:T(8,128)(2,1)} %param.7) | copy-start | bytes 294916
  74.1 17.5 %copy-start.28 = (s32[2]{0:T(128)S(1)}, s32[2]{0:T(128)}, u32[]{:S(2)}) copy-start(s32[2]{0:T(128)} %get-tuple-element.131) | copy-start | bytes 28
  86.0 0.7 copy-start.10
  87.4 14.6 %copy-start.22 = (s32[4,2,3,2]{0,3,2,1:T(2,128)S(1)}, s32[4,2,3,2]{0,3,2,1:T(2,128)}, u32[]{:S(2)}) copy-start(s32[4,2,3,2]{0,3,2,1:T(2,128)} %get-tuple-element.96) | copy-start | bytes 580
  87.4 14.6 %copy-start.27 = (s32[2]{0:T(128)S(1)}, s32[2]{0:T(128)}, u32[]{:S(2)}) copy-start(s32[2]{0:T(128)} %get-tuple-element.132) | copy-start | bytes 28
  87.4 15.1 %copy-start.26 = (s32[3]{0:T(128)S(1)}, s32[3]{0:T(128)}, u32[]{:S(2)}) copy-start(s32[3]{0:T(128)} %copy-done.25) | copy-start | bytes 40
  87.4 15.2 %copy-start.30 = (pred[6,2]{1,0:T(8,128)(4,1)S(1)}, pred[6,2]{1,0:T(8,128)(4,1)}, u32[]{:S(2)}) copy-start(pred[6,2]{1,0:T(8,128)(4,1)} %copy.133) | copy-start | bytes 40
  87.4 15.2 %copy-start.21 = (bf16[8,2,2,8]{3,2,1,0:T(2,128)(2,1)S(1)}, bf16[8,2,2,8]{3,2,1,0:T(2,128)(2,1)}, u32[]{:S(2)}) copy-start(bf16[8,2,2,8]{3,2,1,0:T(2,128)(2,1)} %compare_convert_fusion.2) | copy-start | bytes 1540
  87.4 6.1 %collective-permute-start.7 = (bf16[192,256]{1,0:T(8,128)(2,1)S(1)}, bf16[192,256]{1,0:T(8,128)(2,1)S(1)}, u32[]{:S(2)}, u32[]{:S(2)}) collective-permute-start(bf16[192,256]{1,0:T(8,128)(2,1)S(1)} %get-tuple-element.49.own), channel_id=1, source_target_pairs={{1,2},{3,4},{5,6},{9,10},{11,12},{13,14},{17,18},{19,20},{21,22},{... | collective-permute-start | bytes 294920 | tf_op jit(solution)/shard_map/ppermute | solution.py:509
  89.5 4.0 %collective-permute-start.6 = (bf16[192,256]{1,0:T(8,128)(2,1)S(1)}, bf16[192,256]{1,0:T(8,128)(2,1)S(1)}, u32[]{:S(2)}, u32[]{:S(2)}) collective-permute-start(bf16[192,256]{1,0:T(8,128)(2,1)S(1)} %get-tuple-element.49.own), channel_id=1, source_target_pairs={{0,1},{1,0},{2,3},{3,2},{4,5},{5,4},{6,7},{7,6},{8,9},{9,8},{10,11... | collective-permute-start | bytes 294920 | tf_op jit(solution)/shard_map/ppermute | solution.py:508
  90.3 2.5 %collective-permute-start.8 = (bf16[16,256]{1,0:T(8,128)(2,1)S(1)}, bf16[16,256]{1,0:T(8,128)(2,1)S(1)}, u32[]{:S(2)}, u32[]{:S(2)}) collective-permute-start(bf16[16,256]{1,0:T(8,128)(2,1)S(1)} %get-tuple-element.50), channel_id=1, source_target_pairs={{0,8},{1,9},{2,10},{3,11},{4,12},{5,13},{6,14},{7,15},{16,24},{17,... | collective-permute-start | bytes 24584 | tf_op jit(solution)/shard_map/ppermute | solution.py:510
  90.9 1.8 collective-permute-start.9
  93.5 0.9 copy-start.16
  96.2 9.4 %copy-start.29 = (pred[6,2]{1,0:T(8,128)(4,1)S(1)}, pred[6,2]{1,0:T(8,128)(4,1)}, u32[]{:S(2)}) copy-start(pred[6,2]{1,0:T(8,128)(4,1)} %copy.129) | copy-start | bytes 40
  96.2 9.4 %copy-start.20 = (bf16[8,2,2,8]{3,2,1,0:T(2,128)(2,1)S(1)}, bf16[8,2,2,8]{3,2,1,0:T(2,128)(2,1)}, u32[]{:S(2)}) copy-start(bf16[8,2,2,8]{3,2,1,0:T(2,128)(2,1)} %compare_convert_fusion.3) | copy-start | bytes 1540
  96.2 29.8 %all-to-all-start.2 = ((bf16[16,64,256]{2,1,0:T(8,128)(2,1)}), bf16[16,64,256]{2,1,0:T(8,128)(2,1)S(1)}, u32[]{:S(2)}, u32[]{:S(2)}) async-start(bf16[16,64,256]{2,1,0:T(8,128)(2,1)} %get-tuple-element.55), calls=%async_computation.2 | async-start | bytes 1048576 | tf_op jit(solution)/shard_map/all_to_all | solution.py:415
  108.6 11.5 %copy-start.11 = (bf16[480,256]{1,0:T(8,128)(2,1)S(1)}, bf16[480,256]{1,0:T(8,128)(2,1)}, u32[]{:S(2)}) copy-start(bf16[480,256]{1,0:T(8,128)(2,1)} %copy-done.10) | copy-start | bytes 737284
  108.6 15.8 %collective-permute-start.10 = (bf16[96,256]{1,0:T(8,128)(2,1)}, bf16[96,256]{1,0:T(8,128)(2,1)}, u32[]{:S(2)}, u32[]{:S(2)}) collective-permute-start(bf16[96,256]{1,0:T(8,128)(2,1)} %get-tuple-element.53), channel_id=1, source_target_pairs={{0,8},{1,9},{2,10},{3,11},{4,12},{5,13},{6,14},{7,15},{16,24},{17,... | collective-permute-start | bytes 147464 | tf_op jit(solution)/shard_map/ppermute | solution.py:558
  112.2 12.2 %collective-permute-start.11 = (bf16[96,256]{1,0:T(8,128)(2,1)}, bf16[96,256]{1,0:T(8,128)(2,1)}, u32[]{:S(2)}, u32[]{:S(2)}) collective-permute-start(bf16[96,256]{1,0:T(8,128)(2,1)} %get-tuple-element.54), channel_id=1, source_target_pairs={{8,16},{9,17},{10,18},{11,19},{12,20},{13,21},{14,22},{15,23},{24,... | collective-permute-start | bytes 147464 | tf_op jit(solution)/shard_map/ppermute | solution.py:558
  120.1 0.9 copy-start.13
  123.3 1.0 copy-start.2
  124.3 7.7 %collective-permute-start.13 = (bf16[16,72,256]{2,1,0:T(8,128)(2,1)}, bf16[16,72,256]{2,1,0:T(8,128)(2,1)}, u32[]{:S(2)}, u32[]{:S(2)}) collective-permute-start(bf16[16,72,256]{2,1,0:T(8,128)(2,1)} %get-tuple-element.66), channel_id=1, source_target_pairs={{0,1},{1,0},{2,3},{3,2},{4,5},{5,4},{6,7},{7,6},{8,9},{9,8},{10,11... | collective-permute-start | bytes 1769480 | tf_op jit(solution)/shard_map/ppermute | solution.py:583
  126.0 1.0 copy-start.5
  127.1 6.5 %copy-start.3 = (f32[16,72,256]{2,1,0:T(8,128)S(1)}, f32[16,72,256]{2,1,0:T(8,128)}, u32[]{:S(2)}) copy-start(f32[16,72,256]{2,1,0:T(8,128)} %copy-done.2) | copy-start | bytes 3538948
  129.0 1.0 copy-start.9
  131.4 2.1 collective-permute-start.12
  206.6 12.3 %collective-permute-start.15 = (bf16[16,144,256]{2,1,0:T(8,128)(2,1)S(1)}, bf16[16,144,256]{2,1,0:T(8,128)(2,1)S(1)}, u32[]{:S(2)}, u32[]{:S(2)}) collective-permute-start(bf16[16,144,256]{2,1,0:T(8,128)(2,1)S(1)} %all_to_all.32.mine), channel_id=1, source_target_pairs={{0,1},{1,0},{2,3},{3,2},{4,5},{5,4},{6,7},{7,6},{8,9},{9,8},{10,11... | collective-permute-start | bytes 3538952 | tf_op jit(solution)/shard_map/ppermute | solution.py:615
  213.1 4.5 %collective-permute-start.14 = (bf16[48,256]{1,0:T(8,128)(2,1)S(1)}, bf16[48,256]{1,0:T(8,128)(2,1)S(1)}, u32[]{:S(2)}, u32[]{:S(2)}) collective-permute-start(bf16[48,256]{1,0:T(8,128)(2,1)S(1)} %get-tuple-element.70), channel_id=1, source_target_pairs={{0,7},{1,6},{2,5},{3,4},{4,3},{5,2},{6,1},{7,0},{8,15},{9,14},{10,... | collective-permute-start | bytes 73736 | tf_op jit(solution)/shard_map/ppermute | solution.py:604
  (2 other events, 1.3 us)

commit v8 on v7

--- a/solution.py
+++ b/solution.py
@@ -416,79 +416,101 @@
     return got.reshape(-1, C)
 
 
-def seam_picks(neighbour, seam_codes, row, col, face_group):
-    tables = (neighbour, seam_codes, face_group, row)
-    gather, add, turned = seam_select(*tables, col, jnp.arange(4, dtype=jnp.int32))
+def picks_kernel(pos, nexts, codes, pick_12, pick_10, add_10, share):
+    row, col, group = pos[0], pos[1], pos[3]
+    bottom, right = row // 4, col // 4
+    mirror = right + 2 * bottom
     centre = (row == 3) | (row == 4)
-    pick_12, pick_10 = expand(gather, turned, 12, 80, centre), expand(gather, turned, 10, 64)
-    add_10 = expand(add, turned, 10, 64, centre)
-    same_side = 2 * jnp.arange(2, dtype=jnp.int32) + col // 4
-    shares = []
-    for to in (col, 7 - col):
-        _, add, turned = seam_select(*tables, to, same_side)
-        shares.append(expand(add, turned, 8, 48))
-    return pick_12, pick_10, add_10, jnp.concatenate(shares, axis=0)
-
-
-def seam_select(neighbour, seam_codes, face_group, row, col, slot_mirror):
-    slots = slot_mirror.shape[0]
-    mirror = col // 4 + 2 * (row // 4)
-    on_edge = jnp.stack([(row == 0) | (row == 7), (col == 0) | (col == 7)])
-    bottom, right = row // 4, col // 4
-    own_side = jnp.stack([bottom, 2 + right])
-    first = face_group * 3
-    opposite, reverse = 1 - seam_codes % 2, seam_codes // 2
-    types = jnp.arange(4) // 2
-    rel_of = jnp.where(types == 0, 2 * opposite + reverse, 2 * reverse + opposite)
-    slot_type = jnp.arange(2, dtype=jnp.int32)
-
-    def on_side(table, side):
-        return jnp.sum(jnp.where(side[..., None] == jnp.arange(4), table, 0), axis=-1)
-
-    own_next = lax.dynamic_slice_in_dim(neighbour, first, 3, 0)
-    own_rel = lax.dynamic_slice_in_dim(rel_of, first, 3, 0)
-    next_face = on_side(own_next[:, None, :], own_side[None])
-    next_rel = on_side(own_rel[:, None, :], own_side[None])
-    faces = jnp.arange(12, dtype=jnp.int32).reshape(4, 1, 3, 1)
-    same_type = (slot_type[:, None, None, None, None] == slot_type) & on_edge[:, None, None, None, None]
-    gather = (
-        (next_face[:, :, None, None, None, None] == faces)
-        & ((next_rel ^ mirror)[:, :, None, None, None, None] == slot_mirror[:, None, None])
-        & same_type
-    )
+    far = 1 << 20
+    begins = [jnp.where((at == 0) | (at == 7), 0, far) for at in (row, col)]
+
+    def seam(face, kind, side):
+        code = codes[face, side]
+        opposite, reverse = 1 - (code & 1), code >> 1
+        rel = 2 * opposite + reverse if kind == 0 else 2 * reverse + opposite
+        return nexts[face, side], rel, reverse
+
+    for length, block, out in ((12, 80, pick_12), (10, 64, pick_10)):
+        rows = out.shape[0]
+        at_row = lax.broadcasted_iota(jnp.int32, (rows, 128), 0)
+        lane = lax.broadcasted_iota(jnp.int32, (rows, 128), 1)
+        target = jnp.full((rows, 128), -1, jnp.int32)
+        for k in range(3):
+            for kind in range(2):
+                across, rel, reverse = seam(3 * group + k, kind, bottom if kind == 0 else 2 + right)
+                slot_mirror = mirror ^ rel
+                slot = (lax.div(across, 3) * 4 + slot_mirror) * block + (lax.rem(across, 3) * 2 + kind) * length
+                here = at_row - (2 * k + kind) * length
+                at = jnp.where(reverse == 1, length - 1 - here, here)
+                place = slot + at
+                if length == 12 and kind == 1:
+                    upper = slot_mirror < 2
+                    high = jnp.where(centre & upper, length - 2, far)
+                    low = jnp.where(centre & (slot_mirror >= 2), 1, -1)
+                    place = jnp.where(at >= high, place + 2 * block - 8, place)
+                    place = jnp.where(at <= low, place - 2 * block + 8, place)
+                inside = (here >= begins[kind]) & (here < length)
+                target = jnp.where(inside, place, target)
+        for c in range(0, 16 * block, 128):
+            out[:, c : c + 128] = (lane + c == target).astype(F32).astype(BF16)
+
+    q = lax.broadcasted_iota(jnp.int32, (8, 1024), 1)
+    within = q & 63
+    strip = (within * 205) >> 11
+    at = within - 10 * strip
+    slot = jnp.where(strip < 6, (q >> 6) * 6 + strip, -1)
+    base = jnp.full((8, 1024), -far, jnp.int32)
+    for f in range(4):
+        for m in range(4):
+            for j in range(3):
+                for kind in range(2):
+                    across, rel, _ = seam(3 * f + j, kind, m // 2 if kind == 0 else 2 + m % 2)
+                    mine = (lax.div(across, 3) == group) & ((m ^ rel) == mirror)
+                    value = jnp.where(mine, (lax.rem(across, 3) * 2 + kind) * 10 - begins[kind], -far)
+                    base = jnp.where(slot == (f * 4 + m) * 6 + j * 2 + kind, value, base)
+    slot_mirror = (q >> 6) & 3
+    kinds = strip & 1
     rel = slot_mirror ^ mirror
-    from_side = jnp.stack([bottom ^ (rel // 2), 2 + (right ^ (rel % 2))], axis=1)[None, :, None, :]
-    slot_next = on_side(neighbour.reshape(4, 1, 3, 1, 4), from_side)
-    slot_rel = on_side(rel_of.reshape(4, 1, 3, 1, 4), from_side)
-    own_faces = (first + jnp.arange(3, dtype=jnp.int32))[:, None, None, None, None, None]
-    add = (slot_next == own_faces) & (slot_rel == rel[:, None, None]) & same_type
-    turned = jnp.stack([rel % 2, rel // 2], axis=1) == 1
-    return gather, add, turned
-
-
-def expand(select, turned, length, block, centre=None):
-    slots = turned.shape[0]
-    at = jnp.arange(length, dtype=jnp.int32)
-    source = jnp.where(turned[:, :, None], length - 1 - at, at)
-    here = source[..., None] == at
-
-    def over_cells(select, here):
-        select = select.reshape(6, 1, 4, slots, 3, 2, 1).astype(BF16)
-        here = here.transpose(2, 0, 1, 3).reshape(1, length, 1, slots, 1, 2, length).astype(BF16)
-        return select * here
-
-    full = over_cells(select, here)
-    if centre is not None:
-        source = jnp.roll(source, 2, axis=0)
-        upper = (jnp.arange(4) < 2)[:, None, None]
-        moved = jnp.where(upper, source + 8, source - 8)
-        across = jnp.where(upper, source <= 1, source >= length - 2)
-        across = across & centre & (jnp.arange(2) == 1)[None, :, None]
-        full = full + over_cells(jnp.roll(select, 2, axis=3), (moved[..., None] == at) & across[..., None])
-    full = full.reshape(6 * length, 4 * slots, 6 * length)
-    rows = -(-6 * length // 16) * 16
-    full = jnp.pad(full, ((0, rows - 6 * length), (0, 0), (0, block - 6 * length)))
-    return full.reshape(rows, 4 * slots * block)
+    flip = jnp.where(kinds == 0, rel & 1, rel >> 1)
+    first = base + jnp.where(flip == 1, 9 - at, at)
+    chunks = [base[:, 128 * (i ^ 1) : 128 * (i ^ 1) + 128] for i in range(8)]
+    source = jnp.where(slot_mirror < 2, at - 8, at + 8)
+    second = jnp.concatenate(chunks, axis=1) + jnp.where(flip == 1, source, 9 - source)
+    reach = jnp.where(centre, 9, -far)
+    second = jnp.where((kinds == 1) & (source >= 0) & (source <= reach) & (strip < 6), second, -far)
+    at_row = lax.broadcasted_iota(jnp.int32, (8, 1024), 0)
+    parts = [((first == at_row + r) | (second == at_row + r)).astype(F32) for r in range(0, 64, 8)]
+    add_10[...] = jnp.concatenate(parts, axis=0).astype(BF16)
+
+    q = lax.broadcasted_iota(jnp.int32, (8, 384), 1)
+    slot, at = q >> 3, q & 7
+    base = jnp.full((8, 384), -far, jnp.int32)
+    step = jnp.zeros((8, 384), jnp.int32)
+    for f in range(4):
+        for half in range(2):
+            m = 2 * half + right
+            for j in range(3):
+                for kind in range(2):
+                    across, rel, reverse = seam(3 * f + j, kind, half if kind == 0 else 2 + right)
+                    to = (m ^ rel) ^ mirror
+                    mine = (lax.div(across, 3) == group) & (to < 2)
+                    value = to * 48 + (lax.rem(across, 3) * 2 + kind) * 8 + 7 * reverse
+                    value = jnp.where(mine, value - begins[kind], -far)
+                    here = slot == (f * 2 + half) * 6 + j * 2 + kind
+                    base = jnp.where(here, value, base)
+                    step = jnp.where(here, 1 - 2 * reverse, step)
+    first = base + step * at
+    at_row = lax.broadcasted_iota(jnp.int32, (8, 384), 0)
+    share[...] = jnp.concatenate([(first == at_row + r).astype(F32) for r in range(0, 96, 8)], axis=0).astype(BF16)
+
+
+def seam_picks(pos, nexts, codes):
+    return pl.pallas_call(
+        picks_kernel,
+        out_shape=[jax.ShapeDtypeStruct(shape, BF16) for shape in ((80, 1280), (64, 1024), (64, 1024), (96, 384))],
+        in_specs=[pl.BlockSpec(memory_space=pltpu.SMEM)] * 3,
+        out_specs=[pl.BlockSpec(memory_space=pltpu.VMEM)] * 4,
+    )(pos, nexts, codes)
 
 
 def body(inputs, cotangent, kernel_one, kernel_two, neighbour, seam_codes):
@@ -496,7 +518,7 @@
     core = lax.axis_index("core")
     row = lax.axis_index("zh") * 4 + lax.axis_index("x")
     col = lax.axis_index("y") * 2 + core
-    pos = jnp.stack([row, col, core]).astype(jnp.int32)
+    pos = jnp.stack([row, col, core, face_group]).astype(jnp.int32)
     flat = 36 * PITCH
     spare = flat + 8
     ends = [((16, C), BF16), ((16, C), BF16)]
@@ -521,7 +543,7 @@
         *beside(x, first, second),
     )
     send, neighbour, seam_codes = lax.optimization_barrier((send, neighbour, seam_codes))
-    pick_12, pick_10, add_10, add_8 = seam_picks(neighbour, seam_codes, row, col, face_group)
+    pick_12, pick_10, add_10, add_8 = seam_picks(pos, neighbour, seam_codes)
     first, second = lax.ppermute(first, TILE, EVEN_ROWS), lax.ppermute(second, TILE, ODD_ROWS)
     filled_in, pre_one, hidden, send = run(
         one_kernel,
@@ -581,7 +603,6 @@
 
     keep_two, payload_two = grad_of(10, 0, 0, filled_hidden, wide_two)
     got_two = lax.ppermute(payload_two, "core", CORES)
-    got, add_8 = lax.optimization_barrier((got, add_8))
     wide_one, own, strips = run(
         delta_kernel,
         [((24 * PITCH, C), BF16), ((192, C), BF16), ((48, C), BF16)],

time: 226 us -> 202 us (0.89)
  local copies, waits for them, and re-layouts: 39.6 us -> 10.9 us
  other arithmetic: 21.8 us -> 0.08 us
  blocking collectives: 70.4 us -> 87.1 us
  waiting for transfers between devices: 20.2 us -> 30.7 us
    all_to_all x0 -> x1, blocking collectives: none -> 22.9 us  [seam_exchange(): got = lax.all_to_all(send, AXES, 0, 0, axis_index_groups=SEAM_GROUPS)]
    all_to_all x3 -> x2, waiting for transfers between devices: 12.9 us -> 22.6 us  [seam_exchange(): got = lax.all_to_all(send, AXES, 0, 0, axis_index_groups=SEAM_GROUPS)]
    add x5 -> x0, other arithmetic: 9.21 us -> none  [the longest x2 9.17 us: expand(): full + over_cells(jnp.roll(select, 2, axis=3), (moved[..., None] == at) &...]
    add x2 -> x0, local copies, waits for them, and re-layouts: 7.29 us -> none  [expand(): full + over_cells(jnp.roll(select, 2, axis=3), (moved[..., None] == at) &...]
    mul x3 -> x0, local copies, waits for them, and re-layouts: 7.03 us -> none  [over_cells(): return select * here]
    all_to_all x2, blocking collectives: 46.2 us -> 39.3 us  [body(): part = lax.all_to_all(part, AXES, 0, 0, axis_index_groups=PLANE_GROUPS)]
    convert_element_type x4 -> x0, local copies, waits for them, and re-layouts: 3.91 us -> none  [over_cells(): select = select.reshape(6, 1, 4, slots, 3, 2, 1).astype(BF16)]
    pad x3 -> x0, local copies, waits for them, and re-layouts: 3.45 us -> none  [expand(): jnp.pad(full, ((0, rows - 6 * length), (0, 0), (0, block - 6 * length)))]
  transfers between devices with their start and end apart: 19 -> 18, of which waited for: 6 -> 7; matrix products, arithmetic and copies ran while one was open for 22% -> 1% of each run, Pallas kernels for 4% -> 6%
where the time goes in v8:
time: 202 us; the launch traced here: 199 us
  blocking collectives  87.1 us (43%)
  starting transfers between devices  43.9 us (22%)
  waiting for transfers between devices  30.7 us (15%)
  Pallas kernels  25 us (12%)
  local copies, waits for them, and re-layouts  10.9 us (5%)
    all_to_all x2, blocking collectives, body(): part = lax.all_to_all(part, AXES, 0, 0, axis_index_groups=PLANE_GROUPS)  39.3 us
    all_to_all x1, blocking collectives, body(): got = lax.all_to_all(part, AXES, 0, 0, axis_index_groups=ACROSS_GROUPS)  25 us
    all_to_all x1, blocking collectives, seam_exchange(): got = lax.all_to_all(send, AXES, 0, 0, axis_index_groups=SEAM_GROUPS)  22.9 us
    all_to_all x2, waiting for transfers between devices, seam_exchange(): got = lax.all_to_all(send, AXES, 0, 0, axis_index_groups=SEAM_GROUPS)  22.6 us
    pallas_call x14, Pallas kernels, run(): pl.pallas_call(kernel, out_shape=[jax.ShapeDtypeStruct(shape, dtype) for...  19.2 us
    all_to_all x2, starting transfers between devices, seam_exchange(): got = lax.all_to_all(send, AXES, 0, 0, axis_index_groups=SEAM_GROUPS)  18.4 us
    unnamed x46, local copies, waits for them, and re-layouts  9.55 us
    ppermute x2, starting transfers between devices, body(): lax.ppermute(first, TILE, EVEN_ROWS)  6.84 us
  transfers between devices with their start and end apart: 18, of which 7 were waited for; matrix products, arithmetic and copies ran while one was open for 1% of the time, Pallas kernels for 6%

profile of v8, /device:TPU:1, one launch (start us, length us, event | category | flops | bytes accessed | tf_op | source)
XLA Modules:
  0.0 198.8 jit_solution(4017151061348916134)
XLA Ops:
  0.6 4.7 %collective-permute-start.1 = (bf16[192,256]{1,0:T(8,128)(2,1)}, bf16[192,256]{1,0:T(8,128)(2,1)S(1)}, u32[]{:S(2)}, u32[]{:S(2)}) collective-permute-start(bf16[192,256]{1,0:T(8,128)(2,1)} %bitcast.17), channel_id=1, source_target_pairs={{1,2},{3,4},{5,6},{9,10},{11,12},{13,14},{17,18},{19,20},{21,22},{... | collective-permute-start | bytes 294920 | tf_op jit(solution)/shard_map/ppermute | solution.py:531
  5.6 0.9 copy-done.6
  7.0 1.3 collective-permute-start.2
  8.3 0.6 collective-permute-start.3
  9.6 1.6 shard_map.86
  11.2 0.7 copy-done.8
  11.9 13.0 %all-to-all-start = ((bf16[16,80,256]{2,1,0:T(8,128)(2,1)}), bf16[16,80,256]{2,1,0:T(8,128)(2,1)S(1)}, u32[]{:S(2)}, u32[]{:S(2)}) async-start(bf16[16,80,256]{2,1,0:T(8,128)(2,1)} %get-tuple-element.46), calls=%async_computation | async-start | bytes 1310720 | tf_op jit(solution)/shard_map/all_to_all | solution.py:415
  24.9 3.1 %collective-permute-start.4 = (bf16[96,256]{1,0:T(8,128)(2,1)S(1)}, bf16[96,256]{1,0:T(8,128)(2,1)S(1)}, u32[]{:S(2)}, u32[]{:S(2)}) collective-permute-start(bf16[96,256]{1,0:T(8,128)(2,1)S(1)} %get-tuple-element.43), channel_id=1, source_target_pairs={{0,8},{1,9},{2,10},{3,11},{4,12},{5,13},{6,14},{7,15},{16,24},{17,... | collective-permute-start | bytes 147464 | tf_op jit(solution)/shard_map/ppermute | solution.py:547
  28.0 0.7 collective-permute-start.5
  28.7 0.7 copy.9.nexts
  29.3 0.7 copy.10.codes
  30.0 2.8 %shard_map.87 = (bf16[80,1280]{1,0:T(8,128)(2,1)}, bf16[64,1024]{1,0:T(8,128)(2,1)}, bf16[64,1024]{1,0:T(8,128)(2,1)}, bf16[96,384]{1,0:T(8,128)(2,1)}) custom-call(s32[4]{0:T(128)} %copy-done.14, s32[12,4]{1,0:T(8,128)} %copy.9.nexts, s32[12,4]{1,0:T(8,128)} %copy.10.codes), custom_call_target="tpu_custom_call" | custom-call | tf_op jit(solution)/shard_map/pallas_call | solution.py:508
  32.9 14.4 %all-to-all-done = bf16[16,80,256]{2,1,0:T(8,128)(2,1)S(1)} async-done(((bf16[16,80,256]{2,1,0:T(8,128)(2,1)}), bf16[16,80,256]{2,1,0:T(8,128)(2,1)S(1)}, u32[]{:S(2)}, u32[]{:S(2)}) %all-to-all-start) | async-done | bytes 655392 | tf_op jit(solution)/shard_map/all_to_all | solution.py:415
  47.3 0.9 copy-done.7
  48.2 0.9 copy-done.9
  49.8 1.9 shard_map.88
  51.6 22.9 %all_to_all.30 = bf16[16,64,256]{2,1,0:T(8,128)(2,1)S(1)} all-to-all(bf16[16,64,256]{2,1,0:T(8,128)(2,1)S(1)} %get-tuple-element.51), channel_id=1, replica_groups={{0,7,56,63,64,71,120,127,128,135,184,191,192,199,248,255},{1,6,57,62,65..., dimensions={0} | all-to-all | bytes 1048576 | tf_op jit(solution)/shard_map/all_to_all | solution.py:415
  74.5 1.6 shard_map.89
  76.1 1.9 collective-permute-start.7
  78.2 1.7 collective-permute-start.8
  79.9 0.8 collective-permute-start.9
  80.9 1.2 collective-permute-done.7.odd
  82.1 1.8 shard_map.90
  83.9 0.7 copy-done.10
  84.6 5.5 %all-to-all-start.2 = ((bf16[16,64,256]{2,1,0:T(8,128)(2,1)}), bf16[16,64,256]{2,1,0:T(8,128)(2,1)S(1)}, u32[]{:S(2)}, u32[]{:S(2)}) async-start(bf16[16,64,256]{2,1,0:T(8,128)(2,1)} %get-tuple-element.59), calls=%async_computation.2 | async-start | bytes 1048576 | tf_op jit(solution)/shard_map/all_to_all | solution.py:415
  90.0 3.7 %collective-permute-start.10 = (bf16[96,256]{1,0:T(8,128)(2,1)S(1)}, bf16[96,256]{1,0:T(8,128)(2,1)S(1)}, u32[]{:S(2)}, u32[]{:S(2)}) collective-permute-start(bf16[96,256]{1,0:T(8,128)(2,1)S(1)} %get-tuple-element.57), channel_id=1, source_target_pairs={{0,8},{1,9},{2,10},{3,11},{4,12},{5,13},{6,14},{7,15},{16,24},{17,... | collective-permute-start | bytes 147464 | tf_op jit(solution)/shard_map/ppermute | solution.py:580
  93.8 0.7 collective-permute-start.11
  94.4 0.9 copy-done.13
  95.4 2.2 %shard_map.94 = (f32[16,72,256]{2,1,0:T(8,128)S(1)}, bf16[16,72,256]{2,1,0:T(8,128)(2,1)}) custom-call(s32[4]{0:T(128)S(1)} %copy-done.16, bf16[480,256]{1,0:T(8,128)(2,1)S(1)} %get-tuple-element.67.refs_1_, bf16[384,256]{1,0:T(8,128)(2,1)S(1)} %copy-done.13), custom_call_target="tpu_custom_call" | custom-call | tf_op jit(solution)/shard_map/pallas_call | solution.py:57
  97.6 1.0 copy-done.2
  98.7 0.9 copy-done.11
  99.6 1.3 shard_map.91.back
  100.9 8.2 %all-to-all-done.2 = bf16[16,64,256]{2,1,0:T(8,128)(2,1)S(1)} async-done(((bf16[16,64,256]{2,1,0:T(8,128)(2,1)}), bf16[16,64,256]{2,1,0:T(8,128)(2,1)S(1)}, u32[]{:S(2)}, u32[]{:S(2)}) %all-to-all-start.2) | async-done | bytes 524320 | tf_op jit(solution)/shard_map/all_to_all | solution.py:415
  109.1 1.0 copy-done.5
  110.1 0.9 copy-done.17
  111.0 2.1 %shard_map.92 = (bf16[384,256]{1,0:T(8,128)(2,1)S(1)}, bf16[192,256]{1,0:T(8,128)(2,1)S(1)}, bf16[48,256]{1,0:T(8,128)(2,1)S(1)}) custom-call(s32[4]{0:T(128)S(1)} %copy-done.16, bf16[480,256]{1,0:T(8,128)(2,1)S(1)} %shard_map.91.back, bf16[1024,256]{1,0:T(8,128)(2,1)S(1)} %bitcast.16, bf16[64,1024]{1,0:T(8,128)(2,1)S(1)} %copy-done.17, ...), custom_call_target="tpu_custom_call" | custom-call | tf_op jit(solution)/shard_map/pallas_call | solution.py:57
  113.1 1.4 shard_map.93
  114.7 2.0 collective-permute-done.12.got_one
  116.7 1.3 shard_map.95
  118.0 22.3 %all_to_all.31.parts = bf16[16,144,256]{2,1,0:T(8,128)(2,1)S(1)} all-to-all(bf16[16,144,256]{2,1,0:T(8,128)(2,1)S(1)} %shard_map.95), channel_id=1, replica_groups={{0,8,16,24,2,10,18,26,4,12,20,28,6,14,22,30},{1,9,17,25,3,11,19,27,5,13..., dimensions={0} | all-to-all | bytes 2359296 | tf_op jit(solution)/shard_map/all_to_all | solution.py:620
  140.3 0.7 shard_map.96
  141.0 25.0 %all_to_all.32.got.parts = bf16[8,192,256]{2,1,0:T(8,128)(2,1)S(1)} all-to-all(bf16[8,192,256]{2,1,0:T(8,128)(2,1)S(1)} %shard_map.96), channel_id=1, replica_groups={{0,56,64,120,128,184,192,248},{1,57,65,121,129,185,193,249},{2,58,66,12..., dimensions={0} | all-to-all | bytes 1572864 | tf_op jit(solution)/shard_map/all_to_all | solution.py:622
  166.6 17.0 %all_to_all.33.mine = bf16[16,144,256]{2,1,0:T(8,128)(2,1)S(1)} all-to-all(bf16[16,144,256]{2,1,0:T(8,128)(2,1)S(1)} %shard_map.99), channel_id=1, replica_groups={{0,8,16,24,2,10,18,26,4,12,20,28,6,14,22,30},{1,9,17,25,3,11,19,27,5,13..., dimensions={0} | all-to-all | bytes 2359296 | tf_op jit(solution)/shard_map/all_to_all | solution.py:635
  183.6 5.4 %collective-permute-start.15 = (bf16[16,144,256]{2,1,0:T(8,128)(2,1)S(1)}, bf16[16,144,256]{2,1,0:T(8,128)(2,1)S(1)}, u32[]{:S(2)}, u32[]{:S(2)}) collective-permute-start(bf16[16,144,256]{2,1,0:T(8,128)(2,1)S(1)} %all_to_all.33.mine), channel_id=1, source_target_pairs={{0,1},{1,0},{2,3},{3,2},{4,5},{5,4},{6,7},{7,6},{8,9},{9,8},{10,11... | collective-permute-start | bytes 3538952 | tf_op jit(solution)/shard_map/ppermute | solution.py:636
  189.0 0.7 shard_map.97
  190.3 4.0 %collective-permute-done.14.two = bf16[48,256]{1,0:T(8,128)(2,1)S(1)} collective-permute-done((bf16[48,256]{1,0:T(8,128)(2,1)S(1)}, bf16[48,256]{1,0:T(8,128)(2,1)S(1)}, u32[]{:S(2)}, u32[]{:S(2)}) %collective-permute-start.14) | collective-permute-done | bytes 24608 | tf_op jit(solution)/shard_map/ppermute | solution.py:625
  194.3 1.3 shard_map.98
  195.5 3.1 %shard_map.100 = (f32[9,256,256]{2,1,0:T(8,128)}, f32[9,256,256]{2,1,0:T(8,128)}) custom-call(s32[4]{0:T(128)S(1)} %copy-done.16, bf16[16,144,256]{2,1,0:T(8,128)(2,1)S(1)} %all_to_all.33.mine, bf16[16,144,256]{2,1,0:T(8,128)(2,1)S(1)} %collective-permute-done.15.other), custom_call_target="tpu_custom_call" | custom-call | tf_op jit(solution)/shard_map/pallas_call | solution.py:637
  (57 shorter events, 3.7 us)
Async XLA Ops:
  0.6 46.7 %copy-start.1 = (bf16[3,3,256,256]{3,2,1,0:T(8,128)(2,1)S(1)}, bf16[3,3,256,256]{3,2,1,0:T(8,128)(2,1)}, u32[]{:S(2)}) copy-start(bf16[3,3,256,256]{3,2,1,0:T(8,128)(2,1)} %kernel.9) | copy-start | bytes 3538948
  0.6 9.0 %collective-permute-start.1 = (bf16[192,256]{1,0:T(8,128)(2,1)}, bf16[192,256]{1,0:T(8,128)(2,1)S(1)}, u32[]{:S(2)}, u32[]{:S(2)}) collective-permute-start(bf16[192,256]{1,0:T(8,128)(2,1)} %bitcast.17), channel_id=1, source_target_pairs={{1,2},{3,4},{5,6},{9,10},{11,12},{13,14},{17,18},{19,20},{21,22},{... | collective-permute-start | bytes 294920 | tf_op jit(solution)/shard_map/ppermute | solution.py:531
  5.4 4.3 %collective-permute-start = (bf16[192,256]{1,0:T(8,128)(2,1)}, bf16[192,256]{1,0:T(8,128)(2,1)S(1)}, u32[]{:S(2)}, u32[]{:S(2)}) collective-permute-start(bf16[192,256]{1,0:T(8,128)(2,1)} %bitcast.18), channel_id=1, source_target_pairs={{0,1},{1,0},{2,3},{3,2},{4,5},{5,4},{6,7},{7,6},{8,9},{9,8},{10,11... | collective-permute-start | bytes 294920 | tf_op jit(solution)/shard_map/ppermute | solution.py:530
  5.6 0.9 copy-start.6
  6.5 23.6 %copy-start.14 = (s32[4]{0:T(128)}, s32[4]{0:T(128)S(1)}, u32[]{:S(2)}) copy-start(s32[4]{0:T(128)S(1)} %pad_add_fusion.pos.refs_0_) | copy-start | bytes 52
  6.5 22.2 %copy-start.21 = (s32[12,4]{0,1:T(4,128)S(1)}, s32[12,4]{0,1:T(4,128)}, u32[]{:S(2)}) copy-start(s32[12,4]{0,1:T(4,128)} %param.10) | copy-start | bytes 580
  6.5 22.9 %copy-start.22 = (s32[12,4]{0,1:T(4,128)S(1)}, s32[12,4]{0,1:T(4,128)}, u32[]{:S(2)}) copy-start(s32[12,4]{0,1:T(4,128)} %param.11) | copy-start | bytes 580
  7.0 2.6 %collective-permute-start.2 = (bf16[16,256]{1,0:T(8,128)(2,1)S(1)}, bf16[16,256]{1,0:T(8,128)(2,1)S(1)}, u32[]{:S(2)}, u32[]{:S(2)}) collective-permute-start(bf16[16,256]{1,0:T(8,128)(2,1)S(1)} %get-tuple-element.40), channel_id=1, source_target_pairs={{0,8},{1,9},{2,10},{3,11},{4,12},{5,13},{6,14},{7,15},{16,24},{17,... | collective-permute-start | bytes 24584 | tf_op jit(solution)/shard_map/ppermute | solution.py:532
  8.3 1.3 collective-permute-start.3
  11.2 0.7 copy-start.8
  11.9 35.4 %all-to-all-start = ((bf16[16,80,256]{2,1,0:T(8,128)(2,1)}), bf16[16,80,256]{2,1,0:T(8,128)(2,1)S(1)}, u32[]{:S(2)}, u32[]{:S(2)}) async-start(bf16[16,80,256]{2,1,0:T(8,128)(2,1)} %get-tuple-element.46), calls=%async_computation | async-start | bytes 1310720 | tf_op jit(solution)/shard_map/all_to_all | solution.py:415
  24.9 8.0 %collective-permute-start.4 = (bf16[96,256]{1,0:T(8,128)(2,1)S(1)}, bf16[96,256]{1,0:T(8,128)(2,1)S(1)}, u32[]{:S(2)}, u32[]{:S(2)}) collective-permute-start(bf16[96,256]{1,0:T(8,128)(2,1)S(1)} %get-tuple-element.43), channel_id=1, source_target_pairs={{0,8},{1,9},{2,10},{3,11},{4,12},{5,13},{6,14},{7,15},{16,24},{17,... | collective-permute-start | bytes 147464 | tf_op jit(solution)/shard_map/ppermute | solution.py:547
  28.0 4.9 %collective-permute-start.5 = (bf16[96,256]{1,0:T(8,128)(2,1)S(1)}, bf16[96,256]{1,0:T(8,128)(2,1)S(1)}, u32[]{:S(2)}, u32[]{:S(2)}) collective-permute-start(bf16[96,256]{1,0:T(8,128)(2,1)S(1)} %get-tuple-element.44), channel_id=1, source_target_pairs={{8,16},{9,17},{10,18},{11,19},{12,20},{13,21},{14,22},{15,23},{24,... | collective-permute-start | bytes 147464 | tf_op jit(solution)/shard_map/ppermute | solution.py:547
  47.3 0.9 copy-start.7
  48.2 0.9 copy-start.9
  49.1 0.6 copy-start.15
  49.8 24.7 %copy-start = (bf16[3,3,256,256]{3,2,1,0:T(8,128)(2,1)S(1)}, bf16[3,3,256,256]{3,2,1,0:T(8,128)(2,1)}, u32[]{:S(2)}) copy-start(bf16[3,3,256,256]{3,2,1,0:T(8,128)(2,1)} %kernel.8) | copy-start | bytes 3538948
  49.8 24.7 %copy-start.18 = (bf16[64,1024]{1,0:T(8,128)(2,1)S(1)}, bf16[64,1024]{1,0:T(8,128)(2,1)}, u32[]{:S(2)}) copy-start(bf16[64,1024]{1,0:T(8,128)(2,1)} %get-tuple-element.52.pick) | copy-start | bytes 393220
  49.8 24.7 %copy-start.19 = (bf16[3,1,8,8,256]{4,3,2,1,0:T(8,128)(2,1)S(1)}, bf16[3,1,8,8,256]{4,3,2,1,0:T(8,128)(2,1)}, u32[]{:S(2)}) copy-start(bf16[3,1,8,8,256]{4,3,2,1,0:T(8,128)(2,1)} %param.7) | copy-start | bytes 294916
  51.6 22.9 %copy-start.4 = (f32[480,256]{1,0:T(8,128)}, f32[480,256]{1,0:T(8,128)S(1)}, u32[]{:S(2)}) copy-start(f32[480,256]{1,0:T(8,128)S(1)} %get-tuple-element.61.pre) | copy-start | bytes 1474564
  76.1 7.8 %copy-start.12 = (bf16[384,256]{1,0:T(8,128)(2,1)}, bf16[384,256]{1,0:T(8,128)(2,1)S(1)}, u32[]{:S(2)}) copy-start(bf16[384,256]{1,0:T(8,128)(2,1)S(1)} %get-tuple-element.68.refs_2_) | copy-start | bytes 589828
  76.1 5.9 %collective-permute-start.7 = (bf16[192,256]{1,0:T(8,128)(2,1)S(1)}, bf16[192,256]{1,0:T(8,128)(2,1)S(1)}, u32[]{:S(2)}, u32[]{:S(2)}) collective-permute-start(bf16[192,256]{1,0:T(8,128)(2,1)S(1)} %get-tuple-element.53.own), channel_id=1, source_target_pairs={{1,2},{3,4},{5,6},{9,10},{11,12},{13,14},{17,18},{19,20},{21,22},{... | collective-permute-start | bytes 294920 | tf_op jit(solution)/shard_map/ppermute | solution.py:531
  78.1 4.0 %collective-permute-start.6 = (bf16[192,256]{1,0:T(8,128)(2,1)S(1)}, bf16[192,256]{1,0:T(8,128)(2,1)S(1)}, u32[]{:S(2)}, u32[]{:S(2)}) collective-permute-start(bf16[192,256]{1,0:T(8,128)(2,1)S(1)} %get-tuple-element.53.own), channel_id=1, source_target_pairs={{0,1},{1,0},{2,3},{3,2},{4,5},{5,4},{6,7},{7,6},{8,9},{9,8},{10,11... | collective-permute-start | bytes 294920 | tf_op jit(solution)/shard_map/ppermute | solution.py:530
  78.2 2.7 %collective-permute-start.8 = (bf16[16,256]{1,0:T(8,128)(2,1)S(1)}, bf16[16,256]{1,0:T(8,128)(2,1)S(1)}, u32[]{:S(2)}, u32[]{:S(2)}) collective-permute-start(bf16[16,256]{1,0:T(8,128)(2,1)S(1)} %get-tuple-element.54), channel_id=1, source_target_pairs={{0,8},{1,9},{2,10},{3,11},{4,12},{5,13},{6,14},{7,15},{16,24},{17,... | collective-permute-start | bytes 24584 | tf_op jit(solution)/shard_map/ppermute | solution.py:532
  79.9 14.6 %copy-start.16 = (s32[4]{0:T(128)S(1)}, s32[4]{0:T(128)}, u32[]{:S(2)}) copy-start(s32[4]{0:T(128)} %copy-done.14) | copy-start | bytes 52
  79.9 1.0 collective-permute-start.9
  83.9 0.7 copy-start.10
  84.6 24.5 %all-to-all-start.2 = ((bf16[16,64,256]{2,1,0:T(8,128)(2,1)}), bf16[16,64,256]{2,1,0:T(8,128)(2,1)S(1)}, u32[]{:S(2)}, u32[]{:S(2)}) async-start(bf16[16,64,256]{2,1,0:T(8,128)(2,1)} %get-tuple-element.59), calls=%async_computation.2 | async-start | bytes 1048576 | tf_op jit(solution)/shard_map/all_to_all | solution.py:415
  90.0 8.6 %collective-permute-start.10 = (bf16[96,256]{1,0:T(8,128)(2,1)S(1)}, bf16[96,256]{1,0:T(8,128)(2,1)S(1)}, u32[]{:S(2)}, u32[]{:S(2)}) collective-permute-start(bf16[96,256]{1,0:T(8,128)(2,1)S(1)} %get-tuple-element.57), channel_id=1, source_target_pairs={{0,8},{1,9},{2,10},{3,11},{4,12},{5,13},{6,14},{7,15},{16,24},{17,... | collective-permute-start | bytes 147464 | tf_op jit(solution)/shard_map/ppermute | solution.py:580
  93.8 4.9 %collective-permute-start.11 = (bf16[96,256]{1,0:T(8,128)(2,1)S(1)}, bf16[96,256]{1,0:T(8,128)(2,1)S(1)}, u32[]{:S(2)}, u32[]{:S(2)}) collective-permute-start(bf16[96,256]{1,0:T(8,128)(2,1)S(1)} %get-tuple-element.58), channel_id=1, source_target_pairs={{8,16},{9,17},{10,18},{11,19},{12,20},{13,21},{14,22},{15,23},{24,... | collective-permute-start | bytes 147464 | tf_op jit(solution)/shard_map/ppermute | solution.py:580
  94.4 0.9 copy-start.13
  97.6 1.0 copy-start.2
  98.6 16.1 %collective-permute-start.13 = (bf16[16,72,256]{2,1,0:T(8,128)(2,1)}, bf16[16,72,256]{2,1,0:T(8,128)(2,1)}, u32[]{:S(2)}, u32[]{:S(2)}) collective-permute-start(bf16[16,72,256]{2,1,0:T(8,128)(2,1)} %get-tuple-element.70), channel_id=1, source_target_pairs={{0,1},{1,0},{2,3},{3,2},{4,5},{5,4},{6,7},{7,6},{8,9},{9,8},{10,11... | collective-permute-start | bytes 1769480 | tf_op jit(solution)/shard_map/ppermute | solution.py:605
  98.6 0.9 copy-start.11
  109.1 1.0 copy-start.5
  110.1 0.9 copy-start.17
  111.0 5.7 %copy-start.3 = (f32[16,72,256]{2,1,0:T(8,128)S(1)}, f32[16,72,256]{2,1,0:T(8,128)}, u32[]{:S(2)}) copy-start(f32[16,72,256]{2,1,0:T(8,128)} %copy-done.2) | copy-start | bytes 3538948
  114.6 2.1 %collective-permute-start.12 = (bf16[16,72,256]{2,1,0:T(8,128)(2,1)S(1)}, bf16[16,72,256]{2,1,0:T(8,128)(2,1)S(1)}, u32[]{:S(2)}, u32[]{:S(2)}) collective-permute-start(bf16[16,72,256]{2,1,0:T(8,128)(2,1)S(1)} %get-tuple-element.66), channel_id=1, source_target_pairs={{0,1},{1,0},{2,3},{3,2},{4,5},{5,4},{6,7},{7,6},{8,9},{9,8},{10,11... | collective-permute-start | bytes 1769480 | tf_op jit(solution)/shard_map/ppermute | solution.py:618
  166.6 22.4 %copy-start.20 = (bf16[96,384]{1,0:T(8,128)(2,1)S(1)}, bf16[96,384]{1,0:T(8,128)(2,1)}, u32[]{:S(2)}) copy-start(bf16[96,384]{1,0:T(8,128)(2,1)} %get-tuple-element.72.pick) | copy-start | bytes 221188
  183.6 11.9 %collective-permute-start.15 = (bf16[16,144,256]{2,1,0:T(8,128)(2,1)S(1)}, bf16[16,144,256]{2,1,0:T(8,128)(2,1)S(1)}, u32[]{:S(2)}, u32[]{:S(2)}) collective-permute-start(bf16[16,144,256]{2,1,0:T(8,128)(2,1)S(1)} %all_to_all.33.mine), channel_id=1, source_target_pairs={{0,1},{1,0},{2,3},{3,2},{4,5},{5,4},{6,7},{7,6},{8,9},{9,8},{10,11... | collective-permute-start | bytes 3538952 | tf_op jit(solution)/shard_map/ppermute | solution.py:636
  189.7 4.5 %collective-permute-start.14 = (bf16[48,256]{1,0:T(8,128)(2,1)S(1)}, bf16[48,256]{1,0:T(8,128)(2,1)S(1)}, u32[]{:S(2)}, u32[]{:S(2)}) collective-permute-start(bf16[48,256]{1,0:T(8,128)(2,1)S(1)} %get-tuple-element.74), channel_id=1, source_target_pairs={{0,7},{1,6},{2,5},{3,4},{4,3},{5,2},{6,1},{7,0},{8,15},{9,14},{10,... | collective-permute-start | bytes 73736 | tf_op jit(solution)/shard_map/ppermute | solution.py:625

commit v9 on v8

--- a/solution.py
+++ b/solution.py
@@ -27,15 +27,17 @@
 EVEN_ROWS = swap_pairs([(r * 8 + c, r * 8 + 8 + c) for r in (0, 2, 4, 6) for c in range(8)])
 ODD_ROWS = swap_pairs([(r * 8 + c, r * 8 + 8 + c) for r in (1, 3, 5) for c in range(8)])
 NEAR_ROWS = swap_pairs([(r * 8 + c, r * 8 + 8 + c) for r in (1, 5) for c in range(8)])
+SPARE = (19, 20, 43, 44)
 
 
 def seam_groups():
     groups = []
     for t in range(64):
         row, col = divmod(t, 8)
-        if row < 4 and col < 4 and (min(row, col) == 0 or row == col == 1):
+        if row < 4 and col < 4 and min(row, col) == 0:
             groups.append([f * 64 + (t ^ m) for f in range(4) for m in MIRRORS])
-    inner = [t for t in range(64) if 0 < t // 8 < 7 and 0 < t % 8 < 7 and t not in (9, 14, 49, 54)]
+    inner = [t for t in range(64) if 0 < t // 8 < 7 and 0 < t % 8 < 7 and t not in SPARE]
+    groups.append([f * 64 + t for f in range(4) for t in SPARE])
     for f in range(4):
         groups.append([f * 64 + t for t in inner if t < 32])
         groups.append([f * 64 + t for t in inner if t >= 32])
@@ -52,16 +54,36 @@
 ACROSS_GROUPS = [[f * 64 + (t ^ m) for f in range(4) for m in (0, 56)] for t in range(32)]
 
 
-def run(kernel, outs, scratch, pos, *args):
+def run(kernel, outs, scratch, pos, *args, taps=None):
     vmem = pl.BlockSpec(memory_space=pltpu.VMEM)
+    in_specs = [pl.BlockSpec(memory_space=pltpu.SMEM)] + [vmem] * len(args)
+    scratch = [pltpu.VMEM(shape, dtype) for shape, dtype in scratch]
+    operands = (pos,) + args
+    inner = kernel
+    if taps is not None:
+        in_specs = in_specs + [pl.BlockSpec(memory_space=pl.ANY)]
+        scratch = scratch + [pltpu.VMEM(taps.shape, taps.dtype), pltpu.SemaphoreType.DMA(())]
+        operands = operands + (taps,)
+
+        def inner(*refs):
+            source, held, sem = refs[len(args) + 1], refs[-2], refs[-1]
+            copy = pltpu.make_async_copy(source, held, sem)
+            copy.start()
+
+            def fetched():
+                copy.wait()
+                return held
+
+            kernel(*refs[: len(args) + 1], fetched, *refs[len(args) + 2 : -2])
+
     return pl.pallas_call(
-        kernel,
+        inner,
         out_shape=[jax.ShapeDtypeStruct(shape, dtype) for shape, dtype in outs],
-        in_specs=[pl.BlockSpec(memory_space=pltpu.SMEM)] + [vmem] * len(args),
+        in_specs=in_specs,
         out_specs=[vmem] * len(outs),
-        scratch_shapes=[pltpu.VMEM(shape, dtype) for shape, dtype in scratch],
+        scratch_shapes=scratch,
         compiler_params=pltpu.CompilerParams(vmem_limit_bytes=24 * 2**20),
-    )(pos, *args)
+    )(*operands)
 
 
 def slope_of(v):
@@ -195,11 +217,12 @@
     post_strips(strips, send)
 
 
-def rim_kernel(pos, own, swapped, odd, end_one, end_two, kernel, wide, first, second, send, cells, ends, lines, strips):
+def rim_kernel(pos, own, swapped, odd, end_one, end_two, fetched, wide, first, second, send, cells, ends, lines, strips):
     row, col = pos[0], pos[1]
     lines[...] = jnp.zeros_like(lines)
     widen(pos, own, swapped, odd, end_one, end_two, wide, first, second, cells, ends, lines, PITCH)
     bottom, right = 2 * (row // 4), 2 * (col // 4)
+    kernel = fetched()
     totals = []
     for kind in range(2):
         total = None
@@ -234,13 +257,13 @@
     cells[36 * PITCH :, :] = jnp.zeros((8, C), F32)
 
 
-def one_kernel(pos, wide, first, second, got, pick, kernel, filled, pre, hidden, send, cells, shifts, strips, lines):
+def one_kernel(pos, wide, first, second, got, pick, fetched, filled, pre, hidden, send, cells, shifts, strips, lines):
     row, col = pos[0], pos[1]
     lines[...] = dot(pick[...], got[...], ((1,), (0,)))
     stack_lines(row, wide, first, second, cells)
     fill_strips(cells, lines, row, col, 12, 1, 10, 12)
     filled[...] = cells[0 : 36 * PITCH, :].astype(BF16)
-    total = convolve(cells, shifts, 12, 10, 0, kernel, False)
+    total = convolve(cells, shifts, 12, 10, 0, fetched(), False)
     pre[...] = total
     inside = cell_mask(row, col)
     for f in range(3):
@@ -253,7 +276,7 @@
 
 
 def two_kernel(
-    pos, hidden, got, pick, kernel, cotangent, filled, delta, wide_delta, first, second, cells, shifts, lines, ends
+    pos, hidden, got, pick, cotangent, fetched, filled, delta, wide_delta, first, second, cells, shifts, lines, ends
 ):
     row, col = pos[0], pos[1]
     lines[...] = dot(pick[...], got[...], ((1,), (0,)))
@@ -261,7 +284,7 @@
     cells[30 * PITCH :, :] = jnp.zeros((8, C), F32)
     fill_strips(cells, lines, row, col, 10, 0, 9, 10)
     filled[...] = cells[0 : 30 * PITCH, :].astype(BF16)
-    total = convolve(cells, shifts, 10, 8, 0, kernel, False).reshape(24, PITCH, C)[:, 0:8, :]
+    total = convolve(cells, shifts, 10, 8, 0, fetched(), False).reshape(24, PITCH, C)[:, 0:8, :]
     product = cotangent[...].astype(F32).reshape(24, 8, C) * slope_of(total)
     delta[...] = product.reshape(192, C).astype(BF16)
     padded = jnp.concatenate([product, jnp.zeros((24, 8, C), F32)], axis=1)
@@ -270,12 +293,12 @@
     post_ends(row, col, cells, first, second, ends)
 
 
-def back_kernel(pos, wide, first, second, kernel, back, cells, shifts):
+def back_kernel(pos, wide, first, second, fetched, back, cells, shifts):
     stack_lines(pos[0], wide, first, second, cells)
-    back[...] = convolve(cells, shifts, 12, 10, 0, kernel, True).astype(BF16)
-
-
-def delta_kernel(pos, back, got, pick, pre, kernel, wide_delta, own, send, cells, grads, shifts, strips, lines):
+    back[...] = convolve(cells, shifts, 12, 10, 0, fetched(), True).astype(BF16)
+
+
+def delta_kernel(pos, back, got, pick, pre, fetched, wide_delta, own, send, cells, grads, shifts, strips, lines):
     row, col = pos[0], pos[1]
     lines[...] = dot(pick[...], got[...], ((1,), (0,)))
     grads[...] = back[...].astype(F32)
@@ -308,7 +331,7 @@
         begin = (f * 12 + 2) * PITCH + 2
         mine = jnp.where(at < 8, cells[begin : begin + 8 * PITCH, :], 0.0)
         wide_delta[f * 8 * PITCH : (f + 1) * 8 * PITCH, :] = mine.astype(BF16)
-    total = convolve(cells, shifts, 12, 10, 0, kernel, True)
+    total = convolve(cells, shifts, 12, 10, 0, fetched(), True)
     grads[...] = total
     take_strips(grads, strips, row, col, 10, 0, 9, 1, 8)
     send[...] = strips[...].astype(BF16)
@@ -430,7 +453,7 @@
         rel = 2 * opposite + reverse if kind == 0 else 2 * reverse + opposite
         return nexts[face, side], rel, reverse
 
-    for length, block, out in ((12, 80, pick_12), (10, 64, pick_10)):
+    for length, block, out in ((12, 72, pick_12), (10, 64, pick_10)):
         rows = out.shape[0]
         at_row = lax.broadcasted_iota(jnp.int32, (rows, 128), 0)
         lane = lax.broadcasted_iota(jnp.int32, (rows, 128), 1)
@@ -507,7 +530,7 @@
 def seam_picks(pos, nexts, codes):
     return pl.pallas_call(
         picks_kernel,
-        out_shape=[jax.ShapeDtypeStruct(shape, BF16) for shape in ((80, 1280), (64, 1024), (64, 1024), (96, 384))],
+        out_shape=[jax.ShapeDtypeStruct(shape, BF16) for shape in ((80, 1152), (64, 1024), (64, 1024), (96, 384))],
         in_specs=[pl.BlockSpec(memory_space=pltpu.SMEM)] * 3,
         out_specs=[pl.BlockSpec(memory_space=pltpu.VMEM)] * 4,
     )(pos, nexts, codes)
@@ -537,8 +560,8 @@
     first, second = run(ends_kernel, ends, [((192, C), F32), ((32, C), F32)], pos, x)
     wide, first, second, send = run(
         input_kernel,
-        regions + [((16, 80, C), BF16)],
-        [((24, PITCH, C), F32), ((32, C), F32), ((80, C), F32)],
+        regions + [((16, 72, C), BF16)],
+        [((24, PITCH, C), F32), ((32, C), F32), ((72, C), F32)],
         pos,
         *beside(x, first, second),
     )
@@ -555,7 +578,7 @@
         second,
         seam_exchange(send),
         pick_12,
-        kernel_one,
+        taps=kernel_one,
     )
     filled_hidden, delta, wide_two, first, second = run(
         two_kernel,
@@ -565,8 +588,8 @@
         hidden,
         seam_exchange(send),
         pick_10,
-        kernel_two,
         cotangent.reshape(192, C),
+        taps=kernel_two,
     )
     wide, first, second, send = run(
         rim_kernel,
@@ -574,7 +597,7 @@
         [((24, PITCH, C), F32), ((32, C), F32), ((6 * PITCH + 8, C), F32), ((64, C), F32)],
         pos,
         *beside(delta, first, second),
-        kernel_two,
+        taps=kernel_two,
     )
     got = seam_exchange(send)
     first, second = lax.ppermute(first, TILE, EVEN_ROWS), lax.ppermute(second, TILE, ODD_ROWS)
@@ -586,7 +609,7 @@
         wide,
         first,
         second,
-        kernel_two,
+        taps=kernel_two,
     )[0]
     pieces = [((16, 72, C), F32), ((16, 72, C), BF16)]
 
@@ -612,7 +635,7 @@
         got,
         add_10,
         pre_one,
-        kernel_one,
+        taps=kernel_one,
     )
     keep_one, payload_one = grad_of(12, 1, 1, filled_in, wide_one)
     got_one = lax.ppermute(payload_one, "core", CORES)
@@ -633,6 +656,7 @@
         mirrored,
     )[0]
     part = lax.all_to_all(part, AXES, 0, 0, axis_index_groups=PLANE_GROUPS)
+    part, input_grad = lax.optimization_barrier((part, input_grad))
     got = lax.ppermute(part, "core", CORES)
     grads = pl.pallas_call(
         place_kernel,

time: 202 us -> 201 us (level)
  blocking collectives: 87.1 us -> 71.9 us
  waiting for transfers between devices: 30.7 us -> 40.9 us
  Pallas kernels: 25 us -> 27.6 us
  starting transfers between devices: 43.9 us -> 46.4 us
    all_to_all x2 -> x1, blocking collectives: 39.3 us -> 22.9 us  [body(): part = lax.all_to_all(part, AXES, 0, 0, axis_index_groups=PLANE_GROUPS)]
    ppermute x1, starting transfers between devices: 0.52 us -> 7.32 us  [body(): mirrored = lax.ppermute(mirrored, TILE, [(t, t ^ 7) for t in range(64)])]
    ppermute x1, waiting for transfers between devices: 4.02 us -> 8.84 us  [body(): mirrored = lax.ppermute(mirrored, TILE, [(t, t ^ 7) for t in range(64)])]
    ppermute x2, starting transfers between devices: 6.84 us -> 2.2 us  [body(): lax.ppermute(first, TILE, EVEN_ROWS)]
    all_to_all x0 -> x1, starting transfers between devices: none -> 3.83 us  [body(): part = lax.all_to_all(part, AXES, 0, 0, axis_index_groups=PLANE_GROUPS)]
    ppermute x1, starting transfers between devices: 5.42 us -> 2.25 us  [body(): got = lax.ppermute(part, 'core', CORES)]
    pallas_call x14, Pallas kernels: 19.2 us -> 21.7 us  [run(): pl.pallas_call(inner, out_shape=[jax.ShapeDtypeStruct(shape, dtype) for s...]
    ppermute x1, waiting for transfers between devices: 0.01 us -> 2.47 us  [body(): got = lax.ppermute(part, 'core', CORES)]
  transfers between devices with their start and end apart: 18 -> 19, of which waited for: 7 -> 8; matrix products, arithmetic and copies ran while one was open for 1% -> 1% of each run, Pallas kernels for 6% -> 7%
where the time goes in v9:
time: 201 us; the launch traced here: 199 us
  blocking collectives  71.9 us (36%)
  starting transfers between devices  46.4 us (23%)
  waiting for transfers between devices  40.9 us (20%)
  Pallas kernels  27.6 us (14%)
  local copies, waits for them, and re-layouts  10.9 us (5%)
    all_to_all x1, blocking collectives, body(): got = lax.all_to_all(part, AXES, 0, 0, axis_index_groups=ACROSS_GROUPS)  25.9 us
    all_to_all x2, waiting for transfers between devices, seam_exchange(): got = lax.all_to_all(send, AXES, 0, 0, axis_index_groups=SEAM_GROUPS)  23.8 us
    all_to_all x1, blocking collectives, seam_exchange(): got = lax.all_to_all(send, AXES, 0, 0, axis_index_groups=SEAM_GROUPS)  23.1 us
    all_to_all x1, blocking collectives, body(): part = lax.all_to_all(part, AXES, 0, 0, axis_index_groups=PLANE_GROUPS)  22.9 us
    pallas_call x14, Pallas kernels, run(): pl.pallas_call(inner, out_shape=[jax.ShapeDtypeStruct(shape, dtype) for s...  21.7 us
    all_to_all x2, starting transfers between devices, seam_exchange(): got = lax.all_to_all(send, AXES, 0, 0, axis_index_groups=SEAM_GROUPS)  17.9 us
    unnamed x46, local copies, waits for them, and re-layouts  9.51 us
    ppermute x1, waiting for transfers between devices, body(): mirrored = lax.ppermute(mirrored, TILE, [(t, t ^ 7) for t in range(64)])  8.84 us
  transfers between devices with their start and end apart: 19, of which 8 were waited for; matrix products, arithmetic and copies ran while one was open for 1% of the time, Pallas kernels for 7%

profile of v9, /device:TPU:1, one launch (start us, length us, event | category | flops | bytes accessed | tf_op | source)
XLA Modules:
  0.0 198.9 jit_solution(355903285006271825)
XLA Ops:
  0.6 4.7 %collective-permute-start.1 = (bf16[192,256]{1,0:T(8,128)(2,1)}, bf16[192,256]{1,0:T(8,128)(2,1)S(1)}, u32[]{:S(2)}, u32[]{:S(2)}) collective-permute-start(bf16[192,256]{1,0:T(8,128)(2,1)} %bitcast.17), channel_id=1, source_target_pairs={{1,2},{3,4},{5,6},{9,10},{11,12},{13,14},{17,18},{19,20},{21,22},{... | collective-permute-start | bytes 294920 | tf_op jit(solution)/shard_map/ppermute | solution.py:554
  5.6 0.9 copy-done.6
  7.0 1.3 collective-permute-start.2
  9.6 1.6 shard_map.86
  11.2 0.7 copy-done.7
  11.9 13.0 %all-to-all-start = ((bf16[16,72,256]{2,1,0:T(8,128)(2,1)}), bf16[16,72,256]{2,1,0:T(8,128)(2,1)S(1)}, u32[]{:S(2)}, u32[]{:S(2)}) async-start(bf16[16,72,256]{2,1,0:T(8,128)(2,1)} %get-tuple-element.48), calls=%async_computation | async-start | bytes 1179648 | tf_op jit(solution)/shard_map/all_to_all | solution.py:438
  25.0 0.7 collective-permute-start.5
  25.6 0.7 copy.9.nexts
  26.3 0.7 copy.10.codes
  27.0 2.8 %shard_map.87 = (bf16[80,1152]{1,0:T(8,128)(2,1)}, bf16[64,1024]{1,0:T(8,128)(2,1)}, bf16[64,1024]{1,0:T(8,128)(2,1)}, bf16[96,384]{1,0:T(8,128)(2,1)}) custom-call(s32[4]{0:T(128)} %copy-done.14, s32[12,4]{1,0:T(8,128)} %copy.9.nexts, s32[12,4]{1,0:T(8,128)} %copy.10.codes), custom_call_target="tpu_custom_call" | custom-call | tf_op jit(solution)/shard_map/pallas_call | solution.py:531
  29.8 16.1 %all-to-all-done = bf16[16,72,256]{2,1,0:T(8,128)(2,1)S(1)} async-done(((bf16[16,72,256]{2,1,0:T(8,128)(2,1)}), bf16[16,72,256]{2,1,0:T(8,128)(2,1)S(1)}, u32[]{:S(2)}, u32[]{:S(2)}) %all-to-all-start) | async-done | bytes 589856 | tf_op jit(solution)/shard_map/all_to_all | solution.py:438
  45.9 0.9 copy-done.8
  46.9 0.9 copy-done.13
  48.4 2.1 %shard_map.88 = (bf16[576,256]{1,0:T(8,128)(2,1)S(1)}, f32[480,256]{1,0:T(8,128)S(1)}, bf16[480,256]{1,0:T(8,128)(2,1)S(1)}, bf16[16,64,256]{2,1,0:T(8,128)(2,1)S(1)}) custom-call(s32[4]{0:T(128)S(1)} %copy-done.15, bf16[384,256]{1,0:T(8,128)(2,1)S(1)} %copy-done.8, bf16[96,256]{1,0:T(8,128)(2,1)S(1)} %collective-permute-done.4.refs_2_, ...), custom_call_target="tpu_custom_call" | custom-call | tf_op jit(solution)/shard_map/pallas_call | solution.py:79
  50.5 23.1 %all_to_all.30 = bf16[16,64,256]{2,1,0:T(8,128)(2,1)S(1)} all-to-all(bf16[16,64,256]{2,1,0:T(8,128)(2,1)S(1)} %get-tuple-element.54), channel_id=1, replica_groups={{0,7,56,63,64,71,120,127,128,135,184,191,192,199,248,255},{1,6,57,62,65..., dimensions={0} | all-to-all | bytes 1048576 | tf_op jit(solution)/shard_map/all_to_all | solution.py:438
  73.6 1.9 shard_map.89
  75.5 1.9 collective-permute-start.7
  78.3 1.8 collective-permute-done.8.refs_4_
  80.2 1.3 collective-permute-done.7.refs_3_
  81.5 2.2 %shard_map.90 = (bf16[384,256]{1,0:T(8,128)(2,1)S(1)}, bf16[96,256]{1,0:T(8,128)(2,1)S(1)}, bf16[96,256]{1,0:T(8,128)(2,1)S(1)}, bf16[16,64,256]{2,1,0:T(8,128)(2,1)}) custom-call(s32[4]{0:T(128)S(1)} %copy-done.15, bf16[192,256]{1,0:T(8,128)(2,1)S(1)} %get-tuple-element.56.refs_1_, bf16[192,256]{1,0:T(8,128)(2,1)S(1)} %collective-permute-done.6.refs_2_, ...), custom_call_target="tpu_custom_call" | custom-call | tf_op jit(solution)/shard_map/pallas_call | solution.py:79
  83.7 0.7 copy-done.9
  84.3 4.9 %all-to-all-start.2 = ((bf16[16,64,256]{2,1,0:T(8,128)(2,1)}), bf16[16,64,256]{2,1,0:T(8,128)(2,1)S(1)}, u32[]{:S(2)}, u32[]{:S(2)}) async-start(bf16[16,64,256]{2,1,0:T(8,128)(2,1)} %get-tuple-element.62), calls=%async_computation.2 | async-start | bytes 1048576 | tf_op jit(solution)/shard_map/all_to_all | solution.py:438
  89.2 2.1 %collective-permute-start.10 = (bf16[96,256]{1,0:T(8,128)(2,1)S(1)}, bf16[96,256]{1,0:T(8,128)(2,1)S(1)}, u32[]{:S(2)}, u32[]{:S(2)}) collective-permute-start(bf16[96,256]{1,0:T(8,128)(2,1)S(1)} %get-tuple-element.60), channel_id=1, source_target_pairs={{0,8},{1,9},{2,10},{3,11},{4,12},{5,13},{6,14},{7,15},{16,24},{17,... | collective-permute-start | bytes 147464 | tf_op jit(solution)/shard_map/ppermute | solution.py:603
  92.0 0.9 copy-done.12
  92.9 2.2 %shard_map.94 = (f32[16,72,256]{2,1,0:T(8,128)S(1)}, bf16[16,72,256]{2,1,0:T(8,128)(2,1)}) custom-call(s32[4]{0:T(128)S(1)} %copy-done.16, bf16[480,256]{1,0:T(8,128)(2,1)S(1)} %get-tuple-element.68.refs_1_, bf16[384,256]{1,0:T(8,128)(2,1)S(1)} %copy-done.12), custom_call_target="tpu_custom_call" | custom-call | tf_op jit(solution)/shard_map/pallas_call | solution.py:79
  95.2 1.0 copy-done.2
  96.2 2.0 collective-permute-start.13
  98.2 0.9 copy-done.10
  99.1 1.6 shard_map.91.refs_1_
  100.7 7.7 %all-to-all-done.2 = bf16[16,64,256]{2,1,0:T(8,128)(2,1)S(1)} async-done(((bf16[16,64,256]{2,1,0:T(8,128)(2,1)}), bf16[16,64,256]{2,1,0:T(8,128)(2,1)S(1)}, u32[]{:S(2)}, u32[]{:S(2)}) %all-to-all-start.2) | async-done | bytes 524320 | tf_op jit(solution)/shard_map/all_to_all | solution.py:438
  108.4 1.0 copy-done.5
  109.5 0.9 copy-done.17
  110.4 2.5 %shard_map.92 = (bf16[384,256]{1,0:T(8,128)(2,1)S(1)}, bf16[192,256]{1,0:T(8,128)(2,1)S(1)}, bf16[48,256]{1,0:T(8,128)(2,1)S(1)}) custom-call(s32[4]{0:T(128)S(1)} %copy-done.16, bf16[480,256]{1,0:T(8,128)(2,1)S(1)} %shard_map.91.refs_1_, bf16[1024,256]{1,0:T(8,128)(2,1)S(1)} %bitcast.16, bf16[64,1024]{1,0:T(8,128)(2,1)S(1)} %copy-done.17, ...), custom_call_target="tpu_custom_call" | custom-call | tf_op jit(solution)/shard_map/pallas_call | solution.py:79
  112.9 1.4 shard_map.93
  114.5 2.0 collective-permute-done.12.got_one
  116.5 1.3 shard_map.95
  117.8 22.9 %all_to_all.31.parts = bf16[16,144,256]{2,1,0:T(8,128)(2,1)S(1)} all-to-all(bf16[16,144,256]{2,1,0:T(8,128)(2,1)S(1)} %shard_map.95), channel_id=1, replica_groups={{0,8,16,24,2,10,18,26,4,12,20,28,6,14,22,30},{1,9,17,25,3,11,19,27,5,13..., dimensions={0} | all-to-all | bytes 2359296 | tf_op jit(solution)/shard_map/all_to_all | solution.py:643
  140.7 0.7 shard_map.96
  141.4 25.9 %all_to_all.32.parts.got = bf16[8,192,256]{2,1,0:T(8,128)(2,1)S(1)} all-to-all(bf16[8,192,256]{2,1,0:T(8,128)(2,1)S(1)} %shard_map.96), channel_id=1, replica_groups={{0,56,64,120,128,184,192,248},{1,57,65,121,129,185,193,249},{2,58,66,12..., dimensions={0} | all-to-all | bytes 1572864 | tf_op jit(solution)/shard_map/all_to_all | solution.py:645
  167.3 1.6 shard_map.97
  168.9 3.8 %all-to-all-start.5 = ((bf16[16,144,256]{2,1,0:T(8,128)(2,1)}), bf16[16,144,256]{2,1,0:T(8,128)(2,1)S(1)}, u32[]{:S(2)}, u32[]{:S(2)}) async-start(bf16[16,144,256]{2,1,0:T(8,128)(2,1)} %shard_map.97), calls=%async_computation.5 | async-start | bytes 2359296 | tf_op jit(solution)/shard_map/all_to_all | solution.py:658
  172.8 0.7 shard_map.98
  173.5 7.3 %collective-permute-start.14 = (bf16[48,256]{1,0:T(8,128)(2,1)S(1)}, bf16[48,256]{1,0:T(8,128)(2,1)S(1)}, u32[]{:S(2)}, u32[]{:S(2)}) collective-permute-start(bf16[48,256]{1,0:T(8,128)(2,1)S(1)} %get-tuple-element.76), channel_id=1, source_target_pairs={{0,7},{1,6},{2,5},{3,4},{4,3},{5,2},{6,1},{7,0},{8,15},{9,14},{10,... | collective-permute-start | bytes 73736 | tf_op jit(solution)/shard_map/ppermute | solution.py:648
  180.8 8.8 %collective-permute-done.14.two = bf16[48,256]{1,0:T(8,128)(2,1)S(1)} collective-permute-done((bf16[48,256]{1,0:T(8,128)(2,1)S(1)}, bf16[48,256]{1,0:T(8,128)(2,1)S(1)}, u32[]{:S(2)}, u32[]{:S(2)}) %collective-permute-start.14) | collective-permute-done | bytes 24608 | tf_op jit(solution)/shard_map/ppermute | solution.py:648
  189.7 1.3 shard_map.99
  190.9 2.3 %collective-permute-start.15 = (bf16[16,144,256]{2,1,0:T(8,128)(2,1)S(1)}, bf16[16,144,256]{2,1,0:T(8,128)(2,1)S(1)}, u32[]{:S(2)}, u32[]{:S(2)}) collective-permute-start(bf16[16,144,256]{2,1,0:T(8,128)(2,1)S(1)} %all-to-all-done.5.mine), channel_id=1, source_target_pairs={{0,1},{1,0},{2,3},{3,2},{4,5},{5,4},{6,7},{7,6},{8,9},{9,8},{10,11... | collective-permute-start | bytes 3538952 | tf_op jit(solution)/shard_map/ppermute | solution.py:660
  193.2 2.5 %collective-permute-done.15.other = bf16[16,144,256]{2,1,0:T(8,128)(2,1)S(1)} collective-permute-done((bf16[16,144,256]{2,1,0:T(8,128)(2,1)S(1)}, bf16[16,144,256]{2,1,0:T(8,128)(2,1)S(1)}, u32[]{:S(2)}, u32[]{:S(2)}) %collective-permute-start.15) | collective-permute-done | bytes 1179680 | tf_op jit(solution)/shard_map/ppermute | solution.py:660
  195.6 3.1 %shard_map.100 = (f32[9,256,256]{2,1,0:T(8,128)}, f32[9,256,256]{2,1,0:T(8,128)}) custom-call(s32[4]{0:T(128)S(1)} %copy-done.16, bf16[16,144,256]{2,1,0:T(8,128)(2,1)S(1)} %all-to-all-done.5.mine, bf16[16,144,256]{2,1,0:T(8,128)(2,1)S(1)} %collective-permute-done.15.other), custom_call_target="tpu_custom_call" | custom-call | tf_op jit(solution)/shard_map/pallas_call | solution.py:661
  (58 shorter events, 4.4 us)
Async XLA Ops:
  0.6 45.3 %copy-start.1 = (bf16[3,3,256,256]{3,2,1,0:T(8,128)(2,1)S(1)}, bf16[3,3,256,256]{3,2,1,0:T(8,128)(2,1)}, u32[]{:S(2)}) copy-start(bf16[3,3,256,256]{3,2,1,0:T(8,128)(2,1)} %refs_5_.3) | copy-start | bytes 3538948
  0.6 9.0 %collective-permute-start.1 = (bf16[192,256]{1,0:T(8,128)(2,1)}, bf16[192,256]{1,0:T(8,128)(2,1)S(1)}, u32[]{:S(2)}, u32[]{:S(2)}) collective-permute-start(bf16[192,256]{1,0:T(8,128)(2,1)} %bitcast.17), channel_id=1, source_target_pairs={{1,2},{3,4},{5,6},{9,10},{11,12},{13,14},{17,18},{19,20},{21,22},{... | collective-permute-start | bytes 294920 | tf_op jit(solution)/shard_map/ppermute | solution.py:554
  5.4 4.3 %collective-permute-start = (bf16[192,256]{1,0:T(8,128)(2,1)}, bf16[192,256]{1,0:T(8,128)(2,1)S(1)}, u32[]{:S(2)}, u32[]{:S(2)}) collective-permute-start(bf16[192,256]{1,0:T(8,128)(2,1)} %bitcast.18), channel_id=1, source_target_pairs={{0,1},{1,0},{2,3},{3,2},{4,5},{5,4},{6,7},{7,6},{8,9},{9,8},{10,11... | collective-permute-start | bytes 294920 | tf_op jit(solution)/shard_map/ppermute | solution.py:553
  5.6 0.9 copy-start.6
  6.5 20.6 %copy-start.14 = (s32[4]{0:T(128)}, s32[4]{0:T(128)S(1)}, u32[]{:S(2)}) copy-start(s32[4]{0:T(128)S(1)} %pad_add_fusion.pos.refs_0_) | copy-start | bytes 52
  6.5 19.2 %copy-start.21 = (s32[12,4]{0,1:T(4,128)S(1)}, s32[12,4]{0,1:T(4,128)}, u32[]{:S(2)}) copy-start(s32[12,4]{0,1:T(4,128)} %param.10) | copy-start | bytes 580
  6.5 19.9 %copy-start.22 = (s32[12,4]{0,1:T(4,128)S(1)}, s32[12,4]{0,1:T(4,128)}, u32[]{:S(2)}) copy-start(s32[12,4]{0,1:T(4,128)} %param.11) | copy-start | bytes 580
  7.0 2.6 %collective-permute-start.2 = (bf16[16,256]{1,0:T(8,128)(2,1)S(1)}, bf16[16,256]{1,0:T(8,128)(2,1)S(1)}, u32[]{:S(2)}, u32[]{:S(2)}) collective-permute-start(bf16[16,256]{1,0:T(8,128)(2,1)S(1)} %get-tuple-element.42), channel_id=1, source_target_pairs={{0,8},{1,9},{2,10},{3,11},{4,12},{5,13},{6,14},{7,15},{16,24},{17,... | collective-permute-start | bytes 24584 | tf_op jit(solution)/shard_map/ppermute | solution.py:555
  8.3 1.3 collective-permute-start.3
  11.2 0.7 copy-start.7
  11.9 34.1 %all-to-all-start = ((bf16[16,72,256]{2,1,0:T(8,128)(2,1)}), bf16[16,72,256]{2,1,0:T(8,128)(2,1)S(1)}, u32[]{:S(2)}, u32[]{:S(2)}) async-start(bf16[16,72,256]{2,1,0:T(8,128)(2,1)} %get-tuple-element.48), calls=%async_computation | async-start | bytes 1179648 | tf_op jit(solution)/shard_map/all_to_all | solution.py:438
  24.9 5.0 %collective-permute-start.4 = (bf16[96,256]{1,0:T(8,128)(2,1)S(1)}, bf16[96,256]{1,0:T(8,128)(2,1)S(1)}, u32[]{:S(2)}, u32[]{:S(2)}) collective-permute-start(bf16[96,256]{1,0:T(8,128)(2,1)S(1)} %get-tuple-element.45), channel_id=1, source_target_pairs={{0,8},{1,9},{2,10},{3,11},{4,12},{5,13},{6,14},{7,15},{16,24},{17,... | collective-permute-start | bytes 147464 | tf_op jit(solution)/shard_map/ppermute | solution.py:570
  25.0 4.9 %collective-permute-start.5 = (bf16[96,256]{1,0:T(8,128)(2,1)S(1)}, bf16[96,256]{1,0:T(8,128)(2,1)S(1)}, u32[]{:S(2)}, u32[]{:S(2)}) collective-permute-start(bf16[96,256]{1,0:T(8,128)(2,1)S(1)} %get-tuple-element.46), channel_id=1, source_target_pairs={{8,16},{9,17},{10,18},{11,19},{12,20},{13,21},{14,22},{15,23},{24,... | collective-permute-start | bytes 147464 | tf_op jit(solution)/shard_map/ppermute | solution.py:570
  45.9 0.9 copy-start.8
  46.9 0.9 copy-start.13
  47.8 0.6 copy-start.15
  48.4 25.2 %copy-start = (bf16[3,3,256,256]{3,2,1,0:T(8,128)(2,1)S(1)}, bf16[3,3,256,256]{3,2,1,0:T(8,128)(2,1)}, u32[]{:S(2)}) copy-start(bf16[3,3,256,256]{3,2,1,0:T(8,128)(2,1)} %refs_4_.1) | copy-start | bytes 3538948
  48.4 25.2 %copy-start.18 = (bf16[64,1024]{1,0:T(8,128)(2,1)S(1)}, bf16[64,1024]{1,0:T(8,128)(2,1)}, u32[]{:S(2)}) copy-start(bf16[64,1024]{1,0:T(8,128)(2,1)} %get-tuple-element.55.refs_3_) | copy-start | bytes 393220
  48.4 25.3 %copy-start.19 = (bf16[3,1,8,8,256]{4,3,2,1,0:T(8,128)(2,1)S(1)}, bf16[3,1,8,8,256]{4,3,2,1,0:T(8,128)(2,1)}, u32[]{:S(2)}) copy-start(bf16[3,1,8,8,256]{4,3,2,1,0:T(8,128)(2,1)} %param.7) | copy-start | bytes 294916
  50.5 23.1 %copy-start.4 = (f32[480,256]{1,0:T(8,128)}, f32[480,256]{1,0:T(8,128)S(1)}, u32[]{:S(2)}) copy-start(f32[480,256]{1,0:T(8,128)S(1)} %get-tuple-element.64.refs_4_) | copy-start | bytes 1474564
  75.5 8.1 %copy-start.11 = (bf16[384,256]{1,0:T(8,128)(2,1)}, bf16[384,256]{1,0:T(8,128)(2,1)S(1)}, u32[]{:S(2)}) copy-start(bf16[384,256]{1,0:T(8,128)(2,1)S(1)} %get-tuple-element.69.refs_2_) | copy-start | bytes 589828
  75.5 5.9 %collective-permute-start.7 = (bf16[192,256]{1,0:T(8,128)(2,1)S(1)}, bf16[192,256]{1,0:T(8,128)(2,1)S(1)}, u32[]{:S(2)}, u32[]{:S(2)}) collective-permute-start(bf16[192,256]{1,0:T(8,128)(2,1)S(1)} %get-tuple-element.56.refs_1_), channel_id=1, source_target_pairs={{1,2},{3,4},{5,6},{9,10},{11,12},{13,14},{17,18},{19,20},{21,22},{... | collective-permute-start | bytes 294920 | tf_op jit(solution)/shard_map/ppermute | solution.py:554
  77.5 4.0 %collective-permute-start.6 = (bf16[192,256]{1,0:T(8,128)(2,1)S(1)}, bf16[192,256]{1,0:T(8,128)(2,1)S(1)}, u32[]{:S(2)}, u32[]{:S(2)}) collective-permute-start(bf16[192,256]{1,0:T(8,128)(2,1)S(1)} %get-tuple-element.56.refs_1_), channel_id=1, source_target_pairs={{0,1},{1,0},{2,3},{3,2},{4,5},{5,4},{6,7},{7,6},{8,9},{9,8},{10,11... | collective-permute-start | bytes 294920 | tf_op jit(solution)/shard_map/ppermute | solution.py:553
  77.6 2.6 %collective-permute-start.8 = (bf16[16,256]{1,0:T(8,128)(2,1)S(1)}, bf16[16,256]{1,0:T(8,128)(2,1)S(1)}, u32[]{:S(2)}, u32[]{:S(2)}) collective-permute-start(bf16[16,256]{1,0:T(8,128)(2,1)S(1)} %get-tuple-element.57), channel_id=1, source_target_pairs={{0,8},{1,9},{2,10},{3,11},{4,12},{5,13},{6,14},{7,15},{16,24},{17,... | collective-permute-start | bytes 24584 | tf_op jit(solution)/shard_map/ppermute | solution.py:555
  77.7 14.3 %copy-start.16 = (s32[4]{0:T(128)S(1)}, s32[4]{0:T(128)}, u32[]{:S(2)}) copy-start(s32[4]{0:T(128)} %copy-done.14) | copy-start | bytes 52
  77.7 2.5 %collective-permute-start.9 = (bf16[16,256]{1,0:T(8,128)(2,1)S(1)}, bf16[16,256]{1,0:T(8,128)(2,1)S(1)}, u32[]{:S(2)}, u32[]{:S(2)}) collective-permute-start(bf16[16,256]{1,0:T(8,128)(2,1)S(1)} %get-tuple-element.58), channel_id=1, source_target_pairs={{8,16},{9,17},{10,18},{11,19},{12,20},{13,21},{14,22},{15,23},{40,... | collective-permute-start | bytes 24584 | tf_op jit(solution)/shard_map/ppermute | solution.py:556
  83.7 0.7 copy-start.9
  84.3 24.1 %all-to-all-start.2 = ((bf16[16,64,256]{2,1,0:T(8,128)(2,1)}), bf16[16,64,256]{2,1,0:T(8,128)(2,1)S(1)}, u32[]{:S(2)}, u32[]{:S(2)}) async-start(bf16[16,64,256]{2,1,0:T(8,128)(2,1)} %get-tuple-element.62), calls=%async_computation.2 | async-start | bytes 1048576 | tf_op jit(solution)/shard_map/all_to_all | solution.py:438
  89.2 9.0 %collective-permute-start.10 = (bf16[96,256]{1,0:T(8,128)(2,1)S(1)}, bf16[96,256]{1,0:T(8,128)(2,1)S(1)}, u32[]{:S(2)}, u32[]{:S(2)}) collective-permute-start(bf16[96,256]{1,0:T(8,128)(2,1)S(1)} %get-tuple-element.60), channel_id=1, source_target_pairs={{0,8},{1,9},{2,10},{3,11},{4,12},{5,13},{6,14},{7,15},{16,24},{17,... | collective-permute-start | bytes 147464 | tf_op jit(solution)/shard_map/ppermute | solution.py:603
  91.3 6.8 %collective-permute-start.11 = (bf16[96,256]{1,0:T(8,128)(2,1)S(1)}, bf16[96,256]{1,0:T(8,128)(2,1)S(1)}, u32[]{:S(2)}, u32[]{:S(2)}) collective-permute-start(bf16[96,256]{1,0:T(8,128)(2,1)S(1)} %get-tuple-element.61), channel_id=1, source_target_pairs={{8,16},{9,17},{10,18},{11,19},{12,20},{13,21},{14,22},{15,23},{24,... | collective-permute-start | bytes 147464 | tf_op jit(solution)/shard_map/ppermute | solution.py:603
  92.0 0.9 copy-start.12
  95.2 1.0 copy-start.2
  96.2 18.3 %collective-permute-start.13 = (bf16[16,72,256]{2,1,0:T(8,128)(2,1)}, bf16[16,72,256]{2,1,0:T(8,128)(2,1)}, u32[]{:S(2)}, u32[]{:S(2)}) collective-permute-start(bf16[16,72,256]{2,1,0:T(8,128)(2,1)} %get-tuple-element.71), channel_id=1, source_target_pairs={{0,1},{1,0},{2,3},{3,2},{4,5},{5,4},{6,7},{7,6},{8,9},{9,8},{10,11... | collective-permute-start | bytes 1769480 | tf_op jit(solution)/shard_map/ppermute | solution.py:628
  98.2 0.9 copy-start.10
  108.4 1.0 copy-start.5
  109.5 0.9 copy-start.17
  110.4 6.1 %copy-start.3 = (f32[16,72,256]{2,1,0:T(8,128)S(1)}, f32[16,72,256]{2,1,0:T(8,128)}, u32[]{:S(2)}) copy-start(f32[16,72,256]{2,1,0:T(8,128)} %copy-done.2) | copy-start | bytes 3538948
  114.4 2.1 %collective-permute-start.12 = (bf16[16,72,256]{2,1,0:T(8,128)(2,1)S(1)}, bf16[16,72,256]{2,1,0:T(8,128)(2,1)S(1)}, u32[]{:S(2)}, u32[]{:S(2)}) collective-permute-start(bf16[16,72,256]{2,1,0:T(8,128)(2,1)S(1)} %get-tuple-element.67), channel_id=1, source_target_pairs={{0,1},{1,0},{2,3},{3,2},{4,5},{5,4},{6,7},{7,6},{8,9},{9,8},{10,11... | collective-permute-start | bytes 1769480 | tf_op jit(solution)/shard_map/ppermute | solution.py:641
  168.9 3.8 %copy-start.20 = (bf16[96,384]{1,0:T(8,128)(2,1)S(1)}, bf16[96,384]{1,0:T(8,128)(2,1)}, u32[]{:S(2)}) copy-start(bf16[96,384]{1,0:T(8,128)(2,1)} %get-tuple-element.74.pick) | copy-start | bytes 221188
  168.9 22.0 %all-to-all-start.5 = ((bf16[16,144,256]{2,1,0:T(8,128)(2,1)}), bf16[16,144,256]{2,1,0:T(8,128)(2,1)S(1)}, u32[]{:S(2)}, u32[]{:S(2)}) async-start(bf16[16,144,256]{2,1,0:T(8,128)(2,1)} %shard_map.97), calls=%async_computation.5 | async-start | bytes 2359296 | tf_op jit(solution)/shard_map/all_to_all | solution.py:658
  173.5 16.2 %collective-permute-start.14 = (bf16[48,256]{1,0:T(8,128)(2,1)S(1)}, bf16[48,256]{1,0:T(8,128)(2,1)S(1)}, u32[]{:S(2)}, u32[]{:S(2)}) collective-permute-start(bf16[48,256]{1,0:T(8,128)(2,1)S(1)} %get-tuple-element.76), channel_id=1, source_target_pairs={{0,7},{1,6},{2,5},{3,4},{4,3},{5,2},{6,1},{7,0},{8,15},{9,14},{10,... | collective-permute-start | bytes 73736 | tf_op jit(solution)/shard_map/ppermute | solution.py:648
  190.9 4.7 %collective-permute-start.15 = (bf16[16,144,256]{2,1,0:T(8,128)(2,1)S(1)}, bf16[16,144,256]{2,1,0:T(8,128)(2,1)S(1)}, u32[]{:S(2)}, u32[]{:S(2)}) collective-permute-start(bf16[16,144,256]{2,1,0:T(8,128)(2,1)S(1)} %all-to-all-done.5.mine), channel_id=1, source_target_pairs={{0,1},{1,0},{2,3},{3,2},{4,5},{5,4},{6,7},{7,6},{8,9},{9,8},{10,11... | collective-permute-start | bytes 3538952 | tf_op jit(solution)/shard_map/ppermute | solution.py:660

commit v10 on v9

--- a/solution.py
+++ b/solution.py
@@ -54,34 +54,61 @@
 ACROSS_GROUPS = [[f * 64 + (t ^ m) for f in range(4) for m in (0, 56)] for t in range(32)]
 
 
-def run(kernel, outs, scratch, pos, *args, taps=None):
-    vmem = pl.BlockSpec(memory_space=pltpu.VMEM)
-    in_specs = [pl.BlockSpec(memory_space=pltpu.SMEM)] + [vmem] * len(args)
-    scratch = [pltpu.VMEM(shape, dtype) for shape, dtype in scratch]
-    operands = (pos,) + args
-    inner = kernel
-    if taps is not None:
-        in_specs = in_specs + [pl.BlockSpec(memory_space=pl.ANY)]
-        scratch = scratch + [pltpu.VMEM(taps.shape, taps.dtype), pltpu.SemaphoreType.DMA(())]
-        operands = operands + (taps,)
-
-        def inner(*refs):
-            source, held, sem = refs[len(args) + 1], refs[-2], refs[-1]
-            copy = pltpu.make_async_copy(source, held, sem)
-            copy.start()
-
-            def fetched():
-                copy.wait()
-                return held
-
-            kernel(*refs[: len(args) + 1], fetched, *refs[len(args) + 2 : -2])
+def run(kernel, outs, scratch, pos, *args, taps=None, far_in=(), far_out=()):
+    vmem, hbm = pl.BlockSpec(memory_space=pltpu.VMEM), pl.BlockSpec(memory_space=pltpu.HBM)
+    operands = [pos, *args] + ([] if taps is None else [taps])
+    far = list(far_in) + ([] if taps is None else [len(args)])
+    in_specs = [pl.BlockSpec(memory_space=pltpu.SMEM)] + [hbm if i in far else vmem for i in range(len(operands) - 1)]
+    out_specs = [hbm if i in far_out else vmem for i in range(len(outs))]
+    held = [pltpu.VMEM(operands[i + 1].shape, operands[i + 1].dtype) for i in far]
+    held = held + [pltpu.VMEM(*outs[i]) for i in far_out]
+    sems = [pltpu.SemaphoreType.DMA(())] * len(held)
+
+    def inner(*refs):
+        refs = list(refs)
+        first_out = len(operands)
+        first_scratch = first_out + len(outs)
+        first_held = first_scratch + len(scratch)
+        buffers, flags = refs[first_held : first_held + len(held)], refs[first_held + len(held) :]
+        fetches = []
+        for n, i in enumerate(far):
+            fetches.append(pltpu.make_async_copy(refs[i + 1], buffers[n], flags[n]))
+            fetches[-1].start()
+            refs[i + 1] = buffers[n]
+        leaves = {}
+        for n, i in enumerate(far_out):
+            n = n + len(far)
+            leaves[i] = pltpu.make_async_copy(buffers[n], refs[first_out + i], flags[n])
+            refs[first_out + i] = buffers[n]
+        left = []
+
+        def flush(i):
+            leaves[i].start()
+            left.append(i)
+
+        for copy in fetches[: len(far_in)]:
+            copy.wait()
+        if taps is not None:
+
+            def fetched(target=refs[first_out - 1]):
+                fetches[-1].wait()
+                return target
+
+            refs[first_out - 1] = fetched
+        extra = {"flush": flush} if far_out else {}
+        kernel(*refs[:first_held], **extra)
+        for i in far_out:
+            if i not in left:
+                flush(i)
+        for i in far_out:
+            leaves[i].wait()
 
     return pl.pallas_call(
         inner,
         out_shape=[jax.ShapeDtypeStruct(shape, dtype) for shape, dtype in outs],
         in_specs=in_specs,
-        out_specs=[vmem] * len(outs),
-        scratch_shapes=scratch,
+        out_specs=out_specs,
+        scratch_shapes=[pltpu.VMEM(shape, dtype) for shape, dtype in scratch] + held + sems,
         compiler_params=pltpu.CompilerParams(vmem_limit_bytes=24 * 2**20),
     )(*operands)
 
@@ -211,16 +238,19 @@
         strips[at + 10 : at + 12, :] = ends[16 + 2 * f : 18 + 2 * f, :]
 
 
-def input_kernel(pos, own, swapped, odd, end_one, end_two, wide, first, second, send, cells, ends, strips):
-    strips[...] = jnp.zeros_like(strips)
+def input_kernel(pos, own, swapped, odd, end_one, end_two, wide, first, second, send, cells, ends, strips, flush):
     widen(pos, own, swapped, odd, end_one, end_two, wide, first, second, cells, ends, strips, 12)
+    flush(0)
     post_strips(strips, send)
 
 
-def rim_kernel(pos, own, swapped, odd, end_one, end_two, fetched, wide, first, second, send, cells, ends, lines, strips):
+def rim_kernel(
+    pos, own, swapped, odd, end_one, end_two, fetched, wide, first, second, send, cells, ends, lines, strips, flush
+):
     row, col = pos[0], pos[1]
     lines[...] = jnp.zeros_like(lines)
     widen(pos, own, swapped, odd, end_one, end_two, wide, first, second, cells, ends, lines, PITCH)
+    flush(0)
     bottom, right = 2 * (row // 4), 2 * (col // 4)
     kernel = fetched()
     totals = []
@@ -257,14 +287,18 @@
     cells[36 * PITCH :, :] = jnp.zeros((8, C), F32)
 
 
-def one_kernel(pos, wide, first, second, got, pick, fetched, filled, pre, hidden, send, cells, shifts, strips, lines):
+def one_kernel(
+    pos, wide, first, second, got, pick, fetched, filled, pre, hidden, send, cells, shifts, strips, lines, flush
+):
     row, col = pos[0], pos[1]
     lines[...] = dot(pick[...], got[...], ((1,), (0,)))
     stack_lines(row, wide, first, second, cells)
     fill_strips(cells, lines, row, col, 12, 1, 10, 12)
     filled[...] = cells[0 : 36 * PITCH, :].astype(BF16)
+    flush(0)
     total = convolve(cells, shifts, 12, 10, 0, fetched(), False)
     pre[...] = total
+    flush(1)
     inside = cell_mask(row, col)
     for f in range(3):
         v = total[f * 10 * PITCH : (f + 1) * 10 * PITCH]
@@ -276,19 +310,20 @@
 
 
 def two_kernel(
-    pos, hidden, got, pick, cotangent, fetched, filled, delta, wide_delta, first, second, cells, shifts, lines, ends
+    pos, hidden, got, pick, cotangent, fetched, packed, delta, first, second, cells, shifts, lines, ends, flush
 ):
     row, col = pos[0], pos[1]
     lines[...] = dot(pick[...], got[...], ((1,), (0,)))
     cells[0 : 30 * PITCH, :] = hidden[...].astype(F32)
     cells[30 * PITCH :, :] = jnp.zeros((8, C), F32)
     fill_strips(cells, lines, row, col, 10, 0, 9, 10)
-    filled[...] = cells[0 : 30 * PITCH, :].astype(BF16)
+    packed[0 : 30 * PITCH, :] = cells[0 : 30 * PITCH, :].astype(BF16)
     total = convolve(cells, shifts, 10, 8, 0, fetched(), False).reshape(24, PITCH, C)[:, 0:8, :]
     product = cotangent[...].astype(F32).reshape(24, 8, C) * slope_of(total)
     delta[...] = product.reshape(192, C).astype(BF16)
     padded = jnp.concatenate([product, jnp.zeros((24, 8, C), F32)], axis=1)
-    wide_delta[...] = padded.reshape(24 * PITCH, C).astype(BF16)
+    packed[30 * PITCH :, :] = padded.reshape(24 * PITCH, C).astype(BF16)
+    flush(0)
     cells[0:192, :] = product.reshape(192, C)
     post_ends(row, col, cells, first, second, ends)
 
@@ -374,30 +409,37 @@
     out[...] = cells[...].astype(BF16)
 
 
-def grad_kernel(height, line0, col0, pos, source, delta, keep, send, cells, shifts, sums):
-    core = pos[2]
+def add_grad(height, line0, col0, core, source, delta, sums, cells, shifts, begin):
     size = 3 * height * PITCH
-    cells[0:size, :] = source[...].astype(F32)
-    cells[size:, :] = jnp.zeros((8, C), F32)
-    right = delta[...]
+    value = source.astype(F32)
+    cells[0:size, :] = jnp.where(core == 0, value[:, 0:128], value[:, 128:256])
+    cells[size:, :] = jnp.zeros((8, 128), F32)
     for b in range(3):
         shifts[...] = cells[col0 + b : col0 + b + size, :].astype(BF16)
         for a in range(3):
             at = [(f * height + line0 + a) * PITCH for f in range(3)]
             left = jnp.concatenate([shifts[i : i + 8 * PITCH, :] for i in at], axis=0)
-            total = dot(left, right, ((0,), (0,))) * SCALE
-            low, high = total[0:128], total[128:256]
+            total = (dot(left, delta, ((0,), (0,))) * SCALE).reshape(16, 8, C)
             lines = slice((a * 3 + b) * 8, (a * 3 + b + 1) * 8)
-            keep[:, lines, :] = jnp.where(core == 0, low, high).reshape(16, 8, C)
-            sums[:, lines, :] = jnp.where(core == 0, high, low).reshape(16, 8, C)
-    send[...] = sums[...].astype(BF16)
-
-
-def pair_kernel(pos, keep_one, got_one, keep_two, got_two, out):
+            sums[:, lines, :] = total if begin else sums[:, lines, :] + total
+
+
+def grad_two_kernel(pos, own, other, out, cells, shifts, sums):
+    for begin, packed in ((True, own), (False, other)):
+        source, delta = packed[0 : 30 * PITCH, :], packed[30 * PITCH :, :]
+        add_grad(10, 0, 0, pos[2], source, delta, sums, cells, shifts, begin)
+    out[...] = sums[...].astype(BF16)
+
+
+def grad_own_kernel(pos, source, delta, sums, cells, shifts):
+    add_grad(12, 1, 1, pos[2], source[...], delta[...], sums, cells, shifts, True)
+
+
+def grad_one_kernel(pos, source, delta, part, two, out, cells, shifts, sums):
+    sums[...] = part[...]
+    add_grad(12, 1, 1, pos[2], source[...], delta[...], sums, cells, shifts, False)
     for i in range(16):
-        one = keep_one[i] + got_one[i].astype(F32)
-        two = keep_two[i] + got_two[i].astype(F32)
-        out[i] = jnp.concatenate([one, two], axis=0).astype(BF16)
+        out[i] = jnp.concatenate([sums[i].astype(BF16), two[i]], axis=0)
 
 
 def across_kernel(pos, parts, strips, out):
@@ -418,20 +460,33 @@
         out[i] = total
 
 
-def place_kernel(pos, mine, other, one, two, rows, sems):
-    core = pos[2]
+def place_kernel(swap, pos, part, *refs):
+    one, two, rows, sems = refs[-4:]
+    half = 1 - pos[2] if swap else pos[2]
+    for p in range(16):
+        block = part[p].astype(F32)
+        for k in range(18):
+            rows[k, p * 8 : (p + 1) * 8, :] = block[k * 8 : (k + 1) * 8]
     copies = []
-    for at, source in ((core, mine), (1 - core, other)):
-        begin = pl.multiple_of(at * 128, 128)
-        for p in range(16):
-            block = source[p].astype(F32)
-            for k in range(18):
-                rows[k, pl.ds(begin + p * 8, 8), :] = block[k * 8 : (k + 1) * 8]
     for k, target in ((0, one), (1, two)):
-        copies.append(pltpu.make_async_copy(rows.at[pl.ds(9 * k, 9)], target, sems.at[k]))
+        to = target.at[:, pl.ds(pl.multiple_of(half * 128, 128), 128), :]
+        copies.append(pltpu.make_async_copy(rows.at[pl.ds(9 * k, 9)], to, sems.at[k]))
         copies[-1].start()
     for copy in copies:
         copy.wait()
+
+
+def place(swap, pos, part, grads):
+    hbm = pl.BlockSpec(memory_space=pltpu.HBM)
+    return pl.pallas_call(
+        lambda *refs: place_kernel(swap, *refs),
+        out_shape=[jax.ShapeDtypeStruct((9, C, C), F32)] * 2,
+        in_specs=[pl.BlockSpec(memory_space=pltpu.SMEM), pl.BlockSpec(memory_space=pltpu.VMEM)] + [hbm] * len(grads),
+        out_specs=[hbm] * 2,
+        scratch_shapes=[pltpu.VMEM((18, 128, C), F32), pltpu.SemaphoreType.DMA((2,))],
+        input_output_aliases={2: 0, 3: 1} if grads else {},
+        compiler_params=pltpu.CompilerParams(vmem_limit_bytes=24 * 2**20),
+    )(pos, part, *grads)
 
 
 def seam_exchange(send):
@@ -564,11 +619,12 @@
         [((24, PITCH, C), F32), ((32, C), F32), ((72, C), F32)],
         pos,
         *beside(x, first, second),
+        far_out=(0,),
     )
     send, neighbour, seam_codes = lax.optimization_barrier((send, neighbour, seam_codes))
     pick_12, pick_10, add_10, add_8 = seam_picks(pos, neighbour, seam_codes)
     first, second = lax.ppermute(first, TILE, EVEN_ROWS), lax.ppermute(second, TILE, ODD_ROWS)
-    filled_in, pre_one, hidden, send = run(
+    filled, pre_one, hidden, send = run(
         one_kernel,
         [((flat, C), BF16), ((30 * PITCH, C), F32), ((30 * PITCH, C), BF16), ((16, 64, C), BF16)],
         [((spare, C), F32), ((flat, C), BF16), ((64, C), F32), ((80, C), F32)],
@@ -579,10 +635,13 @@
         seam_exchange(send),
         pick_12,
         taps=kernel_one,
+        far_in=(0, 4),
+        far_out=(0, 1),
     )
-    filled_hidden, delta, wide_two, first, second = run(
+    filled_other = lax.ppermute(filled, "core", CORES)
+    packed, delta, first, second = run(
         two_kernel,
-        [((30 * PITCH, C), BF16), ((192, C), BF16), ((24 * PITCH, C), BF16)] + ends,
+        [((54 * PITCH, C), BF16), ((192, C), BF16)] + ends,
         [((30 * PITCH + 8, C), F32), ((30 * PITCH, C), BF16), ((64, C), F32), ((32, C), F32)],
         pos,
         hidden,
@@ -590,6 +649,8 @@
         pick_10,
         cotangent.reshape(192, C),
         taps=kernel_two,
+        far_in=(2, 3),
+        far_out=(0,),
     )
     wide, first, second, send = run(
         rim_kernel,
@@ -598,6 +659,7 @@
         pos,
         *beside(delta, first, second),
         taps=kernel_two,
+        far_out=(0,),
     )
     got = seam_exchange(send)
     first, second = lax.ppermute(first, TILE, EVEN_ROWS), lax.ppermute(second, TILE, ODD_ROWS)
@@ -610,22 +672,15 @@
         first,
         second,
         taps=kernel_two,
+        far_in=(0,),
     )[0]
-    pieces = [((16, 72, C), F32), ((16, 72, C), BF16)]
-
-    def grad_of(height, line0, col0, source, delta):
-        size = 3 * height * PITCH
-        return run(
-            lambda *refs: grad_kernel(height, line0, col0, *refs),
-            pieces,
-            [((size + 8, C), F32), ((size, C), BF16), ((16, 72, C), F32)],
-            pos,
-            source,
-            delta,
-        )
-
-    keep_two, payload_two = grad_of(10, 0, 0, filled_hidden, wide_two)
-    got_two = lax.ppermute(payload_two, "core", CORES)
+    piece = (16, 72, C)
+
+    def halves(height):
+        return [((3 * height * PITCH + 8, 128), F32), ((3 * height * PITCH, 128), BF16)]
+
+    packed_other = lax.ppermute(packed, "core", CORES)
+    grad_two = run(grad_two_kernel, [(piece, BF16)], halves(10) + [(piece, F32)], pos, packed, packed_other)[0]
     wide_one, own, strips = run(
         delta_kernel,
         [((24 * PITCH, C), BF16), ((192, C), BF16), ((48, C), BF16)],
@@ -636,10 +691,20 @@
         add_10,
         pre_one,
         taps=kernel_one,
+        far_in=(2, 3),
     )
-    keep_one, payload_one = grad_of(12, 1, 1, filled_in, wide_one)
-    got_one = lax.ppermute(payload_one, "core", CORES)
-    part = run(pair_kernel, [((16, 144, C), BF16)], [], pos, keep_one, got_one, keep_two, got_two)[0]
+    wide_other = lax.ppermute(wide_one, "core", CORES)
+    part = run(grad_own_kernel, [(piece, F32)], halves(12), pos, filled, wide_one)[0]
+    part = run(
+        grad_one_kernel,
+        [((16, 144, C), BF16)],
+        halves(12) + [(piece, F32)],
+        pos,
+        filled_other,
+        wide_other,
+        part,
+        grad_two,
+    )[0]
     part = lax.all_to_all(part, AXES, 0, 0, axis_index_groups=PLANE_GROUPS)
     part = run(across_kernel, [((8, 192, C), BF16)], [], pos, part, strips)[0]
     got = lax.all_to_all(part, AXES, 0, 0, axis_index_groups=ACROSS_GROUPS)
@@ -657,15 +722,8 @@
     )[0]
     part = lax.all_to_all(part, AXES, 0, 0, axis_index_groups=PLANE_GROUPS)
     part, input_grad = lax.optimization_barrier((part, input_grad))
-    got = lax.ppermute(part, "core", CORES)
-    grads = pl.pallas_call(
-        place_kernel,
-        out_shape=[jax.ShapeDtypeStruct((9, C, C), F32)] * 2,
-        in_specs=[pl.BlockSpec(memory_space=pltpu.SMEM)] + [pl.BlockSpec(memory_space=pltpu.VMEM)] * 2,
-        out_specs=[pl.BlockSpec(memory_space=pl.ANY)] * 2,
-        scratch_shapes=[pltpu.VMEM((18, C, C), F32), pltpu.SemaphoreType.DMA((2,))],
-        compiler_params=pltpu.CompilerParams(vmem_limit_bytes=24 * 2**20),
-    )(pos, part, got)
+    grads = place(False, pos, part, [])
+    grads = place(True, pos, lax.ppermute(part, "core", CORES), grads)
     one, two = (grad.reshape(3, 3, C, C) for grad in grads)
     return (input_grad.reshape(inputs.shape), one, two)
 

time: 201 us -> 204 us (1.015)
  Pallas kernels: 27.6 us -> 31.6 us
  local copies, waits for them, and re-layouts: 10.9 us -> 7.4 us
    ppermute x3 -> x4, waiting for transfers between devices: 4.46 us -> 0.36 us  [the longest x1 0.36 us: body(): grads = place(True, pos, lax.ppermute(part, 'core', CORES), grads)]
    unnamed x46 -> x34, local copies, waits for them, and re-layouts: 9.51 us -> 6.04 us
    pallas_call x14, Pallas kernels: 21.7 us -> 24.5 us  [run(): pl.pallas_call(inner, out_shape=[jax.ShapeDtypeStruct(shape, dtype) for s...]
    ppermute x2, waiting for transfers between devices: 0.01 us -> 2.66 us  [body(): lax.ppermute(first, TILE, EVEN_ROWS)]
    ppermute x3 -> x4, starting transfers between devices: 4.32 us -> 3.11 us  [the longest x1 2.25 us: body(): grads = place(True, pos, lax.ppermute(part, 'core', CORES), grads)]
    pallas_call x1 -> x2, Pallas kernels: 3.06 us -> 4.22 us  [place(): pl.pallas_call(lambda *refs: place_kernel(swap, *refs), out_shape=[jax.Sh...]
  transfers between devices with their start and end apart: 19 -> 20, of which waited for: 8 -> 8; matrix products, arithmetic and copies ran while one was open for 1% -> 1% of each run, Pallas kernels for 7% -> 8%
where the time goes in v10:
time: 204 us; the launch traced here: 200 us
  blocking collectives  72.9 us (36%)
  starting transfers between devices  46.5 us (23%)
  waiting for transfers between devices  40.9 us (20%)
  Pallas kernels  31.6 us (15%)
  local copies, waits for them, and re-layouts  7.4 us (4%)
    all_to_all x1, blocking collectives, body(): got = lax.all_to_all(part, AXES, 0, 0, axis_index_groups=ACROSS_GROUPS)  26 us
    all_to_all x2, waiting for transfers between devices, seam_exchange(): got = lax.all_to_all(send, AXES, 0, 0, axis_index_groups=SEAM_GROUPS)  25.4 us
    pallas_call x14, Pallas kernels, run(): pl.pallas_call(inner, out_shape=[jax.ShapeDtypeStruct(shape, dtype) for s...  24.5 us
    all_to_all x1, blocking collectives, body(): part = lax.all_to_all(part, AXES, 0, 0, axis_index_groups=PLANE_GROUPS)  23.7 us
    all_to_all x1, blocking collectives, seam_exchange(): got = lax.all_to_all(send, AXES, 0, 0, axis_index_groups=SEAM_GROUPS)  23.1 us
    all_to_all x2, starting transfers between devices, seam_exchange(): got = lax.all_to_all(send, AXES, 0, 0, axis_index_groups=SEAM_GROUPS)  17.9 us
    ppermute x1, waiting for transfers between devices, body(): mirrored = lax.ppermute(mirrored, TILE, [(t, t ^ 7) for t in range(64)])  8.67 us
    ppermute x1, starting transfers between devices, body(): mirrored = lax.ppermute(mirrored, TILE, [(t, t ^ 7) for t in range(64)])  7.52 us
  transfers between devices with their start and end apart: 20, of which 8 were waited for; matrix products, arithmetic and copies ran while one was open for 1% of the time, Pallas kernels for 8%

profile of v10, /device:TPU:1, one launch (start us, length us, event | category | flops | bytes accessed | tf_op | source)
XLA Modules:
  0.0 200.4 jit_solution(13338316778508250692)
XLA Ops:
  0.6 4.7 %collective-permute-start.1 = (bf16[192,256]{1,0:T(8,128)(2,1)}, bf16[192,256]{1,0:T(8,128)(2,1)S(1)}, u32[]{:S(2)}, u32[]{:S(2)}) collective-permute-start(bf16[192,256]{1,0:T(8,128)(2,1)} %bitcast.17), channel_id=1, source_target_pairs={{1,2},{3,4},{5,6},{9,10},{11,12},{13,14},{17,18},{19,20},{21,22},{... | collective-permute-start | bytes 294920 | tf_op jit(solution)/shard_map/ppermute | solution.py:609
  5.6 0.9 copy-done.4
  7.0 1.3 collective-permute-start.2
  8.3 0.6 collective-permute-start.3
  9.0 0.6 collective-permute-done.2.refs_4_
  9.6 1.8 shard_map.86
  11.5 13.0 %all-to-all-start = ((bf16[16,72,256]{2,1,0:T(8,128)(2,1)}), bf16[16,72,256]{2,1,0:T(8,128)(2,1)S(1)}, u32[]{:S(2)}, u32[]{:S(2)}) async-start(bf16[16,72,256]{2,1,0:T(8,128)(2,1)} %get-tuple-element.45), calls=%async_computation | async-start | bytes 1179648 | tf_op jit(solution)/shard_map/all_to_all | solution.py:493
  24.6 0.7 collective-permute-start.5
  25.2 0.7 copy.11.nexts
  25.9 0.7 copy.12.codes
  26.6 2.8 %shard_map.87 = (bf16[80,1152]{1,0:T(8,128)(2,1)}, bf16[64,1024]{1,0:T(8,128)(2,1)}, bf16[64,1024]{1,0:T(8,128)(2,1)}, bf16[96,384]{1,0:T(8,128)(2,1)}) custom-call(s32[4]{0:T(128)} %copy-done.8, s32[12,4]{1,0:T(8,128)} %copy.11.nexts, s32[12,4]{1,0:T(8,128)} %copy.12.codes), custom_call_target="tpu_custom_call" | custom-call | tf_op jit(solution)/shard_map/pallas_call | solution.py:586
  29.4 16.1 %all-to-all-done = bf16[16,72,256]{2,1,0:T(8,128)(2,1)S(1)} async-done(((bf16[16,72,256]{2,1,0:T(8,128)(2,1)}), bf16[16,72,256]{2,1,0:T(8,128)(2,1)S(1)}, u32[]{:S(2)}, u32[]{:S(2)}) %all-to-all-start) | async-done | bytes 589856 | tf_op jit(solution)/shard_map/all_to_all | solution.py:493
  45.5 0.9 copy-done.7
  46.5 0.7 copy-done.9
  47.1 3.1 %shard_map.88 = (bf16[576,256]{1,0:T(8,128)(2,1)}, f32[480,256]{1,0:T(8,128)S(1)}, bf16[480,256]{1,0:T(8,128)(2,1)S(1)}, bf16[16,64,256]{2,1,0:T(8,128)(2,1)S(1)}) custom-call(s32[4]{0:T(128)S(1)} %copy-done.9, bf16[384,256]{1,0:T(8,128)(2,1)S(1)} %get-tuple-element.41.refs_1_, bf16[96,256]{1,0:T(8,128)(2,1)S(1)} %collective-permute-done.4.refs_2_, ...), custom_call_target="tpu_custom_call" | custom-call | tf_op jit(solution)/shard_map/pallas_call | solution.py:106
  50.2 23.1 %all_to_all.30 = bf16[16,64,256]{2,1,0:T(8,128)(2,1)S(1)} all-to-all(bf16[16,64,256]{2,1,0:T(8,128)(2,1)S(1)} %get-tuple-element.51), channel_id=1, replica_groups={{0,7,56,63,64,71,120,127,128,135,184,191,192,199,248,255},{1,6,57,62,65..., dimensions={0} | all-to-all | bytes 1048576 | tf_op jit(solution)/shard_map/all_to_all | solution.py:493
  73.4 3.0 %shard_map.89 = (bf16[864,256]{1,0:T(8,128)(2,1)}, bf16[192,256]{1,0:T(8,128)(2,1)S(1)}, bf16[16,256]{1,0:T(8,128)(2,1)S(1)}, bf16[16,256]{1,0:T(8,128)(2,1)S(1)}) custom-call(s32[4]{0:T(128)S(1)} %copy-done.10, bf16[480,256]{1,0:T(8,128)(2,1)S(1)} %get-tuple-element.50.refs_1_, bf16[1024,256]{1,0:T(8,128)(2,1)S(1)} %bitcast.15, ...), custom_call_target="tpu_custom_call" | custom-call | tf_op jit(solution)/shard_map/pallas_call | solution.py:106
  76.4 1.9 collective-permute-start.8
  78.5 0.7 collective-permute-start.10
  79.2 1.8 collective-permute-done.9.refs_4_
  81.0 1.3 collective-permute-done.8.refs_3_
  82.3 2.4 %shard_map.90 = (bf16[384,256]{1,0:T(8,128)(2,1)S(1)}, bf16[96,256]{1,0:T(8,128)(2,1)S(1)}, bf16[96,256]{1,0:T(8,128)(2,1)S(1)}, bf16[16,64,256]{2,1,0:T(8,128)(2,1)}) custom-call(s32[4]{0:T(128)S(1)} %copy-done.10, bf16[192,256]{1,0:T(8,128)(2,1)S(1)} %get-tuple-element.53.refs_1_, bf16[192,256]{1,0:T(8,128)(2,1)S(1)} %collective-permute-done.7.refs_2_, ...), custom_call_target="tpu_custom_call" | custom-call | tf_op jit(solution)/shard_map/pallas_call | solution.py:106
  84.7 0.7 copy-done.5
  85.4 4.9 %all-to-all-start.2 = ((bf16[16,64,256]{2,1,0:T(8,128)(2,1)}), bf16[16,64,256]{2,1,0:T(8,128)(2,1)S(1)}, u32[]{:S(2)}, u32[]{:S(2)}) async-start(bf16[16,64,256]{2,1,0:T(8,128)(2,1)} %get-tuple-element.59), calls=%async_computation.2 | async-start | bytes 1048576 | tf_op jit(solution)/shard_map/all_to_all | solution.py:493
  90.9 3.2 %collective-permute-start.11 = (bf16[96,256]{1,0:T(8,128)(2,1)S(1)}, bf16[96,256]{1,0:T(8,128)(2,1)S(1)}, u32[]{:S(2)}, u32[]{:S(2)}) collective-permute-start(bf16[96,256]{1,0:T(8,128)(2,1)S(1)} %get-tuple-element.57), channel_id=1, source_target_pairs={{0,8},{1,9},{2,10},{3,11},{4,12},{5,13},{6,14},{7,15},{16,24},{17,... | collective-permute-start | bytes 147464 | tf_op jit(solution)/shard_map/ppermute | solution.py:665
  94.1 0.7 collective-permute-start.12
  94.7 2.7 %collective-permute-done.11.refs_2_ = bf16[96,256]{1,0:T(8,128)(2,1)S(1)} collective-permute-done((bf16[96,256]{1,0:T(8,128)(2,1)S(1)}, bf16[96,256]{1,0:T(8,128)(2,1)S(1)}, u32[]{:S(2)}, u32[]{:S(2)}) %collective-permute-start.11) | collective-permute-done | bytes 49184 | tf_op jit(solution)/shard_map/ppermute | solution.py:665
  97.4 0.9 copy-done.6
  98.3 1.9 shard_map.91.refs_1_
  100.2 9.3 %all-to-all-done.2 = bf16[16,64,256]{2,1,0:T(8,128)(2,1)S(1)} async-done(((bf16[16,64,256]{2,1,0:T(8,128)(2,1)}), bf16[16,64,256]{2,1,0:T(8,128)(2,1)S(1)}, u32[]{:S(2)}, u32[]{:S(2)}) %all-to-all-start.2) | async-done | bytes 524320 | tf_op jit(solution)/shard_map/all_to_all | solution.py:493
  109.5 1.0 copy-done.3
  110.5 0.9 copy-done.11
  111.4 2.9 %shard_map.92 = (bf16[384,256]{1,0:T(8,128)(2,1)S(1)}, bf16[192,256]{1,0:T(8,128)(2,1)S(1)}, bf16[48,256]{1,0:T(8,128)(2,1)S(1)}) custom-call(s32[4]{0:T(128)S(1)} %copy-done.10, bf16[480,256]{1,0:T(8,128)(2,1)S(1)} %shard_map.91.refs_1_, bf16[1024,256]{1,0:T(8,128)(2,1)S(1)} %bitcast.16, bf16[64,1024]{1,0:T(8,128)(2,1)S(1)} %copy-done.11, ...), custom_call_target="tpu_custom_call" | custom-call | tf_op jit(solution)/shard_map/pallas_call | solution.py:106
  114.6 2.0 %shard_map.94.refs_4_ = bf16[16,72,256]{2,1,0:T(8,128)(2,1)S(1)} custom-call(s32[4]{0:T(128)S(1)} %copy-done.10, bf16[864,256]{1,0:T(8,128)(2,1)} %get-tuple-element.63.refs_1_, bf16[864,256]{1,0:T(8,128)(2,1)} %collective-permute-done.14.refs_2_), custom_call_target="tpu_custom_call" | custom-call | tf_op jit(solution)/shard_map/pallas_call | solution.py:106
  116.6 1.5 shard_map.93.refs_3_
  118.2 1.1 shard_map.95
  119.3 23.7 %all_to_all.31.refs_1_ = bf16[16,144,256]{2,1,0:T(8,128)(2,1)S(1)} all-to-all(bf16[16,144,256]{2,1,0:T(8,128)(2,1)S(1)} %shard_map.95), channel_id=1, replica_groups={{0,8,16,24,2,10,18,26,4,12,20,28,6,14,22,30},{1,9,17,25,3,11,19,27,5,13..., dimensions={0} | all-to-all | bytes 2359296 | tf_op jit(solution)/shard_map/all_to_all | solution.py:708
  143.0 0.7 shard_map.96
  143.7 26.0 %all_to_all.32.refs_1_ = bf16[8,192,256]{2,1,0:T(8,128)(2,1)S(1)} all-to-all(bf16[8,192,256]{2,1,0:T(8,128)(2,1)S(1)} %shard_map.96), channel_id=1, replica_groups={{0,56,64,120,128,184,192,248},{1,57,65,121,129,185,193,249},{2,58,66,12..., dimensions={0} | all-to-all | bytes 1572864 | tf_op jit(solution)/shard_map/all_to_all | solution.py:710
  169.7 1.6 shard_map.97
  171.4 3.8 %all-to-all-start.5 = ((bf16[16,144,256]{2,1,0:T(8,128)(2,1)}), bf16[16,144,256]{2,1,0:T(8,128)(2,1)S(1)}, u32[]{:S(2)}, u32[]{:S(2)}) async-start(bf16[16,144,256]{2,1,0:T(8,128)(2,1)} %shard_map.97), calls=%async_computation.5 | async-start | bytes 2359296 | tf_op jit(solution)/shard_map/all_to_all | solution.py:723
  175.2 0.7 shard_map.98
  176.0 7.5 %collective-permute-start.15 = (bf16[48,256]{1,0:T(8,128)(2,1)S(1)}, bf16[48,256]{1,0:T(8,128)(2,1)S(1)}, u32[]{:S(2)}, u32[]{:S(2)}) collective-permute-start(bf16[48,256]{1,0:T(8,128)(2,1)S(1)} %get-tuple-element.68), channel_id=1, source_target_pairs={{0,7},{1,6},{2,5},{3,4},{4,3},{5,2},{6,1},{7,0},{8,15},{9,14},{10,... | collective-permute-start | bytes 73736 | tf_op jit(solution)/shard_map/ppermute | solution.py:713
  183.5 8.7 %collective-permute-done.15.refs_3_ = bf16[48,256]{1,0:T(8,128)(2,1)S(1)} collective-permute-done((bf16[48,256]{1,0:T(8,128)(2,1)S(1)}, bf16[48,256]{1,0:T(8,128)(2,1)S(1)}, u32[]{:S(2)}, u32[]{:S(2)}) %collective-permute-start.15) | collective-permute-done | bytes 24608 | tf_op jit(solution)/shard_map/ppermute | solution.py:713
  192.1 1.3 shard_map.99
  193.4 2.2 %collective-permute-start.16 = (bf16[16,144,256]{2,1,0:T(8,128)(2,1)S(1)}, bf16[16,144,256]{2,1,0:T(8,128)(2,1)S(1)}, u32[]{:S(2)}, u32[]{:S(2)}) collective-permute-start(bf16[16,144,256]{2,1,0:T(8,128)(2,1)S(1)} %all-to-all-done.5.refs_1_), channel_id=1, source_target_pairs={{0,1},{1,0},{2,3},{3,2},{4,5},{5,4},{6,7},{7,6},{8,9},{9,8},{10,11... | collective-permute-start | bytes 3538952 | tf_op jit(solution)/shard_map/ppermute | solution.py:726
  195.7 2.1 %shard_map.100 = (f32[9,256,256]{2,1,0:T(8,128)}, f32[9,256,256]{2,1,0:T(8,128)}) custom-call(s32[4]{0:T(128)S(1)} %copy-done.10, bf16[16,144,256]{2,1,0:T(8,128)(2,1)S(1)} %all-to-all-done.5.refs_1_), custom_call_target="tpu_custom_call" | custom-call | tf_op jit(solution)/shard_map/pallas_call | solution.py:481
  198.1 2.1 %shard_map.101 = (f32[9,256,256]{2,1,0:T(8,128)}, f32[9,256,256]{2,1,0:T(8,128)}) custom-call(s32[4]{0:T(128)S(1)} %copy-done.10, bf16[16,144,256]{2,1,0:T(8,128)(2,1)S(1)} %collective-permute-done.16.refs_1_, f32[9,256,256]{2,1,0:T(8,128)} %get-tuple-element.71.refs_2_, ...), custom_call_target="tpu_custom_call", output_to_operand_aliasing={{0}: (2, {}), {1}: (3, {})} | custom-call | tf_op jit(solution)/shard_map/pallas_call | solution.py:481
  (49 shorter events, 2.3 us)
Async XLA Ops:
  0.6 44.9 %copy-start.1 = (bf16[3,3,256,256]{3,2,1,0:T(8,128)(2,1)S(1)}, bf16[3,3,256,256]{3,2,1,0:T(8,128)(2,1)}, u32[]{:S(2)}) copy-start(bf16[3,3,256,256]{3,2,1,0:T(8,128)(2,1)} %refs_5_.3) | copy-start | bytes 3538948
  0.6 9.0 %collective-permute-start.1 = (bf16[192,256]{1,0:T(8,128)(2,1)}, bf16[192,256]{1,0:T(8,128)(2,1)S(1)}, u32[]{:S(2)}, u32[]{:S(2)}) collective-permute-start(bf16[192,256]{1,0:T(8,128)(2,1)} %bitcast.17), channel_id=1, source_target_pairs={{1,2},{3,4},{5,6},{9,10},{11,12},{13,14},{17,18},{19,20},{21,22},{... | collective-permute-start | bytes 294920 | tf_op jit(solution)/shard_map/ppermute | solution.py:609
  5.4 4.3 %collective-permute-start = (bf16[192,256]{1,0:T(8,128)(2,1)}, bf16[192,256]{1,0:T(8,128)(2,1)S(1)}, u32[]{:S(2)}, u32[]{:S(2)}) collective-permute-start(bf16[192,256]{1,0:T(8,128)(2,1)} %bitcast.18), channel_id=1, source_target_pairs={{0,1},{1,0},{2,3},{3,2},{4,5},{5,4},{6,7},{7,6},{8,9},{9,8},{10,11... | collective-permute-start | bytes 294920 | tf_op jit(solution)/shard_map/ppermute | solution.py:608
  5.6 0.9 copy-start.4
  6.5 20.1 %copy-start.8 = (s32[4]{0:T(128)}, s32[4]{0:T(128)S(1)}, u32[]{:S(2)}) copy-start(s32[4]{0:T(128)S(1)} %pad_add_fusion.refs_0_.pos) | copy-start | bytes 52
  6.5 18.8 %copy-start.15 = (s32[12,4]{0,1:T(4,128)S(1)}, s32[12,4]{0,1:T(4,128)}, u32[]{:S(2)}) copy-start(s32[12,4]{0,1:T(4,128)} %param.10) | copy-start | bytes 580
  6.5 19.5 %copy-start.16 = (s32[12,4]{0,1:T(4,128)S(1)}, s32[12,4]{0,1:T(4,128)}, u32[]{:S(2)}) copy-start(s32[12,4]{0,1:T(4,128)} %param.11) | copy-start | bytes 580
  7.0 2.6 %collective-permute-start.2 = (bf16[16,256]{1,0:T(8,128)(2,1)S(1)}, bf16[16,256]{1,0:T(8,128)(2,1)S(1)}, u32[]{:S(2)}, u32[]{:S(2)}) collective-permute-start(bf16[16,256]{1,0:T(8,128)(2,1)S(1)} %get-tuple-element.39), channel_id=1, source_target_pairs={{0,8},{1,9},{2,10},{3,11},{4,12},{5,13},{6,14},{7,15},{16,24},{17,... | collective-permute-start | bytes 24584 | tf_op jit(solution)/shard_map/ppermute | solution.py:610
  8.3 1.3 collective-permute-start.3
  11.5 34.1 %all-to-all-start = ((bf16[16,72,256]{2,1,0:T(8,128)(2,1)}), bf16[16,72,256]{2,1,0:T(8,128)(2,1)S(1)}, u32[]{:S(2)}, u32[]{:S(2)}) async-start(bf16[16,72,256]{2,1,0:T(8,128)(2,1)} %get-tuple-element.45), calls=%async_computation | async-start | bytes 1179648 | tf_op jit(solution)/shard_map/all_to_all | solution.py:493
  24.5 5.0 %collective-permute-start.4 = (bf16[96,256]{1,0:T(8,128)(2,1)S(1)}, bf16[96,256]{1,0:T(8,128)(2,1)S(1)}, u32[]{:S(2)}, u32[]{:S(2)}) collective-permute-start(bf16[96,256]{1,0:T(8,128)(2,1)S(1)} %get-tuple-element.42), channel_id=1, source_target_pairs={{0,8},{1,9},{2,10},{3,11},{4,12},{5,13},{6,14},{7,15},{16,24},{17,... | collective-permute-start | bytes 147464 | tf_op jit(solution)/shard_map/ppermute | solution.py:626
  24.6 4.9 %collective-permute-start.5 = (bf16[96,256]{1,0:T(8,128)(2,1)S(1)}, bf16[96,256]{1,0:T(8,128)(2,1)S(1)}, u32[]{:S(2)}, u32[]{:S(2)}) collective-permute-start(bf16[96,256]{1,0:T(8,128)(2,1)S(1)} %get-tuple-element.43), channel_id=1, source_target_pairs={{8,16},{9,17},{10,18},{11,19},{12,20},{13,21},{14,22},{15,23},{24,... | collective-permute-start | bytes 147464 | tf_op jit(solution)/shard_map/ppermute | solution.py:626
  45.5 0.9 copy-start.7
  46.5 0.7 copy-start.9
  47.1 26.2 %copy-start = (bf16[3,3,256,256]{3,2,1,0:T(8,128)(2,1)S(1)}, bf16[3,3,256,256]{3,2,1,0:T(8,128)(2,1)}, u32[]{:S(2)}) copy-start(bf16[3,3,256,256]{3,2,1,0:T(8,128)(2,1)} %refs_4_.1) | copy-start | bytes 3538948
  47.1 26.2 %copy-start.10 = (s32[4]{0:T(128)S(1)}, s32[4]{0:T(128)}, u32[]{:S(2)}) copy-start(s32[4]{0:T(128)} %copy-done.8) | copy-start | bytes 52
  47.1 26.2 %copy-start.12 = (bf16[64,1024]{1,0:T(8,128)(2,1)S(1)}, bf16[64,1024]{1,0:T(8,128)(2,1)}, u32[]{:S(2)}) copy-start(bf16[64,1024]{1,0:T(8,128)(2,1)} %get-tuple-element.52.refs_3_) | copy-start | bytes 393220
  47.1 26.2 %copy-start.13 = (bf16[3,1,8,8,256]{4,3,2,1,0:T(8,128)(2,1)S(1)}, bf16[3,1,8,8,256]{4,3,2,1,0:T(8,128)(2,1)}, u32[]{:S(2)}) copy-start(bf16[3,1,8,8,256]{4,3,2,1,0:T(8,128)(2,1)} %param.7) | copy-start | bytes 294916
  50.2 23.1 %copy-start.2 = (f32[480,256]{1,0:T(8,128)}, f32[480,256]{1,0:T(8,128)S(1)}, u32[]{:S(2)}) copy-start(f32[480,256]{1,0:T(8,128)S(1)} %get-tuple-element.61.refs_4_) | copy-start | bytes 1474564
  76.4 5.9 %collective-permute-start.8 = (bf16[192,256]{1,0:T(8,128)(2,1)S(1)}, bf16[192,256]{1,0:T(8,128)(2,1)S(1)}, u32[]{:S(2)}, u32[]{:S(2)}) collective-permute-start(bf16[192,256]{1,0:T(8,128)(2,1)S(1)} %get-tuple-element.53.refs_1_), channel_id=1, source_target_pairs={{1,2},{3,4},{5,6},{9,10},{11,12},{13,14},{17,18},{19,20},{21,22},{... | collective-permute-start | bytes 294920 | tf_op jit(solution)/shard_map/ppermute | solution.py:609
  78.3 4.0 %collective-permute-start.7 = (bf16[192,256]{1,0:T(8,128)(2,1)S(1)}, bf16[192,256]{1,0:T(8,128)(2,1)S(1)}, u32[]{:S(2)}, u32[]{:S(2)}) collective-permute-start(bf16[192,256]{1,0:T(8,128)(2,1)S(1)} %get-tuple-element.53.refs_1_), channel_id=1, source_target_pairs={{0,1},{1,0},{2,3},{3,2},{4,5},{5,4},{6,7},{7,6},{8,9},{9,8},{10,11... | collective-permute-start | bytes 294920 | tf_op jit(solution)/shard_map/ppermute | solution.py:608
  78.4 2.6 %collective-permute-start.9 = (bf16[16,256]{1,0:T(8,128)(2,1)S(1)}, bf16[16,256]{1,0:T(8,128)(2,1)S(1)}, u32[]{:S(2)}, u32[]{:S(2)}) collective-permute-start(bf16[16,256]{1,0:T(8,128)(2,1)S(1)} %get-tuple-element.54), channel_id=1, source_target_pairs={{0,8},{1,9},{2,10},{3,11},{4,12},{5,13},{6,14},{7,15},{16,24},{17,... | collective-permute-start | bytes 24584 | tf_op jit(solution)/shard_map/ppermute | solution.py:610
  78.5 2.5 %collective-permute-start.10 = (bf16[16,256]{1,0:T(8,128)(2,1)S(1)}, bf16[16,256]{1,0:T(8,128)(2,1)S(1)}, u32[]{:S(2)}, u32[]{:S(2)}) collective-permute-start(bf16[16,256]{1,0:T(8,128)(2,1)S(1)} %get-tuple-element.55), channel_id=1, source_target_pairs={{8,16},{9,17},{10,18},{11,19},{12,20},{13,21},{14,22},{15,23},{40,... | collective-permute-start | bytes 24584 | tf_op jit(solution)/shard_map/ppermute | solution.py:611
  84.7 0.7 copy-start.5
  85.4 24.1 %all-to-all-start.2 = ((bf16[16,64,256]{2,1,0:T(8,128)(2,1)}), bf16[16,64,256]{2,1,0:T(8,128)(2,1)S(1)}, u32[]{:S(2)}, u32[]{:S(2)}) async-start(bf16[16,64,256]{2,1,0:T(8,128)(2,1)} %get-tuple-element.59), calls=%async_computation.2 | async-start | bytes 1048576 | tf_op jit(solution)/shard_map/all_to_all | solution.py:493
  90.3 24.3 %collective-permute-start.14 = (bf16[864,256]{1,0:T(8,128)(2,1)}, bf16[864,256]{1,0:T(8,128)(2,1)}, u32[]{:S(2)}, u32[]{:S(2)}) collective-permute-start(bf16[864,256]{1,0:T(8,128)(2,1)} %get-tuple-element.63.refs_1_), channel_id=1, source_target_pairs={{0,1},{1,0},{2,3},{3,2},{4,5},{5,4},{6,7},{7,6},{8,9},{9,8},{10,11... | collective-permute-start | bytes 1327112 | tf_op jit(solution)/shard_map/ppermute | solution.py:682
  90.4 27.8 %collective-permute-start.6 = (bf16[576,256]{1,0:T(8,128)(2,1)}, bf16[576,256]{1,0:T(8,128)(2,1)S(1)}, u32[]{:S(2)}, u32[]{:S(2)}) collective-permute-start(bf16[576,256]{1,0:T(8,128)(2,1)} %get-tuple-element.49.refs_1_), channel_id=1, source_target_pairs={{0,1},{1,0},{2,3},{3,2},{4,5},{5,4},{6,7},{7,6},{8,9},{9,8},{10,11... | collective-permute-start | bytes 884744 | tf_op jit(solution)/shard_map/ppermute | solution.py:641
  90.9 6.5 %collective-permute-start.11 = (bf16[96,256]{1,0:T(8,128)(2,1)S(1)}, bf16[96,256]{1,0:T(8,128)(2,1)S(1)}, u32[]{:S(2)}, u32[]{:S(2)}) collective-permute-start(bf16[96,256]{1,0:T(8,128)(2,1)S(1)} %get-tuple-element.57), channel_id=1, source_target_pairs={{0,8},{1,9},{2,10},{3,11},{4,12},{5,13},{6,14},{7,15},{16,24},{17,... | collective-permute-start | bytes 147464 | tf_op jit(solution)/shard_map/ppermute | solution.py:665
  94.1 3.3 %collective-permute-start.12 = (bf16[96,256]{1,0:T(8,128)(2,1)S(1)}, bf16[96,256]{1,0:T(8,128)(2,1)S(1)}, u32[]{:S(2)}, u32[]{:S(2)}) collective-permute-start(bf16[96,256]{1,0:T(8,128)(2,1)S(1)} %get-tuple-element.58), channel_id=1, source_target_pairs={{8,16},{9,17},{10,18},{11,19},{12,20},{13,21},{14,22},{15,23},{24,... | collective-permute-start | bytes 147464 | tf_op jit(solution)/shard_map/ppermute | solution.py:665
  97.4 0.9 copy-start.6
  109.5 1.0 copy-start.3
  110.5 0.9 copy-start.11
  114.3 3.9 %collective-permute-start.13 = (bf16[384,256]{1,0:T(8,128)(2,1)S(1)}, bf16[384,256]{1,0:T(8,128)(2,1)S(1)}, u32[]{:S(2)}, u32[]{:S(2)}) collective-permute-start(bf16[384,256]{1,0:T(8,128)(2,1)S(1)} %get-tuple-element.62.refs_2_), channel_id=1, source_target_pairs={{0,1},{1,0},{2,3},{3,2},{4,5},{5,4},{6,7},{7,6},{8,9},{9,8},{10,11... | collective-permute-start | bytes 589832 | tf_op jit(solution)/shard_map/ppermute | solution.py:696
  171.4 3.8 %copy-start.14 = (bf16[96,384]{1,0:T(8,128)(2,1)S(1)}, bf16[96,384]{1,0:T(8,128)(2,1)}, u32[]{:S(2)}) copy-start(bf16[96,384]{1,0:T(8,128)(2,1)} %get-tuple-element.66.refs_2_) | copy-start | bytes 221188
  171.4 22.0 %all-to-all-start.5 = ((bf16[16,144,256]{2,1,0:T(8,128)(2,1)}), bf16[16,144,256]{2,1,0:T(8,128)(2,1)S(1)}, u32[]{:S(2)}, u32[]{:S(2)}) async-start(bf16[16,144,256]{2,1,0:T(8,128)(2,1)} %shard_map.97), calls=%async_computation.5 | async-start | bytes 2359296 | tf_op jit(solution)/shard_map/all_to_all | solution.py:723
  176.0 16.2 %collective-permute-start.15 = (bf16[48,256]{1,0:T(8,128)(2,1)S(1)}, bf16[48,256]{1,0:T(8,128)(2,1)S(1)}, u32[]{:S(2)}, u32[]{:S(2)}) collective-permute-start(bf16[48,256]{1,0:T(8,128)(2,1)S(1)} %get-tuple-element.68), channel_id=1, source_target_pairs={{0,7},{1,6},{2,5},{3,4},{4,3},{5,2},{6,1},{7,0},{8,15},{9,14},{10,... | collective-permute-start | bytes 73736 | tf_op jit(solution)/shard_map/ppermute | solution.py:713
  193.4 4.7 %collective-permute-start.16 = (bf16[16,144,256]{2,1,0:T(8,128)(2,1)S(1)}, bf16[16,144,256]{2,1,0:T(8,128)(2,1)S(1)}, u32[]{:S(2)}, u32[]{:S(2)}) collective-permute-start(bf16[16,144,256]{2,1,0:T(8,128)(2,1)S(1)} %all-to-all-done.5.refs_1_), channel_id=1, source_target_pairs={{0,1},{1,0},{2,3},{3,2},{4,5},{5,4},{6,7},{7,6},{8,9},{9,8},{10,11... | collective-permute-start | bytes 3538952 | tf_op jit(solution)/shard_map/ppermute | solution.py:726

commit v11 on v10

--- a/solution.py
+++ b/solution.py
@@ -54,61 +54,34 @@
 ACROSS_GROUPS = [[f * 64 + (t ^ m) for f in range(4) for m in (0, 56)] for t in range(32)]
 
 
-def run(kernel, outs, scratch, pos, *args, taps=None, far_in=(), far_out=()):
-    vmem, hbm = pl.BlockSpec(memory_space=pltpu.VMEM), pl.BlockSpec(memory_space=pltpu.HBM)
-    operands = [pos, *args] + ([] if taps is None else [taps])
-    far = list(far_in) + ([] if taps is None else [len(args)])
-    in_specs = [pl.BlockSpec(memory_space=pltpu.SMEM)] + [hbm if i in far else vmem for i in range(len(operands) - 1)]
-    out_specs = [hbm if i in far_out else vmem for i in range(len(outs))]
-    held = [pltpu.VMEM(operands[i + 1].shape, operands[i + 1].dtype) for i in far]
-    held = held + [pltpu.VMEM(*outs[i]) for i in far_out]
-    sems = [pltpu.SemaphoreType.DMA(())] * len(held)
-
-    def inner(*refs):
-        refs = list(refs)
-        first_out = len(operands)
-        first_scratch = first_out + len(outs)
-        first_held = first_scratch + len(scratch)
-        buffers, flags = refs[first_held : first_held + len(held)], refs[first_held + len(held) :]
-        fetches = []
-        for n, i in enumerate(far):
-            fetches.append(pltpu.make_async_copy(refs[i + 1], buffers[n], flags[n]))
-            fetches[-1].start()
-            refs[i + 1] = buffers[n]
-        leaves = {}
-        for n, i in enumerate(far_out):
-            n = n + len(far)
-            leaves[i] = pltpu.make_async_copy(buffers[n], refs[first_out + i], flags[n])
-            refs[first_out + i] = buffers[n]
-        left = []
-
-        def flush(i):
-            leaves[i].start()
-            left.append(i)
-
-        for copy in fetches[: len(far_in)]:
-            copy.wait()
-        if taps is not None:
-
-            def fetched(target=refs[first_out - 1]):
-                fetches[-1].wait()
-                return target
-
-            refs[first_out - 1] = fetched
-        extra = {"flush": flush} if far_out else {}
-        kernel(*refs[:first_held], **extra)
-        for i in far_out:
-            if i not in left:
-                flush(i)
-        for i in far_out:
-            leaves[i].wait()
+def run(kernel, outs, scratch, pos, *args, taps=None):
+    vmem = pl.BlockSpec(memory_space=pltpu.VMEM)
+    in_specs = [pl.BlockSpec(memory_space=pltpu.SMEM)] + [vmem] * len(args)
+    scratch = [pltpu.VMEM(shape, dtype) for shape, dtype in scratch]
+    operands = (pos,) + args
+    inner = kernel
+    if taps is not None:
+        in_specs = in_specs + [pl.BlockSpec(memory_space=pl.ANY)]
+        scratch = scratch + [pltpu.VMEM(taps.shape, taps.dtype), pltpu.SemaphoreType.DMA(())]
+        operands = operands + (taps,)
+
+        def inner(*refs):
+            source, held, sem = refs[len(args) + 1], refs[-2], refs[-1]
+            copy = pltpu.make_async_copy(source, held, sem)
+            copy.start()
+
+            def fetched():
+                copy.wait()
+                return held
+
+            kernel(*refs[: len(args) + 1], fetched, *refs[len(args) + 2 : -2])
 
     return pl.pallas_call(
         inner,
         out_shape=[jax.ShapeDtypeStruct(shape, dtype) for shape, dtype in outs],
         in_specs=in_specs,
-        out_specs=out_specs,
-        scratch_shapes=[pltpu.VMEM(shape, dtype) for shape, dtype in scratch] + held + sems,
+        out_specs=[vmem] * len(outs),
+        scratch_shapes=scratch,
         compiler_params=pltpu.CompilerParams(vmem_limit_bytes=24 * 2**20),
     )(*operands)
 
@@ -238,19 +211,17 @@
         strips[at + 10 : at + 12, :] = ends[16 + 2 * f : 18 + 2 * f, :]
 
 
-def input_kernel(pos, own, swapped, odd, end_one, end_two, wide, first, second, send, cells, ends, strips, flush):
+def input_kernel(pos, own, swapped, odd, end_one, end_two, wide, first, second, send, cells, ends, strips):
     widen(pos, own, swapped, odd, end_one, end_two, wide, first, second, cells, ends, strips, 12)
-    flush(0)
     post_strips(strips, send)
 
 
 def rim_kernel(
-    pos, own, swapped, odd, end_one, end_two, fetched, wide, first, second, send, cells, ends, lines, strips, flush
+    pos, own, swapped, odd, end_one, end_two, fetched, wide, first, second, send, cells, ends, lines, strips
 ):
     row, col = pos[0], pos[1]
     lines[...] = jnp.zeros_like(lines)
     widen(pos, own, swapped, odd, end_one, end_two, wide, first, second, cells, ends, lines, PITCH)
-    flush(0)
     bottom, right = 2 * (row // 4), 2 * (col // 4)
     kernel = fetched()
     totals = []
@@ -288,17 +259,15 @@
 
 
 def one_kernel(
-    pos, wide, first, second, got, pick, fetched, filled, pre, hidden, send, cells, shifts, strips, lines, flush
+    pos, wide, first, second, got, pick, fetched, filled, pre, hidden, send, cells, shifts, strips, lines
 ):
     row, col = pos[0], pos[1]
     lines[...] = dot(pick[...], got[...], ((1,), (0,)))
     stack_lines(row, wide, first, second, cells)
     fill_strips(cells, lines, row, col, 12, 1, 10, 12)
     filled[...] = cells[0 : 36 * PITCH, :].astype(BF16)
-    flush(0)
     total = convolve(cells, shifts, 12, 10, 0, fetched(), False)
     pre[...] = total
-    flush(1)
     inside = cell_mask(row, col)
     for f in range(3):
         v = total[f * 10 * PITCH : (f + 1) * 10 * PITCH]
@@ -310,7 +279,7 @@
 
 
 def two_kernel(
-    pos, hidden, got, pick, cotangent, fetched, packed, delta, first, second, cells, shifts, lines, ends, flush
+    pos, hidden, got, pick, cotangent, fetched, packed, delta, first, second, cells, shifts, lines, ends
 ):
     row, col = pos[0], pos[1]
     lines[...] = dot(pick[...], got[...], ((1,), (0,)))
@@ -323,7 +292,6 @@
     delta[...] = product.reshape(192, C).astype(BF16)
     padded = jnp.concatenate([product, jnp.zeros((24, 8, C), F32)], axis=1)
     packed[30 * PITCH :, :] = padded.reshape(24 * PITCH, C).astype(BF16)
-    flush(0)
     cells[0:192, :] = product.reshape(192, C)
     post_ends(row, col, cells, first, second, ends)
 
@@ -378,16 +346,17 @@
     own[...] = cells[0:192, :].astype(BF16)
 
 
-def share_kernel(pos, got, pick, own, mirrored):
-    strips = jnp.concatenate([got[i, 144:192, :] for i in range(8)], axis=0)
-    total = dot(pick[...], strips, ((1,), (0,)))
+def share_kernel(pos, one, two, three, four, pick, own, by_col, by_row, by_both):
+    strips = [one[...], two[...], three[...], four[...], jnp.zeros((64, C), BF16)]
+    total = dot(pick[...], jnp.concatenate(strips, axis=0), ((1,), (0,)))
     own[...] = total[0:48]
-    mirrored[...] = total[48:96].astype(BF16)
-
-
-def final_kernel(pos, own, one, two, out, cells, lines):
+    for i, out in enumerate((by_col, by_row, by_both)):
+        out[...] = total[48 * (i + 1) : 48 * (i + 2)].astype(BF16)
+
+
+def final_kernel(pos, own, mine, by_col, by_row, by_both, out, cells, lines):
     row, col = pos[0], pos[1]
-    lines[...] = one[...] + two[...].astype(F32)
+    lines[...] = mine[...] + by_col[...].astype(F32) + by_row[...].astype(F32) + by_both[...].astype(F32)
     cells[...] = own[...].astype(F32)
     for f in range(3):
         base = f * 64
@@ -442,19 +411,19 @@
         out[i] = jnp.concatenate([sums[i].astype(BF16), two[i]], axis=0)
 
 
-def across_kernel(pos, parts, strips, out):
+def across_kernel(pos, parts, out):
     total = parts[0].astype(F32)
     for i in range(1, 16):
         total = total + parts[i].astype(F32)
-    total = jnp.concatenate([total.astype(BF16), strips[...]], axis=0)
+    total = total.astype(BF16)
     for i in range(8):
         out[i] = total
 
 
 def gather_kernel(pos, parts, out):
-    total = parts[0, 0:144, :].astype(F32)
+    total = parts[0].astype(F32)
     for i in range(1, 8):
-        total = total + parts[i, 0:144, :].astype(F32)
+        total = total + parts[i].astype(F32)
     total = total.astype(BF16)
     for i in range(16):
         out[i] = total
@@ -560,32 +529,29 @@
     parts = [((first == at_row + r) | (second == at_row + r)).astype(F32) for r in range(0, 64, 8)]
     add_10[...] = jnp.concatenate(parts, axis=0).astype(BF16)
 
-    q = lax.broadcasted_iota(jnp.int32, (8, 384), 1)
+    q = lax.broadcasted_iota(jnp.int32, (8, 256), 1)
     slot, at = q >> 3, q & 7
-    base = jnp.full((8, 384), -far, jnp.int32)
-    step = jnp.zeros((8, 384), jnp.int32)
-    for f in range(4):
-        for half in range(2):
-            m = 2 * half + right
-            for j in range(3):
-                for kind in range(2):
-                    across, rel, reverse = seam(3 * f + j, kind, half if kind == 0 else 2 + right)
-                    to = (m ^ rel) ^ mirror
-                    mine = (lax.div(across, 3) == group) & (to < 2)
-                    value = to * 48 + (lax.rem(across, 3) * 2 + kind) * 8 + 7 * reverse
-                    value = jnp.where(mine, value - begins[kind], -far)
-                    here = slot == (f * 2 + half) * 6 + j * 2 + kind
-                    base = jnp.where(here, value, base)
-                    step = jnp.where(here, 1 - 2 * reverse, step)
+    base = jnp.full((8, 256), -far, jnp.int32)
+    step = jnp.zeros((8, 256), jnp.int32)
+    for back in range(4):
+        f = (group - back) & 3
+        for j in range(3):
+            for kind in range(2):
+                across, rel, reverse = seam(3 * f + j, kind, bottom if kind == 0 else 2 + right)
+                value = rel * 48 + (lax.rem(across, 3) * 2 + kind) * 8 + 7 * reverse
+                value = jnp.where(lax.div(across, 3) == group, value - begins[kind], -far)
+                here = slot == back * 6 + j * 2 + kind
+                base = jnp.where(here, value, base)
+                step = jnp.where(here, 1 - 2 * reverse, step)
     first = base + step * at
-    at_row = lax.broadcasted_iota(jnp.int32, (8, 384), 0)
-    share[...] = jnp.concatenate([(first == at_row + r).astype(F32) for r in range(0, 96, 8)], axis=0).astype(BF16)
+    at_row = lax.broadcasted_iota(jnp.int32, (8, 256), 0)
+    share[...] = jnp.concatenate([(first == at_row + r).astype(F32) for r in range(0, 192, 8)], axis=0).astype(BF16)
 
 
 def seam_picks(pos, nexts, codes):
     return pl.pallas_call(
         picks_kernel,
-        out_shape=[jax.ShapeDtypeStruct(shape, BF16) for shape in ((80, 1152), (64, 1024), (64, 1024), (96, 384))],
+        out_shape=[jax.ShapeDtypeStruct(shape, BF16) for shape in ((80, 1152), (64, 1024), (64, 1024), (192, 256))],
         in_specs=[pl.BlockSpec(memory_space=pltpu.SMEM)] * 3,
         out_specs=[pl.BlockSpec(memory_space=pltpu.VMEM)] * 4,
     )(pos, nexts, codes)
@@ -619,7 +585,6 @@
         [((24, PITCH, C), F32), ((32, C), F32), ((72, C), F32)],
         pos,
         *beside(x, first, second),
-        far_out=(0,),
     )
     send, neighbour, seam_codes = lax.optimization_barrier((send, neighbour, seam_codes))
     pick_12, pick_10, add_10, add_8 = seam_picks(pos, neighbour, seam_codes)
@@ -635,8 +600,6 @@
         seam_exchange(send),
         pick_12,
         taps=kernel_one,
-        far_in=(0, 4),
-        far_out=(0, 1),
     )
     filled_other = lax.ppermute(filled, "core", CORES)
     packed, delta, first, second = run(
@@ -649,8 +612,6 @@
         pick_10,
         cotangent.reshape(192, C),
         taps=kernel_two,
-        far_in=(2, 3),
-        far_out=(0,),
     )
     wide, first, second, send = run(
         rim_kernel,
@@ -659,7 +620,6 @@
         pos,
         *beside(delta, first, second),
         taps=kernel_two,
-        far_out=(0,),
     )
     got = seam_exchange(send)
     first, second = lax.ppermute(first, TILE, EVEN_ROWS), lax.ppermute(second, TILE, ODD_ROWS)
@@ -672,7 +632,6 @@
         first,
         second,
         taps=kernel_two,
-        far_in=(0,),
     )[0]
     piece = (16, 72, C)
 
@@ -681,6 +640,7 @@
 
     packed_other = lax.ppermute(packed, "core", CORES)
     grad_two = run(grad_two_kernel, [(piece, BF16)], halves(10) + [(piece, F32)], pos, packed, packed_other)[0]
+    got, grad_two = lax.optimization_barrier((got, grad_two))
     wide_one, own, strips = run(
         delta_kernel,
         [((24 * PITCH, C), BF16), ((192, C), BF16), ((48, C), BF16)],
@@ -691,7 +651,6 @@
         add_10,
         pre_one,
         taps=kernel_one,
-        far_in=(2, 3),
     )
     wide_other = lax.ppermute(wide_one, "core", CORES)
     part = run(grad_own_kernel, [(piece, F32)], halves(12), pos, filled, wide_one)[0]
@@ -705,20 +664,26 @@
         part,
         grad_two,
     )[0]
+    part, strips = lax.optimization_barrier((part, strips))
+    faces = [strips] + [lax.ppermute(strips, "face", [(i, (i + by) % 4) for i in range(4)]) for by in (1, 2, 3)]
     part = lax.all_to_all(part, AXES, 0, 0, axis_index_groups=PLANE_GROUPS)
-    part = run(across_kernel, [((8, 192, C), BF16)], [], pos, part, strips)[0]
-    got = lax.all_to_all(part, AXES, 0, 0, axis_index_groups=ACROSS_GROUPS)
-    part = run(gather_kernel, [((16, 144, C), BF16)], [], pos, got)[0]
-    share, mirrored = run(share_kernel, [((48, C), F32), ((48, C), BF16)], [], pos, got, add_8)
-    mirrored = lax.ppermute(mirrored, TILE, [(t, t ^ 7) for t in range(64)])
+    part, *faces = lax.optimization_barrier((part, *faces))
+    part = run(across_kernel, [((8, 144, C), BF16)], [], pos, part)[0]
+    part, *faces = lax.optimization_barrier((part, *faces))
+    strip = (48, C)
+    mine, *shares = run(share_kernel, [(strip, F32)] + [(strip, BF16)] * 3, [], pos, *faces, add_8)
+    shares = [lax.ppermute(v, TILE, [(t, t ^ m) for t in range(64)]) for v, m in zip(shares, MIRRORS[1:])]
+    part = lax.all_to_all(part, AXES, 0, 0, axis_index_groups=ACROSS_GROUPS)
+    part, *shares = lax.optimization_barrier((part, *shares))
+    part = run(gather_kernel, [((16, 144, C), BF16)], [], pos, part)[0]
     input_grad = run(
         final_kernel,
         [((192, C), BF16)],
         [((192, C), F32), ((48, C), F32)],
         pos,
         own,
-        share,
-        mirrored,
+        mine,
+        *shares,
     )[0]
     part = lax.all_to_all(part, AXES, 0, 0, axis_index_groups=PLANE_GROUPS)
     part, input_grad = lax.optimization_barrier((part, input_grad))

time: 204 us -> 207 us (1.015); the launches traced: 200 us -> 206 us
  blocking collectives: 72.9 us -> 23.1 us
  waiting for transfers between devices: 40.9 us -> 78.1 us
  starting transfers between devices: 46.5 us -> 65.8 us
    all_to_all x2 -> x0, blocking collectives: 49.8 us -> none  [the longest x1 26 us: body(): got = lax.all_to_all(part, AXES, 0, 0, axis_index_groups=ACROSS_GROUPS)]
    all_to_all x1 -> x2, waiting for transfers between devices: 0.01 us -> 32.4 us  [body(): part = lax.all_to_all(part, AXES, 0, 0, axis_index_groups=PLANE_GROUPS)]
    ppermute x1 -> x6, starting transfers between devices: 7.52 us -> 14.7 us  [the longest x3 10.5 us: body(): lax.ppermute(v, TILE, [(t, t ^ m) for t in range(64)])]
    all_to_all x1 -> x2, starting transfers between devices: 3.83 us -> 10.9 us  [body(): part = lax.all_to_all(part, AXES, 0, 0, axis_index_groups=PLANE_GROUPS)]
    all_to_all x0 -> x1, starting transfers between devices: none -> 6.89 us  [body(): part = lax.all_to_all(part, AXES, 0, 0, axis_index_groups=ACROSS_GROUPS)]
    ppermute x1 -> x6, waiting for transfers between devices: 8.67 us -> 15 us  [the longest x3 11.5 us: body(): lax.ppermute(v, TILE, [(t, t ^ m) for t in range(64)])]
  transfers between devices with their start and end apart: 20 -> 27, of which waited for: 8 -> 13; matrix products, arithmetic and copies ran while one was open for 1% -> 1% of each run, Pallas kernels for 8% -> 7%
where the time goes in v11:
time: 207 us; the launch traced here: 206 us
  waiting for transfers between devices  78.1 us (38%)
  starting transfers between devices  65.8 us (32%)
  Pallas kernels  31.1 us (15%)
  blocking collectives  23.1 us (11%)
  local copies, waits for them, and re-layouts  6.42 us (3%)
    all_to_all x2, waiting for transfers between devices, body(): part = lax.all_to_all(part, AXES, 0, 0, axis_index_groups=PLANE_GROUPS)  32.4 us
    pallas_call x14, Pallas kernels, run(): pl.pallas_call(inner, out_shape=[jax.ShapeDtypeStruct(shape, dtype) for s...  24.2 us
    all_to_all x2, waiting for transfers between devices, seam_exchange(): got = lax.all_to_all(send, AXES, 0, 0, axis_index_groups=SEAM_GROUPS)  23.9 us
    all_to_all x1, blocking collectives, seam_exchange(): got = lax.all_to_all(send, AXES, 0, 0, axis_index_groups=SEAM_GROUPS)  23.1 us
    all_to_all x2, starting transfers between devices, seam_exchange(): got = lax.all_to_all(send, AXES, 0, 0, axis_index_groups=SEAM_GROUPS)  17.9 us
    ppermute x3, waiting for transfers between devices, body(): lax.ppermute(v, TILE, [(t, t ^ m) for t in range(64)])  11.5 us
    all_to_all x2, starting transfers between devices, body(): part = lax.all_to_all(part, AXES, 0, 0, axis_index_groups=PLANE_GROUPS)  10.9 us
    ppermute x3, starting transfers between devices, body(): lax.ppermute(v, TILE, [(t, t ^ m) for t in range(64)])  10.5 us
  transfers between devices with their start and end apart: 27, of which 13 were waited for; matrix products, arithmetic and copies ran while one was open for 1% of the time, Pallas kernels for 7%

profile of v11, /device:TPU:1, one launch (start us, length us, event | category | flops | bytes accessed | tf_op | source)
XLA Modules:
  0.0 205.8 jit_solution(17584741247315066045)
XLA Ops:
  0.6 4.7 %collective-permute-start.1 = (bf16[192,256]{1,0:T(8,128)(2,1)}, bf16[192,256]{1,0:T(8,128)(2,1)S(1)}, u32[]{:S(2)}, u32[]{:S(2)}) collective-permute-start(bf16[192,256]{1,0:T(8,128)(2,1)} %bitcast.17), channel_id=1, source_target_pairs={{1,2},{3,4},{5,6},{9,10},{11,12},{13,14},{17,18},{19,20},{21,22},{... | collective-permute-start | bytes 294920 | tf_op jit(solution)/shard_map/ppermute | solution.py:575
  5.6 0.9 copy-done.4
  7.0 1.3 collective-permute-start.2
  9.6 1.6 shard_map.86
  11.2 13.0 %all-to-all-start = ((bf16[16,72,256]{2,1,0:T(8,128)(2,1)}), bf16[16,72,256]{2,1,0:T(8,128)(2,1)S(1)}, u32[]{:S(2)}, u32[]{:S(2)}) async-start(bf16[16,72,256]{2,1,0:T(8,128)(2,1)} %get-tuple-element.65), calls=%async_computation | async-start | bytes 1179648 | tf_op jit(solution)/shard_map/all_to_all | solution.py:462
  25.0 0.7 copy.11.nexts
  25.6 0.7 copy.12.codes
  26.3 2.6 %shard_map.87 = (bf16[80,1152]{1,0:T(8,128)(2,1)}, bf16[64,1024]{1,0:T(8,128)(2,1)}, bf16[64,1024]{1,0:T(8,128)(2,1)}, bf16[192,256]{1,0:T(8,128)(2,1)}) custom-call(s32[4]{0:T(128)} %copy-done.8, s32[12,4]{1,0:T(8,128)} %copy.11.nexts, s32[12,4]{1,0:T(8,128)} %copy.12.codes), custom_call_target="tpu_custom_call" | custom-call | tf_op jit(solution)/shard_map/pallas_call | solution.py:552
  29.0 16.3 %all-to-all-done = bf16[16,72,256]{2,1,0:T(8,128)(2,1)S(1)} async-done(((bf16[16,72,256]{2,1,0:T(8,128)(2,1)}), bf16[16,72,256]{2,1,0:T(8,128)(2,1)S(1)}, u32[]{:S(2)}, u32[]{:S(2)}) %all-to-all-start) | async-done | bytes 589856 | tf_op jit(solution)/shard_map/all_to_all | solution.py:462
  45.3 0.9 copy-done.7
  46.9 2.5 %shard_map.88 = (bf16[576,256]{1,0:T(8,128)(2,1)}, f32[480,256]{1,0:T(8,128)S(1)}, bf16[480,256]{1,0:T(8,128)(2,1)S(1)}, bf16[16,64,256]{2,1,0:T(8,128)(2,1)S(1)}) custom-call(s32[4]{0:T(128)S(1)} %copy-done.9, bf16[384,256]{1,0:T(8,128)(2,1)S(1)} %get-tuple-element.61.refs_1_, bf16[96,256]{1,0:T(8,128)(2,1)S(1)} %collective-permute-done.4.refs_2_, ...), custom_call_target="tpu_custom_call" | custom-call | tf_op jit(solution)/shard_map/pallas_call | solution.py:79
  49.4 23.1 %all_to_all.30 = bf16[16,64,256]{2,1,0:T(8,128)(2,1)S(1)} all-to-all(bf16[16,64,256]{2,1,0:T(8,128)(2,1)S(1)} %get-tuple-element.71), channel_id=1, replica_groups={{0,7,56,63,64,71,120,127,128,135,184,191,192,199,248,255},{1,6,57,62,65..., dimensions={0} | all-to-all | bytes 1048576 | tf_op jit(solution)/shard_map/all_to_all | solution.py:462
  72.6 2.6 %shard_map.89 = (bf16[864,256]{1,0:T(8,128)(2,1)}, bf16[192,256]{1,0:T(8,128)(2,1)S(1)}, bf16[16,256]{1,0:T(8,128)(2,1)S(1)}, bf16[16,256]{1,0:T(8,128)(2,1)S(1)}) custom-call(s32[4]{0:T(128)S(1)} %copy-done.10, bf16[480,256]{1,0:T(8,128)(2,1)S(1)} %get-tuple-element.70.refs_1_, bf16[1024,256]{1,0:T(8,128)(2,1)S(1)} %bitcast.15, ...), custom_call_target="tpu_custom_call" | custom-call | tf_op jit(solution)/shard_map/pallas_call | solution.py:79
  75.2 1.9 collective-permute-start.8
  78.0 1.8 collective-permute-done.9.refs_4_
  79.8 1.3 collective-permute-done.8.refs_3_
  81.1 2.2 %shard_map.90 = (bf16[384,256]{1,0:T(8,128)(2,1)S(1)}, bf16[96,256]{1,0:T(8,128)(2,1)S(1)}, bf16[96,256]{1,0:T(8,128)(2,1)S(1)}, bf16[16,64,256]{2,1,0:T(8,128)(2,1)}) custom-call(s32[4]{0:T(128)S(1)} %copy-done.10, bf16[192,256]{1,0:T(8,128)(2,1)S(1)} %get-tuple-element.73.refs_1_, bf16[192,256]{1,0:T(8,128)(2,1)S(1)} %collective-permute-done.7.refs_2_, ...), custom_call_target="tpu_custom_call" | custom-call | tf_op jit(solution)/shard_map/pallas_call | solution.py:79
  83.3 0.7 copy-done.5
  84.0 4.9 %all-to-all-start.2 = ((bf16[16,64,256]{2,1,0:T(8,128)(2,1)}), bf16[16,64,256]{2,1,0:T(8,128)(2,1)S(1)}, u32[]{:S(2)}, u32[]{:S(2)}) async-start(bf16[16,64,256]{2,1,0:T(8,128)(2,1)} %get-tuple-element.79), calls=%async_computation.2 | async-start | bytes 1048576 | tf_op jit(solution)/shard_map/all_to_all | solution.py:462
  89.5 3.2 %collective-permute-start.11 = (bf16[96,256]{1,0:T(8,128)(2,1)S(1)}, bf16[96,256]{1,0:T(8,128)(2,1)S(1)}, u32[]{:S(2)}, u32[]{:S(2)}) collective-permute-start(bf16[96,256]{1,0:T(8,128)(2,1)S(1)} %get-tuple-element.77), channel_id=1, source_target_pairs={{0,8},{1,9},{2,10},{3,11},{4,12},{5,13},{6,14},{7,15},{16,24},{17,... | collective-permute-start | bytes 147464 | tf_op jit(solution)/shard_map/ppermute | solution.py:625
  93.3 2.7 %collective-permute-done.11.refs_2_ = bf16[96,256]{1,0:T(8,128)(2,1)S(1)} collective-permute-done((bf16[96,256]{1,0:T(8,128)(2,1)S(1)}, bf16[96,256]{1,0:T(8,128)(2,1)S(1)}, u32[]{:S(2)}, u32[]{:S(2)}) %collective-permute-start.11) | collective-permute-done | bytes 49184 | tf_op jit(solution)/shard_map/ppermute | solution.py:625
  96.0 0.9 copy-done.6
  96.9 1.6 shard_map.91.refs_1_
  98.5 1.9 shard_map.92.two
  100.5 7.6 %all-to-all-done.2 = bf16[16,64,256]{2,1,0:T(8,128)(2,1)S(1)} async-done(((bf16[16,64,256]{2,1,0:T(8,128)(2,1)}), bf16[16,64,256]{2,1,0:T(8,128)(2,1)S(1)}, u32[]{:S(2)}, u32[]{:S(2)}) %all-to-all-start.2) | async-done | bytes 524320 | tf_op jit(solution)/shard_map/all_to_all | solution.py:462
  108.1 0.9 copy-done.11
  109.0 2.5 %shard_map.93 = (bf16[384,256]{1,0:T(8,128)(2,1)S(1)}, bf16[192,256]{1,0:T(8,128)(2,1)S(1)}, bf16[48,256]{1,0:T(8,128)(2,1)S(1)}) custom-call(s32[4]{0:T(128)S(1)} %copy-done.10, bf16[480,256]{1,0:T(8,128)(2,1)S(1)} %shard_map.91.refs_1_, bf16[1024,256]{1,0:T(8,128)(2,1)S(1)} %bitcast.16, bf16[64,1024]{1,0:T(8,128)(2,1)S(1)} %copy-done.11, ...), custom_call_target="tpu_custom_call" | custom-call | tf_op jit(solution)/shard_map/pallas_call | solution.py:79
  111.6 1.5 shard_map.94.part
  113.2 2.1 %shard_map.95 = bf16[16,144,256]{2,1,0:T(8,128)(2,1)} custom-call(s32[4]{0:T(128)S(1)} %copy-done.10, bf16[576,256]{1,0:T(8,128)(2,1)S(1)} %collective-permute-done.6.source, bf16[384,256]{1,0:T(8,128)(2,1)S(1)} %collective-permute-done.14.delta, f32[16,72,256]{2,1,0:T(8,128)S(1)} %shard_map.94.part, bf16[16,72,256]{2,1,0:T(8,128)(2,1)S(1)} %shard_map.92.two), custom_call_target="tpu_custom_call" | custom-call | tf_op jit(solution)/shard_map/pallas_call | solution.py:79
  115.3 7.2 %all-to-all-start.3 = ((bf16[16,144,256]{2,1,0:T(8,128)(2,1)}), bf16[16,144,256]{2,1,0:T(8,128)(2,1)S(1)}, u32[]{:S(2)}, u32[]{:S(2)}) async-start(bf16[16,144,256]{2,1,0:T(8,128)(2,1)} %shard_map.95), calls=%async_computation.3 | async-start | bytes 2359296 | tf_op jit(solution)/shard_map/all_to_all | solution.py:669
  122.5 2.3 %collective-permute-start.17 = (bf16[48,256]{1,0:T(8,128)(2,1)S(1)}, bf16[48,256]{1,0:T(8,128)(2,1)S(1)}, u32[]{:S(2)}, u32[]{:S(2)}) collective-permute-start(bf16[48,256]{1,0:T(8,128)(2,1)S(1)} %get-tuple-element.95.one), channel_id=1, source_target_pairs={{0,192},{64,0},{128,64},{192,128},{1,193},{65,1},{129,65},{193,129... | collective-permute-start | bytes 73736 | tf_op jit(solution)/shard_map/ppermute | solution.py:668
  125.5 1.2 collective-permute-start.15
  126.7 1.8 collective-permute-done.16.three
  128.5 1.7 collective-permute-done.15.two
  130.2 12.1 %all-to-all-done.3.parts = bf16[16,144,256]{2,1,0:T(8,128)(2,1)S(1)} async-done(((bf16[16,144,256]{2,1,0:T(8,128)(2,1)}), bf16[16,144,256]{2,1,0:T(8,128)(2,1)S(1)}, u32[]{:S(2)}, u32[]{:S(2)}) %all-to-all-start.3) | async-done | bytes 1179680 | tf_op jit(solution)/shard_map/all_to_all | solution.py:669
  142.3 1.5 shard_map.96
  143.8 6.9 %all-to-all-start.4 = ((bf16[8,144,256]{2,1,0:T(8,128)(2,1)}), bf16[8,144,256]{2,1,0:T(8,128)(2,1)S(1)}, u32[]{:S(2)}, u32[]{:S(2)}) async-start(bf16[8,144,256]{2,1,0:T(8,128)(2,1)} %shard_map.96), calls=%async_computation.4 | async-start | bytes 1179648 | tf_op jit(solution)/shard_map/all_to_all | solution.py:676
  150.7 0.7 shard_map.97
  151.4 2.4 %collective-permute-start.18 = (bf16[48,256]{1,0:T(8,128)(2,1)S(1)}, bf16[48,256]{1,0:T(8,128)(2,1)S(1)}, u32[]{:S(2)}, u32[]{:S(2)}) collective-permute-start(bf16[48,256]{1,0:T(8,128)(2,1)S(1)} %get-tuple-element.100), channel_id=1, source_target_pairs={{0,7},{1,6},{2,5},{3,4},{4,3},{5,2},{6,1},{7,0},{8,15},{9,14},{10,... | collective-permute-start | bytes 73736 | tf_op jit(solution)/shard_map/ppermute | solution.py:675
  153.8 7.8 %collective-permute-start.19 = (bf16[48,256]{1,0:T(8,128)(2,1)S(1)}, bf16[48,256]{1,0:T(8,128)(2,1)S(1)}, u32[]{:S(2)}, u32[]{:S(2)}) collective-permute-start(bf16[48,256]{1,0:T(8,128)(2,1)S(1)} %get-tuple-element.101), channel_id=1, source_target_pairs={{0,56},{1,57},{2,58},{3,59},{4,60},{5,61},{6,62},{7,63},{8,48},{9,... | collective-permute-start | bytes 73736 | tf_op jit(solution)/shard_map/ppermute | solution.py:675
  162.0 8.2 %collective-permute-done.19.by_row = bf16[48,256]{1,0:T(8,128)(2,1)S(1)} collective-permute-done((bf16[48,256]{1,0:T(8,128)(2,1)S(1)}, bf16[48,256]{1,0:T(8,128)(2,1)S(1)}, u32[]{:S(2)}, u32[]{:S(2)}) %collective-permute-start.19) | collective-permute-done | bytes 24608 | tf_op jit(solution)/shard_map/ppermute | solution.py:675
  170.1 3.3 %collective-permute-done.20.by_both = bf16[48,256]{1,0:T(8,128)(2,1)S(1)} collective-permute-done((bf16[48,256]{1,0:T(8,128)(2,1)S(1)}, bf16[48,256]{1,0:T(8,128)(2,1)S(1)}, u32[]{:S(2)}, u32[]{:S(2)}) %collective-permute-start.20) | collective-permute-done | bytes 24608 | tf_op jit(solution)/shard_map/ppermute | solution.py:675
  173.4 1.6 shard_map.98
  175.1 3.7 %all-to-all-start.5 = ((bf16[16,144,256]{2,1,0:T(8,128)(2,1)}), bf16[16,144,256]{2,1,0:T(8,128)(2,1)S(1)}, u32[]{:S(2)}, u32[]{:S(2)}) async-start(bf16[16,144,256]{2,1,0:T(8,128)(2,1)} %shard_map.98), calls=%async_computation.5 | async-start | bytes 2359296 | tf_op jit(solution)/shard_map/all_to_all | solution.py:688
  178.8 1.3 shard_map.99
  180.1 20.3 %all-to-all-done.5.refs_1_ = bf16[16,144,256]{2,1,0:T(8,128)(2,1)S(1)} async-done(((bf16[16,144,256]{2,1,0:T(8,128)(2,1)}), bf16[16,144,256]{2,1,0:T(8,128)(2,1)S(1)}, u32[]{:S(2)}, u32[]{:S(2)}) %all-to-all-start.5) | async-done | bytes 1179680 | tf_op jit(solution)/shard_map/all_to_all | solution.py:688
  201.0 2.1 %shard_map.100 = (f32[9,256,256]{2,1,0:T(8,128)}, f32[9,256,256]{2,1,0:T(8,128)}) custom-call(s32[4]{0:T(128)S(1)} %copy-done.10, bf16[16,144,256]{2,1,0:T(8,128)(2,1)S(1)} %all-to-all-done.5.refs_1_), custom_call_target="tpu_custom_call" | custom-call | tf_op jit(solution)/shard_map/pallas_call | solution.py:450
  203.5 2.1 %shard_map.101 = (f32[9,256,256]{2,1,0:T(8,128)}, f32[9,256,256]{2,1,0:T(8,128)}) custom-call(s32[4]{0:T(128)S(1)} %copy-done.10, bf16[16,144,256]{2,1,0:T(8,128)(2,1)S(1)} %collective-permute-done.21.refs_1_, f32[9,256,256]{2,1,0:T(8,128)} %get-tuple-element.111.refs_2_, ...), custom_call_target="tpu_custom_call", output_to_operand_aliasing={{0}: (2, {}), {1}: (3, {})} | custom-call | tf_op jit(solution)/shard_map/pallas_call | solution.py:450
  (61 shorter events, 7.7 us)
Async XLA Ops:
  0.6 44.6 %copy-start.1 = (bf16[3,3,256,256]{3,2,1,0:T(8,128)(2,1)S(1)}, bf16[3,3,256,256]{3,2,1,0:T(8,128)(2,1)}, u32[]{:S(2)}) copy-start(bf16[3,3,256,256]{3,2,1,0:T(8,128)(2,1)} %refs_5_.3) | copy-start | bytes 3538948
  0.6 9.0 %collective-permute-start.1 = (bf16[192,256]{1,0:T(8,128)(2,1)}, bf16[192,256]{1,0:T(8,128)(2,1)S(1)}, u32[]{:S(2)}, u32[]{:S(2)}) collective-permute-start(bf16[192,256]{1,0:T(8,128)(2,1)} %bitcast.17), channel_id=1, source_target_pairs={{1,2},{3,4},{5,6},{9,10},{11,12},{13,14},{17,18},{19,20},{21,22},{... | collective-permute-start | bytes 294920 | tf_op jit(solution)/shard_map/ppermute | solution.py:575
  5.4 4.3 %collective-permute-start = (bf16[192,256]{1,0:T(8,128)(2,1)}, bf16[192,256]{1,0:T(8,128)(2,1)S(1)}, u32[]{:S(2)}, u32[]{:S(2)}) collective-permute-start(bf16[192,256]{1,0:T(8,128)(2,1)} %bitcast.18), channel_id=1, source_target_pairs={{0,1},{1,0},{2,3},{3,2},{4,5},{5,4},{6,7},{7,6},{8,9},{9,8},{10,11... | collective-permute-start | bytes 294920 | tf_op jit(solution)/shard_map/ppermute | solution.py:574
  5.6 0.9 copy-start.4
  6.5 19.9 %copy-start.8 = (s32[4]{0:T(128)}, s32[4]{0:T(128)S(1)}, u32[]{:S(2)}) copy-start(s32[4]{0:T(128)S(1)} %pad_add_fusion.pos.refs_0_) | copy-start | bytes 52
  6.5 18.5 %copy-start.15 = (s32[12,4]{0,1:T(4,128)S(1)}, s32[12,4]{0,1:T(4,128)}, u32[]{:S(2)}) copy-start(s32[12,4]{0,1:T(4,128)} %param.10) | copy-start | bytes 580
  6.5 19.2 %copy-start.16 = (s32[12,4]{0,1:T(4,128)S(1)}, s32[12,4]{0,1:T(4,128)}, u32[]{:S(2)}) copy-start(s32[12,4]{0,1:T(4,128)} %param.11) | copy-start | bytes 580
  7.0 2.6 %collective-permute-start.2 = (bf16[16,256]{1,0:T(8,128)(2,1)S(1)}, bf16[16,256]{1,0:T(8,128)(2,1)S(1)}, u32[]{:S(2)}, u32[]{:S(2)}) collective-permute-start(bf16[16,256]{1,0:T(8,128)(2,1)S(1)} %get-tuple-element.59), channel_id=1, source_target_pairs={{0,8},{1,9},{2,10},{3,11},{4,12},{5,13},{6,14},{7,15},{16,24},{17,... | collective-permute-start | bytes 24584 | tf_op jit(solution)/shard_map/ppermute | solution.py:576
  8.3 1.3 collective-permute-start.3
  11.2 34.1 %all-to-all-start = ((bf16[16,72,256]{2,1,0:T(8,128)(2,1)}), bf16[16,72,256]{2,1,0:T(8,128)(2,1)S(1)}, u32[]{:S(2)}, u32[]{:S(2)}) async-start(bf16[16,72,256]{2,1,0:T(8,128)(2,1)} %get-tuple-element.65), calls=%async_computation | async-start | bytes 1179648 | tf_op jit(solution)/shard_map/all_to_all | solution.py:462
  24.2 4.8 %collective-permute-start.4 = (bf16[96,256]{1,0:T(8,128)(2,1)S(1)}, bf16[96,256]{1,0:T(8,128)(2,1)S(1)}, u32[]{:S(2)}, u32[]{:S(2)}) collective-permute-start(bf16[96,256]{1,0:T(8,128)(2,1)S(1)} %get-tuple-element.62), channel_id=1, source_target_pairs={{0,8},{1,9},{2,10},{3,11},{4,12},{5,13},{6,14},{7,15},{16,24},{17,... | collective-permute-start | bytes 147464 | tf_op jit(solution)/shard_map/ppermute | solution.py:591
  24.3 4.7 %collective-permute-start.5 = (bf16[96,256]{1,0:T(8,128)(2,1)S(1)}, bf16[96,256]{1,0:T(8,128)(2,1)S(1)}, u32[]{:S(2)}, u32[]{:S(2)}) collective-permute-start(bf16[96,256]{1,0:T(8,128)(2,1)S(1)} %get-tuple-element.63), channel_id=1, source_target_pairs={{8,16},{9,17},{10,18},{11,19},{12,20},{13,21},{14,22},{15,23},{24,... | collective-permute-start | bytes 147464 | tf_op jit(solution)/shard_map/ppermute | solution.py:591
  45.3 0.9 copy-start.7
  46.2 0.7 copy-start.9
  46.9 25.7 %copy-start = (bf16[3,3,256,256]{3,2,1,0:T(8,128)(2,1)S(1)}, bf16[3,3,256,256]{3,2,1,0:T(8,128)(2,1)}, u32[]{:S(2)}) copy-start(bf16[3,3,256,256]{3,2,1,0:T(8,128)(2,1)} %refs_4_.1) | copy-start | bytes 3538948
  46.9 25.7 %copy-start.10 = (s32[4]{0:T(128)S(1)}, s32[4]{0:T(128)}, u32[]{:S(2)}) copy-start(s32[4]{0:T(128)} %copy-done.8) | copy-start | bytes 52
  46.9 25.7 %copy-start.12 = (bf16[64,1024]{1,0:T(8,128)(2,1)S(1)}, bf16[64,1024]{1,0:T(8,128)(2,1)}, u32[]{:S(2)}) copy-start(bf16[64,1024]{1,0:T(8,128)(2,1)} %get-tuple-element.72.refs_3_) | copy-start | bytes 393220
  46.9 25.7 %copy-start.13 = (bf16[3,1,8,8,256]{4,3,2,1,0:T(8,128)(2,1)S(1)}, bf16[3,1,8,8,256]{4,3,2,1,0:T(8,128)(2,1)}, u32[]{:S(2)}) copy-start(bf16[3,1,8,8,256]{4,3,2,1,0:T(8,128)(2,1)} %param.7) | copy-start | bytes 294916
  49.4 23.1 %copy-start.2 = (f32[480,256]{1,0:T(8,128)}, f32[480,256]{1,0:T(8,128)S(1)}, u32[]{:S(2)}) copy-start(f32[480,256]{1,0:T(8,128)S(1)} %get-tuple-element.83.refs_4_) | copy-start | bytes 1474564
  75.2 5.9 %collective-permute-start.8 = (bf16[192,256]{1,0:T(8,128)(2,1)S(1)}, bf16[192,256]{1,0:T(8,128)(2,1)S(1)}, u32[]{:S(2)}, u32[]{:S(2)}) collective-permute-start(bf16[192,256]{1,0:T(8,128)(2,1)S(1)} %get-tuple-element.73.refs_1_), channel_id=1, source_target_pairs={{1,2},{3,4},{5,6},{9,10},{11,12},{13,14},{17,18},{19,20},{21,22},{... | collective-permute-start | bytes 294920 | tf_op jit(solution)/shard_map/ppermute | solution.py:575
  77.1 4.0 %collective-permute-start.7 = (bf16[192,256]{1,0:T(8,128)(2,1)S(1)}, bf16[192,256]{1,0:T(8,128)(2,1)S(1)}, u32[]{:S(2)}, u32[]{:S(2)}) collective-permute-start(bf16[192,256]{1,0:T(8,128)(2,1)S(1)} %get-tuple-element.73.refs_1_), channel_id=1, source_target_pairs={{0,1},{1,0},{2,3},{3,2},{4,5},{5,4},{6,7},{7,6},{8,9},{9,8},{10,11... | collective-permute-start | bytes 294920 | tf_op jit(solution)/shard_map/ppermute | solution.py:574
  77.2 2.6 %collective-permute-start.9 = (bf16[16,256]{1,0:T(8,128)(2,1)S(1)}, bf16[16,256]{1,0:T(8,128)(2,1)S(1)}, u32[]{:S(2)}, u32[]{:S(2)}) collective-permute-start(bf16[16,256]{1,0:T(8,128)(2,1)S(1)} %get-tuple-element.74), channel_id=1, source_target_pairs={{0,8},{1,9},{2,10},{3,11},{4,12},{5,13},{6,14},{7,15},{16,24},{17,... | collective-permute-start | bytes 24584 | tf_op jit(solution)/shard_map/ppermute | solution.py:576
  77.3 2.5 %collective-permute-start.10 = (bf16[16,256]{1,0:T(8,128)(2,1)S(1)}, bf16[16,256]{1,0:T(8,128)(2,1)S(1)}, u32[]{:S(2)}, u32[]{:S(2)}) collective-permute-start(bf16[16,256]{1,0:T(8,128)(2,1)S(1)} %get-tuple-element.75), channel_id=1, source_target_pairs={{8,16},{9,17},{10,18},{11,19},{12,20},{13,21},{14,22},{15,23},{40,... | collective-permute-start | bytes 24584 | tf_op jit(solution)/shard_map/ppermute | solution.py:577
  83.3 0.7 copy-start.5
  84.0 24.1 %all-to-all-start.2 = ((bf16[16,64,256]{2,1,0:T(8,128)(2,1)}), bf16[16,64,256]{2,1,0:T(8,128)(2,1)S(1)}, u32[]{:S(2)}, u32[]{:S(2)}) async-start(bf16[16,64,256]{2,1,0:T(8,128)(2,1)} %get-tuple-element.79), calls=%async_computation.2 | async-start | bytes 1048576 | tf_op jit(solution)/shard_map/all_to_all | solution.py:462
  88.9 9.7 %collective-permute-start.13 = (bf16[864,256]{1,0:T(8,128)(2,1)}, bf16[864,256]{1,0:T(8,128)(2,1)S(1)}, u32[]{:S(2)}, u32[]{:S(2)}) collective-permute-start(bf16[864,256]{1,0:T(8,128)(2,1)} %get-tuple-element.80.own), channel_id=1, source_target_pairs={{0,1},{1,0},{2,3},{3,2},{4,5},{5,4},{6,7},{7,6},{8,9},{9,8},{10,11... | collective-permute-start | bytes 1327112 | tf_op jit(solution)/shard_map/ppermute | solution.py:641
  89.0 24.2 %collective-permute-start.6 = (bf16[576,256]{1,0:T(8,128)(2,1)}, bf16[576,256]{1,0:T(8,128)(2,1)S(1)}, u32[]{:S(2)}, u32[]{:S(2)}) collective-permute-start(bf16[576,256]{1,0:T(8,128)(2,1)} %get-tuple-element.69.source), channel_id=1, source_target_pairs={{0,1},{1,0},{2,3},{3,2},{4,5},{5,4},{6,7},{7,6},{8,9},{9,8},{10,11... | collective-permute-start | bytes 884744 | tf_op jit(solution)/shard_map/ppermute | solution.py:604
  89.5 6.5 %collective-permute-start.11 = (bf16[96,256]{1,0:T(8,128)(2,1)S(1)}, bf16[96,256]{1,0:T(8,128)(2,1)S(1)}, u32[]{:S(2)}, u32[]{:S(2)}) collective-permute-start(bf16[96,256]{1,0:T(8,128)(2,1)S(1)} %get-tuple-element.77), channel_id=1, source_target_pairs={{0,8},{1,9},{2,10},{3,11},{4,12},{5,13},{6,14},{7,15},{16,24},{17,... | collective-permute-start | bytes 147464 | tf_op jit(solution)/shard_map/ppermute | solution.py:625
  92.7 3.3 %collective-permute-start.12 = (bf16[96,256]{1,0:T(8,128)(2,1)S(1)}, bf16[96,256]{1,0:T(8,128)(2,1)S(1)}, u32[]{:S(2)}, u32[]{:S(2)}) collective-permute-start(bf16[96,256]{1,0:T(8,128)(2,1)S(1)} %get-tuple-element.78), channel_id=1, source_target_pairs={{8,16},{9,17},{10,18},{11,19},{12,20},{13,21},{14,22},{15,23},{24,... | collective-permute-start | bytes 147464 | tf_op jit(solution)/shard_map/ppermute | solution.py:625
  96.0 0.9 copy-start.6
  98.5 9.6 %copy-start.3 = (f32[480,256]{1,0:T(8,128)S(1)}, f32[480,256]{1,0:T(8,128)}, u32[]{:S(2)}) copy-start(f32[480,256]{1,0:T(8,128)} %copy-done.2) | copy-start | bytes 1474564
  108.1 0.9 copy-start.11
  111.5 1.6 collective-permute-start.14
  115.3 27.0 %all-to-all-start.3 = ((bf16[16,144,256]{2,1,0:T(8,128)(2,1)}), bf16[16,144,256]{2,1,0:T(8,128)(2,1)S(1)}, u32[]{:S(2)}, u32[]{:S(2)}) async-start(bf16[16,144,256]{2,1,0:T(8,128)(2,1)} %shard_map.95), calls=%async_computation.3 | async-start | bytes 2359296 | tf_op jit(solution)/shard_map/all_to_all | solution.py:669
  122.5 28.2 %copy-start.14 = (bf16[192,256]{1,0:T(8,128)(2,1)S(1)}, bf16[192,256]{1,0:T(8,128)(2,1)}, u32[]{:S(2)}) copy-start(bf16[192,256]{1,0:T(8,128)(2,1)} %get-tuple-element.99.pick) | copy-start | bytes 294916
  122.5 4.2 %collective-permute-start.17 = (bf16[48,256]{1,0:T(8,128)(2,1)S(1)}, bf16[48,256]{1,0:T(8,128)(2,1)S(1)}, u32[]{:S(2)}, u32[]{:S(2)}) collective-permute-start(bf16[48,256]{1,0:T(8,128)(2,1)S(1)} %get-tuple-element.95.one), channel_id=1, source_target_pairs={{0,192},{64,0},{128,64},{192,128},{1,193},{65,1},{129,65},{193,129... | collective-permute-start | bytes 73736 | tf_op jit(solution)/shard_map/ppermute | solution.py:668
  124.8 3.7 %collective-permute-start.16 = (bf16[48,256]{1,0:T(8,128)(2,1)S(1)}, bf16[48,256]{1,0:T(8,128)(2,1)S(1)}, u32[]{:S(2)}, u32[]{:S(2)}) collective-permute-start(bf16[48,256]{1,0:T(8,128)(2,1)S(1)} %get-tuple-element.95.one), channel_id=1, source_target_pairs={{0,128},{64,192},{128,0},{192,64},{1,129},{65,193},{129,1},{193,65... | collective-permute-start | bytes 73736 | tf_op jit(solution)/shard_map/ppermute | solution.py:668
  125.5 4.8 %collective-permute-start.15 = (bf16[48,256]{1,0:T(8,128)(2,1)S(1)}, bf16[48,256]{1,0:T(8,128)(2,1)S(1)}, u32[]{:S(2)}, u32[]{:S(2)}) collective-permute-start(bf16[48,256]{1,0:T(8,128)(2,1)S(1)} %get-tuple-element.95.one), channel_id=1, source_target_pairs={{0,64},{64,128},{128,192},{192,0},{1,65},{65,129},{129,193},{193,1... | collective-permute-start | bytes 73736 | tf_op jit(solution)/shard_map/ppermute | solution.py:668
  143.8 29.6 %all-to-all-start.4 = ((bf16[8,144,256]{2,1,0:T(8,128)(2,1)}), bf16[8,144,256]{2,1,0:T(8,128)(2,1)S(1)}, u32[]{:S(2)}, u32[]{:S(2)}) async-start(bf16[8,144,256]{2,1,0:T(8,128)(2,1)} %shard_map.96), calls=%async_computation.4 | async-start | bytes 1179648 | tf_op jit(solution)/shard_map/all_to_all | solution.py:676
  151.4 10.5 %collective-permute-start.18 = (bf16[48,256]{1,0:T(8,128)(2,1)S(1)}, bf16[48,256]{1,0:T(8,128)(2,1)S(1)}, u32[]{:S(2)}, u32[]{:S(2)}) collective-permute-start(bf16[48,256]{1,0:T(8,128)(2,1)S(1)} %get-tuple-element.100), channel_id=1, source_target_pairs={{0,7},{1,6},{2,5},{3,4},{4,3},{5,2},{6,1},{7,0},{8,15},{9,14},{10,... | collective-permute-start | bytes 73736 | tf_op jit(solution)/shard_map/ppermute | solution.py:675
  153.8 16.3 %collective-permute-start.19 = (bf16[48,256]{1,0:T(8,128)(2,1)S(1)}, bf16[48,256]{1,0:T(8,128)(2,1)S(1)}, u32[]{:S(2)}, u32[]{:S(2)}) collective-permute-start(bf16[48,256]{1,0:T(8,128)(2,1)S(1)} %get-tuple-element.101), channel_id=1, source_target_pairs={{0,56},{1,57},{2,58},{3,59},{4,60},{5,61},{6,62},{7,63},{8,48},{9,... | collective-permute-start | bytes 73736 | tf_op jit(solution)/shard_map/ppermute | solution.py:675
  161.6 11.9 %collective-permute-start.20 = (bf16[48,256]{1,0:T(8,128)(2,1)S(1)}, bf16[48,256]{1,0:T(8,128)(2,1)S(1)}, u32[]{:S(2)}, u32[]{:S(2)}) collective-permute-start(bf16[48,256]{1,0:T(8,128)(2,1)S(1)} %get-tuple-element.102), channel_id=1, source_target_pairs={{0,63},{1,62},{2,61},{3,60},{4,59},{5,58},{6,57},{7,56},{8,55},{9,... | collective-permute-start | bytes 73736 | tf_op jit(solution)/shard_map/ppermute | solution.py:675
  175.1 25.3 %all-to-all-start.5 = ((bf16[16,144,256]{2,1,0:T(8,128)(2,1)}), bf16[16,144,256]{2,1,0:T(8,128)(2,1)S(1)}, u32[]{:S(2)}, u32[]{:S(2)}) async-start(bf16[16,144,256]{2,1,0:T(8,128)(2,1)} %shard_map.98), calls=%async_computation.5 | async-start | bytes 2359296 | tf_op jit(solution)/shard_map/all_to_all | solution.py:688
  200.4 3.1 %collective-permute-start.21 = (bf16[16,144,256]{2,1,0:T(8,128)(2,1)S(1)}, bf16[16,144,256]{2,1,0:T(8,128)(2,1)S(1)}, u32[]{:S(2)}, u32[]{:S(2)}) collective-permute-start(bf16[16,144,256]{2,1,0:T(8,128)(2,1)S(1)} %all-to-all-done.5.refs_1_), channel_id=1, source_target_pairs={{0,1},{1,0},{2,3},{3,2},{4,5},{5,4},{6,7},{7,6},{8,9},{9,8},{10,11... | collective-permute-start | bytes 3538952 | tf_op jit(solution)/shard_map/ppermute | solution.py:691

commit v12 on v11

--- a/solution.py
+++ b/solution.py
@@ -176,12 +176,33 @@
     second[...] = jnp.where(even, up, down).astype(BF16)
 
 
-def ends_kernel(pos, own, first, second, cells, ends):
+def own_rim_kernel(pos, own, send, cells, strips):
+    row, col = pos[0], pos[1]
     cells[...] = own[...].astype(F32)
-    post_ends(pos[0], pos[1], cells, first, second, ends)
-
-
-def widen(pos, own, swapped, odd, end_one, end_two, wide, first, second, cells, ends, strips, length):
+    for f in range(3):
+        at = f * 64
+        strips[16 * f : 16 * f + 8, :] = jnp.where(row >= 4, cells[at + 56 : at + 64, :], cells[at : at + 8, :])
+        for i in range(8):
+            left, right = cells[at + 8 * i : at + 8 * i + 1, :], cells[at + 8 * i + 7 : at + 8 * i + 8, :]
+            strips[16 * f + 8 + i : 16 * f + 9 + i, :] = jnp.where(col >= 4, right, left)
+    post_strips(strips, send)
+
+
+def beyond_kernel(pos, got, pick, lines, core_ends, odd_ends, even_rows, near_rows, ends):
+    row, col = pos[0], pos[1]
+    lines[...] = dot(pick[...], got[...], ((1,), (0,)))
+    ends[...] = jnp.zeros_like(ends)
+    for kind, even, first, second in ((0, col % 2 == 0, core_ends, odd_ends), (1, row % 2 == 0, even_rows, near_rows)):
+        for f in range(3):
+            at = (2 * f + kind) * 12
+            ends[2 * f : 2 * f + 2, :] = lines[at + 2 : at + 4, :]
+            ends[16 + 2 * f : 18 + 2 * f, :] = lines[at + 8 : at + 10, :]
+        begin, end = ends[0:16, :], ends[16:32, :]
+        first[...] = jnp.where(even, end, begin).astype(BF16)
+        second[...] = jnp.where(even, begin, end).astype(BF16)
+
+
+def widen(pos, own, swapped, odd, wide, first, second, cells):
     row, col = pos[0], pos[1]
     even = col % 2 == 0
     cells[...] = jnp.zeros_like(cells)
@@ -193,17 +214,23 @@
     cells[:, 10:12, :] = right[:, 0:2, :]
     wide[...] = cells[...].reshape(24 * PITCH, C).astype(BF16)
     even = row % 2 == 0
-    one, two = end_one[...].astype(F32), end_two[...].astype(F32)
-    ends[0:16, :] = jnp.where(even, two, one)
-    ends[16:32, :] = jnp.where(even, one, two)
     for f in range(3):
         up = cells[8 * f : 8 * f + 2].reshape(2 * PITCH, C)
         down = cells[8 * f + 6 : 8 * f + 8].reshape(2 * PITCH, C)
         first[2 * f * PITCH : (2 * f + 2) * PITCH, :] = jnp.where(even, down, up).astype(BF16)
         second[2 * f * PITCH : (2 * f + 2) * PITCH, :] = jnp.where(even, up, down).astype(BF16)
-        at = 2 * f * length
+
+
+def long_strips(pos, end_one, end_two, cells, ends, strips):
+    row, col = pos[0], pos[1]
+    even = row % 2 == 0
+    one, two = end_one[...].astype(F32), end_two[...].astype(F32)
+    ends[0:16, :] = jnp.where(even, two, one)
+    ends[16:32, :] = jnp.where(even, one, two)
+    for f in range(3):
+        at = 2 * f * PITCH
         strips[at : at + 12, :] = jnp.where(row >= 4, cells[8 * f + 7, 0:12, :], cells[8 * f, 0:12, :])
-        at = (2 * f + 1) * length
+        at = (2 * f + 1) * PITCH
         strips[at : at + 2, :] = ends[2 * f : 2 * f + 2, :]
         for i in range(8):
             rim = jnp.where(col >= 4, cells[8 * f + i, 9:10, :], cells[8 * f + i, 2:3, :])
@@ -211,17 +238,13 @@
         strips[at + 10 : at + 12, :] = ends[16 + 2 * f : 18 + 2 * f, :]
 
 
-def input_kernel(pos, own, swapped, odd, end_one, end_two, wide, first, second, send, cells, ends, strips):
-    widen(pos, own, swapped, odd, end_one, end_two, wide, first, second, cells, ends, strips, 12)
-    post_strips(strips, send)
-
-
 def rim_kernel(
     pos, own, swapped, odd, end_one, end_two, fetched, wide, first, second, send, cells, ends, lines, strips
 ):
     row, col = pos[0], pos[1]
     lines[...] = jnp.zeros_like(lines)
-    widen(pos, own, swapped, odd, end_one, end_two, wide, first, second, cells, ends, lines, PITCH)
+    widen(pos, own, swapped, odd, wide, first, second, cells)
+    long_strips(pos, end_one, end_two, cells, ends, lines)
     bottom, right = 2 * (row // 4), 2 * (col // 4)
     kernel = fetched()
     totals = []
@@ -259,10 +282,19 @@
 
 
 def one_kernel(
-    pos, wide, first, second, got, pick, fetched, filled, pre, hidden, send, cells, shifts, strips, lines
+    pos, wide, first, second, arrived, core_ends, odd_ends, even_rows, near_rows, fetched, *refs
 ):
-    row, col = pos[0], pos[1]
-    lines[...] = dot(pick[...], got[...], ((1,), (0,)))
+    filled, pre, hidden, send, cells, shifts, strips, lines, ends = refs
+    row, col = pos[0], pos[1]
+    lines[...] = arrived[...]
+    for kind, even, one, two in ((0, col % 2 == 0, core_ends, odd_ends), (1, row % 2 == 0, even_rows, near_rows)):
+        one, two = one[...].astype(F32), two[...].astype(F32)
+        ends[0:16, :] = jnp.where(even, two, one)
+        ends[16:32, :] = jnp.where(even, one, two)
+        for f in range(3):
+            at = (2 * f + kind) * 12
+            lines[at : at + 2, :] = lines[at : at + 2, :] + ends[2 * f : 2 * f + 2, :]
+            lines[at + 10 : at + 12, :] = lines[at + 10 : at + 12, :] + ends[16 + 2 * f : 18 + 2 * f, :]
     stack_lines(row, wide, first, second, cells)
     fill_strips(cells, lines, row, col, 12, 1, 10, 12)
     filled[...] = cells[0 : 36 * PITCH, :].astype(BF16)
@@ -463,7 +495,7 @@
     return got.reshape(-1, C)
 
 
-def picks_kernel(pos, nexts, codes, pick_12, pick_10, add_10, share):
+def picks_kernel(pos, nexts, codes, pick_8, pick_10, add_10, share):
     row, col, group = pos[0], pos[1], pos[3]
     bottom, right = row // 4, col // 4
     mirror = right + 2 * bottom
@@ -477,7 +509,7 @@
         rel = 2 * opposite + reverse if kind == 0 else 2 * reverse + opposite
         return nexts[face, side], rel, reverse
 
-    for length, block, out in ((12, 72, pick_12), (10, 64, pick_10)):
+    for length, spare, block, out in ((8, 2, 48, pick_8), (10, 0, 64, pick_10)):
         rows = out.shape[0]
         at_row = lax.broadcasted_iota(jnp.int32, (rows, 128), 0)
         lane = lax.broadcasted_iota(jnp.int32, (rows, 128), 1)
@@ -487,17 +519,18 @@
                 across, rel, reverse = seam(3 * group + k, kind, bottom if kind == 0 else 2 + right)
                 slot_mirror = mirror ^ rel
                 slot = (lax.div(across, 3) * 4 + slot_mirror) * block + (lax.rem(across, 3) * 2 + kind) * length
-                here = at_row - (2 * k + kind) * length
+                here = at_row - (2 * k + kind) * (length + 2 * spare) - spare
                 at = jnp.where(reverse == 1, length - 1 - here, here)
                 place = slot + at
-                if length == 12 and kind == 1:
-                    upper = slot_mirror < 2
-                    high = jnp.where(centre & upper, length - 2, far)
-                    low = jnp.where(centre & (slot_mirror >= 2), 1, -1)
-                    place = jnp.where(at >= high, place + 2 * block - 8, place)
-                    place = jnp.where(at <= low, place - 2 * block + 8, place)
                 inside = (here >= begins[kind]) & (here < length)
                 target = jnp.where(inside, place, target)
+                if spare and kind == 1:
+                    beside = centre & (begins[1] == 0)
+                    above = jnp.where(beside & (slot_mirror < 2), length, far)
+                    below = jnp.where(beside & (slot_mirror >= 2), -spare, far)
+                    near = (here >= -spare) & (here < length + spare)
+                    target = jnp.where(near & (at >= above), place + 2 * block - length, target)
+                    target = jnp.where(near & (at >= below) & (at < 0), place - 2 * block + length, target)
         for c in range(0, 16 * block, 128):
             out[:, c : c + 128] = (lane + c == target).astype(F32).astype(BF16)
 
@@ -551,7 +584,7 @@
 def seam_picks(pos, nexts, codes):
     return pl.pallas_call(
         picks_kernel,
-        out_shape=[jax.ShapeDtypeStruct(shape, BF16) for shape in ((80, 1152), (64, 1024), (64, 1024), (192, 256))],
+        out_shape=[jax.ShapeDtypeStruct(shape, BF16) for shape in ((80, 768), (64, 1024), (64, 1024), (192, 256))],
         in_specs=[pl.BlockSpec(memory_space=pltpu.SMEM)] * 3,
         out_specs=[pl.BlockSpec(memory_space=pltpu.VMEM)] * 4,
     )(pos, nexts, codes)
@@ -578,27 +611,31 @@
         )
 
     x = inputs.reshape(192, C)
-    first, second = run(ends_kernel, ends, [((192, C), F32), ((32, C), F32)], pos, x)
-    wide, first, second, send = run(
-        input_kernel,
-        regions + [((16, 72, C), BF16)],
-        [((24, PITCH, C), F32), ((32, C), F32), ((72, C), F32)],
-        pos,
-        *beside(x, first, second),
-    )
-    send, neighbour, seam_codes = lax.optimization_barrier((send, neighbour, seam_codes))
-    pick_12, pick_10, add_10, add_8 = seam_picks(pos, neighbour, seam_codes)
+    send = run(own_rim_kernel, [((16, 48, C), BF16)], [((192, C), F32), ((48, C), F32)], pos, x)[0]
+    send, x, neighbour, seam_codes = lax.optimization_barrier((send, x, neighbour, seam_codes))
+    got = seam_exchange(send)
+    pick_8, pick_10, add_10, add_8 = seam_picks(pos, neighbour, seam_codes)
+    swapped, odd = lax.ppermute(x, "core", CORES), lax.ppermute(x, TILE, ODD_COLS)
+    wide, first, second = run(widen, regions, [((24, PITCH, C), F32)], pos, x, swapped, odd)
     first, second = lax.ppermute(first, TILE, EVEN_ROWS), lax.ppermute(second, TILE, ODD_ROWS)
+    got, wide, first, second = lax.optimization_barrier((got, wide, first, second))
+    arrived, *sides = run(beyond_kernel, [((80, C), F32)] + ends * 2, [((32, C), F32)], pos, got, pick_8)
+    sides = [
+        lax.ppermute(sides[0], "core", CORES),
+        lax.ppermute(sides[1], TILE, ODD_COLS),
+        lax.ppermute(sides[2], TILE, EVEN_ROWS),
+        lax.ppermute(sides[3], TILE, NEAR_ROWS),
+    ]
     filled, pre_one, hidden, send = run(
         one_kernel,
         [((flat, C), BF16), ((30 * PITCH, C), F32), ((30 * PITCH, C), BF16), ((16, 64, C), BF16)],
-        [((spare, C), F32), ((flat, C), BF16), ((64, C), F32), ((80, C), F32)],
+        [((spare, C), F32), ((flat, C), BF16), ((64, C), F32), ((80, C), F32), ((32, C), F32)],
         pos,
         wide,
         first,
         second,
-        seam_exchange(send),
-        pick_12,
+        arrived,
+        *sides,
         taps=kernel_one,
     )
     filled_other = lax.ppermute(filled, "core", CORES)
@@ -672,9 +709,9 @@
     part, *faces = lax.optimization_barrier((part, *faces))
     strip = (48, C)
     mine, *shares = run(share_kernel, [(strip, F32)] + [(strip, BF16)] * 3, [], pos, *faces, add_8)
-    shares = [lax.ppermute(v, TILE, [(t, t ^ m) for t in range(64)]) for v, m in zip(shares, MIRRORS[1:])]
     part = lax.all_to_all(part, AXES, 0, 0, axis_index_groups=ACROSS_GROUPS)
     part, *shares = lax.optimization_barrier((part, *shares))
+    shares = [lax.ppermute(v, TILE, [(t, t ^ m) for t in range(64)]) for v, m in zip(shares, MIRRORS[1:])]
     part = run(gather_kernel, [((16, 144, C), BF16)], [], pos, part)[0]
     input_grad = run(
         final_kernel,

time: 207 us -> 199 us (0.961)
  waiting for transfers between devices: 78.1 us -> 62.5 us
  starting transfers between devices: 65.8 us -> 68.4 us
  blocking collectives: 23.1 us -> 25.6 us
    all_to_all x2, waiting for transfers between devices: 32.4 us -> 12.1 us  [body(): part = lax.all_to_all(part, AXES, 0, 0, axis_index_groups=PLANE_GROUPS)]
    all_to_all x1, waiting for transfers between devices: 0.01 us -> 14.6 us  [body(): part = lax.all_to_all(part, AXES, 0, 0, axis_index_groups=ACROSS_GROUPS)]
    all_to_all x2, waiting for transfers between devices: 23.9 us -> 12.9 us  [seam_exchange(): got = lax.all_to_all(send, AXES, 0, 0, axis_index_groups=SEAM_GROUPS)]
    ppermute x0 -> x6, waiting for transfers between devices: none -> 6.47 us  [the longest x1 4.2 us: body(): lax.ppermute(x, TILE, ODD_COLS)]
    ppermute x0 -> x6, starting transfers between devices: none -> 4.78 us  [the longest x1 1.92 us: body(): lax.ppermute(x, TILE, ODD_COLS)]
    ppermute x3, waiting for transfers between devices: 11.5 us -> 6.82 us  [body(): lax.ppermute(v, TILE, [(t, t ^ m) for t in range(64)])]
    ppermute x2 -> x1, starting transfers between devices: 6.65 us -> 2.04 us  [beside(): lax.ppermute(field, TILE, ODD_COLS)]
    ppermute x3, starting transfers between devices: 10.5 us -> 13.5 us  [body(): lax.ppermute(v, TILE, [(t, t ^ m) for t in range(64)])]
  transfers between devices with their start and end apart: 27 -> 29, of which waited for: 13 -> 14; matrix products, arithmetic and copies ran while one was open for 1% -> 1% of each run, Pallas kernels for 7% -> 8%
where the time goes in v12:
time: 199 us; the launch traced here: 197 us
  starting transfers between devices  68.4 us (34%)
  waiting for transfers between devices  62.5 us (31%)
  Pallas kernels  31.5 us (16%)
  blocking collectives  25.6 us (13%)
  local copies, waits for them, and re-layouts  7.75 us (4%)
    all_to_all x1, blocking collectives, seam_exchange(): got = lax.all_to_all(send, AXES, 0, 0, axis_index_groups=SEAM_GROUPS)  25.6 us
    pallas_call x15, Pallas kernels, run(): pl.pallas_call(inner, out_shape=[jax.ShapeDtypeStruct(shape, dtype) for s...  24.7 us
    all_to_all x2, starting transfers between devices, seam_exchange(): got = lax.all_to_all(send, AXES, 0, 0, axis_index_groups=SEAM_GROUPS)  20.1 us
    all_to_all x1, waiting for transfers between devices, body(): part = lax.all_to_all(part, AXES, 0, 0, axis_index_groups=ACROSS_GROUPS)  14.6 us
    ppermute x3, starting transfers between devices, body(): lax.ppermute(v, TILE, [(t, t ^ m) for t in range(64)])  13.5 us
    all_to_all x2, waiting for transfers between devices, seam_exchange(): got = lax.all_to_all(send, AXES, 0, 0, axis_index_groups=SEAM_GROUPS)  12.9 us
    all_to_all x2, waiting for transfers between devices, body(): part = lax.all_to_all(part, AXES, 0, 0, axis_index_groups=PLANE_GROUPS)  12.1 us
    all_to_all x2, starting transfers between devices, body(): part = lax.all_to_all(part, AXES, 0, 0, axis_index_groups=PLANE_GROUPS)  11.1 us
  transfers between devices with their start and end apart: 29, of which 14 were waited for; matrix products, arithmetic and copies ran while one was open for 1% of the time, Pallas kernels for 8%

profile of v12, /device:TPU:1, one launch (start us, length us, event | category | flops | bytes accessed | tf_op | source)
XLA Modules:
  0.0 197.0 jit_solution(9198884632510987051)
XLA Ops:
  0.7 1.0 copy-done.4
  1.7 1.3 shard_map.85
  3.0 14.3 %all-to-all-start = ((bf16[16,48,256]{2,1,0:T(8,128)(2,1)}), bf16[16,48,256]{2,1,0:T(8,128)(2,1)S(1)}, u32[]{:S(2)}, u32[]{:S(2)}) async-start(bf16[16,48,256]{2,1,0:T(8,128)(2,1)} %shard_map.85), calls=%async_computation | async-start | bytes 786432 | tf_op jit(solution)/shard_map/all_to_all | solution.py:494
  17.4 1.9 collective-permute-start.1
  19.4 4.2 %collective-permute-done.1.odd = bf16[192,256]{1,0:T(8,128)(2,1)S(1)} collective-permute-done((bf16[192,256]{1,0:T(8,128)(2,1)S(1)}, bf16[192,256]{1,0:T(8,128)(2,1)S(1)}, u32[]{:S(2)}, u32[]{:S(2)}) %collective-permute-start.1) | collective-permute-done | bytes 98336 | tf_op jit(solution)/shard_map/ppermute | solution.py:618
  26.5 2.6 %shard_map.87 = (bf16[80,768]{1,0:T(8,128)(2,1)}, bf16[64,1024]{1,0:T(8,128)(2,1)}, bf16[64,1024]{1,0:T(8,128)(2,1)}, bf16[192,256]{1,0:T(8,128)(2,1)}) custom-call(s32[4]{0:T(128)} %copy-done.8, s32[12,4]{1,0:T(8,128)} %copy.11.nexts, s32[12,4]{1,0:T(8,128)} %copy.12.codes), custom_call_target="tpu_custom_call" | custom-call | tf_op jit(solution)/shard_map/pallas_call | solution.py:585
  29.1 4.9 %all-to-all-done = bf16[16,48,256]{2,1,0:T(8,128)(2,1)S(1)} async-done(((bf16[16,48,256]{2,1,0:T(8,128)(2,1)}), bf16[16,48,256]{2,1,0:T(8,128)(2,1)S(1)}, u32[]{:S(2)}, u32[]{:S(2)}) %all-to-all-start) | async-done | bytes 393248 | tf_op jit(solution)/shard_map/all_to_all | solution.py:494
  34.6 0.9 copy-done.14
  36.4 1.9 collective-permute-start.5
  39.1 2.3 %collective-permute-done.5.refs_6_ = bf16[16,256]{1,0:T(8,128)(2,1)S(1)} collective-permute-done((bf16[16,256]{1,0:T(8,128)(2,1)S(1)}, bf16[16,256]{1,0:T(8,128)(2,1)S(1)}, u32[]{:S(2)}, u32[]{:S(2)}) %collective-permute-start.5) | collective-permute-done | bytes 8224 | tf_op jit(solution)/shard_map/ppermute | solution.py:625
  42.0 2.3 %shard_map.89 = (bf16[576,256]{1,0:T(8,128)(2,1)}, f32[480,256]{1,0:T(8,128)S(1)}, bf16[480,256]{1,0:T(8,128)(2,1)S(1)}, bf16[16,64,256]{2,1,0:T(8,128)(2,1)S(1)}) custom-call(s32[4]{0:T(128)S(1)} %copy-done.10, bf16[384,256]{1,0:T(8,128)(2,1)S(1)} %get-tuple-element.71.refs_1_, bf16[96,256]{1,0:T(8,128)(2,1)S(1)} %collective-permute-done.2.refs_2_, ...), custom_call_target="tpu_custom_call" | custom-call | tf_op jit(solution)/shard_map/pallas_call | solution.py:79
  45.1 25.6 %all_to_all.30 = bf16[16,64,256]{2,1,0:T(8,128)(2,1)S(1)} all-to-all(bf16[16,64,256]{2,1,0:T(8,128)(2,1)S(1)} %get-tuple-element.85), channel_id=1, replica_groups={{0,7,56,63,64,71,120,127,128,135,184,191,192,199,248,255},{1,6,57,62,65..., dimensions={0} | all-to-all | bytes 1048576 | tf_op jit(solution)/shard_map/all_to_all | solution.py:494
  70.6 2.6 %shard_map.90 = (bf16[864,256]{1,0:T(8,128)(2,1)}, bf16[192,256]{1,0:T(8,128)(2,1)S(1)}, bf16[16,256]{1,0:T(8,128)(2,1)S(1)}, bf16[16,256]{1,0:T(8,128)(2,1)S(1)}) custom-call(s32[4]{0:T(128)S(1)} %copy-done.10, bf16[480,256]{1,0:T(8,128)(2,1)S(1)} %get-tuple-element.84.refs_1_, bf16[1024,256]{1,0:T(8,128)(2,1)S(1)} %bitcast.14, ...), custom_call_target="tpu_custom_call" | custom-call | tf_op jit(solution)/shard_map/pallas_call | solution.py:79
  73.3 2.0 %collective-permute-start.10 = (bf16[192,256]{1,0:T(8,128)(2,1)S(1)}, bf16[192,256]{1,0:T(8,128)(2,1)S(1)}, u32[]{:S(2)}, u32[]{:S(2)}) collective-permute-start(bf16[192,256]{1,0:T(8,128)(2,1)S(1)} %get-tuple-element.87.refs_1_), channel_id=1, source_target_pairs={{1,2},{3,4},{5,6},{9,10},{11,12},{13,14},{17,18},{19,20},{21,22},{... | collective-permute-start | bytes 294920 | tf_op jit(solution)/shard_map/ppermute | solution.py:608
  76.2 1.8 collective-permute-done.11.refs_4_
  78.0 1.2 collective-permute-done.10.refs_3_
  79.2 2.2 %shard_map.91 = (bf16[384,256]{1,0:T(8,128)(2,1)S(1)}, bf16[96,256]{1,0:T(8,128)(2,1)S(1)}, bf16[96,256]{1,0:T(8,128)(2,1)S(1)}, bf16[16,64,256]{2,1,0:T(8,128)(2,1)}) custom-call(s32[4]{0:T(128)S(1)} %copy-done.10, bf16[192,256]{1,0:T(8,128)(2,1)S(1)} %get-tuple-element.87.refs_1_, bf16[192,256]{1,0:T(8,128)(2,1)S(1)} %collective-permute-done.9.refs_2_, ...), custom_call_target="tpu_custom_call" | custom-call | tf_op jit(solution)/shard_map/pallas_call | solution.py:79
  82.1 5.7 %all-to-all-start.2 = ((bf16[16,64,256]{2,1,0:T(8,128)(2,1)}), bf16[16,64,256]{2,1,0:T(8,128)(2,1)S(1)}, u32[]{:S(2)}, u32[]{:S(2)}) async-start(bf16[16,64,256]{2,1,0:T(8,128)(2,1)} %get-tuple-element.93), calls=%async_computation.2 | async-start | bytes 1048576 | tf_op jit(solution)/shard_map/all_to_all | solution.py:494
  88.4 3.2 %collective-permute-start.13 = (bf16[96,256]{1,0:T(8,128)(2,1)S(1)}, bf16[96,256]{1,0:T(8,128)(2,1)S(1)}, u32[]{:S(2)}, u32[]{:S(2)}) collective-permute-start(bf16[96,256]{1,0:T(8,128)(2,1)S(1)} %get-tuple-element.91), channel_id=1, source_target_pairs={{0,8},{1,9},{2,10},{3,11},{4,12},{5,13},{6,14},{7,15},{16,24},{17,... | collective-permute-start | bytes 147464 | tf_op jit(solution)/shard_map/ppermute | solution.py:662
  92.3 2.2 %collective-permute-done.13.refs_2_ = bf16[96,256]{1,0:T(8,128)(2,1)S(1)} collective-permute-done((bf16[96,256]{1,0:T(8,128)(2,1)S(1)}, bf16[96,256]{1,0:T(8,128)(2,1)S(1)}, u32[]{:S(2)}, u32[]{:S(2)}) %collective-permute-start.13) | collective-permute-done | bytes 49184 | tf_op jit(solution)/shard_map/ppermute | solution.py:662
  94.5 0.9 copy-done.7
  95.4 1.6 shard_map.92.refs_1_
  97.1 1.9 shard_map.93.two
  99.0 8.0 %all-to-all-done.2 = bf16[16,64,256]{2,1,0:T(8,128)(2,1)S(1)} async-done(((bf16[16,64,256]{2,1,0:T(8,128)(2,1)}), bf16[16,64,256]{2,1,0:T(8,128)(2,1)S(1)}, u32[]{:S(2)}, u32[]{:S(2)}) %all-to-all-start.2) | async-done | bytes 524320 | tf_op jit(solution)/shard_map/all_to_all | solution.py:494
  107.0 0.9 copy-done.12
  107.9 2.5 %shard_map.94 = (bf16[384,256]{1,0:T(8,128)(2,1)S(1)}, bf16[192,256]{1,0:T(8,128)(2,1)S(1)}, bf16[48,256]{1,0:T(8,128)(2,1)S(1)}) custom-call(s32[4]{0:T(128)S(1)} %copy-done.11, bf16[480,256]{1,0:T(8,128)(2,1)S(1)} %shard_map.92.refs_1_, bf16[1024,256]{1,0:T(8,128)(2,1)S(1)} %bitcast.15, bf16[64,1024]{1,0:T(8,128)(2,1)S(1)} %copy-done.12, ...), custom_call_target="tpu_custom_call" | custom-call | tf_op jit(solution)/shard_map/pallas_call | solution.py:79
  110.5 1.5 shard_map.95.part
  112.1 2.1 %shard_map.96 = bf16[16,144,256]{2,1,0:T(8,128)(2,1)} custom-call(s32[4]{0:T(128)S(1)} %copy-done.11, bf16[576,256]{1,0:T(8,128)(2,1)S(1)} %collective-permute-done.8.source, bf16[384,256]{1,0:T(8,128)(2,1)S(1)} %collective-permute-done.16.delta, f32[16,72,256]{2,1,0:T(8,128)S(1)} %shard_map.95.part, bf16[16,72,256]{2,1,0:T(8,128)(2,1)S(1)} %shard_map.93.two), custom_call_target="tpu_custom_call" | custom-call | tf_op jit(solution)/shard_map/pallas_call | solution.py:79
  114.2 7.4 %all-to-all-start.3 = ((bf16[16,144,256]{2,1,0:T(8,128)(2,1)}), bf16[16,144,256]{2,1,0:T(8,128)(2,1)S(1)}, u32[]{:S(2)}, u32[]{:S(2)}) async-start(bf16[16,144,256]{2,1,0:T(8,128)(2,1)} %shard_map.96), calls=%async_computation.3 | async-start | bytes 2359296 | tf_op jit(solution)/shard_map/all_to_all | solution.py:706
  121.6 2.1 %collective-permute-start.19 = (bf16[48,256]{1,0:T(8,128)(2,1)S(1)}, bf16[48,256]{1,0:T(8,128)(2,1)S(1)}, u32[]{:S(2)}, u32[]{:S(2)}) collective-permute-start(bf16[48,256]{1,0:T(8,128)(2,1)S(1)} %get-tuple-element.109.one), channel_id=1, source_target_pairs={{0,192},{64,0},{128,64},{192,128},{1,193},{65,1},{129,65},{193,129... | collective-permute-start | bytes 73736 | tf_op jit(solution)/shard_map/ppermute | solution.py:705
  123.7 0.9 collective-permute-start.18
  124.6 1.0 collective-permute-start.17
  125.6 1.9 collective-permute-done.18.three
  127.6 1.8 collective-permute-done.17.two
  129.4 12.1 %all-to-all-done.3.parts = bf16[16,144,256]{2,1,0:T(8,128)(2,1)S(1)} async-done(((bf16[16,144,256]{2,1,0:T(8,128)(2,1)}), bf16[16,144,256]{2,1,0:T(8,128)(2,1)S(1)}, u32[]{:S(2)}, u32[]{:S(2)}) %all-to-all-start.3) | async-done | bytes 1179680 | tf_op jit(solution)/shard_map/all_to_all | solution.py:706
  141.5 1.5 shard_map.97
  143.0 6.6 %all-to-all-start.4 = ((bf16[8,144,256]{2,1,0:T(8,128)(2,1)}), bf16[8,144,256]{2,1,0:T(8,128)(2,1)S(1)}, u32[]{:S(2)}, u32[]{:S(2)}) async-start(bf16[8,144,256]{2,1,0:T(8,128)(2,1)} %shard_map.97), calls=%async_computation.4 | async-start | bytes 1179648 | tf_op jit(solution)/shard_map/all_to_all | solution.py:712
  150.3 14.6 %all-to-all-done.4.parts = bf16[8,144,256]{2,1,0:T(8,128)(2,1)S(1)} async-done(((bf16[8,144,256]{2,1,0:T(8,128)(2,1)}), bf16[8,144,256]{2,1,0:T(8,128)(2,1)S(1)}, u32[]{:S(2)}, u32[]{:S(2)}) %all-to-all-start.4) | async-done | bytes 589856 | tf_op jit(solution)/shard_map/all_to_all | solution.py:712
  164.9 1.6 shard_map.99
  166.5 3.7 %all-to-all-start.5 = ((bf16[16,144,256]{2,1,0:T(8,128)(2,1)}), bf16[16,144,256]{2,1,0:T(8,128)(2,1)S(1)}, u32[]{:S(2)}, u32[]{:S(2)}) async-start(bf16[16,144,256]{2,1,0:T(8,128)(2,1)} %shard_map.99), calls=%async_computation.5 | async-start | bytes 2359296 | tf_op jit(solution)/shard_map/all_to_all | solution.py:725
  170.2 6.0 %collective-permute-start.20 = (bf16[48,256]{1,0:T(8,128)(2,1)S(1)}, bf16[48,256]{1,0:T(8,128)(2,1)S(1)}, u32[]{:S(2)}, u32[]{:S(2)}) collective-permute-start(bf16[48,256]{1,0:T(8,128)(2,1)S(1)} %get-tuple-element.120), channel_id=1, source_target_pairs={{0,7},{1,6},{2,5},{3,4},{4,3},{5,2},{6,1},{7,0},{8,15},{9,14},{10,... | collective-permute-start | bytes 73736 | tf_op jit(solution)/shard_map/ppermute | solution.py:714
  176.2 3.0 %collective-permute-start.21 = (bf16[48,256]{1,0:T(8,128)(2,1)S(1)}, bf16[48,256]{1,0:T(8,128)(2,1)S(1)}, u32[]{:S(2)}, u32[]{:S(2)}) collective-permute-start(bf16[48,256]{1,0:T(8,128)(2,1)S(1)} %get-tuple-element.121), channel_id=1, source_target_pairs={{0,56},{1,57},{2,58},{3,59},{4,60},{5,61},{6,62},{7,63},{8,48},{9,... | collective-permute-start | bytes 73736 | tf_op jit(solution)/shard_map/ppermute | solution.py:714
  179.2 4.6 %collective-permute-start.22 = (bf16[48,256]{1,0:T(8,128)(2,1)S(1)}, bf16[48,256]{1,0:T(8,128)(2,1)S(1)}, u32[]{:S(2)}, u32[]{:S(2)}) collective-permute-start(bf16[48,256]{1,0:T(8,128)(2,1)S(1)} %get-tuple-element.122), channel_id=1, source_target_pairs={{0,63},{1,62},{2,61},{3,60},{4,59},{5,58},{6,57},{7,56},{8,55},{9,... | collective-permute-start | bytes 73736 | tf_op jit(solution)/shard_map/ppermute | solution.py:714
  183.8 3.6 %collective-permute-done.20.by_col = bf16[48,256]{1,0:T(8,128)(2,1)S(1)} collective-permute-done((bf16[48,256]{1,0:T(8,128)(2,1)S(1)}, bf16[48,256]{1,0:T(8,128)(2,1)S(1)}, u32[]{:S(2)}, u32[]{:S(2)}) %collective-permute-start.20) | collective-permute-done | bytes 24608 | tf_op jit(solution)/shard_map/ppermute | solution.py:714
  187.4 3.2 %collective-permute-done.22.by_both = bf16[48,256]{1,0:T(8,128)(2,1)S(1)} collective-permute-done((bf16[48,256]{1,0:T(8,128)(2,1)S(1)}, bf16[48,256]{1,0:T(8,128)(2,1)S(1)}, u32[]{:S(2)}, u32[]{:S(2)}) %collective-permute-start.22) | collective-permute-done | bytes 24608 | tf_op jit(solution)/shard_map/ppermute | solution.py:714
  190.6 1.3 shard_map.100
  191.9 2.1 %shard_map.101 = (f32[9,256,256]{2,1,0:T(8,128)}, f32[9,256,256]{2,1,0:T(8,128)}) custom-call(s32[4]{0:T(128)S(1)} %copy-done.11, bf16[16,144,256]{2,1,0:T(8,128)(2,1)S(1)} %all-to-all-done.5.refs_1_), custom_call_target="tpu_custom_call" | custom-call | tf_op jit(solution)/shard_map/pallas_call | solution.py:482
  194.7 2.1 %shard_map.102 = (f32[9,256,256]{2,1,0:T(8,128)}, f32[9,256,256]{2,1,0:T(8,128)}) custom-call(s32[4]{0:T(128)S(1)} %copy-done.11, bf16[16,144,256]{2,1,0:T(8,128)(2,1)S(1)} %collective-permute-done.23.refs_1_, f32[9,256,256]{2,1,0:T(8,128)} %get-tuple-element.125.refs_2_, ...), custom_call_target="tpu_custom_call", output_to_operand_aliasing={{0}: (2, {}), {1}: (3, {})} | custom-call | tf_op jit(solution)/shard_map/pallas_call | solution.py:482
  (70 shorter events, 10.9 us)
Async XLA Ops:
  0.6 40.7 %copy-start.1 = (bf16[3,3,256,256]{3,2,1,0:T(8,128)(2,1)S(1)}, bf16[3,3,256,256]{3,2,1,0:T(8,128)(2,1)}, u32[]{:S(2)}) copy-start(bf16[3,3,256,256]{3,2,1,0:T(8,128)(2,1)} %refs_5_.3) | copy-start | bytes 3538948
  0.7 25.7 %copy-start.8 = (s32[4]{0:T(128)}, s32[4]{0:T(128)S(1)}, u32[]{:S(2)}) copy-start(s32[4]{0:T(128)S(1)} %pad_add_fusion.pos.refs_0_) | copy-start | bytes 52
  0.7 1.0 copy-start.4
  1.7 15.7 %copy-start.5 = (bf16[3,1,8,8,256]{4,3,2,1,0:T(8,128)(2,1)S(1)}, bf16[3,1,8,8,256]{4,3,2,1,0:T(8,128)(2,1)}, u32[]{:S(2)}) copy-start(bf16[3,1,8,8,256]{4,3,2,1,0:T(8,128)(2,1)} %param.6) | copy-start | bytes 294916
  1.7 23.4 %copy-start.17 = (s32[12,4]{0,1:T(4,128)S(1)}, s32[12,4]{0,1:T(4,128)}, u32[]{:S(2)}) copy-start(s32[12,4]{0,1:T(4,128)} %param.10) | copy-start | bytes 580
  1.7 24.1 %copy-start.18 = (s32[12,4]{0,1:T(4,128)S(1)}, s32[12,4]{0,1:T(4,128)}, u32[]{:S(2)}) copy-start(s32[12,4]{0,1:T(4,128)} %param.11) | copy-start | bytes 580
  3.0 30.9 %all-to-all-start = ((bf16[16,48,256]{2,1,0:T(8,128)(2,1)}), bf16[16,48,256]{2,1,0:T(8,128)(2,1)S(1)}, u32[]{:S(2)}, u32[]{:S(2)}) async-start(bf16[16,48,256]{2,1,0:T(8,128)(2,1)} %shard_map.85), calls=%async_computation | async-start | bytes 786432 | tf_op jit(solution)/shard_map/all_to_all | solution.py:494
  17.4 6.2 %collective-permute-start.1 = (bf16[192,256]{1,0:T(8,128)(2,1)S(1)}, bf16[192,256]{1,0:T(8,128)(2,1)S(1)}, u32[]{:S(2)}, u32[]{:S(2)}) collective-permute-start(bf16[192,256]{1,0:T(8,128)(2,1)S(1)} %bitcast.18), channel_id=1, source_target_pairs={{1,2},{3,4},{5,6},{9,10},{11,12},{13,14},{17,18},{19,20},{21,22},{... | collective-permute-start | bytes 294920 | tf_op jit(solution)/shard_map/ppermute | solution.py:618
  19.3 4.3 %collective-permute-start = (bf16[192,256]{1,0:T(8,128)(2,1)S(1)}, bf16[192,256]{1,0:T(8,128)(2,1)S(1)}, u32[]{:S(2)}, u32[]{:S(2)}) collective-permute-start(bf16[192,256]{1,0:T(8,128)(2,1)S(1)} %bitcast.19), channel_id=1, source_target_pairs={{0,1},{1,0},{2,3},{3,2},{4,5},{5,4},{6,7},{7,6},{8,9},{9,8},{10,11... | collective-permute-start | bytes 294920 | tf_op jit(solution)/shard_map/ppermute | solution.py:618
  24.3 4.8 %collective-permute-start.2 = (bf16[96,256]{1,0:T(8,128)(2,1)S(1)}, bf16[96,256]{1,0:T(8,128)(2,1)S(1)}, u32[]{:S(2)}, u32[]{:S(2)}) collective-permute-start(bf16[96,256]{1,0:T(8,128)(2,1)S(1)} %get-tuple-element.69), channel_id=1, source_target_pairs={{0,8},{1,9},{2,10},{3,11},{4,12},{5,13},{6,14},{7,15},{16,24},{17,... | collective-permute-start | bytes 147464 | tf_op jit(solution)/shard_map/ppermute | solution.py:620
  24.4 4.7 %collective-permute-start.3 = (bf16[96,256]{1,0:T(8,128)(2,1)S(1)}, bf16[96,256]{1,0:T(8,128)(2,1)S(1)}, u32[]{:S(2)}, u32[]{:S(2)}) collective-permute-start(bf16[96,256]{1,0:T(8,128)(2,1)S(1)} %get-tuple-element.70), channel_id=1, source_target_pairs={{8,16},{9,17},{10,18},{11,19},{12,20},{13,21},{14,22},{15,23},{24,... | collective-permute-start | bytes 147464 | tf_op jit(solution)/shard_map/ppermute | solution.py:620
  34.0 0.6 copy-start.9
  34.6 0.9 copy-start.14
  36.3 2.8 %collective-permute-start.4 = (bf16[16,256]{1,0:T(8,128)(2,1)S(1)}, bf16[16,256]{1,0:T(8,128)(2,1)S(1)}, u32[]{:S(2)}, u32[]{:S(2)}) collective-permute-start(bf16[16,256]{1,0:T(8,128)(2,1)S(1)} %get-tuple-element.79), channel_id=1, source_target_pairs={{0,1},{1,0},{2,3},{3,2},{4,5},{5,4},{6,7},{7,6},{8,9},{9,8},{10,11... | collective-permute-start | bytes 24584 | tf_op jit(solution)/shard_map/ppermute | solution.py:624
  36.4 5.0 %collective-permute-start.5 = (bf16[16,256]{1,0:T(8,128)(2,1)S(1)}, bf16[16,256]{1,0:T(8,128)(2,1)S(1)}, u32[]{:S(2)}, u32[]{:S(2)}) collective-permute-start(bf16[16,256]{1,0:T(8,128)(2,1)S(1)} %get-tuple-element.80), channel_id=1, source_target_pairs={{1,2},{3,4},{5,6},{9,10},{11,12},{13,14},{17,18},{19,20},{21,22},{... | collective-permute-start | bytes 24584 | tf_op jit(solution)/shard_map/ppermute | solution.py:625
  38.3 3.0 %collective-permute-start.6 = (bf16[16,256]{1,0:T(8,128)(2,1)S(1)}, bf16[16,256]{1,0:T(8,128)(2,1)S(1)}, u32[]{:S(2)}, u32[]{:S(2)}) collective-permute-start(bf16[16,256]{1,0:T(8,128)(2,1)S(1)} %get-tuple-element.81), channel_id=1, source_target_pairs={{0,8},{1,9},{2,10},{3,11},{4,12},{5,13},{6,14},{7,15},{16,24},{17,... | collective-permute-start | bytes 24584 | tf_op jit(solution)/shard_map/ppermute | solution.py:626
  38.4 2.9 %collective-permute-start.7 = (bf16[16,256]{1,0:T(8,128)(2,1)S(1)}, bf16[16,256]{1,0:T(8,128)(2,1)S(1)}, u32[]{:S(2)}, u32[]{:S(2)}) collective-permute-start(bf16[16,256]{1,0:T(8,128)(2,1)S(1)} %get-tuple-element.82), channel_id=1, source_target_pairs={{8,16},{9,17},{10,18},{11,19},{12,20},{13,21},{14,22},{15,23},{40,... | collective-permute-start | bytes 24584 | tf_op jit(solution)/shard_map/ppermute | solution.py:627
  41.3 0.6 copy-start.10
  42.0 28.7 %copy-start = (bf16[3,3,256,256]{3,2,1,0:T(8,128)(2,1)S(1)}, bf16[3,3,256,256]{3,2,1,0:T(8,128)(2,1)}, u32[]{:S(2)}) copy-start(bf16[3,3,256,256]{3,2,1,0:T(8,128)(2,1)} %refs_4_.1) | copy-start | bytes 3538948
  42.0 28.7 %copy-start.13 = (bf16[64,1024]{1,0:T(8,128)(2,1)S(1)}, bf16[64,1024]{1,0:T(8,128)(2,1)}, u32[]{:S(2)}) copy-start(bf16[64,1024]{1,0:T(8,128)(2,1)} %get-tuple-element.86.refs_3_) | copy-start | bytes 393220
  42.0 28.7 %copy-start.15 = (bf16[3,1,8,8,256]{4,3,2,1,0:T(8,128)(2,1)S(1)}, bf16[3,1,8,8,256]{4,3,2,1,0:T(8,128)(2,1)}, u32[]{:S(2)}) copy-start(bf16[3,1,8,8,256]{4,3,2,1,0:T(8,128)(2,1)} %param.7) | copy-start | bytes 294916
  44.3 0.8 copy-start.2
  73.3 5.9 %collective-permute-start.10 = (bf16[192,256]{1,0:T(8,128)(2,1)S(1)}, bf16[192,256]{1,0:T(8,128)(2,1)S(1)}, u32[]{:S(2)}, u32[]{:S(2)}) collective-permute-start(bf16[192,256]{1,0:T(8,128)(2,1)S(1)} %get-tuple-element.87.refs_1_), channel_id=1, source_target_pairs={{1,2},{3,4},{5,6},{9,10},{11,12},{13,14},{17,18},{19,20},{21,22},{... | collective-permute-start | bytes 294920 | tf_op jit(solution)/shard_map/ppermute | solution.py:608
  75.3 3.9 %collective-permute-start.9 = (bf16[192,256]{1,0:T(8,128)(2,1)S(1)}, bf16[192,256]{1,0:T(8,128)(2,1)S(1)}, u32[]{:S(2)}, u32[]{:S(2)}) collective-permute-start(bf16[192,256]{1,0:T(8,128)(2,1)S(1)} %get-tuple-element.87.refs_1_), channel_id=1, source_target_pairs={{0,1},{1,0},{2,3},{3,2},{4,5},{5,4},{6,7},{7,6},{8,9},{9,8},{10,11... | collective-permute-start | bytes 294920 | tf_op jit(solution)/shard_map/ppermute | solution.py:607
  75.4 2.6 %collective-permute-start.11 = (bf16[16,256]{1,0:T(8,128)(2,1)S(1)}, bf16[16,256]{1,0:T(8,128)(2,1)S(1)}, u32[]{:S(2)}, u32[]{:S(2)}) collective-permute-start(bf16[16,256]{1,0:T(8,128)(2,1)S(1)} %get-tuple-element.88), channel_id=1, source_target_pairs={{0,8},{1,9},{2,10},{3,11},{4,12},{5,13},{6,14},{7,15},{16,24},{17,... | collective-permute-start | bytes 24584 | tf_op jit(solution)/shard_map/ppermute | solution.py:609
  75.5 19.0 %copy-start.11 = (s32[4]{0:T(128)S(1)}, s32[4]{0:T(128)}, u32[]{:S(2)}) copy-start(s32[4]{0:T(128)} %copy-done.8) | copy-start | bytes 52
  75.5 2.5 %collective-permute-start.12 = (bf16[16,256]{1,0:T(8,128)(2,1)S(1)}, bf16[16,256]{1,0:T(8,128)(2,1)S(1)}, u32[]{:S(2)}, u32[]{:S(2)}) collective-permute-start(bf16[16,256]{1,0:T(8,128)(2,1)S(1)} %get-tuple-element.89), channel_id=1, source_target_pairs={{8,16},{9,17},{10,18},{11,19},{12,20},{13,21},{14,22},{15,23},{40,... | collective-permute-start | bytes 24584 | tf_op jit(solution)/shard_map/ppermute | solution.py:610
  81.4 0.7 copy-start.6
  82.1 24.9 %all-to-all-start.2 = ((bf16[16,64,256]{2,1,0:T(8,128)(2,1)}), bf16[16,64,256]{2,1,0:T(8,128)(2,1)S(1)}, u32[]{:S(2)}, u32[]{:S(2)}) async-start(bf16[16,64,256]{2,1,0:T(8,128)(2,1)} %get-tuple-element.93), calls=%async_computation.2 | async-start | bytes 1048576 | tf_op jit(solution)/shard_map/all_to_all | solution.py:494
  87.8 9.3 %collective-permute-start.15 = (bf16[864,256]{1,0:T(8,128)(2,1)}, bf16[864,256]{1,0:T(8,128)(2,1)S(1)}, u32[]{:S(2)}, u32[]{:S(2)}) collective-permute-start(bf16[864,256]{1,0:T(8,128)(2,1)} %get-tuple-element.94.own), channel_id=1, source_target_pairs={{0,1},{1,0},{2,3},{3,2},{4,5},{5,4},{6,7},{7,6},{8,9},{9,8},{10,11... | collective-permute-start | bytes 1327112 | tf_op jit(solution)/shard_map/ppermute | solution.py:678
  87.9 24.1 %collective-permute-start.8 = (bf16[576,256]{1,0:T(8,128)(2,1)}, bf16[576,256]{1,0:T(8,128)(2,1)S(1)}, u32[]{:S(2)}, u32[]{:S(2)}) collective-permute-start(bf16[576,256]{1,0:T(8,128)(2,1)} %get-tuple-element.83.source), channel_id=1, source_target_pairs={{0,1},{1,0},{2,3},{3,2},{4,5},{5,4},{6,7},{7,6},{8,9},{9,8},{10,11... | collective-permute-start | bytes 884744 | tf_op jit(solution)/shard_map/ppermute | solution.py:641
  88.4 6.1 %collective-permute-start.13 = (bf16[96,256]{1,0:T(8,128)(2,1)S(1)}, bf16[96,256]{1,0:T(8,128)(2,1)S(1)}, u32[]{:S(2)}, u32[]{:S(2)}) collective-permute-start(bf16[96,256]{1,0:T(8,128)(2,1)S(1)} %get-tuple-element.91), channel_id=1, source_target_pairs={{0,8},{1,9},{2,10},{3,11},{4,12},{5,13},{6,14},{7,15},{16,24},{17,... | collective-permute-start | bytes 147464 | tf_op jit(solution)/shard_map/ppermute | solution.py:662
  91.7 2.8 %collective-permute-start.14 = (bf16[96,256]{1,0:T(8,128)(2,1)S(1)}, bf16[96,256]{1,0:T(8,128)(2,1)S(1)}, u32[]{:S(2)}, u32[]{:S(2)}) collective-permute-start(bf16[96,256]{1,0:T(8,128)(2,1)S(1)} %get-tuple-element.92), channel_id=1, source_target_pairs={{8,16},{9,17},{10,18},{11,19},{12,20},{13,21},{14,22},{15,23},{24,... | collective-permute-start | bytes 147464 | tf_op jit(solution)/shard_map/ppermute | solution.py:662
  94.5 0.9 copy-start.7
  97.1 9.9 %copy-start.3 = (f32[480,256]{1,0:T(8,128)S(1)}, f32[480,256]{1,0:T(8,128)}, u32[]{:S(2)}) copy-start(f32[480,256]{1,0:T(8,128)} %copy-done.2) | copy-start | bytes 1474564
  107.0 0.9 copy-start.12
  110.4 1.6 collective-permute-start.16
  114.2 27.3 %all-to-all-start.3 = ((bf16[16,144,256]{2,1,0:T(8,128)(2,1)}), bf16[16,144,256]{2,1,0:T(8,128)(2,1)S(1)}, u32[]{:S(2)}, u32[]{:S(2)}) async-start(bf16[16,144,256]{2,1,0:T(8,128)(2,1)} %shard_map.96), calls=%async_computation.3 | async-start | bytes 2359296 | tf_op jit(solution)/shard_map/all_to_all | solution.py:706
  121.6 28.0 %copy-start.16 = (bf16[192,256]{1,0:T(8,128)(2,1)S(1)}, bf16[192,256]{1,0:T(8,128)(2,1)}, u32[]{:S(2)}) copy-start(bf16[192,256]{1,0:T(8,128)(2,1)} %get-tuple-element.113.pick) | copy-start | bytes 294916
  121.6 4.0 %collective-permute-start.19 = (bf16[48,256]{1,0:T(8,128)(2,1)S(1)}, bf16[48,256]{1,0:T(8,128)(2,1)S(1)}, u32[]{:S(2)}, u32[]{:S(2)}) collective-permute-start(bf16[48,256]{1,0:T(8,128)(2,1)S(1)} %get-tuple-element.109.one), channel_id=1, source_target_pairs={{0,192},{64,0},{128,64},{192,128},{1,193},{65,1},{129,65},{193,129... | collective-permute-start | bytes 73736 | tf_op jit(solution)/shard_map/ppermute | solution.py:705
  123.7 3.9 %collective-permute-start.18 = (bf16[48,256]{1,0:T(8,128)(2,1)S(1)}, bf16[48,256]{1,0:T(8,128)(2,1)S(1)}, u32[]{:S(2)}, u32[]{:S(2)}) collective-permute-start(bf16[48,256]{1,0:T(8,128)(2,1)S(1)} %get-tuple-element.109.one), channel_id=1, source_target_pairs={{0,128},{64,192},{128,0},{192,64},{1,129},{65,193},{129,1},{193,65... | collective-permute-start | bytes 73736 | tf_op jit(solution)/shard_map/ppermute | solution.py:705
  124.6 4.8 %collective-permute-start.17 = (bf16[48,256]{1,0:T(8,128)(2,1)S(1)}, bf16[48,256]{1,0:T(8,128)(2,1)S(1)}, u32[]{:S(2)}, u32[]{:S(2)}) collective-permute-start(bf16[48,256]{1,0:T(8,128)(2,1)S(1)} %get-tuple-element.109.one), channel_id=1, source_target_pairs={{0,64},{64,128},{128,192},{192,0},{1,65},{65,129},{129,193},{193,1... | collective-permute-start | bytes 73736 | tf_op jit(solution)/shard_map/ppermute | solution.py:705
  143.0 21.9 %all-to-all-start.4 = ((bf16[8,144,256]{2,1,0:T(8,128)(2,1)}), bf16[8,144,256]{2,1,0:T(8,128)(2,1)S(1)}, u32[]{:S(2)}, u32[]{:S(2)}) async-start(bf16[8,144,256]{2,1,0:T(8,128)(2,1)} %shard_map.97), calls=%async_computation.4 | async-start | bytes 1179648 | tf_op jit(solution)/shard_map/all_to_all | solution.py:712
  166.5 25.3 %all-to-all-start.5 = ((bf16[16,144,256]{2,1,0:T(8,128)(2,1)}), bf16[16,144,256]{2,1,0:T(8,128)(2,1)S(1)}, u32[]{:S(2)}, u32[]{:S(2)}) async-start(bf16[16,144,256]{2,1,0:T(8,128)(2,1)} %shard_map.99), calls=%async_computation.5 | async-start | bytes 2359296 | tf_op jit(solution)/shard_map/all_to_all | solution.py:725
  170.2 17.2 %collective-permute-start.20 = (bf16[48,256]{1,0:T(8,128)(2,1)S(1)}, bf16[48,256]{1,0:T(8,128)(2,1)S(1)}, u32[]{:S(2)}, u32[]{:S(2)}) collective-permute-start(bf16[48,256]{1,0:T(8,128)(2,1)S(1)} %get-tuple-element.120), channel_id=1, source_target_pairs={{0,7},{1,6},{2,5},{3,4},{4,3},{5,2},{6,1},{7,0},{8,15},{9,14},{10,... | collective-permute-start | bytes 73736 | tf_op jit(solution)/shard_map/ppermute | solution.py:714
  176.2 11.2 %collective-permute-start.21 = (bf16[48,256]{1,0:T(8,128)(2,1)S(1)}, bf16[48,256]{1,0:T(8,128)(2,1)S(1)}, u32[]{:S(2)}, u32[]{:S(2)}) collective-permute-start(bf16[48,256]{1,0:T(8,128)(2,1)S(1)} %get-tuple-element.121), channel_id=1, source_target_pairs={{0,56},{1,57},{2,58},{3,59},{4,60},{5,61},{6,62},{7,63},{8,48},{9,... | collective-permute-start | bytes 73736 | tf_op jit(solution)/shard_map/ppermute | solution.py:714
  179.2 11.4 %collective-permute-start.22 = (bf16[48,256]{1,0:T(8,128)(2,1)S(1)}, bf16[48,256]{1,0:T(8,128)(2,1)S(1)}, u32[]{:S(2)}, u32[]{:S(2)}) collective-permute-start(bf16[48,256]{1,0:T(8,128)(2,1)S(1)} %get-tuple-element.122), channel_id=1, source_target_pairs={{0,63},{1,62},{2,61},{3,60},{4,59},{5,58},{6,57},{7,56},{8,55},{9,... | collective-permute-start | bytes 73736 | tf_op jit(solution)/shard_map/ppermute | solution.py:714
  191.9 2.8 %collective-permute-start.23 = (bf16[16,144,256]{2,1,0:T(8,128)(2,1)S(1)}, bf16[16,144,256]{2,1,0:T(8,128)(2,1)S(1)}, u32[]{:S(2)}, u32[]{:S(2)}) collective-permute-start(bf16[16,144,256]{2,1,0:T(8,128)(2,1)S(1)} %all-to-all-done.5.refs_1_), channel_id=1, source_target_pairs={{0,1},{1,0},{2,3},{3,2},{4,5},{5,4},{6,7},{7,6},{8,9},{9,8},{10,11... | collective-permute-start | bytes 3538952 | tf_op jit(solution)/shard_map/ppermute | solution.py:728

commit v13 on v12

--- a/solution.py
+++ b/solution.py
@@ -51,7 +51,6 @@
     for zh in range(2)
     for core in range(2)
 ]
-ACROSS_GROUPS = [[f * 64 + (t ^ m) for f in range(4) for m in (0, 56)] for t in range(32)]
 
 
 def run(kernel, outs, scratch, pos, *args, taps=None):
@@ -443,20 +442,19 @@
         out[i] = jnp.concatenate([sums[i].astype(BF16), two[i]], axis=0)
 
 
-def across_kernel(pos, parts, out):
+def plane_kernel(pos, parts, out):
     total = parts[0].astype(F32)
     for i in range(1, 16):
         total = total + parts[i].astype(F32)
-    total = total.astype(BF16)
-    for i in range(8):
-        out[i] = total
-
-
-def gather_kernel(pos, parts, out):
-    total = parts[0].astype(F32)
-    for i in range(1, 8):
-        total = total + parts[i].astype(F32)
-    total = total.astype(BF16)
+    out[...] = total.astype(BF16)
+
+
+def add_kernel(pos, one, two, out):
+    out[...] = (one[...].astype(F32) + two[...].astype(F32)).astype(BF16)
+
+
+def gather_kernel(pos, one, two, out):
+    total = (one[...].astype(F32) + two[...].astype(F32)).astype(BF16)
     for i in range(16):
         out[i] = total
 
@@ -704,15 +702,17 @@
     part, strips = lax.optimization_barrier((part, strips))
     faces = [strips] + [lax.ppermute(strips, "face", [(i, (i + by) % 4) for i in range(4)]) for by in (1, 2, 3)]
     part = lax.all_to_all(part, AXES, 0, 0, axis_index_groups=PLANE_GROUPS)
-    part, *faces = lax.optimization_barrier((part, *faces))
-    part = run(across_kernel, [((8, 144, C), BF16)], [], pos, part)[0]
-    part, *faces = lax.optimization_barrier((part, *faces))
     strip = (48, C)
     mine, *shares = run(share_kernel, [(strip, F32)] + [(strip, BF16)] * 3, [], pos, *faces, add_8)
-    part = lax.all_to_all(part, AXES, 0, 0, axis_index_groups=ACROSS_GROUPS)
-    part, *shares = lax.optimization_barrier((part, *shares))
     shares = [lax.ppermute(v, TILE, [(t, t ^ m) for t in range(64)]) for v, m in zip(shares, MIRRORS[1:])]
-    part = run(gather_kernel, [((16, 144, C), BF16)], [], pos, part)[0]
+    piece = [((144, C), BF16)]
+    part = run(plane_kernel, piece, [], pos, part)[0]
+    for by in (1, 2):
+        got = lax.ppermute(part, "face", [(i, i ^ by) for i in range(4)])
+        part = run(add_kernel, piece, [], pos, part, got)[0]
+    got = lax.ppermute(part, TILE, [(t, t ^ 56) for t in range(64)])
+    part, got, *shares = lax.optimization_barrier((part, got, *shares))
+    part = run(gather_kernel, [((16, 144, C), BF16)], [], pos, part, got)[0]
     input_grad = run(
         final_kernel,
         [((192, C), BF16)],

time: 199 us -> 215 us (1.080)
  blocking collectives: 25.6 us -> 51.2 us
  starting transfers between devices: 68.4 us -> 62.1 us
    all_to_all x0 -> x1, blocking collectives: none -> 25.6 us  [body(): part = lax.all_to_all(part, AXES, 0, 0, axis_index_groups=PLANE_GROUPS)]
    all_to_all x1 -> x0, waiting for transfers between devices: 14.6 us -> none  [body(): part = lax.all_to_all(part, AXES, 0, 0, axis_index_groups=ACROSS_GROUPS)]
    ppermute x0 -> x3, starting transfers between devices: none -> 10.1 us  [the longest x1 5.97 us: body(): got = lax.ppermute(part, TILE, [(t, t ^ 56) for t in range(64)])]
    all_to_all x2 -> x1, waiting for transfers between devices: 12.1 us -> 20.5 us  [body(): part = lax.all_to_all(part, AXES, 0, 0, axis_index_groups=PLANE_GROUPS)]
    all_to_all x2 -> x1, starting transfers between devices: 11.1 us -> 3.7 us  [body(): part = lax.all_to_all(part, AXES, 0, 0, axis_index_groups=PLANE_GROUPS)]
    all_to_all x1 -> x0, starting transfers between devices: 6.64 us -> none  [body(): part = lax.all_to_all(part, AXES, 0, 0, axis_index_groups=ACROSS_GROUPS)]
    ppermute x0 -> x3, waiting for transfers between devices: none -> 3.63 us  [the longest x2 3.63 us: body(): got = lax.ppermute(part, 'face', [(i, i ^ by) for i in range(4)])]
    ppermute x3, starting transfers between devices: 4.03 us -> 1.47 us  [body(): lax.ppermute(strips, 'face', [(i, (i + by) % 4) for i in range(4)])]
  transfers between devices with their start and end apart: 29 -> 30, of which waited for: 14 -> 16; matrix products, arithmetic and copies ran while one was open for 1% -> 1% of each run, Pallas kernels for 8% -> 7%
where the time goes in v13:
time: 215 us; the launch traced here: 214 us
  starting transfers between devices  62.1 us (29%)
  waiting for transfers between devices  60.6 us (28%)
  blocking collectives  51.2 us (24%)
  Pallas kernels  30.8 us (14%)
  local copies, waits for them, and re-layouts  7.74 us (4%)
    all_to_all x1, blocking collectives, body(): part = lax.all_to_all(part, AXES, 0, 0, axis_index_groups=PLANE_GROUPS)  25.6 us
    all_to_all x1, blocking collectives, seam_exchange(): got = lax.all_to_all(send, AXES, 0, 0, axis_index_groups=SEAM_GROUPS)  25.6 us
    pallas_call x17, Pallas kernels, run(): pl.pallas_call(inner, out_shape=[jax.ShapeDtypeStruct(shape, dtype) for s...  24 us
    all_to_all x1, waiting for transfers between devices, body(): part = lax.all_to_all(part, AXES, 0, 0, axis_index_groups=PLANE_GROUPS)  20.5 us
    all_to_all x2, starting transfers between devices, seam_exchange(): got = lax.all_to_all(send, AXES, 0, 0, axis_index_groups=SEAM_GROUPS)  20.1 us
    ppermute x3, starting transfers between devices, body(): lax.ppermute(v, TILE, [(t, t ^ m) for t in range(64)])  13.2 us
    all_to_all x2, waiting for transfers between devices, seam_exchange(): got = lax.all_to_all(send, AXES, 0, 0, axis_index_groups=SEAM_GROUPS)  12.9 us
    ppermute x3, waiting for transfers between devices, body(): lax.ppermute(v, TILE, [(t, t ^ m) for t in range(64)])  7.15 us
  transfers between devices with their start and end apart: 30, of which 16 were waited for; matrix products, arithmetic and copies ran while one was open for 1% of the time, Pallas kernels for 7%

profile of v13, /device:TPU:1, one launch (start us, length us, event | category | flops | bytes accessed | tf_op | source)
XLA Modules:
  0.0 213.7 jit_solution(7857139713001469433)
XLA Ops:
  0.7 1.0 copy-done.4
  1.7 1.3 shard_map.85
  3.0 14.3 %all-to-all-start = ((bf16[16,48,256]{2,1,0:T(8,128)(2,1)}), bf16[16,48,256]{2,1,0:T(8,128)(2,1)S(1)}, u32[]{:S(2)}, u32[]{:S(2)}) async-start(bf16[16,48,256]{2,1,0:T(8,128)(2,1)} %shard_map.85), calls=%async_computation | async-start | bytes 786432 | tf_op jit(solution)/shard_map/all_to_all | solution.py:492
  17.4 1.9 collective-permute-start.1
  19.4 4.2 %collective-permute-done.1.odd = bf16[192,256]{1,0:T(8,128)(2,1)S(1)} collective-permute-done((bf16[192,256]{1,0:T(8,128)(2,1)S(1)}, bf16[192,256]{1,0:T(8,128)(2,1)S(1)}, u32[]{:S(2)}, u32[]{:S(2)}) %collective-permute-start.1) | collective-permute-done | bytes 98336 | tf_op jit(solution)/shard_map/ppermute | solution.py:616
  26.5 2.6 %shard_map.87 = (bf16[80,768]{1,0:T(8,128)(2,1)}, bf16[64,1024]{1,0:T(8,128)(2,1)}, bf16[64,1024]{1,0:T(8,128)(2,1)}, bf16[192,256]{1,0:T(8,128)(2,1)}) custom-call(s32[4]{0:T(128)} %copy-done.6, s32[12,4]{1,0:T(8,128)} %copy.11.nexts, s32[12,4]{1,0:T(8,128)} %copy.12.codes), custom_call_target="tpu_custom_call" | custom-call | tf_op jit(solution)/shard_map/pallas_call | solution.py:583
  29.1 4.9 %all-to-all-done = bf16[16,48,256]{2,1,0:T(8,128)(2,1)S(1)} async-done(((bf16[16,48,256]{2,1,0:T(8,128)(2,1)}), bf16[16,48,256]{2,1,0:T(8,128)(2,1)S(1)}, u32[]{:S(2)}, u32[]{:S(2)}) %all-to-all-start) | async-done | bytes 393248 | tf_op jit(solution)/shard_map/all_to_all | solution.py:492
  34.6 0.9 copy-done.14
  36.4 1.9 collective-permute-start.5
  39.1 2.3 %collective-permute-done.5.refs_6_ = bf16[16,256]{1,0:T(8,128)(2,1)S(1)} collective-permute-done((bf16[16,256]{1,0:T(8,128)(2,1)S(1)}, bf16[16,256]{1,0:T(8,128)(2,1)S(1)}, u32[]{:S(2)}, u32[]{:S(2)}) %collective-permute-start.5) | collective-permute-done | bytes 8224 | tf_op jit(solution)/shard_map/ppermute | solution.py:623
  41.9 2.3 %shard_map.89 = (bf16[576,256]{1,0:T(8,128)(2,1)}, f32[480,256]{1,0:T(8,128)S(1)}, bf16[480,256]{1,0:T(8,128)(2,1)S(1)}, bf16[16,64,256]{2,1,0:T(8,128)(2,1)S(1)}) custom-call(s32[4]{0:T(128)S(1)} %copy-done.8, bf16[384,256]{1,0:T(8,128)(2,1)S(1)} %get-tuple-element.62.refs_1_, bf16[96,256]{1,0:T(8,128)(2,1)S(1)} %collective-permute-done.2.refs_2_, ...), custom_call_target="tpu_custom_call" | custom-call | tf_op jit(solution)/shard_map/pallas_call | solution.py:78
  45.1 25.6 %all_to_all.25 = bf16[16,64,256]{2,1,0:T(8,128)(2,1)S(1)} all-to-all(bf16[16,64,256]{2,1,0:T(8,128)(2,1)S(1)} %get-tuple-element.76), channel_id=1, replica_groups={{0,7,56,63,64,71,120,127,128,135,184,191,192,199,248,255},{1,6,57,62,65..., dimensions={0} | all-to-all | bytes 1048576 | tf_op jit(solution)/shard_map/all_to_all | solution.py:492
  70.6 2.6 %shard_map.90 = (bf16[864,256]{1,0:T(8,128)(2,1)}, bf16[192,256]{1,0:T(8,128)(2,1)S(1)}, bf16[16,256]{1,0:T(8,128)(2,1)S(1)}, bf16[16,256]{1,0:T(8,128)(2,1)S(1)}) custom-call(s32[4]{0:T(128)S(1)} %copy-done.8, bf16[480,256]{1,0:T(8,128)(2,1)S(1)} %get-tuple-element.75.refs_1_, bf16[1024,256]{1,0:T(8,128)(2,1)S(1)} %bitcast.14, ...), custom_call_target="tpu_custom_call" | custom-call | tf_op jit(solution)/shard_map/pallas_call | solution.py:78
  73.3 2.0 collective-permute-start.10
  76.2 1.8 collective-permute-done.11.refs_4_
  78.0 1.2 collective-permute-done.10.refs_3_
  79.2 2.2 %shard_map.91 = (bf16[384,256]{1,0:T(8,128)(2,1)S(1)}, bf16[96,256]{1,0:T(8,128)(2,1)S(1)}, bf16[96,256]{1,0:T(8,128)(2,1)S(1)}, bf16[16,64,256]{2,1,0:T(8,128)(2,1)}) custom-call(s32[4]{0:T(128)S(1)} %copy-done.8, bf16[192,256]{1,0:T(8,128)(2,1)S(1)} %get-tuple-element.78.refs_1_, bf16[192,256]{1,0:T(8,128)(2,1)S(1)} %collective-permute-done.9.refs_2_, ...), custom_call_target="tpu_custom_call" | custom-call | tf_op jit(solution)/shard_map/pallas_call | solution.py:78
  82.1 5.7 %all-to-all-start.2 = ((bf16[16,64,256]{2,1,0:T(8,128)(2,1)}), bf16[16,64,256]{2,1,0:T(8,128)(2,1)S(1)}, u32[]{:S(2)}, u32[]{:S(2)}) async-start(bf16[16,64,256]{2,1,0:T(8,128)(2,1)} %get-tuple-element.84), calls=%async_computation.2 | async-start | bytes 1048576 | tf_op jit(solution)/shard_map/all_to_all | solution.py:492
  88.4 3.3 %collective-permute-start.13 = (bf16[96,256]{1,0:T(8,128)(2,1)S(1)}, bf16[96,256]{1,0:T(8,128)(2,1)S(1)}, u32[]{:S(2)}, u32[]{:S(2)}) collective-permute-start(bf16[96,256]{1,0:T(8,128)(2,1)S(1)} %get-tuple-element.82), channel_id=1, source_target_pairs={{0,8},{1,9},{2,10},{3,11},{4,12},{5,13},{6,14},{7,15},{16,24},{17,... | collective-permute-start | bytes 147464 | tf_op jit(solution)/shard_map/ppermute | solution.py:660
  92.3 2.2 %collective-permute-done.13.refs_2_ = bf16[96,256]{1,0:T(8,128)(2,1)S(1)} collective-permute-done((bf16[96,256]{1,0:T(8,128)(2,1)S(1)}, bf16[96,256]{1,0:T(8,128)(2,1)S(1)}, u32[]{:S(2)}, u32[]{:S(2)}) %collective-permute-start.13) | collective-permute-done | bytes 49184 | tf_op jit(solution)/shard_map/ppermute | solution.py:660
  94.5 0.9 copy-done.11
  95.4 1.6 shard_map.92.refs_1_
  97.1 1.9 shard_map.93.two
  99.0 8.0 %all-to-all-done.2 = bf16[16,64,256]{2,1,0:T(8,128)(2,1)S(1)} async-done(((bf16[16,64,256]{2,1,0:T(8,128)(2,1)}), bf16[16,64,256]{2,1,0:T(8,128)(2,1)S(1)}, u32[]{:S(2)}, u32[]{:S(2)}) %all-to-all-start.2) | async-done | bytes 524320 | tf_op jit(solution)/shard_map/all_to_all | solution.py:492
  107.0 0.9 copy-done.12
  107.9 2.5 %shard_map.94 = (bf16[384,256]{1,0:T(8,128)(2,1)S(1)}, bf16[192,256]{1,0:T(8,128)(2,1)S(1)}, bf16[48,256]{1,0:T(8,128)(2,1)S(1)}) custom-call(s32[4]{0:T(128)S(1)} %copy-done.9, bf16[480,256]{1,0:T(8,128)(2,1)S(1)} %shard_map.92.refs_1_, bf16[1024,256]{1,0:T(8,128)(2,1)S(1)} %bitcast.15, bf16[64,1024]{1,0:T(8,128)(2,1)S(1)} %copy-done.12, ...), custom_call_target="tpu_custom_call" | custom-call | tf_op jit(solution)/shard_map/pallas_call | solution.py:78
  110.5 1.5 shard_map.95.part
  112.1 1.1 shard_map.96
  113.2 25.6 %all_to_all.26.parts = bf16[16,144,256]{2,1,0:T(8,128)(2,1)S(1)} all-to-all(bf16[16,144,256]{2,1,0:T(8,128)(2,1)S(1)} %shard_map.96), channel_id=1, replica_groups={{0,8,16,24,2,10,18,26,4,12,20,28,6,14,22,30},{1,9,17,25,3,11,19,27,5,13..., dimensions={0} | all-to-all | bytes 2359296 | tf_op jit(solution)/shard_map/all_to_all | solution.py:704
  139.5 1.8 collective-permute-start.17
  141.3 1.7 collective-permute-done.17.two
  143.6 2.3 %collective-permute-start.18 = (bf16[144,256]{1,0:T(8,128)(2,1)S(1)}, bf16[144,256]{1,0:T(8,128)(2,1)S(1)}, u32[]{:S(2)}, u32[]{:S(2)}) collective-permute-start(bf16[144,256]{1,0:T(8,128)(2,1)S(1)} %shard_map.98.one), channel_id=1, source_target_pairs={{0,128},{64,192},{128,0},{192,64},{1,129},{65,193},{129,1},{193,65... | collective-permute-start | bytes 221192 | tf_op jit(solution)/shard_map/ppermute | solution.py:711
  145.9 1.9 collective-permute-done.18.two
  148.4 6.0 %collective-permute-start.19 = (bf16[144,256]{1,0:T(8,128)(2,1)S(1)}, bf16[144,256]{1,0:T(8,128)(2,1)S(1)}, u32[]{:S(2)}, u32[]{:S(2)}) collective-permute-start(bf16[144,256]{1,0:T(8,128)(2,1)S(1)} %shard_map.99.one), channel_id=1, source_target_pairs={{0,56},{1,57},{2,58},{3,59},{4,60},{5,61},{6,62},{7,63},{8,48},{9,... | collective-permute-start | bytes 221192 | tf_op jit(solution)/shard_map/ppermute | solution.py:713
  154.4 1.0 collective-permute-start.22
  155.8 1.6 collective-permute-done.22.four
  157.4 2.1 collective-permute-done.21.three
  161.0 5.6 %collective-permute-start.23 = (bf16[48,256]{1,0:T(8,128)(2,1)S(1)}, bf16[48,256]{1,0:T(8,128)(2,1)S(1)}, u32[]{:S(2)}, u32[]{:S(2)}) collective-permute-start(bf16[48,256]{1,0:T(8,128)(2,1)S(1)} %get-tuple-element.95), channel_id=1, source_target_pairs={{0,7},{1,6},{2,5},{3,4},{4,3},{5,2},{6,1},{7,0},{8,15},{9,14},{10,... | collective-permute-start | bytes 73736 | tf_op jit(solution)/shard_map/ppermute | solution.py:707
  166.6 3.1 %collective-permute-start.24 = (bf16[48,256]{1,0:T(8,128)(2,1)S(1)}, bf16[48,256]{1,0:T(8,128)(2,1)S(1)}, u32[]{:S(2)}, u32[]{:S(2)}) collective-permute-start(bf16[48,256]{1,0:T(8,128)(2,1)S(1)} %get-tuple-element.96), channel_id=1, source_target_pairs={{0,56},{1,57},{2,58},{3,59},{4,60},{5,61},{6,62},{7,63},{8,48},{9,... | collective-permute-start | bytes 73736 | tf_op jit(solution)/shard_map/ppermute | solution.py:707
  169.8 4.5 %collective-permute-start.25 = (bf16[48,256]{1,0:T(8,128)(2,1)S(1)}, bf16[48,256]{1,0:T(8,128)(2,1)S(1)}, u32[]{:S(2)}, u32[]{:S(2)}) collective-permute-start(bf16[48,256]{1,0:T(8,128)(2,1)S(1)} %get-tuple-element.97), channel_id=1, source_target_pairs={{0,63},{1,62},{2,61},{3,60},{4,59},{5,58},{6,57},{7,56},{8,55},{9,... | collective-permute-start | bytes 73736 | tf_op jit(solution)/shard_map/ppermute | solution.py:707
  174.2 1.6 collective-permute-done.24.by_row
  175.8 5.6 %collective-permute-done.25.by_both = bf16[48,256]{1,0:T(8,128)(2,1)S(1)} collective-permute-done((bf16[48,256]{1,0:T(8,128)(2,1)S(1)}, bf16[48,256]{1,0:T(8,128)(2,1)S(1)}, u32[]{:S(2)}, u32[]{:S(2)}) %collective-permute-start.25) | collective-permute-done | bytes 24608 | tf_op jit(solution)/shard_map/ppermute | solution.py:707
  181.4 1.6 shard_map.101
  183.0 3.7 %all-to-all-start.4 = ((bf16[16,144,256]{2,1,0:T(8,128)(2,1)}), bf16[16,144,256]{2,1,0:T(8,128)(2,1)S(1)}, u32[]{:S(2)}, u32[]{:S(2)}) async-start(bf16[16,144,256]{2,1,0:T(8,128)(2,1)} %shard_map.101), calls=%async_computation.4 | async-start | bytes 2359296 | tf_op jit(solution)/shard_map/all_to_all | solution.py:725
  186.7 1.3 shard_map.102
  188.0 20.5 %all-to-all-done.4.refs_1_ = bf16[16,144,256]{2,1,0:T(8,128)(2,1)S(1)} async-done(((bf16[16,144,256]{2,1,0:T(8,128)(2,1)}), bf16[16,144,256]{2,1,0:T(8,128)(2,1)S(1)}, u32[]{:S(2)}, u32[]{:S(2)}) %all-to-all-start.4) | async-done | bytes 1179680 | tf_op jit(solution)/shard_map/all_to_all | solution.py:725
  209.0 2.1 shard_map.103
  211.5 2.1 shard_map.104
  (75 shorter events, 14.0 us)
Async XLA Ops:
  0.6 40.7 %copy-start.1 = (bf16[3,3,256,256]{3,2,1,0:T(8,128)(2,1)S(1)}, bf16[3,3,256,256]{3,2,1,0:T(8,128)(2,1)}, u32[]{:S(2)}) copy-start(bf16[3,3,256,256]{3,2,1,0:T(8,128)(2,1)} %refs_5_.3) | copy-start | bytes 3538948
  0.7 25.7 %copy-start.6 = (s32[4]{0:T(128)}, s32[4]{0:T(128)S(1)}, u32[]{:S(2)}) copy-start(s32[4]{0:T(128)S(1)} %pad_add_fusion.pos.refs_0_) | copy-start | bytes 52
  0.7 1.0 copy-start.4
  1.7 15.7 %copy-start.5 = (bf16[3,1,8,8,256]{4,3,2,1,0:T(8,128)(2,1)S(1)}, bf16[3,1,8,8,256]{4,3,2,1,0:T(8,128)(2,1)}, u32[]{:S(2)}) copy-start(bf16[3,1,8,8,256]{4,3,2,1,0:T(8,128)(2,1)} %param.6) | copy-start | bytes 294916
  1.7 23.4 %copy-start.17 = (s32[12,4]{0,1:T(4,128)S(1)}, s32[12,4]{0,1:T(4,128)}, u32[]{:S(2)}) copy-start(s32[12,4]{0,1:T(4,128)} %param.10) | copy-start | bytes 580
  1.7 24.1 %copy-start.18 = (s32[12,4]{0,1:T(4,128)S(1)}, s32[12,4]{0,1:T(4,128)}, u32[]{:S(2)}) copy-start(s32[12,4]{0,1:T(4,128)} %param.11) | copy-start | bytes 580
  3.0 30.9 %all-to-all-start = ((bf16[16,48,256]{2,1,0:T(8,128)(2,1)}), bf16[16,48,256]{2,1,0:T(8,128)(2,1)S(1)}, u32[]{:S(2)}, u32[]{:S(2)}) async-start(bf16[16,48,256]{2,1,0:T(8,128)(2,1)} %shard_map.85), calls=%async_computation | async-start | bytes 786432 | tf_op jit(solution)/shard_map/all_to_all | solution.py:492
  17.4 6.2 %collective-permute-start.1 = (bf16[192,256]{1,0:T(8,128)(2,1)S(1)}, bf16[192,256]{1,0:T(8,128)(2,1)S(1)}, u32[]{:S(2)}, u32[]{:S(2)}) collective-permute-start(bf16[192,256]{1,0:T(8,128)(2,1)S(1)} %bitcast.18), channel_id=1, source_target_pairs={{1,2},{3,4},{5,6},{9,10},{11,12},{13,14},{17,18},{19,20},{21,22},{... | collective-permute-start | bytes 294920 | tf_op jit(solution)/shard_map/ppermute | solution.py:616
  19.3 4.3 %collective-permute-start = (bf16[192,256]{1,0:T(8,128)(2,1)S(1)}, bf16[192,256]{1,0:T(8,128)(2,1)S(1)}, u32[]{:S(2)}, u32[]{:S(2)}) collective-permute-start(bf16[192,256]{1,0:T(8,128)(2,1)S(1)} %bitcast.19), channel_id=1, source_target_pairs={{0,1},{1,0},{2,3},{3,2},{4,5},{5,4},{6,7},{7,6},{8,9},{9,8},{10,11... | collective-permute-start | bytes 294920 | tf_op jit(solution)/shard_map/ppermute | solution.py:616
  24.3 4.8 %collective-permute-start.2 = (bf16[96,256]{1,0:T(8,128)(2,1)S(1)}, bf16[96,256]{1,0:T(8,128)(2,1)S(1)}, u32[]{:S(2)}, u32[]{:S(2)}) collective-permute-start(bf16[96,256]{1,0:T(8,128)(2,1)S(1)} %get-tuple-element.60), channel_id=1, source_target_pairs={{0,8},{1,9},{2,10},{3,11},{4,12},{5,13},{6,14},{7,15},{16,24},{17,... | collective-permute-start | bytes 147464 | tf_op jit(solution)/shard_map/ppermute | solution.py:618
  24.4 4.7 %collective-permute-start.3 = (bf16[96,256]{1,0:T(8,128)(2,1)S(1)}, bf16[96,256]{1,0:T(8,128)(2,1)S(1)}, u32[]{:S(2)}, u32[]{:S(2)}) collective-permute-start(bf16[96,256]{1,0:T(8,128)(2,1)S(1)} %get-tuple-element.61), channel_id=1, source_target_pairs={{8,16},{9,17},{10,18},{11,19},{12,20},{13,21},{14,22},{15,23},{24,... | collective-permute-start | bytes 147464 | tf_op jit(solution)/shard_map/ppermute | solution.py:618
  34.6 0.9 copy-start.14
  36.3 2.8 %collective-permute-start.4 = (bf16[16,256]{1,0:T(8,128)(2,1)S(1)}, bf16[16,256]{1,0:T(8,128)(2,1)S(1)}, u32[]{:S(2)}, u32[]{:S(2)}) collective-permute-start(bf16[16,256]{1,0:T(8,128)(2,1)S(1)} %get-tuple-element.70), channel_id=1, source_target_pairs={{0,1},{1,0},{2,3},{3,2},{4,5},{5,4},{6,7},{7,6},{8,9},{9,8},{10,11... | collective-permute-start | bytes 24584 | tf_op jit(solution)/shard_map/ppermute | solution.py:622
  36.4 5.0 %collective-permute-start.5 = (bf16[16,256]{1,0:T(8,128)(2,1)S(1)}, bf16[16,256]{1,0:T(8,128)(2,1)S(1)}, u32[]{:S(2)}, u32[]{:S(2)}) collective-permute-start(bf16[16,256]{1,0:T(8,128)(2,1)S(1)} %get-tuple-element.71), channel_id=1, source_target_pairs={{1,2},{3,4},{5,6},{9,10},{11,12},{13,14},{17,18},{19,20},{21,22},{... | collective-permute-start | bytes 24584 | tf_op jit(solution)/shard_map/ppermute | solution.py:623
  38.3 3.0 %collective-permute-start.6 = (bf16[16,256]{1,0:T(8,128)(2,1)S(1)}, bf16[16,256]{1,0:T(8,128)(2,1)S(1)}, u32[]{:S(2)}, u32[]{:S(2)}) collective-permute-start(bf16[16,256]{1,0:T(8,128)(2,1)S(1)} %get-tuple-element.72), channel_id=1, source_target_pairs={{0,8},{1,9},{2,10},{3,11},{4,12},{5,13},{6,14},{7,15},{16,24},{17,... | collective-permute-start | bytes 24584 | tf_op jit(solution)/shard_map/ppermute | solution.py:624
  38.4 2.9 %collective-permute-start.7 = (bf16[16,256]{1,0:T(8,128)(2,1)S(1)}, bf16[16,256]{1,0:T(8,128)(2,1)S(1)}, u32[]{:S(2)}, u32[]{:S(2)}) collective-permute-start(bf16[16,256]{1,0:T(8,128)(2,1)S(1)} %get-tuple-element.73), channel_id=1, source_target_pairs={{8,16},{9,17},{10,18},{11,19},{12,20},{13,21},{14,22},{15,23},{40,... | collective-permute-start | bytes 24584 | tf_op jit(solution)/shard_map/ppermute | solution.py:625
  41.3 0.6 copy-start.8
  41.9 28.7 %copy-start = (bf16[3,3,256,256]{3,2,1,0:T(8,128)(2,1)S(1)}, bf16[3,3,256,256]{3,2,1,0:T(8,128)(2,1)}, u32[]{:S(2)}) copy-start(bf16[3,3,256,256]{3,2,1,0:T(8,128)(2,1)} %refs_4_.1) | copy-start | bytes 3538948
  41.9 28.7 %copy-start.13 = (bf16[64,1024]{1,0:T(8,128)(2,1)S(1)}, bf16[64,1024]{1,0:T(8,128)(2,1)}, u32[]{:S(2)}) copy-start(bf16[64,1024]{1,0:T(8,128)(2,1)} %get-tuple-element.77.refs_3_) | copy-start | bytes 393220
  41.9 28.7 %copy-start.15 = (bf16[3,1,8,8,256]{4,3,2,1,0:T(8,128)(2,1)S(1)}, bf16[3,1,8,8,256]{4,3,2,1,0:T(8,128)(2,1)}, u32[]{:S(2)}) copy-start(bf16[3,1,8,8,256]{4,3,2,1,0:T(8,128)(2,1)} %param.7) | copy-start | bytes 294916
  44.3 0.8 copy-start.2
  73.3 5.9 %collective-permute-start.10 = (bf16[192,256]{1,0:T(8,128)(2,1)S(1)}, bf16[192,256]{1,0:T(8,128)(2,1)S(1)}, u32[]{:S(2)}, u32[]{:S(2)}) collective-permute-start(bf16[192,256]{1,0:T(8,128)(2,1)S(1)} %get-tuple-element.78.refs_1_), channel_id=1, source_target_pairs={{1,2},{3,4},{5,6},{9,10},{11,12},{13,14},{17,18},{19,20},{21,22},{... | collective-permute-start | bytes 294920 | tf_op jit(solution)/shard_map/ppermute | solution.py:606
  75.3 3.9 %collective-permute-start.9 = (bf16[192,256]{1,0:T(8,128)(2,1)S(1)}, bf16[192,256]{1,0:T(8,128)(2,1)S(1)}, u32[]{:S(2)}, u32[]{:S(2)}) collective-permute-start(bf16[192,256]{1,0:T(8,128)(2,1)S(1)} %get-tuple-element.78.refs_1_), channel_id=1, source_target_pairs={{0,1},{1,0},{2,3},{3,2},{4,5},{5,4},{6,7},{7,6},{8,9},{9,8},{10,11... | collective-permute-start | bytes 294920 | tf_op jit(solution)/shard_map/ppermute | solution.py:605
  75.4 2.6 %collective-permute-start.11 = (bf16[16,256]{1,0:T(8,128)(2,1)S(1)}, bf16[16,256]{1,0:T(8,128)(2,1)S(1)}, u32[]{:S(2)}, u32[]{:S(2)}) collective-permute-start(bf16[16,256]{1,0:T(8,128)(2,1)S(1)} %get-tuple-element.79), channel_id=1, source_target_pairs={{0,8},{1,9},{2,10},{3,11},{4,12},{5,13},{6,14},{7,15},{16,24},{17,... | collective-permute-start | bytes 24584 | tf_op jit(solution)/shard_map/ppermute | solution.py:607
  75.5 19.0 %copy-start.9 = (s32[4]{0:T(128)S(1)}, s32[4]{0:T(128)}, u32[]{:S(2)}) copy-start(s32[4]{0:T(128)} %copy-done.6) | copy-start | bytes 52
  75.5 2.5 %collective-permute-start.12 = (bf16[16,256]{1,0:T(8,128)(2,1)S(1)}, bf16[16,256]{1,0:T(8,128)(2,1)S(1)}, u32[]{:S(2)}, u32[]{:S(2)}) collective-permute-start(bf16[16,256]{1,0:T(8,128)(2,1)S(1)} %get-tuple-element.80), channel_id=1, source_target_pairs={{8,16},{9,17},{10,18},{11,19},{12,20},{13,21},{14,22},{15,23},{40,... | collective-permute-start | bytes 24584 | tf_op jit(solution)/shard_map/ppermute | solution.py:608
  81.4 0.7 copy-start.10
  82.1 24.9 %all-to-all-start.2 = ((bf16[16,64,256]{2,1,0:T(8,128)(2,1)}), bf16[16,64,256]{2,1,0:T(8,128)(2,1)S(1)}, u32[]{:S(2)}, u32[]{:S(2)}) async-start(bf16[16,64,256]{2,1,0:T(8,128)(2,1)} %get-tuple-element.84), calls=%async_computation.2 | async-start | bytes 1048576 | tf_op jit(solution)/shard_map/all_to_all | solution.py:492
  87.8 9.2 %collective-permute-start.15 = (bf16[864,256]{1,0:T(8,128)(2,1)}, bf16[864,256]{1,0:T(8,128)(2,1)S(1)}, u32[]{:S(2)}, u32[]{:S(2)}) collective-permute-start(bf16[864,256]{1,0:T(8,128)(2,1)} %get-tuple-element.85.own), channel_id=1, source_target_pairs={{0,1},{1,0},{2,3},{3,2},{4,5},{5,4},{6,7},{7,6},{8,9},{9,8},{10,11... | collective-permute-start | bytes 1327112 | tf_op jit(solution)/shard_map/ppermute | solution.py:676
  87.9 24.1 %collective-permute-start.8 = (bf16[576,256]{1,0:T(8,128)(2,1)}, bf16[576,256]{1,0:T(8,128)(2,1)S(1)}, u32[]{:S(2)}, u32[]{:S(2)}) collective-permute-start(bf16[576,256]{1,0:T(8,128)(2,1)} %get-tuple-element.74.source), channel_id=1, source_target_pairs={{0,1},{1,0},{2,3},{3,2},{4,5},{5,4},{6,7},{7,6},{8,9},{9,8},{10,11... | collective-permute-start | bytes 884744 | tf_op jit(solution)/shard_map/ppermute | solution.py:639
  88.4 6.1 %collective-permute-start.13 = (bf16[96,256]{1,0:T(8,128)(2,1)S(1)}, bf16[96,256]{1,0:T(8,128)(2,1)S(1)}, u32[]{:S(2)}, u32[]{:S(2)}) collective-permute-start(bf16[96,256]{1,0:T(8,128)(2,1)S(1)} %get-tuple-element.82), channel_id=1, source_target_pairs={{0,8},{1,9},{2,10},{3,11},{4,12},{5,13},{6,14},{7,15},{16,24},{17,... | collective-permute-start | bytes 147464 | tf_op jit(solution)/shard_map/ppermute | solution.py:660
  91.7 2.8 %collective-permute-start.14 = (bf16[96,256]{1,0:T(8,128)(2,1)S(1)}, bf16[96,256]{1,0:T(8,128)(2,1)S(1)}, u32[]{:S(2)}, u32[]{:S(2)}) collective-permute-start(bf16[96,256]{1,0:T(8,128)(2,1)S(1)} %get-tuple-element.83), channel_id=1, source_target_pairs={{8,16},{9,17},{10,18},{11,19},{12,20},{13,21},{14,22},{15,23},{24,... | collective-permute-start | bytes 147464 | tf_op jit(solution)/shard_map/ppermute | solution.py:660
  94.5 0.9 copy-start.11
  97.0 10.0 %copy-start.3 = (f32[480,256]{1,0:T(8,128)S(1)}, f32[480,256]{1,0:T(8,128)}, u32[]{:S(2)}) copy-start(f32[480,256]{1,0:T(8,128)} %copy-done.2) | copy-start | bytes 1474564
  107.0 0.9 copy-start.12
  110.4 1.6 collective-permute-start.16
  138.8 21.5 %copy-start.16 = (bf16[192,256]{1,0:T(8,128)(2,1)S(1)}, bf16[192,256]{1,0:T(8,128)(2,1)}, u32[]{:S(2)}) copy-start(bf16[192,256]{1,0:T(8,128)(2,1)} %get-tuple-element.94.pick) | copy-start | bytes 294916
  139.5 3.6 %collective-permute-start.17 = (bf16[144,256]{1,0:T(8,128)(2,1)S(1)}, bf16[144,256]{1,0:T(8,128)(2,1)S(1)}, u32[]{:S(2)}, u32[]{:S(2)}) collective-permute-start(bf16[144,256]{1,0:T(8,128)(2,1)S(1)} %shard_map.97.one), channel_id=1, source_target_pairs={{0,64},{64,0},{128,192},{192,128},{1,65},{65,1},{129,193},{193,129... | collective-permute-start | bytes 221192 | tf_op jit(solution)/shard_map/ppermute | solution.py:711
  143.6 4.2 %collective-permute-start.18 = (bf16[144,256]{1,0:T(8,128)(2,1)S(1)}, bf16[144,256]{1,0:T(8,128)(2,1)S(1)}, u32[]{:S(2)}, u32[]{:S(2)}) collective-permute-start(bf16[144,256]{1,0:T(8,128)(2,1)S(1)} %shard_map.98.one), channel_id=1, source_target_pairs={{0,128},{64,192},{128,0},{192,64},{1,129},{65,193},{129,1},{193,65... | collective-permute-start | bytes 221192 | tf_op jit(solution)/shard_map/ppermute | solution.py:711
  148.4 33.0 %collective-permute-start.19 = (bf16[144,256]{1,0:T(8,128)(2,1)S(1)}, bf16[144,256]{1,0:T(8,128)(2,1)S(1)}, u32[]{:S(2)}, u32[]{:S(2)}) collective-permute-start(bf16[144,256]{1,0:T(8,128)(2,1)S(1)} %shard_map.99.one), channel_id=1, source_target_pairs={{0,56},{1,57},{2,58},{3,59},{4,60},{5,61},{6,62},{7,63},{8,48},{9,... | collective-permute-start | bytes 221192 | tf_op jit(solution)/shard_map/ppermute | solution.py:713
  154.4 3.1 %collective-permute-start.22 = (bf16[48,256]{1,0:T(8,128)(2,1)S(1)}, bf16[48,256]{1,0:T(8,128)(2,1)S(1)}, u32[]{:S(2)}, u32[]{:S(2)}) collective-permute-start(bf16[48,256]{1,0:T(8,128)(2,1)S(1)} %get-tuple-element.93.one), channel_id=1, source_target_pairs={{0,192},{64,0},{128,64},{192,128},{1,193},{65,1},{129,65},{193,129... | collective-permute-start | bytes 73736 | tf_op jit(solution)/shard_map/ppermute | solution.py:703
  155.4 4.1 %collective-permute-start.21 = (bf16[48,256]{1,0:T(8,128)(2,1)S(1)}, bf16[48,256]{1,0:T(8,128)(2,1)S(1)}, u32[]{:S(2)}, u32[]{:S(2)}) collective-permute-start(bf16[48,256]{1,0:T(8,128)(2,1)S(1)} %get-tuple-element.93.one), channel_id=1, source_target_pairs={{0,128},{64,192},{128,0},{192,64},{1,129},{65,193},{129,1},{193,65... | collective-permute-start | bytes 73736 | tf_op jit(solution)/shard_map/ppermute | solution.py:703
  155.5 4.8 %collective-permute-start.20 = (bf16[48,256]{1,0:T(8,128)(2,1)S(1)}, bf16[48,256]{1,0:T(8,128)(2,1)S(1)}, u32[]{:S(2)}, u32[]{:S(2)}) collective-permute-start(bf16[48,256]{1,0:T(8,128)(2,1)S(1)} %get-tuple-element.93.one), channel_id=1, source_target_pairs={{0,64},{64,128},{128,192},{192,0},{1,65},{65,129},{129,193},{193,1... | collective-permute-start | bytes 73736 | tf_op jit(solution)/shard_map/ppermute | solution.py:703
  161.0 13.2 %collective-permute-start.23 = (bf16[48,256]{1,0:T(8,128)(2,1)S(1)}, bf16[48,256]{1,0:T(8,128)(2,1)S(1)}, u32[]{:S(2)}, u32[]{:S(2)}) collective-permute-start(bf16[48,256]{1,0:T(8,128)(2,1)S(1)} %get-tuple-element.95), channel_id=1, source_target_pairs={{0,7},{1,6},{2,5},{3,4},{4,3},{5,2},{6,1},{7,0},{8,15},{9,14},{10,... | collective-permute-start | bytes 73736 | tf_op jit(solution)/shard_map/ppermute | solution.py:707
  166.6 9.1 %collective-permute-start.24 = (bf16[48,256]{1,0:T(8,128)(2,1)S(1)}, bf16[48,256]{1,0:T(8,128)(2,1)S(1)}, u32[]{:S(2)}, u32[]{:S(2)}) collective-permute-start(bf16[48,256]{1,0:T(8,128)(2,1)S(1)} %get-tuple-element.96), channel_id=1, source_target_pairs={{0,56},{1,57},{2,58},{3,59},{4,60},{5,61},{6,62},{7,63},{8,48},{9,... | collective-permute-start | bytes 73736 | tf_op jit(solution)/shard_map/ppermute | solution.py:707
  169.8 11.6 %collective-permute-start.25 = (bf16[48,256]{1,0:T(8,128)(2,1)S(1)}, bf16[48,256]{1,0:T(8,128)(2,1)S(1)}, u32[]{:S(2)}, u32[]{:S(2)}) collective-permute-start(bf16[48,256]{1,0:T(8,128)(2,1)S(1)} %get-tuple-element.97), channel_id=1, source_target_pairs={{0,63},{1,62},{2,61},{3,60},{4,59},{5,58},{6,57},{7,56},{8,55},{9,... | collective-permute-start | bytes 73736 | tf_op jit(solution)/shard_map/ppermute | solution.py:707
  183.0 25.5 %all-to-all-start.4 = ((bf16[16,144,256]{2,1,0:T(8,128)(2,1)}), bf16[16,144,256]{2,1,0:T(8,128)(2,1)S(1)}, u32[]{:S(2)}, u32[]{:S(2)}) async-start(bf16[16,144,256]{2,1,0:T(8,128)(2,1)} %shard_map.101), calls=%async_computation.4 | async-start | bytes 2359296 | tf_op jit(solution)/shard_map/all_to_all | solution.py:725
  208.5 3.0 %collective-permute-start.26 = (bf16[16,144,256]{2,1,0:T(8,128)(2,1)S(1)}, bf16[16,144,256]{2,1,0:T(8,128)(2,1)S(1)}, u32[]{:S(2)}, u32[]{:S(2)}) collective-permute-start(bf16[16,144,256]{2,1,0:T(8,128)(2,1)S(1)} %all-to-all-done.4.refs_1_), channel_id=1, source_target_pairs={{0,1},{1,0},{2,3},{3,2},{4,5},{5,4},{6,7},{7,6},{8,9},{9,8},{10,11... | collective-permute-start | bytes 3538952 | tf_op jit(solution)/shard_map/ppermute | solution.py:728
  (1 other events, 0.6 us)

commit v14 on v13

--- a/solution.py
+++ b/solution.py
@@ -702,17 +702,18 @@
     part, strips = lax.optimization_barrier((part, strips))
     faces = [strips] + [lax.ppermute(strips, "face", [(i, (i + by) % 4) for i in range(4)]) for by in (1, 2, 3)]
     part = lax.all_to_all(part, AXES, 0, 0, axis_index_groups=PLANE_GROUPS)
-    strip = (48, C)
-    mine, *shares = run(share_kernel, [(strip, F32)] + [(strip, BF16)] * 3, [], pos, *faces, add_8)
-    shares = [lax.ppermute(v, TILE, [(t, t ^ m) for t in range(64)]) for v, m in zip(shares, MIRRORS[1:])]
+    part, *faces = lax.optimization_barrier((part, *faces))
     piece = [((144, C), BF16)]
     part = run(plane_kernel, piece, [], pos, part)[0]
     for by in (1, 2):
         got = lax.ppermute(part, "face", [(i, i ^ by) for i in range(4)])
         part = run(add_kernel, piece, [], pos, part, got)[0]
     got = lax.ppermute(part, TILE, [(t, t ^ 56) for t in range(64)])
-    part, got, *shares = lax.optimization_barrier((part, got, *shares))
+    part, got, *faces = lax.optimization_barrier((part, got, *faces))
     part = run(gather_kernel, [((16, 144, C), BF16)], [], pos, part, got)[0]
+    strip = (48, C)
+    mine, *shares = run(share_kernel, [(strip, F32)] + [(strip, BF16)] * 3, [], pos, *faces, add_8)
+    shares = [lax.ppermute(v, TILE, [(t, t ^ m) for t in range(64)]) for v, m in zip(shares, MIRRORS[1:])]
     input_grad = run(
         final_kernel,
         [((192, C), BF16)],

time: 215 us -> 199 us (0.926)
  blocking collectives: 51.2 us -> 25.6 us
  starting transfers between devices: 62.1 us -> 73.7 us
  waiting for transfers between devices: 60.6 us -> 57.4 us
    all_to_all x1 -> x0, blocking collectives: 25.6 us -> none  [body(): part = lax.all_to_all(part, AXES, 0, 0, axis_index_groups=PLANE_GROUPS)]
    all_to_all x1 -> x2, waiting for transfers between devices: 20.5 us -> 12.1 us  [body(): part = lax.all_to_all(part, AXES, 0, 0, axis_index_groups=PLANE_GROUPS)]
    all_to_all x1 -> x2, starting transfers between devices: 3.7 us -> 11.2 us  [body(): part = lax.all_to_all(part, AXES, 0, 0, axis_index_groups=PLANE_GROUPS)]
    ppermute x1, waiting for transfers between devices: 0.01 us -> 3.4 us  [body(): got = lax.ppermute(part, TILE, [(t, t ^ 56) for t in range(64)])]
    ppermute x3, starting transfers between devices: 1.47 us -> 4.03 us  [body(): lax.ppermute(strips, 'face', [(i, (i + by) % 4) for i in range(4)])]
    ppermute x3, waiting for transfers between devices: 7.15 us -> 9.3 us  [body(): lax.ppermute(v, TILE, [(t, t ^ m) for t in range(64)])]
  transfers between devices with their start and end apart: 30 -> 31, of which waited for: 16 -> 17; matrix products, arithmetic and copies ran while one was open for 1% -> 1% of each run, Pallas kernels for 7% -> 8%
where the time goes in v14:
time: 199 us; the launch traced here: 198 us
  starting transfers between devices  73.7 us (37%)
  waiting for transfers between devices  57.4 us (29%)
  Pallas kernels  31.9 us (16%)
  blocking collectives  25.6 us (13%)
  local copies, waits for them, and re-layouts  7.81 us (4%)
    all_to_all x1, blocking collectives, seam_exchange(): got = lax.all_to_all(send, AXES, 0, 0, axis_index_groups=SEAM_GROUPS)  25.6 us
    pallas_call x17, Pallas kernels, run(): pl.pallas_call(inner, out_shape=[jax.ShapeDtypeStruct(shape, dtype) for s...  25 us
    all_to_all x2, starting transfers between devices, seam_exchange(): got = lax.all_to_all(send, AXES, 0, 0, axis_index_groups=SEAM_GROUPS)  20.1 us
    ppermute x3, starting transfers between devices, body(): lax.ppermute(v, TILE, [(t, t ^ m) for t in range(64)])  15.2 us
    all_to_all x2, waiting for transfers between devices, seam_exchange(): got = lax.all_to_all(send, AXES, 0, 0, axis_index_groups=SEAM_GROUPS)  12.9 us
    all_to_all x2, waiting for transfers between devices, body(): part = lax.all_to_all(part, AXES, 0, 0, axis_index_groups=PLANE_GROUPS)  12.1 us
    all_to_all x2, starting transfers between devices, body(): part = lax.all_to_all(part, AXES, 0, 0, axis_index_groups=PLANE_GROUPS)  11.2 us
    ppermute x3, waiting for transfers between devices, body(): lax.ppermute(v, TILE, [(t, t ^ m) for t in range(64)])  9.3 us
  transfers between devices with their start and end apart: 31, of which 17 were waited for; matrix products, arithmetic and copies ran while one was open for 1% of the time, Pallas kernels for 8%

profile of v14, /device:TPU:1, one launch (start us, length us, event | category | flops | bytes accessed | tf_op | source)
XLA Modules:
  0.0 197.6 jit_solution(2452232037969711183)
XLA Ops:
  0.7 1.0 copy-done.4
  1.7 1.3 shard_map.85
  3.0 14.3 %all-to-all-start = ((bf16[16,48,256]{2,1,0:T(8,128)(2,1)}), bf16[16,48,256]{2,1,0:T(8,128)(2,1)S(1)}, u32[]{:S(2)}, u32[]{:S(2)}) async-start(bf16[16,48,256]{2,1,0:T(8,128)(2,1)} %shard_map.85), calls=%async_computation | async-start | bytes 786432 | tf_op jit(solution)/shard_map/all_to_all | solution.py:492
  17.4 1.9 collective-permute-start.1
  19.4 4.2 %collective-permute-done.1.odd = bf16[192,256]{1,0:T(8,128)(2,1)S(1)} collective-permute-done((bf16[192,256]{1,0:T(8,128)(2,1)S(1)}, bf16[192,256]{1,0:T(8,128)(2,1)S(1)}, u32[]{:S(2)}, u32[]{:S(2)}) %collective-permute-start.1) | collective-permute-done | bytes 98336 | tf_op jit(solution)/shard_map/ppermute | solution.py:616
  26.5 2.6 %shard_map.87 = (bf16[80,768]{1,0:T(8,128)(2,1)}, bf16[64,1024]{1,0:T(8,128)(2,1)}, bf16[64,1024]{1,0:T(8,128)(2,1)}, bf16[192,256]{1,0:T(8,128)(2,1)}) custom-call(s32[4]{0:T(128)} %copy-done.6, s32[12,4]{1,0:T(8,128)} %copy.11.nexts, s32[12,4]{1,0:T(8,128)} %copy.12.codes), custom_call_target="tpu_custom_call" | custom-call | tf_op jit(solution)/shard_map/pallas_call | solution.py:583
  29.1 4.9 %all-to-all-done = bf16[16,48,256]{2,1,0:T(8,128)(2,1)S(1)} async-done(((bf16[16,48,256]{2,1,0:T(8,128)(2,1)}), bf16[16,48,256]{2,1,0:T(8,128)(2,1)S(1)}, u32[]{:S(2)}, u32[]{:S(2)}) %all-to-all-start) | async-done | bytes 393248 | tf_op jit(solution)/shard_map/all_to_all | solution.py:492
  36.4 1.9 collective-permute-start.5
  39.1 2.3 %collective-permute-done.5.refs_6_ = bf16[16,256]{1,0:T(8,128)(2,1)S(1)} collective-permute-done((bf16[16,256]{1,0:T(8,128)(2,1)S(1)}, bf16[16,256]{1,0:T(8,128)(2,1)S(1)}, u32[]{:S(2)}, u32[]{:S(2)}) %collective-permute-start.5) | collective-permute-done | bytes 8224 | tf_op jit(solution)/shard_map/ppermute | solution.py:623
  42.0 2.3 %shard_map.89 = (bf16[576,256]{1,0:T(8,128)(2,1)}, f32[480,256]{1,0:T(8,128)S(1)}, bf16[480,256]{1,0:T(8,128)(2,1)S(1)}, bf16[16,64,256]{2,1,0:T(8,128)(2,1)S(1)}) custom-call(s32[4]{0:T(128)S(1)} %copy-done.8, bf16[384,256]{1,0:T(8,128)(2,1)S(1)} %get-tuple-element.68.refs_1_, bf16[96,256]{1,0:T(8,128)(2,1)S(1)} %collective-permute-done.2.refs_2_, ...), custom_call_target="tpu_custom_call" | custom-call | tf_op jit(solution)/shard_map/pallas_call | solution.py:78
  45.1 25.6 %all_to_all.25 = bf16[16,64,256]{2,1,0:T(8,128)(2,1)S(1)} all-to-all(bf16[16,64,256]{2,1,0:T(8,128)(2,1)S(1)} %get-tuple-element.82), channel_id=1, replica_groups={{0,7,56,63,64,71,120,127,128,135,184,191,192,199,248,255},{1,6,57,62,65..., dimensions={0} | all-to-all | bytes 1048576 | tf_op jit(solution)/shard_map/all_to_all | solution.py:492
  70.7 2.6 %shard_map.90 = (bf16[864,256]{1,0:T(8,128)(2,1)}, bf16[192,256]{1,0:T(8,128)(2,1)S(1)}, bf16[16,256]{1,0:T(8,128)(2,1)S(1)}, bf16[16,256]{1,0:T(8,128)(2,1)S(1)}) custom-call(s32[4]{0:T(128)S(1)} %copy-done.8, bf16[480,256]{1,0:T(8,128)(2,1)S(1)} %get-tuple-element.81.refs_1_, bf16[1024,256]{1,0:T(8,128)(2,1)S(1)} %bitcast.14, ...), custom_call_target="tpu_custom_call" | custom-call | tf_op jit(solution)/shard_map/pallas_call | solution.py:78
  73.4 2.0 %collective-permute-start.10 = (bf16[192,256]{1,0:T(8,128)(2,1)S(1)}, bf16[192,256]{1,0:T(8,128)(2,1)S(1)}, u32[]{:S(2)}, u32[]{:S(2)}) collective-permute-start(bf16[192,256]{1,0:T(8,128)(2,1)S(1)} %get-tuple-element.84.refs_1_), channel_id=1, source_target_pairs={{1,2},{3,4},{5,6},{9,10},{11,12},{13,14},{17,18},{19,20},{21,22},{... | collective-permute-start | bytes 294920 | tf_op jit(solution)/shard_map/ppermute | solution.py:606
  76.3 1.8 collective-permute-done.11.refs_4_
  78.1 1.2 collective-permute-done.10.refs_3_
  79.3 2.2 %shard_map.91 = (bf16[384,256]{1,0:T(8,128)(2,1)S(1)}, bf16[96,256]{1,0:T(8,128)(2,1)S(1)}, bf16[96,256]{1,0:T(8,128)(2,1)S(1)}, bf16[16,64,256]{2,1,0:T(8,128)(2,1)}) custom-call(s32[4]{0:T(128)S(1)} %copy-done.8, bf16[192,256]{1,0:T(8,128)(2,1)S(1)} %get-tuple-element.84.refs_1_, bf16[192,256]{1,0:T(8,128)(2,1)S(1)} %collective-permute-done.9.refs_2_, ...), custom_call_target="tpu_custom_call" | custom-call | tf_op jit(solution)/shard_map/pallas_call | solution.py:78
  82.1 5.7 %all-to-all-start.2 = ((bf16[16,64,256]{2,1,0:T(8,128)(2,1)}), bf16[16,64,256]{2,1,0:T(8,128)(2,1)S(1)}, u32[]{:S(2)}, u32[]{:S(2)}) async-start(bf16[16,64,256]{2,1,0:T(8,128)(2,1)} %get-tuple-element.90), calls=%async_computation.2 | async-start | bytes 1048576 | tf_op jit(solution)/shard_map/all_to_all | solution.py:492
  88.5 3.3 %collective-permute-start.13 = (bf16[96,256]{1,0:T(8,128)(2,1)S(1)}, bf16[96,256]{1,0:T(8,128)(2,1)S(1)}, u32[]{:S(2)}, u32[]{:S(2)}) collective-permute-start(bf16[96,256]{1,0:T(8,128)(2,1)S(1)} %get-tuple-element.88), channel_id=1, source_target_pairs={{0,8},{1,9},{2,10},{3,11},{4,12},{5,13},{6,14},{7,15},{16,24},{17,... | collective-permute-start | bytes 147464 | tf_op jit(solution)/shard_map/ppermute | solution.py:660
  92.4 2.2 %collective-permute-done.13.refs_2_ = bf16[96,256]{1,0:T(8,128)(2,1)S(1)} collective-permute-done((bf16[96,256]{1,0:T(8,128)(2,1)S(1)}, bf16[96,256]{1,0:T(8,128)(2,1)S(1)}, u32[]{:S(2)}, u32[]{:S(2)}) %collective-permute-start.13) | collective-permute-done | bytes 49184 | tf_op jit(solution)/shard_map/ppermute | solution.py:660
  94.6 0.9 copy-done.11
  95.5 1.6 shard_map.92.refs_1_
  97.1 1.9 shard_map.93.two
  99.1 8.0 %all-to-all-done.2 = bf16[16,64,256]{2,1,0:T(8,128)(2,1)S(1)} async-done(((bf16[16,64,256]{2,1,0:T(8,128)(2,1)}), bf16[16,64,256]{2,1,0:T(8,128)(2,1)S(1)}, u32[]{:S(2)}, u32[]{:S(2)}) %all-to-all-start.2) | async-done | bytes 524320 | tf_op jit(solution)/shard_map/all_to_all | solution.py:492
  108.0 2.5 %shard_map.94 = (bf16[384,256]{1,0:T(8,128)(2,1)S(1)}, bf16[192,256]{1,0:T(8,128)(2,1)S(1)}, bf16[48,256]{1,0:T(8,128)(2,1)S(1)}) custom-call(s32[4]{0:T(128)S(1)} %copy-done.9, bf16[480,256]{1,0:T(8,128)(2,1)S(1)} %shard_map.92.refs_1_, bf16[1024,256]{1,0:T(8,128)(2,1)S(1)} %bitcast.15, bf16[64,1024]{1,0:T(8,128)(2,1)S(1)} %copy-done.12, ...), custom_call_target="tpu_custom_call" | custom-call | tf_op jit(solution)/shard_map/pallas_call | solution.py:78
  110.6 1.5 shard_map.95.part
  112.2 2.1 %shard_map.96 = bf16[16,144,256]{2,1,0:T(8,128)(2,1)} custom-call(s32[4]{0:T(128)S(1)} %copy-done.9, bf16[576,256]{1,0:T(8,128)(2,1)S(1)} %collective-permute-done.8.source, bf16[384,256]{1,0:T(8,128)(2,1)S(1)} %collective-permute-done.16.delta, f32[16,72,256]{2,1,0:T(8,128)S(1)} %shard_map.95.part, bf16[16,72,256]{2,1,0:T(8,128)(2,1)S(1)} %shard_map.93.two), custom_call_target="tpu_custom_call" | custom-call | tf_op jit(solution)/shard_map/pallas_call | solution.py:78
  114.3 7.4 %all-to-all-start.3 = ((bf16[16,144,256]{2,1,0:T(8,128)(2,1)}), bf16[16,144,256]{2,1,0:T(8,128)(2,1)S(1)}, u32[]{:S(2)}, u32[]{:S(2)}) async-start(bf16[16,144,256]{2,1,0:T(8,128)(2,1)} %shard_map.96), calls=%async_computation.3 | async-start | bytes 2359296 | tf_op jit(solution)/shard_map/all_to_all | solution.py:704
  121.7 2.1 %collective-permute-start.19 = (bf16[48,256]{1,0:T(8,128)(2,1)S(1)}, bf16[48,256]{1,0:T(8,128)(2,1)S(1)}, u32[]{:S(2)}, u32[]{:S(2)}) collective-permute-start(bf16[48,256]{1,0:T(8,128)(2,1)S(1)} %get-tuple-element.108.one), channel_id=1, source_target_pairs={{0,192},{64,0},{128,64},{192,128},{1,193},{65,1},{129,65},{193,129... | collective-permute-start | bytes 73736 | tf_op jit(solution)/shard_map/ppermute | solution.py:703
  124.7 1.0 collective-permute-start.17
  125.7 1.9 collective-permute-done.18.three
  127.7 1.8 collective-permute-done.17.two
  129.4 12.1 %all-to-all-done.3.parts = bf16[16,144,256]{2,1,0:T(8,128)(2,1)S(1)} async-done(((bf16[16,144,256]{2,1,0:T(8,128)(2,1)}), bf16[16,144,256]{2,1,0:T(8,128)(2,1)S(1)}, u32[]{:S(2)}, u32[]{:S(2)}) %all-to-all-start.3) | async-done | bytes 1179680 | tf_op jit(solution)/shard_map/all_to_all | solution.py:704
  142.2 1.8 collective-permute-start.20
  144.1 1.7 collective-permute-done.20.two
  146.4 2.3 %collective-permute-start.21 = (bf16[144,256]{1,0:T(8,128)(2,1)S(1)}, bf16[144,256]{1,0:T(8,128)(2,1)S(1)}, u32[]{:S(2)}, u32[]{:S(2)}) collective-permute-start(bf16[144,256]{1,0:T(8,128)(2,1)S(1)} %shard_map.98.one), channel_id=1, source_target_pairs={{0,128},{64,192},{128,0},{192,64},{1,129},{65,193},{129,1},{193,65... | collective-permute-start | bytes 221192 | tf_op jit(solution)/shard_map/ppermute | solution.py:709
  148.7 1.9 collective-permute-done.21.two
  151.1 6.0 %collective-permute-start.22 = (bf16[144,256]{1,0:T(8,128)(2,1)S(1)}, bf16[144,256]{1,0:T(8,128)(2,1)S(1)}, u32[]{:S(2)}, u32[]{:S(2)}) collective-permute-start(bf16[144,256]{1,0:T(8,128)(2,1)S(1)} %shard_map.99.one), channel_id=1, source_target_pairs={{0,56},{1,57},{2,58},{3,59},{4,60},{5,61},{6,62},{7,63},{8,48},{9,... | collective-permute-start | bytes 221192 | tf_op jit(solution)/shard_map/ppermute | solution.py:711
  157.1 3.4 %collective-permute-done.22.two = bf16[144,256]{1,0:T(8,128)(2,1)S(1)} collective-permute-done((bf16[144,256]{1,0:T(8,128)(2,1)S(1)}, bf16[144,256]{1,0:T(8,128)(2,1)S(1)}, u32[]{:S(2)}, u32[]{:S(2)}) %collective-permute-start.22) | collective-permute-done | bytes 73760 | tf_op jit(solution)/shard_map/ppermute | solution.py:711
  160.5 1.6 shard_map.100
  162.1 3.8 %all-to-all-start.4 = ((bf16[16,144,256]{2,1,0:T(8,128)(2,1)}), bf16[16,144,256]{2,1,0:T(8,128)(2,1)S(1)}, u32[]{:S(2)}, u32[]{:S(2)}) async-start(bf16[16,144,256]{2,1,0:T(8,128)(2,1)} %shard_map.100), calls=%async_computation.4 | async-start | bytes 2359296 | tf_op jit(solution)/shard_map/all_to_all | solution.py:726
  166.7 7.7 %collective-permute-start.23 = (bf16[48,256]{1,0:T(8,128)(2,1)S(1)}, bf16[48,256]{1,0:T(8,128)(2,1)S(1)}, u32[]{:S(2)}, u32[]{:S(2)}) collective-permute-start(bf16[48,256]{1,0:T(8,128)(2,1)S(1)} %get-tuple-element.114), channel_id=1, source_target_pairs={{0,7},{1,6},{2,5},{3,4},{4,3},{5,2},{6,1},{7,0},{8,15},{9,14},{10,... | collective-permute-start | bytes 73736 | tf_op jit(solution)/shard_map/ppermute | solution.py:716
  174.4 5.5 %collective-permute-start.24 = (bf16[48,256]{1,0:T(8,128)(2,1)S(1)}, bf16[48,256]{1,0:T(8,128)(2,1)S(1)}, u32[]{:S(2)}, u32[]{:S(2)}) collective-permute-start(bf16[48,256]{1,0:T(8,128)(2,1)S(1)} %get-tuple-element.115), channel_id=1, source_target_pairs={{0,56},{1,57},{2,58},{3,59},{4,60},{5,61},{6,62},{7,63},{8,48},{9,... | collective-permute-start | bytes 73736 | tf_op jit(solution)/shard_map/ppermute | solution.py:716
  179.9 2.1 %collective-permute-start.25 = (bf16[48,256]{1,0:T(8,128)(2,1)S(1)}, bf16[48,256]{1,0:T(8,128)(2,1)S(1)}, u32[]{:S(2)}, u32[]{:S(2)}) collective-permute-start(bf16[48,256]{1,0:T(8,128)(2,1)S(1)} %get-tuple-element.116), channel_id=1, source_target_pairs={{0,63},{1,62},{2,61},{3,60},{4,59},{5,58},{6,57},{7,56},{8,55},{9,... | collective-permute-start | bytes 73736 | tf_op jit(solution)/shard_map/ppermute | solution.py:716
  181.9 1.0 collective-permute-done.23.by_col
  183.2 8.1 %collective-permute-done.25.by_both = bf16[48,256]{1,0:T(8,128)(2,1)S(1)} collective-permute-done((bf16[48,256]{1,0:T(8,128)(2,1)S(1)}, bf16[48,256]{1,0:T(8,128)(2,1)S(1)}, u32[]{:S(2)}, u32[]{:S(2)}) %collective-permute-start.25) | collective-permute-done | bytes 24608 | tf_op jit(solution)/shard_map/ppermute | solution.py:716
  191.2 1.3 shard_map.102
  192.5 2.1 %shard_map.103 = (f32[9,256,256]{2,1,0:T(8,128)}, f32[9,256,256]{2,1,0:T(8,128)}) custom-call(s32[4]{0:T(128)S(1)} %copy-done.9, bf16[16,144,256]{2,1,0:T(8,128)(2,1)S(1)} %all-to-all-done.4.refs_1_), custom_call_target="tpu_custom_call" | custom-call | tf_op jit(solution)/shard_map/pallas_call | solution.py:480
  195.4 2.1 %shard_map.104 = (f32[9,256,256]{2,1,0:T(8,128)}, f32[9,256,256]{2,1,0:T(8,128)}) custom-call(s32[4]{0:T(128)S(1)} %copy-done.9, bf16[16,144,256]{2,1,0:T(8,128)(2,1)S(1)} %collective-permute-done.26.refs_1_, f32[9,256,256]{2,1,0:T(8,128)} %get-tuple-element.119.refs_2_, ...), custom_call_target="tpu_custom_call", output_to_operand_aliasing={{0}: (2, {}), {1}: (3, {})} | custom-call | tf_op jit(solution)/shard_map/pallas_call | solution.py:480
  (76 shorter events, 15.7 us)
Async XLA Ops:
  0.6 40.7 %copy-start.1 = (bf16[3,3,256,256]{3,2,1,0:T(8,128)(2,1)S(1)}, bf16[3,3,256,256]{3,2,1,0:T(8,128)(2,1)}, u32[]{:S(2)}) copy-start(bf16[3,3,256,256]{3,2,1,0:T(8,128)(2,1)} %refs_5_.3) | copy-start | bytes 3538948
  0.7 25.7 %copy-start.6 = (s32[4]{0:T(128)}, s32[4]{0:T(128)S(1)}, u32[]{:S(2)}) copy-start(s32[4]{0:T(128)S(1)} %pad_add_fusion.pos.refs_0_) | copy-start | bytes 52
  0.7 1.0 copy-start.4
  1.7 15.7 %copy-start.5 = (bf16[3,1,8,8,256]{4,3,2,1,0:T(8,128)(2,1)S(1)}, bf16[3,1,8,8,256]{4,3,2,1,0:T(8,128)(2,1)}, u32[]{:S(2)}) copy-start(bf16[3,1,8,8,256]{4,3,2,1,0:T(8,128)(2,1)} %param.6) | copy-start | bytes 294916
  1.7 23.4 %copy-start.17 = (s32[12,4]{0,1:T(4,128)S(1)}, s32[12,4]{0,1:T(4,128)}, u32[]{:S(2)}) copy-start(s32[12,4]{0,1:T(4,128)} %param.10) | copy-start | bytes 580
  1.7 24.1 %copy-start.18 = (s32[12,4]{0,1:T(4,128)S(1)}, s32[12,4]{0,1:T(4,128)}, u32[]{:S(2)}) copy-start(s32[12,4]{0,1:T(4,128)} %param.11) | copy-start | bytes 580
  3.0 30.9 %all-to-all-start = ((bf16[16,48,256]{2,1,0:T(8,128)(2,1)}), bf16[16,48,256]{2,1,0:T(8,128)(2,1)S(1)}, u32[]{:S(2)}, u32[]{:S(2)}) async-start(bf16[16,48,256]{2,1,0:T(8,128)(2,1)} %shard_map.85), calls=%async_computation | async-start | bytes 786432 | tf_op jit(solution)/shard_map/all_to_all | solution.py:492
  17.4 6.2 %collective-permute-start.1 = (bf16[192,256]{1,0:T(8,128)(2,1)S(1)}, bf16[192,256]{1,0:T(8,128)(2,1)S(1)}, u32[]{:S(2)}, u32[]{:S(2)}) collective-permute-start(bf16[192,256]{1,0:T(8,128)(2,1)S(1)} %bitcast.18), channel_id=1, source_target_pairs={{1,2},{3,4},{5,6},{9,10},{11,12},{13,14},{17,18},{19,20},{21,22},{... | collective-permute-start | bytes 294920 | tf_op jit(solution)/shard_map/ppermute | solution.py:616
  19.3 4.3 %collective-permute-start = (bf16[192,256]{1,0:T(8,128)(2,1)S(1)}, bf16[192,256]{1,0:T(8,128)(2,1)S(1)}, u32[]{:S(2)}, u32[]{:S(2)}) collective-permute-start(bf16[192,256]{1,0:T(8,128)(2,1)S(1)} %bitcast.19), channel_id=1, source_target_pairs={{0,1},{1,0},{2,3},{3,2},{4,5},{5,4},{6,7},{7,6},{8,9},{9,8},{10,11... | collective-permute-start | bytes 294920 | tf_op jit(solution)/shard_map/ppermute | solution.py:616
  24.3 4.8 %collective-permute-start.2 = (bf16[96,256]{1,0:T(8,128)(2,1)S(1)}, bf16[96,256]{1,0:T(8,128)(2,1)S(1)}, u32[]{:S(2)}, u32[]{:S(2)}) collective-permute-start(bf16[96,256]{1,0:T(8,128)(2,1)S(1)} %get-tuple-element.66), channel_id=1, source_target_pairs={{0,8},{1,9},{2,10},{3,11},{4,12},{5,13},{6,14},{7,15},{16,24},{17,... | collective-permute-start | bytes 147464 | tf_op jit(solution)/shard_map/ppermute | solution.py:618
  24.4 4.7 %collective-permute-start.3 = (bf16[96,256]{1,0:T(8,128)(2,1)S(1)}, bf16[96,256]{1,0:T(8,128)(2,1)S(1)}, u32[]{:S(2)}, u32[]{:S(2)}) collective-permute-start(bf16[96,256]{1,0:T(8,128)(2,1)S(1)} %get-tuple-element.67), channel_id=1, source_target_pairs={{8,16},{9,17},{10,18},{11,19},{12,20},{13,21},{14,22},{15,23},{24,... | collective-permute-start | bytes 147464 | tf_op jit(solution)/shard_map/ppermute | solution.py:618
  34.6 0.9 copy-start.14
  36.3 2.8 %collective-permute-start.4 = (bf16[16,256]{1,0:T(8,128)(2,1)S(1)}, bf16[16,256]{1,0:T(8,128)(2,1)S(1)}, u32[]{:S(2)}, u32[]{:S(2)}) collective-permute-start(bf16[16,256]{1,0:T(8,128)(2,1)S(1)} %get-tuple-element.76), channel_id=1, source_target_pairs={{0,1},{1,0},{2,3},{3,2},{4,5},{5,4},{6,7},{7,6},{8,9},{9,8},{10,11... | collective-permute-start | bytes 24584 | tf_op jit(solution)/shard_map/ppermute | solution.py:622
  36.4 5.0 %collective-permute-start.5 = (bf16[16,256]{1,0:T(8,128)(2,1)S(1)}, bf16[16,256]{1,0:T(8,128)(2,1)S(1)}, u32[]{:S(2)}, u32[]{:S(2)}) collective-permute-start(bf16[16,256]{1,0:T(8,128)(2,1)S(1)} %get-tuple-element.77), channel_id=1, source_target_pairs={{1,2},{3,4},{5,6},{9,10},{11,12},{13,14},{17,18},{19,20},{21,22},{... | collective-permute-start | bytes 24584 | tf_op jit(solution)/shard_map/ppermute | solution.py:623
  38.3 3.0 %collective-permute-start.6 = (bf16[16,256]{1,0:T(8,128)(2,1)S(1)}, bf16[16,256]{1,0:T(8,128)(2,1)S(1)}, u32[]{:S(2)}, u32[]{:S(2)}) collective-permute-start(bf16[16,256]{1,0:T(8,128)(2,1)S(1)} %get-tuple-element.78), channel_id=1, source_target_pairs={{0,8},{1,9},{2,10},{3,11},{4,12},{5,13},{6,14},{7,15},{16,24},{17,... | collective-permute-start | bytes 24584 | tf_op jit(solution)/shard_map/ppermute | solution.py:624
  38.4 2.9 %collective-permute-start.7 = (bf16[16,256]{1,0:T(8,128)(2,1)S(1)}, bf16[16,256]{1,0:T(8,128)(2,1)S(1)}, u32[]{:S(2)}, u32[]{:S(2)}) collective-permute-start(bf16[16,256]{1,0:T(8,128)(2,1)S(1)} %get-tuple-element.79), channel_id=1, source_target_pairs={{8,16},{9,17},{10,18},{11,19},{12,20},{13,21},{14,22},{15,23},{40,... | collective-permute-start | bytes 24584 | tf_op jit(solution)/shard_map/ppermute | solution.py:625
  42.0 28.7 %copy-start = (bf16[3,3,256,256]{3,2,1,0:T(8,128)(2,1)S(1)}, bf16[3,3,256,256]{3,2,1,0:T(8,128)(2,1)}, u32[]{:S(2)}) copy-start(bf16[3,3,256,256]{3,2,1,0:T(8,128)(2,1)} %refs_4_.1) | copy-start | bytes 3538948
  42.0 28.7 %copy-start.13 = (bf16[64,1024]{1,0:T(8,128)(2,1)S(1)}, bf16[64,1024]{1,0:T(8,128)(2,1)}, u32[]{:S(2)}) copy-start(bf16[64,1024]{1,0:T(8,128)(2,1)} %get-tuple-element.83.refs_3_) | copy-start | bytes 393220
  42.0 28.7 %copy-start.15 = (bf16[3,1,8,8,256]{4,3,2,1,0:T(8,128)(2,1)S(1)}, bf16[3,1,8,8,256]{4,3,2,1,0:T(8,128)(2,1)}, u32[]{:S(2)}) copy-start(bf16[3,1,8,8,256]{4,3,2,1,0:T(8,128)(2,1)} %param.7) | copy-start | bytes 294916
  44.4 0.8 copy-start.2
  73.4 5.9 %collective-permute-start.10 = (bf16[192,256]{1,0:T(8,128)(2,1)S(1)}, bf16[192,256]{1,0:T(8,128)(2,1)S(1)}, u32[]{:S(2)}, u32[]{:S(2)}) collective-permute-start(bf16[192,256]{1,0:T(8,128)(2,1)S(1)} %get-tuple-element.84.refs_1_), channel_id=1, source_target_pairs={{1,2},{3,4},{5,6},{9,10},{11,12},{13,14},{17,18},{19,20},{21,22},{... | collective-permute-start | bytes 294920 | tf_op jit(solution)/shard_map/ppermute | solution.py:606
  75.4 3.9 %collective-permute-start.9 = (bf16[192,256]{1,0:T(8,128)(2,1)S(1)}, bf16[192,256]{1,0:T(8,128)(2,1)S(1)}, u32[]{:S(2)}, u32[]{:S(2)}) collective-permute-start(bf16[192,256]{1,0:T(8,128)(2,1)S(1)} %get-tuple-element.84.refs_1_), channel_id=1, source_target_pairs={{0,1},{1,0},{2,3},{3,2},{4,5},{5,4},{6,7},{7,6},{8,9},{9,8},{10,11... | collective-permute-start | bytes 294920 | tf_op jit(solution)/shard_map/ppermute | solution.py:605
  75.5 2.6 %collective-permute-start.11 = (bf16[16,256]{1,0:T(8,128)(2,1)S(1)}, bf16[16,256]{1,0:T(8,128)(2,1)S(1)}, u32[]{:S(2)}, u32[]{:S(2)}) collective-permute-start(bf16[16,256]{1,0:T(8,128)(2,1)S(1)} %get-tuple-element.85), channel_id=1, source_target_pairs={{0,8},{1,9},{2,10},{3,11},{4,12},{5,13},{6,14},{7,15},{16,24},{17,... | collective-permute-start | bytes 24584 | tf_op jit(solution)/shard_map/ppermute | solution.py:607
  75.6 19.0 %copy-start.9 = (s32[4]{0:T(128)S(1)}, s32[4]{0:T(128)}, u32[]{:S(2)}) copy-start(s32[4]{0:T(128)} %copy-done.6) | copy-start | bytes 52
  75.6 2.5 %collective-permute-start.12 = (bf16[16,256]{1,0:T(8,128)(2,1)S(1)}, bf16[16,256]{1,0:T(8,128)(2,1)S(1)}, u32[]{:S(2)}, u32[]{:S(2)}) collective-permute-start(bf16[16,256]{1,0:T(8,128)(2,1)S(1)} %get-tuple-element.86), channel_id=1, source_target_pairs={{8,16},{9,17},{10,18},{11,19},{12,20},{13,21},{14,22},{15,23},{40,... | collective-permute-start | bytes 24584 | tf_op jit(solution)/shard_map/ppermute | solution.py:608
  81.5 0.7 copy-start.10
  82.1 24.9 %all-to-all-start.2 = ((bf16[16,64,256]{2,1,0:T(8,128)(2,1)}), bf16[16,64,256]{2,1,0:T(8,128)(2,1)S(1)}, u32[]{:S(2)}, u32[]{:S(2)}) async-start(bf16[16,64,256]{2,1,0:T(8,128)(2,1)} %get-tuple-element.90), calls=%async_computation.2 | async-start | bytes 1048576 | tf_op jit(solution)/shard_map/all_to_all | solution.py:492
  87.9 9.2 %collective-permute-start.15 = (bf16[864,256]{1,0:T(8,128)(2,1)}, bf16[864,256]{1,0:T(8,128)(2,1)S(1)}, u32[]{:S(2)}, u32[]{:S(2)}) collective-permute-start(bf16[864,256]{1,0:T(8,128)(2,1)} %get-tuple-element.91.own), channel_id=1, source_target_pairs={{0,1},{1,0},{2,3},{3,2},{4,5},{5,4},{6,7},{7,6},{8,9},{9,8},{10,11... | collective-permute-start | bytes 1327112 | tf_op jit(solution)/shard_map/ppermute | solution.py:676
  88.0 24.1 %collective-permute-start.8 = (bf16[576,256]{1,0:T(8,128)(2,1)}, bf16[576,256]{1,0:T(8,128)(2,1)S(1)}, u32[]{:S(2)}, u32[]{:S(2)}) collective-permute-start(bf16[576,256]{1,0:T(8,128)(2,1)} %get-tuple-element.80.source), channel_id=1, source_target_pairs={{0,1},{1,0},{2,3},{3,2},{4,5},{5,4},{6,7},{7,6},{8,9},{9,8},{10,11... | collective-permute-start | bytes 884744 | tf_op jit(solution)/shard_map/ppermute | solution.py:639
  88.5 6.1 %collective-permute-start.13 = (bf16[96,256]{1,0:T(8,128)(2,1)S(1)}, bf16[96,256]{1,0:T(8,128)(2,1)S(1)}, u32[]{:S(2)}, u32[]{:S(2)}) collective-permute-start(bf16[96,256]{1,0:T(8,128)(2,1)S(1)} %get-tuple-element.88), channel_id=1, source_target_pairs={{0,8},{1,9},{2,10},{3,11},{4,12},{5,13},{6,14},{7,15},{16,24},{17,... | collective-permute-start | bytes 147464 | tf_op jit(solution)/shard_map/ppermute | solution.py:660
  91.8 2.8 %collective-permute-start.14 = (bf16[96,256]{1,0:T(8,128)(2,1)S(1)}, bf16[96,256]{1,0:T(8,128)(2,1)S(1)}, u32[]{:S(2)}, u32[]{:S(2)}) collective-permute-start(bf16[96,256]{1,0:T(8,128)(2,1)S(1)} %get-tuple-element.89), channel_id=1, source_target_pairs={{8,16},{9,17},{10,18},{11,19},{12,20},{13,21},{14,22},{15,23},{24,... | collective-permute-start | bytes 147464 | tf_op jit(solution)/shard_map/ppermute | solution.py:660
  94.6 0.9 copy-start.11
  97.1 10.0 %copy-start.3 = (f32[480,256]{1,0:T(8,128)S(1)}, f32[480,256]{1,0:T(8,128)}, u32[]{:S(2)}) copy-start(f32[480,256]{1,0:T(8,128)} %copy-done.2) | copy-start | bytes 1474564
  107.1 0.9 copy-start.12
  110.5 1.6 collective-permute-start.16
  114.3 27.3 %all-to-all-start.3 = ((bf16[16,144,256]{2,1,0:T(8,128)(2,1)}), bf16[16,144,256]{2,1,0:T(8,128)(2,1)S(1)}, u32[]{:S(2)}, u32[]{:S(2)}) async-start(bf16[16,144,256]{2,1,0:T(8,128)(2,1)} %shard_map.96), calls=%async_computation.3 | async-start | bytes 2359296 | tf_op jit(solution)/shard_map/all_to_all | solution.py:704
  121.7 4.0 %collective-permute-start.19 = (bf16[48,256]{1,0:T(8,128)(2,1)S(1)}, bf16[48,256]{1,0:T(8,128)(2,1)S(1)}, u32[]{:S(2)}, u32[]{:S(2)}) collective-permute-start(bf16[48,256]{1,0:T(8,128)(2,1)S(1)} %get-tuple-element.108.one), channel_id=1, source_target_pairs={{0,192},{64,0},{128,64},{192,128},{1,193},{65,1},{129,65},{193,129... | collective-permute-start | bytes 73736 | tf_op jit(solution)/shard_map/ppermute | solution.py:703
  123.8 3.9 %collective-permute-start.18 = (bf16[48,256]{1,0:T(8,128)(2,1)S(1)}, bf16[48,256]{1,0:T(8,128)(2,1)S(1)}, u32[]{:S(2)}, u32[]{:S(2)}) collective-permute-start(bf16[48,256]{1,0:T(8,128)(2,1)S(1)} %get-tuple-element.108.one), channel_id=1, source_target_pairs={{0,128},{64,192},{128,0},{192,64},{1,129},{65,193},{129,1},{193,65... | collective-permute-start | bytes 73736 | tf_op jit(solution)/shard_map/ppermute | solution.py:703
  124.7 4.8 %collective-permute-start.17 = (bf16[48,256]{1,0:T(8,128)(2,1)S(1)}, bf16[48,256]{1,0:T(8,128)(2,1)S(1)}, u32[]{:S(2)}, u32[]{:S(2)}) collective-permute-start(bf16[48,256]{1,0:T(8,128)(2,1)S(1)} %get-tuple-element.108.one), channel_id=1, source_target_pairs={{0,64},{64,128},{128,192},{192,0},{1,65},{65,129},{129,193},{193,1... | collective-permute-start | bytes 73736 | tf_op jit(solution)/shard_map/ppermute | solution.py:703
  142.2 3.6 %collective-permute-start.20 = (bf16[144,256]{1,0:T(8,128)(2,1)S(1)}, bf16[144,256]{1,0:T(8,128)(2,1)S(1)}, u32[]{:S(2)}, u32[]{:S(2)}) collective-permute-start(bf16[144,256]{1,0:T(8,128)(2,1)S(1)} %shard_map.97.one), channel_id=1, source_target_pairs={{0,64},{64,0},{128,192},{192,128},{1,65},{65,1},{129,193},{193,129... | collective-permute-start | bytes 221192 | tf_op jit(solution)/shard_map/ppermute | solution.py:709
  146.4 4.2 %collective-permute-start.21 = (bf16[144,256]{1,0:T(8,128)(2,1)S(1)}, bf16[144,256]{1,0:T(8,128)(2,1)S(1)}, u32[]{:S(2)}, u32[]{:S(2)}) collective-permute-start(bf16[144,256]{1,0:T(8,128)(2,1)S(1)} %shard_map.98.one), channel_id=1, source_target_pairs={{0,128},{64,192},{128,0},{192,64},{1,129},{65,193},{129,1},{193,65... | collective-permute-start | bytes 221192 | tf_op jit(solution)/shard_map/ppermute | solution.py:709
  151.1 9.4 %collective-permute-start.22 = (bf16[144,256]{1,0:T(8,128)(2,1)S(1)}, bf16[144,256]{1,0:T(8,128)(2,1)S(1)}, u32[]{:S(2)}, u32[]{:S(2)}) collective-permute-start(bf16[144,256]{1,0:T(8,128)(2,1)S(1)} %shard_map.99.one), channel_id=1, source_target_pairs={{0,56},{1,57},{2,58},{3,59},{4,60},{5,61},{6,62},{7,63},{8,48},{9,... | collective-permute-start | bytes 221192 | tf_op jit(solution)/shard_map/ppermute | solution.py:711
  162.1 3.8 %copy-start.16 = (bf16[192,256]{1,0:T(8,128)(2,1)S(1)}, bf16[192,256]{1,0:T(8,128)(2,1)}, u32[]{:S(2)}) copy-start(bf16[192,256]{1,0:T(8,128)(2,1)} %get-tuple-element.112.pick) | copy-start | bytes 294916
  162.1 30.4 %all-to-all-start.4 = ((bf16[16,144,256]{2,1,0:T(8,128)(2,1)}), bf16[16,144,256]{2,1,0:T(8,128)(2,1)S(1)}, u32[]{:S(2)}, u32[]{:S(2)}) async-start(bf16[16,144,256]{2,1,0:T(8,128)(2,1)} %shard_map.100), calls=%async_computation.4 | async-start | bytes 2359296 | tf_op jit(solution)/shard_map/all_to_all | solution.py:726
  166.7 16.2 %collective-permute-start.23 = (bf16[48,256]{1,0:T(8,128)(2,1)S(1)}, bf16[48,256]{1,0:T(8,128)(2,1)S(1)}, u32[]{:S(2)}, u32[]{:S(2)}) collective-permute-start(bf16[48,256]{1,0:T(8,128)(2,1)S(1)} %get-tuple-element.114), channel_id=1, source_target_pairs={{0,7},{1,6},{2,5},{3,4},{4,3},{5,2},{6,1},{7,0},{8,15},{9,14},{10,... | collective-permute-start | bytes 73736 | tf_op jit(solution)/shard_map/ppermute | solution.py:716
  174.4 8.8 %collective-permute-start.24 = (bf16[48,256]{1,0:T(8,128)(2,1)S(1)}, bf16[48,256]{1,0:T(8,128)(2,1)S(1)}, u32[]{:S(2)}, u32[]{:S(2)}) collective-permute-start(bf16[48,256]{1,0:T(8,128)(2,1)S(1)} %get-tuple-element.115), channel_id=1, source_target_pairs={{0,56},{1,57},{2,58},{3,59},{4,60},{5,61},{6,62},{7,63},{8,48},{9,... | collective-permute-start | bytes 73736 | tf_op jit(solution)/shard_map/ppermute | solution.py:716
  179.9 11.4 %collective-permute-start.25 = (bf16[48,256]{1,0:T(8,128)(2,1)S(1)}, bf16[48,256]{1,0:T(8,128)(2,1)S(1)}, u32[]{:S(2)}, u32[]{:S(2)}) collective-permute-start(bf16[48,256]{1,0:T(8,128)(2,1)S(1)} %get-tuple-element.116), channel_id=1, source_target_pairs={{0,63},{1,62},{2,61},{3,60},{4,59},{5,58},{6,57},{7,56},{8,55},{9,... | collective-permute-start | bytes 73736 | tf_op jit(solution)/shard_map/ppermute | solution.py:716
  192.5 2.8 %collective-permute-start.26 = (bf16[16,144,256]{2,1,0:T(8,128)(2,1)S(1)}, bf16[16,144,256]{2,1,0:T(8,128)(2,1)S(1)}, u32[]{:S(2)}, u32[]{:S(2)}) collective-permute-start(bf16[16,144,256]{2,1,0:T(8,128)(2,1)S(1)} %all-to-all-done.4.refs_1_), channel_id=1, source_target_pairs={{0,1},{1,0},{2,3},{3,2},{4,5},{5,4},{6,7},{7,6},{8,9},{9,8},{10,11... | collective-permute-start | bytes 3538952 | tf_op jit(solution)/shard_map/ppermute | solution.py:729
  (2 other events, 1.3 us)

commit v15 on v13

--- a/solution.py
+++ b/solution.py
@@ -377,17 +377,17 @@
     own[...] = cells[0:192, :].astype(BF16)
 
 
-def share_kernel(pos, one, two, three, four, pick, own, by_col, by_row, by_both):
+def share_kernel(pos, one, two, three, four, pick, own, by_col, by_row):
     strips = [one[...], two[...], three[...], four[...], jnp.zeros((64, C), BF16)]
     total = dot(pick[...], jnp.concatenate(strips, axis=0), ((1,), (0,)))
     own[...] = total[0:48]
-    for i, out in enumerate((by_col, by_row, by_both)):
-        out[...] = total[48 * (i + 1) : 48 * (i + 2)].astype(BF16)
-
-
-def final_kernel(pos, own, mine, by_col, by_row, by_both, out, cells, lines):
-    row, col = pos[0], pos[1]
-    lines[...] = mine[...] + by_col[...].astype(F32) + by_row[...].astype(F32) + by_both[...].astype(F32)
+    by_col[...] = total[48:96].astype(BF16)
+    by_row[...] = total[96:192].astype(BF16)
+
+
+def final_kernel(pos, own, mine, by_col, out, cells, lines):
+    row, col = pos[0], pos[1]
+    lines[...] = mine[...] + by_col[...].astype(F32)
     cells[...] = own[...].astype(F32)
     for f in range(3):
         base = f * 64
@@ -453,10 +453,17 @@
     out[...] = (one[...].astype(F32) + two[...].astype(F32)).astype(BF16)
 
 
-def gather_kernel(pos, one, two, out):
+def add_more_kernel(pos, one, two, more, out):
     total = (one[...].astype(F32) + two[...].astype(F32)).astype(BF16)
+    out[...] = jnp.concatenate([total, more[...]], axis=0)
+
+
+def gather_kernel(pos, one, two, mine, by_col, out, own, onward):
+    total = (one[0:144, :].astype(F32) + two[0:144, :].astype(F32)).astype(BF16)
     for i in range(16):
         out[i] = total
+    own[...] = mine[...] + two[144:192, :].astype(F32)
+    onward[...] = (by_col[...].astype(F32) + two[192:240, :].astype(F32)).astype(BF16)
 
 
 def place_kernel(swap, pos, part, *refs):
@@ -702,26 +709,20 @@
     part, strips = lax.optimization_barrier((part, strips))
     faces = [strips] + [lax.ppermute(strips, "face", [(i, (i + by) % 4) for i in range(4)]) for by in (1, 2, 3)]
     part = lax.all_to_all(part, AXES, 0, 0, axis_index_groups=PLANE_GROUPS)
-    strip = (48, C)
-    mine, *shares = run(share_kernel, [(strip, F32)] + [(strip, BF16)] * 3, [], pos, *faces, add_8)
-    shares = [lax.ppermute(v, TILE, [(t, t ^ m) for t in range(64)]) for v, m in zip(shares, MIRRORS[1:])]
-    piece = [((144, C), BF16)]
+    strip, piece = (48, C), [((144, C), BF16)]
+    shares = run(share_kernel, [(strip, F32), (strip, BF16), ((96, C), BF16)], [], pos, *faces, add_8)
+    part, mine, by_col, by_row = lax.optimization_barrier((part, *shares))
     part = run(plane_kernel, piece, [], pos, part)[0]
-    for by in (1, 2):
-        got = lax.ppermute(part, "face", [(i, i ^ by) for i in range(4)])
-        part = run(add_kernel, piece, [], pos, part, got)[0]
+    got = lax.ppermute(part, "face", [(i, i ^ 1) for i in range(4)])
+    part = run(add_kernel, piece, [], pos, part, got)[0]
+    got = lax.ppermute(part, "face", [(i, i ^ 2) for i in range(4)])
+    part = run(add_more_kernel, [((240, C), BF16)], [], pos, part, got, by_row)[0]
     got = lax.ppermute(part, TILE, [(t, t ^ 56) for t in range(64)])
-    part, got, *shares = lax.optimization_barrier((part, got, *shares))
-    part = run(gather_kernel, [((16, 144, C), BF16)], [], pos, part, got)[0]
-    input_grad = run(
-        final_kernel,
-        [((192, C), BF16)],
-        [((192, C), F32), ((48, C), F32)],
-        pos,
-        own,
-        mine,
-        *shares,
-    )[0]
+    outs = [((16, 144, C), BF16), (strip, F32), (strip, BF16)]
+    part, mine, onward = run(gather_kernel, outs, [], pos, part, got, mine, by_col)
+    onward = lax.ppermute(onward, TILE, [(t, t ^ 7) for t in range(64)])
+    scratch = [((192, C), F32), ((48, C), F32)]
+    input_grad = run(final_kernel, [((192, C), BF16)], scratch, pos, own, mine, onward)[0]
     part = lax.all_to_all(part, AXES, 0, 0, axis_index_groups=PLANE_GROUPS)
     part, input_grad = lax.optimization_barrier((part, input_grad))
     grads = place(False, pos, part, [])

time: 215 us -> 193 us (0.90)
  blocking collectives: 51.2 us -> 25.6 us
  starting transfers between devices: 62.1 us -> 68.8 us
  waiting for transfers between devices: 60.6 us -> 56.6 us
    all_to_all x1 -> x0, blocking collectives: 25.6 us -> none  [body(): part = lax.all_to_all(part, AXES, 0, 0, axis_index_groups=PLANE_GROUPS)]
    all_to_all x1 -> x2, waiting for transfers between devices: 20.5 us -> 11.4 us  [body(): part = lax.all_to_all(part, AXES, 0, 0, axis_index_groups=PLANE_GROUPS)]
    all_to_all x1 -> x2, starting transfers between devices: 3.7 us -> 11.2 us  [body(): part = lax.all_to_all(part, AXES, 0, 0, axis_index_groups=PLANE_GROUPS)]
    ppermute x5 -> x3, starting transfers between devices: 17.3 us -> 12.1 us  [the longest x1 8.03 us: body(): onward = lax.ppermute(onward, TILE, [(t, t ^ 7) for t in range(64)])]
    ppermute x1, waiting for transfers between devices: 0.01 us -> 4 us  [body(): got = lax.ppermute(part, TILE, [(t, t ^ 56) for t in range(64)])]
    ppermute x3, starting transfers between devices: 1.47 us -> 4.03 us  [body(): lax.ppermute(strips, 'face', [(i, (i + by) % 4) for i in range(4)])]
    ppermute x5 -> x3, waiting for transfers between devices: 10.8 us -> 12.6 us  [the longest x1 8.9 us: body(): onward = lax.ppermute(onward, TILE, [(t, t ^ 7) for t in range(64)])]
  transfers between devices with their start and end apart: 30 -> 29, of which waited for: 16 -> 15; matrix products, arithmetic and copies ran while one was open for 1% -> 1% of each run, Pallas kernels for 7% -> 8%
where the time goes in v15:
time: 193 us; the launch traced here: 192 us
  starting transfers between devices  68.8 us (36%)
  waiting for transfers between devices  56.6 us (29%)
  Pallas kernels  31.8 us (16%)
  blocking collectives  25.6 us (13%)
  local copies, waits for them, and re-layouts  7.75 us (4%)
    all_to_all x1, blocking collectives, seam_exchange(): got = lax.all_to_all(send, AXES, 0, 0, axis_index_groups=SEAM_GROUPS)  25.6 us
    pallas_call x17, Pallas kernels, run(): pl.pallas_call(inner, out_shape=[jax.ShapeDtypeStruct(shape, dtype) for s...  25 us
    all_to_all x2, starting transfers between devices, seam_exchange(): got = lax.all_to_all(send, AXES, 0, 0, axis_index_groups=SEAM_GROUPS)  20.1 us
    all_to_all x2, waiting for transfers between devices, seam_exchange(): got = lax.all_to_all(send, AXES, 0, 0, axis_index_groups=SEAM_GROUPS)  12.9 us
    all_to_all x2, waiting for transfers between devices, body(): part = lax.all_to_all(part, AXES, 0, 0, axis_index_groups=PLANE_GROUPS)  11.4 us
    all_to_all x2, starting transfers between devices, body(): part = lax.all_to_all(part, AXES, 0, 0, axis_index_groups=PLANE_GROUPS)  11.2 us
    ppermute x1, waiting for transfers between devices, body(): onward = lax.ppermute(onward, TILE, [(t, t ^ 7) for t in range(64)])  8.9 us
    ppermute x1, starting transfers between devices, body(): onward = lax.ppermute(onward, TILE, [(t, t ^ 7) for t in range(64)])  8.03 us
  transfers between devices with their start and end apart: 29, of which 15 were waited for; matrix products, arithmetic and copies ran while one was open for 1% of the time, Pallas kernels for 8%

profile of v15, /device:TPU:1, one launch (start us, length us, event | category | flops | bytes accessed | tf_op | source)
XLA Modules:
  0.0 191.8 jit_solution(13558382017348034779)
XLA Ops:
  0.7 1.0 copy-done.4
  1.7 1.3 shard_map.85
  3.0 14.3 %all-to-all-start = ((bf16[16,48,256]{2,1,0:T(8,128)(2,1)}), bf16[16,48,256]{2,1,0:T(8,128)(2,1)S(1)}, u32[]{:S(2)}, u32[]{:S(2)}) async-start(bf16[16,48,256]{2,1,0:T(8,128)(2,1)} %shard_map.85), calls=%async_computation | async-start | bytes 786432 | tf_op jit(solution)/shard_map/all_to_all | solution.py:499
  17.4 1.9 %collective-permute-start.1 = (bf16[192,256]{1,0:T(8,128)(2,1)S(1)}, bf16[192,256]{1,0:T(8,128)(2,1)S(1)}, u32[]{:S(2)}, u32[]{:S(2)}) collective-permute-start(bf16[192,256]{1,0:T(8,128)(2,1)S(1)} %bitcast.18), channel_id=1, source_target_pairs={{1,2},{3,4},{5,6},{9,10},{11,12},{13,14},{17,18},{19,20},{21,22},{... | collective-permute-start | bytes 294920 | tf_op jit(solution)/shard_map/ppermute | solution.py:623
  19.4 4.2 %collective-permute-done.1.odd = bf16[192,256]{1,0:T(8,128)(2,1)S(1)} collective-permute-done((bf16[192,256]{1,0:T(8,128)(2,1)S(1)}, bf16[192,256]{1,0:T(8,128)(2,1)S(1)}, u32[]{:S(2)}, u32[]{:S(2)}) %collective-permute-start.1) | collective-permute-done | bytes 98336 | tf_op jit(solution)/shard_map/ppermute | solution.py:623
  26.5 2.6 %shard_map.87 = (bf16[80,768]{1,0:T(8,128)(2,1)}, bf16[64,1024]{1,0:T(8,128)(2,1)}, bf16[64,1024]{1,0:T(8,128)(2,1)}, bf16[192,256]{1,0:T(8,128)(2,1)}) custom-call(s32[4]{0:T(128)} %copy-done.6, s32[12,4]{1,0:T(8,128)} %copy.11.nexts, s32[12,4]{1,0:T(8,128)} %copy.12.codes), custom_call_target="tpu_custom_call" | custom-call | tf_op jit(solution)/shard_map/pallas_call | solution.py:590
  29.1 4.9 %all-to-all-done = bf16[16,48,256]{2,1,0:T(8,128)(2,1)S(1)} async-done(((bf16[16,48,256]{2,1,0:T(8,128)(2,1)}), bf16[16,48,256]{2,1,0:T(8,128)(2,1)S(1)}, u32[]{:S(2)}, u32[]{:S(2)}) %all-to-all-start) | async-done | bytes 393248 | tf_op jit(solution)/shard_map/all_to_all | solution.py:499
  34.6 0.9 copy-done.14
  36.4 1.9 %collective-permute-start.5 = (bf16[16,256]{1,0:T(8,128)(2,1)S(1)}, bf16[16,256]{1,0:T(8,128)(2,1)S(1)}, u32[]{:S(2)}, u32[]{:S(2)}) collective-permute-start(bf16[16,256]{1,0:T(8,128)(2,1)S(1)} %get-tuple-element.72), channel_id=1, source_target_pairs={{1,2},{3,4},{5,6},{9,10},{11,12},{13,14},{17,18},{19,20},{21,22},{... | collective-permute-start | bytes 24584 | tf_op jit(solution)/shard_map/ppermute | solution.py:630
  39.1 2.3 %collective-permute-done.5.refs_6_ = bf16[16,256]{1,0:T(8,128)(2,1)S(1)} collective-permute-done((bf16[16,256]{1,0:T(8,128)(2,1)S(1)}, bf16[16,256]{1,0:T(8,128)(2,1)S(1)}, u32[]{:S(2)}, u32[]{:S(2)}) %collective-permute-start.5) | collective-permute-done | bytes 8224 | tf_op jit(solution)/shard_map/ppermute | solution.py:630
  42.0 2.3 %shard_map.89 = (bf16[576,256]{1,0:T(8,128)(2,1)}, f32[480,256]{1,0:T(8,128)S(1)}, bf16[480,256]{1,0:T(8,128)(2,1)S(1)}, bf16[16,64,256]{2,1,0:T(8,128)(2,1)S(1)}) custom-call(s32[4]{0:T(128)S(1)} %copy-done.8, bf16[384,256]{1,0:T(8,128)(2,1)S(1)} %get-tuple-element.63.refs_1_, bf16[96,256]{1,0:T(8,128)(2,1)S(1)} %collective-permute-done.2.refs_2_, ...), custom_call_target="tpu_custom_call" | custom-call | tf_op jit(solution)/shard_map/pallas_call | solution.py:78
  45.1 25.6 %all_to_all.25 = bf16[16,64,256]{2,1,0:T(8,128)(2,1)S(1)} all-to-all(bf16[16,64,256]{2,1,0:T(8,128)(2,1)S(1)} %get-tuple-element.77), channel_id=1, replica_groups={{0,7,56,63,64,71,120,127,128,135,184,191,192,199,248,255},{1,6,57,62,65..., dimensions={0} | all-to-all | bytes 1048576 | tf_op jit(solution)/shard_map/all_to_all | solution.py:499
  70.6 2.6 %shard_map.90 = (bf16[864,256]{1,0:T(8,128)(2,1)}, bf16[192,256]{1,0:T(8,128)(2,1)S(1)}, bf16[16,256]{1,0:T(8,128)(2,1)S(1)}, bf16[16,256]{1,0:T(8,128)(2,1)S(1)}) custom-call(s32[4]{0:T(128)S(1)} %copy-done.8, bf16[480,256]{1,0:T(8,128)(2,1)S(1)} %get-tuple-element.76.refs_1_, bf16[1024,256]{1,0:T(8,128)(2,1)S(1)} %bitcast.14, ...), custom_call_target="tpu_custom_call" | custom-call | tf_op jit(solution)/shard_map/pallas_call | solution.py:78
  73.3 2.0 %collective-permute-start.10 = (bf16[192,256]{1,0:T(8,128)(2,1)S(1)}, bf16[192,256]{1,0:T(8,128)(2,1)S(1)}, u32[]{:S(2)}, u32[]{:S(2)}) collective-permute-start(bf16[192,256]{1,0:T(8,128)(2,1)S(1)} %get-tuple-element.79.refs_1_), channel_id=1, source_target_pairs={{1,2},{3,4},{5,6},{9,10},{11,12},{13,14},{17,18},{19,20},{21,22},{... | collective-permute-start | bytes 294920 | tf_op jit(solution)/shard_map/ppermute | solution.py:613
  76.2 1.8 collective-permute-done.11.refs_4_
  78.0 1.2 collective-permute-done.10.refs_3_
  79.2 2.2 %shard_map.91 = (bf16[384,256]{1,0:T(8,128)(2,1)S(1)}, bf16[96,256]{1,0:T(8,128)(2,1)S(1)}, bf16[96,256]{1,0:T(8,128)(2,1)S(1)}, bf16[16,64,256]{2,1,0:T(8,128)(2,1)}) custom-call(s32[4]{0:T(128)S(1)} %copy-done.8, bf16[192,256]{1,0:T(8,128)(2,1)S(1)} %get-tuple-element.79.refs_1_, bf16[192,256]{1,0:T(8,128)(2,1)S(1)} %collective-permute-done.9.refs_2_, ...), custom_call_target="tpu_custom_call" | custom-call | tf_op jit(solution)/shard_map/pallas_call | solution.py:78
  82.1 5.7 %all-to-all-start.2 = ((bf16[16,64,256]{2,1,0:T(8,128)(2,1)}), bf16[16,64,256]{2,1,0:T(8,128)(2,1)S(1)}, u32[]{:S(2)}, u32[]{:S(2)}) async-start(bf16[16,64,256]{2,1,0:T(8,128)(2,1)} %get-tuple-element.85), calls=%async_computation.2 | async-start | bytes 1048576 | tf_op jit(solution)/shard_map/all_to_all | solution.py:499
  88.4 3.2 %collective-permute-start.13 = (bf16[96,256]{1,0:T(8,128)(2,1)S(1)}, bf16[96,256]{1,0:T(8,128)(2,1)S(1)}, u32[]{:S(2)}, u32[]{:S(2)}) collective-permute-start(bf16[96,256]{1,0:T(8,128)(2,1)S(1)} %get-tuple-element.83), channel_id=1, source_target_pairs={{0,8},{1,9},{2,10},{3,11},{4,12},{5,13},{6,14},{7,15},{16,24},{17,... | collective-permute-start | bytes 147464 | tf_op jit(solution)/shard_map/ppermute | solution.py:667
  92.3 2.2 %collective-permute-done.13.refs_2_ = bf16[96,256]{1,0:T(8,128)(2,1)S(1)} collective-permute-done((bf16[96,256]{1,0:T(8,128)(2,1)S(1)}, bf16[96,256]{1,0:T(8,128)(2,1)S(1)}, u32[]{:S(2)}, u32[]{:S(2)}) %collective-permute-start.13) | collective-permute-done | bytes 49184 | tf_op jit(solution)/shard_map/ppermute | solution.py:667
  94.5 0.9 copy-done.11
  95.4 1.6 shard_map.92.refs_1_
  97.1 1.9 %shard_map.93.two = bf16[16,72,256]{2,1,0:T(8,128)(2,1)S(1)} custom-call(s32[4]{0:T(128)S(1)} %copy-done.9, bf16[864,256]{1,0:T(8,128)(2,1)} %get-tuple-element.86.own, bf16[864,256]{1,0:T(8,128)(2,1)S(1)} %collective-permute-done.15.other), custom_call_target="tpu_custom_call" | custom-call | tf_op jit(solution)/shard_map/pallas_call | solution.py:78
  99.0 8.0 %all-to-all-done.2 = bf16[16,64,256]{2,1,0:T(8,128)(2,1)S(1)} async-done(((bf16[16,64,256]{2,1,0:T(8,128)(2,1)}), bf16[16,64,256]{2,1,0:T(8,128)(2,1)S(1)}, u32[]{:S(2)}, u32[]{:S(2)}) %all-to-all-start.2) | async-done | bytes 524320 | tf_op jit(solution)/shard_map/all_to_all | solution.py:499
  107.0 0.9 copy-done.12
  107.9 2.5 %shard_map.94 = (bf16[384,256]{1,0:T(8,128)(2,1)S(1)}, bf16[192,256]{1,0:T(8,128)(2,1)S(1)}, bf16[48,256]{1,0:T(8,128)(2,1)S(1)}) custom-call(s32[4]{0:T(128)S(1)} %copy-done.9, bf16[480,256]{1,0:T(8,128)(2,1)S(1)} %shard_map.92.refs_1_, bf16[1024,256]{1,0:T(8,128)(2,1)S(1)} %bitcast.15, bf16[64,1024]{1,0:T(8,128)(2,1)S(1)} %copy-done.12, ...), custom_call_target="tpu_custom_call" | custom-call | tf_op jit(solution)/shard_map/pallas_call | solution.py:78
  110.5 1.5 shard_map.95.part
  112.1 2.1 %shard_map.96 = bf16[16,144,256]{2,1,0:T(8,128)(2,1)} custom-call(s32[4]{0:T(128)S(1)} %copy-done.9, bf16[576,256]{1,0:T(8,128)(2,1)S(1)} %collective-permute-done.8.source, bf16[384,256]{1,0:T(8,128)(2,1)S(1)} %collective-permute-done.16.delta, f32[16,72,256]{2,1,0:T(8,128)S(1)} %shard_map.95.part, bf16[16,72,256]{2,1,0:T(8,128)(2,1)S(1)} %shard_map.93.two), custom_call_target="tpu_custom_call" | custom-call | tf_op jit(solution)/shard_map/pallas_call | solution.py:78
  114.2 7.5 %all-to-all-start.3 = ((bf16[16,144,256]{2,1,0:T(8,128)(2,1)}), bf16[16,144,256]{2,1,0:T(8,128)(2,1)S(1)}, u32[]{:S(2)}, u32[]{:S(2)}) async-start(bf16[16,144,256]{2,1,0:T(8,128)(2,1)} %shard_map.96), calls=%async_computation.3 | async-start | bytes 2359296 | tf_op jit(solution)/shard_map/all_to_all | solution.py:711
  121.7 2.1 %collective-permute-start.19 = (bf16[48,256]{1,0:T(8,128)(2,1)S(1)}, bf16[48,256]{1,0:T(8,128)(2,1)S(1)}, u32[]{:S(2)}, u32[]{:S(2)}) collective-permute-start(bf16[48,256]{1,0:T(8,128)(2,1)S(1)} %get-tuple-element.94.one), channel_id=1, source_target_pairs={{0,192},{64,0},{128,64},{192,128},{1,193},{65,1},{129,65},{193,129... | collective-permute-start | bytes 73736 | tf_op jit(solution)/shard_map/ppermute | solution.py:710
  124.7 1.0 collective-permute-start.17
  125.8 1.9 %collective-permute-done.18.three = bf16[48,256]{1,0:T(8,128)(2,1)S(1)} collective-permute-done((bf16[48,256]{1,0:T(8,128)(2,1)S(1)}, bf16[48,256]{1,0:T(8,128)(2,1)S(1)}, u32[]{:S(2)}, u32[]{:S(2)}) %collective-permute-start.18) | collective-permute-done | bytes 24608 | tf_op jit(solution)/shard_map/ppermute | solution.py:710
  127.7 1.8 collective-permute-done.17.two
  130.2 11.4 %all-to-all-done.3.parts = bf16[16,144,256]{2,1,0:T(8,128)(2,1)S(1)} async-done(((bf16[16,144,256]{2,1,0:T(8,128)(2,1)}), bf16[16,144,256]{2,1,0:T(8,128)(2,1)S(1)}, u32[]{:S(2)}, u32[]{:S(2)}) %all-to-all-start.3) | async-done | bytes 1179680 | tf_op jit(solution)/shard_map/all_to_all | solution.py:711
  142.3 1.8 collective-permute-start.20
  144.1 1.7 collective-permute-done.20.two
  146.4 2.3 %collective-permute-start.21 = (bf16[144,256]{1,0:T(8,128)(2,1)S(1)}, bf16[144,256]{1,0:T(8,128)(2,1)S(1)}, u32[]{:S(2)}, u32[]{:S(2)}) collective-permute-start(bf16[144,256]{1,0:T(8,128)(2,1)S(1)} %shard_map.99.one), channel_id=1, source_target_pairs={{0,128},{64,192},{128,0},{192,64},{1,129},{65,193},{129,1},{193,65... | collective-permute-start | bytes 221192 | tf_op jit(solution)/shard_map/ppermute | solution.py:718
  148.7 1.9 %collective-permute-done.21.two = bf16[144,256]{1,0:T(8,128)(2,1)S(1)} collective-permute-done((bf16[144,256]{1,0:T(8,128)(2,1)S(1)}, bf16[144,256]{1,0:T(8,128)(2,1)S(1)}, u32[]{:S(2)}, u32[]{:S(2)}) %collective-permute-start.21) | collective-permute-done | bytes 73760 | tf_op jit(solution)/shard_map/ppermute | solution.py:718
  151.2 6.0 %collective-permute-start.22 = (bf16[240,256]{1,0:T(8,128)(2,1)S(1)}, bf16[240,256]{1,0:T(8,128)(2,1)S(1)}, u32[]{:S(2)}, u32[]{:S(2)}) collective-permute-start(bf16[240,256]{1,0:T(8,128)(2,1)S(1)} %shard_map.100.one), channel_id=1, source_target_pairs={{0,56},{1,57},{2,58},{3,59},{4,60},{5,61},{6,62},{7,63},{8,48},{9,... | collective-permute-start | bytes 368648 | tf_op jit(solution)/shard_map/ppermute | solution.py:720
  157.2 4.0 %collective-permute-done.22.two = bf16[240,256]{1,0:T(8,128)(2,1)S(1)} collective-permute-done((bf16[240,256]{1,0:T(8,128)(2,1)S(1)}, bf16[240,256]{1,0:T(8,128)(2,1)S(1)}, u32[]{:S(2)}, u32[]{:S(2)}) %collective-permute-start.22) | collective-permute-done | bytes 122912 | tf_op jit(solution)/shard_map/ppermute | solution.py:720
  161.2 1.6 shard_map.101
  162.8 3.7 %all-to-all-start.4 = ((bf16[16,144,256]{2,1,0:T(8,128)(2,1)}), bf16[16,144,256]{2,1,0:T(8,128)(2,1)S(1)}, u32[]{:S(2)}, u32[]{:S(2)}) async-start(bf16[16,144,256]{2,1,0:T(8,128)(2,1)} %get-tuple-element.103), calls=%async_computation.4 | async-start | bytes 2359296 | tf_op jit(solution)/shard_map/all_to_all | solution.py:726
  166.5 8.0 %collective-permute-start.23 = (bf16[48,256]{1,0:T(8,128)(2,1)S(1)}, bf16[48,256]{1,0:T(8,128)(2,1)S(1)}, u32[]{:S(2)}, u32[]{:S(2)}) collective-permute-start(bf16[48,256]{1,0:T(8,128)(2,1)S(1)} %get-tuple-element.106), channel_id=1, source_target_pairs={{0,7},{1,6},{2,5},{3,4},{4,3},{5,2},{6,1},{7,0},{8,15},{9,14},{10,... | collective-permute-start | bytes 73736 | tf_op jit(solution)/shard_map/ppermute | solution.py:723
  174.5 8.9 %collective-permute-done.23.by_col = bf16[48,256]{1,0:T(8,128)(2,1)S(1)} collective-permute-done((bf16[48,256]{1,0:T(8,128)(2,1)S(1)}, bf16[48,256]{1,0:T(8,128)(2,1)S(1)}, u32[]{:S(2)}, u32[]{:S(2)}) %collective-permute-start.23) | collective-permute-done | bytes 24608 | tf_op jit(solution)/shard_map/ppermute | solution.py:723
  183.4 1.3 shard_map.102
  184.7 2.4 %collective-permute-start.24 = (bf16[16,144,256]{2,1,0:T(8,128)(2,1)S(1)}, bf16[16,144,256]{2,1,0:T(8,128)(2,1)S(1)}, u32[]{:S(2)}, u32[]{:S(2)}) collective-permute-start(bf16[16,144,256]{2,1,0:T(8,128)(2,1)S(1)} %all-to-all-done.4.refs_1_), channel_id=1, source_target_pairs={{0,1},{1,0},{2,3},{3,2},{4,5},{5,4},{6,7},{7,6},{8,9},{9,8},{10,11... | collective-permute-start | bytes 3538952 | tf_op jit(solution)/shard_map/ppermute | solution.py:729
  187.1 2.1 %shard_map.103 = (f32[9,256,256]{2,1,0:T(8,128)}, f32[9,256,256]{2,1,0:T(8,128)}) custom-call(s32[4]{0:T(128)S(1)} %copy-done.9, bf16[16,144,256]{2,1,0:T(8,128)(2,1)S(1)} %all-to-all-done.4.refs_1_), custom_call_target="tpu_custom_call" | custom-call | tf_op jit(solution)/shard_map/pallas_call | solution.py:487
  189.6 2.1 %shard_map.104 = (f32[9,256,256]{2,1,0:T(8,128)}, f32[9,256,256]{2,1,0:T(8,128)}) custom-call(s32[4]{0:T(128)S(1)} %copy-done.9, bf16[16,144,256]{2,1,0:T(8,128)(2,1)S(1)} %collective-permute-done.24.refs_1_, f32[9,256,256]{2,1,0:T(8,128)} %get-tuple-element.109.refs_2_, ...), custom_call_target="tpu_custom_call", output_to_operand_aliasing={{0}: (2, {}), {1}: (3, {})} | custom-call | tf_op jit(solution)/shard_map/pallas_call | solution.py:487
  (72 shorter events, 13.3 us)
Async XLA Ops:
  0.6 40.7 %copy-start.1 = (bf16[3,3,256,256]{3,2,1,0:T(8,128)(2,1)S(1)}, bf16[3,3,256,256]{3,2,1,0:T(8,128)(2,1)}, u32[]{:S(2)}) copy-start(bf16[3,3,256,256]{3,2,1,0:T(8,128)(2,1)} %refs_5_.3) | copy-start | bytes 3538948
  0.7 25.7 %copy-start.6 = (s32[4]{0:T(128)}, s32[4]{0:T(128)S(1)}, u32[]{:S(2)}) copy-start(s32[4]{0:T(128)S(1)} %pad_add_fusion.pos.refs_0_) | copy-start | bytes 52
  0.7 1.0 copy-start.4
  1.7 15.7 %copy-start.5 = (bf16[3,1,8,8,256]{4,3,2,1,0:T(8,128)(2,1)S(1)}, bf16[3,1,8,8,256]{4,3,2,1,0:T(8,128)(2,1)}, u32[]{:S(2)}) copy-start(bf16[3,1,8,8,256]{4,3,2,1,0:T(8,128)(2,1)} %param.6) | copy-start | bytes 294916
  1.7 23.4 %copy-start.17 = (s32[12,4]{0,1:T(4,128)S(1)}, s32[12,4]{0,1:T(4,128)}, u32[]{:S(2)}) copy-start(s32[12,4]{0,1:T(4,128)} %param.10) | copy-start | bytes 580
  1.7 24.1 %copy-start.18 = (s32[12,4]{0,1:T(4,128)S(1)}, s32[12,4]{0,1:T(4,128)}, u32[]{:S(2)}) copy-start(s32[12,4]{0,1:T(4,128)} %param.11) | copy-start | bytes 580
  3.0 30.9 %all-to-all-start = ((bf16[16,48,256]{2,1,0:T(8,128)(2,1)}), bf16[16,48,256]{2,1,0:T(8,128)(2,1)S(1)}, u32[]{:S(2)}, u32[]{:S(2)}) async-start(bf16[16,48,256]{2,1,0:T(8,128)(2,1)} %shard_map.85), calls=%async_computation | async-start | bytes 786432 | tf_op jit(solution)/shard_map/all_to_all | solution.py:499
  17.4 6.2 %collective-permute-start.1 = (bf16[192,256]{1,0:T(8,128)(2,1)S(1)}, bf16[192,256]{1,0:T(8,128)(2,1)S(1)}, u32[]{:S(2)}, u32[]{:S(2)}) collective-permute-start(bf16[192,256]{1,0:T(8,128)(2,1)S(1)} %bitcast.18), channel_id=1, source_target_pairs={{1,2},{3,4},{5,6},{9,10},{11,12},{13,14},{17,18},{19,20},{21,22},{... | collective-permute-start | bytes 294920 | tf_op jit(solution)/shard_map/ppermute | solution.py:623
  19.3 4.3 %collective-permute-start = (bf16[192,256]{1,0:T(8,128)(2,1)S(1)}, bf16[192,256]{1,0:T(8,128)(2,1)S(1)}, u32[]{:S(2)}, u32[]{:S(2)}) collective-permute-start(bf16[192,256]{1,0:T(8,128)(2,1)S(1)} %bitcast.19), channel_id=1, source_target_pairs={{0,1},{1,0},{2,3},{3,2},{4,5},{5,4},{6,7},{7,6},{8,9},{9,8},{10,11... | collective-permute-start | bytes 294920 | tf_op jit(solution)/shard_map/ppermute | solution.py:623
  24.3 4.8 %collective-permute-start.2 = (bf16[96,256]{1,0:T(8,128)(2,1)S(1)}, bf16[96,256]{1,0:T(8,128)(2,1)S(1)}, u32[]{:S(2)}, u32[]{:S(2)}) collective-permute-start(bf16[96,256]{1,0:T(8,128)(2,1)S(1)} %get-tuple-element.61), channel_id=1, source_target_pairs={{0,8},{1,9},{2,10},{3,11},{4,12},{5,13},{6,14},{7,15},{16,24},{17,... | collective-permute-start | bytes 147464 | tf_op jit(solution)/shard_map/ppermute | solution.py:625
  24.4 4.7 %collective-permute-start.3 = (bf16[96,256]{1,0:T(8,128)(2,1)S(1)}, bf16[96,256]{1,0:T(8,128)(2,1)S(1)}, u32[]{:S(2)}, u32[]{:S(2)}) collective-permute-start(bf16[96,256]{1,0:T(8,128)(2,1)S(1)} %get-tuple-element.62), channel_id=1, source_target_pairs={{8,16},{9,17},{10,18},{11,19},{12,20},{13,21},{14,22},{15,23},{24,... | collective-permute-start | bytes 147464 | tf_op jit(solution)/shard_map/ppermute | solution.py:625
  34.0 0.6 copy-start.7
  34.6 0.9 copy-start.14
  36.3 2.8 %collective-permute-start.4 = (bf16[16,256]{1,0:T(8,128)(2,1)S(1)}, bf16[16,256]{1,0:T(8,128)(2,1)S(1)}, u32[]{:S(2)}, u32[]{:S(2)}) collective-permute-start(bf16[16,256]{1,0:T(8,128)(2,1)S(1)} %get-tuple-element.71), channel_id=1, source_target_pairs={{0,1},{1,0},{2,3},{3,2},{4,5},{5,4},{6,7},{7,6},{8,9},{9,8},{10,11... | collective-permute-start | bytes 24584 | tf_op jit(solution)/shard_map/ppermute | solution.py:629
  36.4 5.0 %collective-permute-start.5 = (bf16[16,256]{1,0:T(8,128)(2,1)S(1)}, bf16[16,256]{1,0:T(8,128)(2,1)S(1)}, u32[]{:S(2)}, u32[]{:S(2)}) collective-permute-start(bf16[16,256]{1,0:T(8,128)(2,1)S(1)} %get-tuple-element.72), channel_id=1, source_target_pairs={{1,2},{3,4},{5,6},{9,10},{11,12},{13,14},{17,18},{19,20},{21,22},{... | collective-permute-start | bytes 24584 | tf_op jit(solution)/shard_map/ppermute | solution.py:630
  38.3 3.0 %collective-permute-start.6 = (bf16[16,256]{1,0:T(8,128)(2,1)S(1)}, bf16[16,256]{1,0:T(8,128)(2,1)S(1)}, u32[]{:S(2)}, u32[]{:S(2)}) collective-permute-start(bf16[16,256]{1,0:T(8,128)(2,1)S(1)} %get-tuple-element.73), channel_id=1, source_target_pairs={{0,8},{1,9},{2,10},{3,11},{4,12},{5,13},{6,14},{7,15},{16,24},{17,... | collective-permute-start | bytes 24584 | tf_op jit(solution)/shard_map/ppermute | solution.py:631
  38.4 2.9 %collective-permute-start.7 = (bf16[16,256]{1,0:T(8,128)(2,1)S(1)}, bf16[16,256]{1,0:T(8,128)(2,1)S(1)}, u32[]{:S(2)}, u32[]{:S(2)}) collective-permute-start(bf16[16,256]{1,0:T(8,128)(2,1)S(1)} %get-tuple-element.74), channel_id=1, source_target_pairs={{8,16},{9,17},{10,18},{11,19},{12,20},{13,21},{14,22},{15,23},{40,... | collective-permute-start | bytes 24584 | tf_op jit(solution)/shard_map/ppermute | solution.py:632
  41.3 0.6 copy-start.8
  42.0 28.7 %copy-start = (bf16[3,3,256,256]{3,2,1,0:T(8,128)(2,1)S(1)}, bf16[3,3,256,256]{3,2,1,0:T(8,128)(2,1)}, u32[]{:S(2)}) copy-start(bf16[3,3,256,256]{3,2,1,0:T(8,128)(2,1)} %refs_4_.1) | copy-start | bytes 3538948
  42.0 28.7 %copy-start.13 = (bf16[64,1024]{1,0:T(8,128)(2,1)S(1)}, bf16[64,1024]{1,0:T(8,128)(2,1)}, u32[]{:S(2)}) copy-start(bf16[64,1024]{1,0:T(8,128)(2,1)} %get-tuple-element.78.refs_3_) | copy-start | bytes 393220
  42.0 28.7 %copy-start.15 = (bf16[3,1,8,8,256]{4,3,2,1,0:T(8,128)(2,1)S(1)}, bf16[3,1,8,8,256]{4,3,2,1,0:T(8,128)(2,1)}, u32[]{:S(2)}) copy-start(bf16[3,1,8,8,256]{4,3,2,1,0:T(8,128)(2,1)} %param.7) | copy-start | bytes 294916
  44.3 0.8 copy-start.2
  73.3 5.9 %collective-permute-start.10 = (bf16[192,256]{1,0:T(8,128)(2,1)S(1)}, bf16[192,256]{1,0:T(8,128)(2,1)S(1)}, u32[]{:S(2)}, u32[]{:S(2)}) collective-permute-start(bf16[192,256]{1,0:T(8,128)(2,1)S(1)} %get-tuple-element.79.refs_1_), channel_id=1, source_target_pairs={{1,2},{3,4},{5,6},{9,10},{11,12},{13,14},{17,18},{19,20},{21,22},{... | collective-permute-start | bytes 294920 | tf_op jit(solution)/shard_map/ppermute | solution.py:613
  75.3 3.9 %collective-permute-start.9 = (bf16[192,256]{1,0:T(8,128)(2,1)S(1)}, bf16[192,256]{1,0:T(8,128)(2,1)S(1)}, u32[]{:S(2)}, u32[]{:S(2)}) collective-permute-start(bf16[192,256]{1,0:T(8,128)(2,1)S(1)} %get-tuple-element.79.refs_1_), channel_id=1, source_target_pairs={{0,1},{1,0},{2,3},{3,2},{4,5},{5,4},{6,7},{7,6},{8,9},{9,8},{10,11... | collective-permute-start | bytes 294920 | tf_op jit(solution)/shard_map/ppermute | solution.py:612
  75.4 2.6 %collective-permute-start.11 = (bf16[16,256]{1,0:T(8,128)(2,1)S(1)}, bf16[16,256]{1,0:T(8,128)(2,1)S(1)}, u32[]{:S(2)}, u32[]{:S(2)}) collective-permute-start(bf16[16,256]{1,0:T(8,128)(2,1)S(1)} %get-tuple-element.80), channel_id=1, source_target_pairs={{0,8},{1,9},{2,10},{3,11},{4,12},{5,13},{6,14},{7,15},{16,24},{17,... | collective-permute-start | bytes 24584 | tf_op jit(solution)/shard_map/ppermute | solution.py:614
  75.5 19.0 %copy-start.9 = (s32[4]{0:T(128)S(1)}, s32[4]{0:T(128)}, u32[]{:S(2)}) copy-start(s32[4]{0:T(128)} %copy-done.6) | copy-start | bytes 52
  75.5 2.5 %collective-permute-start.12 = (bf16[16,256]{1,0:T(8,128)(2,1)S(1)}, bf16[16,256]{1,0:T(8,128)(2,1)S(1)}, u32[]{:S(2)}, u32[]{:S(2)}) collective-permute-start(bf16[16,256]{1,0:T(8,128)(2,1)S(1)} %get-tuple-element.81), channel_id=1, source_target_pairs={{8,16},{9,17},{10,18},{11,19},{12,20},{13,21},{14,22},{15,23},{40,... | collective-permute-start | bytes 24584 | tf_op jit(solution)/shard_map/ppermute | solution.py:615
  81.4 0.7 copy-start.10
  82.1 24.9 %all-to-all-start.2 = ((bf16[16,64,256]{2,1,0:T(8,128)(2,1)}), bf16[16,64,256]{2,1,0:T(8,128)(2,1)S(1)}, u32[]{:S(2)}, u32[]{:S(2)}) async-start(bf16[16,64,256]{2,1,0:T(8,128)(2,1)} %get-tuple-element.85), calls=%async_computation.2 | async-start | bytes 1048576 | tf_op jit(solution)/shard_map/all_to_all | solution.py:499
  87.8 9.3 %collective-permute-start.15 = (bf16[864,256]{1,0:T(8,128)(2,1)}, bf16[864,256]{1,0:T(8,128)(2,1)S(1)}, u32[]{:S(2)}, u32[]{:S(2)}) collective-permute-start(bf16[864,256]{1,0:T(8,128)(2,1)} %get-tuple-element.86.own), channel_id=1, source_target_pairs={{0,1},{1,0},{2,3},{3,2},{4,5},{5,4},{6,7},{7,6},{8,9},{9,8},{10,11... | collective-permute-start | bytes 1327112 | tf_op jit(solution)/shard_map/ppermute | solution.py:683
  87.9 24.1 %collective-permute-start.8 = (bf16[576,256]{1,0:T(8,128)(2,1)}, bf16[576,256]{1,0:T(8,128)(2,1)S(1)}, u32[]{:S(2)}, u32[]{:S(2)}) collective-permute-start(bf16[576,256]{1,0:T(8,128)(2,1)} %get-tuple-element.75.source), channel_id=1, source_target_pairs={{0,1},{1,0},{2,3},{3,2},{4,5},{5,4},{6,7},{7,6},{8,9},{9,8},{10,11... | collective-permute-start | bytes 884744 | tf_op jit(solution)/shard_map/ppermute | solution.py:646
  88.4 6.1 %collective-permute-start.13 = (bf16[96,256]{1,0:T(8,128)(2,1)S(1)}, bf16[96,256]{1,0:T(8,128)(2,1)S(1)}, u32[]{:S(2)}, u32[]{:S(2)}) collective-permute-start(bf16[96,256]{1,0:T(8,128)(2,1)S(1)} %get-tuple-element.83), channel_id=1, source_target_pairs={{0,8},{1,9},{2,10},{3,11},{4,12},{5,13},{6,14},{7,15},{16,24},{17,... | collective-permute-start | bytes 147464 | tf_op jit(solution)/shard_map/ppermute | solution.py:667
  91.7 2.8 %collective-permute-start.14 = (bf16[96,256]{1,0:T(8,128)(2,1)S(1)}, bf16[96,256]{1,0:T(8,128)(2,1)S(1)}, u32[]{:S(2)}, u32[]{:S(2)}) collective-permute-start(bf16[96,256]{1,0:T(8,128)(2,1)S(1)} %get-tuple-element.84), channel_id=1, source_target_pairs={{8,16},{9,17},{10,18},{11,19},{12,20},{13,21},{14,22},{15,23},{24,... | collective-permute-start | bytes 147464 | tf_op jit(solution)/shard_map/ppermute | solution.py:667
  94.5 0.9 copy-start.11
  97.1 9.9 %copy-start.3 = (f32[480,256]{1,0:T(8,128)S(1)}, f32[480,256]{1,0:T(8,128)}, u32[]{:S(2)}) copy-start(f32[480,256]{1,0:T(8,128)} %copy-done.2) | copy-start | bytes 1474564
  107.0 0.9 copy-start.12
  110.4 1.6 collective-permute-start.16
  114.2 15.3 %copy-start.16 = (bf16[192,256]{1,0:T(8,128)(2,1)S(1)}, bf16[192,256]{1,0:T(8,128)(2,1)}, u32[]{:S(2)}) copy-start(bf16[192,256]{1,0:T(8,128)(2,1)} %get-tuple-element.95.pick) | copy-start | bytes 294916
  114.2 27.4 %all-to-all-start.3 = ((bf16[16,144,256]{2,1,0:T(8,128)(2,1)}), bf16[16,144,256]{2,1,0:T(8,128)(2,1)S(1)}, u32[]{:S(2)}, u32[]{:S(2)}) async-start(bf16[16,144,256]{2,1,0:T(8,128)(2,1)} %shard_map.96), calls=%async_computation.3 | async-start | bytes 2359296 | tf_op jit(solution)/shard_map/all_to_all | solution.py:711
  121.7 4.0 %collective-permute-start.19 = (bf16[48,256]{1,0:T(8,128)(2,1)S(1)}, bf16[48,256]{1,0:T(8,128)(2,1)S(1)}, u32[]{:S(2)}, u32[]{:S(2)}) collective-permute-start(bf16[48,256]{1,0:T(8,128)(2,1)S(1)} %get-tuple-element.94.one), channel_id=1, source_target_pairs={{0,192},{64,0},{128,64},{192,128},{1,193},{65,1},{129,65},{193,129... | collective-permute-start | bytes 73736 | tf_op jit(solution)/shard_map/ppermute | solution.py:710
  123.8 3.9 %collective-permute-start.18 = (bf16[48,256]{1,0:T(8,128)(2,1)S(1)}, bf16[48,256]{1,0:T(8,128)(2,1)S(1)}, u32[]{:S(2)}, u32[]{:S(2)}) collective-permute-start(bf16[48,256]{1,0:T(8,128)(2,1)S(1)} %get-tuple-element.94.one), channel_id=1, source_target_pairs={{0,128},{64,192},{128,0},{192,64},{1,129},{65,193},{129,1},{193,65... | collective-permute-start | bytes 73736 | tf_op jit(solution)/shard_map/ppermute | solution.py:710
  124.7 4.8 %collective-permute-start.17 = (bf16[48,256]{1,0:T(8,128)(2,1)S(1)}, bf16[48,256]{1,0:T(8,128)(2,1)S(1)}, u32[]{:S(2)}, u32[]{:S(2)}) collective-permute-start(bf16[48,256]{1,0:T(8,128)(2,1)S(1)} %get-tuple-element.94.one), channel_id=1, source_target_pairs={{0,64},{64,128},{128,192},{192,0},{1,65},{65,129},{129,193},{193,1... | collective-permute-start | bytes 73736 | tf_op jit(solution)/shard_map/ppermute | solution.py:710
  142.3 3.6 %collective-permute-start.20 = (bf16[144,256]{1,0:T(8,128)(2,1)S(1)}, bf16[144,256]{1,0:T(8,128)(2,1)S(1)}, u32[]{:S(2)}, u32[]{:S(2)}) collective-permute-start(bf16[144,256]{1,0:T(8,128)(2,1)S(1)} %shard_map.98.one), channel_id=1, source_target_pairs={{0,64},{64,0},{128,192},{192,128},{1,65},{65,1},{129,193},{193,129... | collective-permute-start | bytes 221192 | tf_op jit(solution)/shard_map/ppermute | solution.py:716
  146.4 4.2 %collective-permute-start.21 = (bf16[144,256]{1,0:T(8,128)(2,1)S(1)}, bf16[144,256]{1,0:T(8,128)(2,1)S(1)}, u32[]{:S(2)}, u32[]{:S(2)}) collective-permute-start(bf16[144,256]{1,0:T(8,128)(2,1)S(1)} %shard_map.99.one), channel_id=1, source_target_pairs={{0,128},{64,192},{128,0},{192,64},{1,129},{65,193},{129,1},{193,65... | collective-permute-start | bytes 221192 | tf_op jit(solution)/shard_map/ppermute | solution.py:718
  151.2 10.0 %collective-permute-start.22 = (bf16[240,256]{1,0:T(8,128)(2,1)S(1)}, bf16[240,256]{1,0:T(8,128)(2,1)S(1)}, u32[]{:S(2)}, u32[]{:S(2)}) collective-permute-start(bf16[240,256]{1,0:T(8,128)(2,1)S(1)} %shard_map.100.one), channel_id=1, source_target_pairs={{0,56},{1,57},{2,58},{3,59},{4,60},{5,61},{6,62},{7,63},{8,48},{9,... | collective-permute-start | bytes 368648 | tf_op jit(solution)/shard_map/ppermute | solution.py:720
  162.8 21.9 %all-to-all-start.4 = ((bf16[16,144,256]{2,1,0:T(8,128)(2,1)}), bf16[16,144,256]{2,1,0:T(8,128)(2,1)S(1)}, u32[]{:S(2)}, u32[]{:S(2)}) async-start(bf16[16,144,256]{2,1,0:T(8,128)(2,1)} %get-tuple-element.103), calls=%async_computation.4 | async-start | bytes 2359296 | tf_op jit(solution)/shard_map/all_to_all | solution.py:726
  166.5 16.9 %collective-permute-start.23 = (bf16[48,256]{1,0:T(8,128)(2,1)S(1)}, bf16[48,256]{1,0:T(8,128)(2,1)S(1)}, u32[]{:S(2)}, u32[]{:S(2)}) collective-permute-start(bf16[48,256]{1,0:T(8,128)(2,1)S(1)} %get-tuple-element.106), channel_id=1, source_target_pairs={{0,7},{1,6},{2,5},{3,4},{4,3},{5,2},{6,1},{7,0},{8,15},{9,14},{10,... | collective-permute-start | bytes 73736 | tf_op jit(solution)/shard_map/ppermute | solution.py:723
  184.7 4.9 %collective-permute-start.24 = (bf16[16,144,256]{2,1,0:T(8,128)(2,1)S(1)}, bf16[16,144,256]{2,1,0:T(8,128)(2,1)S(1)}, u32[]{:S(2)}, u32[]{:S(2)}) collective-permute-start(bf16[16,144,256]{2,1,0:T(8,128)(2,1)S(1)} %all-to-all-done.4.refs_1_), channel_id=1, source_target_pairs={{0,1},{1,0},{2,3},{3,2},{4,5},{5,4},{6,7},{7,6},{8,9},{9,8},{10,11... | collective-permute-start | bytes 3538952 | tf_op jit(solution)/shard_map/ppermute | solution.py:729

commit v16 on v15

--- a/solution.py
+++ b/solution.py
@@ -26,7 +26,10 @@
 ODD_COLS = swap_pairs([(r * 8 + c, r * 8 + c + 1) for r in range(8) for c in (1, 3, 5)])
 EVEN_ROWS = swap_pairs([(r * 8 + c, r * 8 + 8 + c) for r in (0, 2, 4, 6) for c in range(8)])
 ODD_ROWS = swap_pairs([(r * 8 + c, r * 8 + 8 + c) for r in (1, 3, 5) for c in range(8)])
-NEAR_ROWS = swap_pairs([(r * 8 + c, r * 8 + 8 + c) for r in (1, 5) for c in range(8)])
+RIM_EVEN = swap_pairs([(r * 8 + c, r * 8 + 8 + c) for r in (0, 2, 4, 6) for c in (0, 7)])
+RIM_NEAR = swap_pairs([(r * 8 + c, r * 8 + 8 + c) for r in (1, 5) for c in (0, 7)])
+RIM_FIRST = swap_pairs([(r * 8 + c, r * 8 + c + 1) for r in (0, 7) for c in (0, 2, 4, 6)]) + RIM_NEAR
+RIM_SECOND = swap_pairs([(r * 8 + c, r * 8 + c + 1) for r in (0, 7) for c in (1, 3, 5)]) + RIM_EVEN
 SPARE = (19, 20, 43, 44)
 
 
@@ -187,18 +190,21 @@
     post_strips(strips, send)
 
 
-def beyond_kernel(pos, got, pick, lines, core_ends, odd_ends, even_rows, near_rows, ends):
+def beyond_kernel(pos, got, pick, lines, first, second, ends):
     row, col = pos[0], pos[1]
     lines[...] = dot(pick[...], got[...], ((1,), (0,)))
     ends[...] = jnp.zeros_like(ends)
-    for kind, even, first, second in ((0, col % 2 == 0, core_ends, odd_ends), (1, row % 2 == 0, even_rows, near_rows)):
+    for kind in range(2):
         for f in range(3):
             at = (2 * f + kind) * 12
-            ends[2 * f : 2 * f + 2, :] = lines[at + 2 : at + 4, :]
-            ends[16 + 2 * f : 18 + 2 * f, :] = lines[at + 8 : at + 10, :]
-        begin, end = ends[0:16, :], ends[16:32, :]
-        first[...] = jnp.where(even, end, begin).astype(BF16)
-        second[...] = jnp.where(even, begin, end).astype(BF16)
+            ends[32 * kind + 2 * f : 32 * kind + 2 * f + 2, :] = lines[at + 2 : at + 4, :]
+            ends[32 * kind + 16 + 2 * f : 32 * kind + 18 + 2 * f, :] = lines[at + 8 : at + 10, :]
+    left, right, top, low = (ends[16 * i : 16 * i + 16, :] for i in range(4))
+    on_row, on_col = (row == 0) | (row == 7), (col == 0) | (col == 7)
+    along = jnp.where(col % 2 == 0, right, left), jnp.where(col % 2 == 0, left, right)
+    down = jnp.where(row % 2 == 0, top, low), jnp.where(row % 2 == 0, low, top)
+    first[...] = jnp.where(on_row, along[0], down[0]).astype(BF16)
+    second[...] = jnp.where(on_col, down[1], along[1]).astype(BF16)
 
 
 def widen(pos, own, swapped, odd, wide, first, second, cells):
@@ -281,15 +287,21 @@
 
 
 def one_kernel(
-    pos, wide, first, second, arrived, core_ends, odd_ends, even_rows, near_rows, fetched, *refs
+    pos, wide, first, second, arrived, rim_first, rim_second, fetched, filled, pre, hidden, send, *scratch
 ):
-    filled, pre, hidden, send, cells, shifts, strips, lines, ends = refs
+    cells, shifts, strips, lines, ends = scratch
     row, col = pos[0], pos[1]
     lines[...] = arrived[...]
-    for kind, even, one, two in ((0, col % 2 == 0, core_ends, odd_ends), (1, row % 2 == 0, even_rows, near_rows)):
-        one, two = one[...].astype(F32), two[...].astype(F32)
-        ends[0:16, :] = jnp.where(even, two, one)
-        ends[16:32, :] = jnp.where(even, one, two)
+    one, two = rim_first[...].astype(F32), rim_second[...].astype(F32)
+    none = jnp.zeros_like(one)
+    on_row, on_col = (row == 0) | (row == 7), (col == 0) | (col == 7)
+    for kind in range(2):
+        if kind == 0:
+            even, toward, away = col % 2 == 0, one, jnp.where(on_col, none, two)
+        else:
+            even, toward, away = row % 2 == 0, two, jnp.where(on_row, none, one)
+        ends[0:16, :] = jnp.where(even, away, toward)
+        ends[16:32, :] = jnp.where(even, toward, away)
         for f in range(3):
             at = (2 * f + kind) * 12
             lines[at : at + 2, :] = lines[at : at + 2, :] + ends[2 * f : 2 * f + 2, :]
@@ -611,8 +623,8 @@
             field,
             lax.ppermute(field, "core", CORES),
             lax.ppermute(field, TILE, ODD_COLS),
-            lax.ppermute(first, TILE, EVEN_ROWS),
-            lax.ppermute(second, TILE, NEAR_ROWS),
+            lax.ppermute(first, TILE, RIM_EVEN),
+            lax.ppermute(second, TILE, RIM_NEAR),
         )
 
     x = inputs.reshape(192, C)
@@ -624,13 +636,8 @@
     wide, first, second = run(widen, regions, [((24, PITCH, C), F32)], pos, x, swapped, odd)
     first, second = lax.ppermute(first, TILE, EVEN_ROWS), lax.ppermute(second, TILE, ODD_ROWS)
     got, wide, first, second = lax.optimization_barrier((got, wide, first, second))
-    arrived, *sides = run(beyond_kernel, [((80, C), F32)] + ends * 2, [((32, C), F32)], pos, got, pick_8)
-    sides = [
-        lax.ppermute(sides[0], "core", CORES),
-        lax.ppermute(sides[1], TILE, ODD_COLS),
-        lax.ppermute(sides[2], TILE, EVEN_ROWS),
-        lax.ppermute(sides[3], TILE, NEAR_ROWS),
-    ]
+    arrived, *sides = run(beyond_kernel, [((80, C), F32)] + ends, [((64, C), F32)], pos, got, pick_8)
+    sides = [lax.ppermute(v, TILE, pairs) for v, pairs in zip(sides, (RIM_FIRST, RIM_SECOND))]
     filled, pre_one, hidden, send = run(
         one_kernel,
         [((flat, C), BF16), ((30 * PITCH, C), F32), ((30 * PITCH, C), BF16), ((16, 64, C), BF16)],

time: 193 us -> 194 us (level)
    ppermute x1, starting transfers between devices: 0.09 us -> 2.6 us  [body(): wide_other = lax.ppermute(wide_one, 'core', CORES)]
    ppermute x6 -> x4, starting transfers between devices: 3.52 us -> 5.16 us  [the longest x2 3.84 us: body(): lax.ppermute(v, TILE, pairs)]
    ppermute x6 -> x4, waiting for transfers between devices: 4.08 us -> 3.04 us  [the longest x2 3.03 us: body(): lax.ppermute(v, TILE, pairs)]
  transfers between devices with their start and end apart: 29 -> 27, of which waited for: 15 -> 14; matrix products, arithmetic and copies ran while one was open for 1% -> 1% of each run, Pallas kernels for 8% -> 8%
where the time goes in v16:
time: 194 us; the launch traced here: 193 us
  starting transfers between devices  70.3 us (36%)
  waiting for transfers between devices  57.8 us (30%)
  Pallas kernels  31.6 us (16%)
  blocking collectives  25.4 us (13%)
  local copies, waits for them, and re-layouts  7.12 us (4%)
    all_to_all x1, blocking collectives, seam_exchange(): got = lax.all_to_all(send, AXES, 0, 0, axis_index_groups=SEAM_GROUPS)  25.4 us
    pallas_call x17, Pallas kernels, run(): pl.pallas_call(inner, out_shape=[jax.ShapeDtypeStruct(shape, dtype) for s...  24.8 us
    all_to_all x2, starting transfers between devices, seam_exchange(): got = lax.all_to_all(send, AXES, 0, 0, axis_index_groups=SEAM_GROUPS)  19.2 us
    all_to_all x2, waiting for transfers between devices, body(): part = lax.all_to_all(part, AXES, 0, 0, axis_index_groups=PLANE_GROUPS)  12.4 us
    all_to_all x2, waiting for transfers between devices, seam_exchange(): got = lax.all_to_all(send, AXES, 0, 0, axis_index_groups=SEAM_GROUPS)  11.2 us
    all_to_all x2, starting transfers between devices, body(): part = lax.all_to_all(part, AXES, 0, 0, axis_index_groups=PLANE_GROUPS)  10.7 us
    ppermute x1, waiting for transfers between devices, body(): onward = lax.ppermute(onward, TILE, [(t, t ^ 7) for t in range(64)])  9.11 us
    ppermute x1, starting transfers between devices, body(): onward = lax.ppermute(onward, TILE, [(t, t ^ 7) for t in range(64)])  7.82 us
  transfers between devices with their start and end apart: 27, of which 14 were waited for; matrix products, arithmetic and copies ran while one was open for 1% of the time, Pallas kernels for 8%

profile of v16, /device:TPU:1, one launch (start us, length us, event | category | flops | bytes accessed | tf_op | source)
XLA Modules:
  0.0 193.5 jit_solution(1569127937234689047)
XLA Ops:
  0.7 1.0 copy-done.4
  1.7 1.3 shard_map.85
  3.0 14.3 %all-to-all-start = ((bf16[16,48,256]{2,1,0:T(8,128)(2,1)}), bf16[16,48,256]{2,1,0:T(8,128)(2,1)S(1)}, u32[]{:S(2)}, u32[]{:S(2)}) async-start(bf16[16,48,256]{2,1,0:T(8,128)(2,1)} %shard_map.85), calls=%async_computation | async-start | bytes 786432 | tf_op jit(solution)/shard_map/all_to_all | solution.py:511
  17.4 1.9 collective-permute-start.1
  19.4 4.2 %collective-permute-done.1.odd = bf16[192,256]{1,0:T(8,128)(2,1)S(1)} collective-permute-done((bf16[192,256]{1,0:T(8,128)(2,1)S(1)}, bf16[192,256]{1,0:T(8,128)(2,1)S(1)}, u32[]{:S(2)}, u32[]{:S(2)}) %collective-permute-start.1) | collective-permute-done | bytes 98336 | tf_op jit(solution)/shard_map/ppermute | solution.py:635
  26.5 2.6 %shard_map.87 = (bf16[80,768]{1,0:T(8,128)(2,1)}, bf16[64,1024]{1,0:T(8,128)(2,1)}, bf16[64,1024]{1,0:T(8,128)(2,1)}, bf16[192,256]{1,0:T(8,128)(2,1)}) custom-call(s32[4]{0:T(128)} %copy-done.6, s32[12,4]{1,0:T(8,128)} %copy.11.nexts, s32[12,4]{1,0:T(8,128)} %copy.12.codes), custom_call_target="tpu_custom_call" | custom-call | tf_op jit(solution)/shard_map/pallas_call | solution.py:602
  29.1 4.9 %all-to-all-done = bf16[16,48,256]{2,1,0:T(8,128)(2,1)S(1)} async-done(((bf16[16,48,256]{2,1,0:T(8,128)(2,1)}), bf16[16,48,256]{2,1,0:T(8,128)(2,1)S(1)}, u32[]{:S(2)}, u32[]{:S(2)}) %all-to-all-start) | async-done | bytes 393248 | tf_op jit(solution)/shard_map/all_to_all | solution.py:511
  34.7 0.9 copy-done.14
  36.3 1.9 collective-permute-start.4
  38.2 1.9 collective-permute-start.5
  40.2 3.0 %collective-permute-done.5.refs_6_ = bf16[16,256]{1,0:T(8,128)(2,1)S(1)} collective-permute-done((bf16[16,256]{1,0:T(8,128)(2,1)S(1)}, bf16[16,256]{1,0:T(8,128)(2,1)S(1)}, u32[]{:S(2)}, u32[]{:S(2)}) %collective-permute-start.5) | collective-permute-done | bytes 8224 | tf_op jit(solution)/shard_map/ppermute | solution.py:640
  43.9 2.3 %shard_map.89 = (bf16[576,256]{1,0:T(8,128)(2,1)}, f32[480,256]{1,0:T(8,128)S(1)}, bf16[480,256]{1,0:T(8,128)(2,1)S(1)}, bf16[16,64,256]{2,1,0:T(8,128)(2,1)S(1)}) custom-call(s32[4]{0:T(128)S(1)} %copy-done.8, bf16[384,256]{1,0:T(8,128)(2,1)S(1)} %get-tuple-element.61.refs_1_, bf16[96,256]{1,0:T(8,128)(2,1)S(1)} %collective-permute-done.2.refs_2_, ...), custom_call_target="tpu_custom_call" | custom-call | tf_op jit(solution)/shard_map/pallas_call | solution.py:81
  46.2 25.4 %all_to_all.25 = bf16[16,64,256]{2,1,0:T(8,128)(2,1)S(1)} all-to-all(bf16[16,64,256]{2,1,0:T(8,128)(2,1)S(1)} %get-tuple-element.73), channel_id=1, replica_groups={{0,7,56,63,64,71,120,127,128,135,184,191,192,199,248,255},{1,6,57,62,65..., dimensions={0} | all-to-all | bytes 1048576 | tf_op jit(solution)/shard_map/all_to_all | solution.py:511
  71.7 2.6 %shard_map.90 = (bf16[864,256]{1,0:T(8,128)(2,1)}, bf16[192,256]{1,0:T(8,128)(2,1)S(1)}, bf16[16,256]{1,0:T(8,128)(2,1)S(1)}, bf16[16,256]{1,0:T(8,128)(2,1)S(1)}) custom-call(s32[4]{0:T(128)S(1)} %copy-done.9, bf16[480,256]{1,0:T(8,128)(2,1)S(1)} %get-tuple-element.72.refs_1_, bf16[1024,256]{1,0:T(8,128)(2,1)S(1)} %bitcast.14, ...), custom_call_target="tpu_custom_call" | custom-call | tf_op jit(solution)/shard_map/pallas_call | solution.py:81
  74.3 1.9 collective-permute-start.8
  77.7 2.5 %collective-permute-done.8.refs_3_ = bf16[192,256]{1,0:T(8,128)(2,1)S(1)} collective-permute-done((bf16[192,256]{1,0:T(8,128)(2,1)S(1)}, bf16[192,256]{1,0:T(8,128)(2,1)S(1)}, u32[]{:S(2)}, u32[]{:S(2)}) %collective-permute-start.8) | collective-permute-done | bytes 98336 | tf_op jit(solution)/shard_map/ppermute | solution.py:625
  80.2 2.2 %shard_map.91 = (bf16[384,256]{1,0:T(8,128)(2,1)S(1)}, bf16[96,256]{1,0:T(8,128)(2,1)S(1)}, bf16[96,256]{1,0:T(8,128)(2,1)S(1)}, bf16[16,64,256]{2,1,0:T(8,128)(2,1)}) custom-call(s32[4]{0:T(128)S(1)} %copy-done.9, bf16[192,256]{1,0:T(8,128)(2,1)S(1)} %get-tuple-element.75.refs_1_, bf16[192,256]{1,0:T(8,128)(2,1)S(1)} %collective-permute-done.7.refs_2_, ...), custom_call_target="tpu_custom_call" | custom-call | tf_op jit(solution)/shard_map/pallas_call | solution.py:81
  83.1 4.9 %all-to-all-start.2 = ((bf16[16,64,256]{2,1,0:T(8,128)(2,1)}), bf16[16,64,256]{2,1,0:T(8,128)(2,1)S(1)}, u32[]{:S(2)}, u32[]{:S(2)}) async-start(bf16[16,64,256]{2,1,0:T(8,128)(2,1)} %get-tuple-element.81), calls=%async_computation.2 | async-start | bytes 1048576 | tf_op jit(solution)/shard_map/all_to_all | solution.py:511
  88.0 1.9 collective-permute-start.13
  90.0 3.7 %collective-permute-start.11 = (bf16[96,256]{1,0:T(8,128)(2,1)S(1)}, bf16[96,256]{1,0:T(8,128)(2,1)S(1)}, u32[]{:S(2)}, u32[]{:S(2)}) collective-permute-start(bf16[96,256]{1,0:T(8,128)(2,1)S(1)} %get-tuple-element.79), channel_id=1, source_target_pairs={{0,8},{1,9},{2,10},{3,11},{4,12},{5,13},{6,14},{7,15},{16,24},{17,... | collective-permute-start | bytes 147464 | tf_op jit(solution)/shard_map/ppermute | solution.py:674
  94.3 1.1 collective-permute-done.11.refs_2_
  95.5 0.9 copy-done.11
  96.4 1.6 shard_map.92.refs_1_
  98.0 1.9 %shard_map.93.two = bf16[16,72,256]{2,1,0:T(8,128)(2,1)S(1)} custom-call(s32[4]{0:T(128)S(1)} %copy-done.9, bf16[864,256]{1,0:T(8,128)(2,1)} %get-tuple-element.82.own, bf16[864,256]{1,0:T(8,128)(2,1)S(1)} %collective-permute-done.13.other), custom_call_target="tpu_custom_call" | custom-call | tf_op jit(solution)/shard_map/pallas_call | solution.py:81
  100.0 6.4 %all-to-all-done.2 = bf16[16,64,256]{2,1,0:T(8,128)(2,1)S(1)} async-done(((bf16[16,64,256]{2,1,0:T(8,128)(2,1)}), bf16[16,64,256]{2,1,0:T(8,128)(2,1)S(1)}, u32[]{:S(2)}, u32[]{:S(2)}) %all-to-all-start.2) | async-done | bytes 524320 | tf_op jit(solution)/shard_map/all_to_all | solution.py:511
  106.3 0.9 copy-done.12
  107.2 2.3 %shard_map.94 = (bf16[384,256]{1,0:T(8,128)(2,1)S(1)}, bf16[192,256]{1,0:T(8,128)(2,1)S(1)}, bf16[48,256]{1,0:T(8,128)(2,1)S(1)}) custom-call(s32[4]{0:T(128)S(1)} %copy-done.9, bf16[480,256]{1,0:T(8,128)(2,1)S(1)} %shard_map.92.refs_1_, bf16[1024,256]{1,0:T(8,128)(2,1)S(1)} %bitcast.15, bf16[64,1024]{1,0:T(8,128)(2,1)S(1)} %copy-done.12, ...), custom_call_target="tpu_custom_call" | custom-call | tf_op jit(solution)/shard_map/pallas_call | solution.py:81
  109.6 2.6 %collective-permute-start.14 = (bf16[384,256]{1,0:T(8,128)(2,1)S(1)}, bf16[384,256]{1,0:T(8,128)(2,1)S(1)}, u32[]{:S(2)}, u32[]{:S(2)}) collective-permute-start(bf16[384,256]{1,0:T(8,128)(2,1)S(1)} %get-tuple-element.86.delta), channel_id=1, source_target_pairs={{0,1},{1,0},{2,3},{3,2},{4,5},{5,4},{6,7},{7,6},{8,9},{9,8},{10,11... | collective-permute-start | bytes 589832 | tf_op jit(solution)/shard_map/ppermute | solution.py:704
  112.2 1.5 shard_map.95.part
  113.7 2.1 %shard_map.96 = bf16[16,144,256]{2,1,0:T(8,128)(2,1)} custom-call(s32[4]{0:T(128)S(1)} %copy-done.9, bf16[576,256]{1,0:T(8,128)(2,1)S(1)} %collective-permute-done.6.source, bf16[384,256]{1,0:T(8,128)(2,1)S(1)} %collective-permute-done.14.delta, f32[16,72,256]{2,1,0:T(8,128)S(1)} %shard_map.95.part, bf16[16,72,256]{2,1,0:T(8,128)(2,1)S(1)} %shard_map.93.two), custom_call_target="tpu_custom_call" | custom-call | tf_op jit(solution)/shard_map/pallas_call | solution.py:81
  115.8 7.0 %all-to-all-start.3 = ((bf16[16,144,256]{2,1,0:T(8,128)(2,1)}), bf16[16,144,256]{2,1,0:T(8,128)(2,1)S(1)}, u32[]{:S(2)}, u32[]{:S(2)}) async-start(bf16[16,144,256]{2,1,0:T(8,128)(2,1)} %shard_map.96), calls=%async_computation.3 | async-start | bytes 2359296 | tf_op jit(solution)/shard_map/all_to_all | solution.py:718
  122.8 2.3 %collective-permute-start.17 = (bf16[48,256]{1,0:T(8,128)(2,1)S(1)}, bf16[48,256]{1,0:T(8,128)(2,1)S(1)}, u32[]{:S(2)}, u32[]{:S(2)}) collective-permute-start(bf16[48,256]{1,0:T(8,128)(2,1)S(1)} %get-tuple-element.90.one), channel_id=1, source_target_pairs={{0,192},{64,0},{128,64},{192,128},{1,193},{65,1},{129,65},{193,129... | collective-permute-start | bytes 73736 | tf_op jit(solution)/shard_map/ppermute | solution.py:717
  125.2 1.2 collective-permute-start.15
  126.3 2.6 %collective-permute-done.16.three = bf16[48,256]{1,0:T(8,128)(2,1)S(1)} collective-permute-done((bf16[48,256]{1,0:T(8,128)(2,1)S(1)}, bf16[48,256]{1,0:T(8,128)(2,1)S(1)}, u32[]{:S(2)}, u32[]{:S(2)}) %collective-permute-start.16) | collective-permute-done | bytes 24608 | tf_op jit(solution)/shard_map/ppermute | solution.py:717
  130.4 12.4 %all-to-all-done.3.parts = bf16[16,144,256]{2,1,0:T(8,128)(2,1)S(1)} async-done(((bf16[16,144,256]{2,1,0:T(8,128)(2,1)}), bf16[16,144,256]{2,1,0:T(8,128)(2,1)S(1)}, u32[]{:S(2)}, u32[]{:S(2)}) %all-to-all-start.3) | async-done | bytes 1179680 | tf_op jit(solution)/shard_map/all_to_all | solution.py:718
  143.9 2.8 %collective-permute-done.18.two = bf16[144,256]{1,0:T(8,128)(2,1)S(1)} collective-permute-done((bf16[144,256]{1,0:T(8,128)(2,1)S(1)}, bf16[144,256]{1,0:T(8,128)(2,1)S(1)}, u32[]{:S(2)}, u32[]{:S(2)}) %collective-permute-start.18) | collective-permute-done | bytes 73760 | tf_op jit(solution)/shard_map/ppermute | solution.py:723
  147.3 2.0 %collective-permute-start.19 = (bf16[144,256]{1,0:T(8,128)(2,1)S(1)}, bf16[144,256]{1,0:T(8,128)(2,1)S(1)}, u32[]{:S(2)}, u32[]{:S(2)}) collective-permute-start(bf16[144,256]{1,0:T(8,128)(2,1)S(1)} %shard_map.99.one), channel_id=1, source_target_pairs={{0,128},{64,192},{128,0},{192,64},{1,129},{65,193},{129,1},{193,65... | collective-permute-start | bytes 221192 | tf_op jit(solution)/shard_map/ppermute | solution.py:725
  149.3 3.0 %collective-permute-done.19.two = bf16[144,256]{1,0:T(8,128)(2,1)S(1)} collective-permute-done((bf16[144,256]{1,0:T(8,128)(2,1)S(1)}, bf16[144,256]{1,0:T(8,128)(2,1)S(1)}, u32[]{:S(2)}, u32[]{:S(2)}) %collective-permute-start.19) | collective-permute-done | bytes 73760 | tf_op jit(solution)/shard_map/ppermute | solution.py:725
  152.8 5.3 %collective-permute-start.20 = (bf16[240,256]{1,0:T(8,128)(2,1)S(1)}, bf16[240,256]{1,0:T(8,128)(2,1)S(1)}, u32[]{:S(2)}, u32[]{:S(2)}) collective-permute-start(bf16[240,256]{1,0:T(8,128)(2,1)S(1)} %shard_map.100.one), channel_id=1, source_target_pairs={{0,56},{1,57},{2,58},{3,59},{4,60},{5,61},{6,62},{7,63},{8,48},{9,... | collective-permute-start | bytes 368648 | tf_op jit(solution)/shard_map/ppermute | solution.py:727
  158.1 4.7 %collective-permute-done.20.two = bf16[240,256]{1,0:T(8,128)(2,1)S(1)} collective-permute-done((bf16[240,256]{1,0:T(8,128)(2,1)S(1)}, bf16[240,256]{1,0:T(8,128)(2,1)S(1)}, u32[]{:S(2)}, u32[]{:S(2)}) %collective-permute-start.20) | collective-permute-done | bytes 122912 | tf_op jit(solution)/shard_map/ppermute | solution.py:727
  162.9 1.6 shard_map.101
  164.5 3.7 %all-to-all-start.4 = ((bf16[16,144,256]{2,1,0:T(8,128)(2,1)}), bf16[16,144,256]{2,1,0:T(8,128)(2,1)S(1)}, u32[]{:S(2)}, u32[]{:S(2)}) async-start(bf16[16,144,256]{2,1,0:T(8,128)(2,1)} %get-tuple-element.99), calls=%async_computation.4 | async-start | bytes 2359296 | tf_op jit(solution)/shard_map/all_to_all | solution.py:733
  168.2 7.8 %collective-permute-start.21 = (bf16[48,256]{1,0:T(8,128)(2,1)S(1)}, bf16[48,256]{1,0:T(8,128)(2,1)S(1)}, u32[]{:S(2)}, u32[]{:S(2)}) collective-permute-start(bf16[48,256]{1,0:T(8,128)(2,1)S(1)} %get-tuple-element.102), channel_id=1, source_target_pairs={{0,7},{1,6},{2,5},{3,4},{4,3},{5,2},{6,1},{7,0},{8,15},{9,14},{10,... | collective-permute-start | bytes 73736 | tf_op jit(solution)/shard_map/ppermute | solution.py:730
  176.0 9.1 %collective-permute-done.21.by_col = bf16[48,256]{1,0:T(8,128)(2,1)S(1)} collective-permute-done((bf16[48,256]{1,0:T(8,128)(2,1)S(1)}, bf16[48,256]{1,0:T(8,128)(2,1)S(1)}, u32[]{:S(2)}, u32[]{:S(2)}) %collective-permute-start.21) | collective-permute-done | bytes 24608 | tf_op jit(solution)/shard_map/ppermute | solution.py:730
  185.1 1.3 shard_map.102
  186.4 2.3 %collective-permute-start.22 = (bf16[16,144,256]{2,1,0:T(8,128)(2,1)S(1)}, bf16[16,144,256]{2,1,0:T(8,128)(2,1)S(1)}, u32[]{:S(2)}, u32[]{:S(2)}) collective-permute-start(bf16[16,144,256]{2,1,0:T(8,128)(2,1)S(1)} %all-to-all-done.4.refs_1_), channel_id=1, source_target_pairs={{0,1},{1,0},{2,3},{3,2},{4,5},{5,4},{6,7},{7,6},{8,9},{9,8},{10,11... | collective-permute-start | bytes 3538952 | tf_op jit(solution)/shard_map/ppermute | solution.py:736
  188.7 2.1 %shard_map.103 = (f32[9,256,256]{2,1,0:T(8,128)}, f32[9,256,256]{2,1,0:T(8,128)}) custom-call(s32[4]{0:T(128)S(1)} %copy-done.9, bf16[16,144,256]{2,1,0:T(8,128)(2,1)S(1)} %all-to-all-done.4.refs_1_), custom_call_target="tpu_custom_call" | custom-call | tf_op jit(solution)/shard_map/pallas_call | solution.py:499
  191.2 2.1 %shard_map.104 = (f32[9,256,256]{2,1,0:T(8,128)}, f32[9,256,256]{2,1,0:T(8,128)}) custom-call(s32[4]{0:T(128)S(1)} %copy-done.9, bf16[16,144,256]{2,1,0:T(8,128)(2,1)S(1)} %collective-permute-done.22.refs_1_, f32[9,256,256]{2,1,0:T(8,128)} %get-tuple-element.105.refs_2_, ...), custom_call_target="tpu_custom_call", output_to_operand_aliasing={{0}: (2, {}), {1}: (3, {})} | custom-call | tf_op jit(solution)/shard_map/pallas_call | solution.py:499
  (68 shorter events, 12.0 us)
Async XLA Ops:
  0.6 42.6 %copy-start.1 = (bf16[3,3,256,256]{3,2,1,0:T(8,128)(2,1)S(1)}, bf16[3,3,256,256]{3,2,1,0:T(8,128)(2,1)}, u32[]{:S(2)}) copy-start(bf16[3,3,256,256]{3,2,1,0:T(8,128)(2,1)} %refs_5_.3) | copy-start | bytes 3538948
  0.7 25.7 %copy-start.6 = (s32[4]{0:T(128)}, s32[4]{0:T(128)S(1)}, u32[]{:S(2)}) copy-start(s32[4]{0:T(128)S(1)} %pad_add_fusion.pos.refs_0_) | copy-start | bytes 52
  0.7 1.0 copy-start.4
  1.7 15.7 %copy-start.5 = (bf16[3,1,8,8,256]{4,3,2,1,0:T(8,128)(2,1)S(1)}, bf16[3,1,8,8,256]{4,3,2,1,0:T(8,128)(2,1)}, u32[]{:S(2)}) copy-start(bf16[3,1,8,8,256]{4,3,2,1,0:T(8,128)(2,1)} %param.6) | copy-start | bytes 294916
  1.7 23.4 %copy-start.17 = (s32[12,4]{0,1:T(4,128)S(1)}, s32[12,4]{0,1:T(4,128)}, u32[]{:S(2)}) copy-start(s32[12,4]{0,1:T(4,128)} %param.10) | copy-start | bytes 580
  1.7 24.1 %copy-start.18 = (s32[12,4]{0,1:T(4,128)S(1)}, s32[12,4]{0,1:T(4,128)}, u32[]{:S(2)}) copy-start(s32[12,4]{0,1:T(4,128)} %param.11) | copy-start | bytes 580
  3.0 30.9 %all-to-all-start = ((bf16[16,48,256]{2,1,0:T(8,128)(2,1)}), bf16[16,48,256]{2,1,0:T(8,128)(2,1)S(1)}, u32[]{:S(2)}, u32[]{:S(2)}) async-start(bf16[16,48,256]{2,1,0:T(8,128)(2,1)} %shard_map.85), calls=%async_computation | async-start | bytes 786432 | tf_op jit(solution)/shard_map/all_to_all | solution.py:511
  17.4 6.2 %collective-permute-start.1 = (bf16[192,256]{1,0:T(8,128)(2,1)S(1)}, bf16[192,256]{1,0:T(8,128)(2,1)S(1)}, u32[]{:S(2)}, u32[]{:S(2)}) collective-permute-start(bf16[192,256]{1,0:T(8,128)(2,1)S(1)} %bitcast.18), channel_id=1, source_target_pairs={{1,2},{3,4},{5,6},{9,10},{11,12},{13,14},{17,18},{19,20},{21,22},{... | collective-permute-start | bytes 294920 | tf_op jit(solution)/shard_map/ppermute | solution.py:635
  19.3 4.3 %collective-permute-start = (bf16[192,256]{1,0:T(8,128)(2,1)S(1)}, bf16[192,256]{1,0:T(8,128)(2,1)S(1)}, u32[]{:S(2)}, u32[]{:S(2)}) collective-permute-start(bf16[192,256]{1,0:T(8,128)(2,1)S(1)} %bitcast.19), channel_id=1, source_target_pairs={{0,1},{1,0},{2,3},{3,2},{4,5},{5,4},{6,7},{7,6},{8,9},{9,8},{10,11... | collective-permute-start | bytes 294920 | tf_op jit(solution)/shard_map/ppermute | solution.py:635
  24.3 4.8 %collective-permute-start.2 = (bf16[96,256]{1,0:T(8,128)(2,1)S(1)}, bf16[96,256]{1,0:T(8,128)(2,1)S(1)}, u32[]{:S(2)}, u32[]{:S(2)}) collective-permute-start(bf16[96,256]{1,0:T(8,128)(2,1)S(1)} %get-tuple-element.59), channel_id=1, source_target_pairs={{0,8},{1,9},{2,10},{3,11},{4,12},{5,13},{6,14},{7,15},{16,24},{17,... | collective-permute-start | bytes 147464 | tf_op jit(solution)/shard_map/ppermute | solution.py:637
  24.4 4.7 %collective-permute-start.3 = (bf16[96,256]{1,0:T(8,128)(2,1)S(1)}, bf16[96,256]{1,0:T(8,128)(2,1)S(1)}, u32[]{:S(2)}, u32[]{:S(2)}) collective-permute-start(bf16[96,256]{1,0:T(8,128)(2,1)S(1)} %get-tuple-element.60), channel_id=1, source_target_pairs={{8,16},{9,17},{10,18},{11,19},{12,20},{13,21},{14,22},{15,23},{24,... | collective-permute-start | bytes 147464 | tf_op jit(solution)/shard_map/ppermute | solution.py:637
  34.0 0.7 copy-start.7
  34.6 0.9 copy-start.14
  36.3 3.9 %collective-permute-start.4 = (bf16[16,256]{1,0:T(8,128)(2,1)S(1)}, bf16[16,256]{1,0:T(8,128)(2,1)S(1)}, u32[]{:S(2)}, u32[]{:S(2)}) collective-permute-start(bf16[16,256]{1,0:T(8,128)(2,1)S(1)} %get-tuple-element.69), channel_id=1, source_target_pairs={{0,1},{2,3},{4,5},{6,7},{56,57},{58,59},{60,61},{62,63},{1,0},{3,2... | collective-permute-start | bytes 24584 | tf_op jit(solution)/shard_map/ppermute | solution.py:640
  38.2 5.0 %collective-permute-start.5 = (bf16[16,256]{1,0:T(8,128)(2,1)S(1)}, bf16[16,256]{1,0:T(8,128)(2,1)S(1)}, u32[]{:S(2)}, u32[]{:S(2)}) collective-permute-start(bf16[16,256]{1,0:T(8,128)(2,1)S(1)} %get-tuple-element.70), channel_id=1, source_target_pairs={{1,2},{3,4},{5,6},{57,58},{59,60},{61,62},{2,1},{4,3},{6,5},{58,57... | collective-permute-start | bytes 24584 | tf_op jit(solution)/shard_map/ppermute | solution.py:640
  43.2 0.7 copy-start.8
  43.9 27.8 %copy-start = (bf16[3,3,256,256]{3,2,1,0:T(8,128)(2,1)S(1)}, bf16[3,3,256,256]{3,2,1,0:T(8,128)(2,1)}, u32[]{:S(2)}) copy-start(bf16[3,3,256,256]{3,2,1,0:T(8,128)(2,1)} %refs_4_.1) | copy-start | bytes 3538948
  43.9 27.8 %copy-start.9 = (s32[4]{0:T(128)S(1)}, s32[4]{0:T(128)}, u32[]{:S(2)}) copy-start(s32[4]{0:T(128)} %copy-done.6) | copy-start | bytes 52
  43.9 27.8 %copy-start.13 = (bf16[64,1024]{1,0:T(8,128)(2,1)S(1)}, bf16[64,1024]{1,0:T(8,128)(2,1)}, u32[]{:S(2)}) copy-start(bf16[64,1024]{1,0:T(8,128)(2,1)} %get-tuple-element.74.refs_3_) | copy-start | bytes 393220
  43.9 27.8 %copy-start.15 = (bf16[3,1,8,8,256]{4,3,2,1,0:T(8,128)(2,1)S(1)}, bf16[3,1,8,8,256]{4,3,2,1,0:T(8,128)(2,1)}, u32[]{:S(2)}) copy-start(bf16[3,1,8,8,256]{4,3,2,1,0:T(8,128)(2,1)} %param.7) | copy-start | bytes 294916
  46.2 25.4 %copy-start.2 = (f32[480,256]{1,0:T(8,128)}, f32[480,256]{1,0:T(8,128)S(1)}, u32[]{:S(2)}) copy-start(f32[480,256]{1,0:T(8,128)S(1)} %get-tuple-element.85.refs_4_) | copy-start | bytes 1474564
  74.3 5.9 %collective-permute-start.8 = (bf16[192,256]{1,0:T(8,128)(2,1)S(1)}, bf16[192,256]{1,0:T(8,128)(2,1)S(1)}, u32[]{:S(2)}, u32[]{:S(2)}) collective-permute-start(bf16[192,256]{1,0:T(8,128)(2,1)S(1)} %get-tuple-element.75.refs_1_), channel_id=1, source_target_pairs={{1,2},{3,4},{5,6},{9,10},{11,12},{13,14},{17,18},{19,20},{21,22},{... | collective-permute-start | bytes 294920 | tf_op jit(solution)/shard_map/ppermute | solution.py:625
  76.2 4.0 %collective-permute-start.7 = (bf16[192,256]{1,0:T(8,128)(2,1)S(1)}, bf16[192,256]{1,0:T(8,128)(2,1)S(1)}, u32[]{:S(2)}, u32[]{:S(2)}) collective-permute-start(bf16[192,256]{1,0:T(8,128)(2,1)S(1)} %get-tuple-element.75.refs_1_), channel_id=1, source_target_pairs={{0,1},{1,0},{2,3},{3,2},{4,5},{5,4},{6,7},{7,6},{8,9},{9,8},{10,11... | collective-permute-start | bytes 294920 | tf_op jit(solution)/shard_map/ppermute | solution.py:624
  76.3 1.3 collective-permute-start.9
  77.0 0.7 collective-permute-start.10
  82.4 0.7 copy-start.10
  83.1 23.2 %all-to-all-start.2 = ((bf16[16,64,256]{2,1,0:T(8,128)(2,1)}), bf16[16,64,256]{2,1,0:T(8,128)(2,1)S(1)}, u32[]{:S(2)}, u32[]{:S(2)}) async-start(bf16[16,64,256]{2,1,0:T(8,128)(2,1)} %get-tuple-element.81), calls=%async_computation.2 | async-start | bytes 1048576 | tf_op jit(solution)/shard_map/all_to_all | solution.py:511
  88.0 10.0 %collective-permute-start.13 = (bf16[864,256]{1,0:T(8,128)(2,1)}, bf16[864,256]{1,0:T(8,128)(2,1)S(1)}, u32[]{:S(2)}, u32[]{:S(2)}) collective-permute-start(bf16[864,256]{1,0:T(8,128)(2,1)} %get-tuple-element.82.own), channel_id=1, source_target_pairs={{0,1},{1,0},{2,3},{3,2},{4,5},{5,4},{6,7},{7,6},{8,9},{9,8},{10,11... | collective-permute-start | bytes 1327112 | tf_op jit(solution)/shard_map/ppermute | solution.py:690
  89.9 23.8 %collective-permute-start.6 = (bf16[576,256]{1,0:T(8,128)(2,1)}, bf16[576,256]{1,0:T(8,128)(2,1)S(1)}, u32[]{:S(2)}, u32[]{:S(2)}) collective-permute-start(bf16[576,256]{1,0:T(8,128)(2,1)} %get-tuple-element.71.source), channel_id=1, source_target_pairs={{0,1},{1,0},{2,3},{3,2},{4,5},{5,4},{6,7},{7,6},{8,9},{9,8},{10,11... | collective-permute-start | bytes 884744 | tf_op jit(solution)/shard_map/ppermute | solution.py:653
  90.0 5.4 %collective-permute-start.11 = (bf16[96,256]{1,0:T(8,128)(2,1)S(1)}, bf16[96,256]{1,0:T(8,128)(2,1)S(1)}, u32[]{:S(2)}, u32[]{:S(2)}) collective-permute-start(bf16[96,256]{1,0:T(8,128)(2,1)S(1)} %get-tuple-element.79), channel_id=1, source_target_pairs={{0,8},{1,9},{2,10},{3,11},{4,12},{5,13},{6,14},{7,15},{16,24},{17,... | collective-permute-start | bytes 147464 | tf_op jit(solution)/shard_map/ppermute | solution.py:674
  93.7 1.8 collective-permute-start.12
  95.5 0.9 copy-start.11
  98.0 8.3 %copy-start.3 = (f32[480,256]{1,0:T(8,128)S(1)}, f32[480,256]{1,0:T(8,128)}, u32[]{:S(2)}) copy-start(f32[480,256]{1,0:T(8,128)} %copy-done.2) | copy-start | bytes 1474564
  106.3 0.9 copy-start.12
  109.6 4.1 %collective-permute-start.14 = (bf16[384,256]{1,0:T(8,128)(2,1)S(1)}, bf16[384,256]{1,0:T(8,128)(2,1)S(1)}, u32[]{:S(2)}, u32[]{:S(2)}) collective-permute-start(bf16[384,256]{1,0:T(8,128)(2,1)S(1)} %get-tuple-element.86.delta), channel_id=1, source_target_pairs={{0,1},{1,0},{2,3},{3,2},{4,5},{5,4},{6,7},{7,6},{8,9},{9,8},{10,11... | collective-permute-start | bytes 589832 | tf_op jit(solution)/shard_map/ppermute | solution.py:704
  115.8 13.8 %copy-start.16 = (bf16[192,256]{1,0:T(8,128)(2,1)S(1)}, bf16[192,256]{1,0:T(8,128)(2,1)}, u32[]{:S(2)}) copy-start(bf16[192,256]{1,0:T(8,128)(2,1)} %get-tuple-element.91.pick) | copy-start | bytes 294916
  115.8 26.9 %all-to-all-start.3 = ((bf16[16,144,256]{2,1,0:T(8,128)(2,1)}), bf16[16,144,256]{2,1,0:T(8,128)(2,1)S(1)}, u32[]{:S(2)}, u32[]{:S(2)}) async-start(bf16[16,144,256]{2,1,0:T(8,128)(2,1)} %shard_map.96), calls=%async_computation.3 | async-start | bytes 2359296 | tf_op jit(solution)/shard_map/all_to_all | solution.py:718
  122.8 3.5 %collective-permute-start.17 = (bf16[48,256]{1,0:T(8,128)(2,1)S(1)}, bf16[48,256]{1,0:T(8,128)(2,1)S(1)}, u32[]{:S(2)}, u32[]{:S(2)}) collective-permute-start(bf16[48,256]{1,0:T(8,128)(2,1)S(1)} %get-tuple-element.90.one), channel_id=1, source_target_pairs={{0,192},{64,0},{128,64},{192,128},{1,193},{65,1},{129,65},{193,129... | collective-permute-start | bytes 73736 | tf_op jit(solution)/shard_map/ppermute | solution.py:717
  125.2 3.8 %collective-permute-start.16 = (bf16[48,256]{1,0:T(8,128)(2,1)S(1)}, bf16[48,256]{1,0:T(8,128)(2,1)S(1)}, u32[]{:S(2)}, u32[]{:S(2)}) collective-permute-start(bf16[48,256]{1,0:T(8,128)(2,1)S(1)} %get-tuple-element.90.one), channel_id=1, source_target_pairs={{0,128},{64,192},{128,0},{192,64},{1,129},{65,193},{129,1},{193,65... | collective-permute-start | bytes 73736 | tf_op jit(solution)/shard_map/ppermute | solution.py:717
  125.2 4.5 %collective-permute-start.15 = (bf16[48,256]{1,0:T(8,128)(2,1)S(1)}, bf16[48,256]{1,0:T(8,128)(2,1)S(1)}, u32[]{:S(2)}, u32[]{:S(2)}) collective-permute-start(bf16[48,256]{1,0:T(8,128)(2,1)S(1)} %get-tuple-element.90.one), channel_id=1, source_target_pairs={{0,64},{64,128},{128,192},{192,0},{1,65},{65,129},{129,193},{193,1... | collective-permute-start | bytes 73736 | tf_op jit(solution)/shard_map/ppermute | solution.py:717
  143.4 3.3 %collective-permute-start.18 = (bf16[144,256]{1,0:T(8,128)(2,1)S(1)}, bf16[144,256]{1,0:T(8,128)(2,1)S(1)}, u32[]{:S(2)}, u32[]{:S(2)}) collective-permute-start(bf16[144,256]{1,0:T(8,128)(2,1)S(1)} %shard_map.98.one), channel_id=1, source_target_pairs={{0,64},{64,0},{128,192},{192,128},{1,65},{65,1},{129,193},{193,129... | collective-permute-start | bytes 221192 | tf_op jit(solution)/shard_map/ppermute | solution.py:723
  147.3 5.0 %collective-permute-start.19 = (bf16[144,256]{1,0:T(8,128)(2,1)S(1)}, bf16[144,256]{1,0:T(8,128)(2,1)S(1)}, u32[]{:S(2)}, u32[]{:S(2)}) collective-permute-start(bf16[144,256]{1,0:T(8,128)(2,1)S(1)} %shard_map.99.one), channel_id=1, source_target_pairs={{0,128},{64,192},{128,0},{192,64},{1,129},{65,193},{129,1},{193,65... | collective-permute-start | bytes 221192 | tf_op jit(solution)/shard_map/ppermute | solution.py:725
  152.8 10.0 %collective-permute-start.20 = (bf16[240,256]{1,0:T(8,128)(2,1)S(1)}, bf16[240,256]{1,0:T(8,128)(2,1)S(1)}, u32[]{:S(2)}, u32[]{:S(2)}) collective-permute-start(bf16[240,256]{1,0:T(8,128)(2,1)S(1)} %shard_map.100.one), channel_id=1, source_target_pairs={{0,56},{1,57},{2,58},{3,59},{4,60},{5,61},{6,62},{7,63},{8,48},{9,... | collective-permute-start | bytes 368648 | tf_op jit(solution)/shard_map/ppermute | solution.py:727
  164.5 21.9 %all-to-all-start.4 = ((bf16[16,144,256]{2,1,0:T(8,128)(2,1)}), bf16[16,144,256]{2,1,0:T(8,128)(2,1)S(1)}, u32[]{:S(2)}, u32[]{:S(2)}) async-start(bf16[16,144,256]{2,1,0:T(8,128)(2,1)} %get-tuple-element.99), calls=%async_computation.4 | async-start | bytes 2359296 | tf_op jit(solution)/shard_map/all_to_all | solution.py:733
  168.2 16.9 %collective-permute-start.21 = (bf16[48,256]{1,0:T(8,128)(2,1)S(1)}, bf16[48,256]{1,0:T(8,128)(2,1)S(1)}, u32[]{:S(2)}, u32[]{:S(2)}) collective-permute-start(bf16[48,256]{1,0:T(8,128)(2,1)S(1)} %get-tuple-element.102), channel_id=1, source_target_pairs={{0,7},{1,6},{2,5},{3,4},{4,3},{5,2},{6,1},{7,0},{8,15},{9,14},{10,... | collective-permute-start | bytes 73736 | tf_op jit(solution)/shard_map/ppermute | solution.py:730
  186.4 4.8 %collective-permute-start.22 = (bf16[16,144,256]{2,1,0:T(8,128)(2,1)S(1)}, bf16[16,144,256]{2,1,0:T(8,128)(2,1)S(1)}, u32[]{:S(2)}, u32[]{:S(2)}) collective-permute-start(bf16[16,144,256]{2,1,0:T(8,128)(2,1)S(1)} %all-to-all-done.4.refs_1_), channel_id=1, source_target_pairs={{0,1},{1,0},{2,3},{3,2},{4,5},{5,4},{6,7},{7,6},{8,9},{9,8},{10,11... | collective-permute-start | bytes 3538952 | tf_op jit(solution)/shard_map/ppermute | solution.py:736

commit v17 on v15

--- a/solution.py
+++ b/solution.py
@@ -53,36 +53,16 @@
 ]
 
 
-def run(kernel, outs, scratch, pos, *args, taps=None):
+def run(kernel, outs, scratch, pos, *args):
     vmem = pl.BlockSpec(memory_space=pltpu.VMEM)
-    in_specs = [pl.BlockSpec(memory_space=pltpu.SMEM)] + [vmem] * len(args)
-    scratch = [pltpu.VMEM(shape, dtype) for shape, dtype in scratch]
-    operands = (pos,) + args
-    inner = kernel
-    if taps is not None:
-        in_specs = in_specs + [pl.BlockSpec(memory_space=pl.ANY)]
-        scratch = scratch + [pltpu.VMEM(taps.shape, taps.dtype), pltpu.SemaphoreType.DMA(())]
-        operands = operands + (taps,)
-
-        def inner(*refs):
-            source, held, sem = refs[len(args) + 1], refs[-2], refs[-1]
-            copy = pltpu.make_async_copy(source, held, sem)
-            copy.start()
-
-            def fetched():
-                copy.wait()
-                return held
-
-            kernel(*refs[: len(args) + 1], fetched, *refs[len(args) + 2 : -2])
-
     return pl.pallas_call(
-        inner,
+        kernel,
         out_shape=[jax.ShapeDtypeStruct(shape, dtype) for shape, dtype in outs],
-        in_specs=in_specs,
+        in_specs=[pl.BlockSpec(memory_space=pltpu.SMEM)] + [vmem] * len(args),
         out_specs=[vmem] * len(outs),
-        scratch_shapes=scratch,
+        scratch_shapes=[pltpu.VMEM(shape, dtype) for shape, dtype in scratch],
         compiler_params=pltpu.CompilerParams(vmem_limit_bytes=24 * 2**20),
-    )(*operands)
+    )(pos, *args)
 
 
 def slope_of(v):
@@ -238,21 +218,20 @@
 
 
 def rim_kernel(
-    pos, own, swapped, odd, end_one, end_two, fetched, wide, first, second, send, cells, ends, lines, strips
+    pos, own, swapped, odd, end_one, end_two, taps, wide, first, second, send, cells, ends, lines, strips
 ):
     row, col = pos[0], pos[1]
     lines[...] = jnp.zeros_like(lines)
     widen(pos, own, swapped, odd, wide, first, second, cells)
     long_strips(pos, end_one, end_two, cells, ends, lines)
     bottom, right = 2 * (row // 4), 2 * (col // 4)
-    kernel = fetched()
     totals = []
     for kind in range(2):
         total = None
         for k in range(3):
             at = [(2 * f + kind) * PITCH + k for f in range(3)]
             left = jnp.concatenate([lines[i : i + PITCH, :] for i in at], axis=0).astype(BF16)
-            tap = kernel[bottom, 2 - k] if kind == 0 else kernel[2 - k, right]
+            tap = taps[bottom, 2 - k] if kind == 0 else taps[2 - k, right]
             part = dot(left, tap, ((1,), (1,)))
             total = part if total is None else total + part
         totals.append(total)
@@ -281,7 +260,7 @@
 
 
 def one_kernel(
-    pos, wide, first, second, arrived, core_ends, odd_ends, even_rows, near_rows, fetched, *refs
+    pos, wide, first, second, arrived, core_ends, odd_ends, even_rows, near_rows, taps, *refs
 ):
     filled, pre, hidden, send, cells, shifts, strips, lines, ends = refs
     row, col = pos[0], pos[1]
@@ -297,7 +276,7 @@
     stack_lines(row, wide, first, second, cells)
     fill_strips(cells, lines, row, col, 12, 1, 10, 12)
     filled[...] = cells[0 : 36 * PITCH, :].astype(BF16)
-    total = convolve(cells, shifts, 12, 10, 0, fetched(), False)
+    total = convolve(cells, shifts, 12, 10, 0, taps, False)
     pre[...] = total
     inside = cell_mask(row, col)
     for f in range(3):
@@ -310,7 +289,7 @@
 
 
 def two_kernel(
-    pos, hidden, got, pick, cotangent, fetched, packed, delta, first, second, cells, shifts, lines, ends
+    pos, hidden, got, pick, cotangent, taps, packed, delta, first, second, cells, shifts, lines, ends
 ):
     row, col = pos[0], pos[1]
     lines[...] = dot(pick[...], got[...], ((1,), (0,)))
@@ -318,7 +297,7 @@
     cells[30 * PITCH :, :] = jnp.zeros((8, C), F32)
     fill_strips(cells, lines, row, col, 10, 0, 9, 10)
     packed[0 : 30 * PITCH, :] = cells[0 : 30 * PITCH, :].astype(BF16)
-    total = convolve(cells, shifts, 10, 8, 0, fetched(), False).reshape(24, PITCH, C)[:, 0:8, :]
+    total = convolve(cells, shifts, 10, 8, 0, taps, False).reshape(24, PITCH, C)[:, 0:8, :]
     product = cotangent[...].astype(F32).reshape(24, 8, C) * slope_of(total)
     delta[...] = product.reshape(192, C).astype(BF16)
     padded = jnp.concatenate([product, jnp.zeros((24, 8, C), F32)], axis=1)
@@ -327,12 +306,12 @@
     post_ends(row, col, cells, first, second, ends)
 
 
-def back_kernel(pos, wide, first, second, fetched, back, cells, shifts):
+def back_kernel(pos, wide, first, second, taps, back, cells, shifts):
     stack_lines(pos[0], wide, first, second, cells)
-    back[...] = convolve(cells, shifts, 12, 10, 0, fetched(), True).astype(BF16)
-
-
-def delta_kernel(pos, back, got, pick, pre, fetched, wide_delta, own, send, cells, grads, shifts, strips, lines):
+    back[...] = convolve(cells, shifts, 12, 10, 0, taps, True).astype(BF16)
+
+
+def delta_kernel(pos, back, got, pick, pre, taps, wide_delta, own, send, cells, grads, shifts, strips, lines):
     row, col = pos[0], pos[1]
     lines[...] = dot(pick[...], got[...], ((1,), (0,)))
     grads[...] = back[...].astype(F32)
@@ -365,7 +344,7 @@
         begin = (f * 12 + 2) * PITCH + 2
         mine = jnp.where(at < 8, cells[begin : begin + 8 * PITCH, :], 0.0)
         wide_delta[f * 8 * PITCH : (f + 1) * 8 * PITCH, :] = mine.astype(BF16)
-    total = convolve(cells, shifts, 12, 10, 0, fetched(), True)
+    total = convolve(cells, shifts, 12, 10, 0, taps, True)
     grads[...] = total
     take_strips(grads, strips, row, col, 10, 0, 9, 1, 8)
     send[...] = strips[...].astype(BF16)
@@ -641,7 +620,7 @@
         second,
         arrived,
         *sides,
-        taps=kernel_one,
+        kernel_one,
     )
     filled_other = lax.ppermute(filled, "core", CORES)
     packed, delta, first, second = run(
@@ -653,7 +632,7 @@
         seam_exchange(send),
         pick_10,
         cotangent.reshape(192, C),
-        taps=kernel_two,
+        kernel_two,
     )
     wide, first, second, send = run(
         rim_kernel,
@@ -661,10 +640,18 @@
         [((24, PITCH, C), F32), ((32, C), F32), ((6 * PITCH + 8, C), F32), ((64, C), F32)],
         pos,
         *beside(delta, first, second),
-        taps=kernel_two,
+        kernel_two,
     )
     got = seam_exchange(send)
     first, second = lax.ppermute(first, TILE, EVEN_ROWS), lax.ppermute(second, TILE, ODD_ROWS)
+    piece = (16, 72, C)
+
+    def halves(height):
+        return [((3 * height * PITCH + 8, 128), F32), ((3 * height * PITCH, 128), BF16)]
+
+    packed_other = lax.ppermute(packed, "core", CORES)
+    grad_two = run(grad_two_kernel, [(piece, BF16)], halves(10) + [(piece, F32)], pos, packed, packed_other)[0]
+    grad_two, wide = lax.optimization_barrier((grad_two, wide))
     back = run(
         back_kernel,
         [((30 * PITCH, C), BF16)],
@@ -673,16 +660,9 @@
         wide,
         first,
         second,
-        taps=kernel_two,
+        kernel_two,
     )[0]
-    piece = (16, 72, C)
-
-    def halves(height):
-        return [((3 * height * PITCH + 8, 128), F32), ((3 * height * PITCH, 128), BF16)]
-
-    packed_other = lax.ppermute(packed, "core", CORES)
-    grad_two = run(grad_two_kernel, [(piece, BF16)], halves(10) + [(piece, F32)], pos, packed, packed_other)[0]
-    got, grad_two = lax.optimization_barrier((got, grad_two))
+    got, back = lax.optimization_barrier((got, back))
     wide_one, own, strips = run(
         delta_kernel,
         [((24 * PITCH, C), BF16), ((192, C), BF16), ((48, C), BF16)],
@@ -692,7 +672,7 @@
         got,
         add_10,
         pre_one,
-        taps=kernel_one,
+        kernel_one,
     )
     wide_other = lax.ppermute(wide_one, "core", CORES)
     part = run(grad_own_kernel, [(piece, F32)], halves(12), pos, filled, wide_one)[0]

time: 193 us -> 189 us (0.979)
  Pallas kernels: 31.8 us -> 28.5 us
  starting transfers between devices: 68.8 us -> 66.4 us
  local copies, waits for them, and re-layouts: 7.75 us -> 9.97 us
    pallas_call x17, Pallas kernels: 25 us -> 21.6 us  [run(): pl.pallas_call(kernel, out_shape=[jax.ShapeDtypeStruct(shape, dtype) for...]
    all_to_all x2, starting transfers between devices: 11.2 us -> 8.64 us  [body(): part = lax.all_to_all(part, AXES, 0, 0, axis_index_groups=PLANE_GROUPS)]
    unnamed x38 -> x52, local copies, waits for them, and re-layouts: 6.38 us -> 8.61 us
    ppermute x2, waiting for transfers between devices: 2.18 us -> 0.01 us  [body(): lax.ppermute(first, TILE, EVEN_ROWS)]
    all_to_all x2, waiting for transfers between devices: 12.9 us -> 15 us  [seam_exchange(): got = lax.all_to_all(send, AXES, 0, 0, axis_index_groups=SEAM_GROUPS)]
  transfers between devices with their start and end apart: 29 -> 29, of which waited for: 15 -> 15; matrix products, arithmetic and copies ran while one was open for 1% -> 1% of each run, Pallas kernels for 8% -> 7%
where the time goes in v17:
time: 189 us; the launch traced here: 188 us
  starting transfers between devices  66.4 us (35%)
  waiting for transfers between devices  56.3 us (30%)
  Pallas kernels  28.5 us (15%)
  blocking collectives  25.6 us (14%)
  local copies, waits for them, and re-layouts  9.97 us (5%)
    all_to_all x1, blocking collectives, seam_exchange(): got = lax.all_to_all(send, AXES, 0, 0, axis_index_groups=SEAM_GROUPS)  25.6 us
    pallas_call x17, Pallas kernels, run(): pl.pallas_call(kernel, out_shape=[jax.ShapeDtypeStruct(shape, dtype) for...  21.6 us
    all_to_all x2, starting transfers between devices, seam_exchange(): got = lax.all_to_all(send, AXES, 0, 0, axis_index_groups=SEAM_GROUPS)  20.1 us
    all_to_all x2, waiting for transfers between devices, seam_exchange(): got = lax.all_to_all(send, AXES, 0, 0, axis_index_groups=SEAM_GROUPS)  15 us
    all_to_all x2, waiting for transfers between devices, body(): part = lax.all_to_all(part, AXES, 0, 0, axis_index_groups=PLANE_GROUPS)  9.81 us
    ppermute x1, waiting for transfers between devices, body(): onward = lax.ppermute(onward, TILE, [(t, t ^ 7) for t in range(64)])  8.88 us
    all_to_all x2, starting transfers between devices, body(): part = lax.all_to_all(part, AXES, 0, 0, axis_index_groups=PLANE_GROUPS)  8.64 us
    unnamed x52, local copies, waits for them, and re-layouts  8.61 us
  transfers between devices with their start and end apart: 29, of which 15 were waited for; matrix products, arithmetic and copies ran while one was open for 1% of the time, Pallas kernels for 7%

profile of v17, /device:TPU:1, one launch (start us, length us, event | category | flops | bytes accessed | tf_op | source)
XLA Modules:
  0.0 188.0 jit_solution(429209647919090893)
XLA Ops:
  0.7 1.0 copy-done.8
  1.7 1.3 shard_map.85
  3.0 14.3 %all-to-all-start = ((bf16[16,48,256]{2,1,0:T(8,128)(2,1)}), bf16[16,48,256]{2,1,0:T(8,128)(2,1)S(1)}, u32[]{:S(2)}, u32[]{:S(2)}) async-start(bf16[16,48,256]{2,1,0:T(8,128)(2,1)} %shard_map.85), calls=%async_computation | async-start | bytes 786432 | tf_op jit(solution)/shard_map/all_to_all | solution.py:478
  17.4 1.9 %collective-permute-start.1 = (bf16[192,256]{1,0:T(8,128)(2,1)S(1)}, bf16[192,256]{1,0:T(8,128)(2,1)S(1)}, u32[]{:S(2)}, u32[]{:S(2)}) collective-permute-start(bf16[192,256]{1,0:T(8,128)(2,1)S(1)} %bitcast.18), channel_id=1, source_target_pairs={{1,2},{3,4},{5,6},{9,10},{11,12},{13,14},{17,18},{19,20},{21,22},{... | collective-permute-start | bytes 294920 | tf_op jit(solution)/shard_map/ppermute | solution.py:602
  19.4 4.2 %collective-permute-done.1.odd = bf16[192,256]{1,0:T(8,128)(2,1)S(1)} collective-permute-done((bf16[192,256]{1,0:T(8,128)(2,1)S(1)}, bf16[192,256]{1,0:T(8,128)(2,1)S(1)}, u32[]{:S(2)}, u32[]{:S(2)}) %collective-permute-start.1) | collective-permute-done | bytes 98336 | tf_op jit(solution)/shard_map/ppermute | solution.py:602
  26.5 2.6 %shard_map.87 = (bf16[80,768]{1,0:T(8,128)(2,1)}, bf16[64,1024]{1,0:T(8,128)(2,1)}, bf16[64,1024]{1,0:T(8,128)(2,1)}, bf16[192,256]{1,0:T(8,128)(2,1)}) custom-call(s32[4]{0:T(128)} %copy-done.12, s32[12,4]{1,0:T(8,128)} %copy.11.nexts, s32[12,4]{1,0:T(8,128)} %copy.12.codes), custom_call_target="tpu_custom_call" | custom-call | tf_op jit(solution)/shard_map/pallas_call | solution.py:569
  29.1 4.9 %all-to-all-done = bf16[16,48,256]{2,1,0:T(8,128)(2,1)S(1)} async-done(((bf16[16,48,256]{2,1,0:T(8,128)(2,1)}), bf16[16,48,256]{2,1,0:T(8,128)(2,1)S(1)}, u32[]{:S(2)}, u32[]{:S(2)}) %all-to-all-start) | async-done | bytes 393248 | tf_op jit(solution)/shard_map/all_to_all | solution.py:478
  36.4 1.9 %collective-permute-start.5 = (bf16[16,256]{1,0:T(8,128)(2,1)S(1)}, bf16[16,256]{1,0:T(8,128)(2,1)S(1)}, u32[]{:S(2)}, u32[]{:S(2)}) collective-permute-start(bf16[16,256]{1,0:T(8,128)(2,1)S(1)} %get-tuple-element.74), channel_id=1, source_target_pairs={{1,2},{3,4},{5,6},{9,10},{11,12},{13,14},{17,18},{19,20},{21,22},{... | collective-permute-start | bytes 24584 | tf_op jit(solution)/shard_map/ppermute | solution.py:609
  39.1 2.3 %collective-permute-done.5.odd_ends = bf16[16,256]{1,0:T(8,128)(2,1)S(1)} collective-permute-done((bf16[16,256]{1,0:T(8,128)(2,1)S(1)}, bf16[16,256]{1,0:T(8,128)(2,1)S(1)}, u32[]{:S(2)}, u32[]{:S(2)}) %collective-permute-start.5) | collective-permute-done | bytes 8224 | tf_op jit(solution)/shard_map/ppermute | solution.py:609
  41.4 1.5 shard_map.89
  43.7 25.6 %all_to_all.25 = bf16[16,64,256]{2,1,0:T(8,128)(2,1)S(1)} all-to-all(bf16[16,64,256]{2,1,0:T(8,128)(2,1)S(1)} %get-tuple-element.79), channel_id=1, replica_groups={{0,7,56,63,64,71,120,127,128,135,184,191,192,199,248,255},{1,6,57,62,65..., dimensions={0} | all-to-all | bytes 1048576 | tf_op jit(solution)/shard_map/all_to_all | solution.py:478
  69.3 1.6 shard_map.90
  70.9 2.0 %collective-permute-start.10 = (bf16[192,256]{1,0:T(8,128)(2,1)S(1)}, bf16[192,256]{1,0:T(8,128)(2,1)S(1)}, u32[]{:S(2)}, u32[]{:S(2)}) collective-permute-start(bf16[192,256]{1,0:T(8,128)(2,1)S(1)} %get-tuple-element.81.own), channel_id=1, source_target_pairs={{1,2},{3,4},{5,6},{9,10},{11,12},{13,14},{17,18},{19,20},{21,22},{... | collective-permute-start | bytes 294920 | tf_op jit(solution)/shard_map/ppermute | solution.py:592
  73.9 1.8 collective-permute-done.11.end_one
  75.7 1.2 collective-permute-done.10.odd
  76.9 1.8 shard_map.91
  79.4 5.7 %all-to-all-start.2 = ((bf16[16,64,256]{2,1,0:T(8,128)(2,1)}), bf16[16,64,256]{2,1,0:T(8,128)(2,1)S(1)}, u32[]{:S(2)}, u32[]{:S(2)}) async-start(bf16[16,64,256]{2,1,0:T(8,128)(2,1)} %get-tuple-element.84), calls=%async_computation.2 | async-start | bytes 1048576 | tf_op jit(solution)/shard_map/all_to_all | solution.py:478
  85.7 3.3 %collective-permute-start.14 = (bf16[96,256]{1,0:T(8,128)(2,1)}, bf16[96,256]{1,0:T(8,128)(2,1)S(1)}, u32[]{:S(2)}, u32[]{:S(2)}) collective-permute-start(bf16[96,256]{1,0:T(8,128)(2,1)} %get-tuple-element.88), channel_id=1, source_target_pairs={{0,8},{1,9},{2,10},{3,11},{4,12},{5,13},{6,14},{7,15},{16,24},{17,... | collective-permute-start | bytes 147464 | tf_op jit(solution)/shard_map/ppermute | solution.py:646
  89.7 1.0 copy-done.7
  90.7 1.4 shard_map.92.two
  92.1 1.3 shard_map.93.back
  94.2 10.1 %all-to-all-done.2 = bf16[16,64,256]{2,1,0:T(8,128)(2,1)S(1)} async-done(((bf16[16,64,256]{2,1,0:T(8,128)(2,1)}), bf16[16,64,256]{2,1,0:T(8,128)(2,1)S(1)}, u32[]{:S(2)}, u32[]{:S(2)}) %all-to-all-start.2) | async-done | bytes 524320 | tf_op jit(solution)/shard_map/all_to_all | solution.py:478
  104.3 0.9 copy-done.3
  105.2 1.0 copy-done.5
  106.3 0.9 copy-done.17
  107.2 2.1 %shard_map.94 = (bf16[384,256]{1,0:T(8,128)(2,1)S(1)}, bf16[192,256]{1,0:T(8,128)(2,1)S(1)}, bf16[48,256]{1,0:T(8,128)(2,1)S(1)}) custom-call(s32[4]{0:T(128)S(1)} %copy-done.14, bf16[480,256]{1,0:T(8,128)(2,1)S(1)} %copy-done.3, bf16[1024,256]{1,0:T(8,128)(2,1)S(1)} %bitcast.15, bf16[64,1024]{1,0:T(8,128)(2,1)S(1)} %copy-done.17, f32[480,256]{1,0:T(8,128)S(1)} %copy-done.5, ...), custom_call_target="tpu_custom_call" | custom-call | tf_op jit(solution)/shard_map/pallas_call | solution.py:58
  109.4 1.1 shard_map.95.part
  110.9 2.5 %shard_map.96 = bf16[16,144,256]{2,1,0:T(8,128)(2,1)} custom-call(s32[4]{0:T(128)S(1)} %copy-done.14, bf16[576,256]{1,0:T(8,128)(2,1)} %collective-permute-done.8.source, bf16[384,256]{1,0:T(8,128)(2,1)S(1)} %collective-permute-done.16.delta, f32[16,72,256]{2,1,0:T(8,128)S(1)} %shard_map.95.part, bf16[16,72,256]{2,1,0:T(8,128)(2,1)S(1)} %shard_map.92.two), custom_call_target="tpu_custom_call" | custom-call | tf_op jit(solution)/shard_map/pallas_call | solution.py:58
  113.4 4.8 %all-to-all-start.3 = ((bf16[16,144,256]{2,1,0:T(8,128)(2,1)}), bf16[16,144,256]{2,1,0:T(8,128)(2,1)S(1)}, u32[]{:S(2)}, u32[]{:S(2)}) async-start(bf16[16,144,256]{2,1,0:T(8,128)(2,1)} %shard_map.96), calls=%async_computation.3 | async-start | bytes 2359296 | tf_op jit(solution)/shard_map/all_to_all | solution.py:691
  118.2 2.1 %collective-permute-start.19 = (bf16[48,256]{1,0:T(8,128)(2,1)S(1)}, bf16[48,256]{1,0:T(8,128)(2,1)S(1)}, u32[]{:S(2)}, u32[]{:S(2)}) collective-permute-start(bf16[48,256]{1,0:T(8,128)(2,1)S(1)} %get-tuple-element.98.one), channel_id=1, source_target_pairs={{0,192},{64,0},{128,64},{192,128},{1,193},{65,1},{129,65},{193,129... | collective-permute-start | bytes 73736 | tf_op jit(solution)/shard_map/ppermute | solution.py:690
  121.2 1.1 collective-permute-start.17
  122.3 2.0 %collective-permute-done.18.three = bf16[48,256]{1,0:T(8,128)(2,1)S(1)} collective-permute-done((bf16[48,256]{1,0:T(8,128)(2,1)S(1)}, bf16[48,256]{1,0:T(8,128)(2,1)S(1)}, u32[]{:S(2)}, u32[]{:S(2)}) %collective-permute-start.18) | collective-permute-done | bytes 24608 | tf_op jit(solution)/shard_map/ppermute | solution.py:690
  124.3 1.7 collective-permute-done.17.two
  126.7 9.8 %all-to-all-done.3.parts = bf16[16,144,256]{2,1,0:T(8,128)(2,1)S(1)} async-done(((bf16[16,144,256]{2,1,0:T(8,128)(2,1)}), bf16[16,144,256]{2,1,0:T(8,128)(2,1)S(1)}, u32[]{:S(2)}, u32[]{:S(2)}) %all-to-all-start.3) | async-done | bytes 1179680 | tf_op jit(solution)/shard_map/all_to_all | solution.py:691
  137.2 1.8 collective-permute-start.20
  138.9 1.7 collective-permute-done.20.two
  141.2 2.3 %collective-permute-start.21 = (bf16[144,256]{1,0:T(8,128)(2,1)S(1)}, bf16[144,256]{1,0:T(8,128)(2,1)S(1)}, u32[]{:S(2)}, u32[]{:S(2)}) collective-permute-start(bf16[144,256]{1,0:T(8,128)(2,1)S(1)} %shard_map.99.one), channel_id=1, source_target_pairs={{0,128},{64,192},{128,0},{192,64},{1,129},{65,193},{129,1},{193,65... | collective-permute-start | bytes 221192 | tf_op jit(solution)/shard_map/ppermute | solution.py:698
  143.6 1.9 collective-permute-done.21.two
  146.0 6.1 %collective-permute-start.22 = (bf16[240,256]{1,0:T(8,128)(2,1)S(1)}, bf16[240,256]{1,0:T(8,128)(2,1)S(1)}, u32[]{:S(2)}, u32[]{:S(2)}) collective-permute-start(bf16[240,256]{1,0:T(8,128)(2,1)S(1)} %shard_map.100.one), channel_id=1, source_target_pairs={{0,56},{1,57},{2,58},{3,59},{4,60},{5,61},{6,62},{7,63},{8,48},{9,... | collective-permute-start | bytes 368648 | tf_op jit(solution)/shard_map/ppermute | solution.py:700
  152.1 5.1 %collective-permute-done.22.two = bf16[240,256]{1,0:T(8,128)(2,1)S(1)} collective-permute-done((bf16[240,256]{1,0:T(8,128)(2,1)S(1)}, bf16[240,256]{1,0:T(8,128)(2,1)S(1)}, u32[]{:S(2)}, u32[]{:S(2)}) %collective-permute-start.22) | collective-permute-done | bytes 122912 | tf_op jit(solution)/shard_map/ppermute | solution.py:700
  157.2 1.6 shard_map.101
  158.8 3.8 %all-to-all-start.4 = ((bf16[16,144,256]{2,1,0:T(8,128)(2,1)}), bf16[16,144,256]{2,1,0:T(8,128)(2,1)S(1)}, u32[]{:S(2)}, u32[]{:S(2)}) async-start(bf16[16,144,256]{2,1,0:T(8,128)(2,1)} %get-tuple-element.107), calls=%async_computation.4 | async-start | bytes 2359296 | tf_op jit(solution)/shard_map/all_to_all | solution.py:706
  162.7 8.0 %collective-permute-start.23 = (bf16[48,256]{1,0:T(8,128)(2,1)S(1)}, bf16[48,256]{1,0:T(8,128)(2,1)S(1)}, u32[]{:S(2)}, u32[]{:S(2)}) collective-permute-start(bf16[48,256]{1,0:T(8,128)(2,1)S(1)} %get-tuple-element.110), channel_id=1, source_target_pairs={{0,7},{1,6},{2,5},{3,4},{4,3},{5,2},{6,1},{7,0},{8,15},{9,14},{10,... | collective-permute-start | bytes 73736 | tf_op jit(solution)/shard_map/ppermute | solution.py:703
  170.7 8.9 %collective-permute-done.23.by_col = bf16[48,256]{1,0:T(8,128)(2,1)S(1)} collective-permute-done((bf16[48,256]{1,0:T(8,128)(2,1)S(1)}, bf16[48,256]{1,0:T(8,128)(2,1)S(1)}, u32[]{:S(2)}, u32[]{:S(2)}) %collective-permute-start.23) | collective-permute-done | bytes 24608 | tf_op jit(solution)/shard_map/ppermute | solution.py:703
  179.6 1.3 shard_map.102
  180.8 2.4 %collective-permute-start.24 = (bf16[16,144,256]{2,1,0:T(8,128)(2,1)S(1)}, bf16[16,144,256]{2,1,0:T(8,128)(2,1)S(1)}, u32[]{:S(2)}, u32[]{:S(2)}) collective-permute-start(bf16[16,144,256]{2,1,0:T(8,128)(2,1)S(1)} %all-to-all-done.4.refs_1_), channel_id=1, source_target_pairs={{0,1},{1,0},{2,3},{3,2},{4,5},{5,4},{6,7},{7,6},{8,9},{9,8},{10,11... | collective-permute-start | bytes 3538952 | tf_op jit(solution)/shard_map/ppermute | solution.py:709
  183.3 2.1 %shard_map.103 = (f32[9,256,256]{2,1,0:T(8,128)}, f32[9,256,256]{2,1,0:T(8,128)}) custom-call(s32[4]{0:T(128)S(1)} %copy-done.14, bf16[16,144,256]{2,1,0:T(8,128)(2,1)S(1)} %all-to-all-done.4.refs_1_), custom_call_target="tpu_custom_call" | custom-call | tf_op jit(solution)/shard_map/pallas_call | solution.py:466
  185.7 2.1 %shard_map.104 = (f32[9,256,256]{2,1,0:T(8,128)}, f32[9,256,256]{2,1,0:T(8,128)}) custom-call(s32[4]{0:T(128)S(1)} %copy-done.14, bf16[16,144,256]{2,1,0:T(8,128)(2,1)S(1)} %collective-permute-done.24.refs_1_, f32[9,256,256]{2,1,0:T(8,128)} %get-tuple-element.113.refs_2_, ...), custom_call_target="tpu_custom_call", output_to_operand_aliasing={{0}: (2, {}), {1}: (3, {})} | custom-call | tf_op jit(solution)/shard_map/pallas_call | solution.py:466
  (86 shorter events, 14.6 us)
Async XLA Ops:
  0.6 40.7 %copy-start.1 = (bf16[3,3,256,256]{3,2,1,0:T(8,128)(2,1)S(1)}, bf16[3,3,256,256]{3,2,1,0:T(8,128)(2,1)}, u32[]{:S(2)}) copy-start(bf16[3,3,256,256]{3,2,1,0:T(8,128)(2,1)} %taps.9) | copy-start | bytes 3538948
  0.7 25.7 %copy-start.12 = (s32[4]{0:T(128)}, s32[4]{0:T(128)S(1)}, u32[]{:S(2)}) copy-start(s32[4]{0:T(128)S(1)} %pad_add_fusion.pos.refs_0_) | copy-start | bytes 52
  0.7 1.0 copy-start.8
  1.7 15.7 %copy-start.9 = (bf16[3,1,8,8,256]{4,3,2,1,0:T(8,128)(2,1)S(1)}, bf16[3,1,8,8,256]{4,3,2,1,0:T(8,128)(2,1)}, u32[]{:S(2)}) copy-start(bf16[3,1,8,8,256]{4,3,2,1,0:T(8,128)(2,1)} %param.6) | copy-start | bytes 294916
  1.7 23.4 %copy-start.24 = (s32[12,4]{0,1:T(4,128)S(1)}, s32[12,4]{0,1:T(4,128)}, u32[]{:S(2)}) copy-start(s32[12,4]{0,1:T(4,128)} %param.10) | copy-start | bytes 580
  1.7 24.1 %copy-start.25 = (s32[12,4]{0,1:T(4,128)S(1)}, s32[12,4]{0,1:T(4,128)}, u32[]{:S(2)}) copy-start(s32[12,4]{0,1:T(4,128)} %param.11) | copy-start | bytes 580
  3.0 30.9 %all-to-all-start = ((bf16[16,48,256]{2,1,0:T(8,128)(2,1)}), bf16[16,48,256]{2,1,0:T(8,128)(2,1)S(1)}, u32[]{:S(2)}, u32[]{:S(2)}) async-start(bf16[16,48,256]{2,1,0:T(8,128)(2,1)} %shard_map.85), calls=%async_computation | async-start | bytes 786432 | tf_op jit(solution)/shard_map/all_to_all | solution.py:478
  17.4 6.2 %collective-permute-start.1 = (bf16[192,256]{1,0:T(8,128)(2,1)S(1)}, bf16[192,256]{1,0:T(8,128)(2,1)S(1)}, u32[]{:S(2)}, u32[]{:S(2)}) collective-permute-start(bf16[192,256]{1,0:T(8,128)(2,1)S(1)} %bitcast.18), channel_id=1, source_target_pairs={{1,2},{3,4},{5,6},{9,10},{11,12},{13,14},{17,18},{19,20},{21,22},{... | collective-permute-start | bytes 294920 | tf_op jit(solution)/shard_map/ppermute | solution.py:602
  19.3 4.3 %collective-permute-start = (bf16[192,256]{1,0:T(8,128)(2,1)S(1)}, bf16[192,256]{1,0:T(8,128)(2,1)S(1)}, u32[]{:S(2)}, u32[]{:S(2)}) collective-permute-start(bf16[192,256]{1,0:T(8,128)(2,1)S(1)} %bitcast.19), channel_id=1, source_target_pairs={{0,1},{1,0},{2,3},{3,2},{4,5},{5,4},{6,7},{7,6},{8,9},{9,8},{10,11... | collective-permute-start | bytes 294920 | tf_op jit(solution)/shard_map/ppermute | solution.py:602
  24.3 4.8 %collective-permute-start.2 = (bf16[96,256]{1,0:T(8,128)(2,1)S(1)}, bf16[96,256]{1,0:T(8,128)(2,1)S(1)}, u32[]{:S(2)}, u32[]{:S(2)}) collective-permute-start(bf16[96,256]{1,0:T(8,128)(2,1)S(1)} %get-tuple-element.63), channel_id=1, source_target_pairs={{0,8},{1,9},{2,10},{3,11},{4,12},{5,13},{6,14},{7,15},{16,24},{17,... | collective-permute-start | bytes 147464 | tf_op jit(solution)/shard_map/ppermute | solution.py:604
  24.4 4.7 %collective-permute-start.3 = (bf16[96,256]{1,0:T(8,128)(2,1)S(1)}, bf16[96,256]{1,0:T(8,128)(2,1)S(1)}, u32[]{:S(2)}, u32[]{:S(2)}) collective-permute-start(bf16[96,256]{1,0:T(8,128)(2,1)S(1)} %get-tuple-element.64), channel_id=1, source_target_pairs={{8,16},{9,17},{10,18},{11,19},{12,20},{13,21},{14,22},{15,23},{24,... | collective-permute-start | bytes 147464 | tf_op jit(solution)/shard_map/ppermute | solution.py:604
  36.3 2.8 %collective-permute-start.4 = (bf16[16,256]{1,0:T(8,128)(2,1)S(1)}, bf16[16,256]{1,0:T(8,128)(2,1)S(1)}, u32[]{:S(2)}, u32[]{:S(2)}) collective-permute-start(bf16[16,256]{1,0:T(8,128)(2,1)S(1)} %get-tuple-element.73), channel_id=1, source_target_pairs={{0,1},{1,0},{2,3},{3,2},{4,5},{5,4},{6,7},{7,6},{8,9},{9,8},{10,11... | collective-permute-start | bytes 24584 | tf_op jit(solution)/shard_map/ppermute | solution.py:608
  36.4 5.0 %collective-permute-start.5 = (bf16[16,256]{1,0:T(8,128)(2,1)S(1)}, bf16[16,256]{1,0:T(8,128)(2,1)S(1)}, u32[]{:S(2)}, u32[]{:S(2)}) collective-permute-start(bf16[16,256]{1,0:T(8,128)(2,1)S(1)} %get-tuple-element.74), channel_id=1, source_target_pairs={{1,2},{3,4},{5,6},{9,10},{11,12},{13,14},{17,18},{19,20},{21,22},{... | collective-permute-start | bytes 24584 | tf_op jit(solution)/shard_map/ppermute | solution.py:609
  38.3 3.0 %collective-permute-start.6 = (bf16[16,256]{1,0:T(8,128)(2,1)S(1)}, bf16[16,256]{1,0:T(8,128)(2,1)S(1)}, u32[]{:S(2)}, u32[]{:S(2)}) collective-permute-start(bf16[16,256]{1,0:T(8,128)(2,1)S(1)} %get-tuple-element.75), channel_id=1, source_target_pairs={{0,8},{1,9},{2,10},{3,11},{4,12},{5,13},{6,14},{7,15},{16,24},{17,... | collective-permute-start | bytes 24584 | tf_op jit(solution)/shard_map/ppermute | solution.py:610
  38.4 2.9 %collective-permute-start.7 = (bf16[16,256]{1,0:T(8,128)(2,1)S(1)}, bf16[16,256]{1,0:T(8,128)(2,1)S(1)}, u32[]{:S(2)}, u32[]{:S(2)}) collective-permute-start(bf16[16,256]{1,0:T(8,128)(2,1)S(1)} %get-tuple-element.76), channel_id=1, source_target_pairs={{8,16},{9,17},{10,18},{11,19},{12,20},{13,21},{14,22},{15,23},{40,... | collective-permute-start | bytes 24584 | tf_op jit(solution)/shard_map/ppermute | solution.py:611
  41.4 27.9 %copy-start = (bf16[3,3,256,256]{3,2,1,0:T(8,128)(2,1)S(1)}, bf16[3,3,256,256]{3,2,1,0:T(8,128)(2,1)}, u32[]{:S(2)}) copy-start(bf16[3,3,256,256]{3,2,1,0:T(8,128)(2,1)} %taps.8) | copy-start | bytes 3538948
  41.4 27.9 %copy-start.18 = (bf16[64,1024]{1,0:T(8,128)(2,1)S(1)}, bf16[64,1024]{1,0:T(8,128)(2,1)}, u32[]{:S(2)}) copy-start(bf16[64,1024]{1,0:T(8,128)(2,1)} %get-tuple-element.80.pick) | copy-start | bytes 393220
  41.4 27.9 %copy-start.20 = (bf16[3,1,8,8,256]{4,3,2,1,0:T(8,128)(2,1)S(1)}, bf16[3,1,8,8,256]{4,3,2,1,0:T(8,128)(2,1)}, u32[]{:S(2)}) copy-start(bf16[3,1,8,8,256]{4,3,2,1,0:T(8,128)(2,1)} %param.7) | copy-start | bytes 294916
  43.7 27.2 %copy-start.10 = (bf16[576,256]{1,0:T(8,128)(2,1)}, bf16[576,256]{1,0:T(8,128)(2,1)S(1)}, u32[]{:S(2)}) copy-start(bf16[576,256]{1,0:T(8,128)(2,1)S(1)} %get-tuple-element.77.source) | copy-start | bytes 884740
  70.9 14.2 %copy-start.6 = (bf16[864,256]{1,0:T(8,128)(2,1)}, bf16[864,256]{1,0:T(8,128)(2,1)S(1)}, u32[]{:S(2)}) copy-start(bf16[864,256]{1,0:T(8,128)(2,1)S(1)} %get-tuple-element.85.own) | copy-start | bytes 1327108
  70.9 5.9 %collective-permute-start.10 = (bf16[192,256]{1,0:T(8,128)(2,1)S(1)}, bf16[192,256]{1,0:T(8,128)(2,1)S(1)}, u32[]{:S(2)}, u32[]{:S(2)}) collective-permute-start(bf16[192,256]{1,0:T(8,128)(2,1)S(1)} %get-tuple-element.81.own), channel_id=1, source_target_pairs={{1,2},{3,4},{5,6},{9,10},{11,12},{13,14},{17,18},{19,20},{21,22},{... | collective-permute-start | bytes 294920 | tf_op jit(solution)/shard_map/ppermute | solution.py:592
  73.0 3.9 %collective-permute-start.9 = (bf16[192,256]{1,0:T(8,128)(2,1)S(1)}, bf16[192,256]{1,0:T(8,128)(2,1)S(1)}, u32[]{:S(2)}, u32[]{:S(2)}) collective-permute-start(bf16[192,256]{1,0:T(8,128)(2,1)S(1)} %get-tuple-element.81.own), channel_id=1, source_target_pairs={{0,1},{1,0},{2,3},{3,2},{4,5},{5,4},{6,7},{7,6},{8,9},{9,8},{10,11... | collective-permute-start | bytes 294920 | tf_op jit(solution)/shard_map/ppermute | solution.py:591
  73.1 2.6 %collective-permute-start.11 = (bf16[16,256]{1,0:T(8,128)(2,1)S(1)}, bf16[16,256]{1,0:T(8,128)(2,1)S(1)}, u32[]{:S(2)}, u32[]{:S(2)}) collective-permute-start(bf16[16,256]{1,0:T(8,128)(2,1)S(1)} %get-tuple-element.82), channel_id=1, source_target_pairs={{0,8},{1,9},{2,10},{3,11},{4,12},{5,13},{6,14},{7,15},{16,24},{17,... | collective-permute-start | bytes 24584 | tf_op jit(solution)/shard_map/ppermute | solution.py:593
  73.2 16.5 %copy-start.14 = (s32[4]{0:T(128)S(1)}, s32[4]{0:T(128)}, u32[]{:S(2)}) copy-start(s32[4]{0:T(128)} %copy-done.12) | copy-start | bytes 52
  73.2 2.5 %collective-permute-start.12 = (bf16[16,256]{1,0:T(8,128)(2,1)S(1)}, bf16[16,256]{1,0:T(8,128)(2,1)S(1)}, u32[]{:S(2)}, u32[]{:S(2)}) collective-permute-start(bf16[16,256]{1,0:T(8,128)(2,1)S(1)} %get-tuple-element.83), channel_id=1, source_target_pairs={{8,16},{9,17},{10,18},{11,19},{12,20},{13,21},{14,22},{15,23},{40,... | collective-permute-start | bytes 24584 | tf_op jit(solution)/shard_map/ppermute | solution.py:594
  79.4 24.9 %all-to-all-start.2 = ((bf16[16,64,256]{2,1,0:T(8,128)(2,1)}), bf16[16,64,256]{2,1,0:T(8,128)(2,1)S(1)}, u32[]{:S(2)}, u32[]{:S(2)}) async-start(bf16[16,64,256]{2,1,0:T(8,128)(2,1)} %get-tuple-element.84), calls=%async_computation.2 | async-start | bytes 1048576 | tf_op jit(solution)/shard_map/all_to_all | solution.py:478
  85.1 4.5 %collective-permute-start.13 = (bf16[864,256]{1,0:T(8,128)(2,1)S(1)}, bf16[864,256]{1,0:T(8,128)(2,1)S(1)}, u32[]{:S(2)}, u32[]{:S(2)}) collective-permute-start(bf16[864,256]{1,0:T(8,128)(2,1)S(1)} %get-tuple-element.85.own), channel_id=1, source_target_pairs={{0,1},{1,0},{2,3},{3,2},{4,5},{5,4},{6,7},{7,6},{8,9},{9,8},{10,11... | collective-permute-start | bytes 1327112 | tf_op jit(solution)/shard_map/ppermute | solution.py:652
  85.2 25.3 %collective-permute-start.8 = (bf16[576,256]{1,0:T(8,128)(2,1)}, bf16[576,256]{1,0:T(8,128)(2,1)}, u32[]{:S(2)}, u32[]{:S(2)}) collective-permute-start(bf16[576,256]{1,0:T(8,128)(2,1)} %copy-done.10), channel_id=1, source_target_pairs={{0,1},{1,0},{2,3},{3,2},{4,5},{5,4},{6,7},{7,6},{8,9},{9,8},{10,11... | collective-permute-start | bytes 884744 | tf_op jit(solution)/shard_map/ppermute | solution.py:625
  85.7 6.4 %collective-permute-start.14 = (bf16[96,256]{1,0:T(8,128)(2,1)}, bf16[96,256]{1,0:T(8,128)(2,1)S(1)}, u32[]{:S(2)}, u32[]{:S(2)}) collective-permute-start(bf16[96,256]{1,0:T(8,128)(2,1)} %get-tuple-element.88), channel_id=1, source_target_pairs={{0,8},{1,9},{2,10},{3,11},{4,12},{5,13},{6,14},{7,15},{16,24},{17,... | collective-permute-start | bytes 147464 | tf_op jit(solution)/shard_map/ppermute | solution.py:646
  89.0 3.1 %collective-permute-start.15 = (bf16[96,256]{1,0:T(8,128)(2,1)S(1)}, bf16[96,256]{1,0:T(8,128)(2,1)S(1)}, u32[]{:S(2)}, u32[]{:S(2)}) collective-permute-start(bf16[96,256]{1,0:T(8,128)(2,1)S(1)} %get-tuple-element.89), channel_id=1, source_target_pairs={{8,16},{9,17},{10,18},{11,19},{12,20},{13,21},{14,22},{15,23},{24,... | collective-permute-start | bytes 147464 | tf_op jit(solution)/shard_map/ppermute | solution.py:646
  89.7 1.0 copy-start.7
  90.7 1.5 copy-start.16
  105.2 1.0 copy-start.5
  107.2 2.2 %copy-start.11 = (bf16[576,256]{1,0:T(8,128)(2,1)S(1)}, bf16[576,256]{1,0:T(8,128)(2,1)}, u32[]{:S(2)}) copy-start(bf16[576,256]{1,0:T(8,128)(2,1)} %copy-done.10) | copy-start | bytes 884740
  109.3 1.2 copy-start.22
  109.3 1.5 collective-permute-start.16
  113.4 12.6 %copy-start.21 = (bf16[192,256]{1,0:T(8,128)(2,1)S(1)}, bf16[192,256]{1,0:T(8,128)(2,1)}, u32[]{:S(2)}) copy-start(bf16[192,256]{1,0:T(8,128)(2,1)} %get-tuple-element.99.pick) | copy-start | bytes 294916
  113.4 23.1 %all-to-all-start.3 = ((bf16[16,144,256]{2,1,0:T(8,128)(2,1)}), bf16[16,144,256]{2,1,0:T(8,128)(2,1)S(1)}, u32[]{:S(2)}, u32[]{:S(2)}) async-start(bf16[16,144,256]{2,1,0:T(8,128)(2,1)} %shard_map.96), calls=%async_computation.3 | async-start | bytes 2359296 | tf_op jit(solution)/shard_map/all_to_all | solution.py:691
  118.2 4.0 %collective-permute-start.19 = (bf16[48,256]{1,0:T(8,128)(2,1)S(1)}, bf16[48,256]{1,0:T(8,128)(2,1)S(1)}, u32[]{:S(2)}, u32[]{:S(2)}) collective-permute-start(bf16[48,256]{1,0:T(8,128)(2,1)S(1)} %get-tuple-element.98.one), channel_id=1, source_target_pairs={{0,192},{64,0},{128,64},{192,128},{1,193},{65,1},{129,65},{193,129... | collective-permute-start | bytes 73736 | tf_op jit(solution)/shard_map/ppermute | solution.py:690
  120.3 3.9 %collective-permute-start.18 = (bf16[48,256]{1,0:T(8,128)(2,1)S(1)}, bf16[48,256]{1,0:T(8,128)(2,1)S(1)}, u32[]{:S(2)}, u32[]{:S(2)}) collective-permute-start(bf16[48,256]{1,0:T(8,128)(2,1)S(1)} %get-tuple-element.98.one), channel_id=1, source_target_pairs={{0,128},{64,192},{128,0},{192,64},{1,129},{65,193},{129,1},{193,65... | collective-permute-start | bytes 73736 | tf_op jit(solution)/shard_map/ppermute | solution.py:690
  121.2 4.8 %collective-permute-start.17 = (bf16[48,256]{1,0:T(8,128)(2,1)S(1)}, bf16[48,256]{1,0:T(8,128)(2,1)S(1)}, u32[]{:S(2)}, u32[]{:S(2)}) collective-permute-start(bf16[48,256]{1,0:T(8,128)(2,1)S(1)} %get-tuple-element.98.one), channel_id=1, source_target_pairs={{0,64},{64,128},{128,192},{192,0},{1,65},{65,129},{129,193},{193,1... | collective-permute-start | bytes 73736 | tf_op jit(solution)/shard_map/ppermute | solution.py:690
  137.2 3.5 %collective-permute-start.20 = (bf16[144,256]{1,0:T(8,128)(2,1)S(1)}, bf16[144,256]{1,0:T(8,128)(2,1)S(1)}, u32[]{:S(2)}, u32[]{:S(2)}) collective-permute-start(bf16[144,256]{1,0:T(8,128)(2,1)S(1)} %shard_map.98.one), channel_id=1, source_target_pairs={{0,64},{64,0},{128,192},{192,128},{1,65},{65,1},{129,193},{193,129... | collective-permute-start | bytes 221192 | tf_op jit(solution)/shard_map/ppermute | solution.py:696
  141.2 4.2 %collective-permute-start.21 = (bf16[144,256]{1,0:T(8,128)(2,1)S(1)}, bf16[144,256]{1,0:T(8,128)(2,1)S(1)}, u32[]{:S(2)}, u32[]{:S(2)}) collective-permute-start(bf16[144,256]{1,0:T(8,128)(2,1)S(1)} %shard_map.99.one), channel_id=1, source_target_pairs={{0,128},{64,192},{128,0},{192,64},{1,129},{65,193},{129,1},{193,65... | collective-permute-start | bytes 221192 | tf_op jit(solution)/shard_map/ppermute | solution.py:698
  146.0 11.2 %collective-permute-start.22 = (bf16[240,256]{1,0:T(8,128)(2,1)S(1)}, bf16[240,256]{1,0:T(8,128)(2,1)S(1)}, u32[]{:S(2)}, u32[]{:S(2)}) collective-permute-start(bf16[240,256]{1,0:T(8,128)(2,1)S(1)} %shard_map.100.one), channel_id=1, source_target_pairs={{0,56},{1,57},{2,58},{3,59},{4,60},{5,61},{6,62},{7,63},{8,48},{9,... | collective-permute-start | bytes 368648 | tf_op jit(solution)/shard_map/ppermute | solution.py:700
  158.8 20.8 %copy-start.23 = (bf16[192,256]{1,0:T(8,128)(2,1)S(1)}, bf16[192,256]{1,0:T(8,128)(2,1)}, u32[]{:S(2)}) copy-start(bf16[192,256]{1,0:T(8,128)(2,1)} %copy-done.22) | copy-start | bytes 294916
  158.8 22.0 %all-to-all-start.4 = ((bf16[16,144,256]{2,1,0:T(8,128)(2,1)}), bf16[16,144,256]{2,1,0:T(8,128)(2,1)S(1)}, u32[]{:S(2)}, u32[]{:S(2)}) async-start(bf16[16,144,256]{2,1,0:T(8,128)(2,1)} %get-tuple-element.107), calls=%async_computation.4 | async-start | bytes 2359296 | tf_op jit(solution)/shard_map/all_to_all | solution.py:706
  162.7 16.9 %collective-permute-start.23 = (bf16[48,256]{1,0:T(8,128)(2,1)S(1)}, bf16[48,256]{1,0:T(8,128)(2,1)S(1)}, u32[]{:S(2)}, u32[]{:S(2)}) collective-permute-start(bf16[48,256]{1,0:T(8,128)(2,1)S(1)} %get-tuple-element.110), channel_id=1, source_target_pairs={{0,7},{1,6},{2,5},{3,4},{4,3},{5,2},{6,1},{7,0},{8,15},{9,14},{10,... | collective-permute-start | bytes 73736 | tf_op jit(solution)/shard_map/ppermute | solution.py:703
  180.8 4.9 %collective-permute-start.24 = (bf16[16,144,256]{2,1,0:T(8,128)(2,1)S(1)}, bf16[16,144,256]{2,1,0:T(8,128)(2,1)S(1)}, u32[]{:S(2)}, u32[]{:S(2)}) collective-permute-start(bf16[16,144,256]{2,1,0:T(8,128)(2,1)S(1)} %all-to-all-done.4.refs_1_), channel_id=1, source_target_pairs={{0,1},{1,0},{2,3},{3,2},{4,5},{5,4},{6,7},{7,6},{8,9},{9,8},{10,11... | collective-permute-start | bytes 3538952 | tf_op jit(solution)/shard_map/ppermute | solution.py:709
  (7 other events, 5.6 us)

commit v18 on v17

--- a/solution.py
+++ b/solution.py
@@ -306,12 +306,18 @@
     post_ends(row, col, cells, first, second, ends)
 
 
-def back_kernel(pos, wide, first, second, taps, back, cells, shifts):
-    stack_lines(pos[0], wide, first, second, cells)
+def back_kernel(pos, wide, first, second, pre, add, taps, back, slope, handed, cells, shifts):
+    row, col = pos[0], pos[1]
+    stack_lines(row, wide, first, second, cells)
     back[...] = convolve(cells, shifts, 12, 10, 0, taps, True).astype(BF16)
-
-
-def delta_kernel(pos, back, got, pick, pre, taps, wide_delta, own, send, cells, grads, shifts, strips, lines):
+    inside = cell_mask(row, col)
+    for f in range(3):
+        where = slice(f * 10 * PITCH, (f + 1) * 10 * PITCH)
+        slope[where, :] = jnp.where(inside, slope_of(pre[where, :]), 0.0)
+    handed[...] = add[...]
+
+
+def delta_kernel(pos, back, got, pick, slope, taps, wide_delta, own, send, cells, grads, shifts, strips, lines):
     row, col = pos[0], pos[1]
     lines[...] = dot(pick[...], got[...], ((1,), (0,)))
     grads[...] = back[...].astype(F32)
@@ -333,10 +339,9 @@
                     grads[where, :] = grads[where, :] + lines[(2 * f + 1) * 10 + i : (2 * f + 1) * 10 + i + 1, :]
 
     cells[...] = jnp.zeros_like(cells)
-    inside = cell_mask(row, col)
     for f in range(3):
         where = slice(f * 10 * PITCH, (f + 1) * 10 * PITCH)
-        value = jnp.where(inside, grads[where, :] * slope_of(pre[where, :]), 0.0)
+        value = grads[where, :] * slope[where, :]
         at = (f * 12 + 1) * PITCH + 1
         cells[at : at + 10 * PITCH, :] = value.astype(BF16).astype(F32)
     at = lax.broadcasted_iota(jnp.int32, (8 * PITCH, C), 0) % PITCH
@@ -652,17 +657,19 @@
     packed_other = lax.ppermute(packed, "core", CORES)
     grad_two = run(grad_two_kernel, [(piece, BF16)], halves(10) + [(piece, F32)], pos, packed, packed_other)[0]
     grad_two, wide = lax.optimization_barrier((grad_two, wide))
-    back = run(
+    back, slope, add_10 = run(
         back_kernel,
-        [((30 * PITCH, C), BF16)],
+        [((30 * PITCH, C), BF16), ((30 * PITCH, C), F32), ((64, 1024), BF16)],
         [((spare, C), F32), ((flat, C), BF16)],
         pos,
         wide,
         first,
         second,
+        pre_one,
+        add_10,
         kernel_two,
-    )[0]
-    got, back = lax.optimization_barrier((got, back))
+    )
+    got, back, slope, add_10 = lax.optimization_barrier((got, back, slope, add_10))
     wide_one, own, strips = run(
         delta_kernel,
         [((24 * PITCH, C), BF16), ((192, C), BF16), ((48, C), BF16)],
@@ -671,7 +678,7 @@
         back,
         got,
         add_10,
-        pre_one,
+        slope,
         kernel_one,
     )
     wide_other = lax.ppermute(wide_one, "core", CORES)

time: 189 us -> 192 us (1.016)
  starting transfers between devices: 66.4 us -> 70.7 us
  waiting for transfers between devices: 56.3 us -> 52.1 us
  local copies, waits for them, and re-layouts: 9.97 us -> 12.3 us
    all_to_all x2, waiting for transfers between devices: 15 us -> 12.5 us  [seam_exchange(): got = lax.all_to_all(send, AXES, 0, 0, axis_index_groups=SEAM_GROUPS)]
    all_to_all x2, starting transfers between devices: 8.64 us -> 11.2 us  [body(): part = lax.all_to_all(part, AXES, 0, 0, axis_index_groups=PLANE_GROUPS)]
    unnamed x52 -> x60, local copies, waits for them, and re-layouts: 8.61 us -> 11 us
where the time goes in v18:
time: 192 us; the launch traced here: 191 us
  starting transfers between devices  70.7 us (37%)
  waiting for transfers between devices  52.1 us (27%)
  Pallas kernels  28.5 us (15%)
  blocking collectives  25.6 us (13%)
  local copies, waits for them, and re-layouts  12.3 us (6%)
    all_to_all x1, blocking collectives, seam_exchange(): got = lax.all_to_all(send, AXES, 0, 0, axis_index_groups=SEAM_GROUPS)  25.6 us
    pallas_call x17, Pallas kernels, run(): pl.pallas_call(kernel, out_shape=[jax.ShapeDtypeStruct(shape, dtype) for...  21.7 us
    all_to_all x2, starting transfers between devices, seam_exchange(): got = lax.all_to_all(send, AXES, 0, 0, axis_index_groups=SEAM_GROUPS)  20.1 us
    all_to_all x2, waiting for transfers between devices, seam_exchange(): got = lax.all_to_all(send, AXES, 0, 0, axis_index_groups=SEAM_GROUPS)  12.5 us
    all_to_all x2, starting transfers between devices, body(): part = lax.all_to_all(part, AXES, 0, 0, axis_index_groups=PLANE_GROUPS)  11.2 us
    unnamed x60, local copies, waits for them, and re-layouts  11 us
    all_to_all x2, waiting for transfers between devices, body(): part = lax.all_to_all(part, AXES, 0, 0, axis_index_groups=PLANE_GROUPS)  9.41 us
    ppermute x1, starting transfers between devices, body(): onward = lax.ppermute(onward, TILE, [(t, t ^ 7) for t in range(64)])  8.34 us
  transfers between devices with their start and end apart: 29, of which 15 were waited for; matrix products, arithmetic and copies ran while one was open for 1% of the time, Pallas kernels for 7%

profile of v18, /device:TPU:1, one launch (start us, length us, event | category | flops | bytes accessed | tf_op | source)
XLA Modules:
  0.0 190.5 jit_solution(17397363155482421608)
XLA Ops:
  0.7 1.0 copy-done.8
  1.7 1.3 shard_map.85
  3.0 14.3 %all-to-all-start = ((bf16[16,48,256]{2,1,0:T(8,128)(2,1)}), bf16[16,48,256]{2,1,0:T(8,128)(2,1)S(1)}, u32[]{:S(2)}, u32[]{:S(2)}) async-start(bf16[16,48,256]{2,1,0:T(8,128)(2,1)} %shard_map.85), calls=%async_computation | async-start | bytes 786432 | tf_op jit(solution)/shard_map/all_to_all | solution.py:483
  17.4 1.9 %collective-permute-start.1 = (bf16[192,256]{1,0:T(8,128)(2,1)S(1)}, bf16[192,256]{1,0:T(8,128)(2,1)S(1)}, u32[]{:S(2)}, u32[]{:S(2)}) collective-permute-start(bf16[192,256]{1,0:T(8,128)(2,1)S(1)} %bitcast.18), channel_id=1, source_target_pairs={{1,2},{3,4},{5,6},{9,10},{11,12},{13,14},{17,18},{19,20},{21,22},{... | collective-permute-start | bytes 294920 | tf_op jit(solution)/shard_map/ppermute | solution.py:607
  19.4 4.2 %collective-permute-done.1.odd = bf16[192,256]{1,0:T(8,128)(2,1)S(1)} collective-permute-done((bf16[192,256]{1,0:T(8,128)(2,1)S(1)}, bf16[192,256]{1,0:T(8,128)(2,1)S(1)}, u32[]{:S(2)}, u32[]{:S(2)}) %collective-permute-start.1) | collective-permute-done | bytes 98336 | tf_op jit(solution)/shard_map/ppermute | solution.py:607
  26.5 2.6 %shard_map.87 = (bf16[80,768]{1,0:T(8,128)(2,1)}, bf16[64,1024]{1,0:T(8,128)(2,1)}, bf16[64,1024]{1,0:T(8,128)(2,1)}, bf16[192,256]{1,0:T(8,128)(2,1)}) custom-call(s32[4]{0:T(128)} %copy-done.14, s32[12,4]{1,0:T(8,128)} %copy.11.nexts, s32[12,4]{1,0:T(8,128)} %copy.12.codes), custom_call_target="tpu_custom_call" | custom-call | tf_op jit(solution)/shard_map/pallas_call | solution.py:574
  29.1 4.9 %all-to-all-done = bf16[16,48,256]{2,1,0:T(8,128)(2,1)S(1)} async-done(((bf16[16,48,256]{2,1,0:T(8,128)(2,1)}), bf16[16,48,256]{2,1,0:T(8,128)(2,1)S(1)}, u32[]{:S(2)}, u32[]{:S(2)}) %all-to-all-start) | async-done | bytes 393248 | tf_op jit(solution)/shard_map/all_to_all | solution.py:483
  36.4 1.9 %collective-permute-start.5 = (bf16[16,256]{1,0:T(8,128)(2,1)S(1)}, bf16[16,256]{1,0:T(8,128)(2,1)S(1)}, u32[]{:S(2)}, u32[]{:S(2)}) collective-permute-start(bf16[16,256]{1,0:T(8,128)(2,1)S(1)} %get-tuple-element.79), channel_id=1, source_target_pairs={{1,2},{3,4},{5,6},{9,10},{11,12},{13,14},{17,18},{19,20},{21,22},{... | collective-permute-start | bytes 24584 | tf_op jit(solution)/shard_map/ppermute | solution.py:614
  39.1 2.3 %collective-permute-done.5.odd_ends = bf16[16,256]{1,0:T(8,128)(2,1)S(1)} collective-permute-done((bf16[16,256]{1,0:T(8,128)(2,1)S(1)}, bf16[16,256]{1,0:T(8,128)(2,1)S(1)}, u32[]{:S(2)}, u32[]{:S(2)}) %collective-permute-start.5) | collective-permute-done | bytes 8224 | tf_op jit(solution)/shard_map/ppermute | solution.py:614
  41.4 1.5 shard_map.89
  43.8 25.6 %all_to_all.25 = bf16[16,64,256]{2,1,0:T(8,128)(2,1)S(1)} all-to-all(bf16[16,64,256]{2,1,0:T(8,128)(2,1)S(1)} %get-tuple-element.84), channel_id=1, replica_groups={{0,7,56,63,64,71,120,127,128,135,184,191,192,199,248,255},{1,6,57,62,65..., dimensions={0} | all-to-all | bytes 1048576 | tf_op jit(solution)/shard_map/all_to_all | solution.py:483
  69.3 1.6 shard_map.90
  71.0 2.0 %collective-permute-start.10 = (bf16[192,256]{1,0:T(8,128)(2,1)S(1)}, bf16[192,256]{1,0:T(8,128)(2,1)S(1)}, u32[]{:S(2)}, u32[]{:S(2)}) collective-permute-start(bf16[192,256]{1,0:T(8,128)(2,1)S(1)} %get-tuple-element.86.own), channel_id=1, source_target_pairs={{1,2},{3,4},{5,6},{9,10},{11,12},{13,14},{17,18},{19,20},{21,22},{... | collective-permute-start | bytes 294920 | tf_op jit(solution)/shard_map/ppermute | solution.py:597
  73.9 1.8 collective-permute-done.11.end_one
  75.7 1.2 collective-permute-done.10.odd
  76.9 1.8 shard_map.91
  79.4 5.7 %all-to-all-start.2 = ((bf16[16,64,256]{2,1,0:T(8,128)(2,1)}), bf16[16,64,256]{2,1,0:T(8,128)(2,1)S(1)}, u32[]{:S(2)}, u32[]{:S(2)}) async-start(bf16[16,64,256]{2,1,0:T(8,128)(2,1)} %get-tuple-element.89), calls=%async_computation.2 | async-start | bytes 1048576 | tf_op jit(solution)/shard_map/all_to_all | solution.py:483
  85.7 3.2 %collective-permute-start.14 = (bf16[96,256]{1,0:T(8,128)(2,1)}, bf16[96,256]{1,0:T(8,128)(2,1)S(1)}, u32[]{:S(2)}, u32[]{:S(2)}) collective-permute-start(bf16[96,256]{1,0:T(8,128)(2,1)} %get-tuple-element.93), channel_id=1, source_target_pairs={{0,8},{1,9},{2,10},{3,11},{4,12},{5,13},{6,14},{7,15},{16,24},{17,... | collective-permute-start | bytes 147464 | tf_op jit(solution)/shard_map/ppermute | solution.py:651
  89.7 1.0 copy-done.7
  90.7 1.4 shard_map.92.two
  93.1 1.5 shard_map.93
  96.7 7.6 %all-to-all-done.2 = bf16[16,64,256]{2,1,0:T(8,128)(2,1)S(1)} async-done(((bf16[16,64,256]{2,1,0:T(8,128)(2,1)}), bf16[16,64,256]{2,1,0:T(8,128)(2,1)S(1)}, u32[]{:S(2)}, u32[]{:S(2)}) %all-to-all-start.2) | async-done | bytes 524320 | tf_op jit(solution)/shard_map/all_to_all | solution.py:483
  104.3 1.0 copy-done.5
  105.3 0.9 copy-done.13
  106.3 0.9 copy-done.22
  107.2 1.9 %shard_map.94 = (bf16[384,256]{1,0:T(8,128)(2,1)S(1)}, bf16[192,256]{1,0:T(8,128)(2,1)S(1)}, bf16[48,256]{1,0:T(8,128)(2,1)S(1)}) custom-call(s32[4]{0:T(128)S(1)} %copy-done.16, bf16[480,256]{1,0:T(8,128)(2,1)S(1)} %copy-done.13, bf16[1024,256]{1,0:T(8,128)(2,1)S(1)} %bitcast.15, bf16[64,1024]{1,0:T(8,128)(2,1)S(1)} %copy-done.22, ...), custom_call_target="tpu_custom_call" | custom-call | tf_op jit(solution)/shard_map/pallas_call | solution.py:58
  109.3 1.1 shard_map.95.part
  110.7 2.5 %shard_map.96 = bf16[16,144,256]{2,1,0:T(8,128)(2,1)} custom-call(s32[4]{0:T(128)S(1)} %copy-done.16, bf16[576,256]{1,0:T(8,128)(2,1)} %collective-permute-done.8.source, bf16[384,256]{1,0:T(8,128)(2,1)S(1)} %collective-permute-done.16.delta, f32[16,72,256]{2,1,0:T(8,128)S(1)} %shard_map.95.part, bf16[16,72,256]{2,1,0:T(8,128)(2,1)S(1)} %shard_map.92.two), custom_call_target="tpu_custom_call" | custom-call | tf_op jit(solution)/shard_map/pallas_call | solution.py:58
  113.2 7.4 %all-to-all-start.3 = ((bf16[16,144,256]{2,1,0:T(8,128)(2,1)}), bf16[16,144,256]{2,1,0:T(8,128)(2,1)S(1)}, u32[]{:S(2)}, u32[]{:S(2)}) async-start(bf16[16,144,256]{2,1,0:T(8,128)(2,1)} %shard_map.96), calls=%async_computation.3 | async-start | bytes 2359296 | tf_op jit(solution)/shard_map/all_to_all | solution.py:698
  120.6 2.1 %collective-permute-start.19 = (bf16[48,256]{1,0:T(8,128)(2,1)S(1)}, bf16[48,256]{1,0:T(8,128)(2,1)S(1)}, u32[]{:S(2)}, u32[]{:S(2)}) collective-permute-start(bf16[48,256]{1,0:T(8,128)(2,1)S(1)} %get-tuple-element.108.one), channel_id=1, source_target_pairs={{0,192},{64,0},{128,64},{192,128},{1,193},{65,1},{129,65},{193,129... | collective-permute-start | bytes 73736 | tf_op jit(solution)/shard_map/ppermute | solution.py:697
  122.7 1.2 collective-permute-start.18
  124.7 2.3 %collective-permute-done.18.three = bf16[48,256]{1,0:T(8,128)(2,1)S(1)} collective-permute-done((bf16[48,256]{1,0:T(8,128)(2,1)S(1)}, bf16[48,256]{1,0:T(8,128)(2,1)S(1)}, u32[]{:S(2)}, u32[]{:S(2)}) %collective-permute-start.18) | collective-permute-done | bytes 24608 | tf_op jit(solution)/shard_map/ppermute | solution.py:697
  126.9 1.7 collective-permute-done.17.two
  129.4 9.4 %all-to-all-done.3.parts = bf16[16,144,256]{2,1,0:T(8,128)(2,1)S(1)} async-done(((bf16[16,144,256]{2,1,0:T(8,128)(2,1)}), bf16[16,144,256]{2,1,0:T(8,128)(2,1)S(1)}, u32[]{:S(2)}, u32[]{:S(2)}) %all-to-all-start.3) | async-done | bytes 1179680 | tf_op jit(solution)/shard_map/all_to_all | solution.py:698
  139.5 2.1 %collective-permute-start.20 = (bf16[144,256]{1,0:T(8,128)(2,1)S(1)}, bf16[144,256]{1,0:T(8,128)(2,1)S(1)}, u32[]{:S(2)}, u32[]{:S(2)}) collective-permute-start(bf16[144,256]{1,0:T(8,128)(2,1)S(1)} %shard_map.98.one), channel_id=1, source_target_pairs={{0,64},{64,0},{128,192},{192,128},{1,65},{65,1},{129,193},{193,129... | collective-permute-start | bytes 221192 | tf_op jit(solution)/shard_map/ppermute | solution.py:703
  141.7 1.7 collective-permute-done.20.two
  144.0 2.1 %collective-permute-start.21 = (bf16[144,256]{1,0:T(8,128)(2,1)S(1)}, bf16[144,256]{1,0:T(8,128)(2,1)S(1)}, u32[]{:S(2)}, u32[]{:S(2)}) collective-permute-start(bf16[144,256]{1,0:T(8,128)(2,1)S(1)} %shard_map.99.one), channel_id=1, source_target_pairs={{0,128},{64,192},{128,0},{192,64},{1,129},{65,193},{129,1},{193,65... | collective-permute-start | bytes 221192 | tf_op jit(solution)/shard_map/ppermute | solution.py:705
  146.1 2.1 %collective-permute-done.21.two = bf16[144,256]{1,0:T(8,128)(2,1)S(1)} collective-permute-done((bf16[144,256]{1,0:T(8,128)(2,1)S(1)}, bf16[144,256]{1,0:T(8,128)(2,1)S(1)}, u32[]{:S(2)}, u32[]{:S(2)}) %collective-permute-start.21) | collective-permute-done | bytes 73760 | tf_op jit(solution)/shard_map/ppermute | solution.py:705
  148.7 5.7 %collective-permute-start.22 = (bf16[240,256]{1,0:T(8,128)(2,1)S(1)}, bf16[240,256]{1,0:T(8,128)(2,1)S(1)}, u32[]{:S(2)}, u32[]{:S(2)}) collective-permute-start(bf16[240,256]{1,0:T(8,128)(2,1)S(1)} %shard_map.100.one), channel_id=1, source_target_pairs={{0,56},{1,57},{2,58},{3,59},{4,60},{5,61},{6,62},{7,63},{8,48},{9,... | collective-permute-start | bytes 368648 | tf_op jit(solution)/shard_map/ppermute | solution.py:707
  154.4 5.2 %collective-permute-done.22.two = bf16[240,256]{1,0:T(8,128)(2,1)S(1)} collective-permute-done((bf16[240,256]{1,0:T(8,128)(2,1)S(1)}, bf16[240,256]{1,0:T(8,128)(2,1)S(1)}, u32[]{:S(2)}, u32[]{:S(2)}) %collective-permute-start.22) | collective-permute-done | bytes 122912 | tf_op jit(solution)/shard_map/ppermute | solution.py:707
  159.6 1.6 shard_map.101
  161.2 3.8 %all-to-all-start.4 = ((bf16[16,144,256]{2,1,0:T(8,128)(2,1)}), bf16[16,144,256]{2,1,0:T(8,128)(2,1)S(1)}, u32[]{:S(2)}, u32[]{:S(2)}) async-start(bf16[16,144,256]{2,1,0:T(8,128)(2,1)} %get-tuple-element.117), calls=%async_computation.4 | async-start | bytes 2359296 | tf_op jit(solution)/shard_map/all_to_all | solution.py:713
  165.1 8.3 %collective-permute-start.23 = (bf16[48,256]{1,0:T(8,128)(2,1)S(1)}, bf16[48,256]{1,0:T(8,128)(2,1)S(1)}, u32[]{:S(2)}, u32[]{:S(2)}) collective-permute-start(bf16[48,256]{1,0:T(8,128)(2,1)S(1)} %get-tuple-element.120), channel_id=1, source_target_pairs={{0,7},{1,6},{2,5},{3,4},{4,3},{5,2},{6,1},{7,0},{8,15},{9,14},{10,... | collective-permute-start | bytes 73736 | tf_op jit(solution)/shard_map/ppermute | solution.py:710
  173.4 7.0 %collective-permute-done.23.by_col = bf16[48,256]{1,0:T(8,128)(2,1)S(1)} collective-permute-done((bf16[48,256]{1,0:T(8,128)(2,1)S(1)}, bf16[48,256]{1,0:T(8,128)(2,1)S(1)}, u32[]{:S(2)}, u32[]{:S(2)}) %collective-permute-start.23) | collective-permute-done | bytes 24608 | tf_op jit(solution)/shard_map/ppermute | solution.py:710
  180.4 1.3 shard_map.102
  181.7 4.1 %collective-permute-start.24 = (bf16[16,144,256]{2,1,0:T(8,128)(2,1)S(1)}, bf16[16,144,256]{2,1,0:T(8,128)(2,1)S(1)}, u32[]{:S(2)}, u32[]{:S(2)}) collective-permute-start(bf16[16,144,256]{2,1,0:T(8,128)(2,1)S(1)} %all-to-all-done.4.refs_1_), channel_id=1, source_target_pairs={{0,1},{1,0},{2,3},{3,2},{4,5},{5,4},{6,7},{7,6},{8,9},{9,8},{10,11... | collective-permute-start | bytes 3538952 | tf_op jit(solution)/shard_map/ppermute | solution.py:716
  185.8 2.1 %shard_map.103 = (f32[9,256,256]{2,1,0:T(8,128)}, f32[9,256,256]{2,1,0:T(8,128)}) custom-call(s32[4]{0:T(128)S(1)} %copy-done.16, bf16[16,144,256]{2,1,0:T(8,128)(2,1)S(1)} %all-to-all-done.4.refs_1_), custom_call_target="tpu_custom_call" | custom-call | tf_op jit(solution)/shard_map/pallas_call | solution.py:471
  188.2 2.1 %shard_map.104 = (f32[9,256,256]{2,1,0:T(8,128)}, f32[9,256,256]{2,1,0:T(8,128)}) custom-call(s32[4]{0:T(128)S(1)} %copy-done.16, bf16[16,144,256]{2,1,0:T(8,128)(2,1)S(1)} %collective-permute-done.24.refs_1_, f32[9,256,256]{2,1,0:T(8,128)} %get-tuple-element.123.refs_2_, ...), custom_call_target="tpu_custom_call", output_to_operand_aliasing={{0}: (2, {}), {1}: (3, {})} | custom-call | tf_op jit(solution)/shard_map/pallas_call | solution.py:471
  (94 shorter events, 16.8 us)
Async XLA Ops:
  0.6 40.8 %copy-start.1 = (bf16[3,3,256,256]{3,2,1,0:T(8,128)(2,1)S(1)}, bf16[3,3,256,256]{3,2,1,0:T(8,128)(2,1)}, u32[]{:S(2)}) copy-start(bf16[3,3,256,256]{3,2,1,0:T(8,128)(2,1)} %taps.9) | copy-start | bytes 3538948
  0.7 25.7 %copy-start.14 = (s32[4]{0:T(128)}, s32[4]{0:T(128)S(1)}, u32[]{:S(2)}) copy-start(s32[4]{0:T(128)S(1)} %pad_add_fusion.pos.refs_0_) | copy-start | bytes 52
  1.7 15.7 %copy-start.9 = (bf16[3,1,8,8,256]{4,3,2,1,0:T(8,128)(2,1)S(1)}, bf16[3,1,8,8,256]{4,3,2,1,0:T(8,128)(2,1)}, u32[]{:S(2)}) copy-start(bf16[3,1,8,8,256]{4,3,2,1,0:T(8,128)(2,1)} %param.6) | copy-start | bytes 294916
  1.7 23.4 %copy-start.28 = (s32[12,4]{0,1:T(4,128)S(1)}, s32[12,4]{0,1:T(4,128)}, u32[]{:S(2)}) copy-start(s32[12,4]{0,1:T(4,128)} %param.10) | copy-start | bytes 580
  1.7 24.1 %copy-start.29 = (s32[12,4]{0,1:T(4,128)S(1)}, s32[12,4]{0,1:T(4,128)}, u32[]{:S(2)}) copy-start(s32[12,4]{0,1:T(4,128)} %param.11) | copy-start | bytes 580
  3.0 30.9 %all-to-all-start = ((bf16[16,48,256]{2,1,0:T(8,128)(2,1)}), bf16[16,48,256]{2,1,0:T(8,128)(2,1)S(1)}, u32[]{:S(2)}, u32[]{:S(2)}) async-start(bf16[16,48,256]{2,1,0:T(8,128)(2,1)} %shard_map.85), calls=%async_computation | async-start | bytes 786432 | tf_op jit(solution)/shard_map/all_to_all | solution.py:483
  17.4 6.2 %collective-permute-start.1 = (bf16[192,256]{1,0:T(8,128)(2,1)S(1)}, bf16[192,256]{1,0:T(8,128)(2,1)S(1)}, u32[]{:S(2)}, u32[]{:S(2)}) collective-permute-start(bf16[192,256]{1,0:T(8,128)(2,1)S(1)} %bitcast.18), channel_id=1, source_target_pairs={{1,2},{3,4},{5,6},{9,10},{11,12},{13,14},{17,18},{19,20},{21,22},{... | collective-permute-start | bytes 294920 | tf_op jit(solution)/shard_map/ppermute | solution.py:607
  19.3 4.3 %collective-permute-start = (bf16[192,256]{1,0:T(8,128)(2,1)S(1)}, bf16[192,256]{1,0:T(8,128)(2,1)S(1)}, u32[]{:S(2)}, u32[]{:S(2)}) collective-permute-start(bf16[192,256]{1,0:T(8,128)(2,1)S(1)} %bitcast.19), channel_id=1, source_target_pairs={{0,1},{1,0},{2,3},{3,2},{4,5},{5,4},{6,7},{7,6},{8,9},{9,8},{10,11... | collective-permute-start | bytes 294920 | tf_op jit(solution)/shard_map/ppermute | solution.py:607
  24.3 4.8 %collective-permute-start.2 = (bf16[96,256]{1,0:T(8,128)(2,1)S(1)}, bf16[96,256]{1,0:T(8,128)(2,1)S(1)}, u32[]{:S(2)}, u32[]{:S(2)}) collective-permute-start(bf16[96,256]{1,0:T(8,128)(2,1)S(1)} %get-tuple-element.68), channel_id=1, source_target_pairs={{0,8},{1,9},{2,10},{3,11},{4,12},{5,13},{6,14},{7,15},{16,24},{17,... | collective-permute-start | bytes 147464 | tf_op jit(solution)/shard_map/ppermute | solution.py:609
  24.4 4.7 %collective-permute-start.3 = (bf16[96,256]{1,0:T(8,128)(2,1)S(1)}, bf16[96,256]{1,0:T(8,128)(2,1)S(1)}, u32[]{:S(2)}, u32[]{:S(2)}) collective-permute-start(bf16[96,256]{1,0:T(8,128)(2,1)S(1)} %get-tuple-element.69), channel_id=1, source_target_pairs={{8,16},{9,17},{10,18},{11,19},{12,20},{13,21},{14,22},{15,23},{24,... | collective-permute-start | bytes 147464 | tf_op jit(solution)/shard_map/ppermute | solution.py:609
  36.3 2.8 %collective-permute-start.4 = (bf16[16,256]{1,0:T(8,128)(2,1)S(1)}, bf16[16,256]{1,0:T(8,128)(2,1)S(1)}, u32[]{:S(2)}, u32[]{:S(2)}) collective-permute-start(bf16[16,256]{1,0:T(8,128)(2,1)S(1)} %get-tuple-element.78), channel_id=1, source_target_pairs={{0,1},{1,0},{2,3},{3,2},{4,5},{5,4},{6,7},{7,6},{8,9},{9,8},{10,11... | collective-permute-start | bytes 24584 | tf_op jit(solution)/shard_map/ppermute | solution.py:613
  36.4 5.0 %collective-permute-start.5 = (bf16[16,256]{1,0:T(8,128)(2,1)S(1)}, bf16[16,256]{1,0:T(8,128)(2,1)S(1)}, u32[]{:S(2)}, u32[]{:S(2)}) collective-permute-start(bf16[16,256]{1,0:T(8,128)(2,1)S(1)} %get-tuple-element.79), channel_id=1, source_target_pairs={{1,2},{3,4},{5,6},{9,10},{11,12},{13,14},{17,18},{19,20},{21,22},{... | collective-permute-start | bytes 24584 | tf_op jit(solution)/shard_map/ppermute | solution.py:614
  38.4 3.0 %collective-permute-start.6 = (bf16[16,256]{1,0:T(8,128)(2,1)S(1)}, bf16[16,256]{1,0:T(8,128)(2,1)S(1)}, u32[]{:S(2)}, u32[]{:S(2)}) collective-permute-start(bf16[16,256]{1,0:T(8,128)(2,1)S(1)} %get-tuple-element.80), channel_id=1, source_target_pairs={{0,8},{1,9},{2,10},{3,11},{4,12},{5,13},{6,14},{7,15},{16,24},{17,... | collective-permute-start | bytes 24584 | tf_op jit(solution)/shard_map/ppermute | solution.py:615
  38.5 2.9 %collective-permute-start.7 = (bf16[16,256]{1,0:T(8,128)(2,1)S(1)}, bf16[16,256]{1,0:T(8,128)(2,1)S(1)}, u32[]{:S(2)}, u32[]{:S(2)}) collective-permute-start(bf16[16,256]{1,0:T(8,128)(2,1)S(1)} %get-tuple-element.81), channel_id=1, source_target_pairs={{8,16},{9,17},{10,18},{11,19},{12,20},{13,21},{14,22},{15,23},{40,... | collective-permute-start | bytes 24584 | tf_op jit(solution)/shard_map/ppermute | solution.py:616
  41.4 27.9 %copy-start = (bf16[3,3,256,256]{3,2,1,0:T(8,128)(2,1)S(1)}, bf16[3,3,256,256]{3,2,1,0:T(8,128)(2,1)}, u32[]{:S(2)}) copy-start(bf16[3,3,256,256]{3,2,1,0:T(8,128)(2,1)} %taps.8) | copy-start | bytes 3538948
  41.4 27.9 %copy-start.20 = (bf16[64,1024]{1,0:T(8,128)(2,1)S(1)}, bf16[64,1024]{1,0:T(8,128)(2,1)}, u32[]{:S(2)}) copy-start(bf16[64,1024]{1,0:T(8,128)(2,1)} %get-tuple-element.85.pick) | copy-start | bytes 393220
  41.4 27.9 %copy-start.24 = (bf16[3,1,8,8,256]{4,3,2,1,0:T(8,128)(2,1)S(1)}, bf16[3,1,8,8,256]{4,3,2,1,0:T(8,128)(2,1)}, u32[]{:S(2)}) copy-start(bf16[3,1,8,8,256]{4,3,2,1,0:T(8,128)(2,1)} %param.7) | copy-start | bytes 294916
  43.8 27.2 %copy-start.10 = (bf16[576,256]{1,0:T(8,128)(2,1)}, bf16[576,256]{1,0:T(8,128)(2,1)S(1)}, u32[]{:S(2)}) copy-start(bf16[576,256]{1,0:T(8,128)(2,1)S(1)} %get-tuple-element.82.source) | copy-start | bytes 884740
  71.0 14.2 %copy-start.6 = (bf16[864,256]{1,0:T(8,128)(2,1)}, bf16[864,256]{1,0:T(8,128)(2,1)S(1)}, u32[]{:S(2)}) copy-start(bf16[864,256]{1,0:T(8,128)(2,1)S(1)} %get-tuple-element.90.own) | copy-start | bytes 1327108
  71.0 5.9 %collective-permute-start.10 = (bf16[192,256]{1,0:T(8,128)(2,1)S(1)}, bf16[192,256]{1,0:T(8,128)(2,1)S(1)}, u32[]{:S(2)}, u32[]{:S(2)}) collective-permute-start(bf16[192,256]{1,0:T(8,128)(2,1)S(1)} %get-tuple-element.86.own), channel_id=1, source_target_pairs={{1,2},{3,4},{5,6},{9,10},{11,12},{13,14},{17,18},{19,20},{21,22},{... | collective-permute-start | bytes 294920 | tf_op jit(solution)/shard_map/ppermute | solution.py:597
  73.0 3.9 %collective-permute-start.9 = (bf16[192,256]{1,0:T(8,128)(2,1)S(1)}, bf16[192,256]{1,0:T(8,128)(2,1)S(1)}, u32[]{:S(2)}, u32[]{:S(2)}) collective-permute-start(bf16[192,256]{1,0:T(8,128)(2,1)S(1)} %get-tuple-element.86.own), channel_id=1, source_target_pairs={{0,1},{1,0},{2,3},{3,2},{4,5},{5,4},{6,7},{7,6},{8,9},{9,8},{10,11... | collective-permute-start | bytes 294920 | tf_op jit(solution)/shard_map/ppermute | solution.py:596
  73.1 2.6 %collective-permute-start.11 = (bf16[16,256]{1,0:T(8,128)(2,1)S(1)}, bf16[16,256]{1,0:T(8,128)(2,1)S(1)}, u32[]{:S(2)}, u32[]{:S(2)}) collective-permute-start(bf16[16,256]{1,0:T(8,128)(2,1)S(1)} %get-tuple-element.87), channel_id=1, source_target_pairs={{0,8},{1,9},{2,10},{3,11},{4,12},{5,13},{6,14},{7,15},{16,24},{17,... | collective-permute-start | bytes 24584 | tf_op jit(solution)/shard_map/ppermute | solution.py:598
  73.2 16.5 %copy-start.16 = (s32[4]{0:T(128)S(1)}, s32[4]{0:T(128)}, u32[]{:S(2)}) copy-start(s32[4]{0:T(128)} %copy-done.14) | copy-start | bytes 52
  73.2 2.5 %collective-permute-start.12 = (bf16[16,256]{1,0:T(8,128)(2,1)S(1)}, bf16[16,256]{1,0:T(8,128)(2,1)S(1)}, u32[]{:S(2)}, u32[]{:S(2)}) collective-permute-start(bf16[16,256]{1,0:T(8,128)(2,1)S(1)} %get-tuple-element.88), channel_id=1, source_target_pairs={{8,16},{9,17},{10,18},{11,19},{12,20},{13,21},{14,22},{15,23},{40,... | collective-permute-start | bytes 24584 | tf_op jit(solution)/shard_map/ppermute | solution.py:599
  79.4 24.9 %all-to-all-start.2 = ((bf16[16,64,256]{2,1,0:T(8,128)(2,1)}), bf16[16,64,256]{2,1,0:T(8,128)(2,1)S(1)}, u32[]{:S(2)}, u32[]{:S(2)}) async-start(bf16[16,64,256]{2,1,0:T(8,128)(2,1)} %get-tuple-element.89), calls=%async_computation.2 | async-start | bytes 1048576 | tf_op jit(solution)/shard_map/all_to_all | solution.py:483
  85.1 7.0 %copy-start.3 = (f32[480,256]{1,0:T(8,128)S(1)}, f32[480,256]{1,0:T(8,128)}, u32[]{:S(2)}) copy-start(f32[480,256]{1,0:T(8,128)} %copy-done.2) | copy-start | bytes 1474564
  85.1 4.5 %collective-permute-start.13 = (bf16[864,256]{1,0:T(8,128)(2,1)S(1)}, bf16[864,256]{1,0:T(8,128)(2,1)S(1)}, u32[]{:S(2)}, u32[]{:S(2)}) collective-permute-start(bf16[864,256]{1,0:T(8,128)(2,1)S(1)} %get-tuple-element.90.own), channel_id=1, source_target_pairs={{0,1},{1,0},{2,3},{3,2},{4,5},{5,4},{6,7},{7,6},{8,9},{9,8},{10,11... | collective-permute-start | bytes 1327112 | tf_op jit(solution)/shard_map/ppermute | solution.py:657
  85.2 25.1 %collective-permute-start.8 = (bf16[576,256]{1,0:T(8,128)(2,1)}, bf16[576,256]{1,0:T(8,128)(2,1)}, u32[]{:S(2)}, u32[]{:S(2)}) collective-permute-start(bf16[576,256]{1,0:T(8,128)(2,1)} %copy-done.10), channel_id=1, source_target_pairs={{0,1},{1,0},{2,3},{3,2},{4,5},{5,4},{6,7},{7,6},{8,9},{9,8},{10,11... | collective-permute-start | bytes 884744 | tf_op jit(solution)/shard_map/ppermute | solution.py:630
  85.7 6.4 %collective-permute-start.14 = (bf16[96,256]{1,0:T(8,128)(2,1)}, bf16[96,256]{1,0:T(8,128)(2,1)S(1)}, u32[]{:S(2)}, u32[]{:S(2)}) collective-permute-start(bf16[96,256]{1,0:T(8,128)(2,1)} %get-tuple-element.93), channel_id=1, source_target_pairs={{0,8},{1,9},{2,10},{3,11},{4,12},{5,13},{6,14},{7,15},{16,24},{17,... | collective-permute-start | bytes 147464 | tf_op jit(solution)/shard_map/ppermute | solution.py:651
  89.0 3.1 %collective-permute-start.15 = (bf16[96,256]{1,0:T(8,128)(2,1)S(1)}, bf16[96,256]{1,0:T(8,128)(2,1)S(1)}, u32[]{:S(2)}, u32[]{:S(2)}) collective-permute-start(bf16[96,256]{1,0:T(8,128)(2,1)S(1)} %get-tuple-element.94), channel_id=1, source_target_pairs={{8,16},{9,17},{10,18},{11,19},{12,20},{13,21},{14,22},{15,23},{24,... | collective-permute-start | bytes 147464 | tf_op jit(solution)/shard_map/ppermute | solution.py:651
  89.7 1.0 copy-start.7
  90.7 1.5 copy-start.18
  104.3 1.0 copy-start.5
  107.2 2.1 %copy-start.11 = (bf16[576,256]{1,0:T(8,128)(2,1)S(1)}, bf16[576,256]{1,0:T(8,128)(2,1)}, u32[]{:S(2)}) copy-start(bf16[576,256]{1,0:T(8,128)(2,1)} %copy-done.10) | copy-start | bytes 884740
  109.1 1.2 copy-start.26
  109.1 1.5 collective-permute-start.16
  113.2 15.5 %copy-start.25 = (bf16[192,256]{1,0:T(8,128)(2,1)S(1)}, bf16[192,256]{1,0:T(8,128)(2,1)}, u32[]{:S(2)}) copy-start(bf16[192,256]{1,0:T(8,128)(2,1)} %get-tuple-element.109.pick) | copy-start | bytes 294916
  113.2 25.6 %all-to-all-start.3 = ((bf16[16,144,256]{2,1,0:T(8,128)(2,1)}), bf16[16,144,256]{2,1,0:T(8,128)(2,1)S(1)}, u32[]{:S(2)}, u32[]{:S(2)}) async-start(bf16[16,144,256]{2,1,0:T(8,128)(2,1)} %shard_map.96), calls=%async_computation.3 | async-start | bytes 2359296 | tf_op jit(solution)/shard_map/all_to_all | solution.py:698
  120.6 4.1 %collective-permute-start.19 = (bf16[48,256]{1,0:T(8,128)(2,1)S(1)}, bf16[48,256]{1,0:T(8,128)(2,1)S(1)}, u32[]{:S(2)}, u32[]{:S(2)}) collective-permute-start(bf16[48,256]{1,0:T(8,128)(2,1)S(1)} %get-tuple-element.108.one), channel_id=1, source_target_pairs={{0,192},{64,0},{128,64},{192,128},{1,193},{65,1},{129,65},{193,129... | collective-permute-start | bytes 73736 | tf_op jit(solution)/shard_map/ppermute | solution.py:697
  122.7 4.2 %collective-permute-start.18 = (bf16[48,256]{1,0:T(8,128)(2,1)S(1)}, bf16[48,256]{1,0:T(8,128)(2,1)S(1)}, u32[]{:S(2)}, u32[]{:S(2)}) collective-permute-start(bf16[48,256]{1,0:T(8,128)(2,1)S(1)} %get-tuple-element.108.one), channel_id=1, source_target_pairs={{0,128},{64,192},{128,0},{192,64},{1,129},{65,193},{129,1},{193,65... | collective-permute-start | bytes 73736 | tf_op jit(solution)/shard_map/ppermute | solution.py:697
  123.9 4.8 %collective-permute-start.17 = (bf16[48,256]{1,0:T(8,128)(2,1)S(1)}, bf16[48,256]{1,0:T(8,128)(2,1)S(1)}, u32[]{:S(2)}, u32[]{:S(2)}) collective-permute-start(bf16[48,256]{1,0:T(8,128)(2,1)S(1)} %get-tuple-element.108.one), channel_id=1, source_target_pairs={{0,64},{64,128},{128,192},{192,0},{1,65},{65,129},{129,193},{193,1... | collective-permute-start | bytes 73736 | tf_op jit(solution)/shard_map/ppermute | solution.py:697
  139.5 3.9 %collective-permute-start.20 = (bf16[144,256]{1,0:T(8,128)(2,1)S(1)}, bf16[144,256]{1,0:T(8,128)(2,1)S(1)}, u32[]{:S(2)}, u32[]{:S(2)}) collective-permute-start(bf16[144,256]{1,0:T(8,128)(2,1)S(1)} %shard_map.98.one), channel_id=1, source_target_pairs={{0,64},{64,0},{128,192},{192,128},{1,65},{65,1},{129,193},{193,129... | collective-permute-start | bytes 221192 | tf_op jit(solution)/shard_map/ppermute | solution.py:703
  144.0 4.2 %collective-permute-start.21 = (bf16[144,256]{1,0:T(8,128)(2,1)S(1)}, bf16[144,256]{1,0:T(8,128)(2,1)S(1)}, u32[]{:S(2)}, u32[]{:S(2)}) collective-permute-start(bf16[144,256]{1,0:T(8,128)(2,1)S(1)} %shard_map.99.one), channel_id=1, source_target_pairs={{0,128},{64,192},{128,0},{192,64},{1,129},{65,193},{129,1},{193,65... | collective-permute-start | bytes 221192 | tf_op jit(solution)/shard_map/ppermute | solution.py:705
  148.7 10.9 %collective-permute-start.22 = (bf16[240,256]{1,0:T(8,128)(2,1)S(1)}, bf16[240,256]{1,0:T(8,128)(2,1)S(1)}, u32[]{:S(2)}, u32[]{:S(2)}) collective-permute-start(bf16[240,256]{1,0:T(8,128)(2,1)S(1)} %shard_map.100.one), channel_id=1, source_target_pairs={{0,56},{1,57},{2,58},{3,59},{4,60},{5,61},{6,62},{7,63},{8,48},{9,... | collective-permute-start | bytes 368648 | tf_op jit(solution)/shard_map/ppermute | solution.py:707
  161.2 19.2 %copy-start.27 = (bf16[192,256]{1,0:T(8,128)(2,1)S(1)}, bf16[192,256]{1,0:T(8,128)(2,1)}, u32[]{:S(2)}) copy-start(bf16[192,256]{1,0:T(8,128)(2,1)} %copy-done.26) | copy-start | bytes 294916
  161.2 20.4 %all-to-all-start.4 = ((bf16[16,144,256]{2,1,0:T(8,128)(2,1)}), bf16[16,144,256]{2,1,0:T(8,128)(2,1)S(1)}, u32[]{:S(2)}, u32[]{:S(2)}) async-start(bf16[16,144,256]{2,1,0:T(8,128)(2,1)} %get-tuple-element.117), calls=%async_computation.4 | async-start | bytes 2359296 | tf_op jit(solution)/shard_map/all_to_all | solution.py:713
  165.1 15.3 %collective-permute-start.23 = (bf16[48,256]{1,0:T(8,128)(2,1)S(1)}, bf16[48,256]{1,0:T(8,128)(2,1)S(1)}, u32[]{:S(2)}, u32[]{:S(2)}) collective-permute-start(bf16[48,256]{1,0:T(8,128)(2,1)S(1)} %get-tuple-element.120), channel_id=1, source_target_pairs={{0,7},{1,6},{2,5},{3,4},{4,3},{5,2},{6,1},{7,0},{8,15},{9,14},{10,... | collective-permute-start | bytes 73736 | tf_op jit(solution)/shard_map/ppermute | solution.py:710
  181.7 6.6 %collective-permute-start.24 = (bf16[16,144,256]{2,1,0:T(8,128)(2,1)S(1)}, bf16[16,144,256]{2,1,0:T(8,128)(2,1)S(1)}, u32[]{:S(2)}, u32[]{:S(2)}) collective-permute-start(bf16[16,144,256]{2,1,0:T(8,128)(2,1)S(1)} %all-to-all-done.4.refs_1_), channel_id=1, source_target_pairs={{0,1},{1,0},{2,3},{3,2},{4,5},{5,4},{6,7},{7,6},{8,9},{9,8},{10,11... | collective-permute-start | bytes 3538952 | tf_op jit(solution)/shard_map/ppermute | solution.py:716
  (11 other events, 8.9 us)

commit v19 on v18

--- a/solution.py
+++ b/solution.py
@@ -306,21 +306,26 @@
     post_ends(row, col, cells, first, second, ends)
 
 
-def back_kernel(pos, wide, first, second, pre, add, taps, back, slope, handed, cells, shifts):
+def back_kernel(pos, wide, first, second, pre, add, taps, handed, cells, shifts):
     row, col = pos[0], pos[1]
     stack_lines(row, wide, first, second, cells)
-    back[...] = convolve(cells, shifts, 12, 10, 0, taps, True).astype(BF16)
+    size = 30 * PITCH
+    handed[0:size, :] = convolve(cells, shifts, 12, 10, 0, taps, True).astype(BF16).astype(F32)
     inside = cell_mask(row, col)
     for f in range(3):
         where = slice(f * 10 * PITCH, (f + 1) * 10 * PITCH)
-        slope[where, :] = jnp.where(inside, slope_of(pre[where, :]), 0.0)
-    handed[...] = add[...]
-
-
-def delta_kernel(pos, back, got, pick, slope, taps, wide_delta, own, send, cells, grads, shifts, strips, lines):
-    row, col = pos[0], pos[1]
-    lines[...] = dot(pick[...], got[...], ((1,), (0,)))
-    grads[...] = back[...].astype(F32)
+        slope = jnp.where(inside, slope_of(pre[where, :]), 0.0)
+        handed[size + f * 10 * PITCH : size + (f + 1) * 10 * PITCH, :] = slope
+    for i in range(4):
+        handed[2 * size + 64 * i : 2 * size + 64 * (i + 1), :] = add[:, C * i : C * (i + 1)].astype(F32)
+
+
+def delta_kernel(pos, handed, got, taps, wide_delta, own, send, cells, grads, shifts, strips, lines):
+    row, col = pos[0], pos[1]
+    size = 30 * PITCH
+    add = jnp.concatenate([handed[2 * size + 64 * i : 2 * size + 64 * (i + 1), :] for i in range(4)], axis=1)
+    lines[...] = dot(add.astype(BF16), got[...], ((1,), (0,)))
+    grads[...] = handed[0:size, :]
     for f in range(3):
         base = f * 10 * PITCH
         for at, here in ((1, row == 0), (8, row == 7)):
@@ -341,7 +346,7 @@
     cells[...] = jnp.zeros_like(cells)
     for f in range(3):
         where = slice(f * 10 * PITCH, (f + 1) * 10 * PITCH)
-        value = grads[where, :] * slope[where, :]
+        value = grads[where, :] * handed[size + f * 10 * PITCH : size + (f + 1) * 10 * PITCH, :]
         at = (f * 12 + 1) * PITCH + 1
         cells[at : at + 10 * PITCH, :] = value.astype(BF16).astype(F32)
     at = lax.broadcasted_iota(jnp.int32, (8 * PITCH, C), 0) % PITCH
@@ -657,9 +662,9 @@
     packed_other = lax.ppermute(packed, "core", CORES)
     grad_two = run(grad_two_kernel, [(piece, BF16)], halves(10) + [(piece, F32)], pos, packed, packed_other)[0]
     grad_two, wide = lax.optimization_barrier((grad_two, wide))
-    back, slope, add_10 = run(
+    handed = run(
         back_kernel,
-        [((30 * PITCH, C), BF16), ((30 * PITCH, C), F32), ((64, 1024), BF16)],
+        [((60 * PITCH + 256, C), F32)],
         [((spare, C), F32), ((flat, C), BF16)],
         pos,
         wide,
@@ -668,17 +673,15 @@
         pre_one,
         add_10,
         kernel_two,
-    )
-    got, back, slope, add_10 = lax.optimization_barrier((got, back, slope, add_10))
+    )[0]
+    got, handed = lax.optimization_barrier((got, handed))
     wide_one, own, strips = run(
         delta_kernel,
         [((24 * PITCH, C), BF16), ((192, C), BF16), ((48, C), BF16)],
         [((spare, C), F32), ((30 * PITCH, C), F32), ((flat, C), BF16), ((48, C), F32), ((64, C), F32)],
         pos,
-        back,
+        handed,
         got,
-        add_10,
-        slope,
         kernel_one,
     )
     wide_other = lax.ppermute(wide_one, "core", CORES)

time: 192 us -> 190 us (0.990)
  waiting for transfers between devices: 52.1 us -> 58.9 us
  starting transfers between devices: 70.7 us -> 65.4 us
  local copies, waits for them, and re-layouts: 12.3 us -> 7.96 us
    unnamed x60 -> x46, local copies, waits for them, and re-layouts: 11 us -> 6.58 us
    all_to_all x2, waiting for transfers between devices: 12.5 us -> 15.8 us  [seam_exchange(): got = lax.all_to_all(send, AXES, 0, 0, axis_index_groups=SEAM_GROUPS)]
    all_to_all x2, starting transfers between devices: 11.2 us -> 8.5 us  [body(): part = lax.all_to_all(part, AXES, 0, 0, axis_index_groups=PLANE_GROUPS)]
    ppermute x1, waiting for transfers between devices: 7 us -> 9.24 us  [body(): onward = lax.ppermute(onward, TILE, [(t, t ^ 7) for t in range(64)])]
where the time goes in v19:
time: 190 us; the launch traced here: 189 us
  starting transfers between devices  65.4 us (34%)
  waiting for transfers between devices  58.9 us (31%)
  Pallas kernels  29.6 us (16%)
  blocking collectives  25.6 us (13%)
  local copies, waits for them, and re-layouts  7.96 us (4%)
    all_to_all x1, blocking collectives, seam_exchange(): got = lax.all_to_all(send, AXES, 0, 0, axis_index_groups=SEAM_GROUPS)  25.6 us
    pallas_call x17, Pallas kernels, run(): pl.pallas_call(kernel, out_shape=[jax.ShapeDtypeStruct(shape, dtype) for...  22.7 us
    all_to_all x2, starting transfers between devices, seam_exchange(): got = lax.all_to_all(send, AXES, 0, 0, axis_index_groups=SEAM_GROUPS)  20.1 us
    all_to_all x2, waiting for transfers between devices, seam_exchange(): got = lax.all_to_all(send, AXES, 0, 0, axis_index_groups=SEAM_GROUPS)  15.8 us
    all_to_all x2, waiting for transfers between devices, body(): part = lax.all_to_all(part, AXES, 0, 0, axis_index_groups=PLANE_GROUPS)  11.1 us
    ppermute x1, waiting for transfers between devices, body(): onward = lax.ppermute(onward, TILE, [(t, t ^ 7) for t in range(64)])  9.24 us
    all_to_all x2, starting transfers between devices, body(): part = lax.all_to_all(part, AXES, 0, 0, axis_index_groups=PLANE_GROUPS)  8.5 us
    ppermute x1, starting transfers between devices, body(): onward = lax.ppermute(onward, TILE, [(t, t ^ 7) for t in range(64)])  7.74 us
  transfers between devices with their start and end apart: 29, of which 15 were waited for; matrix products, arithmetic and copies ran while one was open for 1% of the time, Pallas kernels for 7%

profile of v19, /device:TPU:1, one launch (start us, length us, event | category | flops | bytes accessed | tf_op | source)
XLA Modules:
  0.0 188.7 jit_solution(10286346638753558680)
XLA Ops:
  0.7 1.0 copy-done.5
  1.7 1.3 shard_map.85
  3.1 14.3 %all-to-all-start = ((bf16[16,48,256]{2,1,0:T(8,128)(2,1)}), bf16[16,48,256]{2,1,0:T(8,128)(2,1)S(1)}, u32[]{:S(2)}, u32[]{:S(2)}) async-start(bf16[16,48,256]{2,1,0:T(8,128)(2,1)} %shard_map.85), calls=%async_computation | async-start | bytes 786432 | tf_op jit(solution)/shard_map/all_to_all | solution.py:488
  17.4 1.9 %collective-permute-start.1 = (bf16[192,256]{1,0:T(8,128)(2,1)S(1)}, bf16[192,256]{1,0:T(8,128)(2,1)S(1)}, u32[]{:S(2)}, u32[]{:S(2)}) collective-permute-start(bf16[192,256]{1,0:T(8,128)(2,1)S(1)} %bitcast.18), channel_id=1, source_target_pairs={{1,2},{3,4},{5,6},{9,10},{11,12},{13,14},{17,18},{19,20},{21,22},{... | collective-permute-start | bytes 294920 | tf_op jit(solution)/shard_map/ppermute | solution.py:612
  19.4 4.2 %collective-permute-done.1.odd = bf16[192,256]{1,0:T(8,128)(2,1)S(1)} collective-permute-done((bf16[192,256]{1,0:T(8,128)(2,1)S(1)}, bf16[192,256]{1,0:T(8,128)(2,1)S(1)}, u32[]{:S(2)}, u32[]{:S(2)}) %collective-permute-start.1) | collective-permute-done | bytes 98336 | tf_op jit(solution)/shard_map/ppermute | solution.py:612
  26.5 2.6 %shard_map.87 = (bf16[80,768]{1,0:T(8,128)(2,1)}, bf16[64,1024]{1,0:T(8,128)(2,1)}, bf16[64,1024]{1,0:T(8,128)(2,1)}, bf16[192,256]{1,0:T(8,128)(2,1)}) custom-call(s32[4]{0:T(128)} %copy-done.7, s32[12,4]{1,0:T(8,128)} %copy.11.nexts, s32[12,4]{1,0:T(8,128)} %copy.12.codes), custom_call_target="tpu_custom_call" | custom-call | tf_op jit(solution)/shard_map/pallas_call | solution.py:579
  29.1 4.9 %all-to-all-done = bf16[16,48,256]{2,1,0:T(8,128)(2,1)S(1)} async-done(((bf16[16,48,256]{2,1,0:T(8,128)(2,1)}), bf16[16,48,256]{2,1,0:T(8,128)(2,1)S(1)}, u32[]{:S(2)}, u32[]{:S(2)}) %all-to-all-start) | async-done | bytes 393248 | tf_op jit(solution)/shard_map/all_to_all | solution.py:488
  34.7 0.9 copy-done.14
  35.6 0.8 shard_map.88
  36.4 1.9 %collective-permute-start.5 = (bf16[16,256]{1,0:T(8,128)(2,1)S(1)}, bf16[16,256]{1,0:T(8,128)(2,1)S(1)}, u32[]{:S(2)}, u32[]{:S(2)}) collective-permute-start(bf16[16,256]{1,0:T(8,128)(2,1)S(1)} %get-tuple-element.74), channel_id=1, source_target_pairs={{1,2},{3,4},{5,6},{9,10},{11,12},{13,14},{17,18},{19,20},{21,22},{... | collective-permute-start | bytes 24584 | tf_op jit(solution)/shard_map/ppermute | solution.py:619
  39.1 2.3 %collective-permute-done.5.odd_ends = bf16[16,256]{1,0:T(8,128)(2,1)S(1)} collective-permute-done((bf16[16,256]{1,0:T(8,128)(2,1)S(1)}, bf16[16,256]{1,0:T(8,128)(2,1)S(1)}, u32[]{:S(2)}, u32[]{:S(2)}) %collective-permute-start.5) | collective-permute-done | bytes 8224 | tf_op jit(solution)/shard_map/ppermute | solution.py:619
  41.4 2.2 %shard_map.89 = (bf16[576,256]{1,0:T(8,128)(2,1)}, f32[480,256]{1,0:T(8,128)S(1)}, bf16[480,256]{1,0:T(8,128)(2,1)S(1)}, bf16[16,64,256]{2,1,0:T(8,128)(2,1)S(1)}) custom-call(s32[4]{0:T(128)S(1)} %copy-done.8, bf16[384,256]{1,0:T(8,128)(2,1)S(1)} %get-tuple-element.65.wide, bf16[96,256]{1,0:T(8,128)(2,1)S(1)} %collective-permute-done.2.first, ...), custom_call_target="tpu_custom_call" | custom-call | tf_op jit(solution)/shard_map/pallas_call | solution.py:58
  43.7 0.8 copy-done.3
  44.4 25.6 %all_to_all.25 = bf16[16,64,256]{2,1,0:T(8,128)(2,1)S(1)} all-to-all(bf16[16,64,256]{2,1,0:T(8,128)(2,1)S(1)} %get-tuple-element.79), channel_id=1, replica_groups={{0,7,56,63,64,71,120,127,128,135,184,191,192,199,248,255},{1,6,57,62,65..., dimensions={0} | all-to-all | bytes 1048576 | tf_op jit(solution)/shard_map/all_to_all | solution.py:488
  70.0 1.6 shard_map.90
  71.6 2.0 %collective-permute-start.10 = (bf16[192,256]{1,0:T(8,128)(2,1)S(1)}, bf16[192,256]{1,0:T(8,128)(2,1)S(1)}, u32[]{:S(2)}, u32[]{:S(2)}) collective-permute-start(bf16[192,256]{1,0:T(8,128)(2,1)S(1)} %get-tuple-element.81.own), channel_id=1, source_target_pairs={{1,2},{3,4},{5,6},{9,10},{11,12},{13,14},{17,18},{19,20},{21,22},{... | collective-permute-start | bytes 294920 | tf_op jit(solution)/shard_map/ppermute | solution.py:602
  74.5 1.8 collective-permute-done.11.end_one
  76.3 1.2 collective-permute-done.10.odd
  77.5 1.8 shard_map.91
  80.0 5.7 %all-to-all-start.2 = ((bf16[16,64,256]{2,1,0:T(8,128)(2,1)}), bf16[16,64,256]{2,1,0:T(8,128)(2,1)S(1)}, u32[]{:S(2)}, u32[]{:S(2)}) async-start(bf16[16,64,256]{2,1,0:T(8,128)(2,1)} %get-tuple-element.84), calls=%async_computation.2 | async-start | bytes 1048576 | tf_op jit(solution)/shard_map/all_to_all | solution.py:488
  86.4 3.3 %collective-permute-start.14 = (bf16[96,256]{1,0:T(8,128)(2,1)S(1)}, bf16[96,256]{1,0:T(8,128)(2,1)S(1)}, u32[]{:S(2)}, u32[]{:S(2)}) collective-permute-start(bf16[96,256]{1,0:T(8,128)(2,1)S(1)} %get-tuple-element.88), channel_id=1, source_target_pairs={{0,8},{1,9},{2,10},{3,11},{4,12},{5,13},{6,14},{7,15},{16,24},{17,... | collective-permute-start | bytes 147464 | tf_op jit(solution)/shard_map/ppermute | solution.py:656
  90.4 1.4 shard_map.92.two
  92.5 1.5 shard_map.93.handed
  94.0 10.9 %all-to-all-done.2 = bf16[16,64,256]{2,1,0:T(8,128)(2,1)S(1)} async-done(((bf16[16,64,256]{2,1,0:T(8,128)(2,1)}), bf16[16,64,256]{2,1,0:T(8,128)(2,1)S(1)}, u32[]{:S(2)}, u32[]{:S(2)}) %all-to-all-start.2) | async-done | bytes 524320 | tf_op jit(solution)/shard_map/all_to_all | solution.py:488
  105.0 1.3 copy-done.2
  106.2 1.9 %shard_map.94 = (bf16[384,256]{1,0:T(8,128)(2,1)S(1)}, bf16[192,256]{1,0:T(8,128)(2,1)S(1)}, bf16[48,256]{1,0:T(8,128)(2,1)S(1)}) custom-call(s32[4]{0:T(128)S(1)} %copy-done.9, f32[1216,256]{1,0:T(8,128)S(1)} %shard_map.93.handed, bf16[1024,256]{1,0:T(8,128)(2,1)S(1)} %bitcast.14, bf16[3,3,256,256]{3,2,1,0:T(8,128)(2,1)S(1)} %copy-done.2), custom_call_target="tpu_custom_call" | custom-call | tf_op jit(solution)/shard_map/pallas_call | solution.py:58
  109.4 1.5 shard_map.95.part
  111.0 2.5 %shard_map.96 = bf16[16,144,256]{2,1,0:T(8,128)(2,1)} custom-call(s32[4]{0:T(128)S(1)} %copy-done.9, bf16[576,256]{1,0:T(8,128)(2,1)} %collective-permute-done.8.source, bf16[384,256]{1,0:T(8,128)(2,1)S(1)} %collective-permute-done.16.delta, f32[16,72,256]{2,1,0:T(8,128)S(1)} %shard_map.95.part, bf16[16,72,256]{2,1,0:T(8,128)(2,1)S(1)} %shard_map.92.two), custom_call_target="tpu_custom_call" | custom-call | tf_op jit(solution)/shard_map/pallas_call | solution.py:58
  113.5 4.7 %all-to-all-start.3 = ((bf16[16,144,256]{2,1,0:T(8,128)(2,1)}), bf16[16,144,256]{2,1,0:T(8,128)(2,1)S(1)}, u32[]{:S(2)}, u32[]{:S(2)}) async-start(bf16[16,144,256]{2,1,0:T(8,128)(2,1)} %shard_map.96), calls=%async_computation.3 | async-start | bytes 2359296 | tf_op jit(solution)/shard_map/all_to_all | solution.py:701
  118.2 2.1 %collective-permute-start.19 = (bf16[48,256]{1,0:T(8,128)(2,1)S(1)}, bf16[48,256]{1,0:T(8,128)(2,1)S(1)}, u32[]{:S(2)}, u32[]{:S(2)}) collective-permute-start(bf16[48,256]{1,0:T(8,128)(2,1)S(1)} %copy-done.20), channel_id=1, source_target_pairs={{0,192},{64,0},{128,64},{192,128},{1,193},{65,1},{129,65},{193,129... | collective-permute-start | bytes 73736 | tf_op jit(solution)/shard_map/ppermute | solution.py:700
  120.3 1.2 collective-permute-start.18
  122.3 2.0 %collective-permute-done.18.three = bf16[48,256]{1,0:T(8,128)(2,1)S(1)} collective-permute-done((bf16[48,256]{1,0:T(8,128)(2,1)S(1)}, bf16[48,256]{1,0:T(8,128)(2,1)S(1)}, u32[]{:S(2)}, u32[]{:S(2)}) %collective-permute-start.18) | collective-permute-done | bytes 24608 | tf_op jit(solution)/shard_map/ppermute | solution.py:700
  124.2 2.1 %collective-permute-done.17.two = bf16[48,256]{1,0:T(8,128)(2,1)S(1)} collective-permute-done((bf16[48,256]{1,0:T(8,128)(2,1)S(1)}, bf16[48,256]{1,0:T(8,128)(2,1)S(1)}, u32[]{:S(2)}, u32[]{:S(2)}) %collective-permute-start.17) | collective-permute-done | bytes 24608 | tf_op jit(solution)/shard_map/ppermute | solution.py:700
  127.0 11.1 %all-to-all-done.3.parts = bf16[16,144,256]{2,1,0:T(8,128)(2,1)S(1)} async-done(((bf16[16,144,256]{2,1,0:T(8,128)(2,1)}), bf16[16,144,256]{2,1,0:T(8,128)(2,1)S(1)}, u32[]{:S(2)}, u32[]{:S(2)}) %all-to-all-start.3) | async-done | bytes 1179680 | tf_op jit(solution)/shard_map/all_to_all | solution.py:701
  138.8 2.1 %collective-permute-start.20 = (bf16[144,256]{1,0:T(8,128)(2,1)S(1)}, bf16[144,256]{1,0:T(8,128)(2,1)S(1)}, u32[]{:S(2)}, u32[]{:S(2)}) collective-permute-start(bf16[144,256]{1,0:T(8,128)(2,1)S(1)} %shard_map.98.one), channel_id=1, source_target_pairs={{0,64},{64,0},{128,192},{192,128},{1,65},{65,1},{129,193},{193,129... | collective-permute-start | bytes 221192 | tf_op jit(solution)/shard_map/ppermute | solution.py:706
  140.9 1.7 collective-permute-done.20.two
  143.2 2.0 %collective-permute-start.21 = (bf16[144,256]{1,0:T(8,128)(2,1)S(1)}, bf16[144,256]{1,0:T(8,128)(2,1)S(1)}, u32[]{:S(2)}, u32[]{:S(2)}) collective-permute-start(bf16[144,256]{1,0:T(8,128)(2,1)S(1)} %shard_map.99.one), channel_id=1, source_target_pairs={{0,128},{64,192},{128,0},{192,64},{1,129},{65,193},{129,1},{193,65... | collective-permute-start | bytes 221192 | tf_op jit(solution)/shard_map/ppermute | solution.py:708
  145.2 2.2 %collective-permute-done.21.two = bf16[144,256]{1,0:T(8,128)(2,1)S(1)} collective-permute-done((bf16[144,256]{1,0:T(8,128)(2,1)S(1)}, bf16[144,256]{1,0:T(8,128)(2,1)S(1)}, u32[]{:S(2)}, u32[]{:S(2)}) %collective-permute-start.21) | collective-permute-done | bytes 73760 | tf_op jit(solution)/shard_map/ppermute | solution.py:708
  148.0 5.7 %collective-permute-start.22 = (bf16[240,256]{1,0:T(8,128)(2,1)S(1)}, bf16[240,256]{1,0:T(8,128)(2,1)S(1)}, u32[]{:S(2)}, u32[]{:S(2)}) collective-permute-start(bf16[240,256]{1,0:T(8,128)(2,1)S(1)} %shard_map.100.one), channel_id=1, source_target_pairs={{0,56},{1,57},{2,58},{3,59},{4,60},{5,61},{6,62},{7,63},{8,48},{9,... | collective-permute-start | bytes 368648 | tf_op jit(solution)/shard_map/ppermute | solution.py:710
  153.7 4.2 %collective-permute-done.22.two = bf16[240,256]{1,0:T(8,128)(2,1)S(1)} collective-permute-done((bf16[240,256]{1,0:T(8,128)(2,1)S(1)}, bf16[240,256]{1,0:T(8,128)(2,1)S(1)}, u32[]{:S(2)}, u32[]{:S(2)}) %collective-permute-start.22) | collective-permute-done | bytes 122912 | tf_op jit(solution)/shard_map/ppermute | solution.py:710
  157.9 1.6 shard_map.101
  159.6 3.8 %all-to-all-start.4 = ((bf16[16,144,256]{2,1,0:T(8,128)(2,1)}), bf16[16,144,256]{2,1,0:T(8,128)(2,1)S(1)}, u32[]{:S(2)}, u32[]{:S(2)}) async-start(bf16[16,144,256]{2,1,0:T(8,128)(2,1)} %get-tuple-element.107), calls=%async_computation.4 | async-start | bytes 2359296 | tf_op jit(solution)/shard_map/all_to_all | solution.py:716
  163.4 7.7 %collective-permute-start.23 = (bf16[48,256]{1,0:T(8,128)(2,1)S(1)}, bf16[48,256]{1,0:T(8,128)(2,1)S(1)}, u32[]{:S(2)}, u32[]{:S(2)}) collective-permute-start(bf16[48,256]{1,0:T(8,128)(2,1)S(1)} %get-tuple-element.110), channel_id=1, source_target_pairs={{0,7},{1,6},{2,5},{3,4},{4,3},{5,2},{6,1},{7,0},{8,15},{9,14},{10,... | collective-permute-start | bytes 73736 | tf_op jit(solution)/shard_map/ppermute | solution.py:713
  171.2 9.2 %collective-permute-done.23.by_col = bf16[48,256]{1,0:T(8,128)(2,1)S(1)} collective-permute-done((bf16[48,256]{1,0:T(8,128)(2,1)S(1)}, bf16[48,256]{1,0:T(8,128)(2,1)S(1)}, u32[]{:S(2)}, u32[]{:S(2)}) %collective-permute-start.23) | collective-permute-done | bytes 24608 | tf_op jit(solution)/shard_map/ppermute | solution.py:713
  180.4 1.3 shard_map.102
  181.7 2.3 %collective-permute-start.24 = (bf16[16,144,256]{2,1,0:T(8,128)(2,1)S(1)}, bf16[16,144,256]{2,1,0:T(8,128)(2,1)S(1)}, u32[]{:S(2)}, u32[]{:S(2)}) collective-permute-start(bf16[16,144,256]{2,1,0:T(8,128)(2,1)S(1)} %all-to-all-done.4.refs_1_), channel_id=1, source_target_pairs={{0,1},{1,0},{2,3},{3,2},{4,5},{5,4},{6,7},{7,6},{8,9},{9,8},{10,11... | collective-permute-start | bytes 3538952 | tf_op jit(solution)/shard_map/ppermute | solution.py:719
  183.9 2.1 %shard_map.103 = (f32[9,256,256]{2,1,0:T(8,128)}, f32[9,256,256]{2,1,0:T(8,128)}) custom-call(s32[4]{0:T(128)S(1)} %copy-done.9, bf16[16,144,256]{2,1,0:T(8,128)(2,1)S(1)} %all-to-all-done.4.refs_1_), custom_call_target="tpu_custom_call" | custom-call | tf_op jit(solution)/shard_map/pallas_call | solution.py:476
  186.4 2.1 %shard_map.104 = (f32[9,256,256]{2,1,0:T(8,128)}, f32[9,256,256]{2,1,0:T(8,128)}) custom-call(s32[4]{0:T(128)S(1)} %copy-done.9, bf16[16,144,256]{2,1,0:T(8,128)(2,1)S(1)} %collective-permute-done.24.refs_1_, f32[9,256,256]{2,1,0:T(8,128)} %get-tuple-element.113.refs_2_, ...), custom_call_target="tpu_custom_call", output_to_operand_aliasing={{0}: (2, {}), {1}: (3, {})} | custom-call | tf_op jit(solution)/shard_map/pallas_call | solution.py:476
  (80 shorter events, 12.9 us)
Async XLA Ops:
  0.6 40.8 %copy-start.1 = (bf16[3,3,256,256]{3,2,1,0:T(8,128)(2,1)S(1)}, bf16[3,3,256,256]{3,2,1,0:T(8,128)(2,1)}, u32[]{:S(2)}) copy-start(bf16[3,3,256,256]{3,2,1,0:T(8,128)(2,1)} %taps.9) | copy-start | bytes 3538948
  0.7 25.8 %copy-start.7 = (s32[4]{0:T(128)}, s32[4]{0:T(128)S(1)}, u32[]{:S(2)}) copy-start(s32[4]{0:T(128)S(1)} %pad_add_fusion.pos.refs_0_) | copy-start | bytes 52
  0.7 1.0 copy-start.5
  1.7 15.7 %copy-start.6 = (bf16[3,1,8,8,256]{4,3,2,1,0:T(8,128)(2,1)S(1)}, bf16[3,1,8,8,256]{4,3,2,1,0:T(8,128)(2,1)}, u32[]{:S(2)}) copy-start(bf16[3,1,8,8,256]{4,3,2,1,0:T(8,128)(2,1)} %param.6) | copy-start | bytes 294916
  1.7 23.4 %copy-start.21 = (s32[12,4]{0,1:T(4,128)S(1)}, s32[12,4]{0,1:T(4,128)}, u32[]{:S(2)}) copy-start(s32[12,4]{0,1:T(4,128)} %param.10) | copy-start | bytes 580
  1.7 24.1 %copy-start.22 = (s32[12,4]{0,1:T(4,128)S(1)}, s32[12,4]{0,1:T(4,128)}, u32[]{:S(2)}) copy-start(s32[12,4]{0,1:T(4,128)} %param.11) | copy-start | bytes 580
  3.1 30.9 %all-to-all-start = ((bf16[16,48,256]{2,1,0:T(8,128)(2,1)}), bf16[16,48,256]{2,1,0:T(8,128)(2,1)S(1)}, u32[]{:S(2)}, u32[]{:S(2)}) async-start(bf16[16,48,256]{2,1,0:T(8,128)(2,1)} %shard_map.85), calls=%async_computation | async-start | bytes 786432 | tf_op jit(solution)/shard_map/all_to_all | solution.py:488
  17.4 6.2 %collective-permute-start.1 = (bf16[192,256]{1,0:T(8,128)(2,1)S(1)}, bf16[192,256]{1,0:T(8,128)(2,1)S(1)}, u32[]{:S(2)}, u32[]{:S(2)}) collective-permute-start(bf16[192,256]{1,0:T(8,128)(2,1)S(1)} %bitcast.18), channel_id=1, source_target_pairs={{1,2},{3,4},{5,6},{9,10},{11,12},{13,14},{17,18},{19,20},{21,22},{... | collective-permute-start | bytes 294920 | tf_op jit(solution)/shard_map/ppermute | solution.py:612
  19.3 4.3 %collective-permute-start = (bf16[192,256]{1,0:T(8,128)(2,1)S(1)}, bf16[192,256]{1,0:T(8,128)(2,1)S(1)}, u32[]{:S(2)}, u32[]{:S(2)}) collective-permute-start(bf16[192,256]{1,0:T(8,128)(2,1)S(1)} %bitcast.19), channel_id=1, source_target_pairs={{0,1},{1,0},{2,3},{3,2},{4,5},{5,4},{6,7},{7,6},{8,9},{9,8},{10,11... | collective-permute-start | bytes 294920 | tf_op jit(solution)/shard_map/ppermute | solution.py:612
  24.3 4.8 %collective-permute-start.2 = (bf16[96,256]{1,0:T(8,128)(2,1)S(1)}, bf16[96,256]{1,0:T(8,128)(2,1)S(1)}, u32[]{:S(2)}, u32[]{:S(2)}) collective-permute-start(bf16[96,256]{1,0:T(8,128)(2,1)S(1)} %get-tuple-element.63), channel_id=1, source_target_pairs={{0,8},{1,9},{2,10},{3,11},{4,12},{5,13},{6,14},{7,15},{16,24},{17,... | collective-permute-start | bytes 147464 | tf_op jit(solution)/shard_map/ppermute | solution.py:614
  24.4 4.7 %collective-permute-start.3 = (bf16[96,256]{1,0:T(8,128)(2,1)S(1)}, bf16[96,256]{1,0:T(8,128)(2,1)S(1)}, u32[]{:S(2)}, u32[]{:S(2)}) collective-permute-start(bf16[96,256]{1,0:T(8,128)(2,1)S(1)} %get-tuple-element.64), channel_id=1, source_target_pairs={{8,16},{9,17},{10,18},{11,19},{12,20},{13,21},{14,22},{15,23},{24,... | collective-permute-start | bytes 147464 | tf_op jit(solution)/shard_map/ppermute | solution.py:614
  34.7 0.9 copy-start.14
  36.3 2.8 %collective-permute-start.4 = (bf16[16,256]{1,0:T(8,128)(2,1)S(1)}, bf16[16,256]{1,0:T(8,128)(2,1)S(1)}, u32[]{:S(2)}, u32[]{:S(2)}) collective-permute-start(bf16[16,256]{1,0:T(8,128)(2,1)S(1)} %get-tuple-element.73), channel_id=1, source_target_pairs={{0,1},{1,0},{2,3},{3,2},{4,5},{5,4},{6,7},{7,6},{8,9},{9,8},{10,11... | collective-permute-start | bytes 24584 | tf_op jit(solution)/shard_map/ppermute | solution.py:618
  36.4 5.0 %collective-permute-start.5 = (bf16[16,256]{1,0:T(8,128)(2,1)S(1)}, bf16[16,256]{1,0:T(8,128)(2,1)S(1)}, u32[]{:S(2)}, u32[]{:S(2)}) collective-permute-start(bf16[16,256]{1,0:T(8,128)(2,1)S(1)} %get-tuple-element.74), channel_id=1, source_target_pairs={{1,2},{3,4},{5,6},{9,10},{11,12},{13,14},{17,18},{19,20},{21,22},{... | collective-permute-start | bytes 24584 | tf_op jit(solution)/shard_map/ppermute | solution.py:619
  38.4 3.0 %collective-permute-start.6 = (bf16[16,256]{1,0:T(8,128)(2,1)S(1)}, bf16[16,256]{1,0:T(8,128)(2,1)S(1)}, u32[]{:S(2)}, u32[]{:S(2)}) collective-permute-start(bf16[16,256]{1,0:T(8,128)(2,1)S(1)} %get-tuple-element.75), channel_id=1, source_target_pairs={{0,8},{1,9},{2,10},{3,11},{4,12},{5,13},{6,14},{7,15},{16,24},{17,... | collective-permute-start | bytes 24584 | tf_op jit(solution)/shard_map/ppermute | solution.py:620
  38.5 2.9 %collective-permute-start.7 = (bf16[16,256]{1,0:T(8,128)(2,1)S(1)}, bf16[16,256]{1,0:T(8,128)(2,1)S(1)}, u32[]{:S(2)}, u32[]{:S(2)}) collective-permute-start(bf16[16,256]{1,0:T(8,128)(2,1)S(1)} %get-tuple-element.76), channel_id=1, source_target_pairs={{8,16},{9,17},{10,18},{11,19},{12,20},{13,21},{14,22},{15,23},{40,... | collective-permute-start | bytes 24584 | tf_op jit(solution)/shard_map/ppermute | solution.py:621
  41.4 28.6 %copy-start = (bf16[3,3,256,256]{3,2,1,0:T(8,128)(2,1)S(1)}, bf16[3,3,256,256]{3,2,1,0:T(8,128)(2,1)}, u32[]{:S(2)}) copy-start(bf16[3,3,256,256]{3,2,1,0:T(8,128)(2,1)} %taps.8) | copy-start | bytes 3538948
  41.4 28.6 %copy-start.13 = (bf16[64,1024]{1,0:T(8,128)(2,1)S(1)}, bf16[64,1024]{1,0:T(8,128)(2,1)}, u32[]{:S(2)}) copy-start(bf16[64,1024]{1,0:T(8,128)(2,1)} %get-tuple-element.80.pick) | copy-start | bytes 393220
  41.4 28.6 %copy-start.15 = (bf16[3,1,8,8,256]{4,3,2,1,0:T(8,128)(2,1)S(1)}, bf16[3,1,8,8,256]{4,3,2,1,0:T(8,128)(2,1)}, u32[]{:S(2)}) copy-start(bf16[3,1,8,8,256]{4,3,2,1,0:T(8,128)(2,1)} %param.7) | copy-start | bytes 294916
  43.6 0.8 copy-start.3
  71.6 5.9 %collective-permute-start.10 = (bf16[192,256]{1,0:T(8,128)(2,1)S(1)}, bf16[192,256]{1,0:T(8,128)(2,1)S(1)}, u32[]{:S(2)}, u32[]{:S(2)}) collective-permute-start(bf16[192,256]{1,0:T(8,128)(2,1)S(1)} %get-tuple-element.81.own), channel_id=1, source_target_pairs={{1,2},{3,4},{5,6},{9,10},{11,12},{13,14},{17,18},{19,20},{21,22},{... | collective-permute-start | bytes 294920 | tf_op jit(solution)/shard_map/ppermute | solution.py:602
  73.7 3.9 %collective-permute-start.9 = (bf16[192,256]{1,0:T(8,128)(2,1)S(1)}, bf16[192,256]{1,0:T(8,128)(2,1)S(1)}, u32[]{:S(2)}, u32[]{:S(2)}) collective-permute-start(bf16[192,256]{1,0:T(8,128)(2,1)S(1)} %get-tuple-element.81.own), channel_id=1, source_target_pairs={{0,1},{1,0},{2,3},{3,2},{4,5},{5,4},{6,7},{7,6},{8,9},{9,8},{10,11... | collective-permute-start | bytes 294920 | tf_op jit(solution)/shard_map/ppermute | solution.py:601
  73.8 2.6 %collective-permute-start.11 = (bf16[16,256]{1,0:T(8,128)(2,1)S(1)}, bf16[16,256]{1,0:T(8,128)(2,1)S(1)}, u32[]{:S(2)}, u32[]{:S(2)}) collective-permute-start(bf16[16,256]{1,0:T(8,128)(2,1)S(1)} %get-tuple-element.82), channel_id=1, source_target_pairs={{0,8},{1,9},{2,10},{3,11},{4,12},{5,13},{6,14},{7,15},{16,24},{17,... | collective-permute-start | bytes 24584 | tf_op jit(solution)/shard_map/ppermute | solution.py:603
  73.9 16.5 %copy-start.9 = (s32[4]{0:T(128)S(1)}, s32[4]{0:T(128)}, u32[]{:S(2)}) copy-start(s32[4]{0:T(128)} %copy-done.7) | copy-start | bytes 52
  73.9 2.5 %collective-permute-start.12 = (bf16[16,256]{1,0:T(8,128)(2,1)S(1)}, bf16[16,256]{1,0:T(8,128)(2,1)S(1)}, u32[]{:S(2)}, u32[]{:S(2)}) collective-permute-start(bf16[16,256]{1,0:T(8,128)(2,1)S(1)} %get-tuple-element.83), channel_id=1, source_target_pairs={{8,16},{9,17},{10,18},{11,19},{12,20},{13,21},{14,22},{15,23},{40,... | collective-permute-start | bytes 24584 | tf_op jit(solution)/shard_map/ppermute | solution.py:604
  80.0 24.9 %all-to-all-start.2 = ((bf16[16,64,256]{2,1,0:T(8,128)(2,1)}), bf16[16,64,256]{2,1,0:T(8,128)(2,1)S(1)}, u32[]{:S(2)}, u32[]{:S(2)}) async-start(bf16[16,64,256]{2,1,0:T(8,128)(2,1)} %get-tuple-element.84), calls=%async_computation.2 | async-start | bytes 1048576 | tf_op jit(solution)/shard_map/all_to_all | solution.py:488
  85.8 6.7 %copy-start.4 = (f32[480,256]{1,0:T(8,128)S(1)}, f32[480,256]{1,0:T(8,128)}, u32[]{:S(2)}) copy-start(f32[480,256]{1,0:T(8,128)} %copy-done.3) | copy-start | bytes 1474564
  85.8 6.7 %copy-start.11 = (bf16[384,256]{1,0:T(8,128)(2,1)S(1)}, bf16[384,256]{1,0:T(8,128)(2,1)}, u32[]{:S(2)}) copy-start(bf16[384,256]{1,0:T(8,128)(2,1)} %copy-done.10) | copy-start | bytes 589828
  85.8 6.7 %copy-start.12 = (bf16[64,1024]{1,0:T(8,128)(2,1)S(1)}, bf16[64,1024]{1,0:T(8,128)(2,1)}, u32[]{:S(2)}) copy-start(bf16[64,1024]{1,0:T(8,128)(2,1)} %get-tuple-element.91.add) | copy-start | bytes 393220
  85.8 4.5 %collective-permute-start.13 = (bf16[864,256]{1,0:T(8,128)(2,1)S(1)}, bf16[864,256]{1,0:T(8,128)(2,1)S(1)}, u32[]{:S(2)}, u32[]{:S(2)}) collective-permute-start(bf16[864,256]{1,0:T(8,128)(2,1)S(1)} %get-tuple-element.85.own), channel_id=1, source_target_pairs={{0,1},{1,0},{2,3},{3,2},{4,5},{5,4},{6,7},{7,6},{8,9},{9,8},{10,11... | collective-permute-start | bytes 1327112 | tf_op jit(solution)/shard_map/ppermute | solution.py:662
  85.9 25.1 %collective-permute-start.8 = (bf16[576,256]{1,0:T(8,128)(2,1)}, bf16[576,256]{1,0:T(8,128)(2,1)}, u32[]{:S(2)}, u32[]{:S(2)}) collective-permute-start(bf16[576,256]{1,0:T(8,128)(2,1)} %get-tuple-element.77.source), channel_id=1, source_target_pairs={{0,1},{1,0},{2,3},{3,2},{4,5},{5,4},{6,7},{7,6},{8,9},{9,8},{10,11... | collective-permute-start | bytes 884744 | tf_op jit(solution)/shard_map/ppermute | solution.py:635
  86.4 6.0 %collective-permute-start.14 = (bf16[96,256]{1,0:T(8,128)(2,1)S(1)}, bf16[96,256]{1,0:T(8,128)(2,1)S(1)}, u32[]{:S(2)}, u32[]{:S(2)}) collective-permute-start(bf16[96,256]{1,0:T(8,128)(2,1)S(1)} %get-tuple-element.88), channel_id=1, source_target_pairs={{0,8},{1,9},{2,10},{3,11},{4,12},{5,13},{6,14},{7,15},{16,24},{17,... | collective-permute-start | bytes 147464 | tf_op jit(solution)/shard_map/ppermute | solution.py:656
  89.7 2.8 %collective-permute-start.15 = (bf16[96,256]{1,0:T(8,128)(2,1)S(1)}, bf16[96,256]{1,0:T(8,128)(2,1)S(1)}, u32[]{:S(2)}, u32[]{:S(2)}) collective-permute-start(bf16[96,256]{1,0:T(8,128)(2,1)S(1)} %get-tuple-element.89), channel_id=1, source_target_pairs={{8,16},{9,17},{10,18},{11,19},{12,20},{13,21},{14,22},{15,23},{24,... | collective-permute-start | bytes 147464 | tf_op jit(solution)/shard_map/ppermute | solution.py:656
  105.0 1.3 copy-start.2
  109.4 1.5 collective-permute-start.16
  113.5 4.7 %copy-start.20 = (bf16[48,256]{1,0:T(8,128)(2,1)S(1)}, bf16[48,256]{1,0:T(8,128)(2,1)}, u32[]{:S(2)}) copy-start(bf16[48,256]{1,0:T(8,128)(2,1)} %copy-done.19) | copy-start | bytes 73732
  113.5 12.8 %copy-start.16 = (bf16[192,256]{1,0:T(8,128)(2,1)S(1)}, bf16[192,256]{1,0:T(8,128)(2,1)}, u32[]{:S(2)}) copy-start(bf16[192,256]{1,0:T(8,128)(2,1)} %get-tuple-element.99.pick) | copy-start | bytes 294916
  113.5 24.6 %all-to-all-start.3 = ((bf16[16,144,256]{2,1,0:T(8,128)(2,1)}), bf16[16,144,256]{2,1,0:T(8,128)(2,1)S(1)}, u32[]{:S(2)}, u32[]{:S(2)}) async-start(bf16[16,144,256]{2,1,0:T(8,128)(2,1)} %shard_map.96), calls=%async_computation.3 | async-start | bytes 2359296 | tf_op jit(solution)/shard_map/all_to_all | solution.py:701
  118.2 4.1 %collective-permute-start.19 = (bf16[48,256]{1,0:T(8,128)(2,1)S(1)}, bf16[48,256]{1,0:T(8,128)(2,1)S(1)}, u32[]{:S(2)}, u32[]{:S(2)}) collective-permute-start(bf16[48,256]{1,0:T(8,128)(2,1)S(1)} %copy-done.20), channel_id=1, source_target_pairs={{0,192},{64,0},{128,64},{192,128},{1,193},{65,1},{129,65},{193,129... | collective-permute-start | bytes 73736 | tf_op jit(solution)/shard_map/ppermute | solution.py:700
  120.3 3.9 %collective-permute-start.18 = (bf16[48,256]{1,0:T(8,128)(2,1)S(1)}, bf16[48,256]{1,0:T(8,128)(2,1)S(1)}, u32[]{:S(2)}, u32[]{:S(2)}) collective-permute-start(bf16[48,256]{1,0:T(8,128)(2,1)S(1)} %copy-done.20), channel_id=1, source_target_pairs={{0,128},{64,192},{128,0},{192,64},{1,129},{65,193},{129,1},{193,65... | collective-permute-start | bytes 73736 | tf_op jit(solution)/shard_map/ppermute | solution.py:700
  121.5 4.8 %collective-permute-start.17 = (bf16[48,256]{1,0:T(8,128)(2,1)S(1)}, bf16[48,256]{1,0:T(8,128)(2,1)S(1)}, u32[]{:S(2)}, u32[]{:S(2)}) collective-permute-start(bf16[48,256]{1,0:T(8,128)(2,1)S(1)} %copy-done.20), channel_id=1, source_target_pairs={{0,64},{64,128},{128,192},{192,0},{1,65},{65,129},{129,193},{193,1... | collective-permute-start | bytes 73736 | tf_op jit(solution)/shard_map/ppermute | solution.py:700
  138.8 3.9 %collective-permute-start.20 = (bf16[144,256]{1,0:T(8,128)(2,1)S(1)}, bf16[144,256]{1,0:T(8,128)(2,1)S(1)}, u32[]{:S(2)}, u32[]{:S(2)}) collective-permute-start(bf16[144,256]{1,0:T(8,128)(2,1)S(1)} %shard_map.98.one), channel_id=1, source_target_pairs={{0,64},{64,0},{128,192},{192,128},{1,65},{65,1},{129,193},{193,129... | collective-permute-start | bytes 221192 | tf_op jit(solution)/shard_map/ppermute | solution.py:706
  143.2 4.2 %collective-permute-start.21 = (bf16[144,256]{1,0:T(8,128)(2,1)S(1)}, bf16[144,256]{1,0:T(8,128)(2,1)S(1)}, u32[]{:S(2)}, u32[]{:S(2)}) collective-permute-start(bf16[144,256]{1,0:T(8,128)(2,1)S(1)} %shard_map.99.one), channel_id=1, source_target_pairs={{0,128},{64,192},{128,0},{192,64},{1,129},{65,193},{129,1},{193,65... | collective-permute-start | bytes 221192 | tf_op jit(solution)/shard_map/ppermute | solution.py:708
  148.0 9.9 %collective-permute-start.22 = (bf16[240,256]{1,0:T(8,128)(2,1)S(1)}, bf16[240,256]{1,0:T(8,128)(2,1)S(1)}, u32[]{:S(2)}, u32[]{:S(2)}) collective-permute-start(bf16[240,256]{1,0:T(8,128)(2,1)S(1)} %shard_map.100.one), channel_id=1, source_target_pairs={{0,56},{1,57},{2,58},{3,59},{4,60},{5,61},{6,62},{7,63},{8,48},{9,... | collective-permute-start | bytes 368648 | tf_op jit(solution)/shard_map/ppermute | solution.py:710
  159.6 20.8 %copy-start.18 = (bf16[192,256]{1,0:T(8,128)(2,1)S(1)}, bf16[192,256]{1,0:T(8,128)(2,1)}, u32[]{:S(2)}) copy-start(bf16[192,256]{1,0:T(8,128)(2,1)} %copy-done.17) | copy-start | bytes 294916
  159.6 22.1 %all-to-all-start.4 = ((bf16[16,144,256]{2,1,0:T(8,128)(2,1)}), bf16[16,144,256]{2,1,0:T(8,128)(2,1)S(1)}, u32[]{:S(2)}, u32[]{:S(2)}) async-start(bf16[16,144,256]{2,1,0:T(8,128)(2,1)} %get-tuple-element.107), calls=%async_computation.4 | async-start | bytes 2359296 | tf_op jit(solution)/shard_map/all_to_all | solution.py:716
  163.4 17.0 %collective-permute-start.23 = (bf16[48,256]{1,0:T(8,128)(2,1)S(1)}, bf16[48,256]{1,0:T(8,128)(2,1)S(1)}, u32[]{:S(2)}, u32[]{:S(2)}) collective-permute-start(bf16[48,256]{1,0:T(8,128)(2,1)S(1)} %get-tuple-element.110), channel_id=1, source_target_pairs={{0,7},{1,6},{2,5},{3,4},{4,3},{5,2},{6,1},{7,0},{8,15},{9,14},{10,... | collective-permute-start | bytes 73736 | tf_op jit(solution)/shard_map/ppermute | solution.py:713
  181.7 4.7 %collective-permute-start.24 = (bf16[16,144,256]{2,1,0:T(8,128)(2,1)S(1)}, bf16[16,144,256]{2,1,0:T(8,128)(2,1)S(1)}, u32[]{:S(2)}, u32[]{:S(2)}) collective-permute-start(bf16[16,144,256]{2,1,0:T(8,128)(2,1)S(1)} %all-to-all-done.4.refs_1_), channel_id=1, source_target_pairs={{0,1},{1,0},{2,3},{3,2},{4,5},{5,4},{6,7},{7,6},{8,9},{9,8},{10,11... | collective-permute-start | bytes 3538952 | tf_op jit(solution)/shard_map/ppermute | solution.py:719
  (4 other events, 2.6 us)

commit v20 on v17

--- a/solution.py
+++ b/solution.py
@@ -428,13 +428,10 @@
     out[...] = total.astype(BF16)
 
 
-def add_kernel(pos, one, two, out):
-    out[...] = (one[...].astype(F32) + two[...].astype(F32)).astype(BF16)
-
-
-def add_more_kernel(pos, one, two, more, out):
-    total = (one[...].astype(F32) + two[...].astype(F32)).astype(BF16)
-    out[...] = jnp.concatenate([total, more[...]], axis=0)
+def add_more_kernel(pos, one, two, three, four, more, out):
+    total = one[...].astype(F32) + two[...].astype(F32)
+    total = total + (three[...].astype(F32) + four[...].astype(F32))
+    out[...] = jnp.concatenate([total.astype(BF16), more[...]], axis=0)
 
 
 def gather_kernel(pos, one, two, mine, by_col, out, own, onward):
@@ -693,10 +690,8 @@
     shares = run(share_kernel, [(strip, F32), (strip, BF16), ((96, C), BF16)], [], pos, *faces, add_8)
     part, mine, by_col, by_row = lax.optimization_barrier((part, *shares))
     part = run(plane_kernel, piece, [], pos, part)[0]
-    got = lax.ppermute(part, "face", [(i, i ^ 1) for i in range(4)])
-    part = run(add_kernel, piece, [], pos, part, got)[0]
-    got = lax.ppermute(part, "face", [(i, i ^ 2) for i in range(4)])
-    part = run(add_more_kernel, [((240, C), BF16)], [], pos, part, got, by_row)[0]
+    others = [lax.ppermute(part, "face", [(i, i ^ by) for i in range(4)]) for by in (1, 2, 3)]
+    part = run(add_more_kernel, [((240, C), BF16)], [], pos, part, *others, by_row)[0]
     got = lax.ppermute(part, TILE, [(t, t ^ 56) for t in range(64)])
     outs = [((16, 144, C), BF16), (strip, F32), (strip, BF16)]
     part, mine, onward = run(gather_kernel, outs, [], pos, part, got, mine, by_col)

time: 189 us -> 191 us (1.011)
  waiting for transfers between devices: 56.3 us -> 58.3 us
    ppermute x1, starting transfers between devices: 8.03 us -> 4.11 us  [body(): onward = lax.ppermute(onward, TILE, [(t, t ^ 7) for t in range(64)])]
    all_to_all x2, starting transfers between devices: 8.64 us -> 12.5 us  [body(): part = lax.all_to_all(part, AXES, 0, 0, axis_index_groups=PLANE_GROUPS)]
    ppermute x1, waiting for transfers between devices: 8.88 us -> 11.8 us  [body(): onward = lax.ppermute(onward, TILE, [(t, t ^ 7) for t in range(64)])]
    ppermute x2 -> x3, waiting for transfers between devices: 3.6 us -> 4.42 us  [body(): lax.ppermute(part, 'face', [(i, i ^ by) for i in range(4)])]
    pallas_call x17 -> x16, Pallas kernels: 21.6 us -> 21.1 us  [run(): pl.pallas_call(kernel, out_shape=[jax.ShapeDtypeStruct(shape, dtype) for...]
    ppermute x2 -> x3, starting transfers between devices: 4.09 us -> 3.63 us  [body(): lax.ppermute(part, 'face', [(i, i ^ by) for i in range(4)])]
  transfers between devices with their start and end apart: 29 -> 30, of which waited for: 15 -> 15; matrix products, arithmetic and copies ran while one was open for 1% -> 1% of each run, Pallas kernels for 7% -> 7%
where the time goes in v20:
time: 191 us; the launch traced here: 190 us
  starting transfers between devices  66.8 us (35%)
  waiting for transfers between devices  58.3 us (31%)
  Pallas kernels  27.9 us (15%)
  blocking collectives  25.6 us (13%)
  local copies, waits for them, and re-layouts  9.94 us (5%)
    all_to_all x1, blocking collectives, seam_exchange(): got = lax.all_to_all(send, AXES, 0, 0, axis_index_groups=SEAM_GROUPS)  25.6 us
    pallas_call x16, Pallas kernels, run(): pl.pallas_call(kernel, out_shape=[jax.ShapeDtypeStruct(shape, dtype) for...  21.1 us
    all_to_all x2, starting transfers between devices, seam_exchange(): got = lax.all_to_all(send, AXES, 0, 0, axis_index_groups=SEAM_GROUPS)  20.1 us
    all_to_all x2, waiting for transfers between devices, seam_exchange(): got = lax.all_to_all(send, AXES, 0, 0, axis_index_groups=SEAM_GROUPS)  15 us
    all_to_all x2, starting transfers between devices, body(): part = lax.all_to_all(part, AXES, 0, 0, axis_index_groups=PLANE_GROUPS)  12.5 us
    ppermute x1, waiting for transfers between devices, body(): onward = lax.ppermute(onward, TILE, [(t, t ^ 7) for t in range(64)])  11.8 us
    all_to_all x2, waiting for transfers between devices, body(): part = lax.all_to_all(part, AXES, 0, 0, axis_index_groups=PLANE_GROUPS)  9.81 us
    unnamed x52, local copies, waits for them, and re-layouts  8.58 us
  transfers between devices with their start and end apart: 30, of which 15 were waited for; matrix products, arithmetic and copies ran while one was open for 1% of the time, Pallas kernels for 7%

profile of v20, /device:TPU:1, one launch (start us, length us, event | category | flops | bytes accessed | tf_op | source)
XLA Modules:
  0.0 189.9 jit_solution(8185896578586132941)
XLA Ops:
  0.7 1.0 copy-done.8
  1.7 1.3 shard_map.85
  3.0 14.3 %all-to-all-start = ((bf16[16,48,256]{2,1,0:T(8,128)(2,1)}), bf16[16,48,256]{2,1,0:T(8,128)(2,1)S(1)}, u32[]{:S(2)}, u32[]{:S(2)}) async-start(bf16[16,48,256]{2,1,0:T(8,128)(2,1)} %shard_map.85), calls=%async_computation | async-start | bytes 786432 | tf_op jit(solution)/shard_map/all_to_all | solution.py:475
  17.4 1.9 %collective-permute-start.1 = (bf16[192,256]{1,0:T(8,128)(2,1)S(1)}, bf16[192,256]{1,0:T(8,128)(2,1)S(1)}, u32[]{:S(2)}, u32[]{:S(2)}) collective-permute-start(bf16[192,256]{1,0:T(8,128)(2,1)S(1)} %bitcast.18), channel_id=1, source_target_pairs={{1,2},{3,4},{5,6},{9,10},{11,12},{13,14},{17,18},{19,20},{21,22},{... | collective-permute-start | bytes 294920 | tf_op jit(solution)/shard_map/ppermute | solution.py:599
  19.4 4.2 %collective-permute-done.1.odd = bf16[192,256]{1,0:T(8,128)(2,1)S(1)} collective-permute-done((bf16[192,256]{1,0:T(8,128)(2,1)S(1)}, bf16[192,256]{1,0:T(8,128)(2,1)S(1)}, u32[]{:S(2)}, u32[]{:S(2)}) %collective-permute-start.1) | collective-permute-done | bytes 98336 | tf_op jit(solution)/shard_map/ppermute | solution.py:599
  26.5 2.6 %shard_map.87 = (bf16[80,768]{1,0:T(8,128)(2,1)}, bf16[64,1024]{1,0:T(8,128)(2,1)}, bf16[64,1024]{1,0:T(8,128)(2,1)}, bf16[192,256]{1,0:T(8,128)(2,1)}) custom-call(s32[4]{0:T(128)} %copy-done.12, s32[12,4]{1,0:T(8,128)} %copy.11.nexts, s32[12,4]{1,0:T(8,128)} %copy.12.codes), custom_call_target="tpu_custom_call" | custom-call | tf_op jit(solution)/shard_map/pallas_call | solution.py:566
  29.1 4.9 %all-to-all-done = bf16[16,48,256]{2,1,0:T(8,128)(2,1)S(1)} async-done(((bf16[16,48,256]{2,1,0:T(8,128)(2,1)}), bf16[16,48,256]{2,1,0:T(8,128)(2,1)S(1)}, u32[]{:S(2)}, u32[]{:S(2)}) %all-to-all-start) | async-done | bytes 393248 | tf_op jit(solution)/shard_map/all_to_all | solution.py:475
  34.6 0.9 copy-done.19
  36.4 1.9 %collective-permute-start.5 = (bf16[16,256]{1,0:T(8,128)(2,1)S(1)}, bf16[16,256]{1,0:T(8,128)(2,1)S(1)}, u32[]{:S(2)}, u32[]{:S(2)}) collective-permute-start(bf16[16,256]{1,0:T(8,128)(2,1)S(1)} %get-tuple-element.74), channel_id=1, source_target_pairs={{1,2},{3,4},{5,6},{9,10},{11,12},{13,14},{17,18},{19,20},{21,22},{... | collective-permute-start | bytes 24584 | tf_op jit(solution)/shard_map/ppermute | solution.py:606
  39.1 2.3 %collective-permute-done.5.odd_ends = bf16[16,256]{1,0:T(8,128)(2,1)S(1)} collective-permute-done((bf16[16,256]{1,0:T(8,128)(2,1)S(1)}, bf16[16,256]{1,0:T(8,128)(2,1)S(1)}, u32[]{:S(2)}, u32[]{:S(2)}) %collective-permute-start.5) | collective-permute-done | bytes 8224 | tf_op jit(solution)/shard_map/ppermute | solution.py:606
  41.4 1.5 shard_map.89
  43.7 25.6 %all_to_all.25 = bf16[16,64,256]{2,1,0:T(8,128)(2,1)S(1)} all-to-all(bf16[16,64,256]{2,1,0:T(8,128)(2,1)S(1)} %get-tuple-element.79), channel_id=1, replica_groups={{0,7,56,63,64,71,120,127,128,135,184,191,192,199,248,255},{1,6,57,62,65..., dimensions={0} | all-to-all | bytes 1048576 | tf_op jit(solution)/shard_map/all_to_all | solution.py:475
  69.3 1.6 shard_map.90
  70.9 2.0 %collective-permute-start.10 = (bf16[192,256]{1,0:T(8,128)(2,1)S(1)}, bf16[192,256]{1,0:T(8,128)(2,1)S(1)}, u32[]{:S(2)}, u32[]{:S(2)}) collective-permute-start(bf16[192,256]{1,0:T(8,128)(2,1)S(1)} %get-tuple-element.81.own), channel_id=1, source_target_pairs={{1,2},{3,4},{5,6},{9,10},{11,12},{13,14},{17,18},{19,20},{21,22},{... | collective-permute-start | bytes 294920 | tf_op jit(solution)/shard_map/ppermute | solution.py:589
  73.8 1.8 collective-permute-done.11.end_one
  75.6 1.2 collective-permute-done.10.odd
  76.8 1.8 shard_map.91
  79.3 5.7 %all-to-all-start.2 = ((bf16[16,64,256]{2,1,0:T(8,128)(2,1)}), bf16[16,64,256]{2,1,0:T(8,128)(2,1)S(1)}, u32[]{:S(2)}, u32[]{:S(2)}) async-start(bf16[16,64,256]{2,1,0:T(8,128)(2,1)} %get-tuple-element.84), calls=%async_computation.2 | async-start | bytes 1048576 | tf_op jit(solution)/shard_map/all_to_all | solution.py:475
  85.7 3.3 %collective-permute-start.14 = (bf16[96,256]{1,0:T(8,128)(2,1)}, bf16[96,256]{1,0:T(8,128)(2,1)S(1)}, u32[]{:S(2)}, u32[]{:S(2)}) collective-permute-start(bf16[96,256]{1,0:T(8,128)(2,1)} %get-tuple-element.88), channel_id=1, source_target_pairs={{0,8},{1,9},{2,10},{3,11},{4,12},{5,13},{6,14},{7,15},{16,24},{17,... | collective-permute-start | bytes 147464 | tf_op jit(solution)/shard_map/ppermute | solution.py:643
  89.6 1.0 copy-done.7
  90.6 1.4 shard_map.92.two
  92.1 1.3 shard_map.93.back
  94.1 10.1 %all-to-all-done.2 = bf16[16,64,256]{2,1,0:T(8,128)(2,1)S(1)} async-done(((bf16[16,64,256]{2,1,0:T(8,128)(2,1)}), bf16[16,64,256]{2,1,0:T(8,128)(2,1)S(1)}, u32[]{:S(2)}, u32[]{:S(2)}) %all-to-all-start.2) | async-done | bytes 524320 | tf_op jit(solution)/shard_map/all_to_all | solution.py:475
  104.3 0.9 copy-done.3
  105.2 1.0 copy-done.5
  106.2 0.9 copy-done.17
  107.1 2.1 %shard_map.94 = (bf16[384,256]{1,0:T(8,128)(2,1)S(1)}, bf16[192,256]{1,0:T(8,128)(2,1)S(1)}, bf16[48,256]{1,0:T(8,128)(2,1)S(1)}) custom-call(s32[4]{0:T(128)S(1)} %copy-done.14, bf16[480,256]{1,0:T(8,128)(2,1)S(1)} %copy-done.3, bf16[1024,256]{1,0:T(8,128)(2,1)S(1)} %bitcast.15, bf16[64,1024]{1,0:T(8,128)(2,1)S(1)} %copy-done.17, f32[480,256]{1,0:T(8,128)S(1)} %copy-done.5, ...), custom_call_target="tpu_custom_call" | custom-call | tf_op jit(solution)/shard_map/pallas_call | solution.py:58
  109.4 1.1 shard_map.95.part
  110.8 2.5 %shard_map.96 = bf16[16,144,256]{2,1,0:T(8,128)(2,1)} custom-call(s32[4]{0:T(128)S(1)} %copy-done.14, bf16[576,256]{1,0:T(8,128)(2,1)} %collective-permute-done.8.source, bf16[384,256]{1,0:T(8,128)(2,1)S(1)} %collective-permute-done.16.delta, f32[16,72,256]{2,1,0:T(8,128)S(1)} %shard_map.95.part, bf16[16,72,256]{2,1,0:T(8,128)(2,1)S(1)} %shard_map.92.two), custom_call_target="tpu_custom_call" | custom-call | tf_op jit(solution)/shard_map/pallas_call | solution.py:58
  113.4 4.8 %all-to-all-start.3 = ((bf16[16,144,256]{2,1,0:T(8,128)(2,1)}), bf16[16,144,256]{2,1,0:T(8,128)(2,1)S(1)}, u32[]{:S(2)}, u32[]{:S(2)}) async-start(bf16[16,144,256]{2,1,0:T(8,128)(2,1)} %shard_map.96), calls=%async_computation.3 | async-start | bytes 2359296 | tf_op jit(solution)/shard_map/all_to_all | solution.py:688
  118.2 2.1 %collective-permute-start.19 = (bf16[48,256]{1,0:T(8,128)(2,1)S(1)}, bf16[48,256]{1,0:T(8,128)(2,1)S(1)}, u32[]{:S(2)}, u32[]{:S(2)}) collective-permute-start(bf16[48,256]{1,0:T(8,128)(2,1)S(1)} %get-tuple-element.98.one), channel_id=1, source_target_pairs={{0,192},{64,0},{128,64},{192,128},{1,193},{65,1},{129,65},{193,129... | collective-permute-start | bytes 73736 | tf_op jit(solution)/shard_map/ppermute | solution.py:687
  121.1 1.1 collective-permute-start.17
  122.2 2.0 %collective-permute-done.18.three = bf16[48,256]{1,0:T(8,128)(2,1)S(1)} collective-permute-done((bf16[48,256]{1,0:T(8,128)(2,1)S(1)}, bf16[48,256]{1,0:T(8,128)(2,1)S(1)}, u32[]{:S(2)}, u32[]{:S(2)}) %collective-permute-start.18) | collective-permute-done | bytes 24608 | tf_op jit(solution)/shard_map/ppermute | solution.py:687
  124.2 1.7 collective-permute-done.17.two
  126.6 9.8 %all-to-all-done.3.parts = bf16[16,144,256]{2,1,0:T(8,128)(2,1)S(1)} async-done(((bf16[16,144,256]{2,1,0:T(8,128)(2,1)}), bf16[16,144,256]{2,1,0:T(8,128)(2,1)S(1)}, u32[]{:S(2)}, u32[]{:S(2)}) %all-to-all-start.3) | async-done | bytes 1179680 | tf_op jit(solution)/shard_map/all_to_all | solution.py:688
  137.1 2.1 %collective-permute-start.22 = (bf16[144,256]{1,0:T(8,128)(2,1)S(1)}, bf16[144,256]{1,0:T(8,128)(2,1)S(1)}, u32[]{:S(2)}, u32[]{:S(2)}) collective-permute-start(bf16[144,256]{1,0:T(8,128)(2,1)S(1)} %shard_map.98.one), channel_id=1, source_target_pairs={{0,192},{64,128},{128,64},{192,0},{1,193},{65,129},{129,65},{193,1... | collective-permute-start | bytes 221192 | tf_op jit(solution)/shard_map/ppermute | solution.py:693
  140.8 1.6 collective-permute-done.22.four
  142.3 2.9 %collective-permute-done.21.three = bf16[144,256]{1,0:T(8,128)(2,1)S(1)} collective-permute-done((bf16[144,256]{1,0:T(8,128)(2,1)S(1)}, bf16[144,256]{1,0:T(8,128)(2,1)S(1)}, u32[]{:S(2)}, u32[]{:S(2)}) %collective-permute-start.21) | collective-permute-done | bytes 73760 | tf_op jit(solution)/shard_map/ppermute | solution.py:693
  145.8 6.4 %collective-permute-start.23 = (bf16[240,256]{1,0:T(8,128)(2,1)S(1)}, bf16[240,256]{1,0:T(8,128)(2,1)S(1)}, u32[]{:S(2)}, u32[]{:S(2)}) collective-permute-start(bf16[240,256]{1,0:T(8,128)(2,1)S(1)} %shard_map.99.one), channel_id=1, source_target_pairs={{0,56},{1,57},{2,58},{3,59},{4,60},{5,61},{6,62},{7,63},{8,48},{9,... | collective-permute-start | bytes 368648 | tf_op jit(solution)/shard_map/ppermute | solution.py:695
  152.1 3.5 %collective-permute-done.23.two = bf16[240,256]{1,0:T(8,128)(2,1)S(1)} collective-permute-done((bf16[240,256]{1,0:T(8,128)(2,1)S(1)}, bf16[240,256]{1,0:T(8,128)(2,1)S(1)}, u32[]{:S(2)}, u32[]{:S(2)}) %collective-permute-start.23) | collective-permute-done | bytes 122912 | tf_op jit(solution)/shard_map/ppermute | solution.py:695
  155.6 1.6 shard_map.100
  157.3 7.7 %all-to-all-start.4 = ((bf16[16,144,256]{2,1,0:T(8,128)(2,1)}), bf16[16,144,256]{2,1,0:T(8,128)(2,1)S(1)}, u32[]{:S(2)}, u32[]{:S(2)}) async-start(bf16[16,144,256]{2,1,0:T(8,128)(2,1)} %get-tuple-element.107), calls=%async_computation.4 | async-start | bytes 2359296 | tf_op jit(solution)/shard_map/all_to_all | solution.py:701
  165.0 4.1 %collective-permute-start.24 = (bf16[48,256]{1,0:T(8,128)(2,1)S(1)}, bf16[48,256]{1,0:T(8,128)(2,1)S(1)}, u32[]{:S(2)}, u32[]{:S(2)}) collective-permute-start(bf16[48,256]{1,0:T(8,128)(2,1)S(1)} %get-tuple-element.110), channel_id=1, source_target_pairs={{0,7},{1,6},{2,5},{3,4},{4,3},{5,2},{6,1},{7,0},{8,15},{9,14},{10,... | collective-permute-start | bytes 73736 | tf_op jit(solution)/shard_map/ppermute | solution.py:698
  169.1 11.8 %collective-permute-done.24.by_col = bf16[48,256]{1,0:T(8,128)(2,1)S(1)} collective-permute-done((bf16[48,256]{1,0:T(8,128)(2,1)S(1)}, bf16[48,256]{1,0:T(8,128)(2,1)S(1)}, u32[]{:S(2)}, u32[]{:S(2)}) %collective-permute-start.24) | collective-permute-done | bytes 24608 | tf_op jit(solution)/shard_map/ppermute | solution.py:698
  180.9 1.3 shard_map.101
  182.1 3.0 %collective-permute-start.25 = (bf16[16,144,256]{2,1,0:T(8,128)(2,1)S(1)}, bf16[16,144,256]{2,1,0:T(8,128)(2,1)S(1)}, u32[]{:S(2)}, u32[]{:S(2)}) collective-permute-start(bf16[16,144,256]{2,1,0:T(8,128)(2,1)S(1)} %all-to-all-done.4.refs_1_), channel_id=1, source_target_pairs={{0,1},{1,0},{2,3},{3,2},{4,5},{5,4},{6,7},{7,6},{8,9},{9,8},{10,11... | collective-permute-start | bytes 3538952 | tf_op jit(solution)/shard_map/ppermute | solution.py:704
  185.1 2.1 %shard_map.102 = (f32[9,256,256]{2,1,0:T(8,128)}, f32[9,256,256]{2,1,0:T(8,128)}) custom-call(s32[4]{0:T(128)S(1)} %copy-done.14, bf16[16,144,256]{2,1,0:T(8,128)(2,1)S(1)} %all-to-all-done.4.refs_1_), custom_call_target="tpu_custom_call" | custom-call | tf_op jit(solution)/shard_map/pallas_call | solution.py:463
  187.6 2.1 %shard_map.103 = (f32[9,256,256]{2,1,0:T(8,128)}, f32[9,256,256]{2,1,0:T(8,128)}) custom-call(s32[4]{0:T(128)S(1)} %copy-done.14, bf16[16,144,256]{2,1,0:T(8,128)(2,1)S(1)} %collective-permute-done.25.refs_1_, f32[9,256,256]{2,1,0:T(8,128)} %get-tuple-element.113.refs_2_, ...), custom_call_target="tpu_custom_call", output_to_operand_aliasing={{0}: (2, {}), {1}: (3, {})} | custom-call | tf_op jit(solution)/shard_map/pallas_call | solution.py:463
  (87 shorter events, 14.7 us)
Async XLA Ops:
  0.6 40.7 %copy-start.1 = (bf16[3,3,256,256]{3,2,1,0:T(8,128)(2,1)S(1)}, bf16[3,3,256,256]{3,2,1,0:T(8,128)(2,1)}, u32[]{:S(2)}) copy-start(bf16[3,3,256,256]{3,2,1,0:T(8,128)(2,1)} %taps.9) | copy-start | bytes 3538948
  0.7 25.7 %copy-start.12 = (s32[4]{0:T(128)}, s32[4]{0:T(128)S(1)}, u32[]{:S(2)}) copy-start(s32[4]{0:T(128)S(1)} %pad_add_fusion.pos.refs_0_) | copy-start | bytes 52
  1.7 15.7 %copy-start.9 = (bf16[3,1,8,8,256]{4,3,2,1,0:T(8,128)(2,1)S(1)}, bf16[3,1,8,8,256]{4,3,2,1,0:T(8,128)(2,1)}, u32[]{:S(2)}) copy-start(bf16[3,1,8,8,256]{4,3,2,1,0:T(8,128)(2,1)} %param.6) | copy-start | bytes 294916
  1.7 23.4 %copy-start.24 = (s32[12,4]{0,1:T(4,128)S(1)}, s32[12,4]{0,1:T(4,128)}, u32[]{:S(2)}) copy-start(s32[12,4]{0,1:T(4,128)} %param.10) | copy-start | bytes 580
  1.7 24.1 %copy-start.25 = (s32[12,4]{0,1:T(4,128)S(1)}, s32[12,4]{0,1:T(4,128)}, u32[]{:S(2)}) copy-start(s32[12,4]{0,1:T(4,128)} %param.11) | copy-start | bytes 580
  3.0 30.9 %all-to-all-start = ((bf16[16,48,256]{2,1,0:T(8,128)(2,1)}), bf16[16,48,256]{2,1,0:T(8,128)(2,1)S(1)}, u32[]{:S(2)}, u32[]{:S(2)}) async-start(bf16[16,48,256]{2,1,0:T(8,128)(2,1)} %shard_map.85), calls=%async_computation | async-start | bytes 786432 | tf_op jit(solution)/shard_map/all_to_all | solution.py:475
  17.4 6.2 %collective-permute-start.1 = (bf16[192,256]{1,0:T(8,128)(2,1)S(1)}, bf16[192,256]{1,0:T(8,128)(2,1)S(1)}, u32[]{:S(2)}, u32[]{:S(2)}) collective-permute-start(bf16[192,256]{1,0:T(8,128)(2,1)S(1)} %bitcast.18), channel_id=1, source_target_pairs={{1,2},{3,4},{5,6},{9,10},{11,12},{13,14},{17,18},{19,20},{21,22},{... | collective-permute-start | bytes 294920 | tf_op jit(solution)/shard_map/ppermute | solution.py:599
  19.3 4.3 %collective-permute-start = (bf16[192,256]{1,0:T(8,128)(2,1)S(1)}, bf16[192,256]{1,0:T(8,128)(2,1)S(1)}, u32[]{:S(2)}, u32[]{:S(2)}) collective-permute-start(bf16[192,256]{1,0:T(8,128)(2,1)S(1)} %bitcast.19), channel_id=1, source_target_pairs={{0,1},{1,0},{2,3},{3,2},{4,5},{5,4},{6,7},{7,6},{8,9},{9,8},{10,11... | collective-permute-start | bytes 294920 | tf_op jit(solution)/shard_map/ppermute | solution.py:599
  24.3 4.8 %collective-permute-start.2 = (bf16[96,256]{1,0:T(8,128)(2,1)S(1)}, bf16[96,256]{1,0:T(8,128)(2,1)S(1)}, u32[]{:S(2)}, u32[]{:S(2)}) collective-permute-start(bf16[96,256]{1,0:T(8,128)(2,1)S(1)} %get-tuple-element.63), channel_id=1, source_target_pairs={{0,8},{1,9},{2,10},{3,11},{4,12},{5,13},{6,14},{7,15},{16,24},{17,... | collective-permute-start | bytes 147464 | tf_op jit(solution)/shard_map/ppermute | solution.py:601
  24.4 4.7 %collective-permute-start.3 = (bf16[96,256]{1,0:T(8,128)(2,1)S(1)}, bf16[96,256]{1,0:T(8,128)(2,1)S(1)}, u32[]{:S(2)}, u32[]{:S(2)}) collective-permute-start(bf16[96,256]{1,0:T(8,128)(2,1)S(1)} %get-tuple-element.64), channel_id=1, source_target_pairs={{8,16},{9,17},{10,18},{11,19},{12,20},{13,21},{14,22},{15,23},{24,... | collective-permute-start | bytes 147464 | tf_op jit(solution)/shard_map/ppermute | solution.py:601
  36.3 2.8 %collective-permute-start.4 = (bf16[16,256]{1,0:T(8,128)(2,1)S(1)}, bf16[16,256]{1,0:T(8,128)(2,1)S(1)}, u32[]{:S(2)}, u32[]{:S(2)}) collective-permute-start(bf16[16,256]{1,0:T(8,128)(2,1)S(1)} %get-tuple-element.73), channel_id=1, source_target_pairs={{0,1},{1,0},{2,3},{3,2},{4,5},{5,4},{6,7},{7,6},{8,9},{9,8},{10,11... | collective-permute-start | bytes 24584 | tf_op jit(solution)/shard_map/ppermute | solution.py:605
  36.4 5.0 %collective-permute-start.5 = (bf16[16,256]{1,0:T(8,128)(2,1)S(1)}, bf16[16,256]{1,0:T(8,128)(2,1)S(1)}, u32[]{:S(2)}, u32[]{:S(2)}) collective-permute-start(bf16[16,256]{1,0:T(8,128)(2,1)S(1)} %get-tuple-element.74), channel_id=1, source_target_pairs={{1,2},{3,4},{5,6},{9,10},{11,12},{13,14},{17,18},{19,20},{21,22},{... | collective-permute-start | bytes 24584 | tf_op jit(solution)/shard_map/ppermute | solution.py:606
  38.3 3.0 %collective-permute-start.6 = (bf16[16,256]{1,0:T(8,128)(2,1)S(1)}, bf16[16,256]{1,0:T(8,128)(2,1)S(1)}, u32[]{:S(2)}, u32[]{:S(2)}) collective-permute-start(bf16[16,256]{1,0:T(8,128)(2,1)S(1)} %get-tuple-element.75), channel_id=1, source_target_pairs={{0,8},{1,9},{2,10},{3,11},{4,12},{5,13},{6,14},{7,15},{16,24},{17,... | collective-permute-start | bytes 24584 | tf_op jit(solution)/shard_map/ppermute | solution.py:607
  38.4 2.9 %collective-permute-start.7 = (bf16[16,256]{1,0:T(8,128)(2,1)S(1)}, bf16[16,256]{1,0:T(8,128)(2,1)S(1)}, u32[]{:S(2)}, u32[]{:S(2)}) collective-permute-start(bf16[16,256]{1,0:T(8,128)(2,1)S(1)} %get-tuple-element.76), channel_id=1, source_target_pairs={{8,16},{9,17},{10,18},{11,19},{12,20},{13,21},{14,22},{15,23},{40,... | collective-permute-start | bytes 24584 | tf_op jit(solution)/shard_map/ppermute | solution.py:608
  41.3 27.9 %copy-start = (bf16[3,3,256,256]{3,2,1,0:T(8,128)(2,1)S(1)}, bf16[3,3,256,256]{3,2,1,0:T(8,128)(2,1)}, u32[]{:S(2)}) copy-start(bf16[3,3,256,256]{3,2,1,0:T(8,128)(2,1)} %taps.8) | copy-start | bytes 3538948
  41.4 27.9 %copy-start.18 = (bf16[64,1024]{1,0:T(8,128)(2,1)S(1)}, bf16[64,1024]{1,0:T(8,128)(2,1)}, u32[]{:S(2)}) copy-start(bf16[64,1024]{1,0:T(8,128)(2,1)} %get-tuple-element.80.pick) | copy-start | bytes 393220
  41.4 27.9 %copy-start.20 = (bf16[3,1,8,8,256]{4,3,2,1,0:T(8,128)(2,1)S(1)}, bf16[3,1,8,8,256]{4,3,2,1,0:T(8,128)(2,1)}, u32[]{:S(2)}) copy-start(bf16[3,1,8,8,256]{4,3,2,1,0:T(8,128)(2,1)} %param.7) | copy-start | bytes 294916
  43.7 27.2 %copy-start.10 = (bf16[576,256]{1,0:T(8,128)(2,1)}, bf16[576,256]{1,0:T(8,128)(2,1)S(1)}, u32[]{:S(2)}) copy-start(bf16[576,256]{1,0:T(8,128)(2,1)S(1)} %get-tuple-element.77.source) | copy-start | bytes 884740
  70.9 14.2 %copy-start.6 = (bf16[864,256]{1,0:T(8,128)(2,1)}, bf16[864,256]{1,0:T(8,128)(2,1)S(1)}, u32[]{:S(2)}) copy-start(bf16[864,256]{1,0:T(8,128)(2,1)S(1)} %get-tuple-element.85.own) | copy-start | bytes 1327108
  70.9 5.9 %collective-permute-start.10 = (bf16[192,256]{1,0:T(8,128)(2,1)S(1)}, bf16[192,256]{1,0:T(8,128)(2,1)S(1)}, u32[]{:S(2)}, u32[]{:S(2)}) collective-permute-start(bf16[192,256]{1,0:T(8,128)(2,1)S(1)} %get-tuple-element.81.own), channel_id=1, source_target_pairs={{1,2},{3,4},{5,6},{9,10},{11,12},{13,14},{17,18},{19,20},{21,22},{... | collective-permute-start | bytes 294920 | tf_op jit(solution)/shard_map/ppermute | solution.py:589
  73.0 3.9 %collective-permute-start.9 = (bf16[192,256]{1,0:T(8,128)(2,1)S(1)}, bf16[192,256]{1,0:T(8,128)(2,1)S(1)}, u32[]{:S(2)}, u32[]{:S(2)}) collective-permute-start(bf16[192,256]{1,0:T(8,128)(2,1)S(1)} %get-tuple-element.81.own), channel_id=1, source_target_pairs={{0,1},{1,0},{2,3},{3,2},{4,5},{5,4},{6,7},{7,6},{8,9},{9,8},{10,11... | collective-permute-start | bytes 294920 | tf_op jit(solution)/shard_map/ppermute | solution.py:588
  73.1 2.6 %collective-permute-start.11 = (bf16[16,256]{1,0:T(8,128)(2,1)S(1)}, bf16[16,256]{1,0:T(8,128)(2,1)S(1)}, u32[]{:S(2)}, u32[]{:S(2)}) collective-permute-start(bf16[16,256]{1,0:T(8,128)(2,1)S(1)} %get-tuple-element.82), channel_id=1, source_target_pairs={{0,8},{1,9},{2,10},{3,11},{4,12},{5,13},{6,14},{7,15},{16,24},{17,... | collective-permute-start | bytes 24584 | tf_op jit(solution)/shard_map/ppermute | solution.py:590
  73.2 16.5 %copy-start.14 = (s32[4]{0:T(128)S(1)}, s32[4]{0:T(128)}, u32[]{:S(2)}) copy-start(s32[4]{0:T(128)} %copy-done.12) | copy-start | bytes 52
  73.2 2.5 %collective-permute-start.12 = (bf16[16,256]{1,0:T(8,128)(2,1)S(1)}, bf16[16,256]{1,0:T(8,128)(2,1)S(1)}, u32[]{:S(2)}, u32[]{:S(2)}) collective-permute-start(bf16[16,256]{1,0:T(8,128)(2,1)S(1)} %get-tuple-element.83), channel_id=1, source_target_pairs={{8,16},{9,17},{10,18},{11,19},{12,20},{13,21},{14,22},{15,23},{40,... | collective-permute-start | bytes 24584 | tf_op jit(solution)/shard_map/ppermute | solution.py:591
  79.3 24.9 %all-to-all-start.2 = ((bf16[16,64,256]{2,1,0:T(8,128)(2,1)}), bf16[16,64,256]{2,1,0:T(8,128)(2,1)S(1)}, u32[]{:S(2)}, u32[]{:S(2)}) async-start(bf16[16,64,256]{2,1,0:T(8,128)(2,1)} %get-tuple-element.84), calls=%async_computation.2 | async-start | bytes 1048576 | tf_op jit(solution)/shard_map/all_to_all | solution.py:475
  85.1 4.5 %collective-permute-start.13 = (bf16[864,256]{1,0:T(8,128)(2,1)S(1)}, bf16[864,256]{1,0:T(8,128)(2,1)S(1)}, u32[]{:S(2)}, u32[]{:S(2)}) collective-permute-start(bf16[864,256]{1,0:T(8,128)(2,1)S(1)} %get-tuple-element.85.own), channel_id=1, source_target_pairs={{0,1},{1,0},{2,3},{3,2},{4,5},{5,4},{6,7},{7,6},{8,9},{9,8},{10,11... | collective-permute-start | bytes 1327112 | tf_op jit(solution)/shard_map/ppermute | solution.py:649
  85.2 25.3 %collective-permute-start.8 = (bf16[576,256]{1,0:T(8,128)(2,1)}, bf16[576,256]{1,0:T(8,128)(2,1)}, u32[]{:S(2)}, u32[]{:S(2)}) collective-permute-start(bf16[576,256]{1,0:T(8,128)(2,1)} %copy-done.10), channel_id=1, source_target_pairs={{0,1},{1,0},{2,3},{3,2},{4,5},{5,4},{6,7},{7,6},{8,9},{9,8},{10,11... | collective-permute-start | bytes 884744 | tf_op jit(solution)/shard_map/ppermute | solution.py:622
  85.7 6.4 %collective-permute-start.14 = (bf16[96,256]{1,0:T(8,128)(2,1)}, bf16[96,256]{1,0:T(8,128)(2,1)S(1)}, u32[]{:S(2)}, u32[]{:S(2)}) collective-permute-start(bf16[96,256]{1,0:T(8,128)(2,1)} %get-tuple-element.88), channel_id=1, source_target_pairs={{0,8},{1,9},{2,10},{3,11},{4,12},{5,13},{6,14},{7,15},{16,24},{17,... | collective-permute-start | bytes 147464 | tf_op jit(solution)/shard_map/ppermute | solution.py:643
  89.0 3.1 %collective-permute-start.15 = (bf16[96,256]{1,0:T(8,128)(2,1)S(1)}, bf16[96,256]{1,0:T(8,128)(2,1)S(1)}, u32[]{:S(2)}, u32[]{:S(2)}) collective-permute-start(bf16[96,256]{1,0:T(8,128)(2,1)S(1)} %get-tuple-element.89), channel_id=1, source_target_pairs={{8,16},{9,17},{10,18},{11,19},{12,20},{13,21},{14,22},{15,23},{24,... | collective-permute-start | bytes 147464 | tf_op jit(solution)/shard_map/ppermute | solution.py:643
  89.6 1.0 copy-start.7
  90.6 1.5 copy-start.16
  105.2 1.0 copy-start.5
  107.1 2.2 %copy-start.11 = (bf16[576,256]{1,0:T(8,128)(2,1)S(1)}, bf16[576,256]{1,0:T(8,128)(2,1)}, u32[]{:S(2)}) copy-start(bf16[576,256]{1,0:T(8,128)(2,1)} %copy-done.10) | copy-start | bytes 884740
  109.3 1.2 copy-start.22
  109.3 1.5 collective-permute-start.16
  113.3 12.6 %copy-start.21 = (bf16[192,256]{1,0:T(8,128)(2,1)S(1)}, bf16[192,256]{1,0:T(8,128)(2,1)}, u32[]{:S(2)}) copy-start(bf16[192,256]{1,0:T(8,128)(2,1)} %get-tuple-element.99.pick) | copy-start | bytes 294916
  113.4 23.1 %all-to-all-start.3 = ((bf16[16,144,256]{2,1,0:T(8,128)(2,1)}), bf16[16,144,256]{2,1,0:T(8,128)(2,1)S(1)}, u32[]{:S(2)}, u32[]{:S(2)}) async-start(bf16[16,144,256]{2,1,0:T(8,128)(2,1)} %shard_map.96), calls=%async_computation.3 | async-start | bytes 2359296 | tf_op jit(solution)/shard_map/all_to_all | solution.py:688
  118.2 4.0 %collective-permute-start.19 = (bf16[48,256]{1,0:T(8,128)(2,1)S(1)}, bf16[48,256]{1,0:T(8,128)(2,1)S(1)}, u32[]{:S(2)}, u32[]{:S(2)}) collective-permute-start(bf16[48,256]{1,0:T(8,128)(2,1)S(1)} %get-tuple-element.98.one), channel_id=1, source_target_pairs={{0,192},{64,0},{128,64},{192,128},{1,193},{65,1},{129,65},{193,129... | collective-permute-start | bytes 73736 | tf_op jit(solution)/shard_map/ppermute | solution.py:687
  120.3 3.9 %collective-permute-start.18 = (bf16[48,256]{1,0:T(8,128)(2,1)S(1)}, bf16[48,256]{1,0:T(8,128)(2,1)S(1)}, u32[]{:S(2)}, u32[]{:S(2)}) collective-permute-start(bf16[48,256]{1,0:T(8,128)(2,1)S(1)} %get-tuple-element.98.one), channel_id=1, source_target_pairs={{0,128},{64,192},{128,0},{192,64},{1,129},{65,193},{129,1},{193,65... | collective-permute-start | bytes 73736 | tf_op jit(solution)/shard_map/ppermute | solution.py:687
  121.1 4.8 %collective-permute-start.17 = (bf16[48,256]{1,0:T(8,128)(2,1)S(1)}, bf16[48,256]{1,0:T(8,128)(2,1)S(1)}, u32[]{:S(2)}, u32[]{:S(2)}) collective-permute-start(bf16[48,256]{1,0:T(8,128)(2,1)S(1)} %get-tuple-element.98.one), channel_id=1, source_target_pairs={{0,64},{64,128},{128,192},{192,0},{1,65},{65,129},{129,193},{193,1... | collective-permute-start | bytes 73736 | tf_op jit(solution)/shard_map/ppermute | solution.py:687
  137.1 5.2 %collective-permute-start.22 = (bf16[144,256]{1,0:T(8,128)(2,1)S(1)}, bf16[144,256]{1,0:T(8,128)(2,1)S(1)}, u32[]{:S(2)}, u32[]{:S(2)}) collective-permute-start(bf16[144,256]{1,0:T(8,128)(2,1)S(1)} %shard_map.98.one), channel_id=1, source_target_pairs={{0,192},{64,128},{128,64},{192,0},{1,193},{65,129},{129,65},{193,1... | collective-permute-start | bytes 221192 | tf_op jit(solution)/shard_map/ppermute | solution.py:693
  139.2 6.0 %collective-permute-start.21 = (bf16[144,256]{1,0:T(8,128)(2,1)S(1)}, bf16[144,256]{1,0:T(8,128)(2,1)S(1)}, u32[]{:S(2)}, u32[]{:S(2)}) collective-permute-start(bf16[144,256]{1,0:T(8,128)(2,1)S(1)} %shard_map.98.one), channel_id=1, source_target_pairs={{0,128},{64,192},{128,0},{192,64},{1,129},{65,193},{129,1},{193,65... | collective-permute-start | bytes 221192 | tf_op jit(solution)/shard_map/ppermute | solution.py:693
  140.1 5.1 %collective-permute-start.20 = (bf16[144,256]{1,0:T(8,128)(2,1)S(1)}, bf16[144,256]{1,0:T(8,128)(2,1)S(1)}, u32[]{:S(2)}, u32[]{:S(2)}) collective-permute-start(bf16[144,256]{1,0:T(8,128)(2,1)S(1)} %shard_map.98.one), channel_id=1, source_target_pairs={{0,64},{64,0},{128,192},{192,128},{1,65},{65,1},{129,193},{193,129... | collective-permute-start | bytes 221192 | tf_op jit(solution)/shard_map/ppermute | solution.py:693
  145.8 9.8 %collective-permute-start.23 = (bf16[240,256]{1,0:T(8,128)(2,1)S(1)}, bf16[240,256]{1,0:T(8,128)(2,1)S(1)}, u32[]{:S(2)}, u32[]{:S(2)}) collective-permute-start(bf16[240,256]{1,0:T(8,128)(2,1)S(1)} %shard_map.99.one), channel_id=1, source_target_pairs={{0,56},{1,57},{2,58},{3,59},{4,60},{5,61},{6,62},{7,63},{8,48},{9,... | collective-permute-start | bytes 368648 | tf_op jit(solution)/shard_map/ppermute | solution.py:695
  157.2 23.6 %copy-start.23 = (bf16[192,256]{1,0:T(8,128)(2,1)S(1)}, bf16[192,256]{1,0:T(8,128)(2,1)}, u32[]{:S(2)}) copy-start(bf16[192,256]{1,0:T(8,128)(2,1)} %copy-done.22) | copy-start | bytes 294916
  157.3 24.9 %all-to-all-start.4 = ((bf16[16,144,256]{2,1,0:T(8,128)(2,1)}), bf16[16,144,256]{2,1,0:T(8,128)(2,1)S(1)}, u32[]{:S(2)}, u32[]{:S(2)}) async-start(bf16[16,144,256]{2,1,0:T(8,128)(2,1)} %get-tuple-element.107), calls=%async_computation.4 | async-start | bytes 2359296 | tf_op jit(solution)/shard_map/all_to_all | solution.py:701
  165.0 15.9 %collective-permute-start.24 = (bf16[48,256]{1,0:T(8,128)(2,1)S(1)}, bf16[48,256]{1,0:T(8,128)(2,1)S(1)}, u32[]{:S(2)}, u32[]{:S(2)}) collective-permute-start(bf16[48,256]{1,0:T(8,128)(2,1)S(1)} %get-tuple-element.110), channel_id=1, source_target_pairs={{0,7},{1,6},{2,5},{3,4},{4,3},{5,2},{6,1},{7,0},{8,15},{9,14},{10,... | collective-permute-start | bytes 73736 | tf_op jit(solution)/shard_map/ppermute | solution.py:698
  182.1 5.5 %collective-permute-start.25 = (bf16[16,144,256]{2,1,0:T(8,128)(2,1)S(1)}, bf16[16,144,256]{2,1,0:T(8,128)(2,1)S(1)}, u32[]{:S(2)}, u32[]{:S(2)}) collective-permute-start(bf16[16,144,256]{2,1,0:T(8,128)(2,1)S(1)} %all-to-all-done.4.refs_1_), channel_id=1, source_target_pairs={{0,1},{1,0},{2,3},{3,2},{4,5},{5,4},{6,7},{7,6},{8,9},{9,8},{10,11... | collective-permute-start | bytes 3538952 | tf_op jit(solution)/shard_map/ppermute | solution.py:704
  (8 other events, 6.5 us)
